TPU v7x, 32 devices: a whole 2x2x4 slice. The times are simulated.
32 devices in a mesh: group: 2 (over x), expert: 8 (over z, y), tensor: 2 (over core).
Axes of the slice: x: 2, y: 2, z: 4, core: 2. Of those that a mesh axis runs over, the one named last changes fastest.
Arguments:
- tokens: bfloat16 [2048, 4096], P(('group', 'expert'), 'tensor'), parts along dimension 0, may hold values from -6 to 6
- down_weight: bfloat16 [4096, 1024], P('tensor', 'expert'), may hold values from -0.09375 to 0.09375
- up_weight: bfloat16 [4096, 1024], P('tensor', 'expert'), may hold values from -0.1875 to 0.1875
- gate_proj: bfloat16 [32, 1024, 768], P('expert', None, 'tensor'), may hold values from -0.1875 to 0.1875
- up_proj: bfloat16 [32, 1024, 768], P('expert', None, 'tensor'), may hold values from -0.1875 to 0.1875
- down_proj: bfloat16 [32, 768, 1024], P('expert', 'tensor'), may hold values from -0.21875 to 0.21875
- routes: int32 [2048, 16], P('group'), parts along dimension 0, may hold values from 0 to 31, all different within a row; in each aligned block of 128 rows (0 to 127, 128 to 255, ...) at most 80 rows name the same one
- gates: int32 [2048, 16], P('group'), parts along dimension 0, may hold values from 1 to 16384
- cotangent: bfloat16 [2048, 4096], P(('group', 'expert'), 'tensor'), parts along dimension 0, may hold values from -6 to 6
Outputs:
- out: bfloat16 [2048, 4096], P(('group', 'expert'), 'tensor'), parts along dimension 0
- tokens_grad: bfloat16 [2048, 4096], P(('group', 'expert'), 'tensor'), parts along dimension 0
- gate_proj_grad: bfloat16 [64, 1024, 768], P(('group', 'expert'), None, 'tensor'), parts along dimension 0
- up_proj_grad: bfloat16 [64, 1024, 768], P(('group', 'expert'), None, 'tensor'), parts along dimension 0
- down_proj_grad: bfloat16 [64, 768, 1024], P(('group', 'expert'), 'tensor'), parts along dimension 0
- down_grad: float32 [8192, 1024], P(('group', 'tensor'), 'expert'), parts along dimension 0
- up_grad: float32 [8192, 1024], P(('group', 'tensor'), 'expert'), parts along dimension 0
There are 2 independent parts, one for each index of `group`. A program takes and returns all parts, laid end to end along the dimension named above; an argument that names none is the same for every part. Nothing has to cross between parts.
Inputs may be any that keep to these rules, and one draw needn't show every extreme that they name: `routes`: each row names 16 different experts. In each aligned block of 128 rows (the tokens of one index of expert) no expert is named by more than 80 rows, and in every draw some expert is named by exactly 80 rows of one block.
All inputs are finite; a program needn't handle non-finite values.
Results may differ from a plain program's by a relative error of at most 0.025.
Values may be sent and summed in bfloat16 or wider, within the bound.
No kernel may reach another device: no remote copies, remote signals or barrier semaphores. Data moves between devices by JAX's collectives and lax.ppermute only.
A program may use at most 192 MiB of HBM per device.

v0:
```python
import jax
import jax.numpy as jnp
from jax import lax
from jax.sharding import PartitionSpec as P

gate_unit = 2.0 ** (-15)


def block_slots(block_routes, expert_total, capacity):
    choose = (
        block_routes[:, :, None] == jnp.arange(expert_total, dtype=jnp.int32)[None, None, :]
    ).astype(jnp.int32)
    token_hits = jnp.sum(choose, axis=1)
    before = jnp.cumsum(token_hits, axis=0) - token_hits
    position = jnp.sum(choose * before[:, None, :], axis=2)
    return block_routes * capacity + position


def tensor_total(partial_value):
    return lax.psum(partial_value.astype(jnp.bfloat16), "tensor").astype(jnp.float32)


def to_experts(row_data, send_token, peer_count, exp_local, capacity):
    latent_width = row_data.shape[1]
    padded = jnp.concatenate([row_data, jnp.zeros((1, latent_width), row_data.dtype)], axis=0)
    buffer = jnp.take(padded, send_token, axis=0).reshape(
        peer_count, exp_local, capacity, latent_width
    )
    arrived = lax.all_to_all(buffer, "expert", split_axis=0, concat_axis=2, tiled=True)
    return arrived.reshape(exp_local, peer_count * capacity, latent_width)


def from_experts(pieces, send_where, peer_count, exp_local, capacity):
    latent_width = pieces.shape[2]
    buffer = pieces.reshape(1, exp_local, peer_count * capacity, latent_width)
    returned = lax.all_to_all(buffer, "expert", split_axis=2, concat_axis=0, tiled=True)
    flat_rows = returned.reshape(peer_count * exp_local * capacity, latent_width)
    return jnp.take(flat_rows, send_where, axis=0)


def local(tokens, down_weight, up_weight, gate_proj, up_proj, down_proj, routes, gates, cotangent):
    peer_count = lax.axis_size("expert")
    own_index = lax.axis_index("expert")
    tok_rows = tokens.shape[0]
    route_count = routes.shape[1]
    exp_local = gate_proj.shape[0]
    expert_total = exp_local * peer_count
    capacity = 5 * tok_rows * route_count // (4 * expert_total)
    expert_span = peer_count * capacity
    down_full, up_full = (
        lax.all_gather(down_weight, "expert", axis=1, tiled=True),
        lax.all_gather(up_weight, "expert", axis=1, tiled=True),
    )
    gate_value = gates.astype(jnp.float32) * gate_unit
    routed = routes.reshape(peer_count, tok_rows, route_count)
    slots = jax.vmap(lambda block_routes: block_slots(block_routes, expert_total, capacity))(routed)
    position = slots - routed * capacity
    local_expert = routed - own_index * exp_local
    is_local = (local_expert >= 0) & (local_expert < exp_local)
    slot_where = (
        local_expert * expert_span
        + jnp.arange(peer_count, dtype=jnp.int32)[:, None, None] * capacity
        + position
    )
    slot_where = jnp.where(is_local, slot_where, exp_local * expert_span).reshape(-1)
    slot_gate = (
        jnp.zeros((exp_local * expert_span + 1,), jnp.float32)
        .at[slot_where]
        .set(gate_value.reshape(-1))[:-1]
    )
    gate_column = slot_gate.reshape(exp_local, expert_span, 1)
    send_where = lax.dynamic_index_in_dim(slots, own_index, 0, keepdims=False)
    own_gate = lax.dynamic_slice_in_dim(gate_value, own_index * tok_rows, tok_rows, 0)
    own_ids = jnp.broadcast_to(
        jnp.arange(tok_rows, dtype=jnp.int32)[:, None], (tok_rows, route_count)
    ).reshape(-1)
    send_token = (
        jnp.full((expert_total * capacity,), tok_rows, jnp.int32)
        .at[send_where.reshape(-1)]
        .set(own_ids)
    )
    partial_in = jnp.dot(tokens, down_full, preferred_element_type=jnp.float32)
    latent_in = tensor_total(partial_in).astype(jnp.bfloat16)
    expert_in = to_experts(latent_in, send_token, peer_count, exp_local, capacity)
    gate_pre = jnp.einsum("erl,elh->erh", expert_in, gate_proj, preferred_element_type=jnp.float32)
    up_pre = jnp.einsum("erl,elh->erh", expert_in, up_proj, preferred_element_type=jnp.float32)
    sigmoid_gate = jax.nn.sigmoid(gate_pre)
    activated = gate_pre * sigmoid_gate
    hidden = (activated * up_pre).astype(jnp.bfloat16)
    pieces = jnp.einsum(
        "erh,ehl->erl", hidden, down_proj, preferred_element_type=jnp.float32
    ).astype(jnp.bfloat16)
    returned = from_experts(pieces, send_where, peer_count, exp_local, capacity)
    latent_part = jnp.sum(returned.astype(jnp.float32) * own_gate[:, :, None], axis=1)
    latent_out = tensor_total(latent_part).astype(jnp.bfloat16)
    out = jnp.einsum("tl,dl->td", latent_out, up_full, preferred_element_type=jnp.float32).astype(
        jnp.bfloat16
    )
    grad_part = jnp.dot(cotangent, up_full, preferred_element_type=jnp.float32)
    latent_grad = tensor_total(grad_part).astype(jnp.bfloat16)
    arrived = to_experts(latent_grad, send_token, peer_count, exp_local, capacity)
    route_grad = (arrived.astype(jnp.float32) * gate_column).astype(jnp.bfloat16)
    hidden_grad = jnp.einsum(
        "erl,ehl->erh", route_grad, down_proj, preferred_element_type=jnp.float32
    )
    gate_pre_grad = (
        hidden_grad * up_pre * sigmoid_gate * (1.0 + gate_pre * (1.0 - sigmoid_gate))
    ).astype(jnp.bfloat16)
    up_pre_grad = (hidden_grad * activated).astype(jnp.bfloat16)
    down_proj_grad = jnp.einsum(
        "erh,erl->ehl", hidden, route_grad, preferred_element_type=jnp.float32
    ).astype(jnp.bfloat16)
    gate_proj_grad = jnp.einsum(
        "erl,erh->elh", expert_in, gate_pre_grad, preferred_element_type=jnp.float32
    ).astype(jnp.bfloat16)
    up_proj_grad = jnp.einsum(
        "erl,erh->elh", expert_in, up_pre_grad, preferred_element_type=jnp.float32
    ).astype(jnp.bfloat16)
    input_pieces = (
        jnp.einsum("erh,elh->erl", gate_pre_grad, gate_proj, preferred_element_type=jnp.float32)
        + jnp.einsum("erh,elh->erl", up_pre_grad, up_proj, preferred_element_type=jnp.float32)
    ).astype(jnp.bfloat16)
    returned_grad = from_experts(input_pieces, send_where, peer_count, exp_local, capacity)
    in_part = jnp.sum(returned_grad.astype(jnp.float32), axis=1)
    latent_in_grad = tensor_total(in_part).astype(jnp.bfloat16)
    tokens_grad = jnp.einsum(
        "tl,dl->td", latent_in_grad, down_full, preferred_element_type=jnp.float32
    ).astype(jnp.bfloat16)
    down_local = jnp.einsum("td,tl->dl", tokens, latent_in_grad, preferred_element_type=jnp.float32)
    up_local = jnp.einsum("td,tl->dl", cotangent, latent_out, preferred_element_type=jnp.float32)
    down_grad, up_grad = (
        lax.psum_scatter(
            down_local.astype(jnp.bfloat16), "expert", scatter_dimension=1, tiled=True
        ).astype(jnp.float32),
        lax.psum_scatter(
            up_local.astype(jnp.bfloat16), "expert", scatter_dimension=1, tiled=True
        ).astype(jnp.float32),
    )
    return (out, tokens_grad, gate_proj_grad, up_proj_grad, down_proj_grad, down_grad, up_grad)


def solution(mesh):
    in_specs = (
        P(("group", "expert"), "tensor"),
        P("tensor", "expert"),
        P("tensor", "expert"),
        P("expert", None, "tensor"),
        P("expert", None, "tensor"),
        P("expert", "tensor", None),
        P("group", None),
        P("group", None),
        P(("group", "expert"), "tensor"),
    )
    out_specs = (
        P(("group", "expert"), "tensor"),
        P(("group", "expert"), "tensor"),
        P(("group", "expert"), None, "tensor"),
        P(("group", "expert"), None, "tensor"),
        P(("group", "expert"), "tensor", None),
        P(("group", "tensor"), "expert"),
        P(("group", "tensor"), "expert"),
    )
    return jax.shard_map(local, mesh=mesh, in_specs=in_specs, out_specs=out_specs, check_vma=False)
```

profile of v0, /device:TPU:0, one launch (start us, length us, event | category | flops | bytes accessed | tf_op | source)
XLA Modules:
  0.0 1006.1 jit_solution(17970845488661878955)
XLA Ops:
  12.1 1.9 sub.26
  16.1 8.1 scatter_custom_fusion
  24.2 63.6 %all-gather.5.cloned.1.call-done = bf16[2048,1024]{1,0:T(8,128)(2,1)} async-done(((bf16[2048,128]{1,0:T(8,128)(2,1)}), bf16[2048,1024]{1,0:T(8,128)(2,1)}) %all-gather.5.cloned.1.call-update) | async-done | bytes 4194320 | tf_op jit(solution)/shard_map/all_gather | solution.py:52
  87.8 3.8 convolution_convert_fusion.5
  91.6 71.5 %all-gather.3.cloned.1.call-done = bf16[2048,1024]{1,0:T(8,128)(2,1)} async-done(((bf16[2048,128]{1,0:T(8,128)(2,1)}), bf16[2048,1024]{1,0:T(8,128)(2,1)}) %all-gather.3.cloned.1.call-update) | async-done | bytes 4194320 | tf_op jit(solution)/shard_map/all_gather | solution.py:51
  163.1 3.8 convolution_convert_fusion.6
  166.9 17.1 %all-reduce.9.cloned.1.call-done = (bf16[128,1024]{1,0:T(8,128)(2,1)}, bf16[128,1024]{1,0:T(8,128)(2,1)}) async-done(((bf16[128,1024]{1,0:T(8,128)(2,1)}, bf16[128,1024]{1,0:T(8,128)(2,1)}), (bf16[128,1024]{1,0:T(8,128)(2,1)}, bf16[128,1024]{1,0:T(8,128)(2,1)})) %all-reduce.9.cloned.1.call-update) | async-done | bytes 524304 | tf_op jit(solution)/shard_map/psum | solution.py:20
  186.7 13.1 %gather_fusion.2 = bf16[2560,1024]{1,0:T(8,128)(2,1)} fusion(bf16[129,1024]{1,0:T(8,128)(2,1)} %concatenate.7, s32[3072]{0:T(1024)S(1)} %pad_clamp_fusion), kind=kCustom, calls=%fused_computation.2.clone | custom fusion | bytes 10496000 | tf_op jit(solution)/shard_map/jit(_take)/gather | solution.py:26
  199.8 8.8 gather_fusion
  208.6 7.8 broadcast_select_fusion
  216.4 121.7 %all_to_all.54 = bf16[8,4,80,1024]{3,2,1,0:T(8,128)(2,1)} all-to-all(bf16[8,4,80,1024]{3,2,1,0:T(8,128)(2,1)S(1)} %bitcast.83), channel_id=1, replica_groups=mesh['group'=2,'expert'=8,'tensor'=2] {'expert'}, dimensions={0} | all-to-all | bytes 10485760 | tf_op jit(solution)/shard_map/all_to_all | solution.py:29
  338.1 4.8 all-to-all-start.2
  346.3 1.9 reshape.237
  354.7 60.9 %scatter_custom_fusion.1 = f32[2561]{0:T(1024)S(1)} fusion(s32[16384]{0:T(1024)} %bitcast.88, f32[16384]{0:T(1024)} %reshape.237, f32[]{:T(128)} %constant.42.clone.1), kind=kCustom, calls=%fused_computation.46 | custom fusion | bytes 10756 | tf_op jit(solution)/shard_map/scatter | solution.py:69
  415.6 5.8 copy.100
  421.4 36.4 %all-to-all-done.2 = bf16[8,4,80,1024]{3,2,1,0:T(8,128)(2,1)} async-done(((bf16[8,4,80,1024]{3,2,1,0:T(8,128)(2,1)}), bf16[8,4,80,1024]{3,2,1,0:T(8,128)(2,1)}, u32[]{:S(2)}, u32[]{:S(2)}) %all-to-all-start.2) | async-done | bytes 5242912 | tf_op jit(solution)/shard_map/all_to_all | solution.py:29
  457.9 7.8 convert_bitcast_fusion
  465.7 5.1 copy.106
  470.8 12.0 %fusion.8 = f32[4,640,384]{2,1,0:T(8,128)} fusion(bf16[4,640,1024]{2,1,0:T(8,128)(2,1)} %bitcast.84, bf16[4,1024,384]{2,1,0:T(8,128)(2,1)} %param.16), kind=kOutput, calls=%fused_computation.54 | convolution fusion | flops 2013265920 | bytes 12320768 | tf_op jit(solution)/shard_map/erl,elh->erh/dot_general | solution.py:85
  482.8 6.8 fusion.2
  489.6 11.2 %multiply_convert_fusion.3 = (bf16[4,640,384]{2,1,0:T(8,128)(2,1)S(1)}, bf16[4,640,384]{2,1,0:T(8,128)(2,1)}, bf16[4,640,384]{2,1,0:T(8,128)(2,1)}) fusion(f32[4,640,384]{2,1,0:T(8,128)} %fusion.8, f32[4,640,384]{2,1,0:T(8,128)} %fusion.2, bf16[4,640,1024]{2,1,0:T(8,128)(2,1)} %bitcast.85, bf16[4,1024,384]{2,1,0:T(8,128)(2,1)S(1)} %copy-done), kind=kOutput, calls=%fused_computation.19 | convolution fusion | flops 2028011520 | bytes 22151168 | tf_op jit(solution)/shard_map/erl,elh->erh/dot_general | solution.py:86
  502.1 3.2 convert_bitcast_fusion.1
  505.3 6.4 copy.101
  511.8 4.9 all-to-all-start.1
  516.7 5.5 fusion.9
  522.2 4.6 fusion
  526.9 8.9 copy.111
  535.7 95.8 %all-to-all-done.1 = bf16[1,4,640,1024]{3,1,0,2:T(4,128)(2,1)} async-done(((bf16[1,4,640,1024]{3,1,0,2:T(4,128)(2,1)}), bf16[1,4,640,1024]{3,1,0,2:T(4,128)(2,1)}, u32[]{:S(2)}, u32[]{:S(2)}) %all-to-all-start.1) | async-done | bytes 5242912 | tf_op jit(solution)/shard_map/all_to_all | solution.py:36
  631.5 4.6 all-to-all-start.3
  637.0 6.8 copy.102
  643.8 107.4 %all-to-all-done.3 = bf16[1,4,640,1024]{3,1,0,2:T(4,128)(2,1)} async-done(((bf16[1,4,640,1024]{3,1,0,2:T(4,128)(2,1)}), bf16[1,4,640,1024]{3,1,0,2:T(4,128)(2,1)}, u32[]{:S(2)}, u32[]{:S(2)}) %all-to-all-start.3) | async-done | bytes 5242912 | tf_op jit(solution)/shard_map/all_to_all | solution.py:36
  751.1 6.7 copy.112
  757.8 14.2 %gather_fusion.1 = bf16[2048,1024]{1,0:T(8,128)(2,1)} fusion(bf16[2560,1024]{1,0:T(8,128)(2,1)} %bitcast.75, s32[2048]{0:T(1024)S(1)} %broadcast_clamp_fusion), kind=kCustom, calls=%fused_computation.1.clone | custom fusion | bytes 8396800 | tf_op jit(solution)/shard_map/jit(_take)/gather | solution.py:38
  772.0 14.1 %gather_fusion.3 = bf16[2048,1024]{1,0:T(8,128)(2,1)} fusion(bf16[2560,1024]{1,0:T(8,128)(2,1)} %bitcast.76, s32[2048]{0:T(1024)S(1)} %broadcast_clamp_fusion), kind=kCustom, calls=%fused_computation.3.clone | custom fusion | bytes 8396800 | tf_op jit(solution)/shard_map/jit(_take)/gather | solution.py:38
  786.1 4.0 select_reduce_fusion
  790.1 3.0 multiply_reduce_fusion
  793.2 17.9 %all-reduce.7.cloned.1.call-done = (bf16[128,1024]{1,0:T(8,128)(2,1)}, bf16[128,1024]{1,0:T(8,128)(2,1)}) async-done(((bf16[128,1024]{1,0:T(8,128)(2,1)}, bf16[128,1024]{1,0:T(8,128)(2,1)}), (bf16[128,1024]{1,0:T(8,128)(2,1)}, bf16[128,1024]{1,0:T(8,128)(2,1)})) %all-reduce.7.cloned.1.call-update) | async-done | bytes 524304 | tf_op jit(solution)/shard_map/psum | solution.py:20
  811.1 4.4 convert_bitcast_fusion.3
  815.9 4.3 convert_bitcast_fusion.2
  820.3 8.1 convolution_convert_fusion.4
  828.4 7.6 convolution_convert_fusion.3
  836.0 4.2 convolution_convert_fusion.2
  840.2 2.3 convolution_convert_fusion.1
  842.5 2.3 convolution_convert_fusion
  844.8 60.1 %reduce-scatter.3.cloned.1.call-done = bf16[2048,128]{0,1:T(8,128)(2,1)} async-done(((bf16[2048,1024]{0,1:T(8,128)(2,1)}), bf16[2048,128]{0,1:T(8,128)(2,1)}) %reduce-scatter.3.cloned.1.call-update) | async-done | bytes 524304 | tf_op jit(solution)/shard_map/reduce_scatter | solution.py:132
  905.0 2.2 copy.117
  907.2 89.4 %reduce-scatter.5.cloned.1.call-done = bf16[2048,128]{0,1:T(8,128)(2,1)} async-done(((bf16[2048,1024]{0,1:T(8,128)(2,1)}), bf16[2048,128]{0,1:T(8,128)(2,1)}) %reduce-scatter.5.cloned.1.call-update) | async-done | bytes 524304 | tf_op jit(solution)/shard_map/reduce_scatter | solution.py:135
  996.5 2.2 copy.118
  (84 shorter events, 22.1 us)
Async XLA Ops:
  7.2 482.4 %copy-start = (bf16[4,1024,384]{2,1,0:T(8,128)(2,1)S(1)}, bf16[4,1024,384]{2,1,0:T(8,128)(2,1)}, u32[]{:S(2)}) copy-start(bf16[4,1024,384]{2,1,0:T(8,128)(2,1)} %param.17) | copy-start | bytes 9437188
  7.2 80.6 %all-gather.5.cloned.1.call-start = ((), (), s32[]{:S(2)}) async-start(), calls=%async_computation.7 | async-start | bytes 4718592 | tf_op jit(solution)/shard_map/all_gather | solution.py:52
  7.9 155.2 %all-gather.3.cloned.1.call-start = ((), (), s32[]{:S(2)}) async-start(), calls=%async_computation.6 | async-start | bytes 4718592 | tf_op jit(solution)/shard_map/all_gather | solution.py:51
  8.7 175.3 %all-reduce.9.cloned.1.call-start = ((), (), s32[]{:S(2)}) async-start(), calls=%async_computation.11 | async-start | bytes 1048576 | tf_op jit(solution)/shard_map/psum | solution.py:20
  338.1 5.8 copy-start.12
  338.1 119.8 %all-to-all-start.2 = ((bf16[8,4,80,1024]{3,2,1,0:T(8,128)(2,1)}), bf16[8,4,80,1024]{3,2,1,0:T(8,128)(2,1)}, u32[]{:S(2)}, u32[]{:S(2)}) async-start(bf16[8,4,80,1024]{3,2,1,0:T(8,128)(2,1)} %bitcast.82), calls=%async_computation.2 | async-start | bytes 10485760 | tf_op jit(solution)/shard_map/all_to_all | solution.py:29
  470.8 12.0 %copy-start.1 = (f32[1,4,8,80,1024]{4,3,2,1,0:T(8,128)}, f32[1,4,8,80,1024]{4,3,2,1,0:T(8,128)S(1)}, u32[]{:S(2)}) copy-start(f32[1,4,8,80,1024]{4,3,2,1,0:T(8,128)S(1)} %copy.106) | copy-start | bytes 31457284
  489.6 12.5 %copy-start.5 = (bf16[4,384,1024]{2,1,0:T(8,128)(2,1)S(1)}, bf16[4,384,1024]{2,1,0:T(8,128)(2,1)}, u32[]{:S(2)}) copy-start(bf16[4,384,1024]{2,1,0:T(8,128)(2,1)} %param.18) | copy-start | bytes 9437188
  500.8 1.3 copy-start.10
  511.8 119.8 %all-to-all-start.1 = ((bf16[1,4,640,1024]{3,1,0,2:T(4,128)(2,1)}), bf16[1,4,640,1024]{3,1,0,2:T(4,128)(2,1)}, u32[]{:S(2)}, u32[]{:S(2)}) async-start(bf16[1,4,640,1024]{3,1,0,2:T(4,128)(2,1)} %copy.101), calls=%async_computation.1 | async-start | bytes 10485760 | tf_op jit(solution)/shard_map/all_to_all | solution.py:36
  516.7 5.6 copy-start.8
  631.5 119.6 %all-to-all-start.3 = ((bf16[1,4,640,1024]{3,1,0,2:T(4,128)(2,1)}), bf16[1,4,640,1024]{3,1,0,2:T(4,128)(2,1)}, u32[]{:S(2)}, u32[]{:S(2)}) async-start(bf16[1,4,640,1024]{3,1,0,2:T(4,128)(2,1)} %copy.111), calls=%async_computation.3 | async-start | bytes 10485760 | tf_op jit(solution)/shard_map/all_to_all | solution.py:36
  636.2 174.9 %all-reduce.7.cloned.1.call-start = ((), (), s32[]{:S(2)}) async-start(), calls=%async_computation.10 | async-start | bytes 1048576 | tf_op jit(solution)/shard_map/psum | solution.py:20
  786.1 4.0 copy-start.2
  793.2 111.8 %reduce-scatter.3.cloned.1.call-start = ((), (), s32[]{:S(2)}) async-start(), calls=%async_computation.8 | async-start | bytes 4718592 | tf_op jit(solution)/shard_map/reduce_scatter | solution.py:132
  811.1 4.8 copy-start.7
  815.5 181.0 %reduce-scatter.5.cloned.1.call-start = ((), (), s32[]{:S(2)}) async-start(), calls=%async_computation.9 | async-start | bytes 4718592 | tf_op jit(solution)/shard_map/reduce_scatter | solution.py:135
  820.2 8.1 copy-start.9
  820.2 15.7 %slice-start = ((s8[10485760]{0:T(1024)(128)(4,1)}), s8[4194304]{0:T(1024)(128)(4,1)S(1)}, s32[]{:S(2)}) async-start(s8[10485760]{0:T(1024)(128)(4,1)} %bitcast.78), calls=%async_computation.12 | async-start | bytes 8388608
  820.3 15.7 %slice-start.1 = ((s8[10485760]{0:T(1024)(128)(4,1)}), s8[4194304]{0:T(1024)(128)(4,1)S(1)}, s32[]{:S(2)}) async-start(s8[10485760]{0:T(1024)(128)(4,1)} %bitcast.78), calls=%async_computation.13 | async-start | bytes 8388608
  828.4 7.6 slice-start.2
  828.4 7.6 copy-start.11
  836.0 4.2 copy-start.3
  840.2 2.3 copy-start.4
  840.2 2.3 copy-start.6
Sparse Core Ops, SparseCore 0:
  10.1 77.7 all-gather.4
  89.8 73.1 all-gather.2
  167.0 16.9 all-reduce.8
  793.3 17.7 all-reduce.6
  815.7 89.2 reduce-scatter.2
  908.9 87.6 reduce-scatter.4
where the time goes:
time: 1010 us
  waiting for transfers between devices  561 us (56%)
  local copies, waits for them, and re-layouts  181 us (18%)
  blocking collectives  122 us (12%)
  matrix products  84.1 us (8%)
  other arithmetic  28.4 us (3%)
  starting transfers between devices  15.1 us (1%)
  between operations  14.9 us (1%)
    all_to_all x2, waiting for transfers between devices, from_experts(): lax.all_to_all(buffer, 'expert', split_axis=2, concat_axis=0, tiled=True)  203 us
    all_to_all x1, blocking collectives, to_experts(): lax.all_to_all(buffer, 'expert', split_axis=0, concat_axis=2, tiled=True)  122 us
    reduce_scatter x1, waiting for transfers between devices, local(): lax.psum_scatter(up_local.astype(jnp.bfloat16), 'expert', scatter_dimensi...  89.4 us
    all_gather x1, waiting for transfers between devices, local(): lax.all_gather(down_weight, 'expert', axis=1, tiled=True)  71.5 us
    all_gather x1, waiting for transfers between devices, local(): lax.all_gather(up_weight, 'expert', axis=1, tiled=True)  63.6 us
    scatter x1, local copies, waits for them, and re-layouts, local(): slot_gate = jnp.zeros((exp_local * expert_span + 1,), jnp.float32).at[slo...  60.9 us
    reduce_scatter x1, waiting for transfers between devices, local(): lax.psum_scatter(down_local.astype(jnp.bfloat16), 'expert', scatter_dimen...  60.1 us
    all_to_all x1, waiting for transfers between devices, to_experts(): lax.all_to_all(buffer, 'expert', split_axis=0, concat_axis=2, tiled=True)  36.4 us
  transfers between devices with their start and end apart: 9, of which 9 were waited for; matrix products, arithmetic and copies ran while one was open for 15% of the time, Pallas kernels for 0%

commit v1 on v0

v1 whole, which is shorter than its diff:
```python
import jax
import jax.numpy as jnp
from jax import lax
from jax.experimental import pallas as pl
from jax.experimental.pallas import tpu as pltpu
from jax.sharding import PartitionSpec as P

gate_unit = 2.0 ** (-15)
bf16 = jnp.bfloat16
f32 = jnp.float32

NN = (((1,), (0,)), ((), ()))
NT = (((1,), (1,)), ((), ()))
TN = (((0,), (0,)), ((), ()))


def dot(a, b, dims=NN):
    return lax.dot_general(a, b, dims, preferred_element_type=f32)


def expert_kernel(
    x_ref, y_ref, g_ref, wg_ref, wu_ref, wd_ref,
    dwg_ref, dwu_ref, dwd_ref, lo_ref, lig_ref,
    wgu, hs, dpu, lo_acc, lig_acc,
):
    step = pl.program_id(0)
    steps = pl.num_programs(0)
    rows_total, latent = x_ref.shape
    pair, _, width = wg_ref.shape
    block = 256

    for j in range(pair):
        wgu[:, 2 * j * width : (2 * j + 1) * width] = wg_ref[j]
        wgu[:, (2 * j + 1) * width : (2 * j + 2) * width] = wu_ref[j]

    @pl.when(step == 0)
    def _():
        lo_acc[...] = jnp.zeros_like(lo_acc)
        lig_acc[...] = jnp.zeros_like(lig_acc)

    def row_block(i, _):
        rows = pl.ds(pl.multiple_of(i * block, block), block)
        x = x_ref[rows, :]
        hidden_grad = dot(y_ref[rows, :], wd_ref[...], NT)
        for j in range(pair):
            both = dot(x, wgu[:, 2 * j * width : (2 * j + 2) * width])
            gate_pre, up_pre = both[:, :width], both[:, width:]
            gate = g_ref[0, rows, j : j + 1]
            sig = jax.nn.sigmoid(gate_pre)
            act = gate_pre * sig
            hg = hidden_grad[:, j * width : (j + 1) * width] * gate
            hs[rows, j * width : (j + 1) * width] = (act * up_pre * gate).astype(bf16)
            dp = hg * up_pre * (sig * (1.0 + gate_pre * (1.0 - sig)))
            dpu[rows, 2 * j * width : (2 * j + 1) * width] = dp.astype(bf16)
            dpu[rows, (2 * j + 1) * width : (2 * j + 2) * width] = (hg * act).astype(bf16)
        lo_acc[rows, :] += dot(hs[rows, :], wd_ref[...])
        lig_acc[rows, :] += dot(dpu[rows, :], wgu[...], NT)
        return 0

    lax.fori_loop(0, rows_total // block, row_block, 0)

    def col_block(i, _):
        cols = pl.ds(pl.multiple_of(i * block, block), block)
        grads = dot(x_ref[:, cols], dpu[...], TN)
        for j in range(pair):
            dwg_ref[j, cols, :] = grads[:, 2 * j * width : (2 * j + 1) * width].astype(bf16)
            dwu_ref[j, cols, :] = grads[:, (2 * j + 1) * width : (2 * j + 2) * width].astype(bf16)
        return 0

    lax.fori_loop(0, latent // block, col_block, 0)
    dwd_ref[...] = dot(hs[...], y_ref[...], TN).astype(bf16)

    @pl.when(step == steps - 1)
    def _():
        lo_ref[...] = lo_acc[...].astype(bf16)
        lig_ref[...] = lig_acc[...].astype(bf16)


def experts(x, y, gate_columns, gate_proj, up_proj, down_proj):
    rows, latent = x.shape
    count, _, width = gate_proj.shape
    pair = 2 if rows <= 1024 and count % 2 == 0 else 1
    whole = lambda i: (0, 0)
    per_step = lambda i: (i, 0, 0)
    columns = gate_columns.reshape(rows, count // pair, pair).transpose(1, 0, 2)
    dwg, dwu, dwd, lo, lig = pl.pallas_call(
        expert_kernel,
        grid=(count // pair,),
        in_specs=[
            pl.BlockSpec((rows, latent), whole),
            pl.BlockSpec((rows, latent), whole),
            pl.BlockSpec((1, rows, pair), per_step),
            pl.BlockSpec((pair, latent, width), per_step),
            pl.BlockSpec((pair, latent, width), per_step),
            pl.BlockSpec((pair * width, latent), lambda i: (i, 0)),
        ],
        out_specs=[
            pl.BlockSpec((pair, latent, width), per_step),
            pl.BlockSpec((pair, latent, width), per_step),
            pl.BlockSpec((pair * width, latent), lambda i: (i, 0)),
            pl.BlockSpec((rows, latent), whole),
            pl.BlockSpec((rows, latent), whole),
        ],
        out_shape=[
            jax.ShapeDtypeStruct(gate_proj.shape, bf16),
            jax.ShapeDtypeStruct(up_proj.shape, bf16),
            jax.ShapeDtypeStruct((count * width, latent), bf16),
            jax.ShapeDtypeStruct((rows, latent), bf16),
            jax.ShapeDtypeStruct((rows, latent), bf16),
        ],
        scratch_shapes=[
            pltpu.VMEM((latent, 2 * pair * width), bf16),
            pltpu.VMEM((rows, pair * width), bf16),
            pltpu.VMEM((rows, 2 * pair * width), bf16),
            pltpu.VMEM((rows, latent), f32),
            pltpu.VMEM((rows, latent), f32),
        ],
        compiler_params=pltpu.CompilerParams(vmem_limit_bytes=(40 if rows <= 1024 else 60) * 1024 * 1024),
        cost_estimate=pl.CostEstimate(
            flops=18 * rows * latent * width * count,
            bytes_accessed=12 * latent * width * count + 8 * rows * latent,
            transcendentals=rows * width * count,
        ),
    )(x, y, columns, gate_proj, up_proj, down_proj.reshape(count * width, latent))
    return dwg, dwu, dwd.reshape(down_proj.shape), lo, lig


def local(tokens, down_weight, up_weight, gate_proj, up_proj, down_proj, routes, gates, cotangent):
    n_expert = lax.axis_size("expert")
    nz = n_expert // 2
    own = lax.axis_index("expert")
    z, y = own // 2, own % 2
    t = lax.axis_index("tensor")
    tok_rows = tokens.shape[0]
    half_rows = tok_rows // 2
    half_d = tokens.shape[1] // 2
    latent = gate_proj.shape[1]
    exp_local = gate_proj.shape[0]
    shard = down_weight.shape[1]

    y_perm = [(e, e ^ 1) for e in range(n_expert)]
    z_up = [(e, (e + 2) % n_expert) for e in range(n_expert)]
    z_down = [((e + 2) % n_expert, e) for e in range(n_expert)]
    y_swap = lambda v: lax.ppermute(v, "expert", y_perm)
    t_swap = lambda v: lax.ppermute(v, "tensor", [(0, 1), (1, 0)])

    def add(a, b):
        return (a.astype(f32) + b.astype(f32)).astype(bf16)

    def turn(v, axis):
        blocks = jnp.split(v, nz, axis=axis)
        orders = [
            jnp.concatenate([blocks[(c - k) % nz] for k in range(nz)], axis=axis)
            for c in range(nz)
        ]
        result = orders[0]
        for c in range(1, nz):
            result = jnp.where(z == c, orders[c], result)
        return result

    def flip(v, index, axis):
        first, second = jnp.split(v, 2, axis=axis)
        return jnp.where(index == 0, v, jnp.concatenate([second, first], axis=axis))

    def gather_z(v):
        parts = [v]
        for _ in range(nz - 1):
            parts.append(lax.ppermute(parts[-1], "expert", z_up))
        return parts

    def scatter_z(parts):
        total = parts[nz - 1]
        for k in range(nz - 2, -1, -1):
            total = add(lax.ppermute(total, "expert", z_down), parts[k])
        return total

    def plane_rows(v):
        halves = v.reshape(tok_rows, 2, half_d)
        mine = lax.dynamic_index_in_dim(halves, y, 1, keepdims=False)
        other = lax.dynamic_index_in_dim(halves, 1 - y, 1, keepdims=False)
        return jnp.concatenate([mine, y_swap(other)], axis=0)

    def plane_weight(v):
        halves = v.reshape(2, half_d, shard)
        mine = lax.dynamic_index_in_dim(halves, y, 0, keepdims=False)
        received = y_swap(lax.dynamic_index_in_dim(halves, 1 - y, 0, keepdims=False))
        first = jnp.where(y == 0, mine, received)
        second = jnp.where(y == 0, received, mine)
        return jnp.concatenate([first, second], axis=1)

    def project(rows, weights):
        part = jnp.concatenate([dot(rows, w).astype(bf16) for w in weights], axis=1)
        part = part.reshape(2, 2, half_rows, latent)
        mine = lax.dynamic_index_in_dim(part, t, 1, keepdims=False)
        part = add(mine, t_swap(lax.dynamic_index_in_dim(part, 1 - t, 1, keepdims=False)))
        part = add(part[0], y_swap(part[1]))
        part = turn(part, 1)
        part = jnp.stack(gather_z(part))
        part = jnp.stack([part, y_swap(part)])
        part = jnp.stack([part, t_swap(part)])
        return part.reshape(4 * nz * half_rows, latent)

    def collect(part):
        part = part.reshape(2, 2, nz, half_rows, latent)
        part = add(part[0], t_swap(part[1]))
        part = add(part[0], y_swap(part[1]))
        part = scatter_z([part[k] for k in range(nz)])
        part = turn(part, 1)
        part = jnp.stack([part, y_swap(part)])
        part = flip(jnp.stack([part, t_swap(part)], axis=1), t, 1)
        return part.reshape(2 * tok_rows, latent)

    def finish(part, rows, weights):
        cols = latent // nz
        whole = sum(
            dot(part[:, k * cols : (k + 1) * cols], weights[k], NT) for k in range(nz)
        ).astype(bf16)
        theirs = y_swap(whole[tok_rows:])
        result = jnp.where(
            y == 0,
            jnp.concatenate([whole[:tok_rows], theirs], axis=1),
            jnp.concatenate([theirs, whole[:tok_rows]], axis=1),
        )
        grad = scatter_z(
            [dot(rows, part[:, k * cols : (k + 1) * cols], TN).astype(bf16) for k in range(nz)]
        )
        grad = grad.reshape(half_d, 2, shard)
        mine = lax.dynamic_index_in_dim(grad, y, 1, keepdims=False)
        theirs = y_swap(lax.dynamic_index_in_dim(grad, 1 - y, 1, keepdims=False))
        grad = jnp.where(
            y == 0,
            jnp.concatenate([mine, theirs], axis=0),
            jnp.concatenate([theirs, mine], axis=0),
        ).astype(f32)
        return result, grad

    local_ids = own * exp_local + jnp.arange(exp_local, dtype=jnp.int32)
    hit = routes[:, :, None] == local_ids[None, None, :]
    gate_all = jnp.sum(jnp.where(hit, gates[:, :, None], 0), axis=1).astype(f32) * gate_unit
    gate_all = turn(gate_all.reshape(nz, 2, 2, half_rows, exp_local), 0)
    gate_all = flip(flip(gate_all, y, 1), t, 2)
    gate_columns = gate_all.transpose(2, 1, 0, 3, 4).reshape(-1, exp_local)

    down_parts = gather_z(plane_weight(down_weight))
    up_parts = gather_z(plane_weight(up_weight))
    token_rows = plane_rows(tokens)
    cot_rows = plane_rows(cotangent)
    latent_in = project(token_rows, down_parts)
    latent_grad = project(cot_rows, up_parts)

    gate_proj_grad, up_proj_grad, down_proj_grad, out_part, in_part = experts(
        latent_in, latent_grad, gate_columns, gate_proj, up_proj, down_proj
    )

    latent_out = collect(out_part)
    latent_in_grad = collect(in_part)
    out, up_grad = finish(latent_out, cot_rows, up_parts)
    tokens_grad, down_grad = finish(latent_in_grad, token_rows, down_parts)
    return (out, tokens_grad, gate_proj_grad, up_proj_grad, down_proj_grad, down_grad, up_grad)


def solution(mesh):
    in_specs = (
        P(("group", "expert"), "tensor"),
        P("tensor", "expert"),
        P("tensor", "expert"),
        P("expert", None, "tensor"),
        P("expert", None, "tensor"),
        P("expert", "tensor", None),
        P("group", None),
        P("group", None),
        P(("group", "expert"), "tensor"),
    )
    out_specs = (
        P(("group", "expert"), "tensor"),
        P(("group", "expert"), "tensor"),
        P(("group", "expert"), None, "tensor"),
        P(("group", "expert"), None, "tensor"),
        P(("group", "expert"), "tensor", None),
        P(("group", "tensor"), "expert"),
        P(("group", "tensor"), "expert"),
    )
    return jax.shard_map(local, mesh=mesh, in_specs=in_specs, out_specs=out_specs, check_vma=False)
```

time: 1010 us -> 336 us (0.33)
  waiting for transfers between devices: 561 us -> 192 us
  local copies, waits for them, and re-layouts: 181 us -> 10 us
  blocking collectives: 122 us -> 0 us
  matrix products: 84.1 us -> 22.1 us
  Pallas kernels: 0 us -> 42.2 us
  starting transfers between devices: 15.1 us -> 52.5 us
  other arithmetic: 28.4 us -> 14.9 us
  between operations: 14.9 us -> 1.68 us
    all_to_all x3 -> x0, waiting for transfers between devices: 240 us -> none  [the longest x2 203 us: from_experts(): lax.all_to_all(buffer, 'expert', split_axis=2, concat_axis=0, tiled=True)]
    ppermute x0 -> x48, waiting for transfers between devices: none -> 192 us  [the longest x12 72.4 us: gather_z(): parts.append(lax.ppermute(parts[-1], 'expert', z_up))]
    reduce_scatter x2 -> x0, waiting for transfers between devices: 149 us -> none  [the longest x1 89.4 us: local(): lax.psum_scatter(up_local.astype(jnp.bfloat16), 'expert', scatter_dimensi...]
    all_gather x2 -> x0, waiting for transfers between devices: 135 us -> none  [the longest x1 71.5 us: local(): lax.all_gather(down_weight, 'expert', axis=1, tiled=True)]
    all_to_all x1 -> x0, blocking collectives: 122 us -> none  [to_experts(): lax.all_to_all(buffer, 'expert', split_axis=0, concat_axis=2, tiled=True)]
    scatter x2 -> x0, local copies, waits for them, and re-layouts: 69 us -> none  [the longest x1 60.9 us: local(): slot_gate = jnp.zeros((exp_local * expert_span + 1,), jnp.float32).at[slo...]
    dot_general x15 -> x24, matrix products: 84.1 us -> 22.1 us  [dot(): return lax.dot_general(a, b, dims, preferred_element_type=f32)]
    ppermute x0 -> x48, starting transfers between devices: none -> 52.5 us  [the longest x12 26.3 us: scatter_z(): total = add(lax.ppermute(total, 'expert', z_down), parts[k])]
  transfers between devices with their start and end apart: 9 -> 48, of which waited for: 9 -> 36; matrix products, arithmetic and copies ran while one was open for 15% -> 12% of each run, Pallas kernels for 0% -> 0%
where the time goes in v1:
time: 336 us; the launch traced here: 335 us
  waiting for transfers between devices  192 us (57%)
  starting transfers between devices  52.5 us (16%)
  Pallas kernels  42.2 us (13%)
  matrix products  22.1 us (7%)
  other arithmetic  14.9 us (4%)
  local copies, waits for them, and re-layouts  10 us (3%)
    ppermute x12, waiting for transfers between devices, gather_z(): parts.append(lax.ppermute(parts[-1], 'expert', z_up))  72.4 us
    ppermute x16, waiting for transfers between devices, local(): y_swap = lambda v: lax.ppermute(v, 'expert', y_perm)  64.2 us
    ppermute x12, waiting for transfers between devices, scatter_z(): total = add(lax.ppermute(total, 'expert', z_down), parts[k])  53 us
    pallas_call x1, Pallas kernels, experts(): pl.pallas_call(expert_kernel, grid=(count // pair,), in_specs=[pl.BlockSp...  42.2 us
    ppermute x12, starting transfers between devices, scatter_z(): total = add(lax.ppermute(total, 'expert', z_down), parts[k])  26.3 us
    dot_general x24, matrix products, dot(): return lax.dot_general(a, b, dims, preferred_element_type=f32)  22.1 us
    ppermute x16, starting transfers between devices, local(): y_swap = lambda v: lax.ppermute(v, 'expert', y_perm)  21.2 us
  transfers between devices with their start and end apart: 48, of which 36 were waited for; matrix products, arithmetic and copies ran while one was open for 12% of the time, Pallas kernels for 0%

profile of v1, /device:TPU:0, one launch (start us, length us, event | category | flops | bytes accessed | tf_op | source)
XLA Modules:
  0.0 335.4 jit_solution(8515744562687243118)
XLA Ops:
  1.7 3.0 collective-permute-start.13
  5.8 6.1 %collective-permute-done.13 = bf16[1024,128]{1,0:T(8,128)(2,1)S(1)} collective-permute-done((bf16[1024,128]{1,0:T(8,128)(2,1)S(1)}, bf16[1024,128]{1,0:T(8,128)(2,1)S(1)}, u32[]{:S(2)}, u32[]{:S(2)}) %collective-permute-start.13) | collective-permute-done | bytes 262176 | tf_op jit(solution)/shard_map/ppermute | solution.py:144
  13.8 2.1 collective-permute-start.14
  17.6 1.8 collective-permute-start.2
  23.1 8.0 %collective-permute-done.14 = bf16[1024,256]{1,0:T(8,128)(2,1)} collective-permute-done((bf16[1024,256]{1,0:T(8,128)(2,1)}, bf16[1024,256]{1,0:T(8,128)(2,1)}, u32[]{:S(2)}, u32[]{:S(2)}) %collective-permute-start.14) | collective-permute-done | bytes 524320 | tf_op jit(solution)/shard_map/ppermute | solution.py:168
  32.8 9.4 %collective-permute-done.2 = bf16[1024,256]{1,0:T(8,128)(2,1)S(1)} collective-permute-done((bf16[1024,256]{1,0:T(8,128)(2,1)}, bf16[1024,256]{1,0:T(8,128)(2,1)S(1)}, u32[]{:S(2)}, u32[]{:S(2)}) %collective-permute-start.2) | collective-permute-done | bytes 524320 | tf_op jit(solution)/shard_map/ppermute | solution.py:168
  44.0 9.5 %collective-permute-done.15 = bf16[1024,256]{1,0:T(8,128)(2,1)} collective-permute-done((bf16[1024,256]{1,0:T(8,128)(2,1)}, bf16[1024,256]{1,0:T(8,128)(2,1)}, u32[]{:S(2)}, u32[]{:S(2)}) %collective-permute-start.15) | collective-permute-done | bytes 524320 | tf_op jit(solution)/shard_map/ppermute | solution.py:168
  53.6 2.0 convolution_convert_fusion.14
  55.6 9.2 %collective-permute-done.3 = bf16[1024,256]{1,0:T(8,128)(2,1)} collective-permute-done((bf16[1024,256]{1,0:T(8,128)(2,1)S(1)}, bf16[1024,256]{1,0:T(8,128)(2,1)}, u32[]{:S(2)}, u32[]{:S(2)}) %collective-permute-start.3) | collective-permute-done | bytes 524320 | tf_op jit(solution)/shard_map/ppermute | solution.py:168
  67.8 8.2 %collective-permute-done.16 = bf16[1024,256]{1,0:T(8,128)(2,1)S(1)} collective-permute-done((bf16[1024,256]{1,0:T(8,128)(2,1)}, bf16[1024,256]{1,0:T(8,128)(2,1)S(1)}, u32[]{:S(2)}, u32[]{:S(2)}) %collective-permute-start.16) | collective-permute-done | bytes 524320 | tf_op jit(solution)/shard_map/ppermute | solution.py:168
  76.7 7.6 %collective-permute-done.4 = bf16[1024,256]{1,0:T(8,128)(2,1)S(1)} collective-permute-done((bf16[1024,256]{1,0:T(8,128)(2,1)}, bf16[1024,256]{1,0:T(8,128)(2,1)S(1)}, u32[]{:S(2)}, u32[]{:S(2)}) %collective-permute-start.4) | collective-permute-done | bytes 524320 | tf_op jit(solution)/shard_map/ppermute | solution.py:168
  86.9 1.5 collective-permute-start.18
  89.9 3.3 collective-permute-done.18
  93.4 2.2 collective-permute-done.6
  95.9 4.5 %collective-permute-done.19 = bf16[64,1024]{1,0:T(8,128)(2,1)S(1)} collective-permute-done((bf16[64,1024]{1,0:T(8,128)(2,1)S(1)}, bf16[64,1024]{1,0:T(8,128)(2,1)S(1)}, u32[]{:S(2)}, u32[]{:S(2)}) %collective-permute-start.19) | collective-permute-done | bytes 131104 | tf_op jit(solution)/shard_map/ppermute | solution.py:168
  100.4 2.8 collective-permute-done.7
  103.2 4.7 %collective-permute-done.20 = bf16[64,1024]{1,0:T(8,128)(2,1)S(1)} collective-permute-done((bf16[64,1024]{1,0:T(8,128)(2,1)S(1)}, bf16[64,1024]{1,0:T(8,128)(2,1)S(1)}, u32[]{:S(2)}, u32[]{:S(2)}) %collective-permute-start.20) | collective-permute-done | bytes 131104 | tf_op jit(solution)/shard_map/ppermute | solution.py:168
  108.0 3.3 collective-permute-done.8
  111.4 4.2 %collective-permute-done.21 = bf16[64,1024]{1,0:T(8,128)(2,1)S(1)} collective-permute-done((bf16[64,1024]{1,0:T(8,128)(2,1)S(1)}, bf16[64,1024]{1,0:T(8,128)(2,1)S(1)}, u32[]{:S(2)}, u32[]{:S(2)}) %collective-permute-start.21) | collective-permute-done | bytes 131104 | tf_op jit(solution)/shard_map/ppermute | solution.py:168
  118.2 1.5 collective-permute-start.10
  119.9 10.7 %collective-permute-done.22 = bf16[4,64,1024]{2,1,0:T(8,128)(2,1)S(1)} collective-permute-done((bf16[4,64,1024]{2,1,0:T(8,128)(2,1)S(1)}, bf16[4,64,1024]{2,1,0:T(8,128)(2,1)S(1)}, u32[]{:S(2)}, u32[]{:S(2)}) %collective-permute-start.22) | collective-permute-done | bytes 524320 | tf_op jit(solution)/shard_map/ppermute | solution.py:144
  131.7 5.0 %collective-permute-done.10 = bf16[4,64,1024]{2,1,0:T(8,128)(2,1)S(1)} collective-permute-done((bf16[4,64,1024]{2,1,0:T(8,128)(2,1)S(1)}, bf16[4,64,1024]{2,1,0:T(8,128)(2,1)S(1)}, u32[]{:S(2)}, u32[]{:S(2)}) %collective-permute-start.10) | collective-permute-done | bytes 524320 | tf_op jit(solution)/shard_map/ppermute | solution.py:144
  140.8 1.6 pad_maximum_fusion
  143.0 42.2 %shard_map.144 = (bf16[4,1024,384]{2,1,0:T(8,128)(2,1)}, bf16[4,1024,384]{2,1,0:T(8,128)(2,1)}, bf16[1536,1024]{1,0:T(8,128)(2,1)}, bf16[1024,1024]{1,0:T(8,128)(2,1)S(1)}, bf16[1024,1024]{1,0:T(8,128)(2,1)S(1)}) custom-call(bf16[1024,1024]{1,0:T(8,128)(2,1)S(1)} %bitcast.202, bf16[1024,1024]{1,0:T(8,128)(2,1)S(1)} %bitcast.201, ...), custom_call_target="tpu_custom_call" | custom-call | flops 28991029248 | bytes 27262976 | tf_op jit(solution)/shard_map/pallas_call | solution.py:86
  186.2 1.9 collective-permute-done.24
  188.5 1.6 collective-permute-start.25
  191.6 11.7 %collective-permute-done.25 = bf16[4,64,1024]{2,1,0:T(8,128)(2,1)S(1)} collective-permute-done((bf16[4,64,1024]{2,1,0:T(8,128)(2,1)S(1)}, bf16[4,64,1024]{2,1,0:T(8,128)(2,1)S(1)}, u32[]{:S(2)}, u32[]{:S(2)}) %collective-permute-start.25) | collective-permute-done | bytes 524320 | tf_op jit(solution)/shard_map/ppermute | solution.py:144
  204.2 9.6 %collective-permute-done.33 = bf16[4,64,1024]{2,1,0:T(8,128)(2,1)S(1)} collective-permute-done((bf16[4,64,1024]{2,1,0:T(8,128)(2,1)S(1)}, bf16[4,64,1024]{2,1,0:T(8,128)(2,1)S(1)}, u32[]{:S(2)}, u32[]{:S(2)}) %collective-permute-start.33) | collective-permute-done | bytes 524320 | tf_op jit(solution)/shard_map/ppermute | solution.py:144
  214.8 5.7 %collective-permute-done.34 = bf16[64,1024]{1,0:T(8,128)(2,1)S(1)} collective-permute-done((bf16[64,1024]{1,0:T(8,128)(2,1)S(1)}, bf16[64,1024]{1,0:T(8,128)(2,1)S(1)}, u32[]{:S(2)}, u32[]{:S(2)}) %collective-permute-start.34) | collective-permute-done | bytes 131104 | tf_op jit(solution)/shard_map/ppermute | solution.py:174
  220.5 2.2 collective-permute-start.35
  224.1 1.8 collective-permute-done.35
  225.9 4.1 %collective-permute-start.36 = (bf16[64,1024]{1,0:T(8,128)(2,1)S(1)}, bf16[64,1024]{1,0:T(8,128)(2,1)S(1)}, u32[]{:S(2)}, u32[]{:S(2)}) collective-permute-start(bf16[64,1024]{1,0:T(8,128)(2,1)S(1)} %fusion.17), channel_id=1, source_target_pairs={{4,0},{6,2},{8,4},{10,6},{12,8},{14,10},{0,12},{2,14},{5,1},{7,3},... | collective-permute-start | bytes 393224 | tf_op jit(solution)/shard_map/ppermute | solution.py:174
  232.6 2.5 collective-permute-done.29
  236.9 4.4 %collective-permute-done.37 = bf16[64,1024]{1,0:T(8,128)(2,1)S(1)} collective-permute-done((bf16[64,1024]{1,0:T(8,128)(2,1)S(1)}, bf16[64,1024]{1,0:T(8,128)(2,1)S(1)}, u32[]{:S(2)}, u32[]{:S(2)}) %collective-permute-start.37) | collective-permute-done | bytes 131104 | tf_op jit(solution)/shard_map/ppermute | solution.py:144
  247.0 2.1 collective-permute-start.44
  251.4 10.4 %collective-permute-done.44 = bf16[1024,256]{1,0:T(8,128)(2,1)S(1)} collective-permute-done((bf16[1024,256]{1,0:T(8,128)(2,1)S(1)}, bf16[1024,256]{1,0:T(8,128)(2,1)S(1)}, u32[]{:S(2)}, u32[]{:S(2)}) %collective-permute-start.44) | collective-permute-done | bytes 524320 | tf_op jit(solution)/shard_map/ppermute | solution.py:174
  262.2 3.9 %collective-permute-start.45 = (bf16[1024,256]{1,0:T(8,128)(2,1)S(1)}, bf16[1024,256]{1,0:T(8,128)(2,1)S(1)}, u32[]{:S(2)}, u32[]{:S(2)}) collective-permute-start(bf16[1024,256]{1,0:T(8,128)(2,1)S(1)} %add_convert_fusion.2), channel_id=1, source_target_pairs={{4,0},{6,2},{8,4},{10,6},{12,8},{14,10},{0,12},{2,14},{5,1},{7,3},... | collective-permute-start | bytes 1572872 | tf_op jit(solution)/shard_map/ppermute | solution.py:174
  266.1 7.0 %collective-permute-done.40 = bf16[1024,256]{1,0:T(8,128)(2,1)S(1)} collective-permute-done((bf16[1024,256]{1,0:T(8,128)(2,1)S(1)}, bf16[1024,256]{1,0:T(8,128)(2,1)S(1)}, u32[]{:S(2)}, u32[]{:S(2)}) %collective-permute-start.40) | collective-permute-done | bytes 524320 | tf_op jit(solution)/shard_map/ppermute | solution.py:174
  274.4 3.9 %collective-permute-start.41 = (bf16[1024,256]{1,0:T(8,128)(2,1)S(1)}, bf16[1024,256]{1,0:T(8,128)(2,1)S(1)}, u32[]{:S(2)}, u32[]{:S(2)}) collective-permute-start(bf16[1024,256]{1,0:T(8,128)(2,1)S(1)} %add_convert_fusion.5), channel_id=1, source_target_pairs={{4,0},{6,2},{8,4},{10,6},{12,8},{14,10},{0,12},{2,14},{5,1},{7,3},... | collective-permute-start | bytes 1572872 | tf_op jit(solution)/shard_map/ppermute | solution.py:174
  279.7 4.6 %collective-permute-done.45 = bf16[1024,256]{1,0:T(8,128)(2,1)S(1)} collective-permute-done((bf16[1024,256]{1,0:T(8,128)(2,1)S(1)}, bf16[1024,256]{1,0:T(8,128)(2,1)S(1)}, u32[]{:S(2)}, u32[]{:S(2)}) %collective-permute-start.45) | collective-permute-done | bytes 524320 | tf_op jit(solution)/shard_map/ppermute | solution.py:174
  284.7 3.9 %collective-permute-start.46 = (bf16[1024,256]{1,0:T(8,128)(2,1)S(1)}, bf16[1024,256]{1,0:T(8,128)(2,1)S(1)}, u32[]{:S(2)}, u32[]{:S(2)}) collective-permute-start(bf16[1024,256]{1,0:T(8,128)(2,1)S(1)} %add_convert_fusion.1), channel_id=1, source_target_pairs={{4,0},{6,2},{8,4},{10,6},{12,8},{14,10},{0,12},{2,14},{5,1},{7,3},... | collective-permute-start | bytes 1572872 | tf_op jit(solution)/shard_map/ppermute | solution.py:174
  288.6 7.0 %collective-permute-done.41 = bf16[1024,256]{1,0:T(8,128)(2,1)S(1)} collective-permute-done((bf16[1024,256]{1,0:T(8,128)(2,1)S(1)}, bf16[1024,256]{1,0:T(8,128)(2,1)S(1)}, u32[]{:S(2)}, u32[]{:S(2)}) %collective-permute-start.41) | collective-permute-done | bytes 524320 | tf_op jit(solution)/shard_map/ppermute | solution.py:174
  296.9 3.9 %collective-permute-start.42 = (bf16[1024,256]{1,0:T(8,128)(2,1)S(1)}, bf16[1024,256]{1,0:T(8,128)(2,1)S(1)}, u32[]{:S(2)}, u32[]{:S(2)}) collective-permute-start(bf16[1024,256]{1,0:T(8,128)(2,1)S(1)} %add_convert_fusion.4), channel_id=1, source_target_pairs={{4,0},{6,2},{8,4},{10,6},{12,8},{14,10},{0,12},{2,14},{5,1},{7,3},... | collective-permute-start | bytes 1572872 | tf_op jit(solution)/shard_map/ppermute | solution.py:174
  301.7 5.0 %collective-permute-done.46 = bf16[1024,256]{1,0:T(8,128)(2,1)S(1)} collective-permute-done((bf16[1024,256]{1,0:T(8,128)(2,1)S(1)}, bf16[1024,256]{1,0:T(8,128)(2,1)S(1)}, u32[]{:S(2)}, u32[]{:S(2)}) %collective-permute-start.46) | collective-permute-done | bytes 524320 | tf_op jit(solution)/shard_map/ppermute | solution.py:174
  307.1 10.1 %collective-permute-done.42 = bf16[1024,256]{1,0:T(8,128)(2,1)S(1)} collective-permute-done((bf16[1024,256]{1,0:T(8,128)(2,1)S(1)}, bf16[1024,256]{1,0:T(8,128)(2,1)S(1)}, u32[]{:S(2)}, u32[]{:S(2)}) %collective-permute-start.42) | collective-permute-done | bytes 524320 | tf_op jit(solution)/shard_map/ppermute | solution.py:174
  318.8 2.2 constant_dynamic-slice_fusion.1
  325.2 5.2 %collective-permute-done.47 = bf16[1024,128]{1,0:T(8,128)(2,1)S(1)} collective-permute-done((bf16[1024,128]{1,0:T(8,128)(2,1)S(1)}, bf16[1024,128]{1,0:T(8,128)(2,1)S(1)}, u32[]{:S(2)}, u32[]{:S(2)}) %collective-permute-start.47) | collective-permute-done | bytes 262176 | tf_op jit(solution)/shard_map/ppermute | solution.py:144
  331.4 2.9 collective-permute-done.43
  (220 shorter events, 61.6 us)
Async XLA Ops:
  1.7 10.2 %collective-permute-start.13 = (bf16[1024,128]{1,0:T(8,128)(2,1)S(1)}, bf16[1024,128]{1,0:T(8,128)(2,1)S(1)}, u32[]{:S(2)}, u32[]{:S(2)}) collective-permute-start(bf16[1024,128]{1,0:T(8,128)(2,1)S(1)} %dynamic-slice_bitcast_fusion.1), channel_id=1, source_target_pairs={{0,2},{2,0},{4,6},{6,4},{8,10},{10,8},{12,14},{14,12},{1,3},{3,1},... | collective-permute-start | bytes 786440 | tf_op jit(solution)/shard_map/ppermute | solution.py:144
  5.7 11.0 %collective-permute-start.1 = (bf16[1024,128]{1,0:T(8,128)(2,1)S(1)}, bf16[1024,128]{1,0:T(8,128)(2,1)S(1)}, u32[]{:S(2)}, u32[]{:S(2)}) collective-permute-start(bf16[1024,128]{1,0:T(8,128)(2,1)S(1)} %dynamic-slice_bitcast_fusion.3), channel_id=1, source_target_pairs={{0,2},{2,0},{4,6},{6,4},{8,10},{10,8},{12,14},{14,12},{1,3},{3,1},... | collective-permute-start | bytes 786440 | tf_op jit(solution)/shard_map/ppermute | solution.py:144
  13.8 17.3 %collective-permute-start.14 = (bf16[1024,256]{1,0:T(8,128)(2,1)}, bf16[1024,256]{1,0:T(8,128)(2,1)}, u32[]{:S(2)}, u32[]{:S(2)}) collective-permute-start(bf16[1024,256]{1,0:T(8,128)(2,1)} %pad_maximum_fusion.9), channel_id=1, source_target_pairs={{0,4},{2,6},{4,8},{6,10},{8,12},{10,14},{12,0},{14,2},{1,5},{3,7},... | collective-permute-start | bytes 1572872 | tf_op jit(solution)/shard_map/ppermute | solution.py:168
  17.6 24.7 %collective-permute-start.2 = (bf16[1024,256]{1,0:T(8,128)(2,1)}, bf16[1024,256]{1,0:T(8,128)(2,1)S(1)}, u32[]{:S(2)}, u32[]{:S(2)}) collective-permute-start(bf16[1024,256]{1,0:T(8,128)(2,1)} %pad_maximum_fusion.5), channel_id=1, source_target_pairs={{0,4},{2,6},{4,8},{6,10},{8,12},{10,14},{12,0},{14,2},{1,5},{3,7},... | collective-permute-start | bytes 1572872 | tf_op jit(solution)/shard_map/ppermute | solution.py:168
  20.5 10.9 %collective-permute-start = (bf16[128,1024]{1,0:T(8,128)(2,1)}, bf16[128,1024]{1,0:T(8,128)(2,1)}, u32[]{:S(2)}, u32[]{:S(2)}) collective-permute-start(bf16[128,1024]{1,0:T(8,128)(2,1)} %bitcast.2), channel_id=1, source_target_pairs={{0,2},{2,0},{4,6},{6,4},{8,10},{10,8},{12,14},{14,12},{1,3},{3,1},... | collective-permute-start | bytes 786440 | tf_op jit(solution)/shard_map/ppermute | solution.py:144
  22.5 19.7 %collective-permute-start.12 = (bf16[128,1024]{1,0:T(8,128)(2,1)S(1)}, bf16[128,1024]{1,0:T(8,128)(2,1)S(1)}, u32[]{:S(2)}, u32[]{:S(2)}) collective-permute-start(bf16[128,1024]{1,0:T(8,128)(2,1)S(1)} %bitcast.256), channel_id=1, source_target_pairs={{0,2},{2,0},{4,6},{6,4},{8,10},{10,8},{12,14},{14,12},{1,3},{3,1},... | collective-permute-start | bytes 786440 | tf_op jit(solution)/shard_map/ppermute | solution.py:144
  31.1 22.5 %collective-permute-start.15 = (bf16[1024,256]{1,0:T(8,128)(2,1)}, bf16[1024,256]{1,0:T(8,128)(2,1)}, u32[]{:S(2)}, u32[]{:S(2)}) collective-permute-start(bf16[1024,256]{1,0:T(8,128)(2,1)} %collective-permute-done.14), channel_id=1, source_target_pairs={{0,4},{2,6},{4,8},{6,10},{8,12},{10,14},{12,0},{14,2},{1,5},{3,7},... | collective-permute-start | bytes 1572872 | tf_op jit(solution)/shard_map/ppermute | solution.py:168
  42.2 22.6 %collective-permute-start.3 = (bf16[1024,256]{1,0:T(8,128)(2,1)S(1)}, bf16[1024,256]{1,0:T(8,128)(2,1)}, u32[]{:S(2)}, u32[]{:S(2)}) collective-permute-start(bf16[1024,256]{1,0:T(8,128)(2,1)S(1)} %collective-permute-done.2), channel_id=1, source_target_pairs={{0,4},{2,6},{4,8},{6,10},{8,12},{10,14},{12,0},{14,2},{1,5},{3,7},... | collective-permute-start | bytes 1572872 | tf_op jit(solution)/shard_map/ppermute | solution.py:168
  53.6 22.4 %collective-permute-start.16 = (bf16[1024,256]{1,0:T(8,128)(2,1)}, bf16[1024,256]{1,0:T(8,128)(2,1)S(1)}, u32[]{:S(2)}, u32[]{:S(2)}) collective-permute-start(bf16[1024,256]{1,0:T(8,128)(2,1)} %collective-permute-done.15), channel_id=1, source_target_pairs={{0,4},{2,6},{4,8},{6,10},{8,12},{10,14},{12,0},{14,2},{1,5},{3,7},... | collective-permute-start | bytes 1572872 | tf_op jit(solution)/shard_map/ppermute | solution.py:168
  64.8 19.5 %collective-permute-start.4 = (bf16[1024,256]{1,0:T(8,128)(2,1)}, bf16[1024,256]{1,0:T(8,128)(2,1)S(1)}, u32[]{:S(2)}, u32[]{:S(2)}) collective-permute-start(bf16[1024,256]{1,0:T(8,128)(2,1)} %collective-permute-done.3), channel_id=1, source_target_pairs={{0,4},{2,6},{4,8},{6,10},{8,12},{10,14},{12,0},{14,2},{1,5},{3,7},... | collective-permute-start | bytes 1572872 | tf_op jit(solution)/shard_map/ppermute | solution.py:168
  76.6 10.2 %collective-permute-start.17 = (bf16[2,64,1024]{2,1,0:T(8,128)(2,1)S(1)}, bf16[2,64,1024]{2,1,0:T(8,128)(2,1)S(1)}, u32[]{:S(2)}, u32[]{:S(2)}) collective-permute-start(bf16[2,64,1024]{2,1,0:T(8,128)(2,1)S(1)} %dynamic-slice_bitcast_fusion), channel_id=1, source_target_pairs={{0,1},{1,0},{2,3},{3,2},{4,5},{5,4},{6,7},{7,6},{8,9},{9,8},{10,11... | collective-permute-start | bytes 786440 | tf_op jit(solution)/shard_map/ppermute | solution.py:145
  86.7 1.7 collective-permute-start.5
  86.9 6.4 %collective-permute-start.18 = (bf16[64,1024]{1,0:T(8,128)(2,1)S(1)}, bf16[64,1024]{1,0:T(8,128)(2,1)S(1)}, u32[]{:S(2)}, u32[]{:S(2)}) collective-permute-start(bf16[64,1024]{1,0:T(8,128)(2,1)S(1)} %slice_bitcast_fusion.12), channel_id=1, source_target_pairs={{0,2},{2,0},{4,6},{6,4},{8,10},{10,8},{12,14},{14,12},{1,3},{3,1},... | collective-permute-start | bytes 393224 | tf_op jit(solution)/shard_map/ppermute | solution.py:144
  88.5 7.1 %collective-permute-start.6 = (bf16[64,1024]{1,0:T(8,128)(2,1)S(1)}, bf16[64,1024]{1,0:T(8,128)(2,1)S(1)}, u32[]{:S(2)}, u32[]{:S(2)}) collective-permute-start(bf16[64,1024]{1,0:T(8,128)(2,1)S(1)} %slice_bitcast_fusion.14), channel_id=1, source_target_pairs={{0,2},{2,0},{4,6},{6,4},{8,10},{10,8},{12,14},{14,12},{1,3},{3,1},... | collective-permute-start | bytes 393224 | tf_op jit(solution)/shard_map/ppermute | solution.py:144
  93.4 7.0 %collective-permute-start.19 = (bf16[64,1024]{1,0:T(8,128)(2,1)S(1)}, bf16[64,1024]{1,0:T(8,128)(2,1)S(1)}, u32[]{:S(2)}, u32[]{:S(2)}) collective-permute-start(bf16[64,1024]{1,0:T(8,128)(2,1)S(1)} %maximum_select_fusion.15), channel_id=1, source_target_pairs={{0,4},{2,6},{4,8},{6,10},{8,12},{10,14},{12,0},{14,2},{1,5},{3,7},... | collective-permute-start | bytes 393224 | tf_op jit(solution)/shard_map/ppermute | solution.py:168
  95.8 7.4 %collective-permute-start.7 = (bf16[64,1024]{1,0:T(8,128)(2,1)S(1)}, bf16[64,1024]{1,0:T(8,128)(2,1)S(1)}, u32[]{:S(2)}, u32[]{:S(2)}) collective-permute-start(bf16[64,1024]{1,0:T(8,128)(2,1)S(1)} %maximum_select_fusion.9), channel_id=1, source_target_pairs={{0,4},{2,6},{4,8},{6,10},{8,12},{10,14},{12,0},{14,2},{1,5},{3,7},... | collective-permute-start | bytes 393224 | tf_op jit(solution)/shard_map/ppermute | solution.py:168
  100.4 7.5 %collective-permute-start.20 = (bf16[64,1024]{1,0:T(8,128)(2,1)S(1)}, bf16[64,1024]{1,0:T(8,128)(2,1)S(1)}, u32[]{:S(2)}, u32[]{:S(2)}) collective-permute-start(bf16[64,1024]{1,0:T(8,128)(2,1)S(1)} %collective-permute-done.19), channel_id=1, source_target_pairs={{0,4},{2,6},{4,8},{6,10},{8,12},{10,14},{12,0},{14,2},{1,5},{3,7},... | collective-permute-start | bytes 393224 | tf_op jit(solution)/shard_map/ppermute | solution.py:168
  103.2 8.2 %collective-permute-start.8 = (bf16[64,1024]{1,0:T(8,128)(2,1)S(1)}, bf16[64,1024]{1,0:T(8,128)(2,1)S(1)}, u32[]{:S(2)}, u32[]{:S(2)}) collective-permute-start(bf16[64,1024]{1,0:T(8,128)(2,1)S(1)} %collective-permute-done.7), channel_id=1, source_target_pairs={{0,4},{2,6},{4,8},{6,10},{8,12},{10,14},{12,0},{14,2},{1,5},{3,7},... | collective-permute-start | bytes 393224 | tf_op jit(solution)/shard_map/ppermute | solution.py:168
  107.9 7.7 %collective-permute-start.21 = (bf16[64,1024]{1,0:T(8,128)(2,1)S(1)}, bf16[64,1024]{1,0:T(8,128)(2,1)S(1)}, u32[]{:S(2)}, u32[]{:S(2)}) collective-permute-start(bf16[64,1024]{1,0:T(8,128)(2,1)S(1)} %collective-permute-done.20), channel_id=1, source_target_pairs={{0,4},{2,6},{4,8},{6,10},{8,12},{10,14},{12,0},{14,2},{1,5},{3,7},... | collective-permute-start | bytes 393224 | tf_op jit(solution)/shard_map/ppermute | solution.py:168
  111.3 6.8 %collective-permute-start.9 = (bf16[64,1024]{1,0:T(8,128)(2,1)S(1)}, bf16[64,1024]{1,0:T(8,128)(2,1)S(1)}, u32[]{:S(2)}, u32[]{:S(2)}) collective-permute-start(bf16[64,1024]{1,0:T(8,128)(2,1)S(1)} %collective-permute-done.8), channel_id=1, source_target_pairs={{0,4},{2,6},{4,8},{6,10},{8,12},{10,14},{12,0},{14,2},{1,5},{3,7},... | collective-permute-start | bytes 393224 | tf_op jit(solution)/shard_map/ppermute | solution.py:168
  115.7 14.9 %collective-permute-start.22 = (bf16[4,64,1024]{2,1,0:T(8,128)(2,1)S(1)}, bf16[4,64,1024]{2,1,0:T(8,128)(2,1)S(1)}, u32[]{:S(2)}, u32[]{:S(2)}) collective-permute-start(bf16[4,64,1024]{2,1,0:T(8,128)(2,1)S(1)} %get-tuple-element.38), channel_id=1, source_target_pairs={{0,2},{2,0},{4,6},{6,4},{8,10},{10,8},{12,14},{14,12},{1,3},{3,1},... | collective-permute-start | bytes 1572872 | tf_op jit(solution)/shard_map/ppermute | solution.py:144
  118.2 18.5 %collective-permute-start.10 = (bf16[4,64,1024]{2,1,0:T(8,128)(2,1)S(1)}, bf16[4,64,1024]{2,1,0:T(8,128)(2,1)S(1)}, u32[]{:S(2)}, u32[]{:S(2)}) collective-permute-start(bf16[4,64,1024]{2,1,0:T(8,128)(2,1)S(1)} %get-tuple-element.42), channel_id=1, source_target_pairs={{0,2},{2,0},{4,6},{6,4},{8,10},{10,8},{12,14},{14,12},{1,3},{3,1},... | collective-permute-start | bytes 1572872 | tf_op jit(solution)/shard_map/ppermute | solution.py:144
  131.7 7.1 %collective-permute-start.23 = (bf16[2,4,64,1024]{3,2,1,0:T(8,128)(2,1)}, bf16[2,4,64,1024]{3,2,1,0:T(8,128)(2,1)}, u32[]{:S(2)}, u32[]{:S(2)}) collective-permute-start(bf16[2,4,64,1024]{3,2,1,0:T(8,128)(2,1)} %get-tuple-element.22), channel_id=1, source_target_pairs={{0,1},{1,0},{2,3},{3,2},{4,5},{5,4},{6,7},{7,6},{8,9},{9,8},{10,11... | collective-permute-start | bytes 3145736 | tf_op jit(solution)/shard_map/ppermute | solution.py:145
  137.8 3.0 collective-permute-start.11
  185.4 2.7 collective-permute-start.24
  185.7 4.4 %collective-permute-start.32 = (bf16[2,4,64,1024]{3,2,1,0:T(8,128)(2,1)S(1)}, bf16[2,4,64,1024]{3,2,1,0:T(8,128)(2,1)S(1)}, u32[]{:S(2)}, u32[]{:S(2)}) collective-permute-start(bf16[2,4,64,1024]{3,2,1,0:T(8,128)(2,1)S(1)} %bitcast.230), channel_id=1, source_target_pairs={{0,1},{1,0},{2,3},{3,2},{4,5},{5,4},{6,7},{7,6},{8,9},{9,8},{10,11... | collective-permute-start | bytes 3145736 | tf_op jit(solution)/shard_map/ppermute | solution.py:145
  188.5 14.8 %collective-permute-start.25 = (bf16[4,64,1024]{2,1,0:T(8,128)(2,1)S(1)}, bf16[4,64,1024]{2,1,0:T(8,128)(2,1)S(1)}, u32[]{:S(2)}, u32[]{:S(2)}) collective-permute-start(bf16[4,64,1024]{2,1,0:T(8,128)(2,1)S(1)} %slice_bitcast_fusion.2), channel_id=1, source_target_pairs={{0,2},{2,0},{4,6},{6,4},{8,10},{10,8},{12,14},{14,12},{1,3},{3,1},... | collective-permute-start | bytes 1572872 | tf_op jit(solution)/shard_map/ppermute | solution.py:144
  190.6 23.2 %collective-permute-start.33 = (bf16[4,64,1024]{2,1,0:T(8,128)(2,1)S(1)}, bf16[4,64,1024]{2,1,0:T(8,128)(2,1)S(1)}, u32[]{:S(2)}, u32[]{:S(2)}) collective-permute-start(bf16[4,64,1024]{2,1,0:T(8,128)(2,1)S(1)} %slice_bitcast_fusion), channel_id=1, source_target_pairs={{0,2},{2,0},{4,6},{6,4},{8,10},{10,8},{12,14},{14,12},{1,3},{3,1},... | collective-permute-start | bytes 1572872 | tf_op jit(solution)/shard_map/ppermute | solution.py:144
  203.6 11.1 %collective-permute-start.26 = (bf16[64,1024]{1,0:T(8,128)(2,1)S(1)}, bf16[64,1024]{1,0:T(8,128)(2,1)S(1)}, u32[]{:S(2)}, u32[]{:S(2)}) collective-permute-start(bf16[64,1024]{1,0:T(8,128)(2,1)S(1)} %slice_bitcast_fusion.11), channel_id=1, source_target_pairs={{4,0},{6,2},{8,4},{10,6},{12,8},{14,10},{0,12},{2,14},{5,1},{7,3},... | collective-permute-start | bytes 393224 | tf_op jit(solution)/shard_map/ppermute | solution.py:174
  214.0 6.4 %collective-permute-start.34 = (bf16[64,1024]{1,0:T(8,128)(2,1)S(1)}, bf16[64,1024]{1,0:T(8,128)(2,1)S(1)}, u32[]{:S(2)}, u32[]{:S(2)}) collective-permute-start(bf16[64,1024]{1,0:T(8,128)(2,1)S(1)} %slice_bitcast_fusion.7), channel_id=1, source_target_pairs={{4,0},{6,2},{8,4},{10,6},{12,8},{14,10},{0,12},{2,14},{5,1},{7,3},... | collective-permute-start | bytes 393224 | tf_op jit(solution)/shard_map/ppermute | solution.py:174
  214.7 8.5 %collective-permute-start.27 = (bf16[64,1024]{1,0:T(8,128)(2,1)S(1)}, bf16[64,1024]{1,0:T(8,128)(2,1)S(1)}, u32[]{:S(2)}, u32[]{:S(2)}) collective-permute-start(bf16[64,1024]{1,0:T(8,128)(2,1)S(1)} %fusion.21), channel_id=1, source_target_pairs={{4,0},{6,2},{8,4},{10,6},{12,8},{14,10},{0,12},{2,14},{5,1},{7,3},... | collective-permute-start | bytes 393224 | tf_op jit(solution)/shard_map/ppermute | solution.py:174
  220.5 5.3 %collective-permute-start.35 = (bf16[64,1024]{1,0:T(8,128)(2,1)S(1)}, bf16[64,1024]{1,0:T(8,128)(2,1)S(1)}, u32[]{:S(2)}, u32[]{:S(2)}) collective-permute-start(bf16[64,1024]{1,0:T(8,128)(2,1)S(1)} %fusion.18), channel_id=1, source_target_pairs={{4,0},{6,2},{8,4},{10,6},{12,8},{14,10},{0,12},{2,14},{5,1},{7,3},... | collective-permute-start | bytes 393224 | tf_op jit(solution)/shard_map/ppermute | solution.py:174
  223.3 6.7 %collective-permute-start.28 = (bf16[64,1024]{1,0:T(8,128)(2,1)S(1)}, bf16[64,1024]{1,0:T(8,128)(2,1)S(1)}, u32[]{:S(2)}, u32[]{:S(2)}) collective-permute-start(bf16[64,1024]{1,0:T(8,128)(2,1)S(1)} %fusion.20), channel_id=1, source_target_pairs={{4,0},{6,2},{8,4},{10,6},{12,8},{14,10},{0,12},{2,14},{5,1},{7,3},... | collective-permute-start | bytes 393224 | tf_op jit(solution)/shard_map/ppermute | solution.py:174
  225.9 6.6 %collective-permute-start.36 = (bf16[64,1024]{1,0:T(8,128)(2,1)S(1)}, bf16[64,1024]{1,0:T(8,128)(2,1)S(1)}, u32[]{:S(2)}, u32[]{:S(2)}) collective-permute-start(bf16[64,1024]{1,0:T(8,128)(2,1)S(1)} %fusion.17), channel_id=1, source_target_pairs={{4,0},{6,2},{8,4},{10,6},{12,8},{14,10},{0,12},{2,14},{5,1},{7,3},... | collective-permute-start | bytes 393224 | tf_op jit(solution)/shard_map/ppermute | solution.py:174
  230.1 5.0 %collective-permute-start.29 = (bf16[64,1024]{1,0:T(8,128)(2,1)S(1)}, bf16[64,1024]{1,0:T(8,128)(2,1)S(1)}, u32[]{:S(2)}, u32[]{:S(2)}) collective-permute-start(bf16[64,1024]{1,0:T(8,128)(2,1)S(1)} %maximum_select_fusion.21), channel_id=1, source_target_pairs={{0,2},{2,0},{4,6},{6,4},{8,10},{10,8},{12,14},{14,12},{1,3},{3,1},... | collective-permute-start | bytes 393224 | tf_op jit(solution)/shard_map/ppermute | solution.py:144
  235.2 6.2 %collective-permute-start.30 = (bf16[2,64,1024]{2,1,0:T(8,128)(2,1)S(1)}, bf16[2,64,1024]{2,1,0:T(8,128)(2,1)S(1)}, u32[]{:S(2)}, u32[]{:S(2)}) collective-permute-start(bf16[2,64,1024]{2,1,0:T(8,128)(2,1)S(1)} %get-tuple-element.48), channel_id=1, source_target_pairs={{0,1},{1,0},{2,3},{3,2},{4,5},{5,4},{6,7},{7,6},{8,9},{9,8},{10,11... | collective-permute-start | bytes 786440 | tf_op jit(solution)/shard_map/ppermute | solution.py:145
  235.3 6.0 %collective-permute-start.37 = (bf16[64,1024]{1,0:T(8,128)(2,1)S(1)}, bf16[64,1024]{1,0:T(8,128)(2,1)S(1)}, u32[]{:S(2)}, u32[]{:S(2)}) collective-permute-start(bf16[64,1024]{1,0:T(8,128)(2,1)S(1)} %maximum_select_fusion.27), channel_id=1, source_target_pairs={{0,2},{2,0},{4,6},{6,4},{8,10},{10,8},{12,14},{14,12},{1,3},{3,1},... | collective-permute-start | bytes 393224 | tf_op jit(solution)/shard_map/ppermute | solution.py:144
  241.3 7.8 %collective-permute-start.38 = (bf16[2,64,1024]{2,1,0:T(8,128)(2,1)S(1)}, bf16[2,64,1024]{2,1,0:T(8,128)(2,1)S(1)}, u32[]{:S(2)}, u32[]{:S(2)}) collective-permute-start(bf16[2,64,1024]{2,1,0:T(8,128)(2,1)S(1)} %get-tuple-element.46), channel_id=1, source_target_pairs={{0,1},{1,0},{2,3},{3,2},{4,5},{5,4},{6,7},{7,6},{8,9},{9,8},{10,11... | collective-permute-start | bytes 786440 | tf_op jit(solution)/shard_map/ppermute | solution.py:145
  245.1 76.8 %collective-permute-start.31 = (bf16[128,1024]{1,0:T(8,128)(2,1)S(1)}, bf16[128,1024]{1,0:T(8,128)(2,1)S(1)}, u32[]{:S(2)}, u32[]{:S(2)}) collective-permute-start(bf16[128,1024]{1,0:T(8,128)(2,1)S(1)} %get-tuple-element.36), channel_id=1, source_target_pairs={{0,2},{2,0},{4,6},{6,4},{8,10},{10,8},{12,14},{14,12},{1,3},{3,1},... | collective-permute-start | bytes 786440 | tf_op jit(solution)/shard_map/ppermute | solution.py:144
  247.0 14.8 %collective-permute-start.44 = (bf16[1024,256]{1,0:T(8,128)(2,1)S(1)}, bf16[1024,256]{1,0:T(8,128)(2,1)S(1)}, u32[]{:S(2)}, u32[]{:S(2)}) collective-permute-start(bf16[1024,256]{1,0:T(8,128)(2,1)S(1)} %convolution_convert_fusion.3), channel_id=1, source_target_pairs={{4,0},{6,2},{8,4},{10,6},{12,8},{14,10},{0,12},{2,14},{5,1},{7,3},... | collective-permute-start | bytes 1572872 | tf_op jit(solution)/shard_map/ppermute | solution.py:174
  250.6 22.4 %collective-permute-start.40 = (bf16[1024,256]{1,0:T(8,128)(2,1)S(1)}, bf16[1024,256]{1,0:T(8,128)(2,1)S(1)}, u32[]{:S(2)}, u32[]{:S(2)}) collective-permute-start(bf16[1024,256]{1,0:T(8,128)(2,1)S(1)} %convolution_convert_fusion.7), channel_id=1, source_target_pairs={{4,0},{6,2},{8,4},{10,6},{12,8},{14,10},{0,12},{2,14},{5,1},{7,3},... | collective-permute-start | bytes 1572872 | tf_op jit(solution)/shard_map/ppermute | solution.py:174
  262.2 22.1 %collective-permute-start.45 = (bf16[1024,256]{1,0:T(8,128)(2,1)S(1)}, bf16[1024,256]{1,0:T(8,128)(2,1)S(1)}, u32[]{:S(2)}, u32[]{:S(2)}) collective-permute-start(bf16[1024,256]{1,0:T(8,128)(2,1)S(1)} %add_convert_fusion.2), channel_id=1, source_target_pairs={{4,0},{6,2},{8,4},{10,6},{12,8},{14,10},{0,12},{2,14},{5,1},{7,3},... | collective-permute-start | bytes 1572872 | tf_op jit(solution)/shard_map/ppermute | solution.py:174
  274.4 21.2 %collective-permute-start.41 = (bf16[1024,256]{1,0:T(8,128)(2,1)S(1)}, bf16[1024,256]{1,0:T(8,128)(2,1)S(1)}, u32[]{:S(2)}, u32[]{:S(2)}) collective-permute-start(bf16[1024,256]{1,0:T(8,128)(2,1)S(1)} %add_convert_fusion.5), channel_id=1, source_target_pairs={{4,0},{6,2},{8,4},{10,6},{12,8},{14,10},{0,12},{2,14},{5,1},{7,3},... | collective-permute-start | bytes 1572872 | tf_op jit(solution)/shard_map/ppermute | solution.py:174
  284.7 22.1 %collective-permute-start.46 = (bf16[1024,256]{1,0:T(8,128)(2,1)S(1)}, bf16[1024,256]{1,0:T(8,128)(2,1)S(1)}, u32[]{:S(2)}, u32[]{:S(2)}) collective-permute-start(bf16[1024,256]{1,0:T(8,128)(2,1)S(1)} %add_convert_fusion.1), channel_id=1, source_target_pairs={{4,0},{6,2},{8,4},{10,6},{12,8},{14,10},{0,12},{2,14},{5,1},{7,3},... | collective-permute-start | bytes 1572872 | tf_op jit(solution)/shard_map/ppermute | solution.py:174
  296.9 20.4 %collective-permute-start.42 = (bf16[1024,256]{1,0:T(8,128)(2,1)S(1)}, bf16[1024,256]{1,0:T(8,128)(2,1)S(1)}, u32[]{:S(2)}, u32[]{:S(2)}) collective-permute-start(bf16[1024,256]{1,0:T(8,128)(2,1)S(1)} %add_convert_fusion.4), channel_id=1, source_target_pairs={{4,0},{6,2},{8,4},{10,6},{12,8},{14,10},{0,12},{2,14},{5,1},{7,3},... | collective-permute-start | bytes 1572872 | tf_op jit(solution)/shard_map/ppermute | solution.py:174
  301.2 23.0 %collective-permute-start.39 = (bf16[128,1024]{1,0:T(8,128)(2,1)S(1)}, bf16[128,1024]{1,0:T(8,128)(2,1)S(1)}, u32[]{:S(2)}, u32[]{:S(2)}) collective-permute-start(bf16[128,1024]{1,0:T(8,128)(2,1)S(1)} %get-tuple-element.34), channel_id=1, source_target_pairs={{0,2},{2,0},{4,6},{6,4},{8,10},{10,8},{12,14},{14,12},{1,3},{3,1},... | collective-permute-start | bytes 786440 | tf_op jit(solution)/shard_map/ppermute | solution.py:144
  321.1 9.3 %collective-permute-start.47 = (bf16[1024,128]{1,0:T(8,128)(2,1)S(1)}, bf16[1024,128]{1,0:T(8,128)(2,1)S(1)}, u32[]{:S(2)}, u32[]{:S(2)}) collective-permute-start(bf16[1024,128]{1,0:T(8,128)(2,1)S(1)} %bitcast.238), channel_id=1, source_target_pairs={{0,2},{2,0},{4,6},{6,4},{8,10},{10,8},{12,14},{14,12},{1,3},{3,1},... | collective-permute-start | bytes 786440 | tf_op jit(solution)/shard_map/ppermute | solution.py:144
  322.9 11.4 %collective-permute-start.43 = (bf16[1024,128]{1,0:T(8,128)(2,1)S(1)}, bf16[1024,128]{1,0:T(8,128)(2,1)S(1)}, u32[]{:S(2)}, u32[]{:S(2)}) collective-permute-start(bf16[1024,128]{1,0:T(8,128)(2,1)S(1)} %bitcast.239), channel_id=1, source_target_pairs={{0,2},{2,0},{4,6},{6,4},{8,10},{10,8},{12,14},{14,12},{1,3},{3,1},... | collective-permute-start | bytes 786440 | tf_op jit(solution)/shard_map/ppermute | solution.py:144
  (26 other events, 354.9 us)

commit v2 on v1

v2 whole, which is shorter than its diff:
```python
import jax
import jax.numpy as jnp
from jax import lax
from jax.experimental import pallas as pl
from jax.experimental.pallas import tpu as pltpu
from jax.sharding import PartitionSpec as P

gate_unit = 2.0 ** (-15)
bf16 = jnp.bfloat16
f32 = jnp.float32

NN = (((1,), (0,)), ((), ()))
NT = (((1,), (1,)), ((), ()))
TN = (((0,), (0,)), ((), ()))


def dot(a, b, dims=NN):
    return lax.dot_general(a, b, dims, preferred_element_type=f32)


def join_projections(wg_ref, wu_ref, wgu):
    pair, _, width = wg_ref.shape
    for j in range(pair):
        wgu[:, 2 * j * width : (2 * j + 1) * width] = wg_ref[j]
        wgu[:, (2 * j + 1) * width : (2 * j + 2) * width] = wu_ref[j]


def forward_kernel(
    x_ref, g_ref, wg_ref, wu_ref, wd_ref, hs_ref, cp_ref, cu_ref, lo_ref, wgu, lo_acc
):
    step = pl.program_id(0)
    pair, _, width = wg_ref.shape
    block = 256
    join_projections(wg_ref, wu_ref, wgu)

    @pl.when(step == 0)
    def _():
        lo_acc[...] = jnp.zeros_like(lo_acc)

    def row_block(i, _):
        rows = pl.ds(pl.multiple_of(i * block, block), block)
        x = x_ref[rows, :]
        for j in range(pair):
            cols = slice(j * width, (j + 1) * width)
            both = dot(x, wgu[:, 2 * j * width : (2 * j + 2) * width])
            gate_pre, up_pre = both[:, :width], both[:, width:]
            gate = g_ref[0, rows, j : j + 1]
            sig = jax.nn.sigmoid(gate_pre)
            act = gate_pre * sig * gate
            hs_ref[rows, cols] = (act * up_pre).astype(bf16)
            cu_ref[rows, cols] = act.astype(bf16)
            slope = up_pre * (sig * (1.0 + gate_pre * (1.0 - sig)))
            cp_ref[rows, cols] = (slope * gate).astype(bf16)
        lo_acc[rows, :] += dot(hs_ref[rows, :], wd_ref[...])
        return 0

    lax.fori_loop(0, x_ref.shape[0] // block, row_block, 0)

    @pl.when(step == pl.num_programs(0) - 1)
    def _():
        lo_ref[...] = lo_acc[...].astype(bf16)


def backward_kernel(
    y_ref, cp_ref, cu_ref, wg_ref, wu_ref, wd_ref, dpu_ref, lig_ref, wgu, lig_acc
):
    step = pl.program_id(0)
    pair, _, width = wg_ref.shape
    block = 256
    join_projections(wg_ref, wu_ref, wgu)

    @pl.when(step == 0)
    def _():
        lig_acc[...] = jnp.zeros_like(lig_acc)

    def row_block(i, _):
        rows = pl.ds(pl.multiple_of(i * block, block), block)
        hidden_grad = dot(y_ref[rows, :], wd_ref[...], NT)
        for j in range(pair):
            cols = slice(j * width, (j + 1) * width)
            hg = hidden_grad[:, cols]
            dp = hg * cp_ref[rows, cols].astype(f32)
            du = hg * cu_ref[rows, cols].astype(f32)
            dpu_ref[rows, 2 * j * width : (2 * j + 1) * width] = dp.astype(bf16)
            dpu_ref[rows, (2 * j + 1) * width : (2 * j + 2) * width] = du.astype(bf16)
        lig_acc[rows, :] += dot(dpu_ref[rows, :], wgu[...], NT)
        return 0

    lax.fori_loop(0, y_ref.shape[0] // block, row_block, 0)

    @pl.when(step == pl.num_programs(0) - 1)
    def _():
        lig_ref[...] = lig_acc[...].astype(bf16)


def down_grad_kernel(hs_ref, y_ref, dwd_ref):
    dwd_ref[...] = dot(hs_ref[...], y_ref[...], TN).astype(bf16)


def input_grad_kernel(x_ref, dpu_ref, dwg_ref, dwu_ref):
    pair, latent, width = dwg_ref.shape
    block = 256

    def col_block(i, _):
        cols = pl.ds(pl.multiple_of(i * block, block), block)
        grads = dot(x_ref[:, cols], dpu_ref[...], TN)
        for j in range(pair):
            dwg_ref[j, cols, :] = grads[:, 2 * j * width : (2 * j + 1) * width].astype(bf16)
            dwu_ref[j, cols, :] = grads[:, (2 * j + 1) * width : (2 * j + 2) * width].astype(bf16)
        return 0

    lax.fori_loop(0, latent // block, col_block, 0)


def shaped(*shape):
    return jax.ShapeDtypeStruct(shape, bf16)


def expert_calls(rows, latent, count, width):
    pair = 2 if rows <= 1024 and count % 2 == 0 else 1
    whole = pl.BlockSpec((rows, latent), lambda i: (0, 0))
    col_proj = pl.BlockSpec((pair, latent, width), lambda i: (i, 0, 0))
    row_proj = pl.BlockSpec((pair * width, latent), lambda i: (i, 0))
    hidden = pl.BlockSpec((rows, pair * width), lambda i: (0, i))
    hidden2 = pl.BlockSpec((rows, 2 * pair * width), lambda i: (0, i))
    gate_spec = pl.BlockSpec((1, rows, pair), lambda i: (i, 0, 0))
    joined = pltpu.VMEM((latent, 2 * pair * width), bf16)
    total = pltpu.VMEM((rows, latent), f32)
    units = 2 * rows * latent * width * count
    weight_bytes = 2 * latent * width * count
    hidden_bytes = 2 * rows * width * count
    latent_bytes = 2 * rows * latent

    def call(kernel, ins, outs, out_shape, scratch, parts, moved, exps=0):
        return pl.pallas_call(
            kernel,
            grid=(count // pair,),
            in_specs=ins,
            out_specs=outs,
            out_shape=out_shape,
            scratch_shapes=scratch,
            compiler_params=pltpu.CompilerParams(
                vmem_limit_bytes=(40 if rows <= 1024 else 56) * 1024 * 1024
            ),
            cost_estimate=pl.CostEstimate(
                flops=parts * units, bytes_accessed=moved, transcendentals=exps
            ),
        )

    hid = shaped(rows, count * width)
    lat = shaped(rows, latent)
    col = shaped(count, latent, width)
    forward = call(
        forward_kernel,
        [whole, gate_spec, col_proj, col_proj, row_proj],
        [hidden, hidden, hidden, whole],
        [hid, hid, hid, lat],
        [joined, total],
        3,
        3 * weight_bytes + 3 * hidden_bytes + 2 * latent_bytes,
        rows * width * count,
    )
    backward = call(
        backward_kernel,
        [whole, hidden, hidden, col_proj, col_proj, row_proj],
        [hidden2, whole],
        [shaped(rows, 2 * count * width), lat],
        [joined, total],
        3,
        3 * weight_bytes + 4 * hidden_bytes + 2 * latent_bytes,
    )
    down_grads = call(
        down_grad_kernel,
        [hidden, whole],
        row_proj,
        shaped(count * width, latent),
        [],
        1,
        weight_bytes + hidden_bytes + latent_bytes,
    )
    input_grads = call(
        input_grad_kernel,
        [whole, hidden2],
        [col_proj, col_proj],
        [col, col],
        [],
        2,
        2 * weight_bytes + 2 * hidden_bytes + latent_bytes,
    )

    def gate_blocks(gate_columns):
        return gate_columns.reshape(rows, count // pair, pair).transpose(1, 0, 2)

    return forward, backward, down_grads, input_grads, gate_blocks


def local(tokens, down_weight, up_weight, gate_proj, up_proj, down_proj, routes, gates, cotangent):
    n_expert = lax.axis_size("expert")
    n_group = lax.axis_size("group")
    own = lax.axis_index("expert")
    t = lax.axis_index("tensor")
    tok_rows = tokens.shape[0]
    half_rows = tok_rows // 2
    quarter_d = tokens.shape[1] // 4
    exp_local, latent, width = gate_proj.shape
    shard = down_weight.shape[1]

    nh = n_expert // 4
    h, c, y = own // 4, own // 2 % 2, own % 2
    shared = n_group % 2 == 0
    g = lax.axis_index("group") % 2

    def swapper(axis, size, bit):
        perm = [(i, i ^ bit) for i in range(size)]
        return lambda v: lax.ppermute(v, axis, perm)

    y_swap = swapper("expert", n_expert, 1)
    c_swap = swapper("expert", n_expert, 2)
    t_swap = swapper("tensor", 2, 1)
    g_swap = swapper("group", n_group, 1)
    h_up = [(e, (e + 4) % n_expert) for e in range(n_expert)]
    h_down = [((e + 4) % n_expert, e) for e in range(n_expert)]

    def add(a, b):
        return (a.astype(f32) + b.astype(f32)).astype(bf16)

    def turn(v, axis):
        blocks = jnp.split(v, nh, axis=axis)
        orders = [
            jnp.concatenate([blocks[(i - k) % nh] for k in range(nh)], axis=axis)
            for i in range(nh)
        ]
        result = orders[0]
        for i in range(1, nh):
            result = jnp.where(h == i, orders[i], result)
        return result

    def flip(v, index, axis):
        first, second = jnp.split(v, 2, axis=axis)
        return jnp.where(index == 0, v, jnp.concatenate([second, first], axis=axis))

    def pick(v, index, axis):
        mine = lax.dynamic_index_in_dim(v, index, axis, keepdims=False)
        other = lax.dynamic_index_in_dim(v, 1 - index, axis, keepdims=False)
        return mine, other

    def gather_h(v):
        parts = [v]
        for _ in range(nh - 1):
            parts.append(lax.ppermute(parts[-1], "expert", h_up))
        return parts

    def scatter_h(parts):
        total = parts[nh - 1]
        for k in range(nh - 2, -1, -1):
            total = add(lax.ppermute(total, "expert", h_down), parts[k])
        return total

    def square_rows(v):
        mine, other = pick(v.reshape(tok_rows, 2, 2 * quarter_d), c, 1)
        v = jnp.concatenate([mine, c_swap(other)], axis=0)
        mine, other = pick(v.reshape(2 * tok_rows, 2, quarter_d), y, 1)
        received = y_swap(other)
        parts = [mine[:tok_rows], received[:tok_rows], mine[tok_rows:], received[tok_rows:]]
        return jnp.concatenate(parts, axis=0)

    def square_weight(v):
        mine, other = pick(v.reshape(2, 2, quarter_d, shard), y, 1)
        v = flip(jnp.concatenate([mine, y_swap(other)], axis=2), y, 2)
        mine, other = pick(v, c, 0)
        block = flip(jnp.concatenate([mine, c_swap(other)], axis=1), c, 1)
        if not shared:
            return gather_h(block)
        mine, _ = pick(block.reshape(2, quarter_d // 2, 4 * shard), g, 0)
        parts = [block]
        for _ in range(nh - 1):
            mine = lax.ppermute(mine, "expert", h_up)
            parts.append(flip(jnp.concatenate([mine, g_swap(mine)], axis=0), g, 0))
        return parts

    def project(rows, weights):
        part = jnp.concatenate([dot(rows, w).astype(bf16) for w in weights], axis=1)
        mine, other = pick(part.reshape(2, 2, 2, half_rows, latent), t, 2)
        part = add(mine, t_swap(other))
        part = add(part[0], c_swap(part[1]))
        part = add(part[0], y_swap(part[1]))
        return turn(part, 1)

    def gather_first(part):
        part = jnp.stack(gather_h(part))
        part = jnp.stack([part, c_swap(part)])
        part = jnp.stack([part, y_swap(part)])
        part = jnp.stack([part, t_swap(part)])
        return part.reshape(-1, latent)

    def gather_second(part):
        part = jnp.stack([part, y_swap(part)])
        part = jnp.stack(gather_h(part), axis=1)
        part = jnp.stack([part, c_swap(part)], axis=1)
        part = jnp.stack([part, t_swap(part)])
        return part.reshape(-1, latent)

    def collect(part):
        part = part.reshape(2, 2, 2, nh, half_rows, latent)
        part = add(part[0], t_swap(part[1]))
        part = add(part[0], y_swap(part[1]))
        part = add(part[0], c_swap(part[1]))
        part = turn(scatter_h([part[k] for k in range(nh)]), 1)
        part = jnp.stack([part, y_swap(part)])
        part = jnp.stack([part, c_swap(part)])
        part = flip(jnp.stack([part, t_swap(part)], axis=2), t, 2)
        return part.reshape(4 * tok_rows, latent)

    def finish(part, rows, weights):
        cols = latent // nh
        grads = [dot(rows, part[:, k * cols : (k + 1) * cols], TN).astype(bf16) for k in range(nh)]
        grad = scatter_h(grads)
        mine, other = pick(grad.reshape(quarter_d, 2, 2 * shard), c, 1)
        grad = jnp.stack([mine, c_swap(other)])
        mine, other = pick(grad.reshape(2, quarter_d, 2, shard), y, 2)
        grad = jnp.stack([mine, y_swap(other)], axis=1)
        grad = flip(flip(grad, c, 0), y, 1).reshape(4 * quarter_d, shard).astype(f32)

        whole = sum(dot(part[:, k * cols : (k + 1) * cols], weights[k], NT) for k in range(nh))
        whole = whole.astype(bf16)
        theirs = c_swap(whole[2 * tok_rows :])
        pieces = [whole[:tok_rows], theirs[:tok_rows]]
        sent = jnp.concatenate([whole[tok_rows : 2 * tok_rows], theirs[tok_rows:]], axis=1)
        received = y_swap(sent)
        result = [
            flip(jnp.concatenate([p, r], axis=1), y, 1)
            for p, r in zip(pieces, jnp.split(received, 2, axis=1))
        ]
        return flip(jnp.concatenate(result, axis=1), c, 1), grad

    local_ids = own * exp_local + jnp.arange(exp_local, dtype=jnp.int32)
    hit = routes[:, :, None] == local_ids[None, None, :]
    gate_all = jnp.sum(jnp.where(hit, gates[:, :, None], 0), axis=1).astype(f32) * gate_unit
    gate_all = turn(gate_all.reshape(nh, 2, 2, 2, half_rows, exp_local), 0)
    gate_all = flip(flip(flip(gate_all, c, 1), y, 2), t, 3)
    gate_columns = gate_all.transpose(3, 2, 1, 0, 4, 5).reshape(-1, exp_local)

    group_rows = n_expert * tok_rows
    forward, backward, down_grads, input_grads, gate_blocks = expert_calls(
        group_rows, latent, exp_local, width
    )
    down_rows = down_proj.reshape(exp_local * width, latent)

    down_parts = square_weight(down_weight)
    up_parts = square_weight(up_weight)
    token_rows = square_rows(tokens)
    cot_rows = square_rows(cotangent)
    latent_in = gather_first(project(token_rows, down_parts))
    latent_grad = gather_second(project(cot_rows, up_parts))

    hs, cp, cu, out_part = forward(
        latent_in, gate_blocks(gate_columns), gate_proj, up_proj, down_rows
    )
    dpu, in_part = backward(latent_grad, cp, cu, gate_proj, up_proj, down_rows)
    down_proj_grad = down_grads(hs, latent_grad).reshape(down_proj.shape)
    gate_proj_grad, up_proj_grad = input_grads(latent_in, dpu)

    out, up_grad = finish(collect(out_part), cot_rows, up_parts)
    tokens_grad, down_grad = finish(collect(in_part), token_rows, down_parts)
    return (out, tokens_grad, gate_proj_grad, up_proj_grad, down_proj_grad, down_grad, up_grad)


def solution(mesh):
    in_specs = (
        P(("group", "expert"), "tensor"),
        P("tensor", "expert"),
        P("tensor", "expert"),
        P("expert", None, "tensor"),
        P("expert", None, "tensor"),
        P("expert", "tensor", None),
        P("group", None),
        P("group", None),
        P(("group", "expert"), "tensor"),
    )
    out_specs = (
        P(("group", "expert"), "tensor"),
        P(("group", "expert"), "tensor"),
        P(("group", "expert"), None, "tensor"),
        P(("group", "expert"), None, "tensor"),
        P(("group", "expert"), "tensor", None),
        P(("group", "tensor"), "expert"),
        P(("group", "tensor"), "expert"),
    )
    return jax.shard_map(local, mesh=mesh, in_specs=in_specs, out_specs=out_specs, check_vma=False)
```

time: 336 us -> 309 us (0.920)
  waiting for transfers between devices: 192 us -> 158 us
  local copies, waits for them, and re-layouts: 10 us -> 28.4 us
  matrix products: 22.1 us -> 11.9 us
  starting transfers between devices: 52.5 us -> 45 us
  Pallas kernels: 42.2 us -> 48.8 us
    ppermute x48 -> x50, waiting for transfers between devices: 192 us -> 158 us  [the longest x42 105 us: swapper(): return lambda v: lax.ppermute(v, axis, perm)]
    dot_general x24 -> x12, matrix products: 22.1 us -> 11.9 us  [dot(): return lax.dot_general(a, b, dims, preferred_element_type=f32)]
    unnamed x58 -> x90, local copies, waits for them, and re-layouts: 2.24 us -> 12.1 us
    ppermute x48 -> x50, starting transfers between devices: 52.5 us -> 45 us  [the longest x42 35.7 us: swapper(): return lambda v: lax.ppermute(v, axis, perm)]
    pallas_call x1 -> x4, Pallas kernels: 42.2 us -> 48.8 us  [the longest x1 16.9 us: local(): forward(latent_in, gate_blocks(gate_columns), gate_proj, up_proj, down_rows)]
  transfers between devices with their start and end apart: 48 -> 50, of which waited for: 36 -> 30; matrix products, arithmetic and copies ran while one was open for 12% -> 14% of each run, Pallas kernels for 0% -> 10%
where the time goes in v2:
time: 309 us; the launch traced here: 308 us
  waiting for transfers between devices  158 us (51%)
  Pallas kernels  48.8 us (16%)
  starting transfers between devices  45 us (15%)
  local copies, waits for them, and re-layouts  28.4 us (9%)
  other arithmetic  14.2 us (5%)
  matrix products  11.9 us (4%)
    ppermute x42, waiting for transfers between devices, swapper(): return lambda v: lax.ppermute(v, axis, perm)  105 us
    ppermute x42, starting transfers between devices, swapper(): return lambda v: lax.ppermute(v, axis, perm)  35.7 us
    ppermute x4, waiting for transfers between devices, scatter_h(): total = add(lax.ppermute(total, 'expert', h_down), parts[k])  25.4 us
    pallas_call x1, Pallas kernels, local(): forward(latent_in, gate_blocks(gate_columns), gate_proj, up_proj, down_rows)  16.9 us
    pallas_call x1, Pallas kernels, local(): dpu, in_part = backward(latent_grad, cp, cu, gate_proj, up_proj, down_rows)  16.6 us
    ppermute x2, waiting for transfers between devices, gather_h(): parts.append(lax.ppermute(parts[-1], 'expert', h_up))  14.1 us
    ppermute x2, waiting for transfers between devices, square_weight(): mine = lax.ppermute(mine, 'expert', h_up)  13.6 us
    unnamed x90, local copies, waits for them, and re-layouts  12.1 us
  transfers between devices with their start and end apart: 50, of which 30 were waited for; matrix products, arithmetic and copies ran while one was open for 14% of the time, Pallas kernels for 10%

profile of v2, /device:TPU:0, one launch (start us, length us, event | category | flops | bytes accessed | tf_op | source)
XLA Modules:
  0.0 308.2 jit_solution(11408056265275889887)
XLA Ops:
  3.0 3.0 collective-permute-start
  6.7 2.0 collective-permute-start.20
  8.9 4.6 %collective-permute-done = bf16[128,1024]{1,0:T(8,128)(2,1)} collective-permute-done((bf16[128,1024]{1,0:T(8,128)(2,1)}, bf16[128,1024]{1,0:T(8,128)(2,1)}, u32[]{:S(2)}, u32[]{:S(2)}) %collective-permute-start) | collective-permute-done | bytes 262176 | tf_op jit(solution)/shard_map/ppermute | solution.py:215
  14.7 2.1 collective-permute-start.1
  18.4 1.8 collective-permute-start.27
  21.4 1.6 collective-permute-start.21
  24.5 9.0 %collective-permute-done.21 = bf16[512,256]{1,0:T(8,128)(2,1)S(1)} collective-permute-done((bf16[512,256]{1,0:T(8,128)(2,1)S(1)}, bf16[512,256]{1,0:T(8,128)(2,1)S(1)}, u32[]{:S(2)}, u32[]{:S(2)}) %collective-permute-start.21) | collective-permute-done | bytes 262176 | tf_op jit(solution)/shard_map/ppermute | solution.py:215
  34.3 2.5 collective-permute-done.3
  36.9 2.2 collective-permute-start.4
  39.1 13.6 %collective-permute-done.22 = bf16[256,512]{1,0:T(8,128)(2,1)S(1)} collective-permute-done((bf16[256,512]{1,0:T(8,128)(2,1)S(1)}, bf16[256,512]{1,0:T(8,128)(2,1)S(1)}, u32[]{:S(2)}, u32[]{:S(2)}) %collective-permute-start.22) | collective-permute-done | bytes 262176 | tf_op jit(solution)/shard_map/ppermute | solution.py:277
  54.7 1.7 fusion.88
  57.1 4.3 %collective-permute-done.23 = bf16[256,512]{1,0:T(8,128)(2,1)S(1)} collective-permute-done((bf16[256,512]{1,0:T(8,128)(2,1)S(1)}, bf16[256,512]{1,0:T(8,128)(2,1)S(1)}, u32[]{:S(2)}, u32[]{:S(2)}) %collective-permute-start.23) | collective-permute-done | bytes 262176 | tf_op jit(solution)/shard_map/ppermute | solution.py:215
  64.4 1.7 convolution_convert_fusion.6
  69.1 1.9 collective-permute-start.7
  70.9 6.8 %collective-permute-done.29 = bf16[2,64,1024]{2,1,0:T(8,128)(2,1)S(1)} collective-permute-done((bf16[2,64,1024]{2,1,0:T(8,128)(2,1)S(1)}, bf16[2,64,1024]{2,1,0:T(8,128)(2,1)S(1)}, u32[]{:S(2)}, u32[]{:S(2)}) %collective-permute-start.29) | collective-permute-done | bytes 262176 | tf_op jit(solution)/shard_map/ppermute | solution.py:215
  78.6 3.9 %collective-permute-done.7 = bf16[2,64,1024]{2,1,0:T(8,128)(2,1)S(1)} collective-permute-done((bf16[2,64,1024]{2,1,0:T(8,128)(2,1)S(1)}, bf16[2,64,1024]{2,1,0:T(8,128)(2,1)S(1)}, u32[]{:S(2)}, u32[]{:S(2)}) %collective-permute-start.7) | collective-permute-done | bytes 262176 | tf_op jit(solution)/shard_map/ppermute | solution.py:215
  84.9 3.8 %collective-permute-done.8 = bf16[64,1024]{1,0:T(8,128)(2,1)S(1)} collective-permute-done((bf16[64,1024]{1,0:T(8,128)(2,1)S(1)}, bf16[64,1024]{1,0:T(8,128)(2,1)S(1)}, u32[]{:S(2)}, u32[]{:S(2)}) %collective-permute-start.8) | collective-permute-done | bytes 131104 | tf_op jit(solution)/shard_map/ppermute | solution.py:215
  90.1 1.8 collective-permute-start.32
  91.9 10.4 %collective-permute-done.9 = bf16[64,1024]{1,0:T(8,128)(2,1)S(1)} collective-permute-done((bf16[64,1024]{1,0:T(8,128)(2,1)S(1)}, bf16[64,1024]{1,0:T(8,128)(2,1)S(1)}, u32[]{:S(2)}, u32[]{:S(2)}) %collective-permute-start.9) | collective-permute-done | bytes 131104 | tf_op jit(solution)/shard_map/ppermute | solution.py:250
  102.6 3.6 %collective-permute-done.32 = bf16[2,64,1024]{2,1,0:T(8,128)(2,1)S(1)} collective-permute-done((bf16[2,64,1024]{2,1,0:T(8,128)(2,1)S(1)}, bf16[2,64,1024]{2,1,0:T(8,128)(2,1)S(1)}, u32[]{:S(2)}, u32[]{:S(2)}) %collective-permute-start.32) | collective-permute-done | bytes 262176 | tf_op jit(solution)/shard_map/ppermute | solution.py:250
  106.4 4.3 %collective-permute-done.10 = bf16[2,64,1024]{2,1,0:T(8,128)(2,1)S(1)} collective-permute-done((bf16[2,64,1024]{2,1,0:T(8,128)(2,1)S(1)}, bf16[2,64,1024]{2,1,0:T(8,128)(2,1)S(1)}, u32[]{:S(2)}, u32[]{:S(2)}) %collective-permute-start.10) | collective-permute-done | bytes 262176 | tf_op jit(solution)/shard_map/ppermute | solution.py:215
  111.6 8.6 %collective-permute-done.33 = bf16[2,2,64,1024]{3,2,0,1:T(8,128)(2,1)S(1)} collective-permute-done((bf16[2,2,64,1024]{3,2,0,1:T(8,128)(2,1)S(1)}, bf16[2,2,64,1024]{3,2,0,1:T(8,128)(2,1)S(1)}, u32[]{:S(2)}, u32[]{:S(2)}) %collective-permute-start.33) | collective-permute-done | bytes 524320 | tf_op jit(solution)/shard_map/ppermute | solution.py:215
  121.3 2.1 fusion.76
  128.1 16.9 %shard_map.144 = (bf16[1024,1536]{1,0:T(8,128)(2,1)S(1)}, bf16[1024,1536]{1,0:T(8,128)(2,1)S(1)}, bf16[1024,1536]{1,0:T(8,128)(2,1)}, bf16[1024,1024]{1,0:T(8,128)(2,1)S(1)}) custom-call(bf16[1024,1024]{1,0:T(8,128)(2,1)S(1)} %bitcast.207, f32[2,1024,2]{2,1,0:T(8,128)S(1)} %bitcast.209, bf16[4,1024,384]{2,1,0:T(8,128)(2,1)} %wg_ref.3, ...), custom_call_target="tpu_custom_call" | custom-call | flops 9663676416 | bytes 23068672 | tf_op jit(solution)/shard_map/pallas_call | solution.py:356
  144.9 1.7 copy-done.1
  148.5 1.9 copy-done.3
  150.4 16.6 %shard_map.145 = (bf16[1024,3072]{1,0:T(8,128)(2,1)}, bf16[1024,1024]{1,0:T(8,128)(2,1)S(1)}) custom-call(bf16[1024,1024]{1,0:T(8,128)(2,1)S(1)} %bitcast.205, bf16[1024,1536]{1,0:T(8,128)(2,1)S(1)} %get-tuple-element.16.cp_ref, bf16[1024,1536]{1,0:T(8,128)(2,1)S(1)} %copy-done.3, bf16[4,1024,384]{2,1,0:T(8,128)(2,1)S(1)} %copy-done, ...), custom_call_target="tpu_custom_call" | custom-call | flops 9663676416 | bytes 26214400 | tf_op jit(solution)/shard_map/pallas_call | solution.py:359
  171.1 11.8 %collective-permute-done.14 = bf16[2,2,64,1024]{3,2,1,0:T(8,128)(2,1)S(1)} collective-permute-done((bf16[2,2,64,1024]{3,2,1,0:T(8,128)(2,1)S(1)}, bf16[2,2,64,1024]{3,2,1,0:T(8,128)(2,1)S(1)}, u32[]{:S(2)}, u32[]{:S(2)}) %collective-permute-start.14) | collective-permute-done | bytes 524320 | tf_op jit(solution)/shard_map/ppermute | solution.py:215
  183.2 10.1 %collective-permute-done.36 = bf16[2,2,64,1024]{3,2,1,0:T(8,128)(2,1)S(1)} collective-permute-done((bf16[2,2,64,1024]{3,2,1,0:T(8,128)(2,1)S(1)}, bf16[2,2,64,1024]{3,2,1,0:T(8,128)(2,1)S(1)}, u32[]{:S(2)}, u32[]{:S(2)}) %collective-permute-start.36) | collective-permute-done | bytes 524320 | tf_op jit(solution)/shard_map/ppermute | solution.py:215
  193.8 2.1 collective-permute-start.16
  195.9 8.1 %collective-permute-done.37 = bf16[2,64,1024]{2,1,0:T(8,128)(2,1)S(1)} collective-permute-done((bf16[2,64,1024]{2,1,0:T(8,128)(2,1)S(1)}, bf16[2,64,1024]{2,1,0:T(8,128)(2,1)S(1)}, u32[]{:S(2)}, u32[]{:S(2)}) %collective-permute-start.37) | collective-permute-done | bytes 262176 | tf_op jit(solution)/shard_map/ppermute | solution.py:215
  205.0 6.1 %collective-permute-done.38 = bf16[64,1024]{1,0:T(8,128)(2,1)S(1)} collective-permute-done((bf16[64,1024]{1,0:T(8,128)(2,1)S(1)}, bf16[64,1024]{1,0:T(8,128)(2,1)S(1)}, u32[]{:S(2)}, u32[]{:S(2)}) %collective-permute-start.38) | collective-permute-done | bytes 131104 | tf_op jit(solution)/shard_map/ppermute | solution.py:256
  212.1 10.3 %shard_map.146 = (bf16[4,1024,384]{2,1,0:T(8,128)(2,1)}, bf16[4,1024,384]{2,1,0:T(8,128)(2,1)}) custom-call(bf16[1024,1024]{1,0:T(8,128)(2,1)S(1)} %bitcast.208, bf16[1024,3072]{1,0:T(8,128)(2,1)S(1)} %bitcast.211), custom_call_target="tpu_custom_call" | custom-call | flops 6442450944 | bytes 14680064 | tf_op jit(solution)/shard_map/pallas_call | solution.py:361
  222.6 2.0 collective-permute-start.40
  224.7 5.0 %shard_map.147 = bf16[1536,1024]{1,0:T(8,128)(2,1)} custom-call(bf16[1024,1536]{1,0:T(8,128)(2,1)S(1)} %copy-done.2, bf16[1024,1024]{1,0:T(8,128)(2,1)S(1)} %bitcast.206), custom_call_target="tpu_custom_call" | custom-call | flops 3221225472 | bytes 8388608 | tf_op jit(solution)/shard_map/pallas_call | solution.py:360
  229.7 1.9 collective-permute-done.40
  233.9 1.8 collective-permute-start.24
  240.9 1.7 fusion.5
  242.6 1.6 collective-permute-start.42
  245.0 1.8 collective-permute-done.24
  246.8 1.5 collective-permute-start.25
  248.3 10.9 %collective-permute-done.42 = bf16[256,512]{0,1:T(8,128)(2,1)S(1)} collective-permute-done((bf16[256,512]{0,1:T(8,128)(2,1)S(1)}, bf16[256,512]{0,1:T(8,128)(2,1)S(1)}, u32[]{:S(2)}, u32[]{:S(2)}) %collective-permute-start.42) | collective-permute-done | bytes 262176 | tf_op jit(solution)/shard_map/ppermute | solution.py:215
  262.7 12.8 %collective-permute-done.47 = bf16[512,512]{1,0:T(8,128)(2,1)} collective-permute-done((bf16[512,512]{1,0:T(8,128)(2,1)}, bf16[512,512]{1,0:T(8,128)(2,1)}, u32[]{:S(2)}, u32[]{:S(2)}) %collective-permute-start.47) | collective-permute-done | bytes 524320 | tf_op jit(solution)/shard_map/ppermute | solution.py:256
  275.4 1.7 add_convert_fusion
  279.5 6.5 %collective-permute-done.44 = bf16[512,512]{1,0:T(8,128)(2,1)} collective-permute-done((bf16[512,512]{1,0:T(8,128)(2,1)}, bf16[512,512]{1,0:T(8,128)(2,1)}, u32[]{:S(2)}, u32[]{:S(2)}) %collective-permute-start.44) | collective-permute-done | bytes 524320 | tf_op jit(solution)/shard_map/ppermute | solution.py:256
  290.1 1.6 collective-permute-done.48
  299.1 3.1 %collective-permute-done.49 = bf16[2,512,128]{2,1,0:T(8,128)(2,1)S(1)} collective-permute-done((bf16[2,512,128]{2,1,0:T(8,128)(2,1)S(1)}, bf16[2,512,128]{2,1,0:T(8,128)(2,1)S(1)}, u32[]{:S(2)}, u32[]{:S(2)}) %collective-permute-start.49) | collective-permute-done | bytes 262176 | tf_op jit(solution)/shard_map/ppermute | solution.py:215
  303.6 3.2 %collective-permute-done.46 = bf16[2,512,128]{2,1,0:T(8,128)(2,1)S(1)} collective-permute-done((bf16[2,512,128]{2,1,0:T(8,128)(2,1)S(1)}, bf16[2,512,128]{2,1,0:T(8,128)(2,1)S(1)}, u32[]{:S(2)}, u32[]{:S(2)}) %collective-permute-start.46) | collective-permute-done | bytes 262176 | tf_op jit(solution)/shard_map/ppermute | solution.py:215
  (288 shorter events, 65.8 us)
Async XLA Ops:
  3.0 10.5 %collective-permute-start = (bf16[128,1024]{1,0:T(8,128)(2,1)}, bf16[128,1024]{1,0:T(8,128)(2,1)}, u32[]{:S(2)}, u32[]{:S(2)}) collective-permute-start(bf16[128,1024]{1,0:T(8,128)(2,1)} %bitcast.2), channel_id=1, source_target_pairs={{0,4},{2,6},{4,0},{6,2},{8,12},{10,14},{12,8},{14,10},{1,5},{3,7},... | collective-permute-start | bytes 786440 | tf_op jit(solution)/shard_map/ppermute | solution.py:215
  6.5 11.6 %collective-permute-start.26 = (bf16[128,1024]{1,0:T(8,128)(2,1)S(1)}, bf16[128,1024]{1,0:T(8,128)(2,1)S(1)}, u32[]{:S(2)}, u32[]{:S(2)}) collective-permute-start(bf16[128,1024]{1,0:T(8,128)(2,1)S(1)} %bitcast.271), channel_id=1, source_target_pairs={{0,4},{2,6},{4,0},{6,2},{8,12},{10,14},{12,8},{14,10},{1,5},{3,7},... | collective-permute-start | bytes 786440 | tf_op jit(solution)/shard_map/ppermute | solution.py:215
  6.7 13.5 %collective-permute-start.20 = (bf16[2,512,128]{2,1,0:T(8,128)(2,1)S(1)}, bf16[2,512,128]{2,1,0:T(8,128)(2,1)}, u32[]{:S(2)}, u32[]{:S(2)}) collective-permute-start(bf16[2,512,128]{2,1,0:T(8,128)(2,1)S(1)} %get-tuple-element.97), channel_id=1, source_target_pairs={{0,2},{2,0},{4,6},{6,4},{8,10},{10,8},{12,14},{14,12},{1,3},{3,1},... | collective-permute-start | bytes 786440 | tf_op jit(solution)/shard_map/ppermute | solution.py:215
  8.7 15.0 %collective-permute-start.2 = (bf16[2,512,128]{2,1,0:T(8,128)(2,1)S(1)}, bf16[2,512,128]{2,1,0:T(8,128)(2,1)S(1)}, u32[]{:S(2)}, u32[]{:S(2)}) collective-permute-start(bf16[2,512,128]{2,1,0:T(8,128)(2,1)S(1)} %get-tuple-element.109), channel_id=1, source_target_pairs={{0,2},{2,0},{4,6},{6,4},{8,10},{10,8},{12,14},{14,12},{1,3},{3,1},... | collective-permute-start | bytes 786440 | tf_op jit(solution)/shard_map/ppermute | solution.py:215
  14.7 40.1 %collective-permute-start.1 = (bf16[256,512]{0,1:T(8,128)(2,1)S(1)}, bf16[256,512]{0,1:T(8,128)(2,1)}, u32[]{:S(2)}, u32[]{:S(2)}) collective-permute-start(bf16[256,512]{0,1:T(8,128)(2,1)S(1)} %get-tuple-element.103), channel_id=1, source_target_pairs={{0,2},{2,0},{4,6},{6,4},{8,10},{10,8},{12,14},{14,12},{1,3},{3,1},... | collective-permute-start | bytes 786440 | tf_op jit(solution)/shard_map/ppermute | solution.py:215
  18.4 20.7 %collective-permute-start.27 = (bf16[256,512]{0,1:T(8,128)(2,1)S(1)}, bf16[256,512]{0,1:T(8,128)(2,1)S(1)}, u32[]{:S(2)}, u32[]{:S(2)}) collective-permute-start(bf16[256,512]{0,1:T(8,128)(2,1)S(1)} %get-tuple-element.89), channel_id=1, source_target_pairs={{0,2},{2,0},{4,6},{6,4},{8,10},{10,8},{12,14},{14,12},{1,3},{3,1},... | collective-permute-start | bytes 786440 | tf_op jit(solution)/shard_map/ppermute | solution.py:215
  21.4 12.1 %collective-permute-start.21 = (bf16[512,256]{1,0:T(8,128)(2,1)S(1)}, bf16[512,256]{1,0:T(8,128)(2,1)S(1)}, u32[]{:S(2)}, u32[]{:S(2)}) collective-permute-start(bf16[512,256]{1,0:T(8,128)(2,1)S(1)} %get-tuple-element.95), channel_id=1, source_target_pairs={{0,4},{2,6},{4,0},{6,2},{8,12},{10,14},{12,8},{14,10},{1,5},{3,7},... | collective-permute-start | bytes 786440 | tf_op jit(solution)/shard_map/ppermute | solution.py:215
  23.9 12.8 %collective-permute-start.3 = (bf16[512,256]{1,0:T(8,128)(2,1)S(1)}, bf16[512,256]{1,0:T(8,128)(2,1)S(1)}, u32[]{:S(2)}, u32[]{:S(2)}) collective-permute-start(bf16[512,256]{1,0:T(8,128)(2,1)S(1)} %get-tuple-element.107), channel_id=1, source_target_pairs={{0,4},{2,6},{4,0},{6,2},{8,12},{10,14},{12,8},{14,10},{1,5},{3,7},... | collective-permute-start | bytes 786440 | tf_op jit(solution)/shard_map/ppermute | solution.py:215
  33.6 19.1 %collective-permute-start.22 = (bf16[256,512]{1,0:T(8,128)(2,1)S(1)}, bf16[256,512]{1,0:T(8,128)(2,1)S(1)}, u32[]{:S(2)}, u32[]{:S(2)}) collective-permute-start(bf16[256,512]{1,0:T(8,128)(2,1)S(1)} %fusion.34), channel_id=1, source_target_pairs={{0,8},{2,10},{4,12},{6,14},{8,0},{10,2},{12,4},{14,6},{1,9},{3,11}... | collective-permute-start | bytes 786440 | tf_op jit(solution)/shard_map/ppermute | solution.py:277
  36.9 19.5 %collective-permute-start.4 = (bf16[256,512]{1,0:T(8,128)(2,1)S(1)}, bf16[256,512]{1,0:T(8,128)(2,1)}, u32[]{:S(2)}, u32[]{:S(2)}) collective-permute-start(bf16[256,512]{1,0:T(8,128)(2,1)S(1)} %fusion.38), channel_id=1, source_target_pairs={{0,8},{2,10},{4,12},{6,14},{8,0},{10,2},{12,4},{14,6},{1,9},{3,11}... | collective-permute-start | bytes 786440 | tf_op jit(solution)/shard_map/ppermute | solution.py:277
  52.7 8.7 %collective-permute-start.23 = (bf16[256,512]{1,0:T(8,128)(2,1)S(1)}, bf16[256,512]{1,0:T(8,128)(2,1)S(1)}, u32[]{:S(2)}, u32[]{:S(2)}) collective-permute-start(bf16[256,512]{1,0:T(8,128)(2,1)S(1)} %collective-permute-done.22), channel_id=1, source_target_pairs={{0,16},{16,0},{1,17},{17,1},{2,18},{18,2},{3,19},{19,3},{4,20},{20... | collective-permute-start | bytes 786440 | tf_op jit(solution)/shard_map/ppermute | solution.py:215
  56.4 7.9 %collective-permute-start.5 = (bf16[256,512]{1,0:T(8,128)(2,1)}, bf16[256,512]{1,0:T(8,128)(2,1)}, u32[]{:S(2)}, u32[]{:S(2)}) collective-permute-start(bf16[256,512]{1,0:T(8,128)(2,1)} %collective-permute-done.4), channel_id=1, source_target_pairs={{0,16},{16,0},{1,17},{17,1},{2,18},{18,2},{3,19},{19,3},{4,20},{20... | collective-permute-start | bytes 786440 | tf_op jit(solution)/shard_map/ppermute | solution.py:215
  63.8 3.5 %collective-permute-start.28 = (bf16[2,2,64,1024]{3,2,1,0:T(8,128)(2,1)}, bf16[2,2,64,1024]{3,2,1,0:T(8,128)(2,1)}, u32[]{:S(2)}, u32[]{:S(2)}) collective-permute-start(bf16[2,2,64,1024]{3,2,1,0:T(8,128)(2,1)} %dynamic-slice_bitcast_fusion), channel_id=1, source_target_pairs={{0,1},{1,0},{2,3},{3,2},{4,5},{5,4},{6,7},{7,6},{8,9},{9,8},{10,11... | collective-permute-start | bytes 1572872 | tf_op jit(solution)/shard_map/ppermute | solution.py:215
  68.5 9.2 %collective-permute-start.29 = (bf16[2,64,1024]{2,1,0:T(8,128)(2,1)S(1)}, bf16[2,64,1024]{2,1,0:T(8,128)(2,1)S(1)}, u32[]{:S(2)}, u32[]{:S(2)}) collective-permute-start(bf16[2,64,1024]{2,1,0:T(8,128)(2,1)S(1)} %slice_bitcast_fusion.6), channel_id=1, source_target_pairs={{0,4},{2,6},{4,0},{6,2},{8,12},{10,14},{12,8},{14,10},{1,5},{3,7},... | collective-permute-start | bytes 786440 | tf_op jit(solution)/shard_map/ppermute | solution.py:215
  69.1 13.4 %collective-permute-start.7 = (bf16[2,64,1024]{2,1,0:T(8,128)(2,1)S(1)}, bf16[2,64,1024]{2,1,0:T(8,128)(2,1)S(1)}, u32[]{:S(2)}, u32[]{:S(2)}) collective-permute-start(bf16[2,64,1024]{2,1,0:T(8,128)(2,1)S(1)} %slice_bitcast_fusion.10), channel_id=1, source_target_pairs={{0,4},{2,6},{4,0},{6,2},{8,12},{10,14},{12,8},{14,10},{1,5},{3,7},... | collective-permute-start | bytes 786440 | tf_op jit(solution)/shard_map/ppermute | solution.py:215
  77.9 5.4 %collective-permute-start.30 = (bf16[64,1024]{1,0:T(8,128)(2,1)S(1)}, bf16[64,1024]{1,0:T(8,128)(2,1)S(1)}, u32[]{:S(2)}, u32[]{:S(2)}) collective-permute-start(bf16[64,1024]{1,0:T(8,128)(2,1)S(1)} %slice_bitcast_fusion.14), channel_id=1, source_target_pairs={{0,2},{2,0},{4,6},{6,4},{8,10},{10,8},{12,14},{14,12},{1,3},{3,1},... | collective-permute-start | bytes 393224 | tf_op jit(solution)/shard_map/ppermute | solution.py:215
  82.6 6.1 %collective-permute-start.8 = (bf16[64,1024]{1,0:T(8,128)(2,1)S(1)}, bf16[64,1024]{1,0:T(8,128)(2,1)S(1)}, u32[]{:S(2)}, u32[]{:S(2)}) collective-permute-start(bf16[64,1024]{1,0:T(8,128)(2,1)S(1)} %slice_bitcast_fusion.20), channel_id=1, source_target_pairs={{0,2},{2,0},{4,6},{6,4},{8,10},{10,8},{12,14},{14,12},{1,3},{3,1},... | collective-permute-start | bytes 393224 | tf_op jit(solution)/shard_map/ppermute | solution.py:215
  83.4 6.7 %collective-permute-start.31 = (bf16[64,1024]{1,0:T(8,128)(2,1)S(1)}, bf16[64,1024]{1,0:T(8,128)(2,1)S(1)}, u32[]{:S(2)}, u32[]{:S(2)}) collective-permute-start(bf16[64,1024]{1,0:T(8,128)(2,1)S(1)} %maximum_select_fusion.18), channel_id=1, source_target_pairs={{0,2},{2,0},{4,6},{6,4},{8,10},{10,8},{12,14},{14,12},{1,3},{3,1},... | collective-permute-start | bytes 393224 | tf_op jit(solution)/shard_map/ppermute | solution.py:215
  88.8 13.5 %collective-permute-start.9 = (bf16[64,1024]{1,0:T(8,128)(2,1)S(1)}, bf16[64,1024]{1,0:T(8,128)(2,1)S(1)}, u32[]{:S(2)}, u32[]{:S(2)}) collective-permute-start(bf16[64,1024]{1,0:T(8,128)(2,1)S(1)} %maximum_select_fusion.16), channel_id=1, source_target_pairs={{0,8},{2,10},{4,12},{6,14},{8,0},{10,2},{12,4},{14,6},{1,9},{3,11}... | collective-permute-start | bytes 393224 | tf_op jit(solution)/shard_map/ppermute | solution.py:250
  90.1 16.1 %collective-permute-start.32 = (bf16[2,64,1024]{2,1,0:T(8,128)(2,1)S(1)}, bf16[2,64,1024]{2,1,0:T(8,128)(2,1)S(1)}, u32[]{:S(2)}, u32[]{:S(2)}) collective-permute-start(bf16[2,64,1024]{2,1,0:T(8,128)(2,1)S(1)} %get-tuple-element.117), channel_id=1, source_target_pairs={{0,8},{2,10},{4,12},{6,14},{8,0},{10,2},{12,4},{14,6},{1,9},{3,11}... | collective-permute-start | bytes 786440 | tf_op jit(solution)/shard_map/ppermute | solution.py:250
  102.3 8.3 %collective-permute-start.10 = (bf16[2,64,1024]{2,1,0:T(8,128)(2,1)S(1)}, bf16[2,64,1024]{2,1,0:T(8,128)(2,1)S(1)}, u32[]{:S(2)}, u32[]{:S(2)}) collective-permute-start(bf16[2,64,1024]{2,1,0:T(8,128)(2,1)S(1)} %get-tuple-element.129), channel_id=1, source_target_pairs={{0,4},{2,6},{4,0},{6,2},{8,12},{10,14},{12,8},{14,10},{1,5},{3,7},... | collective-permute-start | bytes 786440 | tf_op jit(solution)/shard_map/ppermute | solution.py:215
  106.3 13.9 %collective-permute-start.33 = (bf16[2,2,64,1024]{3,2,0,1:T(8,128)(2,1)S(1)}, bf16[2,2,64,1024]{3,2,0,1:T(8,128)(2,1)S(1)}, u32[]{:S(2)}, u32[]{:S(2)}) collective-permute-start(bf16[2,2,64,1024]{3,2,0,1:T(8,128)(2,1)S(1)} %get-tuple-element.87), channel_id=1, source_target_pairs={{0,4},{2,6},{4,0},{6,2},{8,12},{10,14},{12,8},{14,10},{1,5},{3,7},... | collective-permute-start | bytes 1572872 | tf_op jit(solution)/shard_map/ppermute | solution.py:215
  110.7 10.6 %collective-permute-start.11 = (bf16[2,2,64,1024]{3,2,1,0:T(8,128)(2,1)S(1)}, bf16[2,2,64,1024]{3,2,1,0:T(8,128)(2,1)}, u32[]{:S(2)}, u32[]{:S(2)}) collective-permute-start(bf16[2,2,64,1024]{3,2,1,0:T(8,128)(2,1)S(1)} %get-tuple-element.101), channel_id=1, source_target_pairs={{0,2},{2,0},{4,6},{6,4},{8,10},{10,8},{12,14},{14,12},{1,3},{3,1},... | collective-permute-start | bytes 1572872 | tf_op jit(solution)/shard_map/ppermute | solution.py:215
  121.3 3.4 %collective-permute-start.34 = (bf16[2,2,2,64,1024]{4,3,0,2,1:T(8,128)(2,1)}, bf16[2,2,2,64,1024]{4,3,0,2,1:T(8,128)(2,1)}, u32[]{:S(2)}, u32[]{:S(2)}) collective-permute-start(bf16[2,2,2,64,1024]{4,3,0,2,1:T(8,128)(2,1)} %get-tuple-element.63), channel_id=1, source_target_pairs={{0,1},{1,0},{2,3},{3,2},{4,5},{5,4},{6,7},{7,6},{8,9},{9,8},{10,11... | collective-permute-start | bytes 3145736 | tf_op jit(solution)/shard_map/ppermute | solution.py:215
  123.5 3.1 %collective-permute-start.12 = (bf16[2,2,2,64,1024]{4,3,2,1,0:T(8,128)(2,1)}, bf16[2,2,2,64,1024]{4,3,2,1,0:T(8,128)(2,1)}, u32[]{:S(2)}, u32[]{:S(2)}) collective-permute-start(bf16[2,2,2,64,1024]{4,3,2,1,0:T(8,128)(2,1)} %get-tuple-element.65), channel_id=1, source_target_pairs={{0,1},{1,0},{2,3},{3,2},{4,5},{5,4},{6,7},{7,6},{8,9},{9,8},{10,11... | collective-permute-start | bytes 3145736 | tf_op jit(solution)/shard_map/ppermute | solution.py:215
  146.8 20.8 %collective-permute-start.13 = (bf16[2,2,2,64,1024]{4,3,2,1,0:T(8,128)(2,1)S(1)}, bf16[2,2,2,64,1024]{4,3,2,1,0:T(8,128)(2,1)S(1)}, u32[]{:S(2)}, u32[]{:S(2)}) collective-permute-start(bf16[2,2,2,64,1024]{4,3,2,1,0:T(8,128)(2,1)S(1)} %bitcast.256), channel_id=1, source_target_pairs={{0,1},{1,0},{2,3},{3,2},{4,5},{5,4},{6,7},{7,6},{8,9},{9,8},{10,11... | collective-permute-start | bytes 3145736 | tf_op jit(solution)/shard_map/ppermute | solution.py:215
  168.1 14.8 %collective-permute-start.14 = (bf16[2,2,64,1024]{3,2,1,0:T(8,128)(2,1)S(1)}, bf16[2,2,64,1024]{3,2,1,0:T(8,128)(2,1)S(1)}, u32[]{:S(2)}, u32[]{:S(2)}) collective-permute-start(bf16[2,2,64,1024]{3,2,1,0:T(8,128)(2,1)S(1)} %slice_bitcast_fusion.2), channel_id=1, source_target_pairs={{0,2},{2,0},{4,6},{6,4},{8,10},{10,8},{12,14},{14,12},{1,3},{3,1},... | collective-permute-start | bytes 1572872 | tf_op jit(solution)/shard_map/ppermute | solution.py:215
  170.4 23.0 %collective-permute-start.36 = (bf16[2,2,64,1024]{3,2,1,0:T(8,128)(2,1)S(1)}, bf16[2,2,64,1024]{3,2,1,0:T(8,128)(2,1)S(1)}, u32[]{:S(2)}, u32[]{:S(2)}) collective-permute-start(bf16[2,2,64,1024]{3,2,1,0:T(8,128)(2,1)S(1)} %slice_bitcast_fusion), channel_id=1, source_target_pairs={{0,2},{2,0},{4,6},{6,4},{8,10},{10,8},{12,14},{14,12},{1,3},{3,1},... | collective-permute-start | bytes 1572872 | tf_op jit(solution)/shard_map/ppermute | solution.py:215
  183.2 10.5 %collective-permute-start.15 = (bf16[2,64,1024]{2,1,0:T(8,128)(2,1)S(1)}, bf16[2,64,1024]{2,1,0:T(8,128)(2,1)S(1)}, u32[]{:S(2)}, u32[]{:S(2)}) collective-permute-start(bf16[2,64,1024]{2,1,0:T(8,128)(2,1)S(1)} %slice_bitcast_fusion.8), channel_id=1, source_target_pairs={{0,4},{2,6},{4,0},{6,2},{8,12},{10,14},{12,8},{14,10},{1,5},{3,7},... | collective-permute-start | bytes 786440 | tf_op jit(solution)/shard_map/ppermute | solution.py:215
  193.6 10.4 %collective-permute-start.37 = (bf16[2,64,1024]{2,1,0:T(8,128)(2,1)S(1)}, bf16[2,64,1024]{2,1,0:T(8,128)(2,1)S(1)}, u32[]{:S(2)}, u32[]{:S(2)}) collective-permute-start(bf16[2,64,1024]{2,1,0:T(8,128)(2,1)S(1)} %slice_bitcast_fusion.4), channel_id=1, source_target_pairs={{0,4},{2,6},{4,0},{6,2},{8,12},{10,14},{12,8},{14,10},{1,5},{3,7},... | collective-permute-start | bytes 786440 | tf_op jit(solution)/shard_map/ppermute | solution.py:215
  193.8 10.4 %collective-permute-start.16 = (bf16[64,1024]{1,0:T(8,128)(2,1)S(1)}, bf16[64,1024]{1,0:T(8,128)(2,1)S(1)}, u32[]{:S(2)}, u32[]{:S(2)}) collective-permute-start(bf16[64,1024]{1,0:T(8,128)(2,1)S(1)} %slice_bitcast_fusion.19), channel_id=1, source_target_pairs={{8,0},{10,2},{12,4},{14,6},{0,8},{2,10},{4,12},{6,14},{9,1},{11,3}... | collective-permute-start | bytes 393224 | tf_op jit(solution)/shard_map/ppermute | solution.py:256
  204.1 7.0 %collective-permute-start.38 = (bf16[64,1024]{1,0:T(8,128)(2,1)S(1)}, bf16[64,1024]{1,0:T(8,128)(2,1)S(1)}, u32[]{:S(2)}, u32[]{:S(2)}) collective-permute-start(bf16[64,1024]{1,0:T(8,128)(2,1)S(1)} %slice_bitcast_fusion.13), channel_id=1, source_target_pairs={{8,0},{10,2},{12,4},{14,6},{0,8},{2,10},{4,12},{6,14},{9,1},{11,3}... | collective-permute-start | bytes 393224 | tf_op jit(solution)/shard_map/ppermute | solution.py:256
  204.3 7.6 %collective-permute-start.17 = (bf16[64,1024]{1,0:T(8,128)(2,1)S(1)}, bf16[64,1024]{1,0:T(8,128)(2,1)S(1)}, u32[]{:S(2)}, u32[]{:S(2)}) collective-permute-start(bf16[64,1024]{1,0:T(8,128)(2,1)S(1)} %maximum_select_fusion.17), channel_id=1, source_target_pairs={{0,2},{2,0},{4,6},{6,4},{8,10},{10,8},{12,14},{14,12},{1,3},{3,1},... | collective-permute-start | bytes 393224 | tf_op jit(solution)/shard_map/ppermute | solution.py:215
  211.2 11.4 %collective-permute-start.39 = (bf16[64,1024]{1,0:T(8,128)(2,1)S(1)}, bf16[64,1024]{1,0:T(8,128)(2,1)S(1)}, u32[]{:S(2)}, u32[]{:S(2)}) collective-permute-start(bf16[64,1024]{1,0:T(8,128)(2,1)S(1)} %maximum_select_fusion.19), channel_id=1, source_target_pairs={{0,2},{2,0},{4,6},{6,4},{8,10},{10,8},{12,14},{14,12},{1,3},{3,1},... | collective-permute-start | bytes 393224 | tf_op jit(solution)/shard_map/ppermute | solution.py:215
  212.0 10.5 %collective-permute-start.18 = (bf16[2,64,1024]{2,1,0:T(8,128)(2,1)S(1)}, bf16[2,64,1024]{2,1,0:T(8,128)(2,1)S(1)}, u32[]{:S(2)}, u32[]{:S(2)}) collective-permute-start(bf16[2,64,1024]{2,1,0:T(8,128)(2,1)S(1)} %get-tuple-element.127), channel_id=1, source_target_pairs={{0,4},{2,6},{4,0},{6,2},{8,12},{10,14},{12,8},{14,10},{1,5},{3,7},... | collective-permute-start | bytes 786440 | tf_op jit(solution)/shard_map/ppermute | solution.py:215
  222.5 9.3 %collective-permute-start.19 = (bf16[2,2,64,1024]{3,2,1,0:T(8,128)(2,1)S(1)}, bf16[2,2,64,1024]{3,2,1,0:T(8,128)(2,1)S(1)}, u32[]{:S(2)}, u32[]{:S(2)}) collective-permute-start(bf16[2,2,64,1024]{3,2,1,0:T(8,128)(2,1)S(1)} %get-tuple-element.99), channel_id=1, source_target_pairs={{0,1},{1,0},{2,3},{3,2},{4,5},{5,4},{6,7},{7,6},{8,9},{9,8},{10,11... | collective-permute-start | bytes 1572872 | tf_op jit(solution)/shard_map/ppermute | solution.py:215
  222.6 9.0 %collective-permute-start.40 = (bf16[2,64,1024]{2,1,0:T(8,128)(2,1)S(1)}, bf16[2,64,1024]{2,1,0:T(8,128)(2,1)S(1)}, u32[]{:S(2)}, u32[]{:S(2)}) collective-permute-start(bf16[2,64,1024]{2,1,0:T(8,128)(2,1)S(1)} %get-tuple-element.115), channel_id=1, source_target_pairs={{0,4},{2,6},{4,0},{6,2},{8,12},{10,14},{12,8},{14,10},{1,5},{3,7},... | collective-permute-start | bytes 786440 | tf_op jit(solution)/shard_map/ppermute | solution.py:215
  231.7 6.4 %collective-permute-start.41 = (bf16[2,2,64,1024]{3,2,1,0:T(8,128)(2,1)S(1)}, bf16[2,2,64,1024]{3,2,1,0:T(8,128)(2,1)S(1)}, u32[]{:S(2)}, u32[]{:S(2)}) collective-permute-start(bf16[2,2,64,1024]{3,2,1,0:T(8,128)(2,1)S(1)} %get-tuple-element.85), channel_id=1, source_target_pairs={{0,1},{1,0},{2,3},{3,2},{4,5},{5,4},{6,7},{7,6},{8,9},{9,8},{10,11... | collective-permute-start | bytes 1572872 | tf_op jit(solution)/shard_map/ppermute | solution.py:215
  233.9 12.9 %collective-permute-start.24 = (bf16[256,512]{0,1:T(8,128)(2,1)S(1)}, bf16[256,512]{0,1:T(8,128)(2,1)S(1)}, u32[]{:S(2)}, u32[]{:S(2)}) collective-permute-start(bf16[256,512]{0,1:T(8,128)(2,1)S(1)} %slice.232), channel_id=1, source_target_pairs={{0,4},{2,6},{4,0},{6,2},{8,12},{10,14},{12,8},{14,10},{1,5},{3,7},... | collective-permute-start | bytes 786440 | tf_op jit(solution)/shard_map/ppermute | solution.py:215
  236.9 38.5 %collective-permute-start.47 = (bf16[512,512]{1,0:T(8,128)(2,1)}, bf16[512,512]{1,0:T(8,128)(2,1)}, u32[]{:S(2)}, u32[]{:S(2)}) collective-permute-start(bf16[512,512]{1,0:T(8,128)(2,1)} %convolution_convert_fusion.1), channel_id=1, source_target_pairs={{8,0},{10,2},{12,4},{14,6},{0,8},{2,10},{4,12},{6,14},{9,1},{11,3}... | collective-permute-start | bytes 1572872 | tf_op jit(solution)/shard_map/ppermute | solution.py:256
  242.6 16.6 %collective-permute-start.42 = (bf16[256,512]{0,1:T(8,128)(2,1)S(1)}, bf16[256,512]{0,1:T(8,128)(2,1)S(1)}, u32[]{:S(2)}, u32[]{:S(2)}) collective-permute-start(bf16[256,512]{0,1:T(8,128)(2,1)S(1)} %slice.253), channel_id=1, source_target_pairs={{0,4},{2,6},{4,0},{6,2},{8,12},{10,14},{12,8},{14,10},{1,5},{3,7},... | collective-permute-start | bytes 786440 | tf_op jit(solution)/shard_map/ppermute | solution.py:215
  244.3 41.8 %collective-permute-start.44 = (bf16[512,512]{1,0:T(8,128)(2,1)}, bf16[512,512]{1,0:T(8,128)(2,1)}, u32[]{:S(2)}, u32[]{:S(2)}) collective-permute-start(bf16[512,512]{1,0:T(8,128)(2,1)} %convolution_convert_fusion.3), channel_id=1, source_target_pairs={{8,0},{10,2},{12,4},{14,6},{0,8},{2,10},{4,12},{6,14},{9,1},{11,3}... | collective-permute-start | bytes 1572872 | tf_op jit(solution)/shard_map/ppermute | solution.py:256
  246.8 14.5 %collective-permute-start.25 = (bf16[128,1024]{0,1:T(8,128)(2,1)S(1)}, bf16[128,1024]{0,1:T(8,128)(2,1)S(1)}, u32[]{:S(2)}, u32[]{:S(2)}) collective-permute-start(bf16[128,1024]{0,1:T(8,128)(2,1)S(1)} %pad_maximum_fusion.16), channel_id=1, source_target_pairs={{0,2},{2,0},{4,6},{6,4},{8,10},{10,8},{12,14},{14,12},{1,3},{3,1},... | collective-permute-start | bytes 786440 | tf_op jit(solution)/shard_map/ppermute | solution.py:215
  260.0 29.0 %collective-permute-start.43 = (bf16[128,1024]{0,1:T(8,128)(2,1)}, bf16[128,1024]{0,1:T(8,128)(2,1)}, u32[]{:S(2)}, u32[]{:S(2)}) collective-permute-start(bf16[128,1024]{0,1:T(8,128)(2,1)} %pad_maximum_fusion.19), channel_id=1, source_target_pairs={{0,2},{2,0},{4,6},{6,4},{8,10},{10,8},{12,14},{14,12},{1,3},{3,1},... | collective-permute-start | bytes 786440 | tf_op jit(solution)/shard_map/ppermute | solution.py:215
  279.4 12.2 %collective-permute-start.48 = (bf16[512,256]{1,0:T(8,128)(2,1)S(1)}, bf16[512,256]{1,0:T(8,128)(2,1)}, u32[]{:S(2)}, u32[]{:S(2)}) collective-permute-start(bf16[512,256]{1,0:T(8,128)(2,1)S(1)} %bitcast.268), channel_id=1, source_target_pairs={{0,4},{2,6},{4,0},{6,2},{8,12},{10,14},{12,8},{14,10},{1,5},{3,7},... | collective-permute-start | bytes 786440 | tf_op jit(solution)/shard_map/ppermute | solution.py:215
  288.8 8.3 %collective-permute-start.45 = (bf16[512,256]{1,0:T(8,128)(2,1)S(1)}, bf16[512,256]{1,0:T(8,128)(2,1)S(1)}, u32[]{:S(2)}, u32[]{:S(2)}) collective-permute-start(bf16[512,256]{1,0:T(8,128)(2,1)S(1)} %bitcast.267), channel_id=1, source_target_pairs={{0,4},{2,6},{4,0},{6,2},{8,12},{10,14},{12,8},{14,10},{1,5},{3,7},... | collective-permute-start | bytes 786440 | tf_op jit(solution)/shard_map/ppermute | solution.py:215
  293.0 9.2 %collective-permute-start.49 = (bf16[2,512,128]{2,1,0:T(8,128)(2,1)S(1)}, bf16[2,512,128]{2,1,0:T(8,128)(2,1)S(1)}, u32[]{:S(2)}, u32[]{:S(2)}) collective-permute-start(bf16[2,512,128]{2,1,0:T(8,128)(2,1)S(1)} %bitcast.272), channel_id=1, source_target_pairs={{0,2},{2,0},{4,6},{6,4},{8,10},{10,8},{12,14},{14,12},{1,3},{3,1},... | collective-permute-start | bytes 786440 | tf_op jit(solution)/shard_map/ppermute | solution.py:215
  297.6 9.2 %collective-permute-start.46 = (bf16[2,512,128]{2,1,0:T(8,128)(2,1)S(1)}, bf16[2,512,128]{2,1,0:T(8,128)(2,1)S(1)}, u32[]{:S(2)}, u32[]{:S(2)}) collective-permute-start(bf16[2,512,128]{2,1,0:T(8,128)(2,1)S(1)} %bitcast.273), channel_id=1, source_target_pairs={{0,2},{2,0},{4,6},{6,4},{8,10},{10,8},{12,14},{14,12},{1,3},{3,1},... | collective-permute-start | bytes 786440 | tf_op jit(solution)/shard_map/ppermute | solution.py:215
  (43 other events, 446.1 us)

commit v3 on v2

--- a/solution.py
+++ b/solution.py
@@ -224,15 +224,16 @@
     def add(a, b):
         return (a.astype(f32) + b.astype(f32)).astype(bf16)
 
-    def turn(v, axis):
-        blocks = jnp.split(v, nh, axis=axis)
-        orders = [
-            jnp.concatenate([blocks[(i - k) % nh] for k in range(nh)], axis=axis)
-            for i in range(nh)
-        ]
-        result = orders[0]
-        for i in range(1, nh):
-            result = jnp.where(h == i, orders[i], result)
+    def after(v, *done):
+        return lax.optimization_barrier((v, *done))[0]
+
+    def turn(blocks):
+        result = []
+        for k in range(nh):
+            block = blocks[-k % nh]
+            for i in range(1, nh):
+                block = jnp.where(h == i, blocks[(i - k) % nh], block)
+            result.append(block)
         return result
 
     def flip(v, index, axis):
@@ -243,6 +244,16 @@
         mine = lax.dynamic_index_in_dim(v, index, axis, keepdims=False)
         other = lax.dynamic_index_in_dim(v, 1 - index, axis, keepdims=False)
         return mine, other
+
+    def pick_halves(v, index):
+        size = v.shape[-1] // 2
+        mine = lax.dynamic_slice_in_dim(v, index * size, size, v.ndim - 1)
+        other = lax.dynamic_slice_in_dim(v, (1 - index) * size, size, v.ndim - 1)
+        return mine, other
+
+    def pick_quarters(v, index):
+        pairs = [pick_halves(half, index) for half in jnp.split(v, 2, axis=-1)]
+        return tuple(jnp.concatenate(p, axis=-1) for p in zip(*pairs))
 
     def gather_h(v):
         parts = [v]
@@ -256,72 +267,111 @@
             total = add(lax.ppermute(total, "expert", h_down), parts[k])
         return total
 
-    def square_rows(v):
-        mine, other = pick(v.reshape(tok_rows, 2, 2 * quarter_d), c, 1)
-        v = jnp.concatenate([mine, c_swap(other)], axis=0)
-        mine, other = pick(v.reshape(2 * tok_rows, 2, quarter_d), y, 1)
+    def square_rows(v, y_first):
+        if y_first:
+            mine, other = pick_quarters(v, y)
+            mine, other = pick_halves(jnp.concatenate([mine, y_swap(other)], axis=0), c)
+            return jnp.concatenate([mine, c_swap(other)], axis=0)
+        mine, other = pick_halves(v, c)
+        mine, other = pick_halves(jnp.concatenate([mine, c_swap(other)], axis=0), y)
         received = y_swap(other)
         parts = [mine[:tok_rows], received[:tok_rows], mine[tok_rows:], received[tok_rows:]]
         return jnp.concatenate(parts, axis=0)
 
-    def square_weight(v):
-        mine, other = pick(v.reshape(2, 2, quarter_d, shard), y, 1)
-        v = flip(jnp.concatenate([mine, y_swap(other)], axis=2), y, 2)
-        mine, other = pick(v, c, 0)
-        block = flip(jnp.concatenate([mine, c_swap(other)], axis=1), c, 1)
-        if not shared:
-            return gather_h(block)
-        mine, _ = pick(block.reshape(2, quarter_d // 2, 4 * shard), g, 0)
-        parts = [block]
-        for _ in range(nh - 1):
-            mine = lax.ppermute(mine, "expert", h_up)
-            parts.append(flip(jnp.concatenate([mine, g_swap(mine)], axis=0), g, 0))
-        return parts
-
-    def project(rows, weights):
-        part = jnp.concatenate([dot(rows, w).astype(bf16) for w in weights], axis=1)
-        mine, other = pick(part.reshape(2, 2, 2, half_rows, latent), t, 2)
-        part = add(mine, t_swap(other))
-        part = add(part[0], c_swap(part[1]))
-        part = add(part[0], y_swap(part[1]))
-        return turn(part, 1)
-
-    def gather_first(part):
-        part = jnp.stack(gather_h(part))
-        part = jnp.stack([part, c_swap(part)])
-        part = jnp.stack([part, y_swap(part)])
-        part = jnp.stack([part, t_swap(part)])
-        return part.reshape(-1, latent)
-
-    def gather_second(part):
-        part = jnp.stack([part, y_swap(part)])
-        part = jnp.stack(gather_h(part), axis=1)
-        part = jnp.stack([part, c_swap(part)], axis=1)
-        part = jnp.stack([part, t_swap(part)])
-        return part.reshape(-1, latent)
+    def square_weight(v, y_first, wait):
+        v = v.reshape(2, 2, quarter_d, shard)
+        if shared:
+            v, _ = pick(v.reshape(2, 2, 2, quarter_d // 2, shard), g, 2)
+        if y_first:
+            mine, other = pick(v, y, 1)
+            v = flip(jnp.concatenate([mine, y_swap(other)], axis=2), y, 2)
+            mine, other = pick(v, c, 0)
+            last = c_swap(other)
+            block = flip(jnp.concatenate([mine, last], axis=1), c, 1)
+        else:
+            mine, other = pick(v, c, 0)
+            v = flip(jnp.concatenate([mine, c_swap(other)], axis=2), c, 2)
+            mine, other = pick(v, y, 0)
+            last = y_swap(other)
+            pair = flip(jnp.concatenate([mine, last], axis=1), y, 1)
+            block = jnp.concatenate(
+                [pair[:, i * shard : (i + 1) * shard] for i in (0, 2, 1, 3)], axis=1
+            )
+        parts = gather_h(after(block, *wait))
+        parts[0] = block
+        arrived = parts[-1]
+        if shared:
+            parts = [flip(jnp.concatenate([p, g_swap(p)], axis=0), g, 0) for p in parts]
+        return parts, last, arrived
+
+    def project(rows, weights, y_first):
+        blocks = []
+        for k, weight in enumerate(weights):
+            part = dot(rows, weight).astype(bf16).reshape(2, 2, 2, half_rows, latent // nh)
+            mine, other = pick(part, t, 2)
+            part = add(mine, t_swap(other))
+            if k % 2 == int(y_first):
+                part = add(part[0], c_swap(part[1]))
+                part = add(part[0], y_swap(part[1]))
+            else:
+                part = add(part[:, 0], y_swap(part[:, 1]))
+                part = add(part[0], c_swap(part[1]))
+            blocks.append(part)
+        return turn(blocks)
+
+    def gather(blocks, y_first):
+        whole = []
+        for j, part in enumerate(blocks):
+            part = jnp.stack(gather_h(part))
+            if j % 2 == int(y_first):
+                part = jnp.stack([part, c_swap(part)])
+                part = jnp.stack([part, y_swap(part)])
+            else:
+                part = jnp.stack([part, y_swap(part)])
+                part = jnp.stack([part, c_swap(part)], axis=1)
+            part = jnp.stack([part, t_swap(part)])
+            whole.append(part.reshape(-1, part.shape[-1]))
+        return jnp.concatenate(whole, axis=1)
 
     def collect(part):
         part = part.reshape(2, 2, 2, nh, half_rows, latent)
         part = add(part[0], t_swap(part[1]))
-        part = add(part[0], y_swap(part[1]))
-        part = add(part[0], c_swap(part[1]))
-        part = turn(scatter_h([part[k] for k in range(nh)]), 1)
-        part = jnp.stack([part, y_swap(part)])
-        part = jnp.stack([part, c_swap(part)])
-        part = flip(jnp.stack([part, t_swap(part)], axis=2), t, 2)
-        return part.reshape(4 * tok_rows, latent)
-
-    def finish(part, rows, weights):
-        cols = latent // nh
-        grads = [dot(rows, part[:, k * cols : (k + 1) * cols], TN).astype(bf16) for k in range(nh)]
-        grad = scatter_h(grads)
-        mine, other = pick(grad.reshape(quarter_d, 2, 2 * shard), c, 1)
-        grad = jnp.stack([mine, c_swap(other)])
-        mine, other = pick(grad.reshape(2, quarter_d, 2, shard), y, 2)
-        grad = jnp.stack([mine, y_swap(other)], axis=1)
+        blocks = []
+        for j, block in enumerate(jnp.split(part, nh, axis=-1)):
+            if j % 2 == 0:
+                block = add(block[0], y_swap(block[1]))
+                block = add(block[0], c_swap(block[1]))
+            else:
+                block = add(block[:, 0], c_swap(block[:, 1]))
+                block = add(block[0], y_swap(block[1]))
+            blocks.append(scatter_h([block[k] for k in range(nh)]))
+        whole = []
+        for k, block in enumerate(turn(blocks)):
+            if k % 2 == 0:
+                block = jnp.stack([block, y_swap(block)])
+                block = jnp.stack([block, c_swap(block)])
+            else:
+                block = jnp.stack([block, c_swap(block)])
+                block = jnp.stack([block, y_swap(block)], axis=1)
+            block = flip(jnp.stack([block, t_swap(block)], axis=2), t, 2)
+            whole.append(block.reshape(4 * tok_rows, -1))
+        return whole, part
+
+    def finish(blocks, rows, weights):
+        grads = [dot(rows, block, TN).astype(bf16) for block in blocks]
+        first, second = jnp.split(scatter_h(grads), 2, axis=0)
+        mine, other = pick_halves(first, c)
+        first = jnp.stack([mine, c_swap(other)])
+        mine, other = pick_halves(first, y)
+        first = jnp.stack([mine, y_swap(other)], axis=1)
+        mine, other = pick_quarters(second, y)
+        second = jnp.stack([mine, y_swap(other)])
+        mine, other = pick_halves(second, c)
+        second = jnp.stack([mine, c_swap(other)])
+        grad = jnp.concatenate([first, second], axis=2)
         grad = flip(flip(grad, c, 0), y, 1).reshape(4 * quarter_d, shard).astype(f32)
 
-        whole = sum(dot(part[:, k * cols : (k + 1) * cols], weights[k], NT) for k in range(nh))
+        whole = sum(dot(block, weight, NT) for block, weight in zip(blocks, weights))
         whole = whole.astype(bf16)
         theirs = c_swap(whole[2 * tok_rows :])
         pieces = [whole[:tok_rows], theirs[:tok_rows]]
@@ -336,7 +386,7 @@
     local_ids = own * exp_local + jnp.arange(exp_local, dtype=jnp.int32)
     hit = routes[:, :, None] == local_ids[None, None, :]
     gate_all = jnp.sum(jnp.where(hit, gates[:, :, None], 0), axis=1).astype(f32) * gate_unit
-    gate_all = turn(gate_all.reshape(nh, 2, 2, 2, half_rows, exp_local), 0)
+    gate_all = jnp.stack(turn(list(gate_all.reshape(nh, 2, 2, 2, half_rows, exp_local))))
     gate_all = flip(flip(flip(gate_all, c, 1), y, 2), t, 3)
     gate_columns = gate_all.transpose(3, 2, 1, 0, 4, 5).reshape(-1, exp_local)
 
@@ -346,22 +396,27 @@
     )
     down_rows = down_proj.reshape(exp_local * width, latent)
 
-    down_parts = square_weight(down_weight)
-    up_parts = square_weight(up_weight)
-    token_rows = square_rows(tokens)
-    cot_rows = square_rows(cotangent)
-    latent_in = gather_first(project(token_rows, down_parts))
-    latent_grad = gather_second(project(cot_rows, up_parts))
+    down_parts, down_last, down_far = square_weight(down_weight, True, ())
+    up_parts, up_last, _ = square_weight(up_weight, False, (down_far,))
+    token_rows = square_rows(after(tokens, up_last), True)
+    cot_rows = square_rows(after(cotangent, down_last), False)
+    latent_in = gather(project(token_rows, down_parts, False), False)
+    latent_grad = gather(project(cot_rows, up_parts, True), True)
 
     hs, cp, cu, out_part = forward(
         latent_in, gate_blocks(gate_columns), gate_proj, up_proj, down_rows
     )
-    dpu, in_part = backward(latent_grad, cp, cu, gate_proj, up_proj, down_rows)
-    down_proj_grad = down_grads(hs, latent_grad).reshape(down_proj.shape)
+    down_proj_grad = down_grads(hs, latent_grad)
+    latent_out, out_half = collect(out_part)
+    dpu, in_part = backward(
+        after(latent_grad, down_proj_grad, out_half), cp, cu, gate_proj, up_proj, down_rows
+    )
+    down_proj_grad = down_proj_grad.reshape(down_proj.shape)
     gate_proj_grad, up_proj_grad = input_grads(latent_in, dpu)
 
-    out, up_grad = finish(collect(out_part), cot_rows, up_parts)
-    tokens_grad, down_grad = finish(collect(in_part), token_rows, down_parts)
+    out, up_grad = finish(latent_out, cot_rows, up_parts)
+    latent_in_grad, _ = collect(in_part)
+    tokens_grad, down_grad = finish(latent_in_grad, token_rows, down_parts)
     return (out, tokens_grad, gate_proj_grad, up_proj_grad, down_proj_grad, down_grad, up_grad)
 
 

time: 309 us -> 304 us (0.984)
  starting transfers between devices: 45 us -> 84.9 us
  waiting for transfers between devices: 158 us -> 131 us
  local copies, waits for them, and re-layouts: 28.4 us -> 13.6 us
  matrix products: 11.9 us -> 5.62 us
    ppermute x42 -> x70, starting transfers between devices: 35.7 us -> 64.7 us  [swapper(): return lambda v: lax.ppermute(v, axis, perm)]
    ppermute x2 -> x0, waiting for transfers between devices: 13.6 us -> none  [square_weight(): mine = lax.ppermute(mine, 'expert', h_up)]
    ppermute x4 -> x6, waiting for transfers between devices: 25.4 us -> 15.5 us  [scatter_h(): total = add(lax.ppermute(total, 'expert', h_down), parts[k])]
    ppermute x4 -> x6, starting transfers between devices: 3.97 us -> 11.7 us  [scatter_h(): total = add(lax.ppermute(total, 'expert', h_down), parts[k])]
    dot_general x12, matrix products: 11.9 us -> 5.62 us  [dot(): return lax.dot_general(a, b, dims, preferred_element_type=f32)]
    ppermute x2 -> x6, starting transfers between devices: 2.44 us -> 8.52 us  [gather_h(): parts.append(lax.ppermute(parts[-1], 'expert', h_up))]
    unnamed x90 -> x81, local copies, waits for them, and re-layouts: 12.1 us -> 8.02 us
    dynamic_slice x8 -> x2, local copies, waits for them, and re-layouts: 3.6 us -> 0.04 us  [pick(): other = lax.dynamic_index_in_dim(v, 1 - index, axis, keepdims=False)]
  transfers between devices with their start and end apart: 50 -> 82, of which waited for: 30 -> 44; matrix products, arithmetic and copies ran while one was open for 14% -> 9% of each run, Pallas kernels for 10% -> 16%
where the time goes in v3:
time: 304 us
  waiting for transfers between devices  131 us (43%)
  starting transfers between devices  84.9 us (28%)
  Pallas kernels  49.1 us (16%)
  other arithmetic  17.1 us (6%)
  local copies, waits for them, and re-layouts  13.6 us (4%)
  matrix products  5.62 us (2%)
    ppermute x70, waiting for transfers between devices, swapper(): return lambda v: lax.ppermute(v, axis, perm)  102 us
    ppermute x70, starting transfers between devices, swapper(): return lambda v: lax.ppermute(v, axis, perm)  64.7 us
    pallas_call x1, Pallas kernels, local(): forward(latent_in, gate_blocks(gate_columns), gate_proj, up_proj, down_rows)  17 us
    pallas_call x1, Pallas kernels, local(): backward(after(latent_grad, down_proj_grad, out_half), cp, cu, gate_proj,...  16.8 us
    ppermute x6, waiting for transfers between devices, scatter_h(): total = add(lax.ppermute(total, 'expert', h_down), parts[k])  15.5 us
    ppermute x6, waiting for transfers between devices, gather_h(): parts.append(lax.ppermute(parts[-1], 'expert', h_up))  13.8 us
    ppermute x6, starting transfers between devices, scatter_h(): total = add(lax.ppermute(total, 'expert', h_down), parts[k])  11.7 us
    pallas_call x1, Pallas kernels, local(): gate_proj_grad, up_proj_grad = input_grads(latent_in, dpu)  10.3 us
  transfers between devices with their start and end apart: 82, of which 44 were waited for; matrix products, arithmetic and copies ran while one was open for 9% of the time, Pallas kernels for 16%

profile of v3, /device:TPU:0, one launch (start us, length us, event | category | flops | bytes accessed | tf_op | source)
XLA Modules:
  0.0 304.0 jit_solution(9485216768804172740)
XLA Ops:
  1.7 3.0 collective-permute-start.4
  12.0 1.9 collective-permute-done.5
  17.7 2.6 collective-permute-start.6
  20.3 2.2 collective-permute-start.41
  22.8 7.1 %collective-permute-done.6 = bf16[256,512]{1,0:T(8,128)(2,1)S(1)} collective-permute-done((bf16[256,512]{1,0:T(8,128)(2,1)S(1)}, bf16[256,512]{1,0:T(8,128)(2,1)S(1)}, u32[]{:S(2)}, u32[]{:S(2)}) %collective-permute-start.6) | collective-permute-done | bytes 262176 | tf_op jit(solution)/shard_map/ppermute | solution.py:261
  30.1 1.8 collective-permute-start.42
  32.1 2.9 collective-permute-start.3
  35.0 2.0 collective-permute-done.42
  38.5 6.6 %collective-permute-done.3 = bf16[256,512]{1,0:T(8,128)(2,1)S(1)} collective-permute-done((bf16[256,512]{1,0:T(8,128)(2,1)S(1)}, bf16[256,512]{1,0:T(8,128)(2,1)S(1)}, u32[]{:S(2)}, u32[]{:S(2)}) %collective-permute-start.3) | collective-permute-done | bytes 262176 | tf_op jit(solution)/shard_map/ppermute | solution.py:215
  48.6 6.8 %collective-permute-done.38 = bf16[256,512]{1,0:T(8,128)(2,1)S(1)} collective-permute-done((bf16[256,512]{1,0:T(8,128)(2,1)S(1)}, bf16[256,512]{1,0:T(8,128)(2,1)S(1)}, u32[]{:S(2)}, u32[]{:S(2)}) %collective-permute-start.38) | collective-permute-done | bytes 262176 | tf_op jit(solution)/shard_map/ppermute | solution.py:215
  59.2 3.1 %collective-permute-done.13 = bf16[2,64,512]{2,1,0:T(8,128)(2,1)S(1)} collective-permute-done((bf16[2,64,512]{2,1,0:T(8,128)(2,1)S(1)}, bf16[2,64,512]{2,1,0:T(8,128)(2,1)S(1)}, u32[]{:S(2)}, u32[]{:S(2)}) %collective-permute-start.13) | collective-permute-done | bytes 131104 | tf_op jit(solution)/shard_map/ppermute | solution.py:215
  63.4 1.8 collective-permute-start.10
  66.7 1.7 collective-permute-done.10
  69.4 2.0 collective-permute-start.19
  79.1 1.7 collective-permute-done.20
  84.4 2.9 collective-permute-done.21
  90.8 4.5 %collective-permute-done.50 = bf16[2,64,512]{2,1,0:T(8,128)(2,1)S(1)} collective-permute-done((bf16[2,64,512]{2,1,0:T(8,128)(2,1)S(1)}, bf16[2,64,512]{2,1,0:T(8,128)(2,1)S(1)}, u32[]{:S(2)}, u32[]{:S(2)}) %collective-permute-start.50) | collective-permute-done | bytes 131104 | tf_op jit(solution)/shard_map/ppermute | solution.py:215
  99.0 17.0 %shard_map.144 = (bf16[1024,1536]{1,0:T(8,128)(2,1)S(1)}, bf16[1024,1536]{1,0:T(8,128)(2,1)S(1)}, bf16[1024,1536]{1,0:T(8,128)(2,1)}, bf16[1024,1024]{1,0:T(8,128)(2,1)S(1)}) custom-call(bf16[1024,1024]{1,0:T(8,128)(2,1)S(1)} %pad_maximum_fusion.x_ref, f32[2,1024,2]{2,1,0:T(8,128)S(1)} %bitcast.367, bf16[4,1024,384]{2,1,0:T(8,128)(2,1)} %wg_ref.3, ...), custom_call_target="tpu_custom_call" | custom-call | flops 9663676416 | bytes 23068672 | tf_op jit(solution)/shard_map/pallas_call | solution.py:406
  116.1 1.7 copy-done.4
  122.1 5.2 %collective-permute-done.53 = bf16[64,512]{1,0:T(8,128)(2,1)S(1)} collective-permute-done((bf16[64,512]{1,0:T(8,128)(2,1)S(1)}, bf16[64,512]{1,0:T(8,128)(2,1)S(1)}, u32[]{:S(2)}, u32[]{:S(2)}) %collective-permute-start.53) | collective-permute-done | bytes 65568 | tf_op jit(solution)/shard_map/ppermute | solution.py:261
  128.4 4.1 %collective-permute-done.54 = bf16[2,64,512]{2,1,0:T(8,128)(2,1)S(1)} collective-permute-done((bf16[2,64,512]{2,1,0:T(8,128)(2,1)S(1)}, bf16[2,64,512]{2,1,0:T(8,128)(2,1)S(1)}, u32[]{:S(2)}, u32[]{:S(2)}) %collective-permute-start.54) | collective-permute-done | bytes 131104 | tf_op jit(solution)/shard_map/ppermute | solution.py:215
  134.6 6.0 %collective-permute-done.55 = bf16[2,2,64,512]{3,2,1,0:T(8,128)(2,1)} collective-permute-done((bf16[2,2,64,512]{3,2,1,0:T(8,128)(2,1)}, bf16[2,2,64,512]{3,2,1,0:T(8,128)(2,1)}, u32[]{:S(2)}, u32[]{:S(2)}) %collective-permute-start.55) | collective-permute-done | bytes 262176 | tf_op jit(solution)/shard_map/ppermute | solution.py:215
  145.4 1.7 collective-permute-start.27
  147.5 6.0 %collective-permute-done.24 = bf16[2,2,64,512]{3,2,1,0:T(8,128)(2,1)S(1)} collective-permute-done((bf16[2,2,64,512]{3,2,1,0:T(8,128)(2,1)S(1)}, bf16[2,2,64,512]{3,2,1,0:T(8,128)(2,1)S(1)}, u32[]{:S(2)}, u32[]{:S(2)}) %collective-permute-start.24) | collective-permute-done | bytes 262176 | tf_op jit(solution)/shard_map/ppermute | solution.py:215
  154.1 1.7 collective-permute-start.25
  157.3 1.8 collective-permute-done.25
  159.1 1.8 collective-permute-start.26
  162.3 5.0 %shard_map.145 = bf16[1536,1024]{1,0:T(8,128)(2,1)} custom-call(bf16[1024,1536]{1,0:T(8,128)(2,1)S(1)} %copy-done.2, bf16[1024,1024]{1,0:T(8,128)(2,1)S(1)} %pad_maximum_fusion.1.y_ref), custom_call_target="tpu_custom_call" | custom-call | flops 3221225472 | bytes 8388608 | tf_op jit(solution)/shard_map/pallas_call | solution.py:409
  168.8 16.8 %shard_map.146 = (bf16[1024,3072]{1,0:T(8,128)(2,1)}, bf16[1024,1024]{1,0:T(8,128)(2,1)S(1)}) custom-call(bf16[1024,1024]{1,0:T(8,128)(2,1)S(1)} %pad_maximum_fusion.1.y_ref, bf16[1024,1536]{1,0:T(8,128)(2,1)S(1)} %copy-done.5, bf16[1024,1536]{1,0:T(8,128)(2,1)S(1)} %copy-done.6, bf16[4,1024,384]{2,1,0:T(8,128)(2,1)S(1)} %copy-done, ...), custom_call_target="tpu_custom_call" | custom-call | flops 9663676416 | bytes 26214400 | tf_op jit(solution)/shard_map/pallas_call | solution.py:411
  185.6 1.7 collective-permute-start.30
  187.7 2.1 collective-permute-done.30
  192.5 2.5 collective-permute-done.31
  195.1 10.3 %shard_map.147 = (bf16[4,1024,384]{2,1,0:T(8,128)(2,1)}, bf16[4,1024,384]{2,1,0:T(8,128)(2,1)}) custom-call(bf16[1024,1024]{1,0:T(8,128)(2,1)S(1)} %pad_maximum_fusion.x_ref, bf16[1024,3072]{1,0:T(8,128)(2,1)S(1)} %copy-done.3), custom_call_target="tpu_custom_call" | custom-call | flops 6442450944 | bytes 14680064 | tf_op jit(solution)/shard_map/pallas_call | solution.py:415
  209.1 1.8 collective-permute-start.77
  213.7 8.8 %collective-permute-done.39 = bf16[256,512]{0,1:T(8,128)(2,1)S(1)} collective-permute-done((bf16[256,512]{0,1:T(8,128)(2,1)S(1)}, bf16[256,512]{0,1:T(8,128)(2,1)S(1)}, u32[]{:S(2)}, u32[]{:S(2)}) %collective-permute-start.39) | collective-permute-done | bytes 262176 | tf_op jit(solution)/shard_map/ppermute | solution.py:215
  223.0 8.7 %collective-permute-done.58 = bf16[2,2,64,512]{3,2,1,0:T(8,128)(2,1)S(1)} collective-permute-done((bf16[2,2,64,512]{3,2,1,0:T(8,128)(2,1)S(1)}, bf16[2,2,64,512]{3,2,1,0:T(8,128)(2,1)S(1)}, u32[]{:S(2)}, u32[]{:S(2)}) %collective-permute-start.58) | collective-permute-done | bytes 262176 | tf_op jit(solution)/shard_map/ppermute | solution.py:215
  231.9 1.7 collective-permute-start.59
  233.6 2.5 collective-permute-start.62
  237.9 3.2 %collective-permute-start.60 = (bf16[64,512]{1,0:T(8,128)(2,1)S(1)}, bf16[64,512]{1,0:T(8,128)(2,1)S(1)}, u32[]{:S(2)}, u32[]{:S(2)}) collective-permute-start(bf16[64,512]{1,0:T(8,128)(2,1)S(1)} %slice_bitcast_fusion.27), channel_id=1, source_target_pairs={{8,0},{10,2},{12,4},{14,6},{0,8},{2,10},{4,12},{6,14},{9,1},{11,3}... | collective-permute-start | bytes 196616 | tf_op jit(solution)/shard_map/ppermute | solution.py:267
  241.2 1.8 collective-permute-start.63
  244.8 1.7 collective-permute-done.63
  262.7 1.9 collective-permute-start.72
  264.6 11.0 %collective-permute-done.70 = bf16[256,512]{0,1:T(8,128)(2,1)S(1)} collective-permute-done((bf16[256,512]{0,1:T(8,128)(2,1)S(1)}, bf16[256,512]{0,1:T(8,128)(2,1)S(1)}, u32[]{:S(2)}, u32[]{:S(2)}) %collective-permute-start.70) | collective-permute-done | bytes 262176 | tf_op jit(solution)/shard_map/ppermute | solution.py:215
  275.7 13.3 %collective-permute-done.72 = bf16[512,512]{1,0:T(8,128)(2,1)S(1)} collective-permute-done((bf16[512,512]{1,0:T(8,128)(2,1)S(1)}, bf16[512,512]{1,0:T(8,128)(2,1)S(1)}, u32[]{:S(2)}, u32[]{:S(2)}) %collective-permute-start.72) | collective-permute-done | bytes 524320 | tf_op jit(solution)/shard_map/ppermute | solution.py:267
  289.6 2.0 collective-permute-start.75
  292.0 2.7 collective-permute-done.75
  294.8 2.5 collective-permute-done.73
  299.8 2.6 collective-permute-done.74
  (375 shorter events, 95.5 us)
Async XLA Ops:
  1.7 7.0 %collective-permute-start.4 = (bf16[2,256,128]{2,1,0:T(8,128)(2,1)S(1)}, bf16[2,256,128]{2,1,0:T(8,128)(2,1)S(1)}, u32[]{:S(2)}, u32[]{:S(2)}) collective-permute-start(bf16[2,256,128]{2,1,0:T(8,128)(2,1)S(1)} %get-tuple-element.106), channel_id=1, source_target_pairs={{0,2},{2,0},{4,6},{6,4},{8,10},{10,8},{12,14},{14,12},{1,3},{3,1},... | collective-permute-start | bytes 393224 | tf_op jit(solution)/shard_map/ppermute | solution.py:215
  14.0 24.5 %collective-permute-start.11 = (bf16[256,512]{1,0:T(8,128)(2,1)S(1)}, bf16[256,512]{1,0:T(8,128)(2,1)S(1)}, u32[]{:S(2)}, u32[]{:S(2)}) collective-permute-start(bf16[256,512]{1,0:T(8,128)(2,1)S(1)} %maximum_select_fusion.16), channel_id=1, source_target_pairs={{0,16},{16,0},{1,17},{17,1},{2,18},{18,2},{3,19},{19,3},{4,20},{20... | collective-permute-start | bytes 786440 | tf_op jit(solution)/shard_map/ppermute | solution.py:215
  16.1 21.5 %collective-permute-start.33 = (bf16[256,512]{1,0:T(8,128)(2,1)S(1)}, bf16[256,512]{1,0:T(8,128)(2,1)S(1)}, u32[]{:S(2)}, u32[]{:S(2)}) collective-permute-start(bf16[256,512]{1,0:T(8,128)(2,1)S(1)} %pad_maximum_fusion.17), channel_id=1, source_target_pairs={{0,16},{16,0},{1,17},{17,1},{2,18},{18,2},{3,19},{19,3},{4,20},{20... | collective-permute-start | bytes 786440 | tf_op jit(solution)/shard_map/ppermute | solution.py:215
  17.7 12.2 %collective-permute-start.6 = (bf16[256,512]{1,0:T(8,128)(2,1)S(1)}, bf16[256,512]{1,0:T(8,128)(2,1)S(1)}, u32[]{:S(2)}, u32[]{:S(2)}) collective-permute-start(bf16[256,512]{1,0:T(8,128)(2,1)S(1)} %maximum_select_fusion.16), channel_id=1, source_target_pairs={{0,8},{2,10},{4,12},{6,14},{8,0},{10,2},{12,4},{14,6},{1,9},{3,11}... | collective-permute-start | bytes 786440 | tf_op jit(solution)/shard_map/ppermute | solution.py:261
  20.3 9.8 %collective-permute-start.41 = (bf16[128,1024]{1,0:T(8,128)(2,1)S(1)}, bf16[128,1024]{1,0:T(8,128)(2,1)S(1)}, u32[]{:S(2)}, u32[]{:S(2)}) collective-permute-start(bf16[128,1024]{1,0:T(8,128)(2,1)S(1)} %get-tuple-element.89), channel_id=1, source_target_pairs={{0,4},{2,6},{4,0},{6,2},{8,12},{10,14},{12,8},{14,10},{1,5},{3,7},... | collective-permute-start | bytes 786440 | tf_op jit(solution)/shard_map/ppermute | solution.py:215
  22.7 9.3 %collective-permute-start.2 = (bf16[128,1024]{1,0:T(8,128)(2,1)S(1)}, bf16[128,1024]{1,0:T(8,128)(2,1)S(1)}, u32[]{:S(2)}, u32[]{:S(2)}) collective-permute-start(bf16[128,1024]{1,0:T(8,128)(2,1)S(1)} %pad_maximum_fusion.13), channel_id=1, source_target_pairs={{0,2},{2,0},{4,6},{6,4},{8,10},{10,8},{12,14},{14,12},{1,3},{3,1},... | collective-permute-start | bytes 786440 | tf_op jit(solution)/shard_map/ppermute | solution.py:215
  29.9 17.2 %collective-permute-start.37 = (bf16[256,512]{1,0:T(8,128)(2,1)S(1)}, bf16[256,512]{1,0:T(8,128)(2,1)S(1)}, u32[]{:S(2)}, u32[]{:S(2)}) collective-permute-start(bf16[256,512]{1,0:T(8,128)(2,1)S(1)} %pad_maximum_fusion.17), channel_id=1, source_target_pairs={{0,8},{2,10},{4,12},{6,14},{8,0},{10,2},{12,4},{14,6},{1,9},{3,11}... | collective-permute-start | bytes 786440 | tf_op jit(solution)/shard_map/ppermute | solution.py:261
  30.1 6.9 %collective-permute-start.42 = (bf16[256,512]{1,0:T(8,128)(2,1)S(1)}, bf16[256,512]{1,0:T(8,128)(2,1)S(1)}, u32[]{:S(2)}, u32[]{:S(2)}) collective-permute-start(bf16[256,512]{1,0:T(8,128)(2,1)S(1)} %get-tuple-element.88), channel_id=1, source_target_pairs={{0,2},{2,0},{4,6},{6,4},{8,10},{10,8},{12,14},{14,12},{1,3},{3,1},... | collective-permute-start | bytes 786440 | tf_op jit(solution)/shard_map/ppermute | solution.py:215
  32.1 13.0 %collective-permute-start.3 = (bf16[256,512]{1,0:T(8,128)(2,1)S(1)}, bf16[256,512]{1,0:T(8,128)(2,1)S(1)}, u32[]{:S(2)}, u32[]{:S(2)}) collective-permute-start(bf16[256,512]{1,0:T(8,128)(2,1)S(1)} %get-tuple-element.100), channel_id=1, source_target_pairs={{0,4},{2,6},{4,0},{6,2},{8,12},{10,14},{12,8},{14,10},{1,5},{3,7},... | collective-permute-start | bytes 786440 | tf_op jit(solution)/shard_map/ppermute | solution.py:215
  37.0 8.7 %collective-permute-start.7 = (bf16[256,512]{1,0:T(8,128)(2,1)S(1)}, bf16[256,512]{1,0:T(8,128)(2,1)S(1)}, u32[]{:S(2)}, u32[]{:S(2)}) collective-permute-start(bf16[256,512]{1,0:T(8,128)(2,1)S(1)} %collective-permute-done.6), channel_id=1, source_target_pairs={{0,16},{16,0},{1,17},{17,1},{2,18},{18,2},{3,19},{19,3},{4,20},{20... | collective-permute-start | bytes 786440 | tf_op jit(solution)/shard_map/ppermute | solution.py:215
  38.4 9.0 %collective-permute-start.46 = (bf16[2,2,64,512]{3,2,0,1:T(8,128)(2,1)S(1)}, bf16[2,2,64,512]{3,2,0,1:T(8,128)(2,1)S(1)}, u32[]{:S(2)}, u32[]{:S(2)}) collective-permute-start(bf16[2,2,64,512]{3,2,0,1:T(8,128)(2,1)S(1)} %bitcast.404), channel_id=1, source_target_pairs={{0,1},{1,0},{2,3},{3,2},{4,5},{5,4},{6,7},{7,6},{8,9},{9,8},{10,11... | collective-permute-start | bytes 786440 | tf_op jit(solution)/shard_map/ppermute | solution.py:215
  45.7 10.6 %collective-permute-start.12 = (bf16[2,2,64,512]{3,2,1,0:T(8,128)(2,1)S(1)}, bf16[2,2,64,512]{3,2,1,0:T(8,128)(2,1)S(1)}, u32[]{:S(2)}, u32[]{:S(2)}) collective-permute-start(bf16[2,2,64,512]{3,2,1,0:T(8,128)(2,1)S(1)} %dynamic-slice_bitcast_fusion.1), channel_id=1, source_target_pairs={{0,1},{1,0},{2,3},{3,2},{4,5},{5,4},{6,7},{7,6},{8,9},{9,8},{10,11... | collective-permute-start | bytes 786440 | tf_op jit(solution)/shard_map/ppermute | solution.py:215
  46.6 11.0 %collective-permute-start.8 = (bf16[2,2,64,512]{3,2,0,1:T(8,128)(2,1)S(1)}, bf16[2,2,64,512]{3,2,0,1:T(8,128)(2,1)S(1)}, u32[]{:S(2)}, u32[]{:S(2)}) collective-permute-start(bf16[2,2,64,512]{3,2,0,1:T(8,128)(2,1)S(1)} %bitcast.403), channel_id=1, source_target_pairs={{0,1},{1,0},{2,3},{3,2},{4,5},{5,4},{6,7},{7,6},{8,9},{9,8},{10,11... | collective-permute-start | bytes 786440 | tf_op jit(solution)/shard_map/ppermute | solution.py:215
  47.1 8.3 %collective-permute-start.38 = (bf16[256,512]{1,0:T(8,128)(2,1)S(1)}, bf16[256,512]{1,0:T(8,128)(2,1)S(1)}, u32[]{:S(2)}, u32[]{:S(2)}) collective-permute-start(bf16[256,512]{1,0:T(8,128)(2,1)S(1)} %collective-permute-done.37), channel_id=1, source_target_pairs={{0,16},{16,0},{1,17},{17,1},{2,18},{18,2},{3,19},{19,3},{4,20},{20... | collective-permute-start | bytes 786440 | tf_op jit(solution)/shard_map/ppermute | solution.py:215
  47.6 17.6 %collective-permute-start.47 = (bf16[2,64,512]{2,1,0:T(8,128)(2,1)S(1)}, bf16[2,64,512]{2,1,0:T(8,128)(2,1)S(1)}, u32[]{:S(2)}, u32[]{:S(2)}) collective-permute-start(bf16[2,64,512]{2,1,0:T(8,128)(2,1)S(1)} %slice_bitcast_fusion.12), channel_id=1, source_target_pairs={{0,2},{2,0},{4,6},{6,4},{8,10},{10,8},{12,14},{14,12},{1,3},{3,1},... | collective-permute-start | bytes 393224 | tf_op jit(solution)/shard_map/ppermute | solution.py:215
  56.2 15.2 %collective-permute-start.43 = (bf16[2,2,64,512]{3,2,1,0:T(8,128)(2,1)S(1)}, bf16[2,2,64,512]{3,2,1,0:T(8,128)(2,1)S(1)}, u32[]{:S(2)}, u32[]{:S(2)}) collective-permute-start(bf16[2,2,64,512]{3,2,1,0:T(8,128)(2,1)S(1)} %dynamic-slice_bitcast_fusion), channel_id=1, source_target_pairs={{0,1},{1,0},{2,3},{3,2},{4,5},{5,4},{6,7},{7,6},{8,9},{9,8},{10,11... | collective-permute-start | bytes 786440 | tf_op jit(solution)/shard_map/ppermute | solution.py:215
  65.2 17.6 %collective-permute-start.48 = (bf16[64,512]{1,0:T(8,128)(2,1)S(1)}, bf16[64,512]{1,0:T(8,128)(2,1)S(1)}, u32[]{:S(2)}, u32[]{:S(2)}) collective-permute-start(bf16[64,512]{1,0:T(8,128)(2,1)S(1)} %slice_bitcast_fusion.28), channel_id=1, source_target_pairs={{0,4},{2,6},{4,0},{6,2},{8,12},{10,14},{12,8},{14,10},{1,5},{3,7},... | collective-permute-start | bytes 196616 | tf_op jit(solution)/shard_map/ppermute | solution.py:215
  71.5 6.4 %collective-permute-start.44 = (bf16[2,64,512]{2,1,0:T(8,128)(2,1)S(1)}, bf16[2,64,512]{2,1,0:T(8,128)(2,1)S(1)}, u32[]{:S(2)}, u32[]{:S(2)}) collective-permute-start(bf16[2,64,512]{2,1,0:T(8,128)(2,1)S(1)} %slice_bitcast_fusion.14), channel_id=1, source_target_pairs={{0,4},{2,6},{4,0},{6,2},{8,12},{10,14},{12,8},{14,10},{1,5},{3,7},... | collective-permute-start | bytes 393224 | tf_op jit(solution)/shard_map/ppermute | solution.py:215
  74.2 7.8 %collective-permute-start.16 = (bf16[2,64,512]{2,1,0:T(8,128)(2,1)S(1)}, bf16[2,64,512]{2,1,0:T(8,128)(2,1)S(1)}, u32[]{:S(2)}, u32[]{:S(2)}) collective-permute-start(bf16[2,64,512]{2,1,0:T(8,128)(2,1)S(1)} %get-tuple-element.188), channel_id=1, source_target_pairs={{0,4},{2,6},{4,0},{6,2},{8,12},{10,14},{12,8},{14,10},{1,5},{3,7},... | collective-permute-start | bytes 393224 | tf_op jit(solution)/shard_map/ppermute | solution.py:215
  80.8 6.4 %collective-permute-start.21 = (bf16[2,2,64,512]{3,2,1,0:T(8,128)(2,1)S(1)}, bf16[2,2,64,512]{3,2,1,0:T(8,128)(2,1)S(1)}, u32[]{:S(2)}, u32[]{:S(2)}) collective-permute-start(bf16[2,2,64,512]{3,2,1,0:T(8,128)(2,1)S(1)} %get-tuple-element.160), channel_id=1, source_target_pairs={{0,4},{2,6},{4,0},{6,2},{8,12},{10,14},{12,8},{14,10},{1,5},{3,7},... | collective-permute-start | bytes 786440 | tf_op jit(solution)/shard_map/ppermute | solution.py:215
  82.0 6.4 %collective-permute-start.17 = (bf16[2,2,64,512]{3,2,1,0:T(8,128)(2,1)S(1)}, bf16[2,2,64,512]{3,2,1,0:T(8,128)(2,1)S(1)}, u32[]{:S(2)}, u32[]{:S(2)}) collective-permute-start(bf16[2,2,64,512]{3,2,1,0:T(8,128)(2,1)S(1)} %get-tuple-element.158), channel_id=1, source_target_pairs={{0,2},{2,0},{4,6},{6,4},{8,10},{10,8},{12,14},{14,12},{1,3},{3,1},... | collective-permute-start | bytes 786440 | tf_op jit(solution)/shard_map/ppermute | solution.py:215
  87.3 9.0 %collective-permute-start.22 = (bf16[2,2,2,64,512]{4,3,2,0,1:T(8,128)(2,1)S(1)}, bf16[2,2,2,64,512]{4,3,2,0,1:T(8,128)(2,1)}, u32[]{:S(2)}, u32[]{:S(2)}) collective-permute-start(bf16[2,2,2,64,512]{4,3,2,0,1:T(8,128)(2,1)S(1)} %get-tuple-element.96), channel_id=1, source_target_pairs={{0,1},{1,0},{2,3},{3,2},{4,5},{5,4},{6,7},{7,6},{8,9},{9,8},{10,11... | collective-permute-start | bytes 1572872 | tf_op jit(solution)/shard_map/ppermute | solution.py:215
  89.3 8.3 %collective-permute-start.18 = (bf16[2,2,2,64,512]{4,3,2,1,0:T(8,128)(2,1)}, bf16[2,2,2,64,512]{4,3,2,1,0:T(8,128)(2,1)}, u32[]{:S(2)}, u32[]{:S(2)}) collective-permute-start(bf16[2,2,2,64,512]{4,3,2,1,0:T(8,128)(2,1)} %get-tuple-element.94), channel_id=1, source_target_pairs={{0,1},{1,0},{2,3},{3,2},{4,5},{5,4},{6,7},{7,6},{8,9},{9,8},{10,11... | collective-permute-start | bytes 1572872 | tf_op jit(solution)/shard_map/ppermute | solution.py:215
  95.4 32.0 %collective-permute-start.51 = (bf16[2,2,64,512]{3,2,1,0:T(8,128)(2,1)S(1)}, bf16[2,2,64,512]{3,2,1,0:T(8,128)(2,1)S(1)}, u32[]{:S(2)}, u32[]{:S(2)}) collective-permute-start(bf16[2,2,64,512]{3,2,1,0:T(8,128)(2,1)S(1)} %get-tuple-element.136), channel_id=1, source_target_pairs={{0,4},{2,6},{4,0},{6,2},{8,12},{10,14},{12,8},{14,10},{1,5},{3,7},... | collective-permute-start | bytes 786440 | tf_op jit(solution)/shard_map/ppermute | solution.py:215
  120.4 22.6 %collective-permute-start.23 = (bf16[2,2,2,64,1024]{4,3,2,0,1:T(8,128)(2,1)}, bf16[2,2,2,64,1024]{4,3,2,0,1:T(8,128)(2,1)}, u32[]{:S(2)}, u32[]{:S(2)}) collective-permute-start(bf16[2,2,2,64,1024]{4,3,2,0,1:T(8,128)(2,1)} %copy.92), channel_id=1, source_target_pairs={{0,1},{1,0},{2,3},{3,2},{4,5},{5,4},{6,7},{7,6},{8,9},{9,8},{10,11... | collective-permute-start | bytes 3145736 | tf_op jit(solution)/shard_map/ppermute | solution.py:215
  120.4 6.8 %collective-permute-start.53 = (bf16[64,512]{1,0:T(8,128)(2,1)S(1)}, bf16[64,512]{1,0:T(8,128)(2,1)S(1)}, u32[]{:S(2)}, u32[]{:S(2)}) collective-permute-start(bf16[64,512]{1,0:T(8,128)(2,1)S(1)} %get-tuple-element.110), channel_id=1, source_target_pairs={{0,8},{2,10},{4,12},{6,14},{8,0},{10,2},{12,4},{14,6},{1,9},{3,11}... | collective-permute-start | bytes 196616 | tf_op jit(solution)/shard_map/ppermute | solution.py:261
  128.4 13.3 %collective-permute-start.52 = (bf16[2,2,2,64,512]{4,3,2,0,1:T(8,128)(2,1)}, bf16[2,2,2,64,512]{4,3,2,0,1:T(8,128)(2,1)}, u32[]{:S(2)}, u32[]{:S(2)}) collective-permute-start(bf16[2,2,2,64,512]{4,3,2,0,1:T(8,128)(2,1)} %get-tuple-element.82), channel_id=1, source_target_pairs={{0,1},{1,0},{2,3},{3,2},{4,5},{5,4},{6,7},{7,6},{8,9},{9,8},{10,11... | collective-permute-start | bytes 1572872 | tf_op jit(solution)/shard_map/ppermute | solution.py:215
  133.2 7.4 %collective-permute-start.55 = (bf16[2,2,64,512]{3,2,1,0:T(8,128)(2,1)}, bf16[2,2,64,512]{3,2,1,0:T(8,128)(2,1)}, u32[]{:S(2)}, u32[]{:S(2)}) collective-permute-start(bf16[2,2,64,512]{3,2,1,0:T(8,128)(2,1)} %get-tuple-element.138), channel_id=1, source_target_pairs={{0,2},{2,0},{4,6},{6,4},{8,10},{10,8},{12,14},{14,12},{1,3},{3,1},... | collective-permute-start | bytes 786440 | tf_op jit(solution)/shard_map/ppermute | solution.py:215
  144.7 8.8 %collective-permute-start.24 = (bf16[2,2,64,512]{3,2,1,0:T(8,128)(2,1)S(1)}, bf16[2,2,64,512]{3,2,1,0:T(8,128)(2,1)S(1)}, u32[]{:S(2)}, u32[]{:S(2)}) collective-permute-start(bf16[2,2,64,512]{3,2,1,0:T(8,128)(2,1)S(1)} %slice_bitcast_fusion.6), channel_id=1, source_target_pairs={{0,4},{2,6},{4,0},{6,2},{8,12},{10,14},{12,8},{14,10},{1,5},{3,7},... | collective-permute-start | bytes 786440 | tf_op jit(solution)/shard_map/ppermute | solution.py:215
  145.4 8.5 %collective-permute-start.27 = (bf16[2,2,64,512]{3,2,1,0:T(8,128)(2,1)S(1)}, bf16[2,2,64,512]{3,2,1,0:T(8,128)(2,1)S(1)}, u32[]{:S(2)}, u32[]{:S(2)}) collective-permute-start(bf16[2,2,64,512]{3,2,1,0:T(8,128)(2,1)S(1)} %slice_bitcast_fusion.4), channel_id=1, source_target_pairs={{0,2},{2,0},{4,6},{6,4},{8,10},{10,8},{12,14},{14,12},{1,3},{3,1},... | collective-permute-start | bytes 786440 | tf_op jit(solution)/shard_map/ppermute | solution.py:215
  159.1 8.2 %collective-permute-start.26 = (bf16[64,512]{1,0:T(8,128)(2,1)S(1)}, bf16[64,512]{1,0:T(8,128)(2,1)S(1)}, u32[]{:S(2)}, u32[]{:S(2)}) collective-permute-start(bf16[64,512]{1,0:T(8,128)(2,1)S(1)} %slice_bitcast_fusion.35), channel_id=1, source_target_pairs={{8,0},{10,2},{12,4},{14,6},{0,8},{2,10},{4,12},{6,14},{9,1},{11,3}... | collective-permute-start | bytes 196616 | tf_op jit(solution)/shard_map/ppermute | solution.py:267
  161.0 6.3 %collective-permute-start.29 = (bf16[64,512]{1,0:T(8,128)(2,1)S(1)}, bf16[64,512]{1,0:T(8,128)(2,1)S(1)}, u32[]{:S(2)}, u32[]{:S(2)}) collective-permute-start(bf16[64,512]{1,0:T(8,128)(2,1)S(1)} %slice_bitcast_fusion.33), channel_id=1, source_target_pairs={{8,0},{10,2},{12,4},{14,6},{0,8},{2,10},{4,12},{6,14},{9,1},{11,3}... | collective-permute-start | bytes 196616 | tf_op jit(solution)/shard_map/ppermute | solution.py:267
  167.4 19.9 %collective-permute-start.34 = (bf16[64,512]{1,0:T(8,128)(2,1)S(1)}, bf16[64,512]{1,0:T(8,128)(2,1)S(1)}, u32[]{:S(2)}, u32[]{:S(2)}) collective-permute-start(bf16[64,512]{1,0:T(8,128)(2,1)S(1)} %get-tuple-element.111), channel_id=1, source_target_pairs={{0,4},{2,6},{4,0},{6,2},{8,12},{10,14},{12,8},{14,10},{1,5},{3,7},... | collective-permute-start | bytes 196616 | tf_op jit(solution)/shard_map/ppermute | solution.py:215
  190.8 20.2 %collective-permute-start.57 = (bf16[2,2,2,64,1024]{4,3,2,1,0:T(8,128)(2,1)S(1)}, bf16[2,2,2,64,1024]{4,3,2,1,0:T(8,128)(2,1)S(1)}, u32[]{:S(2)}, u32[]{:S(2)}) collective-permute-start(bf16[2,2,2,64,1024]{4,3,2,1,0:T(8,128)(2,1)S(1)} %bitcast.387), channel_id=1, source_target_pairs={{0,1},{1,0},{2,3},{3,2},{4,5},{5,4},{6,7},{7,6},{8,9},{9,8},{10,11... | collective-permute-start | bytes 3145736 | tf_op jit(solution)/shard_map/ppermute | solution.py:215
  192.4 13.0 %collective-permute-start.36 = (bf16[2,2,64,512]{3,2,0,1:T(8,128)(2,1)S(1)}, bf16[2,2,64,512]{3,2,0,1:T(8,128)(2,1)S(1)}, u32[]{:S(2)}, u32[]{:S(2)}) collective-permute-start(bf16[2,2,64,512]{3,2,0,1:T(8,128)(2,1)S(1)} %get-tuple-element.148), channel_id=1, source_target_pairs={{0,1},{1,0},{2,3},{3,2},{4,5},{5,4},{6,7},{7,6},{8,9},{9,8},{10,11... | collective-permute-start | bytes 786440 | tf_op jit(solution)/shard_map/ppermute | solution.py:215
  195.0 10.5 %collective-permute-start.32 = (bf16[2,2,64,512]{3,2,1,0:T(8,128)(2,1)S(1)}, bf16[2,2,64,512]{3,2,1,0:T(8,128)(2,1)S(1)}, u32[]{:S(2)}, u32[]{:S(2)}) collective-permute-start(bf16[2,2,64,512]{3,2,1,0:T(8,128)(2,1)S(1)} %get-tuple-element.156), channel_id=1, source_target_pairs={{0,1},{1,0},{2,3},{3,2},{4,5},{5,4},{6,7},{7,6},{8,9},{9,8},{10,11... | collective-permute-start | bytes 786440 | tf_op jit(solution)/shard_map/ppermute | solution.py:215
  207.9 14.5 %collective-permute-start.39 = (bf16[256,512]{0,1:T(8,128)(2,1)S(1)}, bf16[256,512]{0,1:T(8,128)(2,1)S(1)}, u32[]{:S(2)}, u32[]{:S(2)}) collective-permute-start(bf16[256,512]{0,1:T(8,128)(2,1)S(1)} %slice.292), channel_id=1, source_target_pairs={{0,4},{2,6},{4,0},{6,2},{8,12},{10,14},{12,8},{14,10},{1,5},{3,7},... | collective-permute-start | bytes 786440 | tf_op jit(solution)/shard_map/ppermute | solution.py:215
  209.1 27.1 %collective-permute-start.77 = (bf16[512,512]{1,0:T(8,128)(2,1)S(1)}, bf16[512,512]{1,0:T(8,128)(2,1)S(1)}, u32[]{:S(2)}, u32[]{:S(2)}) collective-permute-start(bf16[512,512]{1,0:T(8,128)(2,1)S(1)} %convolution_convert_fusion.1), channel_id=1, source_target_pairs={{8,0},{10,2},{12,4},{14,6},{0,8},{2,10},{4,12},{6,14},{9,1},{11,3}... | collective-permute-start | bytes 1572872 | tf_op jit(solution)/shard_map/ppermute | solution.py:267
  211.4 11.6 %collective-permute-start.61 = (bf16[2,2,64,512]{3,2,1,0:T(8,128)(2,1)S(1)}, bf16[2,2,64,512]{3,2,1,0:T(8,128)(2,1)S(1)}, u32[]{:S(2)}, u32[]{:S(2)}) collective-permute-start(bf16[2,2,64,512]{3,2,1,0:T(8,128)(2,1)S(1)} %slice_bitcast_fusion), channel_id=1, source_target_pairs={{0,2},{2,0},{4,6},{6,4},{8,10},{10,8},{12,14},{14,12},{1,3},{3,1},... | collective-permute-start | bytes 786440 | tf_op jit(solution)/shard_map/ppermute | solution.py:215
  212.4 19.4 %collective-permute-start.58 = (bf16[2,2,64,512]{3,2,1,0:T(8,128)(2,1)S(1)}, bf16[2,2,64,512]{3,2,1,0:T(8,128)(2,1)S(1)}, u32[]{:S(2)}, u32[]{:S(2)}) collective-permute-start(bf16[2,2,64,512]{3,2,1,0:T(8,128)(2,1)S(1)} %slice_bitcast_fusion.2), channel_id=1, source_target_pairs={{0,4},{2,6},{4,0},{6,2},{8,12},{10,14},{12,8},{14,10},{1,5},{3,7},... | collective-permute-start | bytes 786440 | tf_op jit(solution)/shard_map/ppermute | solution.py:215
  222.5 20.5 %collective-permute-start.40 = (bf16[128,1024]{0,1:T(8,128)(2,1)S(1)}, bf16[128,1024]{0,1:T(8,128)(2,1)S(1)}, u32[]{:S(2)}, u32[]{:S(2)}) collective-permute-start(bf16[128,1024]{0,1:T(8,128)(2,1)S(1)} %pad_maximum_fusion.19), channel_id=1, source_target_pairs={{0,2},{2,0},{4,6},{6,4},{8,10},{10,8},{12,14},{14,12},{1,3},{3,1},... | collective-permute-start | bytes 786440 | tf_op jit(solution)/shard_map/ppermute | solution.py:215
  233.6 7.5 %collective-permute-start.62 = (bf16[2,64,512]{2,1,0:T(8,128)(2,1)S(1)}, bf16[2,64,512]{2,1,0:T(8,128)(2,1)S(1)}, u32[]{:S(2)}, u32[]{:S(2)}) collective-permute-start(bf16[2,64,512]{2,1,0:T(8,128)(2,1)S(1)} %slice_bitcast_fusion.8), channel_id=1, source_target_pairs={{0,4},{2,6},{4,0},{6,2},{8,12},{10,14},{12,8},{14,10},{1,5},{3,7},... | collective-permute-start | bytes 393224 | tf_op jit(solution)/shard_map/ppermute | solution.py:215
  236.7 11.9 %collective-permute-start.78 = (bf16[256,256]{1,0:T(8,128)(2,1)S(1)}, bf16[256,256]{1,0:T(8,128)(2,1)S(1)}, u32[]{:S(2)}, u32[]{:S(2)}) collective-permute-start(bf16[256,256]{1,0:T(8,128)(2,1)S(1)} %get-tuple-element.117), channel_id=1, source_target_pairs={{0,4},{2,6},{4,0},{6,2},{8,12},{10,14},{12,8},{14,10},{1,5},{3,7},... | collective-permute-start | bytes 393224 | tf_op jit(solution)/shard_map/ppermute | solution.py:215
  236.9 13.1 %collective-permute-start.80 = (bf16[256,256]{1,0:T(8,128)(2,1)S(1)}, bf16[256,256]{1,0:T(8,128)(2,1)S(1)}, u32[]{:S(2)}, u32[]{:S(2)}) collective-permute-start(bf16[256,256]{1,0:T(8,128)(2,1)S(1)} %pad_maximum_fusion.35), channel_id=1, source_target_pairs={{0,2},{2,0},{4,6},{6,4},{8,10},{10,8},{12,14},{14,12},{1,3},{3,1},... | collective-permute-start | bytes 393224 | tf_op jit(solution)/shard_map/ppermute | solution.py:215
  237.9 6.8 %collective-permute-start.60 = (bf16[64,512]{1,0:T(8,128)(2,1)S(1)}, bf16[64,512]{1,0:T(8,128)(2,1)S(1)}, u32[]{:S(2)}, u32[]{:S(2)}) collective-permute-start(bf16[64,512]{1,0:T(8,128)(2,1)S(1)} %slice_bitcast_fusion.27), channel_id=1, source_target_pairs={{8,0},{10,2},{12,4},{14,6},{0,8},{2,10},{4,12},{6,14},{9,1},{11,3}... | collective-permute-start | bytes 196616 | tf_op jit(solution)/shard_map/ppermute | solution.py:267
  261.5 14.1 %collective-permute-start.70 = (bf16[256,512]{0,1:T(8,128)(2,1)S(1)}, bf16[256,512]{0,1:T(8,128)(2,1)S(1)}, u32[]{:S(2)}, u32[]{:S(2)}) collective-permute-start(bf16[256,512]{0,1:T(8,128)(2,1)S(1)} %slice.321), channel_id=1, source_target_pairs={{0,4},{2,6},{4,0},{6,2},{8,12},{10,14},{12,8},{14,10},{1,5},{3,7},... | collective-permute-start | bytes 786440 | tf_op jit(solution)/shard_map/ppermute | solution.py:215
  262.7 26.3 %collective-permute-start.72 = (bf16[512,512]{1,0:T(8,128)(2,1)S(1)}, bf16[512,512]{1,0:T(8,128)(2,1)S(1)}, u32[]{:S(2)}, u32[]{:S(2)}) collective-permute-start(bf16[512,512]{1,0:T(8,128)(2,1)S(1)} %convolution_convert_fusion.3), channel_id=1, source_target_pairs={{8,0},{10,2},{12,4},{14,6},{0,8},{2,10},{4,12},{6,14},{9,1},{11,3}... | collective-permute-start | bytes 1572872 | tf_op jit(solution)/shard_map/ppermute | solution.py:267
  275.7 16.1 %collective-permute-start.71 = (bf16[128,1024]{0,1:T(8,128)(2,1)S(1)}, bf16[128,1024]{0,1:T(8,128)(2,1)S(1)}, u32[]{:S(2)}, u32[]{:S(2)}) collective-permute-start(bf16[128,1024]{0,1:T(8,128)(2,1)S(1)} %pad_maximum_fusion.24), channel_id=1, source_target_pairs={{0,2},{2,0},{4,6},{6,4},{8,10},{10,8},{12,14},{14,12},{1,3},{3,1},... | collective-permute-start | bytes 786440 | tf_op jit(solution)/shard_map/ppermute | solution.py:215
  (73 other events, 466.6 us)

commit v4 on v2

--- a/solution.py
+++ b/solution.py
@@ -206,139 +206,134 @@
     shard = down_weight.shape[1]
 
     nh = n_expert // 4
-    h, c, y = own // 4, own // 2 % 2, own % 2
+    h, q = own // 4, own % 4
+    cols = latent // nh
     shared = n_group % 2 == 0
     g = lax.axis_index("group") % 2
 
-    def swapper(axis, size, bit):
-        perm = [(i, i ^ bit) for i in range(size)]
-        return lambda v: lax.ppermute(v, axis, perm)
-
-    y_swap = swapper("expert", n_expert, 1)
-    c_swap = swapper("expert", n_expert, 2)
-    t_swap = swapper("tensor", 2, 1)
-    g_swap = swapper("group", n_group, 1)
-    h_up = [(e, (e + 4) % n_expert) for e in range(n_expert)]
-    h_down = [((e + 4) % n_expert, e) for e in range(n_expert)]
-
-    def add(a, b):
-        return (a.astype(f32) + b.astype(f32)).astype(bf16)
-
-    def turn(v, axis):
-        blocks = jnp.split(v, nh, axis=axis)
-        orders = [
-            jnp.concatenate([blocks[(i - k) % nh] for k in range(nh)], axis=axis)
-            for i in range(nh)
-        ]
-        result = orders[0]
-        for i in range(1, nh):
-            result = jnp.where(h == i, orders[i], result)
+    def to_peer(v, r):
+        return lax.ppermute(v, "expert", [(e, e ^ r) for e in range(n_expert)])
+
+    def t_swap(v):
+        return lax.ppermute(v, "tensor", [(0, 1), (1, 0)])
+
+    def g_swap(v):
+        return lax.ppermute(v, "group", [(i, i ^ 1) for i in range(n_group)])
+
+    def up(v):
+        return lax.ppermute(v, "expert", [(e, (e + 4) % n_expert) for e in range(n_expert)])
+
+    def down(v):
+        return lax.ppermute(v, "expert", [((e + 4) % n_expert, e) for e in range(n_expert)])
+
+    def add(*terms):
+        return sum(v.astype(f32) for v in terms).astype(bf16)
+
+    def after(v, *done):
+        return lax.optimization_barrier((v, *done))[0]
+
+    def turn(blocks):
+        result = []
+        for k in range(nh):
+            block = blocks[-k % nh]
+            for i in range(1, nh):
+                block = jnp.where(h == i, blocks[(i - k) % nh], block)
+            result.append(block)
         return result
+
+    def by_quarter(parts):
+        low = [jnp.where(q % 2 == 0, parts[i], parts[i ^ 1]) for i in range(4)]
+        return [jnp.where(q < 2, low[i], low[i ^ 2]) for i in range(4)]
 
     def flip(v, index, axis):
         first, second = jnp.split(v, 2, axis=axis)
         return jnp.where(index == 0, v, jnp.concatenate([second, first], axis=axis))
 
-    def pick(v, index, axis):
-        mine = lax.dynamic_index_in_dim(v, index, axis, keepdims=False)
-        other = lax.dynamic_index_in_dim(v, 1 - index, axis, keepdims=False)
-        return mine, other
+    def exchange(block_for):
+        return [block_for(0)] + [to_peer(block_for(r), r) for r in (1, 2, 3)]
+
+    def together(*values):
+        return lax.optimization_barrier(values)
 
     def gather_h(v):
         parts = [v]
         for _ in range(nh - 1):
-            parts.append(lax.ppermute(parts[-1], "expert", h_up))
+            parts.append(up(parts[-1]))
         return parts
 
-    def scatter_h(parts):
-        total = parts[nh - 1]
+    def square_rows(v):
+        parts = exchange(
+            lambda r: lax.dynamic_slice_in_dim(v, (q ^ r) * quarter_d, quarter_d, 1)
+        )
+        return jnp.concatenate(parts, axis=0)
+
+    def square_weight(v):
+        size = quarter_d // 2 if shared else quarter_d
+        first = g * size if shared else 0
+        parts = exchange(
+            lambda r: lax.dynamic_slice_in_dim(v, (q ^ r) * quarter_d + first, size, 0)
+        )
+        return jnp.concatenate(by_quarter(parts), axis=1), parts[3]
+
+    def all_features(v):
+        return flip(jnp.concatenate([v, g_swap(v)], axis=0), g, 0) if shared else v
+
+    def project(rows, weights):
+        blocks = []
+        for weight in weights:
+            part = dot(rows, weight).astype(bf16).reshape(4, 2, half_rows, cols)
+            mine = lax.dynamic_index_in_dim(part, t, 1, keepdims=False)
+            other = lax.dynamic_index_in_dim(part, 1 - t, 1, keepdims=False)
+            part = add(mine, t_swap(other))
+            blocks.append(add(*exchange(lambda r: part[r])))
+        return jnp.concatenate(turn(blocks), axis=1)
+
+    def all_rows(part):
+        return jnp.stack([part, t_swap(part)]).reshape(-1, latent)
+
+    def sum_tensor(part):
+        part = part.reshape(2, 4, nh, half_rows, latent)
+        return add(part[0], t_swap(part[1]))
+
+    def sum_squares(part):
+        if nh == 2:
+            return part, up(part)
+        total = part[nh - 1]
         for k in range(nh - 2, -1, -1):
-            total = add(lax.ppermute(total, "expert", h_down), parts[k])
-        return total
-
-    def square_rows(v):
-        mine, other = pick(v.reshape(tok_rows, 2, 2 * quarter_d), c, 1)
-        v = jnp.concatenate([mine, c_swap(other)], axis=0)
-        mine, other = pick(v.reshape(2 * tok_rows, 2, quarter_d), y, 1)
-        received = y_swap(other)
-        parts = [mine[:tok_rows], received[:tok_rows], mine[tok_rows:], received[tok_rows:]]
-        return jnp.concatenate(parts, axis=0)
-
-    def square_weight(v):
-        mine, other = pick(v.reshape(2, 2, quarter_d, shard), y, 1)
-        v = flip(jnp.concatenate([mine, y_swap(other)], axis=2), y, 2)
-        mine, other = pick(v, c, 0)
-        block = flip(jnp.concatenate([mine, c_swap(other)], axis=1), c, 1)
-        if not shared:
-            return gather_h(block)
-        mine, _ = pick(block.reshape(2, quarter_d // 2, 4 * shard), g, 0)
-        parts = [block]
-        for _ in range(nh - 1):
-            mine = lax.ppermute(mine, "expert", h_up)
-            parts.append(flip(jnp.concatenate([mine, g_swap(mine)], axis=0), g, 0))
-        return parts
-
-    def project(rows, weights):
-        part = jnp.concatenate([dot(rows, w).astype(bf16) for w in weights], axis=1)
-        mine, other = pick(part.reshape(2, 2, 2, half_rows, latent), t, 2)
-        part = add(mine, t_swap(other))
-        part = add(part[0], c_swap(part[1]))
-        part = add(part[0], y_swap(part[1]))
-        return turn(part, 1)
-
-    def gather_first(part):
-        part = jnp.stack(gather_h(part))
-        part = jnp.stack([part, c_swap(part)])
-        part = jnp.stack([part, y_swap(part)])
-        part = jnp.stack([part, t_swap(part)])
-        return part.reshape(-1, latent)
-
-    def gather_second(part):
-        part = jnp.stack([part, y_swap(part)])
-        part = jnp.stack(gather_h(part), axis=1)
-        part = jnp.stack([part, c_swap(part)], axis=1)
-        part = jnp.stack([part, t_swap(part)])
-        return part.reshape(-1, latent)
-
-    def collect(part):
-        part = part.reshape(2, 2, 2, nh, half_rows, latent)
-        part = add(part[0], t_swap(part[1]))
-        part = add(part[0], y_swap(part[1]))
-        part = add(part[0], c_swap(part[1]))
-        part = turn(scatter_h([part[k] for k in range(nh)]), 1)
-        part = jnp.stack([part, y_swap(part)])
-        part = jnp.stack([part, c_swap(part)])
-        part = flip(jnp.stack([part, t_swap(part)], axis=2), t, 2)
-        return part.reshape(4 * tok_rows, latent)
-
-    def finish(part, rows, weights):
-        cols = latent // nh
-        grads = [dot(rows, part[:, k * cols : (k + 1) * cols], TN).astype(bf16) for k in range(nh)]
-        grad = scatter_h(grads)
-        mine, other = pick(grad.reshape(quarter_d, 2, 2 * shard), c, 1)
-        grad = jnp.stack([mine, c_swap(other)])
-        mine, other = pick(grad.reshape(2, quarter_d, 2, shard), y, 2)
-        grad = jnp.stack([mine, y_swap(other)], axis=1)
-        grad = flip(flip(grad, c, 0), y, 1).reshape(4 * quarter_d, shard).astype(f32)
-
-        whole = sum(dot(part[:, k * cols : (k + 1) * cols], weights[k], NT) for k in range(nh))
-        whole = whole.astype(bf16)
-        theirs = c_swap(whole[2 * tok_rows :])
-        pieces = [whole[:tok_rows], theirs[:tok_rows]]
-        sent = jnp.concatenate([whole[tok_rows : 2 * tok_rows], theirs[tok_rows:]], axis=1)
-        received = y_swap(sent)
-        result = [
-            flip(jnp.concatenate([p, r], axis=1), y, 1)
-            for p, r in zip(pieces, jnp.split(received, 2, axis=1))
-        ]
-        return flip(jnp.concatenate(result, axis=1), c, 1), grad
+            total = add(down(total), part[k])
+        return part, jnp.stack(gather_h(total))
+
+    def join_squares(part, theirs):
+        rows = [add(part[0], theirs[1]), add(part[1], theirs[0])] if nh == 2 else list(theirs)
+        split = [turn(jnp.split(v, nh, axis=1)) for v in rows]
+        return jnp.concatenate(split[0] + [v[0] for v in split[1:]], axis=1)
+
+    def square_blocks(part):
+        part = flip(jnp.stack([part, t_swap(part)], axis=1), t, 1)
+        return jnp.split(part.reshape(4 * tok_rows, -1), 2 * nh - 1, axis=1)
+
+    def products(blocks, rows, weights):
+        grad = sum(dot(v, block, TN) for v, block in zip(rows, blocks[:1] + blocks[nh:]))
+        whole = sum(dot(block, weight, NT) for block, weight in zip(blocks, weights))
+        return grad.astype(bf16), whole.astype(bf16)
+
+    def send_products(grad, whole):
+        whole = whole.reshape(4, tok_rows, quarter_d)
+        grads = exchange(lambda r: lax.dynamic_slice_in_dim(grad, (q ^ r) * shard, shard, 1))
+        return grads, exchange(lambda r: whole[r])
+
+    def join_products(grads, wholes):
+        grad = jnp.concatenate(by_quarter(grads), axis=0).astype(f32)
+        return jnp.concatenate(by_quarter(wholes), axis=1), grad
 
     local_ids = own * exp_local + jnp.arange(exp_local, dtype=jnp.int32)
     hit = routes[:, :, None] == local_ids[None, None, :]
     gate_all = jnp.sum(jnp.where(hit, gates[:, :, None], 0), axis=1).astype(f32) * gate_unit
-    gate_all = turn(gate_all.reshape(nh, 2, 2, 2, half_rows, exp_local), 0)
-    gate_all = flip(flip(flip(gate_all, c, 1), y, 2), t, 3)
-    gate_columns = gate_all.transpose(3, 2, 1, 0, 4, 5).reshape(-1, exp_local)
+    gate_all = gate_all.reshape(nh, 4, 2, half_rows, exp_local)
+    gate_all = jnp.stack(turn(list(gate_all)))
+    gate_all = jnp.stack(by_quarter([gate_all[:, i] for i in range(4)]))
+    gate_all = flip(gate_all, t, 2)
+    gate_columns = gate_all.transpose(2, 0, 1, 3, 4).reshape(-1, exp_local)
 
     group_rows = n_expert * tok_rows
     forward, backward, down_grads, input_grads, gate_blocks = expert_calls(
@@ -346,22 +341,56 @@
     )
     down_rows = down_proj.reshape(exp_local * width, latent)
 
-    down_parts = square_weight(down_weight)
-    up_parts = square_weight(up_weight)
-    token_rows = square_rows(tokens)
-    cot_rows = square_rows(cotangent)
-    latent_in = gather_first(project(token_rows, down_parts))
-    latent_grad = gather_second(project(cot_rows, up_parts))
+    down_block, down_last = square_weight(down_weight)
+    up_block, up_last = square_weight(up_weight)
+    token_rows = square_rows(after(tokens, down_last, up_last))
+    cot_rows = square_rows(after(cotangent, down_last, up_last))
+    down_parts = gather_h(down_block)
+    up_parts = gather_h(after(up_block, down_parts[-1]))
+    down_parts = [all_features(v) for v in down_parts]
+    up_parts = [all_features(v) for v in up_parts]
+
+    part_x = jnp.stack(gather_h(project(token_rows, down_parts)))
+    part_x = jnp.stack(exchange(lambda r: part_x))
+    part_y = jnp.stack(gather_h(project(cot_rows, up_parts)))
+    latent_in = all_rows(after(part_x, part_y))
+    token_parts = gather_h(after(token_rows, part_x))
 
     hs, cp, cu, out_part = forward(
         latent_in, gate_blocks(gate_columns), gate_proj, up_proj, down_rows
     )
-    dpu, in_part = backward(latent_grad, cp, cu, gate_proj, up_proj, down_rows)
-    down_proj_grad = down_grads(hs, latent_grad).reshape(down_proj.shape)
-    gate_proj_grad, up_proj_grad = input_grads(latent_in, dpu)
-
-    out, up_grad = finish(collect(out_part), cot_rows, up_parts)
-    tokens_grad, down_grad = finish(collect(in_part), token_rows, down_parts)
+    part_y = exchange(lambda r: part_y)
+    *part_y, token_parts[-1], out_part = together(*part_y, token_parts[-1], out_part)
+    latent_grad = all_rows(jnp.stack(part_y))
+    cot_parts = gather_h(after(cot_rows, token_parts[-1]))
+    out_part = sum_tensor(out_part)
+    down_proj_grad = down_grads(hs, latent_grad)
+    out_part = after(out_part, down_proj_grad)
+    dpu, in_part = backward(
+        after(latent_grad, out_part), cp, cu, gate_proj, up_proj, down_rows
+    )
+    out_part = exchange(lambda r: out_part[r])
+    *out_part, cot_parts[-1], in_part = together(*out_part, cot_parts[-1], in_part)
+    out_part = add(*out_part)
+    in_part = sum_tensor(after(in_part, out_part))
+    gate_proj_grad, up_proj_grad = input_grads(latent_in, after(dpu, in_part))
+    in_part = exchange(lambda r: in_part[r])
+    *in_part, out_theirs, gate_proj_grad = together(
+        *in_part, sum_squares(out_part)[1], gate_proj_grad
+    )
+    out_part = join_squares(out_part, out_theirs)
+    in_part, in_theirs = sum_squares(add(*in_part))
+    out_part = exchange(lambda r: out_part)
+    *out_part, in_theirs = together(*out_part, in_theirs)
+    out_part = jnp.stack(out_part)
+    in_part = join_squares(in_part, in_theirs)
+    in_part = jnp.stack(exchange(lambda r: in_part))
+    out_sent = send_products(*products(square_blocks(out_part), cot_parts, up_parts))
+    in_products = products(square_blocks(in_part), token_parts, down_parts)
+    received = together(*out_sent[0], *out_sent[1], *in_products)
+    out, up_grad = join_products(received[:4], received[4:8])
+    tokens_grad, down_grad = join_products(*send_products(*in_products))
+    down_proj_grad = down_proj_grad.reshape(down_proj.shape)
     return (out, tokens_grad, gate_proj_grad, up_proj_grad, down_proj_grad, down_grad, up_grad)
 
 

time: 309 us -> 252 us (0.82)
  waiting for transfers between devices: 158 us -> 96.7 us
  starting transfers between devices: 45 us -> 76.8 us
  local copies, waits for them, and re-layouts: 28.4 us -> 6.98 us
  matrix products: 11.9 us -> 5.65 us
    ppermute x50 -> x76, waiting for transfers between devices: 158 us -> 96.7 us  [the longest x54 51.1 us: to_peer(): return lax.ppermute(v, 'expert', [(e, e ^ r) for e in range(n_expert)])]
    ppermute x50 -> x76, starting transfers between devices: 45 us -> 76.8 us  [the longest x54 64.4 us: to_peer(): return lax.ppermute(v, 'expert', [(e, e ^ r) for e in range(n_expert)])]
    unnamed x90 -> x75, local copies, waits for them, and re-layouts: 12.1 us -> 3.23 us
    dot_general x12, matrix products: 11.9 us -> 5.65 us  [dot(): return lax.dot_general(a, b, dims, preferred_element_type=f32)]
    another operation x16 -> x12, other arithmetic: 6.71 us -> 3 us  [the longest x3 1.78 us: all_rows(): return jnp.stack([part, t_swap(part)]).reshape(-1, latent)]
  transfers between devices with their start and end apart: 50 -> 76, of which waited for: 30 -> 31; matrix products, arithmetic and copies ran while one was open for 14% -> 8% of each run, Pallas kernels for 10% -> 19%
where the time goes in v4:
time: 252 us
  waiting for transfers between devices  96.7 us (38%)
  starting transfers between devices  76.8 us (30%)
  Pallas kernels  49 us (19%)
  other arithmetic  15 us (6%)
  local copies, waits for them, and re-layouts  6.98 us (3%)
  matrix products  5.65 us (2%)
    ppermute x54, starting transfers between devices, to_peer(): return lax.ppermute(v, 'expert', [(e, e ^ r) for e in range(n_expert)])  64.4 us
    ppermute x54, waiting for transfers between devices, to_peer(): return lax.ppermute(v, 'expert', [(e, e ^ r) for e in range(n_expert)])  51.1 us
    ppermute x8, waiting for transfers between devices, up(): lax.ppermute(v, 'expert', [(e, (e + 4) % n_expert) for e in range(n_exper...  26.9 us
    pallas_call x1, Pallas kernels, local(): forward(latent_in, gate_blocks(gate_columns), gate_proj, up_proj, down_rows)  17 us
    pallas_call x1, Pallas kernels, local(): backward(after(latent_grad, out_part), cp, cu, gate_proj, up_proj, down_r...  16.6 us
    ppermute x4, waiting for transfers between devices, g_swap(): return lax.ppermute(v, 'group', [(i, i ^ 1) for i in range(n_group)])  12.6 us
    pallas_call x1, Pallas kernels, local(): gate_proj_grad, up_proj_grad = input_grads(latent_in, after(dpu, in_part))  10.3 us
    ppermute x8, starting transfers between devices, up(): lax.ppermute(v, 'expert', [(e, (e + 4) % n_expert) for e in range(n_exper...  7.65 us
  transfers between devices with their start and end apart: 76, of which 31 were waited for; matrix products, arithmetic and copies ran while one was open for 8% of the time, Pallas kernels for 19%

profile of v4, /device:TPU:0, one launch (start us, length us, event | category | flops | bytes accessed | tf_op | source)
XLA Modules:
  0.0 251.8 jit_solution(5646869540374096622)
XLA Ops:
  1.7 4.0 %collective-permute-start = (bf16[256,128]{1,0:T(8,128)(2,1)S(1)}, bf16[256,128]{1,0:T(8,128)(2,1)S(1)}, u32[]{:S(2)}, u32[]{:S(2)}) collective-permute-start(bf16[256,128]{1,0:T(8,128)(2,1)S(1)} %get-tuple-element.180), channel_id=1, source_target_pairs={{0,6},{2,4},{4,2},{6,0},{8,14},{10,12},{12,10},{14,8},{1,7},{3,5},... | collective-permute-start | bytes 196616 | tf_op jit(solution)/shard_map/ppermute | solution.py:215
  7.3 2.9 %collective-permute-start.1 = (bf16[256,128]{1,0:T(8,128)(2,1)S(1)}, bf16[256,128]{1,0:T(8,128)(2,1)S(1)}, u32[]{:S(2)}, u32[]{:S(2)}) collective-permute-start(bf16[256,128]{1,0:T(8,128)(2,1)S(1)} %get-tuple-element.183), channel_id=1, source_target_pairs={{0,6},{2,4},{4,2},{6,0},{8,14},{10,12},{12,10},{14,8},{1,7},{3,5},... | collective-permute-start | bytes 196616 | tf_op jit(solution)/shard_map/ppermute | solution.py:215
  12.7 1.6 collective-permute-start.33
  14.3 1.6 collective-permute-start.25
  18.0 2.6 %collective-permute-done.25 = bf16[128,512]{1,0:T(8,128)(2,1)S(1)} collective-permute-done((bf16[128,512]{1,0:T(8,128)(2,1)S(1)}, bf16[128,512]{1,0:T(8,128)(2,1)S(1)}, u32[]{:S(2)}, u32[]{:S(2)}) %collective-permute-start.25) | collective-permute-done | bytes 131104 | tf_op jit(solution)/shard_map/ppermute | solution.py:215
  21.4 3.5 %collective-permute-start.9 = (bf16[256,512]{1,0:T(8,128)(2,1)S(1)}, bf16[256,512]{1,0:T(8,128)(2,1)S(1)}, u32[]{:S(2)}, u32[]{:S(2)}) collective-permute-start(bf16[256,512]{1,0:T(8,128)(2,1)S(1)} %pad_maximum_fusion.11), channel_id=1, source_target_pairs={{0,8},{2,10},{4,12},{6,14},{8,0},{10,2},{12,4},{14,6},{1,9},{3,11}... | collective-permute-start | bytes 786440 | tf_op jit(solution)/shard_map/ppermute | solution.py:224
  24.9 2.2 collective-permute-done.27
  28.9 2.3 collective-permute-start.4
  32.8 1.6 collective-permute-start.16
  34.5 6.9 %collective-permute-done.28 = bf16[256,512]{1,0:T(8,128)(2,1)S(1)} collective-permute-done((bf16[256,512]{1,0:T(8,128)(2,1)S(1)}, bf16[256,512]{1,0:T(8,128)(2,1)S(1)}, u32[]{:S(2)}, u32[]{:S(2)}) %collective-permute-start.28) | collective-permute-done | bytes 262176 | tf_op jit(solution)/shard_map/ppermute | solution.py:221
  44.6 2.4 collective-permute-start.36
  47.8 5.1 %collective-permute-done.10 = bf16[256,512]{1,0:T(8,128)(2,1)S(1)} collective-permute-done((bf16[256,512]{1,0:T(8,128)(2,1)S(1)}, bf16[256,512]{1,0:T(8,128)(2,1)S(1)}, u32[]{:S(2)}, u32[]{:S(2)}) %collective-permute-start.10) | collective-permute-done | bytes 262176 | tf_op jit(solution)/shard_map/ppermute | solution.py:224
  55.9 5.7 %collective-permute-done.11 = bf16[256,512]{1,0:T(8,128)(2,1)S(1)} collective-permute-done((bf16[256,512]{1,0:T(8,128)(2,1)S(1)}, bf16[256,512]{1,0:T(8,128)(2,1)S(1)}, u32[]{:S(2)}, u32[]{:S(2)}) %collective-permute-start.11) | collective-permute-done | bytes 262176 | tf_op jit(solution)/shard_map/ppermute | solution.py:221
  62.3 2.7 %collective-permute-start.32 = (bf16[64,512]{1,0:T(8,128)(2,1)S(1)}, bf16[64,512]{1,0:T(8,128)(2,1)S(1)}, u32[]{:S(2)}, u32[]{:S(2)}) collective-permute-start(bf16[64,512]{1,0:T(8,128)(2,1)S(1)} %get-tuple-element.191), channel_id=1, source_target_pairs={{0,6},{2,4},{4,2},{6,0},{8,14},{10,12},{12,10},{14,8},{1,7},{3,5},... | collective-permute-start | bytes 196616 | tf_op jit(solution)/shard_map/ppermute | solution.py:215
  65.9 2.7 %collective-permute-start.20 = (bf16[64,512]{1,0:T(8,128)(2,1)S(1)}, bf16[64,512]{1,0:T(8,128)(2,1)S(1)}, u32[]{:S(2)}, u32[]{:S(2)}) collective-permute-start(bf16[64,512]{1,0:T(8,128)(2,1)S(1)} %get-tuple-element.194), channel_id=1, source_target_pairs={{0,6},{2,4},{4,2},{6,0},{8,14},{10,12},{12,10},{14,8},{1,7},{3,5},... | collective-permute-start | bytes 196616 | tf_op jit(solution)/shard_map/ppermute | solution.py:215
  71.2 6.8 %collective-permute-done.38 = bf16[64,1024]{1,0:T(8,128)(2,1)S(1)} collective-permute-done((bf16[64,1024]{1,0:T(8,128)(2,1)S(1)}, bf16[64,1024]{1,0:T(8,128)(2,1)S(1)}, u32[]{:S(2)}, u32[]{:S(2)}) %collective-permute-start.38) | collective-permute-done | bytes 131104 | tf_op jit(solution)/shard_map/ppermute | solution.py:224
  78.9 2.7 %collective-permute-start.40 = (bf16[2,64,1024]{2,1,0:T(8,128)(2,1)S(1)}, bf16[2,64,1024]{2,1,0:T(8,128)(2,1)S(1)}, u32[]{:S(2)}, u32[]{:S(2)}) collective-permute-start(bf16[2,64,1024]{2,1,0:T(8,128)(2,1)S(1)} %get-tuple-element.186), channel_id=1, source_target_pairs={{0,4},{2,6},{4,0},{6,2},{8,12},{10,14},{12,8},{14,10},{1,5},{3,7},... | collective-permute-start | bytes 786440 | tf_op jit(solution)/shard_map/ppermute | solution.py:215
  81.9 2.0 collective-permute-done.15
  84.3 11.0 %collective-permute-done.21 = bf16[64,1024]{1,0:T(8,128)(2,1)S(1)} collective-permute-done((bf16[64,1024]{1,0:T(8,128)(2,1)S(1)}, bf16[64,1024]{1,0:T(8,128)(2,1)S(1)}, u32[]{:S(2)}, u32[]{:S(2)}) %collective-permute-start.21) | collective-permute-done | bytes 131104 | tf_op jit(solution)/shard_map/ppermute | solution.py:224
  95.3 1.7 collective-permute-done.41
  100.3 2.4 collective-permute-start.24
  102.6 1.7 collective-permute-start.42
  105.8 17.0 %shard_map.144 = (bf16[1024,1536]{1,0:T(8,128)(2,1)S(1)}, bf16[1024,1536]{1,0:T(8,128)(2,1)S(1)}, bf16[1024,1536]{1,0:T(8,128)(2,1)}, bf16[1024,1024]{1,0:T(8,128)(2,1)S(1)}) custom-call(bf16[1024,1024]{1,0:T(8,128)(2,1)S(1)} %bitcast.230, f32[2,1024,2]{2,1,0:T(8,128)S(1)} %bitcast.234, bf16[4,1024,384]{2,1,0:T(8,128)(2,1)} %wg_ref.3, ...), custom_call_target="tpu_custom_call" | custom-call | flops 9663676416 | bytes 23068672 | tf_op jit(solution)/shard_map/pallas_call | solution.py:359
  124.2 3.9 %collective-permute-done.42 = bf16[512,512]{1,0:T(8,128)(2,1)S(1)} collective-permute-done((bf16[512,512]{1,0:T(8,128)(2,1)S(1)}, bf16[512,512]{1,0:T(8,128)(2,1)S(1)}, u32[]{:S(2)}, u32[]{:S(2)}) %collective-permute-start.42) | collective-permute-done | bytes 524320 | tf_op jit(solution)/shard_map/ppermute | solution.py:224
  130.3 1.6 collective-permute-done.45
  132.1 5.0 %shard_map.145 = bf16[1536,1024]{1,0:T(8,128)(2,1)} custom-call(bf16[1024,1536]{1,0:T(8,128)(2,1)S(1)} %get-tuple-element.65.hs_ref, bf16[1024,1024]{1,0:T(8,128)(2,1)S(1)} %bitcast.232), custom_call_target="tpu_custom_call" | custom-call | flops 3221225472 | bytes 8388608 | tf_op jit(solution)/shard_map/pallas_call | solution.py:367
  139.0 2.2 collective-permute-start.48
  141.2 16.6 %shard_map.146 = (bf16[1024,3072]{1,0:T(8,128)(2,1)}, bf16[1024,1024]{1,0:T(8,128)(2,1)S(1)}) custom-call(bf16[1024,1024]{1,0:T(8,128)(2,1)S(1)} %bitcast.233, bf16[1024,1536]{1,0:T(8,128)(2,1)S(1)} %get-tuple-element.72.cp_ref, bf16[1024,1536]{1,0:T(8,128)(2,1)S(1)} %copy-done.2, bf16[4,1024,384]{2,1,0:T(8,128)(2,1)S(1)} %copy-done, ...), custom_call_target="tpu_custom_call" | custom-call | flops 9663676416 | bytes 26214400 | tf_op jit(solution)/shard_map/pallas_call | solution.py:369
  159.0 5.0 %collective-permute-done.48 = bf16[2,64,1024]{2,1,0:T(8,128)(2,1)S(1)} collective-permute-done((bf16[2,64,1024]{2,1,0:T(8,128)(2,1)S(1)}, bf16[2,64,1024]{2,1,0:T(8,128)(2,1)S(1)}, u32[]{:S(2)}, u32[]{:S(2)}) %collective-permute-start.48) | collective-permute-done | bytes 262176 | tf_op jit(solution)/shard_map/ppermute | solution.py:215
  164.6 2.6 %collective-permute-done.50 = bf16[4,2,64,1024]{3,2,1,0:T(8,128)(2,1)S(1)} collective-permute-done((bf16[4,2,64,1024]{3,2,1,0:T(8,128)(2,1)S(1)}, bf16[4,2,64,1024]{3,2,1,0:T(8,128)(2,1)S(1)}, u32[]{:S(2)}, u32[]{:S(2)}) %collective-permute-start.50) | collective-permute-done | bytes 1048608 | tf_op jit(solution)/shard_map/ppermute | solution.py:218
  168.7 2.5 %collective-permute-start.53 = (bf16[2,64,1024]{2,1,0:T(8,128)(2,1)S(1)}, bf16[2,64,1024]{2,1,0:T(8,128)(2,1)S(1)}, u32[]{:S(2)}, u32[]{:S(2)}) collective-permute-start(bf16[2,64,1024]{2,1,0:T(8,128)(2,1)S(1)} %get-tuple-element.115), channel_id=1, source_target_pairs={{0,6},{2,4},{4,2},{6,0},{8,14},{10,12},{12,10},{14,8},{1,7},{3,5},... | collective-permute-start | bytes 786440 | tf_op jit(solution)/shard_map/ppermute | solution.py:215
  171.2 10.3 %shard_map.147 = (bf16[4,1024,384]{2,1,0:T(8,128)(2,1)}, bf16[4,1024,384]{2,1,0:T(8,128)(2,1)}) custom-call(bf16[1024,1024]{1,0:T(8,128)(2,1)S(1)} %bitcast.231, bf16[1024,3072]{1,0:T(8,128)(2,1)S(1)} %copy-done.1), custom_call_target="tpu_custom_call" | custom-call | flops 6442450944 | bytes 14680064 | tf_op jit(solution)/shard_map/pallas_call | solution.py:376
  181.6 1.8 collective-permute-done.52
  183.4 5.0 %collective-permute-done.53 = bf16[2,64,1024]{2,1,0:T(8,128)(2,1)S(1)} collective-permute-done((bf16[2,64,1024]{2,1,0:T(8,128)(2,1)S(1)}, bf16[2,64,1024]{2,1,0:T(8,128)(2,1)S(1)}, u32[]{:S(2)}, u32[]{:S(2)}) %collective-permute-start.53) | collective-permute-done | bytes 262176 | tf_op jit(solution)/shard_map/ppermute | solution.py:215
  189.8 1.9 collective-permute-start.56
  192.4 2.8 %collective-permute-done.55 = bf16[64,1536]{1,0:T(8,128)(2,1)S(1)} collective-permute-done((bf16[64,1536]{1,0:T(8,128)(2,1)S(1)}, bf16[64,1536]{1,0:T(8,128)(2,1)S(1)}, u32[]{:S(2)}, u32[]{:S(2)}) %collective-permute-start.55) | collective-permute-done | bytes 196640 | tf_op jit(solution)/shard_map/ppermute | solution.py:215
  195.2 7.9 %collective-permute-done.56 = bf16[64,1536]{1,0:T(8,128)(2,1)S(1)} collective-permute-done((bf16[64,1536]{1,0:T(8,128)(2,1)S(1)}, bf16[64,1536]{1,0:T(8,128)(2,1)S(1)}, u32[]{:S(2)}, u32[]{:S(2)}) %collective-permute-start.56) | collective-permute-done | bytes 196640 | tf_op jit(solution)/shard_map/ppermute | solution.py:215
  203.0 2.6 %collective-permute-done.57 = bf16[64,1536]{1,0:T(8,128)(2,1)S(1)} collective-permute-done((bf16[64,1536]{1,0:T(8,128)(2,1)S(1)}, bf16[64,1536]{1,0:T(8,128)(2,1)S(1)}, u32[]{:S(2)}, u32[]{:S(2)}) %collective-permute-start.57) | collective-permute-done | bytes 196640 | tf_op jit(solution)/shard_map/ppermute | solution.py:215
  207.7 2.5 %collective-permute-start.68 = (bf16[64,1536]{1,0:T(8,128)(2,1)}, bf16[64,1536]{1,0:T(8,128)(2,1)S(1)}, u32[]{:S(2)}, u32[]{:S(2)}) collective-permute-start(bf16[64,1536]{1,0:T(8,128)(2,1)} %get-tuple-element.200), channel_id=1, source_target_pairs={{0,6},{2,4},{4,2},{6,0},{8,14},{10,12},{12,10},{14,8},{1,7},{3,5},... | collective-permute-start | bytes 589832 | tf_op jit(solution)/shard_map/ppermute | solution.py:215
  210.2 4.0 %collective-permute-done.66 = bf16[64,1536]{1,0:T(8,128)(2,1)S(1)} collective-permute-done((bf16[64,1536]{1,0:T(8,128)(2,1)}, bf16[64,1536]{1,0:T(8,128)(2,1)S(1)}, u32[]{:S(2)}, u32[]{:S(2)}) %collective-permute-start.66) | collective-permute-done | bytes 196640 | tf_op jit(solution)/shard_map/ppermute | solution.py:215
  215.6 4.0 %collective-permute-done.68 = bf16[64,1536]{1,0:T(8,128)(2,1)S(1)} collective-permute-done((bf16[64,1536]{1,0:T(8,128)(2,1)}, bf16[64,1536]{1,0:T(8,128)(2,1)S(1)}, u32[]{:S(2)}, u32[]{:S(2)}) %collective-permute-start.68) | collective-permute-done | bytes 196640 | tf_op jit(solution)/shard_map/ppermute | solution.py:215
  219.9 1.6 maximum_select_fusion
  224.4 2.2 collective-permute-start.65
  232.0 2.3 collective-permute-start.62
  236.2 2.2 collective-permute-start.75
  240.6 1.6 collective-permute-start.71
  242.2 1.5 collective-permute-done.73
  248.0 2.0 collective-permute-done.72
  (275 shorter events, 60.8 us)
Async XLA Ops:
  1.7 10.0 %collective-permute-start = (bf16[256,128]{1,0:T(8,128)(2,1)S(1)}, bf16[256,128]{1,0:T(8,128)(2,1)S(1)}, u32[]{:S(2)}, u32[]{:S(2)}) collective-permute-start(bf16[256,128]{1,0:T(8,128)(2,1)S(1)} %get-tuple-element.180), channel_id=1, source_target_pairs={{0,6},{2,4},{4,2},{6,0},{8,14},{10,12},{12,10},{14,8},{1,7},{3,5},... | collective-permute-start | bytes 196616 | tf_op jit(solution)/shard_map/ppermute | solution.py:215
  10.2 18.7 %collective-permute-start.5 = (bf16[256,128]{1,0:T(8,128)(2,1)S(1)}, bf16[256,128]{1,0:T(8,128)(2,1)S(1)}, u32[]{:S(2)}, u32[]{:S(2)}) collective-permute-start(bf16[256,128]{1,0:T(8,128)(2,1)S(1)} %get-tuple-element.182), channel_id=1, source_target_pairs={{0,2},{2,0},{4,6},{6,4},{8,10},{10,8},{12,14},{14,12},{1,3},{3,1},... | collective-permute-start | bytes 196616 | tf_op jit(solution)/shard_map/ppermute | solution.py:215
  12.7 15.4 %collective-permute-start.33 = (bf16[256,512]{1,0:T(8,128)(2,1)S(1)}, bf16[256,512]{1,0:T(8,128)(2,1)S(1)}, u32[]{:S(2)}, u32[]{:S(2)}) collective-permute-start(bf16[256,512]{1,0:T(8,128)(2,1)S(1)} %pad_maximum_fusion.11), channel_id=1, source_target_pairs={{0,16},{16,0},{1,17},{17,1},{2,18},{18,2},{3,19},{19,3},{4,20},{20... | collective-permute-start | bytes 786440 | tf_op jit(solution)/shard_map/ppermute | solution.py:221
  16.4 10.7 %collective-permute-start.27 = (bf16[128,512]{1,0:T(8,128)(2,1)S(1)}, bf16[128,512]{1,0:T(8,128)(2,1)S(1)}, u32[]{:S(2)}, u32[]{:S(2)}) collective-permute-start(bf16[128,512]{1,0:T(8,128)(2,1)S(1)} %get-tuple-element.172), channel_id=1, source_target_pairs={{0,6},{2,4},{4,2},{6,0},{8,14},{10,12},{12,10},{14,8},{1,7},{3,5},... | collective-permute-start | bytes 393224 | tf_op jit(solution)/shard_map/ppermute | solution.py:215
  20.6 10.7 %collective-permute-start.6 = (bf16[256,128]{1,0:T(8,128)(2,1)S(1)}, bf16[256,128]{1,0:T(8,128)(2,1)S(1)}, u32[]{:S(2)}, u32[]{:S(2)}) collective-permute-start(bf16[256,128]{1,0:T(8,128)(2,1)S(1)} %get-tuple-element.184), channel_id=1, source_target_pairs={{0,4},{2,6},{4,0},{6,2},{8,12},{10,14},{12,8},{14,10},{1,5},{3,7},... | collective-permute-start | bytes 196616 | tf_op jit(solution)/shard_map/ppermute | solution.py:215
  21.4 10.8 %collective-permute-start.9 = (bf16[256,512]{1,0:T(8,128)(2,1)S(1)}, bf16[256,512]{1,0:T(8,128)(2,1)S(1)}, u32[]{:S(2)}, u32[]{:S(2)}) collective-permute-start(bf16[256,512]{1,0:T(8,128)(2,1)S(1)} %pad_maximum_fusion.11), channel_id=1, source_target_pairs={{0,8},{2,10},{4,12},{6,14},{8,0},{10,2},{12,4},{14,6},{1,9},{3,11}... | collective-permute-start | bytes 786440 | tf_op jit(solution)/shard_map/ppermute | solution.py:224
  27.1 16.1 %collective-permute-start.2 = (bf16[128,512]{1,0:T(8,128)(2,1)S(1)}, bf16[128,512]{1,0:T(8,128)(2,1)S(1)}, u32[]{:S(2)}, u32[]{:S(2)}) collective-permute-start(bf16[128,512]{1,0:T(8,128)(2,1)S(1)} %get-tuple-element.178), channel_id=1, source_target_pairs={{0,2},{2,0},{4,6},{6,4},{8,10},{10,8},{12,14},{14,12},{1,3},{3,1},... | collective-permute-start | bytes 393224 | tf_op jit(solution)/shard_map/ppermute | solution.py:215
  28.2 15.2 %collective-permute-start.3 = (bf16[128,512]{1,0:T(8,128)(2,1)S(1)}, bf16[128,512]{1,0:T(8,128)(2,1)S(1)}, u32[]{:S(2)}, u32[]{:S(2)}) collective-permute-start(bf16[128,512]{1,0:T(8,128)(2,1)S(1)} %get-tuple-element.177), channel_id=1, source_target_pairs={{0,4},{2,6},{4,0},{6,2},{8,12},{10,14},{12,8},{14,10},{1,5},{3,7},... | collective-permute-start | bytes 393224 | tf_op jit(solution)/shard_map/ppermute | solution.py:215
  28.9 15.7 %collective-permute-start.4 = (bf16[128,512]{1,0:T(8,128)(2,1)S(1)}, bf16[128,512]{1,0:T(8,128)(2,1)S(1)}, u32[]{:S(2)}, u32[]{:S(2)}) collective-permute-start(bf16[128,512]{1,0:T(8,128)(2,1)S(1)} %get-tuple-element.176), channel_id=1, source_target_pairs={{0,6},{2,4},{4,2},{6,0},{8,14},{10,12},{12,10},{14,8},{1,7},{3,5},... | collective-permute-start | bytes 393224 | tf_op jit(solution)/shard_map/ppermute | solution.py:215
  32.2 9.2 %collective-permute-start.28 = (bf16[256,512]{1,0:T(8,128)(2,1)S(1)}, bf16[256,512]{1,0:T(8,128)(2,1)S(1)}, u32[]{:S(2)}, u32[]{:S(2)}) collective-permute-start(bf16[256,512]{1,0:T(8,128)(2,1)S(1)} %collective-permute-done.9), channel_id=1, source_target_pairs={{0,16},{16,0},{1,17},{17,1},{2,18},{18,2},{3,19},{19,3},{4,20},{20... | collective-permute-start | bytes 786440 | tf_op jit(solution)/shard_map/ppermute | solution.py:221
  32.8 14.2 %collective-permute-start.16 = (bf16[256,512]{1,0:T(8,128)(2,1)S(1)}, bf16[256,512]{1,0:T(8,128)(2,1)S(1)}, u32[]{:S(2)}, u32[]{:S(2)}) collective-permute-start(bf16[256,512]{1,0:T(8,128)(2,1)S(1)} %pad_maximum_fusion.10), channel_id=1, source_target_pairs={{0,16},{16,0},{1,17},{17,1},{2,18},{18,2},{3,19},{19,3},{4,20},{20... | collective-permute-start | bytes 786440 | tf_op jit(solution)/shard_map/ppermute | solution.py:221
  41.3 11.5 %collective-permute-start.10 = (bf16[256,512]{1,0:T(8,128)(2,1)S(1)}, bf16[256,512]{1,0:T(8,128)(2,1)S(1)}, u32[]{:S(2)}, u32[]{:S(2)}) collective-permute-start(bf16[256,512]{1,0:T(8,128)(2,1)S(1)} %pad_maximum_fusion.10), channel_id=1, source_target_pairs={{0,8},{2,10},{4,12},{6,14},{8,0},{10,2},{12,4},{14,6},{1,9},{3,11}... | collective-permute-start | bytes 786440 | tf_op jit(solution)/shard_map/ppermute | solution.py:224
  43.2 9.7 %collective-permute-start.29 = (bf16[4,64,512]{2,1,0:T(8,128)(2,1)S(1)}, bf16[4,64,512]{2,1,0:T(8,128)(2,1)S(1)}, u32[]{:S(2)}, u32[]{:S(2)}) collective-permute-start(bf16[4,64,512]{2,1,0:T(8,128)(2,1)S(1)} %dynamic-slice_bitcast_fusion.1), channel_id=1, source_target_pairs={{0,1},{1,0},{2,3},{3,2},{4,5},{5,4},{6,7},{7,6},{8,9},{9,8},{10,11... | collective-permute-start | bytes 786440 | tf_op jit(solution)/shard_map/ppermute | solution.py:218
  43.3 19.0 %collective-permute-start.35 = (bf16[64,512]{1,0:T(8,128)(2,1)S(1)}, bf16[64,512]{1,0:T(8,128)(2,1)S(1)}, u32[]{:S(2)}, u32[]{:S(2)}) collective-permute-start(bf16[64,512]{1,0:T(8,128)(2,1)S(1)} %get-tuple-element.187), channel_id=1, source_target_pairs={{0,2},{2,0},{4,6},{6,4},{8,10},{10,8},{12,14},{14,12},{1,3},{3,1},... | collective-permute-start | bytes 196616 | tf_op jit(solution)/shard_map/ppermute | solution.py:215
  44.6 20.5 %collective-permute-start.36 = (bf16[64,512]{1,0:T(8,128)(2,1)S(1)}, bf16[64,512]{1,0:T(8,128)(2,1)S(1)}, u32[]{:S(2)}, u32[]{:S(2)}) collective-permute-start(bf16[64,512]{1,0:T(8,128)(2,1)S(1)} %get-tuple-element.189), channel_id=1, source_target_pairs={{0,4},{2,6},{4,0},{6,2},{8,12},{10,14},{12,8},{14,10},{1,5},{3,7},... | collective-permute-start | bytes 196616 | tf_op jit(solution)/shard_map/ppermute | solution.py:215
  47.0 18.8 %collective-permute-start.37 = (bf16[64,512]{1,0:T(8,128)(2,1)S(1)}, bf16[64,512]{1,0:T(8,128)(2,1)S(1)}, u32[]{:S(2)}, u32[]{:S(2)}) collective-permute-start(bf16[64,512]{1,0:T(8,128)(2,1)S(1)} %get-tuple-element.188), channel_id=1, source_target_pairs={{0,6},{2,4},{4,2},{6,0},{8,14},{10,12},{12,10},{14,8},{1,7},{3,5},... | collective-permute-start | bytes 196616 | tf_op jit(solution)/shard_map/ppermute | solution.py:215
  54.4 11.5 %collective-permute-start.30 = (bf16[64,512]{1,0:T(8,128)(2,1)S(1)}, bf16[64,512]{1,0:T(8,128)(2,1)S(1)}, u32[]{:S(2)}, u32[]{:S(2)}) collective-permute-start(bf16[64,512]{1,0:T(8,128)(2,1)S(1)} %get-tuple-element.190), channel_id=1, source_target_pairs={{0,2},{2,0},{4,6},{6,4},{8,10},{10,8},{12,14},{14,12},{1,3},{3,1},... | collective-permute-start | bytes 196616 | tf_op jit(solution)/shard_map/ppermute | solution.py:215
  65.8 12.3 %collective-permute-start.19 = (bf16[64,512]{1,0:T(8,128)(2,1)S(1)}, bf16[64,512]{1,0:T(8,128)(2,1)S(1)}, u32[]{:S(2)}, u32[]{:S(2)}) collective-permute-start(bf16[64,512]{1,0:T(8,128)(2,1)S(1)} %get-tuple-element.195), channel_id=1, source_target_pairs={{0,4},{2,6},{4,0},{6,2},{8,12},{10,14},{12,8},{14,10},{1,5},{3,7},... | collective-permute-start | bytes 196616 | tf_op jit(solution)/shard_map/ppermute | solution.py:215
  65.9 13.0 %collective-permute-start.20 = (bf16[64,512]{1,0:T(8,128)(2,1)S(1)}, bf16[64,512]{1,0:T(8,128)(2,1)S(1)}, u32[]{:S(2)}, u32[]{:S(2)}) collective-permute-start(bf16[64,512]{1,0:T(8,128)(2,1)S(1)} %get-tuple-element.194), channel_id=1, source_target_pairs={{0,6},{2,4},{4,2},{6,0},{8,14},{10,12},{12,10},{14,8},{1,7},{3,5},... | collective-permute-start | bytes 196616 | tf_op jit(solution)/shard_map/ppermute | solution.py:215
  68.8 9.2 %collective-permute-start.38 = (bf16[64,1024]{1,0:T(8,128)(2,1)S(1)}, bf16[64,1024]{1,0:T(8,128)(2,1)S(1)}, u32[]{:S(2)}, u32[]{:S(2)}) collective-permute-start(bf16[64,1024]{1,0:T(8,128)(2,1)S(1)} %get-tuple-element.206), channel_id=1, source_target_pairs={{0,8},{2,10},{4,12},{6,14},{8,0},{10,2},{12,4},{14,6},{1,9},{3,11}... | collective-permute-start | bytes 393224 | tf_op jit(solution)/shard_map/ppermute | solution.py:224
  70.3 11.3 %collective-permute-start.13 = (bf16[64,512]{1,0:T(8,128)(2,1)S(1)}, bf16[64,512]{1,0:T(8,128)(2,1)S(1)}, u32[]{:S(2)}, u32[]{:S(2)}) collective-permute-start(bf16[64,512]{1,0:T(8,128)(2,1)S(1)} %get-tuple-element.196), channel_id=1, source_target_pairs={{0,2},{2,0},{4,6},{6,4},{8,10},{10,8},{12,14},{14,12},{1,3},{3,1},... | collective-permute-start | bytes 196616 | tf_op jit(solution)/shard_map/ppermute | solution.py:215
  71.0 10.9 %collective-permute-start.14 = (bf16[64,512]{1,0:T(8,128)(2,1)S(1)}, bf16[64,512]{1,0:T(8,128)(2,1)S(1)}, u32[]{:S(2)}, u32[]{:S(2)}) collective-permute-start(bf16[64,512]{1,0:T(8,128)(2,1)S(1)} %get-tuple-element.198), channel_id=1, source_target_pairs={{0,4},{2,6},{4,0},{6,2},{8,12},{10,14},{12,8},{14,10},{1,5},{3,7},... | collective-permute-start | bytes 196616 | tf_op jit(solution)/shard_map/ppermute | solution.py:215
  78.1 17.3 %collective-permute-start.39 = (bf16[2,64,1024]{2,1,0:T(8,128)(2,1)S(1)}, bf16[2,64,1024]{2,1,0:T(8,128)(2,1)S(1)}, u32[]{:S(2)}, u32[]{:S(2)}) collective-permute-start(bf16[2,64,1024]{2,1,0:T(8,128)(2,1)S(1)} %get-tuple-element.186), channel_id=1, source_target_pairs={{0,2},{2,0},{4,6},{6,4},{8,10},{10,8},{12,14},{14,12},{1,3},{3,1},... | collective-permute-start | bytes 786440 | tf_op jit(solution)/shard_map/ppermute | solution.py:215
  78.9 16.5 %collective-permute-start.40 = (bf16[2,64,1024]{2,1,0:T(8,128)(2,1)S(1)}, bf16[2,64,1024]{2,1,0:T(8,128)(2,1)S(1)}, u32[]{:S(2)}, u32[]{:S(2)}) collective-permute-start(bf16[2,64,1024]{2,1,0:T(8,128)(2,1)S(1)} %get-tuple-element.186), channel_id=1, source_target_pairs={{0,4},{2,6},{4,0},{6,2},{8,12},{10,14},{12,8},{14,10},{1,5},{3,7},... | collective-permute-start | bytes 786440 | tf_op jit(solution)/shard_map/ppermute | solution.py:215
  81.6 15.4 %collective-permute-start.41 = (bf16[2,64,1024]{2,1,0:T(8,128)(2,1)S(1)}, bf16[2,64,1024]{2,1,0:T(8,128)(2,1)S(1)}, u32[]{:S(2)}, u32[]{:S(2)}) collective-permute-start(bf16[2,64,1024]{2,1,0:T(8,128)(2,1)S(1)} %get-tuple-element.186), channel_id=1, source_target_pairs={{0,6},{2,4},{4,2},{6,0},{8,14},{10,12},{12,10},{14,8},{1,7},{3,5},... | collective-permute-start | bytes 786440 | tf_op jit(solution)/shard_map/ppermute | solution.py:215
  84.0 11.3 %collective-permute-start.21 = (bf16[64,1024]{1,0:T(8,128)(2,1)S(1)}, bf16[64,1024]{1,0:T(8,128)(2,1)S(1)}, u32[]{:S(2)}, u32[]{:S(2)}) collective-permute-start(bf16[64,1024]{1,0:T(8,128)(2,1)S(1)} %get-tuple-element.208), channel_id=1, source_target_pairs={{0,8},{2,10},{4,12},{6,14},{8,0},{10,2},{12,4},{14,6},{1,9},{3,11}... | collective-permute-start | bytes 393224 | tf_op jit(solution)/shard_map/ppermute | solution.py:224
  99.1 23.7 %collective-permute-start.22 = (bf16[2,64,1024]{2,1,0:T(8,128)(2,1)S(1)}, bf16[2,64,1024]{2,1,0:T(8,128)(2,1)S(1)}, u32[]{:S(2)}, u32[]{:S(2)}) collective-permute-start(bf16[2,64,1024]{2,1,0:T(8,128)(2,1)S(1)} %pad_maximum_fusion.12), channel_id=1, source_target_pairs={{0,2},{2,0},{4,6},{6,4},{8,10},{10,8},{12,14},{14,12},{1,3},{3,1},... | collective-permute-start | bytes 786440 | tf_op jit(solution)/shard_map/ppermute | solution.py:215
  100.1 22.7 %collective-permute-start.23 = (bf16[2,64,1024]{2,1,0:T(8,128)(2,1)S(1)}, bf16[2,64,1024]{2,1,0:T(8,128)(2,1)S(1)}, u32[]{:S(2)}, u32[]{:S(2)}) collective-permute-start(bf16[2,64,1024]{2,1,0:T(8,128)(2,1)S(1)} %pad_maximum_fusion.12), channel_id=1, source_target_pairs={{0,4},{2,6},{4,0},{6,2},{8,12},{10,14},{12,8},{14,10},{1,5},{3,7},... | collective-permute-start | bytes 786440 | tf_op jit(solution)/shard_map/ppermute | solution.py:215
  100.3 23.9 %collective-permute-start.24 = (bf16[2,64,1024]{2,1,0:T(8,128)(2,1)S(1)}, bf16[2,64,1024]{2,1,0:T(8,128)(2,1)S(1)}, u32[]{:S(2)}, u32[]{:S(2)}) collective-permute-start(bf16[2,64,1024]{2,1,0:T(8,128)(2,1)S(1)} %pad_maximum_fusion.12), channel_id=1, source_target_pairs={{0,6},{2,4},{4,2},{6,0},{8,14},{10,12},{12,10},{14,8},{1,7},{3,5},... | collective-permute-start | bytes 786440 | tf_op jit(solution)/shard_map/ppermute | solution.py:215
  102.6 25.5 %collective-permute-start.42 = (bf16[512,512]{1,0:T(8,128)(2,1)S(1)}, bf16[512,512]{1,0:T(8,128)(2,1)S(1)}, u32[]{:S(2)}, u32[]{:S(2)}) collective-permute-start(bf16[512,512]{1,0:T(8,128)(2,1)S(1)} %pad_maximum_fusion.7), channel_id=1, source_target_pairs={{0,8},{2,10},{4,12},{6,14},{8,0},{10,2},{12,4},{14,6},{1,9},{3,11}... | collective-permute-start | bytes 1572872 | tf_op jit(solution)/shard_map/ppermute | solution.py:224
  130.2 27.7 %collective-permute-start.49 = (bf16[512,512]{1,0:T(8,128)(2,1)S(1)}, bf16[512,512]{1,0:T(8,128)(2,1)S(1)}, u32[]{:S(2)}, u32[]{:S(2)}) collective-permute-start(bf16[512,512]{1,0:T(8,128)(2,1)S(1)} %pad_maximum_fusion.6), channel_id=1, source_target_pairs={{0,8},{2,10},{4,12},{6,14},{8,0},{10,2},{12,4},{14,6},{1,9},{3,11}... | collective-permute-start | bytes 1572872 | tf_op jit(solution)/shard_map/ppermute | solution.py:224
  137.7 20.2 %collective-permute-start.46 = (bf16[2,64,1024]{2,1,0:T(8,128)(2,1)S(1)}, bf16[2,64,1024]{2,1,0:T(8,128)(2,1)S(1)}, u32[]{:S(2)}, u32[]{:S(2)}) collective-permute-start(bf16[2,64,1024]{2,1,0:T(8,128)(2,1)S(1)} %get-tuple-element.121), channel_id=1, source_target_pairs={{0,2},{2,0},{4,6},{6,4},{8,10},{10,8},{12,14},{14,12},{1,3},{3,1},... | collective-permute-start | bytes 786440 | tf_op jit(solution)/shard_map/ppermute | solution.py:215
  138.7 20.3 %collective-permute-start.47 = (bf16[2,64,1024]{2,1,0:T(8,128)(2,1)S(1)}, bf16[2,64,1024]{2,1,0:T(8,128)(2,1)S(1)}, u32[]{:S(2)}, u32[]{:S(2)}) collective-permute-start(bf16[2,64,1024]{2,1,0:T(8,128)(2,1)S(1)} %get-tuple-element.120), channel_id=1, source_target_pairs={{0,4},{2,6},{4,0},{6,2},{8,12},{10,14},{12,8},{14,10},{1,5},{3,7},... | collective-permute-start | bytes 786440 | tf_op jit(solution)/shard_map/ppermute | solution.py:215
  139.0 25.0 %collective-permute-start.48 = (bf16[2,64,1024]{2,1,0:T(8,128)(2,1)S(1)}, bf16[2,64,1024]{2,1,0:T(8,128)(2,1)S(1)}, u32[]{:S(2)}, u32[]{:S(2)}) collective-permute-start(bf16[2,64,1024]{2,1,0:T(8,128)(2,1)S(1)} %get-tuple-element.119), channel_id=1, source_target_pairs={{0,6},{2,4},{4,2},{6,0},{8,14},{10,12},{12,10},{14,8},{1,7},{3,5},... | collective-permute-start | bytes 786440 | tf_op jit(solution)/shard_map/ppermute | solution.py:215
  164.5 17.1 %collective-permute-start.54 = (bf16[2,64,1024]{2,1,0:T(8,128)(2,1)S(1)}, bf16[2,64,1024]{2,1,0:T(8,128)(2,1)S(1)}, u32[]{:S(2)}, u32[]{:S(2)}) collective-permute-start(bf16[2,64,1024]{2,1,0:T(8,128)(2,1)S(1)} %add_convert_fusion.2), channel_id=1, source_target_pairs={{0,8},{2,10},{4,12},{6,14},{8,0},{10,2},{12,4},{14,6},{1,9},{3,11}... | collective-permute-start | bytes 786440 | tf_op jit(solution)/shard_map/ppermute | solution.py:224
  167.7 13.9 %collective-permute-start.51 = (bf16[2,64,1024]{2,1,0:T(8,128)(2,1)S(1)}, bf16[2,64,1024]{2,1,0:T(8,128)(2,1)S(1)}, u32[]{:S(2)}, u32[]{:S(2)}) collective-permute-start(bf16[2,64,1024]{2,1,0:T(8,128)(2,1)S(1)} %get-tuple-element.117), channel_id=1, source_target_pairs={{0,2},{2,0},{4,6},{6,4},{8,10},{10,8},{12,14},{14,12},{1,3},{3,1},... | collective-permute-start | bytes 786440 | tf_op jit(solution)/shard_map/ppermute | solution.py:215
  168.7 14.7 %collective-permute-start.52 = (bf16[2,64,1024]{2,1,0:T(8,128)(2,1)S(1)}, bf16[2,64,1024]{2,1,0:T(8,128)(2,1)S(1)}, u32[]{:S(2)}, u32[]{:S(2)}) collective-permute-start(bf16[2,64,1024]{2,1,0:T(8,128)(2,1)S(1)} %get-tuple-element.116), channel_id=1, source_target_pairs={{0,4},{2,6},{4,0},{6,2},{8,12},{10,14},{12,8},{14,10},{1,5},{3,7},... | collective-permute-start | bytes 786440 | tf_op jit(solution)/shard_map/ppermute | solution.py:215
  168.7 19.7 %collective-permute-start.53 = (bf16[2,64,1024]{2,1,0:T(8,128)(2,1)S(1)}, bf16[2,64,1024]{2,1,0:T(8,128)(2,1)S(1)}, u32[]{:S(2)}, u32[]{:S(2)}) collective-permute-start(bf16[2,64,1024]{2,1,0:T(8,128)(2,1)S(1)} %get-tuple-element.115), channel_id=1, source_target_pairs={{0,6},{2,4},{4,2},{6,0},{8,14},{10,12},{12,10},{14,8},{1,7},{3,5},... | collective-permute-start | bytes 786440 | tf_op jit(solution)/shard_map/ppermute | solution.py:215
  188.7 17.0 %collective-permute-start.58 = (bf16[2,64,1024]{2,1,0:T(8,128)(2,1)S(1)}, bf16[2,64,1024]{2,1,0:T(8,128)(2,1)S(1)}, u32[]{:S(2)}, u32[]{:S(2)}) collective-permute-start(bf16[2,64,1024]{2,1,0:T(8,128)(2,1)S(1)} %add_convert_fusion.1), channel_id=1, source_target_pairs={{0,8},{2,10},{4,12},{6,14},{8,0},{10,2},{12,4},{14,6},{1,9},{3,11}... | collective-permute-start | bytes 786440 | tf_op jit(solution)/shard_map/ppermute | solution.py:224
  189.8 13.2 %collective-permute-start.56 = (bf16[64,1536]{1,0:T(8,128)(2,1)S(1)}, bf16[64,1536]{1,0:T(8,128)(2,1)S(1)}, u32[]{:S(2)}, u32[]{:S(2)}) collective-permute-start(bf16[64,1536]{1,0:T(8,128)(2,1)S(1)} %pad_maximum_fusion.14), channel_id=1, source_target_pairs={{0,4},{2,6},{4,0},{6,2},{8,12},{10,14},{12,8},{14,10},{1,5},{3,7},... | collective-permute-start | bytes 589832 | tf_op jit(solution)/shard_map/ppermute | solution.py:215
  191.7 13.9 %collective-permute-start.57 = (bf16[64,1536]{1,0:T(8,128)(2,1)S(1)}, bf16[64,1536]{1,0:T(8,128)(2,1)S(1)}, u32[]{:S(2)}, u32[]{:S(2)}) collective-permute-start(bf16[64,1536]{1,0:T(8,128)(2,1)S(1)} %pad_maximum_fusion.14), channel_id=1, source_target_pairs={{0,6},{2,4},{4,2},{6,0},{8,14},{10,12},{12,10},{14,8},{1,7},{3,5},... | collective-permute-start | bytes 589832 | tf_op jit(solution)/shard_map/ppermute | solution.py:215
  205.9 13.9 %collective-permute-start.59 = (bf16[4,64,1536]{2,1,0:T(8,128)(2,1)S(1)}, bf16[4,64,1536]{2,1,0:T(8,128)(2,1)}, u32[]{:S(2)}, u32[]{:S(2)}) collective-permute-start(bf16[4,64,1536]{2,1,0:T(8,128)(2,1)S(1)} %get-tuple-element.136), channel_id=1, source_target_pairs={{0,1},{1,0},{2,3},{3,2},{4,5},{5,4},{6,7},{7,6},{8,9},{9,8},{10,11... | collective-permute-start | bytes 2359304 | tf_op jit(solution)/shard_map/ppermute | solution.py:218
  207.7 12.0 %collective-permute-start.68 = (bf16[64,1536]{1,0:T(8,128)(2,1)}, bf16[64,1536]{1,0:T(8,128)(2,1)S(1)}, u32[]{:S(2)}, u32[]{:S(2)}) collective-permute-start(bf16[64,1536]{1,0:T(8,128)(2,1)} %get-tuple-element.200), channel_id=1, source_target_pairs={{0,6},{2,4},{4,2},{6,0},{8,14},{10,12},{12,10},{14,8},{1,7},{3,5},... | collective-permute-start | bytes 589832 | tf_op jit(solution)/shard_map/ppermute | solution.py:215
  224.1 10.7 %collective-permute-start.64 = (bf16[128,512]{1,0:T(8,128)(2,1)S(1)}, bf16[128,512]{1,0:T(8,128)(2,1)S(1)}, u32[]{:S(2)}, u32[]{:S(2)}) collective-permute-start(bf16[128,512]{1,0:T(8,128)(2,1)S(1)} %get-tuple-element.162), channel_id=1, source_target_pairs={{0,4},{2,6},{4,0},{6,2},{8,12},{10,14},{12,8},{14,10},{1,5},{3,7},... | collective-permute-start | bytes 393224 | tf_op jit(solution)/shard_map/ppermute | solution.py:215
  224.4 11.4 %collective-permute-start.65 = (bf16[128,512]{1,0:T(8,128)(2,1)S(1)}, bf16[128,512]{1,0:T(8,128)(2,1)S(1)}, u32[]{:S(2)}, u32[]{:S(2)}) collective-permute-start(bf16[128,512]{1,0:T(8,128)(2,1)S(1)} %get-tuple-element.161), channel_id=1, source_target_pairs={{0,6},{2,4},{4,2},{6,0},{8,14},{10,12},{12,10},{14,8},{1,7},{3,5},... | collective-permute-start | bytes 393224 | tf_op jit(solution)/shard_map/ppermute | solution.py:215
  228.7 9.7 %collective-permute-start.61 = (bf16[512,128]{1,0:T(8,128)(2,1)S(1)}, bf16[512,128]{1,0:T(8,128)(2,1)S(1)}, u32[]{:S(2)}, u32[]{:S(2)}) collective-permute-start(bf16[512,128]{1,0:T(8,128)(2,1)S(1)} %get-tuple-element.166), channel_id=1, source_target_pairs={{0,4},{2,6},{4,0},{6,2},{8,12},{10,14},{12,8},{14,10},{1,5},{3,7},... | collective-permute-start | bytes 393224 | tf_op jit(solution)/shard_map/ppermute | solution.py:215
  235.8 9.1 %collective-permute-start.74 = (bf16[512,128]{1,0:T(8,128)(2,1)S(1)}, bf16[512,128]{1,0:T(8,128)(2,1)S(1)}, u32[]{:S(2)}, u32[]{:S(2)}) collective-permute-start(bf16[512,128]{1,0:T(8,128)(2,1)S(1)} %get-tuple-element.151), channel_id=1, source_target_pairs={{0,4},{2,6},{4,0},{6,2},{8,12},{10,14},{12,8},{14,10},{1,5},{3,7},... | collective-permute-start | bytes 393224 | tf_op jit(solution)/shard_map/ppermute | solution.py:215
  236.2 9.4 %collective-permute-start.75 = (bf16[512,128]{1,0:T(8,128)(2,1)S(1)}, bf16[512,128]{1,0:T(8,128)(2,1)S(1)}, u32[]{:S(2)}, u32[]{:S(2)}) collective-permute-start(bf16[512,128]{1,0:T(8,128)(2,1)S(1)} %get-tuple-element.150), channel_id=1, source_target_pairs={{0,6},{2,4},{4,2},{6,0},{8,14},{10,12},{12,10},{14,8},{1,7},{3,5},... | collective-permute-start | bytes 393224 | tf_op jit(solution)/shard_map/ppermute | solution.py:215
  (65 other events, 440.2 us)

commit v5 on v4

--- a/solution.py
+++ b/solution.py
@@ -37,8 +37,8 @@
     def _():
         lo_acc[...] = jnp.zeros_like(lo_acc)
 
-    def row_block(i, _):
-        rows = pl.ds(pl.multiple_of(i * block, block), block)
+    for i in range(x_ref.shape[0] // block):
+        rows = slice(i * block, (i + 1) * block)
         x = x_ref[rows, :]
         for j in range(pair):
             cols = slice(j * width, (j + 1) * width)
@@ -52,9 +52,6 @@
             slope = up_pre * (sig * (1.0 + gate_pre * (1.0 - sig)))
             cp_ref[rows, cols] = (slope * gate).astype(bf16)
         lo_acc[rows, :] += dot(hs_ref[rows, :], wd_ref[...])
-        return 0
-
-    lax.fori_loop(0, x_ref.shape[0] // block, row_block, 0)
 
     @pl.when(step == pl.num_programs(0) - 1)
     def _():
@@ -73,8 +70,8 @@
     def _():
         lig_acc[...] = jnp.zeros_like(lig_acc)
 
-    def row_block(i, _):
-        rows = pl.ds(pl.multiple_of(i * block, block), block)
+    for i in range(y_ref.shape[0] // block):
+        rows = slice(i * block, (i + 1) * block)
         hidden_grad = dot(y_ref[rows, :], wd_ref[...], NT)
         for j in range(pair):
             cols = slice(j * width, (j + 1) * width)
@@ -84,9 +81,6 @@
             dpu_ref[rows, 2 * j * width : (2 * j + 1) * width] = dp.astype(bf16)
             dpu_ref[rows, (2 * j + 1) * width : (2 * j + 2) * width] = du.astype(bf16)
         lig_acc[rows, :] += dot(dpu_ref[rows, :], wgu[...], NT)
-        return 0
-
-    lax.fori_loop(0, y_ref.shape[0] // block, row_block, 0)
 
     @pl.when(step == pl.num_programs(0) - 1)
     def _():
@@ -101,15 +95,12 @@
     pair, latent, width = dwg_ref.shape
     block = 256
 
-    def col_block(i, _):
-        cols = pl.ds(pl.multiple_of(i * block, block), block)
+    for i in range(latent // block):
+        cols = slice(i * block, (i + 1) * block)
         grads = dot(x_ref[:, cols], dpu_ref[...], TN)
         for j in range(pair):
             dwg_ref[j, cols, :] = grads[:, 2 * j * width : (2 * j + 1) * width].astype(bf16)
             dwu_ref[j, cols, :] = grads[:, (2 * j + 1) * width : (2 * j + 2) * width].astype(bf16)
-        return 0
-
-    lax.fori_loop(0, latent // block, col_block, 0)
 
 
 def shaped(*shape):
@@ -262,10 +253,20 @@
         return parts
 
     def square_rows(v):
-        parts = exchange(
+        return exchange(
             lambda r: lax.dynamic_slice_in_dim(v, (q ^ r) * quarter_d, quarter_d, 1)
         )
-        return jnp.concatenate(parts, axis=0)
+
+    def first_rows(v):
+        size = 2 * quarter_d
+        mine = lax.dynamic_slice_in_dim(v, q // 2 * size, size, 1)
+        other = lax.dynamic_slice_in_dim(v, (1 - q // 2) * size, size, 1)
+        return jnp.concatenate([mine, to_peer(other, 2)], axis=0)
+
+    def second_rows(v):
+        mine = lax.dynamic_slice_in_dim(v, q % 2 * quarter_d, quarter_d, 1)
+        other = lax.dynamic_slice_in_dim(v, (1 - q % 2) * quarter_d, quarter_d, 1)
+        return mine, to_peer(other, 1)
 
     def square_weight(v):
         size = quarter_d // 2 if shared else quarter_d
@@ -273,23 +274,25 @@
         parts = exchange(
             lambda r: lax.dynamic_slice_in_dim(v, (q ^ r) * quarter_d + first, size, 0)
         )
-        return jnp.concatenate(by_quarter(parts), axis=1), parts[3]
-
-    def all_features(v):
-        return flip(jnp.concatenate([v, g_swap(v)], axis=0), g, 0) if shared else v
+        return parts
+
+    def join_quarters(parts):
+        return jnp.concatenate(by_quarter(parts), axis=1)
+
+    def swap_features(v):
+        return g_swap(v) if shared else v
+
+    def all_features(v, theirs):
+        return flip(jnp.concatenate([v, theirs], axis=0), g, 0) if shared else v
 
     def project(rows, weights):
-        blocks = []
-        for weight in weights:
-            part = dot(rows, weight).astype(bf16).reshape(4, 2, half_rows, cols)
-            mine = lax.dynamic_index_in_dim(part, t, 1, keepdims=False)
-            other = lax.dynamic_index_in_dim(part, 1 - t, 1, keepdims=False)
-            part = add(mine, t_swap(other))
-            blocks.append(add(*exchange(lambda r: part[r])))
-        return jnp.concatenate(turn(blocks), axis=1)
-
-    def all_rows(part):
-        return jnp.stack([part, t_swap(part)]).reshape(-1, latent)
+        parts = [dot(rows, weight).astype(bf16) for weight in weights]
+        part = jnp.concatenate(parts, axis=1).reshape(4, 2, half_rows, latent)
+        mine = lax.dynamic_index_in_dim(part, t, 1, keepdims=False)
+        return mine, lax.dynamic_index_in_dim(part, 1 - t, 1, keepdims=False)
+
+    def own_latent(parts):
+        return jnp.concatenate(turn(jnp.split(add(*parts), nh, axis=1)), axis=1)
 
     def sum_tensor(part):
         part = part.reshape(2, 4, nh, half_rows, latent)
@@ -341,27 +344,53 @@
     )
     down_rows = down_proj.reshape(exp_local * width, latent)
 
-    down_block, down_last = square_weight(down_weight)
-    up_block, up_last = square_weight(up_weight)
-    token_rows = square_rows(after(tokens, down_last, up_last))
-    cot_rows = square_rows(after(cotangent, down_last, up_last))
-    down_parts = gather_h(down_block)
-    up_parts = gather_h(after(up_block, down_parts[-1]))
-    down_parts = [all_features(v) for v in down_parts]
-    up_parts = [all_features(v) for v in up_parts]
-
-    part_x = jnp.stack(gather_h(project(token_rows, down_parts)))
-    part_x = jnp.stack(exchange(lambda r: part_x))
-    part_y = jnp.stack(gather_h(project(cot_rows, up_parts)))
-    latent_in = all_rows(after(part_x, part_y))
-    token_parts = gather_h(after(token_rows, part_x))
+    def rows_with(part, theirs):
+        return jnp.stack([part, theirs]).reshape(-1, latent)
+
+    down_parts = gather_h(join_quarters(square_weight(down_weight)))
+    up_block = square_weight(up_weight)
+    theirs = [swap_features(down_parts[0])]
+    *up_block, down_parts[-1], theirs[0] = together(*up_block, down_parts[-1], theirs[0])
+    up_parts = gather_h(join_quarters(up_block))
+    token_rows = square_rows(after(tokens, down_parts[-1]))
+    theirs += [swap_features(v) for v in down_parts[1:]]
+    *token_rows, theirs[-1], up_parts[-1] = together(*token_rows, theirs[-1], up_parts[-1])
+    cot_rows = first_rows(after(cotangent, token_rows[-1]))
+    token_rows = jnp.concatenate(token_rows, axis=0)
+    down_parts = [all_features(v, w) for v, w in zip(down_parts, theirs)]
+
+    mine, other = project(token_rows, down_parts)
+    theirs = [swap_features(v) for v in up_parts]
+    part_x = add(mine, t_swap(other))
+    cot_rows = after(cot_rows, part_x)
+    part_x = exchange(lambda r: part_x[r])
+    mine, other = second_rows(cot_rows)
+    *part_x, other, theirs[-1] = together(*part_x, other, theirs[-1])
+    cot_rows = [v[i * tok_rows : (i + 1) * tok_rows] for i in (0, 1) for v in (mine, other)]
+    cot_rows = jnp.concatenate(cot_rows, axis=0)
+    part_x = gather_h(own_latent(part_x))
+    up_parts = [all_features(v, w) for v, w in zip(up_parts, theirs)]
+    mine, other = project(cot_rows, up_parts)
+    *part_x, other = together(*part_x, t_swap(other))
+    part_y = add(mine, other)
+    part_x = jnp.stack(part_x)
+    part_x = exchange(lambda r: part_x)
+    part_y = exchange(lambda r: part_y[r])
+    *part_x, part_y[1], part_y[2], part_y[3] = together(*part_x, *part_y[1:])
+    part_x = jnp.stack(part_x)
+    part_y = gather_h(own_latent(part_y))
+    *part_y, other = together(*part_y, t_swap(part_x))
+    part_y = jnp.stack(part_y)
+    latent_in = rows_with(part_x, other)
+    token_parts = gather_h(after(token_rows, other))
 
     hs, cp, cu, out_part = forward(
         latent_in, gate_blocks(gate_columns), gate_proj, up_proj, down_rows
     )
     part_y = exchange(lambda r: part_y)
     *part_y, token_parts[-1], out_part = together(*part_y, token_parts[-1], out_part)
-    latent_grad = all_rows(jnp.stack(part_y))
+    part_y = jnp.stack(part_y)
+    latent_grad = rows_with(part_y, t_swap(part_y))
     cot_parts = gather_h(after(cot_rows, token_parts[-1]))
     out_part = sum_tensor(out_part)
     down_proj_grad = down_grads(hs, latent_grad)

time: 252 us -> 267 us (1.060)
  waiting for transfers between devices: 96.7 us -> 125 us
  starting transfers between devices: 76.8 us -> 64.8 us
  Pallas kernels: 49 us -> 45.5 us
    ppermute x54 -> x47, waiting for transfers between devices: 51.1 us -> 99 us  [to_peer(): return lax.ppermute(v, 'expert', [(e, e ^ r) for e in range(n_expert)])]
    ppermute x4, waiting for transfers between devices: 12.6 us -> 0.01 us  [g_swap(): return lax.ppermute(v, 'group', [(i, i ^ 1) for i in range(n_group)])]
    ppermute x54 -> x47, starting transfers between devices: 64.4 us -> 53.6 us  [to_peer(): return lax.ppermute(v, 'expert', [(e, e ^ r) for e in range(n_expert)])]
    ppermute x8, waiting for transfers between devices: 26.9 us -> 21.4 us  [up(): lax.ppermute(v, 'expert', [(e, (e + 4) % n_expert) for e in range(n_exper...]
    ppermute x10 -> x8, waiting for transfers between devices: 6.14 us -> 4.23 us  [t_swap(): return lax.ppermute(v, 'tensor', [(0, 1), (1, 0)])]
  transfers between devices with their start and end apart: 76 -> 67, of which waited for: 31 -> 33; matrix products, arithmetic and copies ran while one was open for 8% -> 7% of each run, Pallas kernels for 19% -> 17%
where the time goes in v5:
time: 267 us
  waiting for transfers between devices  125 us (47%)
  starting transfers between devices  64.8 us (24%)
  Pallas kernels  45.5 us (17%)
  other arithmetic  13.6 us (5%)
  matrix products  8.31 us (3%)
  local copies, waits for them, and re-layouts  8.09 us (3%)
    ppermute x47, waiting for transfers between devices, to_peer(): return lax.ppermute(v, 'expert', [(e, e ^ r) for e in range(n_expert)])  99 us
    ppermute x47, starting transfers between devices, to_peer(): return lax.ppermute(v, 'expert', [(e, e ^ r) for e in range(n_expert)])  53.6 us
    ppermute x8, waiting for transfers between devices, up(): lax.ppermute(v, 'expert', [(e, (e + 4) % n_expert) for e in range(n_exper...  21.4 us
    pallas_call x1, Pallas kernels, local(): forward(latent_in, gate_blocks(gate_columns), gate_proj, up_proj, down_rows)  15.8 us
    pallas_call x1, Pallas kernels, local(): backward(after(latent_grad, out_part), cp, cu, gate_proj, up_proj, down_r...  15.4 us
    pallas_call x1, Pallas kernels, local(): gate_proj_grad, up_proj_grad = input_grads(latent_in, after(dpu, in_part))  9.04 us
    dot_general x12, matrix products, dot(): return lax.dot_general(a, b, dims, preferred_element_type=f32)  8.31 us
    ppermute x8, starting transfers between devices, up(): lax.ppermute(v, 'expert', [(e, (e + 4) % n_expert) for e in range(n_exper...  5.5 us
  transfers between devices with their start and end apart: 67, of which 33 were waited for; matrix products, arithmetic and copies ran while one was open for 7% of the time, Pallas kernels for 17%

profile of v5, /device:TPU:0, one launch (start us, length us, event | category | flops | bytes accessed | tf_op | source)
XLA Modules:
  0.0 266.9 jit_solution(9211509647491768057)
XLA Ops:
  1.7 3.0 %collective-permute-start.3 = (bf16[256,128]{1,0:T(8,128)(2,1)S(1)}, bf16[256,128]{1,0:T(8,128)(2,1)S(1)}, u32[]{:S(2)}, u32[]{:S(2)}) collective-permute-start(bf16[256,128]{1,0:T(8,128)(2,1)S(1)} %get-tuple-element.238), channel_id=1, source_target_pairs={{0,2},{2,0},{4,6},{6,4},{8,10},{10,8},{12,14},{14,12},{1,3},{3,1},... | collective-permute-start | bytes 196616 | tf_op jit(solution)/shard_map/ppermute | solution.py:206
  4.7 1.6 collective-permute-start.4
  6.9 2.5 collective-permute-done.4
  9.5 1.9 collective-permute-done.5
  12.4 2.7 collective-permute-start.6
  18.9 2.2 collective-permute-start.2
  22.2 3.9 %collective-permute-done.1 = bf16[256,128]{1,0:T(8,128)(2,1)S(1)} collective-permute-done((bf16[256,128]{1,0:T(8,128)(2,1)S(1)}, bf16[256,128]{1,0:T(8,128)(2,1)S(1)}, u32[]{:S(2)}, u32[]{:S(2)}) %collective-permute-start.1) | collective-permute-done | bytes 65568 | tf_op jit(solution)/shard_map/ppermute | solution.py:206
  29.0 1.7 collective-permute-start.10
  32.6 8.1 %collective-permute-done.10 = bf16[128,512]{1,0:T(8,128)(2,1)S(1)} collective-permute-done((bf16[128,512]{1,0:T(8,128)(2,1)S(1)}, bf16[128,512]{1,0:T(8,128)(2,1)S(1)}, u32[]{:S(2)}, u32[]{:S(2)}) %collective-permute-start.10) | collective-permute-done | bytes 131104 | tf_op jit(solution)/shard_map/ppermute | solution.py:206
  46.7 7.4 %collective-permute-done.13 = bf16[128,1024]{1,0:T(8,128)(2,1)S(1)} collective-permute-done((bf16[128,1024]{1,0:T(8,128)(2,1)S(1)}, bf16[128,1024]{1,0:T(8,128)(2,1)S(1)}, u32[]{:S(2)}, u32[]{:S(2)}) %collective-permute-start.13) | collective-permute-done | bytes 262176 | tf_op jit(solution)/shard_map/ppermute | solution.py:206
  56.8 1.7 collective-permute-start.17
  59.4 8.7 %collective-permute-done.15 = bf16[64,1024]{1,0:T(8,128)(2,1)S(1)} collective-permute-done((bf16[64,1024]{1,0:T(8,128)(2,1)S(1)}, bf16[64,1024]{1,0:T(8,128)(2,1)S(1)}, u32[]{:S(2)}, u32[]{:S(2)}) %collective-permute-start.15) | collective-permute-done | bytes 131104 | tf_op jit(solution)/shard_map/ppermute | solution.py:206
  68.2 1.8 convolution_convert_fusion
  72.4 8.9 %collective-permute-done.21 = bf16[64,1024]{1,0:T(8,128)(2,1)S(1)} collective-permute-done((bf16[64,1024]{1,0:T(8,128)(2,1)S(1)}, bf16[64,1024]{1,0:T(8,128)(2,1)S(1)}, u32[]{:S(2)}, u32[]{:S(2)}) %collective-permute-start.21) | collective-permute-done | bytes 131104 | tf_op jit(solution)/shard_map/ppermute | solution.py:215
  82.1 1.6 collective-permute-start.23
  83.8 1.9 collective-permute-start.25
  85.8 2.2 collective-permute-done.26
  88.8 12.6 %collective-permute-done.27 = bf16[64,1024]{1,0:T(8,128)(2,1)S(1)} collective-permute-done((bf16[64,1024]{1,0:T(8,128)(2,1)S(1)}, bf16[64,1024]{1,0:T(8,128)(2,1)S(1)}, u32[]{:S(2)}, u32[]{:S(2)}) %collective-permute-start.27) | collective-permute-done | bytes 131104 | tf_op jit(solution)/shard_map/ppermute | solution.py:206
  105.6 7.0 %collective-permute-done.29 = bf16[64,1024]{1,0:T(8,128)(2,1)} collective-permute-done((bf16[64,1024]{1,0:T(8,128)(2,1)S(1)}, bf16[64,1024]{1,0:T(8,128)(2,1)}, u32[]{:S(2)}, u32[]{:S(2)}) %collective-permute-start.29) | collective-permute-done | bytes 131104 | tf_op jit(solution)/shard_map/ppermute | solution.py:215
  115.1 2.0 collective-permute-start.33
  119.4 15.8 %shard_map.144 = (bf16[1024,1536]{1,0:T(8,128)(2,1)S(1)}, bf16[1024,1536]{1,0:T(8,128)(2,1)S(1)}, bf16[1024,1536]{1,0:T(8,128)(2,1)}, bf16[1024,1024]{1,0:T(8,128)(2,1)S(1)}) custom-call(bf16[1024,1024]{1,0:T(8,128)(2,1)S(1)} %bitcast.183, f32[2,1024,2]{2,1,0:T(8,128)S(1)} %bitcast.187, bf16[4,1024,384]{2,1,0:T(8,128)(2,1)} %wg_ref.3, ...), custom_call_target="tpu_custom_call" | custom-call | flops 9663676416 | bytes 23068672 | tf_op jit(solution)/shard_map/pallas_call | solution.py:387
  135.2 1.9 collective-permute-done.33
  137.1 5.5 %collective-permute-done.34 = bf16[512,512]{1,0:T(8,128)(2,1)S(1)} collective-permute-done((bf16[512,512]{1,0:T(8,128)(2,1)}, bf16[512,512]{1,0:T(8,128)(2,1)S(1)}, u32[]{:S(2)}, u32[]{:S(2)}) %collective-permute-start.34) | collective-permute-done | bytes 524320 | tf_op jit(solution)/shard_map/ppermute | solution.py:215
  143.8 1.6 collective-permute-done.36
  145.7 5.3 %shard_map.145 = bf16[1536,1024]{1,0:T(8,128)(2,1)} custom-call(bf16[1024,1536]{1,0:T(8,128)(2,1)S(1)} %get-tuple-element.125.hs_ref, bf16[1024,1024]{1,0:T(8,128)(2,1)S(1)} %bitcast.185), custom_call_target="tpu_custom_call" | custom-call | flops 3221225472 | bytes 8388608 | tf_op jit(solution)/shard_map/pallas_call | solution.py:396
  151.5 1.6 collective-permute-start.37
  153.5 1.6 collective-permute-start.39
  155.0 15.4 %shard_map.146 = (bf16[1024,3072]{1,0:T(8,128)(2,1)}, bf16[1024,1024]{1,0:T(8,128)(2,1)S(1)}) custom-call(bf16[1024,1024]{1,0:T(8,128)(2,1)S(1)} %bitcast.186, bf16[1024,1536]{1,0:T(8,128)(2,1)S(1)} %get-tuple-element.132.cp_ref, bf16[1024,1536]{1,0:T(8,128)(2,1)S(1)} %copy-done.2, bf16[4,1024,384]{2,1,0:T(8,128)(2,1)S(1)} %copy-done, ...), custom_call_target="tpu_custom_call" | custom-call | flops 9663676416 | bytes 26214400 | tf_op jit(solution)/shard_map/pallas_call | solution.py:398
  170.5 2.9 %collective-permute-done.38 = bf16[2,64,1024]{2,1,0:T(8,128)(2,1)S(1)} collective-permute-done((bf16[2,64,1024]{2,1,0:T(8,128)(2,1)S(1)}, bf16[2,64,1024]{2,1,0:T(8,128)(2,1)S(1)}, u32[]{:S(2)}, u32[]{:S(2)}) %collective-permute-start.38) | collective-permute-done | bytes 262176 | tf_op jit(solution)/shard_map/ppermute | solution.py:206
  173.4 4.5 %collective-permute-done.39 = bf16[2,64,1024]{2,1,0:T(8,128)(2,1)S(1)} collective-permute-done((bf16[2,64,1024]{2,1,0:T(8,128)(2,1)S(1)}, bf16[2,64,1024]{2,1,0:T(8,128)(2,1)S(1)}, u32[]{:S(2)}, u32[]{:S(2)}) %collective-permute-start.39) | collective-permute-done | bytes 262176 | tf_op jit(solution)/shard_map/ppermute | solution.py:206
  178.4 2.6 collective-permute-done.41
  183.0 2.0 collective-permute-start.44
  185.0 9.0 %shard_map.147 = (bf16[4,1024,384]{2,1,0:T(8,128)(2,1)}, bf16[4,1024,384]{2,1,0:T(8,128)(2,1)}) custom-call(bf16[1024,1024]{1,0:T(8,128)(2,1)S(1)} %bitcast.184, bf16[1024,3072]{1,0:T(8,128)(2,1)S(1)} %copy-done.1), custom_call_target="tpu_custom_call" | custom-call | flops 6442450944 | bytes 14680064 | tf_op jit(solution)/shard_map/pallas_call | solution.py:405
  194.1 3.7 %collective-permute-done.43 = bf16[2,64,1024]{2,1,0:T(8,128)(2,1)S(1)} collective-permute-done((bf16[2,64,1024]{2,1,0:T(8,128)(2,1)S(1)}, bf16[2,64,1024]{2,1,0:T(8,128)(2,1)S(1)}, u32[]{:S(2)}, u32[]{:S(2)}) %collective-permute-start.43) | collective-permute-done | bytes 262176 | tf_op jit(solution)/shard_map/ppermute | solution.py:206
  197.7 4.5 %collective-permute-done.44 = bf16[2,64,1024]{2,1,0:T(8,128)(2,1)S(1)} collective-permute-done((bf16[2,64,1024]{2,1,0:T(8,128)(2,1)S(1)}, bf16[2,64,1024]{2,1,0:T(8,128)(2,1)S(1)}, u32[]{:S(2)}, u32[]{:S(2)}) %collective-permute-start.44) | collective-permute-done | bytes 262176 | tf_op jit(solution)/shard_map/ppermute | solution.py:206
  202.6 1.6 collective-permute-start.46
  204.1 2.1 collective-permute-start.47
  208.4 9.0 %collective-permute-done.47 = bf16[64,1536]{1,0:T(8,128)(2,1)S(1)} collective-permute-done((bf16[64,1536]{1,0:T(8,128)(2,1)S(1)}, bf16[64,1536]{1,0:T(8,128)(2,1)S(1)}, u32[]{:S(2)}, u32[]{:S(2)}) %collective-permute-start.47) | collective-permute-done | bytes 196640 | tf_op jit(solution)/shard_map/ppermute | solution.py:206
  217.4 2.8 %collective-permute-done.48 = bf16[64,1536]{1,0:T(8,128)(2,1)S(1)} collective-permute-done((bf16[64,1536]{1,0:T(8,128)(2,1)S(1)}, bf16[64,1536]{1,0:T(8,128)(2,1)S(1)}, u32[]{:S(2)}, u32[]{:S(2)}) %collective-permute-start.48) | collective-permute-done | bytes 196640 | tf_op jit(solution)/shard_map/ppermute | solution.py:206
  222.0 2.7 %collective-permute-start.59 = (bf16[64,1536]{1,0:T(8,128)(2,1)}, bf16[64,1536]{1,0:T(8,128)(2,1)}, u32[]{:S(2)}, u32[]{:S(2)}) collective-permute-start(bf16[64,1536]{1,0:T(8,128)(2,1)} %get-tuple-element.252), channel_id=1, source_target_pairs={{0,6},{2,4},{4,2},{6,0},{8,14},{10,12},{12,10},{14,8},{1,7},{3,5},... | collective-permute-start | bytes 589832 | tf_op jit(solution)/shard_map/ppermute | solution.py:206
  224.8 4.0 %collective-permute-done.57 = bf16[64,1536]{1,0:T(8,128)(2,1)S(1)} collective-permute-done((bf16[64,1536]{1,0:T(8,128)(2,1)}, bf16[64,1536]{1,0:T(8,128)(2,1)S(1)}, u32[]{:S(2)}, u32[]{:S(2)}) %collective-permute-start.57) | collective-permute-done | bytes 196640 | tf_op jit(solution)/shard_map/ppermute | solution.py:206
  230.0 4.3 %collective-permute-done.59 = bf16[64,1536]{1,0:T(8,128)(2,1)} collective-permute-done((bf16[64,1536]{1,0:T(8,128)(2,1)}, bf16[64,1536]{1,0:T(8,128)(2,1)}, u32[]{:S(2)}, u32[]{:S(2)}) %collective-permute-start.59) | collective-permute-done | bytes 196640 | tf_op jit(solution)/shard_map/ppermute | solution.py:206
  235.9 1.7 fusion.10
  239.4 2.4 collective-permute-start.56
  246.9 2.5 collective-permute-start.53
  251.1 2.4 collective-permute-start.66
  255.7 1.6 collective-permute-start.62
  263.1 2.0 collective-permute-done.63
  (281 shorter events, 64.5 us)
Async XLA Ops:
  12.4 14.8 %collective-permute-start.6 = (bf16[256,512]{1,0:T(8,128)(2,1)S(1)}, bf16[256,512]{1,0:T(8,128)(2,1)S(1)}, u32[]{:S(2)}, u32[]{:S(2)}) collective-permute-start(bf16[256,512]{1,0:T(8,128)(2,1)S(1)} %pad_maximum_fusion.12), channel_id=1, source_target_pairs={{0,8},{2,10},{4,12},{6,14},{8,0},{10,2},{12,4},{14,6},{1,9},{3,11}... | collective-permute-start | bytes 786440 | tf_op jit(solution)/shard_map/ppermute | solution.py:215
  15.1 12.2 %collective-permute-start.7 = (bf16[256,512]{1,0:T(8,128)(2,1)S(1)}, bf16[256,512]{1,0:T(8,128)(2,1)S(1)}, u32[]{:S(2)}, u32[]{:S(2)}) collective-permute-start(bf16[256,512]{1,0:T(8,128)(2,1)S(1)} %pad_maximum_fusion.12), channel_id=1, source_target_pairs={{0,16},{16,0},{1,17},{17,1},{2,18},{18,2},{3,19},{19,3},{4,20},{20... | collective-permute-start | bytes 786440 | tf_op jit(solution)/shard_map/ppermute | solution.py:212
  27.4 14.8 %collective-permute-start.12 = (bf16[256,512]{1,0:T(8,128)(2,1)S(1)}, bf16[256,512]{1,0:T(8,128)(2,1)}, u32[]{:S(2)}, u32[]{:S(2)}) collective-permute-start(bf16[256,512]{1,0:T(8,128)(2,1)S(1)} %pad_maximum_fusion.13), channel_id=1, source_target_pairs={{0,8},{2,10},{4,12},{6,14},{8,0},{10,2},{12,4},{14,6},{1,9},{3,11}... | collective-permute-start | bytes 786440 | tf_op jit(solution)/shard_map/ppermute | solution.py:215
  27.5 14.7 %collective-permute-start.11 = (bf16[256,512]{1,0:T(8,128)(2,1)S(1)}, bf16[256,512]{1,0:T(8,128)(2,1)S(1)}, u32[]{:S(2)}, u32[]{:S(2)}) collective-permute-start(bf16[256,512]{1,0:T(8,128)(2,1)S(1)} %collective-permute-done.6), channel_id=1, source_target_pairs={{0,16},{16,0},{1,17},{17,1},{2,18},{18,2},{3,19},{19,3},{4,20},{20... | collective-permute-start | bytes 786440 | tf_op jit(solution)/shard_map/ppermute | solution.py:212
  29.0 11.7 %collective-permute-start.10 = (bf16[128,512]{1,0:T(8,128)(2,1)S(1)}, bf16[128,512]{1,0:T(8,128)(2,1)S(1)}, u32[]{:S(2)}, u32[]{:S(2)}) collective-permute-start(bf16[128,512]{1,0:T(8,128)(2,1)S(1)} %get-tuple-element.234), channel_id=1, source_target_pairs={{0,6},{2,4},{4,2},{6,0},{8,14},{10,12},{12,10},{14,8},{1,7},{3,5},... | collective-permute-start | bytes 393224 | tf_op jit(solution)/shard_map/ppermute | solution.py:206
  30.7 10.0 %collective-permute-start.8 = (bf16[128,512]{1,0:T(8,128)(2,1)S(1)}, bf16[128,512]{1,0:T(8,128)(2,1)S(1)}, u32[]{:S(2)}, u32[]{:S(2)}) collective-permute-start(bf16[128,512]{1,0:T(8,128)(2,1)S(1)} %get-tuple-element.236), channel_id=1, source_target_pairs={{0,2},{2,0},{4,6},{6,4},{8,10},{10,8},{12,14},{14,12},{1,3},{3,1},... | collective-permute-start | bytes 393224 | tf_op jit(solution)/shard_map/ppermute | solution.py:206
  32.1 10.1 %collective-permute-start.9 = (bf16[128,512]{1,0:T(8,128)(2,1)S(1)}, bf16[128,512]{1,0:T(8,128)(2,1)S(1)}, u32[]{:S(2)}, u32[]{:S(2)}) collective-permute-start(bf16[128,512]{1,0:T(8,128)(2,1)S(1)} %get-tuple-element.235), channel_id=1, source_target_pairs={{0,4},{2,6},{4,0},{6,2},{8,12},{10,14},{12,8},{14,10},{1,5},{3,7},... | collective-permute-start | bytes 393224 | tf_op jit(solution)/shard_map/ppermute | solution.py:206
  45.2 8.9 %collective-permute-start.14 = (bf16[4,64,1024]{2,1,0:T(8,128)(2,1)}, bf16[4,64,1024]{2,1,0:T(8,128)(2,1)S(1)}, u32[]{:S(2)}, u32[]{:S(2)}) collective-permute-start(bf16[4,64,1024]{2,1,0:T(8,128)(2,1)} %dynamic-slice_bitcast_fusion.1), channel_id=1, source_target_pairs={{0,1},{1,0},{2,3},{3,2},{4,5},{5,4},{6,7},{7,6},{8,9},{9,8},{10,11... | collective-permute-start | bytes 1572872 | tf_op jit(solution)/shard_map/ppermute | solution.py:209
  45.3 8.8 %collective-permute-start.13 = (bf16[128,1024]{1,0:T(8,128)(2,1)S(1)}, bf16[128,1024]{1,0:T(8,128)(2,1)S(1)}, u32[]{:S(2)}, u32[]{:S(2)}) collective-permute-start(bf16[128,1024]{1,0:T(8,128)(2,1)S(1)} %get-tuple-element.229), channel_id=1, source_target_pairs={{0,4},{2,6},{4,0},{6,2},{8,12},{10,14},{12,8},{14,10},{1,5},{3,7},... | collective-permute-start | bytes 786440 | tf_op jit(solution)/shard_map/ppermute | solution.py:206
  45.5 13.0 %collective-permute-start.19 = (bf16[256,512]{1,0:T(8,128)(2,1)}, bf16[256,512]{1,0:T(8,128)(2,1)}, u32[]{:S(2)}, u32[]{:S(2)}) collective-permute-start(bf16[256,512]{1,0:T(8,128)(2,1)} %collective-permute-done.12), channel_id=1, source_target_pairs={{0,16},{16,0},{1,17},{17,1},{2,18},{18,2},{3,19},{19,3},{4,20},{20... | collective-permute-start | bytes 786440 | tf_op jit(solution)/shard_map/ppermute | solution.py:212
  54.4 13.7 %collective-permute-start.18 = (bf16[256,512]{1,0:T(8,128)(2,1)S(1)}, bf16[256,512]{1,0:T(8,128)(2,1)S(1)}, u32[]{:S(2)}, u32[]{:S(2)}) collective-permute-start(bf16[256,512]{1,0:T(8,128)(2,1)S(1)} %constant_dynamic-slice_fusion.8), channel_id=1, source_target_pairs={{0,2},{2,0},{4,6},{6,4},{8,10},{10,8},{12,14},{14,12},{1,3},{3,1},... | collective-permute-start | bytes 786440 | tf_op jit(solution)/shard_map/ppermute | solution.py:206
  55.0 13.2 %collective-permute-start.15 = (bf16[64,1024]{1,0:T(8,128)(2,1)S(1)}, bf16[64,1024]{1,0:T(8,128)(2,1)S(1)}, u32[]{:S(2)}, u32[]{:S(2)}) collective-permute-start(bf16[64,1024]{1,0:T(8,128)(2,1)S(1)} %get-tuple-element.232), channel_id=1, source_target_pairs={{0,2},{2,0},{4,6},{6,4},{8,10},{10,8},{12,14},{14,12},{1,3},{3,1},... | collective-permute-start | bytes 393224 | tf_op jit(solution)/shard_map/ppermute | solution.py:206
  56.5 11.6 %collective-permute-start.16 = (bf16[64,1024]{1,0:T(8,128)(2,1)S(1)}, bf16[64,1024]{1,0:T(8,128)(2,1)S(1)}, u32[]{:S(2)}, u32[]{:S(2)}) collective-permute-start(bf16[64,1024]{1,0:T(8,128)(2,1)S(1)} %get-tuple-element.231), channel_id=1, source_target_pairs={{0,4},{2,6},{4,0},{6,2},{8,12},{10,14},{12,8},{14,10},{1,5},{3,7},... | collective-permute-start | bytes 393224 | tf_op jit(solution)/shard_map/ppermute | solution.py:206
  56.8 11.4 %collective-permute-start.17 = (bf16[64,1024]{1,0:T(8,128)(2,1)S(1)}, bf16[64,1024]{1,0:T(8,128)(2,1)S(1)}, u32[]{:S(2)}, u32[]{:S(2)}) collective-permute-start(bf16[64,1024]{1,0:T(8,128)(2,1)S(1)} %get-tuple-element.230), channel_id=1, source_target_pairs={{0,6},{2,4},{4,2},{6,0},{8,14},{10,12},{12,10},{14,8},{1,7},{3,5},... | collective-permute-start | bytes 393224 | tf_op jit(solution)/shard_map/ppermute | solution.py:206
  58.5 11.5 %collective-permute-start.20 = (bf16[256,512]{1,0:T(8,128)(2,1)S(1)}, bf16[256,512]{1,0:T(8,128)(2,1)S(1)}, u32[]{:S(2)}, u32[]{:S(2)}) collective-permute-start(bf16[256,512]{1,0:T(8,128)(2,1)S(1)} %copy-done.16), channel_id=1, source_target_pairs={{0,16},{16,0},{1,17},{17,1},{2,18},{18,2},{3,19},{19,3},{4,20},{20... | collective-permute-start | bytes 786440 | tf_op jit(solution)/shard_map/ppermute | solution.py:212
  71.5 9.8 %collective-permute-start.22 = (bf16[4,64,1024]{2,1,0:T(8,128)(2,1)S(1)}, bf16[4,64,1024]{2,1,0:T(8,128)(2,1)S(1)}, u32[]{:S(2)}, u32[]{:S(2)}) collective-permute-start(bf16[4,64,1024]{2,1,0:T(8,128)(2,1)S(1)} %dynamic-slice_bitcast_fusion), channel_id=1, source_target_pairs={{0,1},{1,0},{2,3},{3,2},{4,5},{5,4},{6,7},{7,6},{8,9},{9,8},{10,11... | collective-permute-start | bytes 1572872 | tf_op jit(solution)/shard_map/ppermute | solution.py:209
  71.7 9.6 %collective-permute-start.21 = (bf16[64,1024]{1,0:T(8,128)(2,1)S(1)}, bf16[64,1024]{1,0:T(8,128)(2,1)S(1)}, u32[]{:S(2)}, u32[]{:S(2)}) collective-permute-start(bf16[64,1024]{1,0:T(8,128)(2,1)S(1)} %pad_maximum_fusion.18), channel_id=1, source_target_pairs={{0,8},{2,10},{4,12},{6,14},{8,0},{10,2},{12,4},{14,6},{1,9},{3,11}... | collective-permute-start | bytes 393224 | tf_op jit(solution)/shard_map/ppermute | solution.py:215
  82.1 20.5 %collective-permute-start.23 = (bf16[2,64,1024]{2,1,0:T(8,128)(2,1)S(1)}, bf16[2,64,1024]{2,1,0:T(8,128)(2,1)S(1)}, u32[]{:S(2)}, u32[]{:S(2)}) collective-permute-start(bf16[2,64,1024]{2,1,0:T(8,128)(2,1)S(1)} %pad_maximum_fusion.14), channel_id=1, source_target_pairs={{0,2},{2,0},{4,6},{6,4},{8,10},{10,8},{12,14},{14,12},{1,3},{3,1},... | collective-permute-start | bytes 786440 | tf_op jit(solution)/shard_map/ppermute | solution.py:206
  83.8 18.9 %collective-permute-start.24 = (bf16[2,64,1024]{2,1,0:T(8,128)(2,1)S(1)}, bf16[2,64,1024]{2,1,0:T(8,128)(2,1)S(1)}, u32[]{:S(2)}, u32[]{:S(2)}) collective-permute-start(bf16[2,64,1024]{2,1,0:T(8,128)(2,1)S(1)} %pad_maximum_fusion.14), channel_id=1, source_target_pairs={{0,4},{2,6},{4,0},{6,2},{8,12},{10,14},{12,8},{14,10},{1,5},{3,7},... | collective-permute-start | bytes 786440 | tf_op jit(solution)/shard_map/ppermute | solution.py:206
  83.8 18.9 %collective-permute-start.25 = (bf16[2,64,1024]{2,1,0:T(8,128)(2,1)S(1)}, bf16[2,64,1024]{2,1,0:T(8,128)(2,1)S(1)}, u32[]{:S(2)}, u32[]{:S(2)}) collective-permute-start(bf16[2,64,1024]{2,1,0:T(8,128)(2,1)S(1)} %pad_maximum_fusion.14), channel_id=1, source_target_pairs={{0,6},{2,4},{4,2},{6,0},{8,14},{10,12},{12,10},{14,8},{1,7},{3,5},... | collective-permute-start | bytes 786440 | tf_op jit(solution)/shard_map/ppermute | solution.py:206
  85.7 15.6 %collective-permute-start.27 = (bf16[64,1024]{1,0:T(8,128)(2,1)S(1)}, bf16[64,1024]{1,0:T(8,128)(2,1)S(1)}, u32[]{:S(2)}, u32[]{:S(2)}) collective-permute-start(bf16[64,1024]{1,0:T(8,128)(2,1)S(1)} %get-tuple-element.224), channel_id=1, source_target_pairs={{0,4},{2,6},{4,0},{6,2},{8,12},{10,14},{12,8},{14,10},{1,5},{3,7},... | collective-permute-start | bytes 393224 | tf_op jit(solution)/shard_map/ppermute | solution.py:206
  88.0 14.7 %collective-permute-start.28 = (bf16[64,1024]{1,0:T(8,128)(2,1)S(1)}, bf16[64,1024]{1,0:T(8,128)(2,1)S(1)}, u32[]{:S(2)}, u32[]{:S(2)}) collective-permute-start(bf16[64,1024]{1,0:T(8,128)(2,1)S(1)} %get-tuple-element.223), channel_id=1, source_target_pairs={{0,6},{2,4},{4,2},{6,0},{8,14},{10,12},{12,10},{14,8},{1,7},{3,5},... | collective-permute-start | bytes 393224 | tf_op jit(solution)/shard_map/ppermute | solution.py:206
  102.9 9.8 %collective-permute-start.30 = (bf16[4,2,64,1024]{3,2,1,0:T(8,128)(2,1)S(1)}, bf16[4,2,64,1024]{3,2,1,0:T(8,128)(2,1)}, u32[]{:S(2)}, u32[]{:S(2)}) collective-permute-start(bf16[4,2,64,1024]{3,2,1,0:T(8,128)(2,1)S(1)} %get-tuple-element.180), channel_id=1, source_target_pairs={{0,1},{1,0},{2,3},{3,2},{4,5},{5,4},{6,7},{7,6},{8,9},{9,8},{10,11... | collective-permute-start | bytes 3145736 | tf_op jit(solution)/shard_map/ppermute | solution.py:209
  103.1 9.5 %collective-permute-start.29 = (bf16[64,1024]{1,0:T(8,128)(2,1)S(1)}, bf16[64,1024]{1,0:T(8,128)(2,1)}, u32[]{:S(2)}, u32[]{:S(2)}) collective-permute-start(bf16[64,1024]{1,0:T(8,128)(2,1)S(1)} %pad_maximum_fusion.19), channel_id=1, source_target_pairs={{0,8},{2,10},{4,12},{6,14},{8,0},{10,2},{12,4},{14,6},{1,9},{3,11}... | collective-permute-start | bytes 393224 | tf_op jit(solution)/shard_map/ppermute | solution.py:215
  113.6 21.6 %collective-permute-start.31 = (bf16[2,64,1024]{2,1,0:T(8,128)(2,1)S(1)}, bf16[2,64,1024]{2,1,0:T(8,128)(2,1)S(1)}, u32[]{:S(2)}, u32[]{:S(2)}) collective-permute-start(bf16[2,64,1024]{2,1,0:T(8,128)(2,1)S(1)} %pad_maximum_fusion.15), channel_id=1, source_target_pairs={{0,2},{2,0},{4,6},{6,4},{8,10},{10,8},{12,14},{14,12},{1,3},{3,1},... | collective-permute-start | bytes 786440 | tf_op jit(solution)/shard_map/ppermute | solution.py:206
  115.1 20.1 %collective-permute-start.32 = (bf16[2,64,1024]{2,1,0:T(8,128)(2,1)S(1)}, bf16[2,64,1024]{2,1,0:T(8,128)(2,1)S(1)}, u32[]{:S(2)}, u32[]{:S(2)}) collective-permute-start(bf16[2,64,1024]{2,1,0:T(8,128)(2,1)S(1)} %pad_maximum_fusion.15), channel_id=1, source_target_pairs={{0,4},{2,6},{4,0},{6,2},{8,12},{10,14},{12,8},{14,10},{1,5},{3,7},... | collective-permute-start | bytes 786440 | tf_op jit(solution)/shard_map/ppermute | solution.py:206
  115.1 22.0 %collective-permute-start.33 = (bf16[2,64,1024]{2,1,0:T(8,128)(2,1)S(1)}, bf16[2,64,1024]{2,1,0:T(8,128)(2,1)S(1)}, u32[]{:S(2)}, u32[]{:S(2)}) collective-permute-start(bf16[2,64,1024]{2,1,0:T(8,128)(2,1)S(1)} %pad_maximum_fusion.15), channel_id=1, source_target_pairs={{0,6},{2,4},{4,2},{6,0},{8,14},{10,12},{12,10},{14,8},{1,7},{3,5},... | collective-permute-start | bytes 786440 | tf_op jit(solution)/shard_map/ppermute | solution.py:206
  117.1 25.4 %collective-permute-start.34 = (bf16[512,512]{1,0:T(8,128)(2,1)}, bf16[512,512]{1,0:T(8,128)(2,1)S(1)}, u32[]{:S(2)}, u32[]{:S(2)}) collective-permute-start(bf16[512,512]{1,0:T(8,128)(2,1)} %copy-done.3), channel_id=1, source_target_pairs={{0,8},{2,10},{4,12},{6,14},{8,0},{10,2},{12,4},{14,6},{1,9},{3,11}... | collective-permute-start | bytes 1572872 | tf_op jit(solution)/shard_map/ppermute | solution.py:215
  143.8 26.7 %collective-permute-start.40 = (bf16[512,512]{1,0:T(8,128)(2,1)S(1)}, bf16[512,512]{1,0:T(8,128)(2,1)S(1)}, u32[]{:S(2)}, u32[]{:S(2)}) collective-permute-start(bf16[512,512]{1,0:T(8,128)(2,1)S(1)} %pad_maximum_fusion.9), channel_id=1, source_target_pairs={{0,8},{2,10},{4,12},{6,14},{8,0},{10,2},{12,4},{14,6},{1,9},{3,11}... | collective-permute-start | bytes 1572872 | tf_op jit(solution)/shard_map/ppermute | solution.py:215
  151.5 19.0 %collective-permute-start.37 = (bf16[2,64,1024]{2,1,0:T(8,128)(2,1)S(1)}, bf16[2,64,1024]{2,1,0:T(8,128)(2,1)S(1)}, u32[]{:S(2)}, u32[]{:S(2)}) collective-permute-start(bf16[2,64,1024]{2,1,0:T(8,128)(2,1)S(1)} %get-tuple-element.175), channel_id=1, source_target_pairs={{0,2},{2,0},{4,6},{6,4},{8,10},{10,8},{12,14},{14,12},{1,3},{3,1},... | collective-permute-start | bytes 786440 | tf_op jit(solution)/shard_map/ppermute | solution.py:206
  153.0 20.3 %collective-permute-start.38 = (bf16[2,64,1024]{2,1,0:T(8,128)(2,1)S(1)}, bf16[2,64,1024]{2,1,0:T(8,128)(2,1)S(1)}, u32[]{:S(2)}, u32[]{:S(2)}) collective-permute-start(bf16[2,64,1024]{2,1,0:T(8,128)(2,1)S(1)} %get-tuple-element.174), channel_id=1, source_target_pairs={{0,4},{2,6},{4,0},{6,2},{8,12},{10,14},{12,8},{14,10},{1,5},{3,7},... | collective-permute-start | bytes 786440 | tf_op jit(solution)/shard_map/ppermute | solution.py:206
  153.5 24.4 %collective-permute-start.39 = (bf16[2,64,1024]{2,1,0:T(8,128)(2,1)S(1)}, bf16[2,64,1024]{2,1,0:T(8,128)(2,1)S(1)}, u32[]{:S(2)}, u32[]{:S(2)}) collective-permute-start(bf16[2,64,1024]{2,1,0:T(8,128)(2,1)S(1)} %get-tuple-element.173), channel_id=1, source_target_pairs={{0,6},{2,4},{4,2},{6,0},{8,14},{10,12},{12,10},{14,8},{1,7},{3,5},... | collective-permute-start | bytes 786440 | tf_op jit(solution)/shard_map/ppermute | solution.py:206
  178.3 15.8 %collective-permute-start.45 = (bf16[2,64,1024]{2,1,0:T(8,128)(2,1)S(1)}, bf16[2,64,1024]{2,1,0:T(8,128)(2,1)S(1)}, u32[]{:S(2)}, u32[]{:S(2)}) collective-permute-start(bf16[2,64,1024]{2,1,0:T(8,128)(2,1)S(1)} %add_convert_fusion.1), channel_id=1, source_target_pairs={{0,8},{2,10},{4,12},{6,14},{8,0},{10,2},{12,4},{14,6},{1,9},{3,11}... | collective-permute-start | bytes 786440 | tf_op jit(solution)/shard_map/ppermute | solution.py:215
  181.4 12.6 %collective-permute-start.42 = (bf16[2,64,1024]{2,1,0:T(8,128)(2,1)S(1)}, bf16[2,64,1024]{2,1,0:T(8,128)(2,1)S(1)}, u32[]{:S(2)}, u32[]{:S(2)}) collective-permute-start(bf16[2,64,1024]{2,1,0:T(8,128)(2,1)S(1)} %get-tuple-element.171), channel_id=1, source_target_pairs={{0,2},{2,0},{4,6},{6,4},{8,10},{10,8},{12,14},{14,12},{1,3},{3,1},... | collective-permute-start | bytes 786440 | tf_op jit(solution)/shard_map/ppermute | solution.py:206
  183.0 14.7 %collective-permute-start.43 = (bf16[2,64,1024]{2,1,0:T(8,128)(2,1)S(1)}, bf16[2,64,1024]{2,1,0:T(8,128)(2,1)S(1)}, u32[]{:S(2)}, u32[]{:S(2)}) collective-permute-start(bf16[2,64,1024]{2,1,0:T(8,128)(2,1)S(1)} %get-tuple-element.170), channel_id=1, source_target_pairs={{0,4},{2,6},{4,0},{6,2},{8,12},{10,14},{12,8},{14,10},{1,5},{3,7},... | collective-permute-start | bytes 786440 | tf_op jit(solution)/shard_map/ppermute | solution.py:206
  183.0 19.2 %collective-permute-start.44 = (bf16[2,64,1024]{2,1,0:T(8,128)(2,1)S(1)}, bf16[2,64,1024]{2,1,0:T(8,128)(2,1)S(1)}, u32[]{:S(2)}, u32[]{:S(2)}) collective-permute-start(bf16[2,64,1024]{2,1,0:T(8,128)(2,1)S(1)} %get-tuple-element.169), channel_id=1, source_target_pairs={{0,6},{2,4},{4,2},{6,0},{8,14},{10,12},{12,10},{14,8},{1,7},{3,5},... | collective-permute-start | bytes 786440 | tf_op jit(solution)/shard_map/ppermute | solution.py:206
  202.5 17.8 %collective-permute-start.49 = (bf16[2,64,1024]{2,1,0:T(8,128)(2,1)S(1)}, bf16[2,64,1024]{2,1,0:T(8,128)(2,1)S(1)}, u32[]{:S(2)}, u32[]{:S(2)}) collective-permute-start(bf16[2,64,1024]{2,1,0:T(8,128)(2,1)S(1)} %add_convert_fusion), channel_id=1, source_target_pairs={{0,8},{2,10},{4,12},{6,14},{8,0},{10,2},{12,4},{14,6},{1,9},{3,11}... | collective-permute-start | bytes 786440 | tf_op jit(solution)/shard_map/ppermute | solution.py:215
  204.1 13.3 %collective-permute-start.47 = (bf16[64,1536]{1,0:T(8,128)(2,1)S(1)}, bf16[64,1536]{1,0:T(8,128)(2,1)S(1)}, u32[]{:S(2)}, u32[]{:S(2)}) collective-permute-start(bf16[64,1536]{1,0:T(8,128)(2,1)S(1)} %pad_maximum_fusion.16), channel_id=1, source_target_pairs={{0,4},{2,6},{4,0},{6,2},{8,12},{10,14},{12,8},{14,10},{1,5},{3,7},... | collective-permute-start | bytes 589832 | tf_op jit(solution)/shard_map/ppermute | solution.py:206
  206.2 14.1 %collective-permute-start.48 = (bf16[64,1536]{1,0:T(8,128)(2,1)S(1)}, bf16[64,1536]{1,0:T(8,128)(2,1)S(1)}, u32[]{:S(2)}, u32[]{:S(2)}) collective-permute-start(bf16[64,1536]{1,0:T(8,128)(2,1)S(1)} %pad_maximum_fusion.16), channel_id=1, source_target_pairs={{0,6},{2,4},{4,2},{6,0},{8,14},{10,12},{12,10},{14,8},{1,7},{3,5},... | collective-permute-start | bytes 589832 | tf_op jit(solution)/shard_map/ppermute | solution.py:206
  220.5 15.0 %collective-permute-start.50 = (bf16[4,64,1536]{2,1,0:T(8,128)(2,1)S(1)}, bf16[4,64,1536]{2,1,0:T(8,128)(2,1)S(1)}, u32[]{:S(2)}, u32[]{:S(2)}) collective-permute-start(bf16[4,64,1536]{2,1,0:T(8,128)(2,1)S(1)} %get-tuple-element.192), channel_id=1, source_target_pairs={{0,1},{1,0},{2,3},{3,2},{4,5},{5,4},{6,7},{7,6},{8,9},{9,8},{10,11... | collective-permute-start | bytes 2359304 | tf_op jit(solution)/shard_map/ppermute | solution.py:209
  222.0 12.3 %collective-permute-start.59 = (bf16[64,1536]{1,0:T(8,128)(2,1)}, bf16[64,1536]{1,0:T(8,128)(2,1)}, u32[]{:S(2)}, u32[]{:S(2)}) collective-permute-start(bf16[64,1536]{1,0:T(8,128)(2,1)} %get-tuple-element.252), channel_id=1, source_target_pairs={{0,6},{2,4},{4,2},{6,0},{8,14},{10,12},{12,10},{14,8},{1,7},{3,5},... | collective-permute-start | bytes 589832 | tf_op jit(solution)/shard_map/ppermute | solution.py:206
  238.2 8.6 %collective-permute-start.54 = (bf16[128,512]{1,0:T(8,128)(2,1)S(1)}, bf16[128,512]{1,0:T(8,128)(2,1)S(1)}, u32[]{:S(2)}, u32[]{:S(2)}) collective-permute-start(bf16[128,512]{1,0:T(8,128)(2,1)S(1)} %get-tuple-element.215), channel_id=1, source_target_pairs={{0,2},{2,0},{4,6},{6,4},{8,10},{10,8},{12,14},{14,12},{1,3},{3,1},... | collective-permute-start | bytes 393224 | tf_op jit(solution)/shard_map/ppermute | solution.py:206
  239.0 10.9 %collective-permute-start.55 = (bf16[128,512]{1,0:T(8,128)(2,1)S(1)}, bf16[128,512]{1,0:T(8,128)(2,1)S(1)}, u32[]{:S(2)}, u32[]{:S(2)}) collective-permute-start(bf16[128,512]{1,0:T(8,128)(2,1)S(1)} %get-tuple-element.214), channel_id=1, source_target_pairs={{0,4},{2,6},{4,0},{6,2},{8,12},{10,14},{12,8},{14,10},{1,5},{3,7},... | collective-permute-start | bytes 393224 | tf_op jit(solution)/shard_map/ppermute | solution.py:206
  239.4 11.4 %collective-permute-start.56 = (bf16[128,512]{1,0:T(8,128)(2,1)S(1)}, bf16[128,512]{1,0:T(8,128)(2,1)S(1)}, u32[]{:S(2)}, u32[]{:S(2)}) collective-permute-start(bf16[128,512]{1,0:T(8,128)(2,1)S(1)} %get-tuple-element.213), channel_id=1, source_target_pairs={{0,6},{2,4},{4,2},{6,0},{8,14},{10,12},{12,10},{14,8},{1,7},{3,5},... | collective-permute-start | bytes 393224 | tf_op jit(solution)/shard_map/ppermute | solution.py:206
  243.7 9.8 %collective-permute-start.52 = (bf16[512,128]{1,0:T(8,128)(2,1)S(1)}, bf16[512,128]{1,0:T(8,128)(2,1)S(1)}, u32[]{:S(2)}, u32[]{:S(2)}) collective-permute-start(bf16[512,128]{1,0:T(8,128)(2,1)S(1)} %get-tuple-element.218), channel_id=1, source_target_pairs={{0,4},{2,6},{4,0},{6,2},{8,12},{10,14},{12,8},{14,10},{1,5},{3,7},... | collective-permute-start | bytes 393224 | tf_op jit(solution)/shard_map/ppermute | solution.py:206
  249.9 8.9 %collective-permute-start.64 = (bf16[512,128]{1,0:T(8,128)(2,1)S(1)}, bf16[512,128]{1,0:T(8,128)(2,1)S(1)}, u32[]{:S(2)}, u32[]{:S(2)}) collective-permute-start(bf16[512,128]{1,0:T(8,128)(2,1)S(1)} %get-tuple-element.201), channel_id=1, source_target_pairs={{0,2},{2,0},{4,6},{6,4},{8,10},{10,8},{12,14},{14,12},{1,3},{3,1},... | collective-permute-start | bytes 393224 | tf_op jit(solution)/shard_map/ppermute | solution.py:206
  250.8 9.0 %collective-permute-start.65 = (bf16[512,128]{1,0:T(8,128)(2,1)S(1)}, bf16[512,128]{1,0:T(8,128)(2,1)S(1)}, u32[]{:S(2)}, u32[]{:S(2)}) collective-permute-start(bf16[512,128]{1,0:T(8,128)(2,1)S(1)} %get-tuple-element.203), channel_id=1, source_target_pairs={{0,4},{2,6},{4,0},{6,2},{8,12},{10,14},{12,8},{14,10},{1,5},{3,7},... | collective-permute-start | bytes 393224 | tf_op jit(solution)/shard_map/ppermute | solution.py:206
  251.1 9.6 %collective-permute-start.66 = (bf16[512,128]{1,0:T(8,128)(2,1)S(1)}, bf16[512,128]{1,0:T(8,128)(2,1)S(1)}, u32[]{:S(2)}, u32[]{:S(2)}) collective-permute-start(bf16[512,128]{1,0:T(8,128)(2,1)S(1)} %get-tuple-element.202), channel_id=1, source_target_pairs={{0,6},{2,4},{4,2},{6,0},{8,14},{10,12},{12,10},{14,8},{1,7},{3,5},... | collective-permute-start | bytes 393224 | tf_op jit(solution)/shard_map/ppermute | solution.py:206
  (65 other events, 497.7 us)

commit v6 on v5

--- a/solution.py
+++ b/solution.py
@@ -279,6 +279,24 @@
     def join_quarters(parts):
         return jnp.concatenate(by_quarter(parts), axis=1)
 
+    def first_weight(v):
+        size = quarter_d // 2 if shared else quarter_d
+        first = g * size if shared else 0
+
+        def half(i):
+            starts = [(2 * i + j) * quarter_d + first for j in (0, 1)]
+            return jnp.stack([lax.dynamic_slice_in_dim(v, at, size, 0) for at in starts])
+
+        return half(q // 2), to_peer(half(1 - q // 2), 2)
+
+    def second_weight(mine, theirs):
+        both = jnp.concatenate([mine, theirs], axis=2)
+        other = lax.dynamic_index_in_dim(both, 1 - q % 2, 0, keepdims=False)
+        return lax.dynamic_index_in_dim(both, q % 2, 0, keepdims=False), to_peer(other, 1)
+
+    def join_steps(mine, theirs):
+        return join_quarters([v[:, i * shard : (i + 1) * shard] for i in (0, 1) for v in (mine, theirs)])
+
     def swap_features(v):
         return g_swap(v) if shared else v
 
@@ -295,19 +313,23 @@
         return jnp.concatenate(turn(jnp.split(add(*parts), nh, axis=1)), axis=1)
 
     def sum_tensor(part):
-        part = part.reshape(2, 4, nh, half_rows, latent)
+        part = part.reshape(2, nh, 4, half_rows, latent)
         return add(part[0], t_swap(part[1]))
+
+    def for_peer(part):
+        return lambda r: lax.dynamic_index_in_dim(part, q ^ r, 1, keepdims=False)
 
     def sum_squares(part):
         if nh == 2:
             return part, up(part)
-        total = part[nh - 1]
+        pieces = turn(list(part))
+        total = pieces[nh - 1]
         for k in range(nh - 2, -1, -1):
-            total = add(down(total), part[k])
-        return part, jnp.stack(gather_h(total))
+            total = add(down(total), pieces[k])
+        return part, jnp.stack(turn(gather_h(total)))
 
     def join_squares(part, theirs):
-        rows = [add(part[0], theirs[1]), add(part[1], theirs[0])] if nh == 2 else list(theirs)
+        rows = turn(list(add(part, theirs) if nh == 2 else theirs))
         split = [turn(jnp.split(v, nh, axis=1)) for v in rows]
         return jnp.concatenate(split[0] + [v[0] for v in split[1:]], axis=1)
 
@@ -332,11 +354,9 @@
     local_ids = own * exp_local + jnp.arange(exp_local, dtype=jnp.int32)
     hit = routes[:, :, None] == local_ids[None, None, :]
     gate_all = jnp.sum(jnp.where(hit, gates[:, :, None], 0), axis=1).astype(f32) * gate_unit
-    gate_all = gate_all.reshape(nh, 4, 2, half_rows, exp_local)
-    gate_all = jnp.stack(turn(list(gate_all)))
-    gate_all = jnp.stack(by_quarter([gate_all[:, i] for i in range(4)]))
-    gate_all = flip(gate_all, t, 2)
-    gate_columns = gate_all.transpose(2, 0, 1, 3, 4).reshape(-1, exp_local)
+    gate_all = gate_all.reshape(n_expert, 2, half_rows, exp_local)
+    gate_all = jnp.stack([gate_all[:, 0], gate_all[:, 1]])
+    gate_columns = flip(gate_all, t, 0).reshape(-1, exp_local)
 
     group_rows = n_expert * tok_rows
     forward, backward, down_grads, input_grads, gate_blocks = expert_calls(
@@ -344,53 +364,51 @@
     )
     down_rows = down_proj.reshape(exp_local * width, latent)
 
-    def rows_with(part, theirs):
-        return jnp.stack([part, theirs]).reshape(-1, latent)
-
-    down_parts = gather_h(join_quarters(square_weight(down_weight)))
-    up_block = square_weight(up_weight)
+    def gather_latent(part):
+        return lax.all_gather(part, "expert").reshape(n_expert * half_rows, latent)
+
+    def join_rows(mine, theirs):
+        return [v[i * tok_rows : (i + 1) * tok_rows] for i in (0, 1) for v in (mine, theirs)]
+
+    down_block = square_weight(down_weight)
+    token_rows = first_rows(tokens)
+    up_mine, up_theirs = first_weight(up_weight)
+    up_mine, up_theirs = second_weight(up_mine, after(up_theirs, *down_block[1:]))
+    down_parts = gather_h(join_quarters(down_block))
     theirs = [swap_features(down_parts[0])]
-    *up_block, down_parts[-1], theirs[0] = together(*up_block, down_parts[-1], theirs[0])
-    up_parts = gather_h(join_quarters(up_block))
-    token_rows = square_rows(after(tokens, down_parts[-1]))
+    token_rows, up_theirs, down_parts[-1], theirs[0] = together(
+        token_rows, up_theirs, down_parts[-1], theirs[0]
+    )
+    up_parts = gather_h(join_steps(up_mine, up_theirs))
     theirs += [swap_features(v) for v in down_parts[1:]]
-    *token_rows, theirs[-1], up_parts[-1] = together(*token_rows, theirs[-1], up_parts[-1])
-    cot_rows = first_rows(after(cotangent, token_rows[-1]))
-    token_rows = jnp.concatenate(token_rows, axis=0)
+    mine, other = second_rows(token_rows)
+    cot_rows = first_rows(after(cotangent, token_rows))
+    other, cot_rows, theirs[-1] = together(other, cot_rows, theirs[-1])
+    token_rows = jnp.concatenate(join_rows(mine, other), axis=0)
     down_parts = [all_features(v, w) for v, w in zip(down_parts, theirs)]
 
+    cot_mine, cot_theirs = second_rows(cot_rows)
     mine, other = project(token_rows, down_parts)
+    other, up_parts[-1] = together(t_swap(other), up_parts[-1])
     theirs = [swap_features(v) for v in up_parts]
-    part_x = add(mine, t_swap(other))
-    cot_rows = after(cot_rows, part_x)
+    part_x = add(mine, other)
     part_x = exchange(lambda r: part_x[r])
-    mine, other = second_rows(cot_rows)
-    *part_x, other, theirs[-1] = together(*part_x, other, theirs[-1])
-    cot_rows = [v[i * tok_rows : (i + 1) * tok_rows] for i in (0, 1) for v in (mine, other)]
-    cot_rows = jnp.concatenate(cot_rows, axis=0)
-    part_x = gather_h(own_latent(part_x))
+    *part_x, cot_theirs, theirs[-1] = together(*part_x, cot_theirs, theirs[-1])
+    part_x = gather_latent(own_latent(part_x))
+    cot_rows = jnp.concatenate(join_rows(cot_mine, cot_theirs), axis=0)
     up_parts = [all_features(v, w) for v, w in zip(up_parts, theirs)]
     mine, other = project(cot_rows, up_parts)
-    *part_x, other = together(*part_x, t_swap(other))
-    part_y = add(mine, other)
-    part_x = jnp.stack(part_x)
-    part_x = exchange(lambda r: part_x)
-    part_y = exchange(lambda r: part_y[r])
-    *part_x, part_y[1], part_y[2], part_y[3] = together(*part_x, *part_y[1:])
-    part_x = jnp.stack(part_x)
-    part_y = gather_h(own_latent(part_y))
-    *part_y, other = together(*part_y, t_swap(part_x))
-    part_y = jnp.stack(part_y)
-    latent_in = rows_with(part_x, other)
+    part_y = add(mine, t_swap(other))
+    part_y = gather_latent(own_latent(exchange(lambda r: part_y[r])))
+    other = t_swap(part_x)
+    latent_in = jnp.concatenate([part_x, other], axis=0)
     token_parts = gather_h(after(token_rows, other))
 
     hs, cp, cu, out_part = forward(
         latent_in, gate_blocks(gate_columns), gate_proj, up_proj, down_rows
     )
-    part_y = exchange(lambda r: part_y)
-    *part_y, token_parts[-1], out_part = together(*part_y, token_parts[-1], out_part)
-    part_y = jnp.stack(part_y)
-    latent_grad = rows_with(part_y, t_swap(part_y))
+    part_y, token_parts[-1], out_part = together(part_y, token_parts[-1], out_part)
+    latent_grad = jnp.concatenate([part_y, t_swap(part_y)], axis=0)
     cot_parts = gather_h(after(cot_rows, token_parts[-1]))
     out_part = sum_tensor(out_part)
     down_proj_grad = down_grads(hs, latent_grad)
@@ -398,12 +416,12 @@
     dpu, in_part = backward(
         after(latent_grad, out_part), cp, cu, gate_proj, up_proj, down_rows
     )
-    out_part = exchange(lambda r: out_part[r])
+    out_part = exchange(for_peer(out_part))
     *out_part, cot_parts[-1], in_part = together(*out_part, cot_parts[-1], in_part)
     out_part = add(*out_part)
     in_part = sum_tensor(after(in_part, out_part))
     gate_proj_grad, up_proj_grad = input_grads(latent_in, after(dpu, in_part))
-    in_part = exchange(lambda r: in_part[r])
+    in_part = exchange(for_peer(in_part))
     *in_part, out_theirs, gate_proj_grad = together(
         *in_part, sum_squares(out_part)[1], gate_proj_grad
     )

time: 267 us -> 303 us (1.13)
  between operations: 1.99 us -> 15.3 us
  local copies, waits for them, and re-layouts: 8.09 us -> 17.5 us
  waiting for transfers between devices: 125 us -> 134 us
  matrix products: 8.31 us -> 13.5 us
    all_gather x0 -> x2, waiting for transfers between devices: none -> 48.4 us  [gather_latent(): return lax.all_gather(part, 'expert').reshape(n_expert * half_rows, latent)]
    ppermute x47 -> x39, waiting for transfers between devices: 99 us -> 67 us  [to_peer(): return lax.ppermute(v, 'expert', [(e, e ^ r) for e in range(n_expert)])]
    ppermute x8 -> x6, waiting for transfers between devices: 21.4 us -> 11.5 us  [up(): lax.ppermute(v, 'expert', [(e, (e + 4) % n_expert) for e in range(n_exper...]
    unnamed x96 -> x106, local copies, waits for them, and re-layouts: 2.18 us -> 8.06 us
    dot_general x12, matrix products: 8.31 us -> 13.5 us  [dot(): return lax.dot_general(a, b, dims, preferred_element_type=f32)]
    ppermute x47 -> x39, starting transfers between devices: 53.6 us -> 48.7 us  [to_peer(): return lax.ppermute(v, 'expert', [(e, e ^ r) for e in range(n_expert)])]
    ppermute x8 -> x6, starting transfers between devices: 5.5 us -> 7.12 us  [up(): lax.ppermute(v, 'expert', [(e, (e + 4) % n_expert) for e in range(n_exper...]
  transfers between devices with their start and end apart: 67 -> 59, of which waited for: 33 -> 30; matrix products, arithmetic and copies ran while one was open for 7% -> 10% of each run, Pallas kernels for 17% -> 15%
where the time goes in v6:
time: 303 us; the launch traced here: 302 us
  waiting for transfers between devices  134 us (44%)
  starting transfers between devices  62 us (20%)
  Pallas kernels  45.6 us (15%)
  local copies, waits for them, and re-layouts  17.5 us (6%)
  between operations  15.3 us (5%)
  other arithmetic  14.4 us (5%)
  matrix products  13.5 us (4%)
    ppermute x39, waiting for transfers between devices, to_peer(): return lax.ppermute(v, 'expert', [(e, e ^ r) for e in range(n_expert)])  67 us
    ppermute x39, starting transfers between devices, to_peer(): return lax.ppermute(v, 'expert', [(e, e ^ r) for e in range(n_expert)])  48.7 us
    all_gather x2, waiting for transfers between devices, gather_latent(): return lax.all_gather(part, 'expert').reshape(n_expert * half_rows, latent)  48.4 us
    pallas_call x1, Pallas kernels, local(): forward(latent_in, gate_blocks(gate_columns), gate_proj, up_proj, down_rows)  15.8 us
    pallas_call x1, Pallas kernels, local(): backward(after(latent_grad, out_part), cp, cu, gate_proj, up_proj, down_r...  15.7 us
    dot_general x12, matrix products, dot(): return lax.dot_general(a, b, dims, preferred_element_type=f32)  13.5 us
    ppermute x6, waiting for transfers between devices, up(): lax.ppermute(v, 'expert', [(e, (e + 4) % n_expert) for e in range(n_exper...  11.5 us
    pallas_call x1, Pallas kernels, local(): gate_proj_grad, up_proj_grad = input_grads(latent_in, after(dpu, in_part))  9.04 us
  transfers between devices with their start and end apart: 59, of which 30 were waited for; matrix products, arithmetic and copies ran while one was open for 10% of the time, Pallas kernels for 15%

profile of v6, /device:TPU:0, one launch (start us, length us, event | category | flops | bytes accessed | tf_op | source)
XLA Modules:
  0.0 302.0 jit_solution(13044514154797848614)
XLA Ops:
  8.2 3.0 %collective-permute-start.2 = (bf16[256,128]{1,0:T(8,128)(2,1)S(1)}, bf16[256,128]{1,0:T(8,128)(2,1)S(1)}, u32[]{:S(2)}, u32[]{:S(2)}) collective-permute-start(bf16[256,128]{1,0:T(8,128)(2,1)S(1)} %get-tuple-element.194), channel_id=1, source_target_pairs={{0,2},{2,0},{4,6},{6,4},{8,10},{10,8},{12,14},{14,12},{1,3},{3,1},... | collective-permute-start | bytes 196616 | tf_op jit(solution)/shard_map/ppermute | solution.py:206
  13.8 2.0 collective-permute-start.1
  19.6 2.7 collective-permute-start.6
  24.5 6.2 %collective-permute-done = bf16[128,1024]{1,0:T(8,128)(2,1)S(1)} collective-permute-done((bf16[128,1024]{1,0:T(8,128)(2,1)S(1)}, bf16[128,1024]{1,0:T(8,128)(2,1)S(1)}, u32[]{:S(2)}, u32[]{:S(2)}) %collective-permute-start) | collective-permute-done | bytes 262176 | tf_op jit(solution)/shard_map/ppermute | solution.py:206
  31.5 2.1 collective-permute-start.9
  36.5 2.5 collective-permute-done.9
  41.7 1.6 convolution_convert_fusion.3
  46.6 2.8 collective-permute-start.12
  50.0 11.5 %collective-permute-done.12 = bf16[256,512]{1,0:T(8,128)(2,1)} collective-permute-done((bf16[256,512]{1,0:T(8,128)(2,1)S(1)}, bf16[256,512]{1,0:T(8,128)(2,1)}, u32[]{:S(2)}, u32[]{:S(2)}) %collective-permute-start.12) | collective-permute-done | bytes 262176 | tf_op jit(solution)/shard_map/ppermute | solution.py:215
  64.2 2.6 collective-permute-start.15
  68.9 1.6 collective-permute-done.14
  70.5 2.0 collective-permute-done.15
  76.3 1.7 convolution_convert_fusion
  78.8 1.9 collective-permute-done.19
  81.8 2.6 collective-permute-start.22
  84.6 1.9 collective-permute-done.20
  86.5 3.4 %collective-permute-done.21 = bf16[64,1024]{1,0:T(8,128)(2,1)S(1)} collective-permute-done((bf16[64,1024]{1,0:T(8,128)(2,1)S(1)}, bf16[64,1024]{1,0:T(8,128)(2,1)S(1)}, u32[]{:S(2)}, u32[]{:S(2)}) %collective-permute-start.21) | collective-permute-done | bytes 131104 | tf_op jit(solution)/shard_map/ppermute | solution.py:206
  89.9 3.4 %collective-permute-done.22 = bf16[64,1024]{1,0:T(8,128)(2,1)S(1)} collective-permute-done((bf16[64,1024]{1,0:T(8,128)(2,1)S(1)}, bf16[64,1024]{1,0:T(8,128)(2,1)S(1)}, u32[]{:S(2)}, u32[]{:S(2)}) %collective-permute-start.22) | collective-permute-done | bytes 131104 | tf_op jit(solution)/shard_map/ppermute | solution.py:206
  93.4 19.4 %all-gather.7.cloned.1.call-done = bf16[512,1024]{1,0:T(8,128)(2,1)} async-done(((bf16[64,1024]{1,0:T(8,128)(2,1)}), bf16[512,1024]{1,0:T(8,128)(2,1)}) %all-gather.7.cloned.1.call-update) | async-done | bytes 1048592 | tf_op jit(solution)/shard_map/all_gather | solution.py:368
  114.1 1.7 pad_maximum_fusion.6
  116.7 15.8 %shard_map.144 = (bf16[1024,1536]{1,0:T(8,128)(2,1)S(1)}, bf16[1024,1536]{1,0:T(8,128)(2,1)S(1)}, bf16[1024,1536]{1,0:T(8,128)(2,1)}, bf16[1024,1024]{1,0:T(8,128)(2,1)S(1)}) custom-call(bf16[1024,1024]{1,0:T(8,128)(2,1)S(1)} %constant_dynamic-update-slice_fusion.x_ref, f32[2,1024,2]{2,1,0:T(8,128)S(1)} %bitcast.111, bf16[4,1024,384]{2,1,0:T(8,128)(2,1)} %wg_ref.3, ...), custom_call_target="tpu_custom_call" | custom-call | flops 9663676416 | bytes 23068672 | tf_op jit(solution)/shard_map/pallas_call | solution.py:407
  133.9 1.7 copy-done.3
  135.6 1.7 copy-done.6
  137.3 29.1 %all-gather.5.cloned.1.call-done = bf16[512,1024]{1,0:T(8,128)(2,1)} async-done(((bf16[64,1024]{1,0:T(8,128)(2,1)}), bf16[512,1024]{1,0:T(8,128)(2,1)}) %all-gather.5.cloned.1.call-update) | async-done | bytes 1048592 | tf_op jit(solution)/shard_map/all_gather | solution.py:368
  171.8 5.0 %shard_map.145 = bf16[1536,1024]{1,0:T(8,128)(2,1)} custom-call(bf16[1024,1536]{1,0:T(8,128)(2,1)S(1)} %copy-done.4, bf16[1024,1024]{1,0:T(8,128)(2,1)S(1)} %constant_dynamic-update-slice_fusion.2.y_ref), custom_call_target="tpu_custom_call" | custom-call | flops 3221225472 | bytes 8388608 | tf_op jit(solution)/shard_map/pallas_call | solution.py:414
  176.8 1.8 fusion.1
  179.3 1.8 collective-permute-start.28
  182.2 15.7 %shard_map.146 = (bf16[1024,3072]{1,0:T(8,128)(2,1)}, bf16[1024,1024]{1,0:T(8,128)(2,1)S(1)}) custom-call(bf16[1024,1024]{1,0:T(8,128)(2,1)S(1)} %constant_dynamic-update-slice_fusion.2.y_ref, bf16[1024,1536]{1,0:T(8,128)(2,1)S(1)} %copy-done.7, bf16[1024,1536]{1,0:T(8,128)(2,1)S(1)} %copy-done.8, bf16[4,1024,384]{2,1,0:T(8,128)(2,1)S(1)} %copy-done.2, ...), custom_call_target="tpu_custom_call" | custom-call | flops 9663676416 | bytes 26214400 | tf_op jit(solution)/shard_map/pallas_call | solution.py:416
  197.9 1.7 collective-permute-done.28
  199.6 5.3 %collective-permute-done.29 = bf16[2,64,1024]{2,1,0:T(8,128)(2,1)S(1)} collective-permute-done((bf16[2,64,1024]{2,1,0:T(8,128)(2,1)S(1)}, bf16[2,64,1024]{2,1,0:T(8,128)(2,1)S(1)}, u32[]{:S(2)}, u32[]{:S(2)}) %collective-permute-start.29) | collective-permute-done | bytes 262176 | tf_op jit(solution)/shard_map/ppermute | solution.py:206
  205.6 2.6 collective-permute-done.31
  209.5 2.7 collective-permute-start.34
  212.2 9.0 %shard_map.147 = (bf16[4,1024,384]{2,1,0:T(8,128)(2,1)}, bf16[4,1024,384]{2,1,0:T(8,128)(2,1)}) custom-call(bf16[1024,1024]{1,0:T(8,128)(2,1)S(1)} %copy-done.1, bf16[1024,3072]{1,0:T(8,128)(2,1)S(1)} %copy-done.5), custom_call_target="tpu_custom_call" | custom-call | flops 6442450944 | bytes 14680064 | tf_op jit(solution)/shard_map/pallas_call | solution.py:423
  221.3 2.7 collective-permute-done.33
  224.0 5.4 %collective-permute-done.34 = bf16[2,64,1024]{2,1,0:T(8,128)(2,1)S(1)} collective-permute-done((bf16[2,64,1024]{2,1,0:T(8,128)(2,1)S(1)}, bf16[2,64,1024]{2,1,0:T(8,128)(2,1)S(1)}, u32[]{:S(2)}, u32[]{:S(2)}) %collective-permute-start.34) | collective-permute-done | bytes 262176 | tf_op jit(solution)/shard_map/ppermute | solution.py:206
  230.8 2.5 collective-permute-start.37
  234.2 1.8 collective-permute-done.36
  235.9 8.5 %collective-permute-done.37 = bf16[64,1536]{1,0:T(8,128)(2,1)S(1)} collective-permute-done((bf16[64,1536]{1,0:T(8,128)(2,1)S(1)}, bf16[64,1536]{1,0:T(8,128)(2,1)S(1)}, u32[]{:S(2)}, u32[]{:S(2)}) %collective-permute-start.37) | collective-permute-done | bytes 196640 | tf_op jit(solution)/shard_map/ppermute | solution.py:206
  244.4 3.0 collective-permute-done.38
  249.2 2.8 collective-permute-start.49
  251.9 4.0 %collective-permute-done.47 = bf16[64,1536]{1,0:T(8,128)(2,1)S(1)} collective-permute-done((bf16[64,1536]{1,0:T(8,128)(2,1)}, bf16[64,1536]{1,0:T(8,128)(2,1)S(1)}, u32[]{:S(2)}, u32[]{:S(2)}) %collective-permute-start.47) | collective-permute-done | bytes 196640 | tf_op jit(solution)/shard_map/ppermute | solution.py:206
  257.1 4.3 %collective-permute-done.49 = bf16[64,1536]{1,0:T(8,128)(2,1)} collective-permute-done((bf16[64,1536]{1,0:T(8,128)(2,1)}, bf16[64,1536]{1,0:T(8,128)(2,1)}, u32[]{:S(2)}, u32[]{:S(2)}) %collective-permute-start.49) | collective-permute-done | bytes 196640 | tf_op jit(solution)/shard_map/ppermute | solution.py:206
  263.0 1.7 fusion.11
  266.5 2.5 collective-permute-start.46
  271.5 1.6 fusion.9
  275.2 2.5 collective-permute-start.43
  280.5 2.5 collective-permute-start.56
  286.7 2.1 collective-permute-start.53
  (278 shorter events, 68.3 us)
Async XLA Ops:
  7.2 105.6 %all-gather.7.cloned.1.call-start = ((), (), s32[]{:S(2)}) async-start(), calls=%async_computation.1 | async-start | bytes 1179648 | tf_op jit(solution)/shard_map/all_gather | solution.py:368
  8.2 8.9 %collective-permute-start.2 = (bf16[256,128]{1,0:T(8,128)(2,1)S(1)}, bf16[256,128]{1,0:T(8,128)(2,1)S(1)}, u32[]{:S(2)}, u32[]{:S(2)}) collective-permute-start(bf16[256,128]{1,0:T(8,128)(2,1)S(1)} %get-tuple-element.194), channel_id=1, source_target_pairs={{0,2},{2,0},{4,6},{6,4},{8,10},{10,8},{12,14},{14,12},{1,3},{3,1},... | collective-permute-start | bytes 196616 | tf_op jit(solution)/shard_map/ppermute | solution.py:206
  13.8 9.9 %collective-permute-start.1 = (bf16[2,256,128]{2,1,0:T(8,128)(2,1)S(1)}, bf16[2,256,128]{2,1,0:T(8,128)(2,1)S(1)}, u32[]{:S(2)}, u32[]{:S(2)}) collective-permute-start(bf16[2,256,128]{2,1,0:T(8,128)(2,1)S(1)} %pad_maximum_fusion.15), channel_id=1, source_target_pairs={{0,4},{2,6},{4,0},{6,2},{8,12},{10,14},{12,8},{14,10},{1,5},{3,7},... | collective-permute-start | bytes 393224 | tf_op jit(solution)/shard_map/ppermute | solution.py:206
  16.9 13.8 %collective-permute-start = (bf16[128,1024]{1,0:T(8,128)(2,1)S(1)}, bf16[128,1024]{1,0:T(8,128)(2,1)S(1)}, u32[]{:S(2)}, u32[]{:S(2)}) collective-permute-start(bf16[128,1024]{1,0:T(8,128)(2,1)S(1)} %get-tuple-element.196), channel_id=1, source_target_pairs={{0,4},{2,6},{4,0},{6,2},{8,12},{10,14},{12,8},{14,10},{1,5},{3,7},... | collective-permute-start | bytes 786440 | tf_op jit(solution)/shard_map/ppermute | solution.py:206
  19.6 11.2 %collective-permute-start.6 = (bf16[256,512]{1,0:T(8,128)(2,1)S(1)}, bf16[256,512]{1,0:T(8,128)(2,1)}, u32[]{:S(2)}, u32[]{:S(2)}) collective-permute-start(bf16[256,512]{1,0:T(8,128)(2,1)S(1)} %pad_maximum_fusion.11), channel_id=1, source_target_pairs={{0,8},{2,10},{4,12},{6,14},{8,0},{10,2},{12,4},{14,6},{1,9},{3,11}... | collective-permute-start | bytes 786440 | tf_op jit(solution)/shard_map/ppermute | solution.py:215
  22.2 9.2 %collective-permute-start.7 = (bf16[256,512]{1,0:T(8,128)(2,1)S(1)}, bf16[256,512]{1,0:T(8,128)(2,1)S(1)}, u32[]{:S(2)}, u32[]{:S(2)}) collective-permute-start(bf16[256,512]{1,0:T(8,128)(2,1)S(1)} %pad_maximum_fusion.11), channel_id=1, source_target_pairs={{0,16},{16,0},{1,17},{17,1},{2,18},{18,2},{3,19},{19,3},{4,20},{20... | collective-permute-start | bytes 786440 | tf_op jit(solution)/shard_map/ppermute | solution.py:212
  23.8 7.0 %collective-permute-start.5 = (bf16[256,256]{1,0:T(8,128)(2,1)S(1)}, bf16[256,256]{1,0:T(8,128)(2,1)S(1)}, u32[]{:S(2)}, u32[]{:S(2)}) collective-permute-start(bf16[256,256]{1,0:T(8,128)(2,1)S(1)} %get-tuple-element.208), channel_id=1, source_target_pairs={{0,2},{2,0},{4,6},{6,4},{8,10},{10,8},{12,14},{14,12},{1,3},{3,1},... | collective-permute-start | bytes 393224 | tf_op jit(solution)/shard_map/ppermute | solution.py:206
  31.5 7.5 %collective-permute-start.9 = (bf16[128,1024]{1,0:T(8,128)(2,1)S(1)}, bf16[128,1024]{1,0:T(8,128)(2,1)S(1)}, u32[]{:S(2)}, u32[]{:S(2)}) collective-permute-start(bf16[128,1024]{1,0:T(8,128)(2,1)S(1)} %get-tuple-element.187), channel_id=1, source_target_pairs={{0,4},{2,6},{4,0},{6,2},{8,12},{10,14},{12,8},{14,10},{1,5},{3,7},... | collective-permute-start | bytes 786440 | tf_op jit(solution)/shard_map/ppermute | solution.py:206
  33.6 7.0 %collective-permute-start.8 = (bf16[256,512]{1,0:T(8,128)(2,1)S(1)}, bf16[256,512]{1,0:T(8,128)(2,1)S(1)}, u32[]{:S(2)}, u32[]{:S(2)}) collective-permute-start(bf16[256,512]{1,0:T(8,128)(2,1)S(1)} %constant_dynamic-slice_fusion.12), channel_id=1, source_target_pairs={{0,2},{2,0},{4,6},{6,4},{8,10},{10,8},{12,14},{14,12},{1,3},{3,1},... | collective-permute-start | bytes 786440 | tf_op jit(solution)/shard_map/ppermute | solution.py:206
  35.0 6.7 %collective-permute-start.10 = (bf16[256,512]{1,0:T(8,128)(2,1)}, bf16[256,512]{1,0:T(8,128)(2,1)S(1)}, u32[]{:S(2)}, u32[]{:S(2)}) collective-permute-start(bf16[256,512]{1,0:T(8,128)(2,1)} %collective-permute-done.6), channel_id=1, source_target_pairs={{0,16},{16,0},{1,17},{17,1},{2,18},{18,2},{3,19},{19,3},{4,20},{20... | collective-permute-start | bytes 786440 | tf_op jit(solution)/shard_map/ppermute | solution.py:212
  45.6 15.9 %collective-permute-start.11 = (bf16[4,64,1024]{2,1,0:T(8,128)(2,1)S(1)}, bf16[4,64,1024]{2,1,0:T(8,128)(2,1)S(1)}, u32[]{:S(2)}, u32[]{:S(2)}) collective-permute-start(bf16[4,64,1024]{2,1,0:T(8,128)(2,1)S(1)} %dynamic-slice_bitcast_fusion.1), channel_id=1, source_target_pairs={{0,1},{1,0},{2,3},{3,2},{4,5},{5,4},{6,7},{7,6},{8,9},{9,8},{10,11... | collective-permute-start | bytes 1572872 | tf_op jit(solution)/shard_map/ppermute | solution.py:209
  46.6 14.9 %collective-permute-start.12 = (bf16[256,512]{1,0:T(8,128)(2,1)S(1)}, bf16[256,512]{1,0:T(8,128)(2,1)}, u32[]{:S(2)}, u32[]{:S(2)}) collective-permute-start(bf16[256,512]{1,0:T(8,128)(2,1)S(1)} %pad_maximum_fusion.12), channel_id=1, source_target_pairs={{0,8},{2,10},{4,12},{6,14},{8,0},{10,2},{12,4},{14,6},{1,9},{3,11}... | collective-permute-start | bytes 786440 | tf_op jit(solution)/shard_map/ppermute | solution.py:215
  49.4 17.4 %collective-permute-start.16 = (bf16[256,512]{1,0:T(8,128)(2,1)S(1)}, bf16[256,512]{1,0:T(8,128)(2,1)}, u32[]{:S(2)}, u32[]{:S(2)}) collective-permute-start(bf16[256,512]{1,0:T(8,128)(2,1)S(1)} %constant_dynamic-slice_fusion.8), channel_id=1, source_target_pairs={{0,2},{2,0},{4,6},{6,4},{8,10},{10,8},{12,14},{14,12},{1,3},{3,1},... | collective-permute-start | bytes 786440 | tf_op jit(solution)/shard_map/ppermute | solution.py:206
  61.5 11.0 %collective-permute-start.17 = (bf16[256,512]{1,0:T(8,128)(2,1)}, bf16[256,512]{1,0:T(8,128)(2,1)}, u32[]{:S(2)}, u32[]{:S(2)}) collective-permute-start(bf16[256,512]{1,0:T(8,128)(2,1)} %collective-permute-done.12), channel_id=1, source_target_pairs={{0,16},{16,0},{1,17},{17,1},{2,18},{18,2},{3,19},{19,3},{4,20},{20... | collective-permute-start | bytes 786440 | tf_op jit(solution)/shard_map/ppermute | solution.py:212
  64.2 8.3 %collective-permute-start.15 = (bf16[64,1024]{1,0:T(8,128)(2,1)S(1)}, bf16[64,1024]{1,0:T(8,128)(2,1)S(1)}, u32[]{:S(2)}, u32[]{:S(2)}) collective-permute-start(bf16[64,1024]{1,0:T(8,128)(2,1)S(1)} %get-tuple-element.180), channel_id=1, source_target_pairs={{0,6},{2,4},{4,2},{6,0},{8,14},{10,12},{12,10},{14,8},{1,7},{3,5},... | collective-permute-start | bytes 393224 | tf_op jit(solution)/shard_map/ppermute | solution.py:206
  66.9 8.7 %collective-permute-start.18 = (bf16[256,512]{1,0:T(8,128)(2,1)S(1)}, bf16[256,512]{1,0:T(8,128)(2,1)S(1)}, u32[]{:S(2)}, u32[]{:S(2)}) collective-permute-start(bf16[256,512]{1,0:T(8,128)(2,1)S(1)} %pad_maximum_fusion.12), channel_id=1, source_target_pairs={{0,16},{16,0},{1,17},{17,1},{2,18},{18,2},{3,19},{19,3},{4,20},{20... | collective-permute-start | bytes 786440 | tf_op jit(solution)/shard_map/ppermute | solution.py:212
  73.3 93.0 %all-gather.5.cloned.1.call-start = ((), (), s32[]{:S(2)}) async-start(), calls=%async_computation | async-start | bytes 1179648 | tf_op jit(solution)/shard_map/all_gather | solution.py:368
  81.8 8.1 %collective-permute-start.21 = (bf16[64,1024]{1,0:T(8,128)(2,1)S(1)}, bf16[64,1024]{1,0:T(8,128)(2,1)S(1)}, u32[]{:S(2)}, u32[]{:S(2)}) collective-permute-start(bf16[64,1024]{1,0:T(8,128)(2,1)S(1)} %get-tuple-element.177), channel_id=1, source_target_pairs={{0,4},{2,6},{4,0},{6,2},{8,12},{10,14},{12,8},{14,10},{1,5},{3,7},... | collective-permute-start | bytes 393224 | tf_op jit(solution)/shard_map/ppermute | solution.py:206
  81.8 11.5 %collective-permute-start.22 = (bf16[64,1024]{1,0:T(8,128)(2,1)S(1)}, bf16[64,1024]{1,0:T(8,128)(2,1)S(1)}, u32[]{:S(2)}, u32[]{:S(2)}) collective-permute-start(bf16[64,1024]{1,0:T(8,128)(2,1)S(1)} %get-tuple-element.176), channel_id=1, source_target_pairs={{0,6},{2,4},{4,2},{6,0},{8,14},{10,12},{12,10},{14,8},{1,7},{3,5},... | collective-permute-start | bytes 393224 | tf_op jit(solution)/shard_map/ppermute | solution.py:206
  115.9 50.4 %collective-permute-start.24 = (bf16[512,512]{1,0:T(8,128)(2,1)}, bf16[512,512]{1,0:T(8,128)(2,1)}, u32[]{:S(2)}, u32[]{:S(2)}) collective-permute-start(bf16[512,512]{1,0:T(8,128)(2,1)} %pad_maximum_fusion.6), channel_id=1, source_target_pairs={{0,8},{2,10},{4,12},{6,14},{8,0},{10,2},{12,4},{14,6},{1,9},{3,11}... | collective-permute-start | bytes 1572872 | tf_op jit(solution)/shard_map/ppermute | solution.py:215
  167.6 9.2 %collective-permute-start.25 = (bf16[2,4,64,1024]{3,2,0,1:T(8,128)(2,1)}, bf16[2,4,64,1024]{3,2,0,1:T(8,128)(2,1)}, u32[]{:S(2)}, u32[]{:S(2)}) collective-permute-start(bf16[2,4,64,1024]{3,2,0,1:T(8,128)(2,1)} %copy.48), channel_id=1, source_target_pairs={{0,1},{1,0},{2,3},{3,2},{4,5},{5,4},{6,7},{7,6},{8,9},{9,8},{10,11... | collective-permute-start | bytes 3145736 | tf_op jit(solution)/shard_map/ppermute | solution.py:209
  168.2 29.7 %collective-permute-start.30 = (bf16[512,512]{1,0:T(8,128)(2,1)S(1)}, bf16[512,512]{1,0:T(8,128)(2,1)S(1)}, u32[]{:S(2)}, u32[]{:S(2)}) collective-permute-start(bf16[512,512]{1,0:T(8,128)(2,1)S(1)} %pad_maximum_fusion.7), channel_id=1, source_target_pairs={{0,8},{2,10},{4,12},{6,14},{8,0},{10,2},{12,4},{14,6},{1,9},{3,11}... | collective-permute-start | bytes 1572872 | tf_op jit(solution)/shard_map/ppermute | solution.py:215
  178.7 19.2 %collective-permute-start.27 = (bf16[2,64,1024]{2,1,0:T(8,128)(2,1)S(1)}, bf16[2,64,1024]{2,1,0:T(8,128)(2,1)S(1)}, u32[]{:S(2)}, u32[]{:S(2)}) collective-permute-start(bf16[2,64,1024]{2,1,0:T(8,128)(2,1)S(1)} %get-tuple-element.135), channel_id=1, source_target_pairs={{0,2},{2,0},{4,6},{6,4},{8,10},{10,8},{12,14},{14,12},{1,3},{3,1},... | collective-permute-start | bytes 786440 | tf_op jit(solution)/shard_map/ppermute | solution.py:206
  179.3 20.3 %collective-permute-start.28 = (bf16[2,64,1024]{2,1,0:T(8,128)(2,1)S(1)}, bf16[2,64,1024]{2,1,0:T(8,128)(2,1)S(1)}, u32[]{:S(2)}, u32[]{:S(2)}) collective-permute-start(bf16[2,64,1024]{2,1,0:T(8,128)(2,1)S(1)} %get-tuple-element.134), channel_id=1, source_target_pairs={{0,4},{2,6},{4,0},{6,2},{8,12},{10,14},{12,8},{14,10},{1,5},{3,7},... | collective-permute-start | bytes 786440 | tf_op jit(solution)/shard_map/ppermute | solution.py:206
  181.1 23.9 %collective-permute-start.29 = (bf16[2,64,1024]{2,1,0:T(8,128)(2,1)S(1)}, bf16[2,64,1024]{2,1,0:T(8,128)(2,1)S(1)}, u32[]{:S(2)}, u32[]{:S(2)}) collective-permute-start(bf16[2,64,1024]{2,1,0:T(8,128)(2,1)S(1)} %get-tuple-element.133), channel_id=1, source_target_pairs={{0,6},{2,4},{4,2},{6,0},{8,14},{10,12},{12,10},{14,8},{1,7},{3,5},... | collective-permute-start | bytes 786440 | tf_op jit(solution)/shard_map/ppermute | solution.py:206
  205.5 15.8 %collective-permute-start.35 = (bf16[2,64,1024]{2,1,0:T(8,128)(2,1)S(1)}, bf16[2,64,1024]{2,1,0:T(8,128)(2,1)S(1)}, u32[]{:S(2)}, u32[]{:S(2)}) collective-permute-start(bf16[2,64,1024]{2,1,0:T(8,128)(2,1)S(1)} %add_convert_fusion.3), channel_id=1, source_target_pairs={{0,8},{2,10},{4,12},{6,14},{8,0},{10,2},{12,4},{14,6},{1,9},{3,11}... | collective-permute-start | bytes 786440 | tf_op jit(solution)/shard_map/ppermute | solution.py:215
  208.7 12.6 %collective-permute-start.32 = (bf16[2,64,1024]{2,1,0:T(8,128)(2,1)S(1)}, bf16[2,64,1024]{2,1,0:T(8,128)(2,1)S(1)}, u32[]{:S(2)}, u32[]{:S(2)}) collective-permute-start(bf16[2,64,1024]{2,1,0:T(8,128)(2,1)S(1)} %get-tuple-element.131), channel_id=1, source_target_pairs={{0,2},{2,0},{4,6},{6,4},{8,10},{10,8},{12,14},{14,12},{1,3},{3,1},... | collective-permute-start | bytes 786440 | tf_op jit(solution)/shard_map/ppermute | solution.py:206
  209.3 14.7 %collective-permute-start.33 = (bf16[2,64,1024]{2,1,0:T(8,128)(2,1)S(1)}, bf16[2,64,1024]{2,1,0:T(8,128)(2,1)S(1)}, u32[]{:S(2)}, u32[]{:S(2)}) collective-permute-start(bf16[2,64,1024]{2,1,0:T(8,128)(2,1)S(1)} %get-tuple-element.130), channel_id=1, source_target_pairs={{0,4},{2,6},{4,0},{6,2},{8,12},{10,14},{12,8},{14,10},{1,5},{3,7},... | collective-permute-start | bytes 786440 | tf_op jit(solution)/shard_map/ppermute | solution.py:206
  209.5 19.9 %collective-permute-start.34 = (bf16[2,64,1024]{2,1,0:T(8,128)(2,1)S(1)}, bf16[2,64,1024]{2,1,0:T(8,128)(2,1)S(1)}, u32[]{:S(2)}, u32[]{:S(2)}) collective-permute-start(bf16[2,64,1024]{2,1,0:T(8,128)(2,1)S(1)} %get-tuple-element.129), channel_id=1, source_target_pairs={{0,6},{2,4},{4,2},{6,0},{8,14},{10,12},{12,10},{14,8},{1,7},{3,5},... | collective-permute-start | bytes 786440 | tf_op jit(solution)/shard_map/ppermute | solution.py:206
  229.6 17.8 %collective-permute-start.39 = (bf16[2,64,1024]{2,1,0:T(8,128)(2,1)S(1)}, bf16[2,64,1024]{2,1,0:T(8,128)(2,1)S(1)}, u32[]{:S(2)}, u32[]{:S(2)}) collective-permute-start(bf16[2,64,1024]{2,1,0:T(8,128)(2,1)S(1)} %add_convert_fusion.1), channel_id=1, source_target_pairs={{0,8},{2,10},{4,12},{6,14},{8,0},{10,2},{12,4},{14,6},{1,9},{3,11}... | collective-permute-start | bytes 786440 | tf_op jit(solution)/shard_map/ppermute | solution.py:215
  230.8 13.6 %collective-permute-start.37 = (bf16[64,1536]{1,0:T(8,128)(2,1)S(1)}, bf16[64,1536]{1,0:T(8,128)(2,1)S(1)}, u32[]{:S(2)}, u32[]{:S(2)}) collective-permute-start(bf16[64,1536]{1,0:T(8,128)(2,1)S(1)} %pad_maximum_fusion.13), channel_id=1, source_target_pairs={{0,4},{2,6},{4,0},{6,2},{8,12},{10,14},{12,8},{14,10},{1,5},{3,7},... | collective-permute-start | bytes 589832 | tf_op jit(solution)/shard_map/ppermute | solution.py:206
  233.3 14.1 %collective-permute-start.38 = (bf16[64,1536]{1,0:T(8,128)(2,1)S(1)}, bf16[64,1536]{1,0:T(8,128)(2,1)S(1)}, u32[]{:S(2)}, u32[]{:S(2)}) collective-permute-start(bf16[64,1536]{1,0:T(8,128)(2,1)S(1)} %pad_maximum_fusion.13), channel_id=1, source_target_pairs={{0,6},{2,4},{4,2},{6,0},{8,14},{10,12},{12,10},{14,8},{1,7},{3,5},... | collective-permute-start | bytes 589832 | tf_op jit(solution)/shard_map/ppermute | solution.py:206
  247.7 15.0 %collective-permute-start.40 = (bf16[4,64,1536]{2,1,0:T(8,128)(2,1)S(1)}, bf16[4,64,1536]{2,1,0:T(8,128)(2,1)S(1)}, u32[]{:S(2)}, u32[]{:S(2)}) collective-permute-start(bf16[4,64,1536]{2,1,0:T(8,128)(2,1)S(1)} %get-tuple-element.148), channel_id=1, source_target_pairs={{0,1},{1,0},{2,3},{3,2},{4,5},{5,4},{6,7},{7,6},{8,9},{9,8},{10,11... | collective-permute-start | bytes 2359304 | tf_op jit(solution)/shard_map/ppermute | solution.py:209
  248.5 7.5 %collective-permute-start.47 = (bf16[64,1536]{1,0:T(8,128)(2,1)}, bf16[64,1536]{1,0:T(8,128)(2,1)S(1)}, u32[]{:S(2)}, u32[]{:S(2)}) collective-permute-start(bf16[64,1536]{1,0:T(8,128)(2,1)} %get-tuple-element.212), channel_id=1, source_target_pairs={{0,2},{2,0},{4,6},{6,4},{8,10},{10,8},{12,14},{14,12},{1,3},{3,1},... | collective-permute-start | bytes 589832 | tf_op jit(solution)/shard_map/ppermute | solution.py:206
  249.2 7.9 %collective-permute-start.48 = (bf16[64,1536]{1,0:T(8,128)(2,1)}, bf16[64,1536]{1,0:T(8,128)(2,1)S(1)}, u32[]{:S(2)}, u32[]{:S(2)}) collective-permute-start(bf16[64,1536]{1,0:T(8,128)(2,1)} %get-tuple-element.212), channel_id=1, source_target_pairs={{0,4},{2,6},{4,0},{6,2},{8,12},{10,14},{12,8},{14,10},{1,5},{3,7},... | collective-permute-start | bytes 589832 | tf_op jit(solution)/shard_map/ppermute | solution.py:206
  249.2 12.3 %collective-permute-start.49 = (bf16[64,1536]{1,0:T(8,128)(2,1)}, bf16[64,1536]{1,0:T(8,128)(2,1)}, u32[]{:S(2)}, u32[]{:S(2)}) collective-permute-start(bf16[64,1536]{1,0:T(8,128)(2,1)} %get-tuple-element.212), channel_id=1, source_target_pairs={{0,6},{2,4},{4,2},{6,0},{8,14},{10,12},{12,10},{14,8},{1,7},{3,5},... | collective-permute-start | bytes 589832 | tf_op jit(solution)/shard_map/ppermute | solution.py:206
  262.5 8.3 %collective-permute-start.50 = (bf16[4,64,1536]{2,1,0:T(8,128)(2,1)S(1)}, bf16[4,64,1536]{2,1,0:T(8,128)(2,1)S(1)}, u32[]{:S(2)}, u32[]{:S(2)}) collective-permute-start(bf16[4,64,1536]{2,1,0:T(8,128)(2,1)S(1)} %get-tuple-element.146), channel_id=1, source_target_pairs={{0,1},{1,0},{2,3},{3,2},{4,5},{5,4},{6,7},{7,6},{8,9},{9,8},{10,11... | collective-permute-start | bytes 2359304 | tf_op jit(solution)/shard_map/ppermute | solution.py:209
  265.4 9.8 %collective-permute-start.44 = (bf16[128,512]{1,0:T(8,128)(2,1)S(1)}, bf16[128,512]{1,0:T(8,128)(2,1)S(1)}, u32[]{:S(2)}, u32[]{:S(2)}) collective-permute-start(bf16[128,512]{1,0:T(8,128)(2,1)S(1)} %get-tuple-element.169), channel_id=1, source_target_pairs={{0,2},{2,0},{4,6},{6,4},{8,10},{10,8},{12,14},{14,12},{1,3},{3,1},... | collective-permute-start | bytes 393224 | tf_op jit(solution)/shard_map/ppermute | solution.py:206
  266.2 13.2 %collective-permute-start.45 = (bf16[128,512]{1,0:T(8,128)(2,1)S(1)}, bf16[128,512]{1,0:T(8,128)(2,1)S(1)}, u32[]{:S(2)}, u32[]{:S(2)}) collective-permute-start(bf16[128,512]{1,0:T(8,128)(2,1)S(1)} %get-tuple-element.168), channel_id=1, source_target_pairs={{0,4},{2,6},{4,0},{6,2},{8,12},{10,14},{12,8},{14,10},{1,5},{3,7},... | collective-permute-start | bytes 393224 | tf_op jit(solution)/shard_map/ppermute | solution.py:206
  266.5 13.7 %collective-permute-start.46 = (bf16[128,512]{1,0:T(8,128)(2,1)S(1)}, bf16[128,512]{1,0:T(8,128)(2,1)S(1)}, u32[]{:S(2)}, u32[]{:S(2)}) collective-permute-start(bf16[128,512]{1,0:T(8,128)(2,1)S(1)} %get-tuple-element.167), channel_id=1, source_target_pairs={{0,6},{2,4},{4,2},{6,0},{8,14},{10,12},{12,10},{14,8},{1,7},{3,5},... | collective-permute-start | bytes 393224 | tf_op jit(solution)/shard_map/ppermute | solution.py:206
  270.0 10.4 %collective-permute-start.41 = (bf16[512,128]{1,0:T(8,128)(2,1)S(1)}, bf16[512,128]{1,0:T(8,128)(2,1)S(1)}, u32[]{:S(2)}, u32[]{:S(2)}) collective-permute-start(bf16[512,128]{1,0:T(8,128)(2,1)S(1)} %get-tuple-element.173), channel_id=1, source_target_pairs={{0,2},{2,0},{4,6},{6,4},{8,10},{10,8},{12,14},{14,12},{1,3},{3,1},... | collective-permute-start | bytes 393224 | tf_op jit(solution)/shard_map/ppermute | solution.py:206
  270.8 12.1 %collective-permute-start.42 = (bf16[512,128]{1,0:T(8,128)(2,1)S(1)}, bf16[512,128]{1,0:T(8,128)(2,1)S(1)}, u32[]{:S(2)}, u32[]{:S(2)}) collective-permute-start(bf16[512,128]{1,0:T(8,128)(2,1)S(1)} %get-tuple-element.172), channel_id=1, source_target_pairs={{0,4},{2,6},{4,0},{6,2},{8,12},{10,14},{12,8},{14,10},{1,5},{3,7},... | collective-permute-start | bytes 393224 | tf_op jit(solution)/shard_map/ppermute | solution.py:206
  275.2 7.7 %collective-permute-start.43 = (bf16[512,128]{1,0:T(8,128)(2,1)S(1)}, bf16[512,128]{1,0:T(8,128)(2,1)S(1)}, u32[]{:S(2)}, u32[]{:S(2)}) collective-permute-start(bf16[512,128]{1,0:T(8,128)(2,1)S(1)} %get-tuple-element.171), channel_id=1, source_target_pairs={{0,6},{2,4},{4,2},{6,0},{8,14},{10,12},{12,10},{14,8},{1,7},{3,5},... | collective-permute-start | bytes 393224 | tf_op jit(solution)/shard_map/ppermute | solution.py:206
  279.4 7.4 %collective-permute-start.54 = (bf16[512,128]{1,0:T(8,128)(2,1)S(1)}, bf16[512,128]{1,0:T(8,128)(2,1)S(1)}, u32[]{:S(2)}, u32[]{:S(2)}) collective-permute-start(bf16[512,128]{1,0:T(8,128)(2,1)S(1)} %get-tuple-element.157), channel_id=1, source_target_pairs={{0,2},{2,0},{4,6},{6,4},{8,10},{10,8},{12,14},{14,12},{1,3},{3,1},... | collective-permute-start | bytes 393224 | tf_op jit(solution)/shard_map/ppermute | solution.py:206
  280.1 8.7 %collective-permute-start.55 = (bf16[512,128]{1,0:T(8,128)(2,1)S(1)}, bf16[512,128]{1,0:T(8,128)(2,1)S(1)}, u32[]{:S(2)}, u32[]{:S(2)}) collective-permute-start(bf16[512,128]{1,0:T(8,128)(2,1)S(1)} %get-tuple-element.159), channel_id=1, source_target_pairs={{0,4},{2,6},{4,0},{6,2},{8,12},{10,14},{12,8},{14,10},{1,5},{3,7},... | collective-permute-start | bytes 393224 | tf_op jit(solution)/shard_map/ppermute | solution.py:206
  280.5 9.8 %collective-permute-start.56 = (bf16[512,128]{1,0:T(8,128)(2,1)S(1)}, bf16[512,128]{1,0:T(8,128)(2,1)S(1)}, u32[]{:S(2)}, u32[]{:S(2)}) collective-permute-start(bf16[512,128]{1,0:T(8,128)(2,1)S(1)} %get-tuple-element.158), channel_id=1, source_target_pairs={{0,6},{2,4},{4,2},{6,0},{8,14},{10,12},{12,10},{14,8},{1,7},{3,5},... | collective-permute-start | bytes 393224 | tf_op jit(solution)/shard_map/ppermute | solution.py:206
  283.0 9.6 %collective-permute-start.51 = (bf16[128,512]{1,0:T(8,128)(2,1)S(1)}, bf16[128,512]{1,0:T(8,128)(2,1)S(1)}, u32[]{:S(2)}, u32[]{:S(2)}) collective-permute-start(bf16[128,512]{1,0:T(8,128)(2,1)S(1)} %get-tuple-element.160), channel_id=1, source_target_pairs={{0,2},{2,0},{4,6},{6,4},{8,10},{10,8},{12,14},{14,12},{1,3},{3,1},... | collective-permute-start | bytes 393224 | tf_op jit(solution)/shard_map/ppermute | solution.py:206
  283.7 8.9 %collective-permute-start.52 = (bf16[128,512]{1,0:T(8,128)(2,1)S(1)}, bf16[128,512]{1,0:T(8,128)(2,1)S(1)}, u32[]{:S(2)}, u32[]{:S(2)}) collective-permute-start(bf16[128,512]{1,0:T(8,128)(2,1)S(1)} %get-tuple-element.162), channel_id=1, source_target_pairs={{0,4},{2,6},{4,0},{6,2},{8,12},{10,14},{12,8},{14,10},{1,5},{3,7},... | collective-permute-start | bytes 393224 | tf_op jit(solution)/shard_map/ppermute | solution.py:206
  (63 other events, 359.0 us)
Sparse Core Ops, SparseCore 0:
  73.4 39.2 all-gather.6
  115.5 50.8 all-gather.4

commit v7 on v5

--- a/solution.py
+++ b/solution.py
@@ -279,6 +279,27 @@
     def join_quarters(parts):
         return jnp.concatenate(by_quarter(parts), axis=1)
 
+    def first_weight(v):
+        pairs = v.reshape(2, 2, quarter_d, shard)
+        mine = lax.dynamic_index_in_dim(pairs, q // 2, 0, keepdims=False)
+        other = lax.dynamic_index_in_dim(pairs, 1 - q // 2, 0, keepdims=False)
+        return mine, to_peer(other, 2)
+
+    def second_weight(mine, theirs):
+        both = jnp.concatenate([mine, theirs], axis=2)
+        other = lax.dynamic_index_in_dim(both, 1 - q % 2, 0, keepdims=False)
+        return lax.dynamic_index_in_dim(both, q % 2, 0, keepdims=False), to_peer(other, 1)
+
+    def join_steps(mine, theirs):
+        return join_quarters([v[:, i * shard : (i + 1) * shard] for i in (0, 1) for v in (mine, theirs)])
+
+    def own_half(v):
+        size = quarter_d // 2
+        return lax.dynamic_slice_in_dim(v, g * size, size, 0) if shared else v
+
+    def join_rows(mine, theirs):
+        return [v[i * tok_rows : (i + 1) * tok_rows] for i in (0, 1) for v in (mine, theirs)]
+
     def swap_features(v):
         return g_swap(v) if shared else v
 
@@ -347,42 +368,46 @@
     def rows_with(part, theirs):
         return jnp.stack([part, theirs]).reshape(-1, latent)
 
-    down_parts = gather_h(join_quarters(square_weight(down_weight)))
-    up_block = square_weight(up_weight)
+    down_block = square_weight(down_weight)
+    token_rows = first_rows(tokens)
+    up_mine, up_theirs = first_weight(up_weight)
+    up_mine, up_theirs = second_weight(up_mine, after(up_theirs, *down_block[1:]))
+    down_parts = gather_h(join_quarters(down_block))
     theirs = [swap_features(down_parts[0])]
-    *up_block, down_parts[-1], theirs[0] = together(*up_block, down_parts[-1], theirs[0])
-    up_parts = gather_h(join_quarters(up_block))
-    token_rows = square_rows(after(tokens, down_parts[-1]))
+    token_rows, up_theirs, down_parts[-1], theirs[0] = together(
+        token_rows, up_theirs, down_parts[-1], theirs[0]
+    )
     theirs += [swap_features(v) for v in down_parts[1:]]
-    *token_rows, theirs[-1], up_parts[-1] = together(*token_rows, theirs[-1], up_parts[-1])
-    cot_rows = first_rows(after(cotangent, token_rows[-1]))
-    token_rows = jnp.concatenate(token_rows, axis=0)
+    mine, other = second_rows(token_rows)
+    cot_rows = first_rows(after(cotangent, token_rows))
+    other, cot_rows, theirs[-1] = together(other, cot_rows, theirs[-1])
+    token_rows = jnp.concatenate(join_rows(mine, other), axis=0)
     down_parts = [all_features(v, w) for v, w in zip(down_parts, theirs)]
 
+    up_block = join_steps(up_mine, up_theirs)
+    up_parts = gather_h(own_half(up_block))
+    cot_mine, cot_theirs = second_rows(cot_rows)
     mine, other = project(token_rows, down_parts)
-    theirs = [swap_features(v) for v in up_parts]
     part_x = add(mine, t_swap(other))
-    cot_rows = after(cot_rows, part_x)
     part_x = exchange(lambda r: part_x[r])
-    mine, other = second_rows(cot_rows)
-    *part_x, other, theirs[-1] = together(*part_x, other, theirs[-1])
-    cot_rows = [v[i * tok_rows : (i + 1) * tok_rows] for i in (0, 1) for v in (mine, other)]
-    cot_rows = jnp.concatenate(cot_rows, axis=0)
+    *part_x, cot_theirs, up_parts[-1] = together(*part_x, cot_theirs, up_parts[-1])
+    cot_rows = jnp.concatenate(join_rows(cot_mine, cot_theirs), axis=0)
     part_x = gather_h(own_latent(part_x))
-    up_parts = [all_features(v, w) for v, w in zip(up_parts, theirs)]
+    theirs = [swap_features(v) for v in up_parts[1:]]
+    *part_x, theirs[-1] = together(*part_x, theirs[-1])
+    part_x = jnp.stack(part_x)
+    up_parts = [up_block] + [all_features(v, w) for v, w in zip(up_parts[1:], theirs)]
+    part_x = exchange(lambda r: part_x)
     mine, other = project(cot_rows, up_parts)
     *part_x, other = together(*part_x, t_swap(other))
+    part_x = jnp.stack(part_x)
     part_y = add(mine, other)
-    part_x = jnp.stack(part_x)
-    part_x = exchange(lambda r: part_x)
     part_y = exchange(lambda r: part_y[r])
-    *part_x, part_y[1], part_y[2], part_y[3] = together(*part_x, *part_y[1:])
-    part_x = jnp.stack(part_x)
-    part_y = gather_h(own_latent(part_y))
     *part_y, other = together(*part_y, t_swap(part_x))
-    part_y = jnp.stack(part_y)
     latent_in = rows_with(part_x, other)
-    token_parts = gather_h(after(token_rows, other))
+    part_y = jnp.stack(gather_h(own_latent(part_y)))
+    latent_in = after(latent_in, part_y)
+    token_parts = gather_h(after(token_rows, part_y))
 
     hs, cp, cu, out_part = forward(
         latent_in, gate_blocks(gate_columns), gate_proj, up_proj, down_rows

time: 267 us -> 267 us (level)
  waiting for transfers between devices: 125 us -> 108 us
  starting transfers between devices: 64.8 us -> 70.3 us
  other arithmetic: 13.6 us -> 18 us
  local copies, waits for them, and re-layouts: 8.09 us -> 11.9 us
    ppermute x47 -> x45, waiting for transfers between devices: 99 us -> 80 us  [to_peer(): return lax.ppermute(v, 'expert', [(e, e ^ r) for e in range(n_expert)])]
    ppermute x8, starting transfers between devices: 5.5 us -> 11.6 us  [up(): lax.ppermute(v, 'expert', [(e, (e + 4) % n_expert) for e in range(n_exper...]
    ppermute x47 -> x45, starting transfers between devices: 53.6 us -> 53.1 us  [to_peer(): return lax.ppermute(v, 'expert', [(e, e ^ r) for e in range(n_expert)])]
  transfers between devices with their start and end apart: 67 -> 64, of which waited for: 33 -> 35; matrix products, arithmetic and copies ran while one was open for 7% -> 9% of each run, Pallas kernels for 17% -> 17%
where the time goes in v7:
time: 267 us; the launch traced here: 266 us
  waiting for transfers between devices  108 us (40%)
  starting transfers between devices  70.3 us (26%)
  Pallas kernels  45.5 us (17%)
  other arithmetic  18 us (7%)
  local copies, waits for them, and re-layouts  11.9 us (4%)
  matrix products  10.3 us (4%)
    ppermute x45, waiting for transfers between devices, to_peer(): return lax.ppermute(v, 'expert', [(e, e ^ r) for e in range(n_expert)])  80 us
    ppermute x45, starting transfers between devices, to_peer(): return lax.ppermute(v, 'expert', [(e, e ^ r) for e in range(n_expert)])  53.1 us
    ppermute x8, waiting for transfers between devices, up(): lax.ppermute(v, 'expert', [(e, (e + 4) % n_expert) for e in range(n_exper...  23 us
    pallas_call x1, Pallas kernels, local(): forward(latent_in, gate_blocks(gate_columns), gate_proj, up_proj, down_rows)  15.8 us
    pallas_call x1, Pallas kernels, local(): backward(after(latent_grad, out_part), cp, cu, gate_proj, up_proj, down_r...  15.4 us
    ppermute x8, starting transfers between devices, up(): lax.ppermute(v, 'expert', [(e, (e + 4) % n_expert) for e in range(n_exper...  11.6 us
    dot_general x12, matrix products, dot(): return lax.dot_general(a, b, dims, preferred_element_type=f32)  10.3 us
    pallas_call x1, Pallas kernels, local(): gate_proj_grad, up_proj_grad = input_grads(latent_in, after(dpu, in_part))  9.03 us
  transfers between devices with their start and end apart: 64, of which 35 were waited for; matrix products, arithmetic and copies ran while one was open for 9% of the time, Pallas kernels for 17%

profile of v7, /device:TPU:0, one launch (start us, length us, event | category | flops | bytes accessed | tf_op | source)
XLA Modules:
  0.0 266.4 jit_solution(8055263660055182199)
XLA Ops:
  1.6 3.0 %collective-permute-start.2 = (bf16[256,128]{1,0:T(8,128)(2,1)S(1)}, bf16[256,128]{1,0:T(8,128)(2,1)S(1)}, u32[]{:S(2)}, u32[]{:S(2)}) collective-permute-start(bf16[256,128]{1,0:T(8,128)(2,1)S(1)} %get-tuple-element.235), channel_id=1, source_target_pairs={{0,2},{2,0},{4,6},{6,4},{8,10},{10,8},{12,14},{14,12},{1,3},{3,1},... | collective-permute-start | bytes 196616 | tf_op jit(solution)/shard_map/ppermute | solution.py:206
  7.3 2.0 collective-permute-start.1
  13.0 2.7 collective-permute-start.6
  17.1 5.3 %collective-permute-done.1 = bf16[2,512,128]{2,1,0:T(8,128)(2,1)S(1)} collective-permute-done((bf16[2,512,128]{2,1,0:T(8,128)(2,1)S(1)}, bf16[2,512,128]{2,1,0:T(8,128)(2,1)S(1)}, u32[]{:S(2)}, u32[]{:S(2)}) %collective-permute-start.1) | collective-permute-done | bytes 262176 | tf_op jit(solution)/shard_map/ppermute | solution.py:206
  24.4 2.6 collective-permute-done
  27.1 1.9 collective-permute-done.5
  33.6 1.9 collective-permute-done.9
  43.6 5.6 %collective-permute-start.16 = (bf16[256,512]{1,0:T(8,128)(2,1)S(1)}, bf16[256,512]{1,0:T(8,128)(2,1)S(1)}, u32[]{:S(2)}, u32[]{:S(2)}) collective-permute-start(bf16[256,512]{1,0:T(8,128)(2,1)S(1)} %constant_dynamic-slice_fusion.7), channel_id=1, source_target_pairs={{0,8},{2,10},{4,12},{6,14},{8,0},{10,2},{12,4},{14,6},{1,9},{3,11}... | collective-permute-start | bytes 786440 | tf_op jit(solution)/shard_map/ppermute | solution.py:215
  49.6 2.0 collective-permute-start.12
  53.8 7.5 %collective-permute-done.16 = bf16[256,512]{1,0:T(8,128)(2,1)S(1)} collective-permute-done((bf16[256,512]{1,0:T(8,128)(2,1)S(1)}, bf16[256,512]{1,0:T(8,128)(2,1)S(1)}, u32[]{:S(2)}, u32[]{:S(2)}) %collective-permute-start.16) | collective-permute-done | bytes 262176 | tf_op jit(solution)/shard_map/ppermute | solution.py:215
  61.4 2.2 collective-permute-done.13
  67.1 4.9 %collective-permute-done.17 = bf16[64,1024]{1,0:T(8,128)(2,1)S(1)} collective-permute-done((bf16[64,1024]{1,0:T(8,128)(2,1)S(1)}, bf16[64,1024]{1,0:T(8,128)(2,1)S(1)}, u32[]{:S(2)}, u32[]{:S(2)}) %collective-permute-start.17) | collective-permute-done | bytes 131104 | tf_op jit(solution)/shard_map/ppermute | solution.py:215
  75.9 2.1 collective-permute-start.21
  79.5 3.5 %collective-permute-done.19 = bf16[2,64,1024]{2,1,0:T(8,128)(2,1)S(1)} collective-permute-done((bf16[2,64,1024]{2,1,0:T(8,128)(2,1)S(1)}, bf16[2,64,1024]{2,1,0:T(8,128)(2,1)S(1)}, u32[]{:S(2)}, u32[]{:S(2)}) %collective-permute-start.19) | collective-permute-done | bytes 262176 | tf_op jit(solution)/shard_map/ppermute | solution.py:206
  83.0 2.1 collective-permute-done.20
  85.1 4.8 %collective-permute-done.21 = bf16[2,64,1024]{2,1,0:T(8,128)(2,1)} collective-permute-done((bf16[2,64,1024]{2,1,0:T(8,128)(2,1)S(1)}, bf16[2,64,1024]{2,1,0:T(8,128)(2,1)}, u32[]{:S(2)}, u32[]{:S(2)}) %collective-permute-start.21) | collective-permute-done | bytes 262176 | tf_op jit(solution)/shard_map/ppermute | solution.py:206
  89.9 2.1 fusion.40
  94.8 1.8 collective-permute-start.25
  97.3 2.0 collective-permute-done.23
  99.2 2.0 collective-permute-done.24
  101.2 2.1 collective-permute-done.25
  104.4 2.3 collective-permute-start.27
  108.1 4.7 %collective-permute-done.27 = bf16[64,1024]{1,0:T(8,128)(2,1)S(1)} collective-permute-done((bf16[64,1024]{1,0:T(8,128)(2,1)S(1)}, bf16[64,1024]{1,0:T(8,128)(2,1)S(1)}, u32[]{:S(2)}, u32[]{:S(2)}) %collective-permute-start.27) | collective-permute-done | bytes 131104 | tf_op jit(solution)/shard_map/ppermute | solution.py:215
  114.2 2.2 collective-permute-start.30
  117.3 15.8 %shard_map.144 = (bf16[1024,1536]{1,0:T(8,128)(2,1)S(1)}, bf16[1024,1536]{1,0:T(8,128)(2,1)S(1)}, bf16[1024,1536]{1,0:T(8,128)(2,1)}, bf16[1024,1024]{1,0:T(8,128)(2,1)S(1)}) custom-call(bf16[1024,1024]{1,0:T(8,128)(2,1)S(1)} %bitcast.188, f32[2,1024,2]{2,1,0:T(8,128)S(1)} %bitcast.192, bf16[4,1024,384]{2,1,0:T(8,128)(2,1)} %wg_ref.3, ...), custom_call_target="tpu_custom_call" | custom-call | flops 9663676416 | bytes 23068672 | tf_op jit(solution)/shard_map/pallas_call | solution.py:412
  133.1 2.7 %collective-permute-done.30 = bf16[2,64,1024]{2,1,0:T(8,128)(2,1)S(1)} collective-permute-done((bf16[2,64,1024]{2,1,0:T(8,128)(2,1)S(1)}, bf16[2,64,1024]{2,1,0:T(8,128)(2,1)S(1)}, u32[]{:S(2)}, u32[]{:S(2)}) %collective-permute-start.30) | collective-permute-done | bytes 262176 | tf_op jit(solution)/shard_map/ppermute | solution.py:206
  135.8 5.8 %collective-permute-done.31 = bf16[512,512]{1,0:T(8,128)(2,1)S(1)} collective-permute-done((bf16[512,512]{1,0:T(8,128)(2,1)S(1)}, bf16[512,512]{1,0:T(8,128)(2,1)S(1)}, u32[]{:S(2)}, u32[]{:S(2)}) %collective-permute-start.31) | collective-permute-done | bytes 524320 | tf_op jit(solution)/shard_map/ppermute | solution.py:215
  145.6 5.3 %shard_map.145 = bf16[1536,1024]{1,0:T(8,128)(2,1)} custom-call(bf16[1024,1536]{1,0:T(8,128)(2,1)S(1)} %get-tuple-element.115.hs_ref, bf16[1024,1024]{1,0:T(8,128)(2,1)S(1)} %bitcast.190), custom_call_target="tpu_custom_call" | custom-call | flops 3221225472 | bytes 8388608 | tf_op jit(solution)/shard_map/pallas_call | solution.py:421
  152.6 2.3 collective-permute-start.36
  154.9 15.4 %shard_map.146 = (bf16[1024,3072]{1,0:T(8,128)(2,1)}, bf16[1024,1024]{1,0:T(8,128)(2,1)S(1)}) custom-call(bf16[1024,1024]{1,0:T(8,128)(2,1)S(1)} %bitcast.191, bf16[1024,1536]{1,0:T(8,128)(2,1)S(1)} %get-tuple-element.122.cp_ref, bf16[1024,1536]{1,0:T(8,128)(2,1)S(1)} %copy-done.2, bf16[4,1024,384]{2,1,0:T(8,128)(2,1)S(1)} %copy-done, ...), custom_call_target="tpu_custom_call" | custom-call | flops 9663676416 | bytes 26214400 | tf_op jit(solution)/shard_map/pallas_call | solution.py:423
  170.4 2.6 collective-permute-done.35
  173.0 4.8 %collective-permute-done.36 = bf16[2,64,1024]{2,1,0:T(8,128)(2,1)S(1)} collective-permute-done((bf16[2,64,1024]{2,1,0:T(8,128)(2,1)S(1)}, bf16[2,64,1024]{2,1,0:T(8,128)(2,1)S(1)}, u32[]{:S(2)}, u32[]{:S(2)}) %collective-permute-start.36) | collective-permute-done | bytes 262176 | tf_op jit(solution)/shard_map/ppermute | solution.py:206
  178.3 2.6 collective-permute-done.38
  182.6 2.3 collective-permute-start.41
  184.9 9.0 %shard_map.147 = (bf16[4,1024,384]{2,1,0:T(8,128)(2,1)}, bf16[4,1024,384]{2,1,0:T(8,128)(2,1)}) custom-call(bf16[1024,1024]{1,0:T(8,128)(2,1)S(1)} %bitcast.189, bf16[1024,3072]{1,0:T(8,128)(2,1)S(1)} %copy-done.1), custom_call_target="tpu_custom_call" | custom-call | flops 6442450944 | bytes 14680064 | tf_op jit(solution)/shard_map/pallas_call | solution.py:430
  194.0 3.4 %collective-permute-done.40 = bf16[2,64,1024]{2,1,0:T(8,128)(2,1)S(1)} collective-permute-done((bf16[2,64,1024]{2,1,0:T(8,128)(2,1)S(1)}, bf16[2,64,1024]{2,1,0:T(8,128)(2,1)S(1)}, u32[]{:S(2)}, u32[]{:S(2)}) %collective-permute-start.40) | collective-permute-done | bytes 262176 | tf_op jit(solution)/shard_map/ppermute | solution.py:206
  197.3 4.8 %collective-permute-done.41 = bf16[2,64,1024]{2,1,0:T(8,128)(2,1)S(1)} collective-permute-done((bf16[2,64,1024]{2,1,0:T(8,128)(2,1)S(1)}, bf16[2,64,1024]{2,1,0:T(8,128)(2,1)S(1)}, u32[]{:S(2)}, u32[]{:S(2)}) %collective-permute-start.41) | collective-permute-done | bytes 262176 | tf_op jit(solution)/shard_map/ppermute | solution.py:206
  206.0 2.7 %collective-permute-done.43 = bf16[64,1536]{1,0:T(8,128)(2,1)S(1)} collective-permute-done((bf16[64,1536]{1,0:T(8,128)(2,1)S(1)}, bf16[64,1536]{1,0:T(8,128)(2,1)S(1)}, u32[]{:S(2)}, u32[]{:S(2)}) %collective-permute-start.43) | collective-permute-done | bytes 196640 | tf_op jit(solution)/shard_map/ppermute | solution.py:206
  208.7 8.2 %collective-permute-done.44 = bf16[64,1536]{1,0:T(8,128)(2,1)S(1)} collective-permute-done((bf16[64,1536]{1,0:T(8,128)(2,1)S(1)}, bf16[64,1536]{1,0:T(8,128)(2,1)S(1)}, u32[]{:S(2)}, u32[]{:S(2)}) %collective-permute-start.44) | collective-permute-done | bytes 196640 | tf_op jit(solution)/shard_map/ppermute | solution.py:206
  217.0 2.4 collective-permute-done.45
  221.6 2.3 collective-permute-start.56
  223.9 4.0 %collective-permute-done.54 = bf16[64,1536]{1,0:T(8,128)(2,1)S(1)} collective-permute-done((bf16[64,1536]{1,0:T(8,128)(2,1)}, bf16[64,1536]{1,0:T(8,128)(2,1)S(1)}, u32[]{:S(2)}, u32[]{:S(2)}) %collective-permute-start.54) | collective-permute-done | bytes 196640 | tf_op jit(solution)/shard_map/ppermute | solution.py:206
  229.5 3.8 %collective-permute-done.56 = bf16[64,1536]{1,0:T(8,128)(2,1)S(1)} collective-permute-done((bf16[64,1536]{1,0:T(8,128)(2,1)}, bf16[64,1536]{1,0:T(8,128)(2,1)S(1)}, u32[]{:S(2)}, u32[]{:S(2)}) %collective-permute-start.56) | collective-permute-done | bytes 196640 | tf_op jit(solution)/shard_map/ppermute | solution.py:206
  238.8 2.0 collective-permute-start.53
  246.8 2.0 collective-permute-start.50
  252.2 2.0 collective-permute-start.63
  255.8 2.2 collective-permute-done.61
  259.5 2.0 collective-permute-done.63
  (280 shorter events, 80.8 us)
Async XLA Ops:
  1.6 9.2 %collective-permute-start.2 = (bf16[256,128]{1,0:T(8,128)(2,1)S(1)}, bf16[256,128]{1,0:T(8,128)(2,1)S(1)}, u32[]{:S(2)}, u32[]{:S(2)}) collective-permute-start(bf16[256,128]{1,0:T(8,128)(2,1)S(1)} %get-tuple-element.235), channel_id=1, source_target_pairs={{0,2},{2,0},{4,6},{6,4},{8,10},{10,8},{12,14},{14,12},{1,3},{3,1},... | collective-permute-start | bytes 196616 | tf_op jit(solution)/shard_map/ppermute | solution.py:206
  7.3 15.1 %collective-permute-start.1 = (bf16[2,512,128]{2,1,0:T(8,128)(2,1)S(1)}, bf16[2,512,128]{2,1,0:T(8,128)(2,1)S(1)}, u32[]{:S(2)}, u32[]{:S(2)}) collective-permute-start(bf16[2,512,128]{2,1,0:T(8,128)(2,1)S(1)} %get-tuple-element.236), channel_id=1, source_target_pairs={{0,4},{2,6},{4,0},{6,2},{8,12},{10,14},{12,8},{14,10},{1,5},{3,7},... | collective-permute-start | bytes 786440 | tf_op jit(solution)/shard_map/ppermute | solution.py:206
  10.5 16.5 %collective-permute-start = (bf16[128,1024]{1,0:T(8,128)(2,1)S(1)}, bf16[128,1024]{1,0:T(8,128)(2,1)S(1)}, u32[]{:S(2)}, u32[]{:S(2)}) collective-permute-start(bf16[128,1024]{1,0:T(8,128)(2,1)S(1)} %get-tuple-element.239), channel_id=1, source_target_pairs={{0,4},{2,6},{4,0},{6,2},{8,12},{10,14},{12,8},{14,10},{1,5},{3,7},... | collective-permute-start | bytes 786440 | tf_op jit(solution)/shard_map/ppermute | solution.py:206
  13.0 14.0 %collective-permute-start.6 = (bf16[256,512]{1,0:T(8,128)(2,1)S(1)}, bf16[256,512]{1,0:T(8,128)(2,1)}, u32[]{:S(2)}, u32[]{:S(2)}) collective-permute-start(bf16[256,512]{1,0:T(8,128)(2,1)S(1)} %pad_maximum_fusion.15), channel_id=1, source_target_pairs={{0,8},{2,10},{4,12},{6,14},{8,0},{10,2},{12,4},{14,6},{1,9},{3,11}... | collective-permute-start | bytes 786440 | tf_op jit(solution)/shard_map/ppermute | solution.py:215
  15.7 11.4 %collective-permute-start.7 = (bf16[256,512]{1,0:T(8,128)(2,1)S(1)}, bf16[256,512]{1,0:T(8,128)(2,1)}, u32[]{:S(2)}, u32[]{:S(2)}) collective-permute-start(bf16[256,512]{1,0:T(8,128)(2,1)S(1)} %pad_maximum_fusion.15), channel_id=1, source_target_pairs={{0,16},{16,0},{1,17},{17,1},{2,18},{18,2},{3,19},{19,3},{4,20},{20... | collective-permute-start | bytes 786440 | tf_op jit(solution)/shard_map/ppermute | solution.py:212
  43.6 17.7 %collective-permute-start.16 = (bf16[256,512]{1,0:T(8,128)(2,1)S(1)}, bf16[256,512]{1,0:T(8,128)(2,1)S(1)}, u32[]{:S(2)}, u32[]{:S(2)}) collective-permute-start(bf16[256,512]{1,0:T(8,128)(2,1)S(1)} %constant_dynamic-slice_fusion.7), channel_id=1, source_target_pairs={{0,8},{2,10},{4,12},{6,14},{8,0},{10,2},{12,4},{14,6},{1,9},{3,11}... | collective-permute-start | bytes 786440 | tf_op jit(solution)/shard_map/ppermute | solution.py:215
  49.2 12.1 %collective-permute-start.15 = (bf16[256,512]{1,0:T(8,128)(2,1)S(1)}, bf16[256,512]{1,0:T(8,128)(2,1)S(1)}, u32[]{:S(2)}, u32[]{:S(2)}) collective-permute-start(bf16[256,512]{1,0:T(8,128)(2,1)S(1)} %constant_dynamic-slice_fusion.9), channel_id=1, source_target_pairs={{0,2},{2,0},{4,6},{6,4},{8,10},{10,8},{12,14},{14,12},{1,3},{3,1},... | collective-permute-start | bytes 786440 | tf_op jit(solution)/shard_map/ppermute | solution.py:206
  49.6 11.7 %collective-permute-start.12 = (bf16[64,1024]{1,0:T(8,128)(2,1)S(1)}, bf16[64,1024]{1,0:T(8,128)(2,1)S(1)}, u32[]{:S(2)}, u32[]{:S(2)}) collective-permute-start(bf16[64,1024]{1,0:T(8,128)(2,1)S(1)} %get-tuple-element.227), channel_id=1, source_target_pairs={{0,2},{2,0},{4,6},{6,4},{8,10},{10,8},{12,14},{14,12},{1,3},{3,1},... | collective-permute-start | bytes 393224 | tf_op jit(solution)/shard_map/ppermute | solution.py:206
  51.6 11.9 %collective-permute-start.13 = (bf16[64,1024]{1,0:T(8,128)(2,1)S(1)}, bf16[64,1024]{1,0:T(8,128)(2,1)S(1)}, u32[]{:S(2)}, u32[]{:S(2)}) collective-permute-start(bf16[64,1024]{1,0:T(8,128)(2,1)S(1)} %get-tuple-element.226), channel_id=1, source_target_pairs={{0,4},{2,6},{4,0},{6,2},{8,12},{10,14},{12,8},{14,10},{1,5},{3,7},... | collective-permute-start | bytes 393224 | tf_op jit(solution)/shard_map/ppermute | solution.py:206
  51.7 13.2 %collective-permute-start.14 = (bf16[64,1024]{1,0:T(8,128)(2,1)S(1)}, bf16[64,1024]{1,0:T(8,128)(2,1)S(1)}, u32[]{:S(2)}, u32[]{:S(2)}) collective-permute-start(bf16[64,1024]{1,0:T(8,128)(2,1)S(1)} %get-tuple-element.225), channel_id=1, source_target_pairs={{0,6},{2,4},{4,2},{6,0},{8,14},{10,12},{12,10},{14,8},{1,7},{3,5},... | collective-permute-start | bytes 393224 | tf_op jit(solution)/shard_map/ppermute | solution.py:206
  65.0 7.7 %collective-permute-start.18 = (bf16[256,512]{1,0:T(8,128)(2,1)S(1)}, bf16[256,512]{1,0:T(8,128)(2,1)S(1)}, u32[]{:S(2)}, u32[]{:S(2)}) collective-permute-start(bf16[256,512]{1,0:T(8,128)(2,1)S(1)} %collective-permute-done.16), channel_id=1, source_target_pairs={{0,16},{16,0},{1,17},{17,1},{2,18},{18,2},{3,19},{19,3},{4,20},{20... | collective-permute-start | bytes 786440 | tf_op jit(solution)/shard_map/ppermute | solution.py:212
  74.1 15.8 %collective-permute-start.22 = (bf16[4,64,1024]{2,1,0:T(8,128)(2,1)S(1)}, bf16[4,64,1024]{2,1,0:T(8,128)(2,1)S(1)}, u32[]{:S(2)}, u32[]{:S(2)}) collective-permute-start(bf16[4,64,1024]{2,1,0:T(8,128)(2,1)S(1)} %dynamic-slice_bitcast_fusion), channel_id=1, source_target_pairs={{0,1},{1,0},{2,3},{3,2},{4,5},{5,4},{6,7},{7,6},{8,9},{9,8},{10,11... | collective-permute-start | bytes 1572872 | tf_op jit(solution)/shard_map/ppermute | solution.py:209
  74.5 8.6 %collective-permute-start.19 = (bf16[2,64,1024]{2,1,0:T(8,128)(2,1)S(1)}, bf16[2,64,1024]{2,1,0:T(8,128)(2,1)S(1)}, u32[]{:S(2)}, u32[]{:S(2)}) collective-permute-start(bf16[2,64,1024]{2,1,0:T(8,128)(2,1)S(1)} %pad_maximum_fusion.16), channel_id=1, source_target_pairs={{0,2},{2,0},{4,6},{6,4},{8,10},{10,8},{12,14},{14,12},{1,3},{3,1},... | collective-permute-start | bytes 786440 | tf_op jit(solution)/shard_map/ppermute | solution.py:206
  75.9 9.2 %collective-permute-start.20 = (bf16[2,64,1024]{2,1,0:T(8,128)(2,1)S(1)}, bf16[2,64,1024]{2,1,0:T(8,128)(2,1)S(1)}, u32[]{:S(2)}, u32[]{:S(2)}) collective-permute-start(bf16[2,64,1024]{2,1,0:T(8,128)(2,1)S(1)} %pad_maximum_fusion.16), channel_id=1, source_target_pairs={{0,4},{2,6},{4,0},{6,2},{8,12},{10,14},{12,8},{14,10},{1,5},{3,7},... | collective-permute-start | bytes 786440 | tf_op jit(solution)/shard_map/ppermute | solution.py:206
  75.9 14.0 %collective-permute-start.21 = (bf16[2,64,1024]{2,1,0:T(8,128)(2,1)S(1)}, bf16[2,64,1024]{2,1,0:T(8,128)(2,1)}, u32[]{:S(2)}, u32[]{:S(2)}) collective-permute-start(bf16[2,64,1024]{2,1,0:T(8,128)(2,1)S(1)} %pad_maximum_fusion.16), channel_id=1, source_target_pairs={{0,6},{2,4},{4,2},{6,0},{8,14},{10,12},{12,10},{14,8},{1,7},{3,5},... | collective-permute-start | bytes 786440 | tf_op jit(solution)/shard_map/ppermute | solution.py:206
  92.0 11.3 %collective-permute-start.26 = (bf16[4,2,64,1024]{3,2,1,0:T(8,128)(2,1)}, bf16[4,2,64,1024]{3,2,1,0:T(8,128)(2,1)}, u32[]{:S(2)}, u32[]{:S(2)}) collective-permute-start(bf16[4,2,64,1024]{3,2,1,0:T(8,128)(2,1)} %get-tuple-element.170), channel_id=1, source_target_pairs={{0,1},{1,0},{2,3},{3,2},{4,5},{5,4},{6,7},{7,6},{8,9},{9,8},{10,11... | collective-permute-start | bytes 3145736 | tf_op jit(solution)/shard_map/ppermute | solution.py:209
  94.8 8.5 %collective-permute-start.25 = (bf16[64,1024]{1,0:T(8,128)(2,1)}, bf16[64,1024]{1,0:T(8,128)(2,1)}, u32[]{:S(2)}, u32[]{:S(2)}) collective-permute-start(bf16[64,1024]{1,0:T(8,128)(2,1)} %get-tuple-element.213), channel_id=1, source_target_pairs={{0,6},{2,4},{4,2},{6,0},{8,14},{10,12},{12,10},{14,8},{1,7},{3,5},... | collective-permute-start | bytes 393224 | tf_op jit(solution)/shard_map/ppermute | solution.py:206
  104.4 8.4 %collective-permute-start.27 = (bf16[64,1024]{1,0:T(8,128)(2,1)S(1)}, bf16[64,1024]{1,0:T(8,128)(2,1)S(1)}, u32[]{:S(2)}, u32[]{:S(2)}) collective-permute-start(bf16[64,1024]{1,0:T(8,128)(2,1)S(1)} %get-tuple-element.251), channel_id=1, source_target_pairs={{0,8},{2,10},{4,12},{6,14},{8,0},{10,2},{12,4},{14,6},{1,9},{3,11}... | collective-permute-start | bytes 393224 | tf_op jit(solution)/shard_map/ppermute | solution.py:215
  112.9 20.2 %collective-permute-start.28 = (bf16[2,64,1024]{2,1,0:T(8,128)(2,1)S(1)}, bf16[2,64,1024]{2,1,0:T(8,128)(2,1)S(1)}, u32[]{:S(2)}, u32[]{:S(2)}) collective-permute-start(bf16[2,64,1024]{2,1,0:T(8,128)(2,1)S(1)} %pad_maximum_fusion.17), channel_id=1, source_target_pairs={{0,2},{2,0},{4,6},{6,4},{8,10},{10,8},{12,14},{14,12},{1,3},{3,1},... | collective-permute-start | bytes 786440 | tf_op jit(solution)/shard_map/ppermute | solution.py:206
  114.2 18.9 %collective-permute-start.29 = (bf16[2,64,1024]{2,1,0:T(8,128)(2,1)S(1)}, bf16[2,64,1024]{2,1,0:T(8,128)(2,1)S(1)}, u32[]{:S(2)}, u32[]{:S(2)}) collective-permute-start(bf16[2,64,1024]{2,1,0:T(8,128)(2,1)S(1)} %pad_maximum_fusion.17), channel_id=1, source_target_pairs={{0,4},{2,6},{4,0},{6,2},{8,12},{10,14},{12,8},{14,10},{1,5},{3,7},... | collective-permute-start | bytes 786440 | tf_op jit(solution)/shard_map/ppermute | solution.py:206
  114.2 21.6 %collective-permute-start.30 = (bf16[2,64,1024]{2,1,0:T(8,128)(2,1)S(1)}, bf16[2,64,1024]{2,1,0:T(8,128)(2,1)S(1)}, u32[]{:S(2)}, u32[]{:S(2)}) collective-permute-start(bf16[2,64,1024]{2,1,0:T(8,128)(2,1)S(1)} %pad_maximum_fusion.17), channel_id=1, source_target_pairs={{0,6},{2,4},{4,2},{6,0},{8,14},{10,12},{12,10},{14,8},{1,7},{3,5},... | collective-permute-start | bytes 786440 | tf_op jit(solution)/shard_map/ppermute | solution.py:206
  116.5 25.2 %collective-permute-start.31 = (bf16[512,512]{1,0:T(8,128)(2,1)S(1)}, bf16[512,512]{1,0:T(8,128)(2,1)S(1)}, u32[]{:S(2)}, u32[]{:S(2)}) collective-permute-start(bf16[512,512]{1,0:T(8,128)(2,1)S(1)} %pad_maximum_fusion.10), channel_id=1, source_target_pairs={{0,8},{2,10},{4,12},{6,14},{8,0},{10,2},{12,4},{14,6},{1,9},{3,11}... | collective-permute-start | bytes 1572872 | tf_op jit(solution)/shard_map/ppermute | solution.py:215
  142.9 7.9 %collective-permute-start.32 = (bf16[4,2,64,1024]{3,2,1,0:T(8,128)(2,1)S(1)}, bf16[4,2,64,1024]{3,2,1,0:T(8,128)(2,1)S(1)}, u32[]{:S(2)}, u32[]{:S(2)}) collective-permute-start(bf16[4,2,64,1024]{3,2,1,0:T(8,128)(2,1)S(1)} %bitcast.209), channel_id=1, source_target_pairs={{0,1},{1,0},{2,3},{3,2},{4,5},{5,4},{6,7},{7,6},{8,9},{9,8},{10,11... | collective-permute-start | bytes 3145736 | tf_op jit(solution)/shard_map/ppermute | solution.py:209
  143.7 26.6 %collective-permute-start.37 = (bf16[512,512]{1,0:T(8,128)(2,1)S(1)}, bf16[512,512]{1,0:T(8,128)(2,1)S(1)}, u32[]{:S(2)}, u32[]{:S(2)}) collective-permute-start(bf16[512,512]{1,0:T(8,128)(2,1)S(1)} %pad_maximum_fusion.12), channel_id=1, source_target_pairs={{0,8},{2,10},{4,12},{6,14},{8,0},{10,2},{12,4},{14,6},{1,9},{3,11}... | collective-permute-start | bytes 1572872 | tf_op jit(solution)/shard_map/ppermute | solution.py:215
  151.4 19.0 %collective-permute-start.34 = (bf16[2,64,1024]{2,1,0:T(8,128)(2,1)S(1)}, bf16[2,64,1024]{2,1,0:T(8,128)(2,1)S(1)}, u32[]{:S(2)}, u32[]{:S(2)}) collective-permute-start(bf16[2,64,1024]{2,1,0:T(8,128)(2,1)S(1)} %get-tuple-element.165), channel_id=1, source_target_pairs={{0,2},{2,0},{4,6},{6,4},{8,10},{10,8},{12,14},{14,12},{1,3},{3,1},... | collective-permute-start | bytes 786440 | tf_op jit(solution)/shard_map/ppermute | solution.py:206
  152.6 20.3 %collective-permute-start.35 = (bf16[2,64,1024]{2,1,0:T(8,128)(2,1)S(1)}, bf16[2,64,1024]{2,1,0:T(8,128)(2,1)S(1)}, u32[]{:S(2)}, u32[]{:S(2)}) collective-permute-start(bf16[2,64,1024]{2,1,0:T(8,128)(2,1)S(1)} %get-tuple-element.164), channel_id=1, source_target_pairs={{0,4},{2,6},{4,0},{6,2},{8,12},{10,14},{12,8},{14,10},{1,5},{3,7},... | collective-permute-start | bytes 786440 | tf_op jit(solution)/shard_map/ppermute | solution.py:206
  152.6 25.1 %collective-permute-start.36 = (bf16[2,64,1024]{2,1,0:T(8,128)(2,1)S(1)}, bf16[2,64,1024]{2,1,0:T(8,128)(2,1)S(1)}, u32[]{:S(2)}, u32[]{:S(2)}) collective-permute-start(bf16[2,64,1024]{2,1,0:T(8,128)(2,1)S(1)} %get-tuple-element.163), channel_id=1, source_target_pairs={{0,6},{2,4},{4,2},{6,0},{8,14},{10,12},{12,10},{14,8},{1,7},{3,5},... | collective-permute-start | bytes 786440 | tf_op jit(solution)/shard_map/ppermute | solution.py:206
  178.2 15.8 %collective-permute-start.42 = (bf16[2,64,1024]{2,1,0:T(8,128)(2,1)S(1)}, bf16[2,64,1024]{2,1,0:T(8,128)(2,1)S(1)}, u32[]{:S(2)}, u32[]{:S(2)}) collective-permute-start(bf16[2,64,1024]{2,1,0:T(8,128)(2,1)S(1)} %add_convert_fusion.1), channel_id=1, source_target_pairs={{0,8},{2,10},{4,12},{6,14},{8,0},{10,2},{12,4},{14,6},{1,9},{3,11}... | collective-permute-start | bytes 786440 | tf_op jit(solution)/shard_map/ppermute | solution.py:215
  181.4 12.6 %collective-permute-start.39 = (bf16[2,64,1024]{2,1,0:T(8,128)(2,1)S(1)}, bf16[2,64,1024]{2,1,0:T(8,128)(2,1)S(1)}, u32[]{:S(2)}, u32[]{:S(2)}) collective-permute-start(bf16[2,64,1024]{2,1,0:T(8,128)(2,1)S(1)} %get-tuple-element.161), channel_id=1, source_target_pairs={{0,2},{2,0},{4,6},{6,4},{8,10},{10,8},{12,14},{14,12},{1,3},{3,1},... | collective-permute-start | bytes 786440 | tf_op jit(solution)/shard_map/ppermute | solution.py:206
  182.6 14.7 %collective-permute-start.40 = (bf16[2,64,1024]{2,1,0:T(8,128)(2,1)S(1)}, bf16[2,64,1024]{2,1,0:T(8,128)(2,1)S(1)}, u32[]{:S(2)}, u32[]{:S(2)}) collective-permute-start(bf16[2,64,1024]{2,1,0:T(8,128)(2,1)S(1)} %get-tuple-element.160), channel_id=1, source_target_pairs={{0,4},{2,6},{4,0},{6,2},{8,12},{10,14},{12,8},{14,10},{1,5},{3,7},... | collective-permute-start | bytes 786440 | tf_op jit(solution)/shard_map/ppermute | solution.py:206
  182.6 19.5 %collective-permute-start.41 = (bf16[2,64,1024]{2,1,0:T(8,128)(2,1)S(1)}, bf16[2,64,1024]{2,1,0:T(8,128)(2,1)S(1)}, u32[]{:S(2)}, u32[]{:S(2)}) collective-permute-start(bf16[2,64,1024]{2,1,0:T(8,128)(2,1)S(1)} %get-tuple-element.159), channel_id=1, source_target_pairs={{0,6},{2,4},{4,2},{6,0},{8,14},{10,12},{12,10},{14,8},{1,7},{3,5},... | collective-permute-start | bytes 786440 | tf_op jit(solution)/shard_map/ppermute | solution.py:206
  202.4 17.0 %collective-permute-start.46 = (bf16[2,64,1024]{2,1,0:T(8,128)(2,1)S(1)}, bf16[2,64,1024]{2,1,0:T(8,128)(2,1)S(1)}, u32[]{:S(2)}, u32[]{:S(2)}) collective-permute-start(bf16[2,64,1024]{2,1,0:T(8,128)(2,1)S(1)} %add_convert_fusion), channel_id=1, source_target_pairs={{0,8},{2,10},{4,12},{6,14},{8,0},{10,2},{12,4},{14,6},{1,9},{3,11}... | collective-permute-start | bytes 786440 | tf_op jit(solution)/shard_map/ppermute | solution.py:215
  203.7 13.2 %collective-permute-start.44 = (bf16[64,1536]{1,0:T(8,128)(2,1)S(1)}, bf16[64,1536]{1,0:T(8,128)(2,1)S(1)}, u32[]{:S(2)}, u32[]{:S(2)}) collective-permute-start(bf16[64,1536]{1,0:T(8,128)(2,1)S(1)} %pad_maximum_fusion.18), channel_id=1, source_target_pairs={{0,4},{2,6},{4,0},{6,2},{8,12},{10,14},{12,8},{14,10},{1,5},{3,7},... | collective-permute-start | bytes 589832 | tf_op jit(solution)/shard_map/ppermute | solution.py:206
  205.1 14.2 %collective-permute-start.45 = (bf16[64,1536]{1,0:T(8,128)(2,1)S(1)}, bf16[64,1536]{1,0:T(8,128)(2,1)S(1)}, u32[]{:S(2)}, u32[]{:S(2)}) collective-permute-start(bf16[64,1536]{1,0:T(8,128)(2,1)S(1)} %pad_maximum_fusion.18), channel_id=1, source_target_pairs={{0,6},{2,4},{4,2},{6,0},{8,14},{10,12},{12,10},{14,8},{1,7},{3,5},... | collective-permute-start | bytes 589832 | tf_op jit(solution)/shard_map/ppermute | solution.py:206
  219.6 13.9 %collective-permute-start.47 = (bf16[4,64,1536]{2,1,0:T(8,128)(2,1)S(1)}, bf16[4,64,1536]{2,1,0:T(8,128)(2,1)}, u32[]{:S(2)}, u32[]{:S(2)}) collective-permute-start(bf16[4,64,1536]{2,1,0:T(8,128)(2,1)S(1)} %get-tuple-element.182), channel_id=1, source_target_pairs={{0,1},{1,0},{2,3},{3,2},{4,5},{5,4},{6,7},{7,6},{8,9},{9,8},{10,11... | collective-permute-start | bytes 2359304 | tf_op jit(solution)/shard_map/ppermute | solution.py:209
  220.4 7.5 %collective-permute-start.54 = (bf16[64,1536]{1,0:T(8,128)(2,1)}, bf16[64,1536]{1,0:T(8,128)(2,1)S(1)}, u32[]{:S(2)}, u32[]{:S(2)}) collective-permute-start(bf16[64,1536]{1,0:T(8,128)(2,1)} %get-tuple-element.245), channel_id=1, source_target_pairs={{0,2},{2,0},{4,6},{6,4},{8,10},{10,8},{12,14},{14,12},{1,3},{3,1},... | collective-permute-start | bytes 589832 | tf_op jit(solution)/shard_map/ppermute | solution.py:206
  221.6 7.9 %collective-permute-start.55 = (bf16[64,1536]{1,0:T(8,128)(2,1)}, bf16[64,1536]{1,0:T(8,128)(2,1)S(1)}, u32[]{:S(2)}, u32[]{:S(2)}) collective-permute-start(bf16[64,1536]{1,0:T(8,128)(2,1)} %get-tuple-element.245), channel_id=1, source_target_pairs={{0,4},{2,6},{4,0},{6,2},{8,12},{10,14},{12,8},{14,10},{1,5},{3,7},... | collective-permute-start | bytes 589832 | tf_op jit(solution)/shard_map/ppermute | solution.py:206
  221.6 11.7 %collective-permute-start.56 = (bf16[64,1536]{1,0:T(8,128)(2,1)}, bf16[64,1536]{1,0:T(8,128)(2,1)S(1)}, u32[]{:S(2)}, u32[]{:S(2)}) collective-permute-start(bf16[64,1536]{1,0:T(8,128)(2,1)} %get-tuple-element.245), channel_id=1, source_target_pairs={{0,6},{2,4},{4,2},{6,0},{8,14},{10,12},{12,10},{14,8},{1,7},{3,5},... | collective-permute-start | bytes 589832 | tf_op jit(solution)/shard_map/ppermute | solution.py:206
  233.4 9.7 %collective-permute-start.57 = (bf16[4,64,1536]{2,1,0:T(8,128)(2,1)S(1)}, bf16[4,64,1536]{2,1,0:T(8,128)(2,1)S(1)}, u32[]{:S(2)}, u32[]{:S(2)}) collective-permute-start(bf16[4,64,1536]{2,1,0:T(8,128)(2,1)S(1)} %get-tuple-element.180), channel_id=1, source_target_pairs={{0,1},{1,0},{2,3},{3,2},{4,5},{5,4},{6,7},{7,6},{8,9},{9,8},{10,11... | collective-permute-start | bytes 2359304 | tf_op jit(solution)/shard_map/ppermute | solution.py:209
  237.2 9.5 %collective-permute-start.51 = (bf16[128,512]{1,0:T(8,128)(2,1)S(1)}, bf16[128,512]{1,0:T(8,128)(2,1)S(1)}, u32[]{:S(2)}, u32[]{:S(2)}) collective-permute-start(bf16[128,512]{1,0:T(8,128)(2,1)S(1)} %get-tuple-element.205), channel_id=1, source_target_pairs={{0,2},{2,0},{4,6},{6,4},{8,10},{10,8},{12,14},{14,12},{1,3},{3,1},... | collective-permute-start | bytes 393224 | tf_op jit(solution)/shard_map/ppermute | solution.py:206
  238.5 12.2 %collective-permute-start.52 = (bf16[128,512]{1,0:T(8,128)(2,1)S(1)}, bf16[128,512]{1,0:T(8,128)(2,1)S(1)}, u32[]{:S(2)}, u32[]{:S(2)}) collective-permute-start(bf16[128,512]{1,0:T(8,128)(2,1)S(1)} %get-tuple-element.204), channel_id=1, source_target_pairs={{0,4},{2,6},{4,0},{6,2},{8,12},{10,14},{12,8},{14,10},{1,5},{3,7},... | collective-permute-start | bytes 393224 | tf_op jit(solution)/shard_map/ppermute | solution.py:206
  238.8 13.1 %collective-permute-start.53 = (bf16[128,512]{1,0:T(8,128)(2,1)S(1)}, bf16[128,512]{1,0:T(8,128)(2,1)S(1)}, u32[]{:S(2)}, u32[]{:S(2)}) collective-permute-start(bf16[128,512]{1,0:T(8,128)(2,1)S(1)} %get-tuple-element.203), channel_id=1, source_target_pairs={{0,6},{2,4},{4,2},{6,0},{8,14},{10,12},{12,10},{14,8},{1,7},{3,5},... | collective-permute-start | bytes 393224 | tf_op jit(solution)/shard_map/ppermute | solution.py:206
  241.8 10.4 %collective-permute-start.48 = (bf16[512,128]{1,0:T(8,128)(2,1)S(1)}, bf16[512,128]{1,0:T(8,128)(2,1)S(1)}, u32[]{:S(2)}, u32[]{:S(2)}) collective-permute-start(bf16[512,128]{1,0:T(8,128)(2,1)S(1)} %get-tuple-element.209), channel_id=1, source_target_pairs={{0,2},{2,0},{4,6},{6,4},{8,10},{10,8},{12,14},{14,12},{1,3},{3,1},... | collective-permute-start | bytes 393224 | tf_op jit(solution)/shard_map/ppermute | solution.py:206
  243.1 11.1 %collective-permute-start.49 = (bf16[512,128]{1,0:T(8,128)(2,1)S(1)}, bf16[512,128]{1,0:T(8,128)(2,1)S(1)}, u32[]{:S(2)}, u32[]{:S(2)}) collective-permute-start(bf16[512,128]{1,0:T(8,128)(2,1)S(1)} %get-tuple-element.208), channel_id=1, source_target_pairs={{0,4},{2,6},{4,0},{6,2},{8,12},{10,14},{12,8},{14,10},{1,5},{3,7},... | collective-permute-start | bytes 393224 | tf_op jit(solution)/shard_map/ppermute | solution.py:206
  251.9 7.6 %collective-permute-start.62 = (bf16[512,128]{1,0:T(8,128)(2,1)S(1)}, bf16[512,128]{1,0:T(8,128)(2,1)S(1)}, u32[]{:S(2)}, u32[]{:S(2)}) collective-permute-start(bf16[512,128]{1,0:T(8,128)(2,1)S(1)} %get-tuple-element.193), channel_id=1, source_target_pairs={{0,4},{2,6},{4,0},{6,2},{8,12},{10,14},{12,8},{14,10},{1,5},{3,7},... | collective-permute-start | bytes 393224 | tf_op jit(solution)/shard_map/ppermute | solution.py:206
  252.2 9.3 %collective-permute-start.63 = (bf16[512,128]{1,0:T(8,128)(2,1)S(1)}, bf16[512,128]{1,0:T(8,128)(2,1)S(1)}, u32[]{:S(2)}, u32[]{:S(2)}) collective-permute-start(bf16[512,128]{1,0:T(8,128)(2,1)S(1)} %get-tuple-element.192), channel_id=1, source_target_pairs={{0,6},{2,4},{4,2},{6,0},{8,14},{10,12},{12,10},{14,8},{1,7},{3,5},... | collective-permute-start | bytes 393224 | tf_op jit(solution)/shard_map/ppermute | solution.py:206
  254.2 9.6 %collective-permute-start.58 = (bf16[128,512]{1,0:T(8,128)(2,1)S(1)}, bf16[128,512]{1,0:T(8,128)(2,1)S(1)}, u32[]{:S(2)}, u32[]{:S(2)}) collective-permute-start(bf16[128,512]{1,0:T(8,128)(2,1)S(1)} %get-tuple-element.194), channel_id=1, source_target_pairs={{0,2},{2,0},{4,6},{6,4},{8,10},{10,8},{12,14},{14,12},{1,3},{3,1},... | collective-permute-start | bytes 393224 | tf_op jit(solution)/shard_map/ppermute | solution.py:206
  255.5 8.4 %collective-permute-start.59 = (bf16[128,512]{1,0:T(8,128)(2,1)S(1)}, bf16[128,512]{1,0:T(8,128)(2,1)S(1)}, u32[]{:S(2)}, u32[]{:S(2)}) collective-permute-start(bf16[128,512]{1,0:T(8,128)(2,1)S(1)} %get-tuple-element.196), channel_id=1, source_target_pairs={{0,4},{2,6},{4,0},{6,2},{8,12},{10,14},{12,8},{14,10},{1,5},{3,7},... | collective-permute-start | bytes 393224 | tf_op jit(solution)/shard_map/ppermute | solution.py:206
  (63 other events, 468.4 us)

commit v8 on v7

--- a/solution.py
+++ b/solution.py
@@ -87,17 +87,18 @@
         lig_ref[...] = lig_acc[...].astype(bf16)
 
 
-def down_grad_kernel(hs_ref, y_ref, dwd_ref):
-    dwd_ref[...] = dot(hs_ref[...], y_ref[...], TN).astype(bf16)
-
-
-def input_grad_kernel(x_ref, dpu_ref, dwg_ref, dwu_ref):
+def down_grad_kernel(hs_ref, hs2_ref, y_ref, y2_ref, dwd_ref):
+    total = dot(hs_ref[...], y_ref[...], TN) + dot(hs2_ref[...], y2_ref[...], TN)
+    dwd_ref[...] = total.astype(bf16)
+
+
+def input_grad_kernel(x_ref, x2_ref, dpu_ref, dpu2_ref, dwg_ref, dwu_ref):
     pair, latent, width = dwg_ref.shape
     block = 256
 
     for i in range(latent // block):
         cols = slice(i * block, (i + 1) * block)
-        grads = dot(x_ref[:, cols], dpu_ref[...], TN)
+        grads = dot(x_ref[:, cols], dpu_ref[...], TN) + dot(x2_ref[:, cols], dpu2_ref[...], TN)
         for j in range(pair):
             dwg_ref[j, cols, :] = grads[:, 2 * j * width : (2 * j + 1) * width].astype(bf16)
             dwu_ref[j, cols, :] = grads[:, (2 * j + 1) * width : (2 * j + 2) * width].astype(bf16)
@@ -162,25 +163,25 @@
     )
     down_grads = call(
         down_grad_kernel,
-        [hidden, whole],
+        [hidden, hidden, whole, whole],
         row_proj,
         shaped(count * width, latent),
         [],
-        1,
-        weight_bytes + hidden_bytes + latent_bytes,
+        2,
+        weight_bytes + 2 * hidden_bytes + 2 * latent_bytes,
     )
     input_grads = call(
         input_grad_kernel,
-        [whole, hidden2],
+        [whole, whole, hidden2, hidden2],
         [col_proj, col_proj],
         [col, col],
         [],
-        2,
-        2 * weight_bytes + 2 * hidden_bytes + latent_bytes,
+        4,
+        2 * weight_bytes + 4 * hidden_bytes + 2 * latent_bytes,
     )
 
     def gate_blocks(gate_columns):
-        return gate_columns.reshape(rows, count // pair, pair).transpose(1, 0, 2)
+        return gate_columns.reshape(2, rows, count // pair, pair).transpose(0, 2, 1, 3)
 
     return forward, backward, down_grads, input_grads, gate_blocks
 
@@ -315,10 +316,6 @@
     def own_latent(parts):
         return jnp.concatenate(turn(jnp.split(add(*parts), nh, axis=1)), axis=1)
 
-    def sum_tensor(part):
-        part = part.reshape(2, 4, nh, half_rows, latent)
-        return add(part[0], t_swap(part[1]))
-
     def sum_squares(part):
         if nh == 2:
             return part, up(part)
@@ -359,14 +356,11 @@
     gate_all = flip(gate_all, t, 2)
     gate_columns = gate_all.transpose(2, 0, 1, 3, 4).reshape(-1, exp_local)
 
-    group_rows = n_expert * tok_rows
+    side_rows = n_expert * half_rows
     forward, backward, down_grads, input_grads, gate_blocks = expert_calls(
-        group_rows, latent, exp_local, width
+        side_rows, latent, exp_local, width
     )
     down_rows = down_proj.reshape(exp_local * width, latent)
-
-    def rows_with(part, theirs):
-        return jnp.stack([part, theirs]).reshape(-1, latent)
 
     down_block = square_weight(down_weight)
     token_rows = first_rows(tokens)
@@ -380,54 +374,59 @@
     theirs += [swap_features(v) for v in down_parts[1:]]
     mine, other = second_rows(token_rows)
     cot_rows = first_rows(after(cotangent, token_rows))
-    other, cot_rows, theirs[-1] = together(other, cot_rows, theirs[-1])
+    up_block = join_steps(up_mine, up_theirs)
+    up_parts = gather_h(own_half(up_block))
+    other, cot_rows, theirs[-1], up_parts[-1] = together(
+        other, cot_rows, theirs[-1], up_parts[-1]
+    )
     token_rows = jnp.concatenate(join_rows(mine, other), axis=0)
     down_parts = [all_features(v, w) for v, w in zip(down_parts, theirs)]
 
-    up_block = join_steps(up_mine, up_theirs)
-    up_parts = gather_h(own_half(up_block))
     cot_mine, cot_theirs = second_rows(cot_rows)
+    theirs = [swap_features(v) for v in up_parts[1:]]
     mine, other = project(token_rows, down_parts)
     part_x = add(mine, t_swap(other))
     part_x = exchange(lambda r: part_x[r])
-    *part_x, cot_theirs, up_parts[-1] = together(*part_x, cot_theirs, up_parts[-1])
+    *part_x, cot_theirs, theirs[-1] = together(*part_x, cot_theirs, theirs[-1])
     cot_rows = jnp.concatenate(join_rows(cot_mine, cot_theirs), axis=0)
+    up_parts = [up_block] + [all_features(v, w) for v, w in zip(up_parts[1:], theirs)]
     part_x = gather_h(own_latent(part_x))
-    theirs = [swap_features(v) for v in up_parts[1:]]
-    *part_x, theirs[-1] = together(*part_x, theirs[-1])
-    part_x = jnp.stack(part_x)
-    up_parts = [up_block] + [all_features(v, w) for v, w in zip(up_parts[1:], theirs)]
-    part_x = exchange(lambda r: part_x)
     mine, other = project(cot_rows, up_parts)
     *part_x, other = together(*part_x, t_swap(other))
     part_x = jnp.stack(part_x)
     part_y = add(mine, other)
+    part_x = exchange(lambda r: part_x)
     part_y = exchange(lambda r: part_y[r])
-    *part_y, other = together(*part_y, t_swap(part_x))
-    latent_in = rows_with(part_x, other)
-    part_y = jnp.stack(gather_h(own_latent(part_y)))
-    latent_in = after(latent_in, part_y)
-    token_parts = gather_h(after(token_rows, part_y))
-
-    hs, cp, cu, out_part = forward(
-        latent_in, gate_blocks(gate_columns), gate_proj, up_proj, down_rows
+    *part_x, part_y[1], part_y[2], part_y[3] = together(*part_x, *part_y[1:])
+    x_own = jnp.stack(part_x).reshape(-1, latent)
+
+    gate_own, gate_other = gate_blocks(gate_columns)
+    hs, cp, cu, out_own = forward(x_own, gate_own, gate_proj, up_proj, down_rows)
+    part_y = gather_h(own_latent(part_y))
+    x_other, part_y[-1], out_own = together(t_swap(x_own), part_y[-1], out_own)
+    part_y = jnp.stack(part_y)
+    token_parts = gather_h(after(token_rows, x_own))
+    hs2, cp2, cu2, out_other = forward(
+        after(x_other, out_own), gate_other, gate_proj, up_proj, down_rows
     )
     part_y = exchange(lambda r: part_y)
-    *part_y, token_parts[-1], out_part = together(*part_y, token_parts[-1], out_part)
-    part_y = jnp.stack(part_y)
-    latent_grad = rows_with(part_y, t_swap(part_y))
-    cot_parts = gather_h(after(cot_rows, token_parts[-1]))
-    out_part = sum_tensor(out_part)
-    down_proj_grad = down_grads(hs, latent_grad)
-    out_part = after(out_part, down_proj_grad)
-    dpu, in_part = backward(
-        after(latent_grad, out_part), cp, cu, gate_proj, up_proj, down_rows
-    )
+    *part_y, token_parts[-1], out_other = together(*part_y, token_parts[-1], out_other)
+    y_own = jnp.stack(part_y).reshape(-1, latent)
+    cot_parts = gather_h(after(cot_rows, y_own))
+    dpu, in_own = backward(y_own, cp, cu, gate_proj, up_proj, down_rows)
+    y_other, out_other, in_own = together(t_swap(y_own), t_swap(out_other), in_own)
+    out_part = add(out_own, out_other).reshape(4, nh, half_rows, latent)
     out_part = exchange(lambda r: out_part[r])
-    *out_part, cot_parts[-1], in_part = together(*out_part, cot_parts[-1], in_part)
+    down_proj_grad = down_grads(hs, hs2, after(y_own, in_own), y_other)
+    dpu2, in_other = backward(
+        after(y_other, down_proj_grad), cp2, cu2, gate_proj, up_proj, down_rows
+    )
+    *out_part, cot_parts[-1], in_other = together(*out_part, cot_parts[-1], in_other)
+    in_part = add(in_own, t_swap(in_other)).reshape(4, nh, half_rows, latent)
     out_part = add(*out_part)
-    in_part = sum_tensor(after(in_part, out_part))
-    gate_proj_grad, up_proj_grad = input_grads(latent_in, after(dpu, in_part))
+    gate_proj_grad, up_proj_grad = input_grads(
+        x_own, x_other, dpu, after(dpu2, in_part)
+    )
     in_part = exchange(lambda r: in_part[r])
     *in_part, out_theirs, gate_proj_grad = together(
         *in_part, sum_squares(out_part)[1], gate_proj_grad

time: 267 us -> 286 us (1.071)
  waiting for transfers between devices: 108 us -> 130 us
  other arithmetic: 18 us -> 14.9 us
  starting transfers between devices: 70.3 us -> 67.2 us
    ppermute x45, waiting for transfers between devices: 80 us -> 95.3 us  [to_peer(): return lax.ppermute(v, 'expert', [(e, e ^ r) for e in range(n_expert)])]
    ppermute x8, waiting for transfers between devices: 23 us -> 32.3 us  [up(): lax.ppermute(v, 'expert', [(e, (e + 4) % n_expert) for e in range(n_exper...]
    another operation x6 -> x4, other arithmetic: 3.92 us -> 0.31 us  [the longest x1 0.13 us: local(): x_own = jnp.stack(part_x).reshape(-1, latent)]
    pallas_call x4 -> x6, Pallas kernels: 45.5 us -> 47.7 us  [the longest x1 9.02 us: local(): input_grads(x_own, x_other, dpu, after(dpu2, in_part))]
  transfers between devices with their start and end apart: 64 -> 64, of which waited for: 35 -> 29; matrix products, arithmetic and copies ran while one was open for 9% -> 8% of each run, Pallas kernels for 17% -> 17%
where the time goes in v8:
time: 286 us; the launch traced here: 285 us
  waiting for transfers between devices  130 us (45%)
  starting transfers between devices  67.2 us (23%)
  Pallas kernels  47.7 us (17%)
  other arithmetic  14.9 us (5%)
  local copies, waits for them, and re-layouts  11.9 us (4%)
  matrix products  11.5 us (4%)
    ppermute x45, waiting for transfers between devices, to_peer(): return lax.ppermute(v, 'expert', [(e, e ^ r) for e in range(n_expert)])  95.3 us
    ppermute x45, starting transfers between devices, to_peer(): return lax.ppermute(v, 'expert', [(e, e ^ r) for e in range(n_expert)])  53.2 us
    ppermute x8, waiting for transfers between devices, up(): lax.ppermute(v, 'expert', [(e, (e + 4) % n_expert) for e in range(n_exper...  32.3 us
    dot_general x12, matrix products, dot(): return lax.dot_general(a, b, dims, preferred_element_type=f32)  11.5 us
    ppermute x8, starting transfers between devices, up(): lax.ppermute(v, 'expert', [(e, (e + 4) % n_expert) for e in range(n_exper...  9.52 us
    pallas_call x1, Pallas kernels, local(): input_grads(x_own, x_other, dpu, after(dpu2, in_part))  9.02 us
    pallas_call x1, Pallas kernels, local(): dpu, in_own = backward(y_own, cp, cu, gate_proj, up_proj, down_rows)  8.84 us
    pallas_call x1, Pallas kernels, local(): backward(after(y_other, down_proj_grad), cp2, cu2, gate_proj, up_proj, do...  8.59 us
  transfers between devices with their start and end apart: 64, of which 29 were waited for; matrix products, arithmetic and copies ran while one was open for 8% of the time, Pallas kernels for 17%

profile of v8, /device:TPU:0, one launch (start us, length us, event | category | flops | bytes accessed | tf_op | source)
XLA Modules:
  0.0 285.2 jit_solution(12430240452980037383)
XLA Ops:
  1.8 3.1 %collective-permute-start = (bf16[128,1024]{1,0:T(8,128)(2,1)S(1)}, bf16[128,1024]{1,0:T(8,128)(2,1)S(1)}, u32[]{:S(2)}, u32[]{:S(2)}) collective-permute-start(bf16[128,1024]{1,0:T(8,128)(2,1)S(1)} %get-tuple-element.248), channel_id=1, source_target_pairs={{0,4},{2,6},{4,0},{6,2},{8,12},{10,14},{12,8},{14,10},{1,5},{3,7},... | collective-permute-start | bytes 786440 | tf_op jit(solution)/shard_map/ppermute | solution.py:207
  6.2 2.0 collective-permute-start.2
  10.5 8.5 %collective-permute-done.3 = bf16[256,128]{1,0:T(8,128)(2,1)S(1)} collective-permute-done((bf16[256,128]{1,0:T(8,128)(2,1)S(1)}, bf16[256,128]{1,0:T(8,128)(2,1)S(1)}, u32[]{:S(2)}, u32[]{:S(2)}) %collective-permute-start.3) | collective-permute-done | bytes 65568 | tf_op jit(solution)/shard_map/ppermute | solution.py:207
  19.0 1.8 collective-permute-done.4
  20.9 2.7 collective-permute-start.6
  26.6 7.9 %collective-permute-done.6 = bf16[256,512]{1,0:T(8,128)(2,1)} collective-permute-done((bf16[256,512]{1,0:T(8,128)(2,1)S(1)}, bf16[256,512]{1,0:T(8,128)(2,1)}, u32[]{:S(2)}, u32[]{:S(2)}) %collective-permute-start.6) | collective-permute-done | bytes 262176 | tf_op jit(solution)/shard_map/ppermute | solution.py:216
  37.4 3.6 %collective-permute-start.11 = (bf16[256,512]{1,0:T(8,128)(2,1)S(1)}, bf16[256,512]{1,0:T(8,128)(2,1)}, u32[]{:S(2)}, u32[]{:S(2)}) collective-permute-start(bf16[256,512]{1,0:T(8,128)(2,1)S(1)} %constant_dynamic-slice_fusion.9), channel_id=1, source_target_pairs={{0,8},{2,10},{4,12},{6,14},{8,0},{10,2},{12,4},{14,6},{1,9},{3,11}... | collective-permute-start | bytes 786440 | tf_op jit(solution)/shard_map/ppermute | solution.py:216
  41.7 4.7 %collective-permute-done.9 = bf16[128,1024]{1,0:T(8,128)(2,1)S(1)} collective-permute-done((bf16[128,1024]{1,0:T(8,128)(2,1)S(1)}, bf16[128,1024]{1,0:T(8,128)(2,1)S(1)}, u32[]{:S(2)}, u32[]{:S(2)}) %collective-permute-start.9) | collective-permute-done | bytes 262176 | tf_op jit(solution)/shard_map/ppermute | solution.py:207
  46.4 6.0 %collective-permute-done.11 = bf16[256,512]{1,0:T(8,128)(2,1)} collective-permute-done((bf16[256,512]{1,0:T(8,128)(2,1)S(1)}, bf16[256,512]{1,0:T(8,128)(2,1)}, u32[]{:S(2)}, u32[]{:S(2)}) %collective-permute-start.11) | collective-permute-done | bytes 262176 | tf_op jit(solution)/shard_map/ppermute | solution.py:216
  61.8 3.0 %collective-permute-start.15 = (bf16[64,1024]{1,0:T(8,128)(2,1)S(1)}, bf16[64,1024]{1,0:T(8,128)(2,1)S(1)}, u32[]{:S(2)}, u32[]{:S(2)}) collective-permute-start(bf16[64,1024]{1,0:T(8,128)(2,1)S(1)} %get-tuple-element.228), channel_id=1, source_target_pairs={{0,6},{2,4},{4,2},{6,0},{8,14},{10,12},{12,10},{14,8},{1,7},{3,5},... | collective-permute-start | bytes 393224 | tf_op jit(solution)/shard_map/ppermute | solution.py:207
  64.9 6.3 %collective-permute-done.16 = bf16[256,512]{1,0:T(8,128)(2,1)} collective-permute-done((bf16[256,512]{1,0:T(8,128)(2,1)}, bf16[256,512]{1,0:T(8,128)(2,1)}, u32[]{:S(2)}, u32[]{:S(2)}) %collective-permute-start.16) | collective-permute-done | bytes 262176 | tf_op jit(solution)/shard_map/ppermute | solution.py:207
  71.1 2.3 collective-permute-done.13
  75.3 1.7 convolution_convert_fusion
  78.3 9.0 %collective-permute-done.18 = bf16[64,1024]{1,0:T(8,128)(2,1)S(1)} collective-permute-done((bf16[64,1024]{1,0:T(8,128)(2,1)S(1)}, bf16[64,1024]{1,0:T(8,128)(2,1)S(1)}, u32[]{:S(2)}, u32[]{:S(2)}) %collective-permute-start.18) | collective-permute-done | bytes 131104 | tf_op jit(solution)/shard_map/ppermute | solution.py:216
  91.0 3.0 %collective-permute-start.22 = (bf16[2,64,1024]{2,1,0:T(8,128)(2,1)S(1)}, bf16[2,64,1024]{2,1,0:T(8,128)(2,1)S(1)}, u32[]{:S(2)}, u32[]{:S(2)}) collective-permute-start(bf16[2,64,1024]{2,1,0:T(8,128)(2,1)S(1)} %pad_maximum_fusion.14), channel_id=1, source_target_pairs={{0,6},{2,4},{4,2},{6,0},{8,14},{10,12},{12,10},{14,8},{1,7},{3,5},... | collective-permute-start | bytes 786440 | tf_op jit(solution)/shard_map/ppermute | solution.py:207
  96.0 12.5 %collective-permute-done.24 = bf16[64,1024]{1,0:T(8,128)(2,1)S(1)} collective-permute-done((bf16[64,1024]{1,0:T(8,128)(2,1)}, bf16[64,1024]{1,0:T(8,128)(2,1)S(1)}, u32[]{:S(2)}, u32[]{:S(2)}) %collective-permute-start.24) | collective-permute-done | bytes 131104 | tf_op jit(solution)/shard_map/ppermute | solution.py:207
  108.6 2.3 collective-permute-done.25
  112.7 2.7 collective-permute-start.31
  115.4 8.1 %shard_map.144 = (bf16[512,1536]{1,0:T(8,128)(2,1)S(1)}, bf16[512,1536]{1,0:T(8,128)(2,1)S(1)}, bf16[512,1536]{1,0:T(8,128)(2,1)S(1)}, bf16[512,1024]{1,0:T(8,128)(2,1)S(1)}) custom-call(bf16[512,1024]{1,0:T(8,128)(2,1)S(1)} %bitcast.176, f32[2,512,2]{2,1,0:T(8,128)S(1)} %get-tuple-element.180.g_ref, bf16[4,1024,384]{2,1,0:T(8,128)(2,1)S(1)} %copy-done, ...), custom_call_target="tpu_custom_call" | custom-call | flops 4831838208 | bytes 16252928 | tf_op jit(solution)/shard_map/pallas_call | solution.py:404
  123.5 9.3 %collective-permute-done.27 = bf16[64,1024]{1,0:T(8,128)(2,1)S(1)} collective-permute-done((bf16[64,1024]{1,0:T(8,128)(2,1)S(1)}, bf16[64,1024]{1,0:T(8,128)(2,1)S(1)}, u32[]{:S(2)}, u32[]{:S(2)}) %collective-permute-start.27) | collective-permute-done | bytes 131104 | tf_op jit(solution)/shard_map/ppermute | solution.py:216
  133.5 3.0 %collective-permute-start.30 = (bf16[2,64,1024]{2,1,0:T(8,128)(2,1)S(1)}, bf16[2,64,1024]{2,1,0:T(8,128)(2,1)S(1)}, u32[]{:S(2)}, u32[]{:S(2)}) collective-permute-start(bf16[2,64,1024]{2,1,0:T(8,128)(2,1)S(1)} %pad_maximum_fusion.15), channel_id=1, source_target_pairs={{0,6},{2,4},{4,2},{6,0},{8,14},{10,12},{12,10},{14,8},{1,7},{3,5},... | collective-permute-start | bytes 786440 | tf_op jit(solution)/shard_map/ppermute | solution.py:207
  136.5 8.1 %shard_map.145 = (bf16[512,1536]{1,0:T(8,128)(2,1)S(1)}, bf16[512,1536]{1,0:T(8,128)(2,1)S(1)}, bf16[512,1536]{1,0:T(8,128)(2,1)S(1)}, bf16[512,1024]{1,0:T(8,128)(2,1)S(1)}) custom-call(bf16[512,1024]{1,0:T(8,128)(2,1)S(1)} %collective-permute-done.26.x_ref.x2_ref, f32[2,512,2]{2,1,0:T(8,128)S(1)} %get-tuple-element.179.g_ref, ...), custom_call_target="tpu_custom_call" | custom-call | flops 4831838208 | bytes 16252928 | tf_op jit(solution)/shard_map/pallas_call | solution.py:409
  144.7 5.1 %collective-permute-done.29 = bf16[2,64,1024]{2,1,0:T(8,128)(2,1)S(1)} collective-permute-done((bf16[2,64,1024]{2,1,0:T(8,128)(2,1)S(1)}, bf16[2,64,1024]{2,1,0:T(8,128)(2,1)S(1)}, u32[]{:S(2)}, u32[]{:S(2)}) %collective-permute-start.29) | collective-permute-done | bytes 262176 | tf_op jit(solution)/shard_map/ppermute | solution.py:207
  149.8 5.5 %collective-permute-done.30 = bf16[2,64,1024]{2,1,0:T(8,128)(2,1)S(1)} collective-permute-done((bf16[2,64,1024]{2,1,0:T(8,128)(2,1)S(1)}, bf16[2,64,1024]{2,1,0:T(8,128)(2,1)S(1)}, u32[]{:S(2)}, u32[]{:S(2)}) %collective-permute-start.30) | collective-permute-done | bytes 262176 | tf_op jit(solution)/shard_map/ppermute | solution.py:207
  156.1 8.8 %shard_map.146 = (bf16[512,3072]{1,0:T(8,128)(2,1)S(1)}, bf16[512,1024]{1,0:T(8,128)(2,1)S(1)}) custom-call(bf16[512,1024]{1,0:T(8,128)(2,1)S(1)} %bitcast.179, bf16[512,1536]{1,0:T(8,128)(2,1)S(1)} %get-tuple-element.128.cp_ref, bf16[512,1536]{1,0:T(8,128)(2,1)S(1)} %get-tuple-element.129.cu_ref, bf16[4,1024,384]{2,1,0:T(8,128)(2,1)S(1)} %copy-done, ...), custom_call_target="tpu_custom_call" | custom-call | flops 4831838208 | bytes 17825792 | tf_op jit(solution)/shard_map/pallas_call | solution.py:416
  168.3 1.8 collective-permute-start.35
  170.2 5.0 %shard_map.147 = bf16[1536,1024]{1,0:T(8,128)(2,1)} custom-call(bf16[512,1536]{1,0:T(8,128)(2,1)S(1)} %get-tuple-element.133.hs_ref, bf16[512,1536]{1,0:T(8,128)(2,1)S(1)} %get-tuple-element.134.hs2_ref, bf16[512,1024]{1,0:T(8,128)(2,1)S(1)} %bitcast.180, bf16[512,1024]{1,0:T(8,128)(2,1)S(1)} %collective-permute-done.32.y2_ref.y_ref), custom_call_target="tpu_custom_call" | custom-call | flops 3221225472 | bytes 8388608 | tf_op jit(solution)/shard_map/pallas_call | solution.py:420
  175.3 8.6 %shard_map.148 = (bf16[512,3072]{1,0:T(8,128)(2,1)S(1)}, bf16[512,1024]{1,0:T(8,128)(2,1)S(1)}) custom-call(bf16[512,1024]{1,0:T(8,128)(2,1)S(1)} %collective-permute-done.32.y2_ref.y_ref, bf16[512,1536]{1,0:T(8,128)(2,1)S(1)} %get-tuple-element.138.cp_ref, bf16[512,1536]{1,0:T(8,128)(2,1)S(1)} %get-tuple-element.139.cu_ref, ...), custom_call_target="tpu_custom_call" | custom-call | flops 4831838208 | bytes 17825792 | tf_op jit(solution)/shard_map/pallas_call | solution.py:421
  183.9 3.0 %collective-permute-done.35 = bf16[2,64,1024]{2,1,0:T(8,128)(2,1)S(1)} collective-permute-done((bf16[2,64,1024]{2,1,0:T(8,128)(2,1)S(1)}, bf16[2,64,1024]{2,1,0:T(8,128)(2,1)S(1)}, u32[]{:S(2)}, u32[]{:S(2)}) %collective-permute-start.35) | collective-permute-done | bytes 262176 | tf_op jit(solution)/shard_map/ppermute | solution.py:207
  186.9 6.1 %collective-permute-done.36 = bf16[2,64,1024]{2,1,0:T(8,128)(2,1)S(1)} collective-permute-done((bf16[2,64,1024]{2,1,0:T(8,128)(2,1)S(1)}, bf16[2,64,1024]{2,1,0:T(8,128)(2,1)S(1)}, u32[]{:S(2)}, u32[]{:S(2)}) %collective-permute-start.36) | collective-permute-done | bytes 262176 | tf_op jit(solution)/shard_map/ppermute | solution.py:207
  193.2 2.4 collective-permute-done.38
  197.4 2.3 collective-permute-start.41
  199.7 9.0 %shard_map.149 = (bf16[4,1024,384]{2,1,0:T(8,128)(2,1)}, bf16[4,1024,384]{2,1,0:T(8,128)(2,1)}) custom-call(bf16[512,1024]{1,0:T(8,128)(2,1)S(1)} %bitcast.177, bf16[512,1024]{1,0:T(8,128)(2,1)S(1)} %collective-permute-done.26.x_ref.x2_ref, bf16[512,3072]{1,0:T(8,128)(2,1)S(1)} %get-tuple-element.146.dpu_ref, bf16[512,3072]{1,0:T(8,128)(2,1)S(1)} %get-tuple-element.147.dpu2_ref), custom_call_target="tpu_custom_call" | custom-call | flops 6442450944 | bytes 14680064 | tf_op jit(solution)/shard_map/pallas_call | solution.py:427
  208.7 3.1 %collective-permute-done.40 = bf16[2,64,1024]{2,1,0:T(8,128)(2,1)S(1)} collective-permute-done((bf16[2,64,1024]{2,1,0:T(8,128)(2,1)S(1)}, bf16[2,64,1024]{2,1,0:T(8,128)(2,1)S(1)}, u32[]{:S(2)}, u32[]{:S(2)}) %collective-permute-start.40) | collective-permute-done | bytes 262176 | tf_op jit(solution)/shard_map/ppermute | solution.py:207
  211.8 5.1 %collective-permute-done.41 = bf16[2,64,1024]{2,1,0:T(8,128)(2,1)S(1)} collective-permute-done((bf16[2,64,1024]{2,1,0:T(8,128)(2,1)S(1)}, bf16[2,64,1024]{2,1,0:T(8,128)(2,1)S(1)}, u32[]{:S(2)}, u32[]{:S(2)}) %collective-permute-start.41) | collective-permute-done | bytes 262176 | tf_op jit(solution)/shard_map/ppermute | solution.py:207
  218.2 2.7 collective-permute-start.44
  221.4 2.1 collective-permute-done.43
  223.5 8.5 %collective-permute-done.44 = bf16[64,1536]{1,0:T(8,128)(2,1)S(1)} collective-permute-done((bf16[64,1536]{1,0:T(8,128)(2,1)S(1)}, bf16[64,1536]{1,0:T(8,128)(2,1)S(1)}, u32[]{:S(2)}, u32[]{:S(2)}) %collective-permute-start.44) | collective-permute-done | bytes 196640 | tf_op jit(solution)/shard_map/ppermute | solution.py:207
  232.1 2.6 collective-permute-done.45
  235.7 2.4 collective-permute-start.55
  239.2 5.4 %collective-permute-done.56 = bf16[64,1536]{1,0:T(8,128)(2,1)S(1)} collective-permute-done((bf16[64,1536]{1,0:T(8,128)(2,1)}, bf16[64,1536]{1,0:T(8,128)(2,1)S(1)}, u32[]{:S(2)}, u32[]{:S(2)}) %collective-permute-start.56) | collective-permute-done | bytes 196640 | tf_op jit(solution)/shard_map/ppermute | solution.py:207
  244.6 3.4 %collective-permute-done.55 = bf16[64,1536]{1,0:T(8,128)(2,1)} collective-permute-done((bf16[64,1536]{1,0:T(8,128)(2,1)}, bf16[64,1536]{1,0:T(8,128)(2,1)}, u32[]{:S(2)}, u32[]{:S(2)}) %collective-permute-start.55) | collective-permute-done | bytes 196640 | tf_op jit(solution)/shard_map/ppermute | solution.py:207
  254.6 2.5 collective-permute-start.50
  257.6 1.7 fusion.1
  264.8 2.6 collective-permute-start.53
  267.4 2.4 collective-permute-start.60
  273.4 2.5 collective-permute-start.63
  277.7 3.4 %collective-permute-done.58 = bf16[128,512]{1,0:T(8,128)(2,1)S(1)} collective-permute-done((bf16[128,512]{1,0:T(8,128)(2,1)S(1)}, bf16[128,512]{1,0:T(8,128)(2,1)S(1)}, u32[]{:S(2)}, u32[]{:S(2)}) %collective-permute-start.58) | collective-permute-done | bytes 131104 | tf_op jit(solution)/shard_map/ppermute | solution.py:207
  (275 shorter events, 63.7 us)
Async XLA Ops:
  1.8 24.7 %collective-permute-start = (bf16[128,1024]{1,0:T(8,128)(2,1)S(1)}, bf16[128,1024]{1,0:T(8,128)(2,1)S(1)}, u32[]{:S(2)}, u32[]{:S(2)}) collective-permute-start(bf16[128,1024]{1,0:T(8,128)(2,1)S(1)} %get-tuple-element.248), channel_id=1, source_target_pairs={{0,4},{2,6},{4,0},{6,2},{8,12},{10,14},{12,8},{14,10},{1,5},{3,7},... | collective-permute-start | bytes 786440 | tf_op jit(solution)/shard_map/ppermute | solution.py:207
  6.0 19.1 %collective-permute-start.1 = (bf16[2,512,128]{2,1,0:T(8,128)(2,1)S(1)}, bf16[2,512,128]{2,1,0:T(8,128)(2,1)S(1)}, u32[]{:S(2)}, u32[]{:S(2)}) collective-permute-start(bf16[2,512,128]{2,1,0:T(8,128)(2,1)S(1)} %get-tuple-element.245), channel_id=1, source_target_pairs={{0,4},{2,6},{4,0},{6,2},{8,12},{10,14},{12,8},{14,10},{1,5},{3,7},... | collective-permute-start | bytes 786440 | tf_op jit(solution)/shard_map/ppermute | solution.py:207
  8.1 10.8 %collective-permute-start.3 = (bf16[256,128]{1,0:T(8,128)(2,1)S(1)}, bf16[256,128]{1,0:T(8,128)(2,1)S(1)}, u32[]{:S(2)}, u32[]{:S(2)}) collective-permute-start(bf16[256,128]{1,0:T(8,128)(2,1)S(1)} %get-tuple-element.243), channel_id=1, source_target_pairs={{0,4},{2,6},{4,0},{6,2},{8,12},{10,14},{12,8},{14,10},{1,5},{3,7},... | collective-permute-start | bytes 196616 | tf_op jit(solution)/shard_map/ppermute | solution.py:207
  9.7 11.1 %collective-permute-start.4 = (bf16[256,128]{1,0:T(8,128)(2,1)S(1)}, bf16[256,128]{1,0:T(8,128)(2,1)S(1)}, u32[]{:S(2)}, u32[]{:S(2)}) collective-permute-start(bf16[256,128]{1,0:T(8,128)(2,1)S(1)} %get-tuple-element.242), channel_id=1, source_target_pairs={{0,6},{2,4},{4,2},{6,0},{8,14},{10,12},{12,10},{14,8},{1,7},{3,5},... | collective-permute-start | bytes 196616 | tf_op jit(solution)/shard_map/ppermute | solution.py:207
  20.9 13.6 %collective-permute-start.6 = (bf16[256,512]{1,0:T(8,128)(2,1)S(1)}, bf16[256,512]{1,0:T(8,128)(2,1)}, u32[]{:S(2)}, u32[]{:S(2)}) collective-permute-start(bf16[256,512]{1,0:T(8,128)(2,1)S(1)} %pad_maximum_fusion.13), channel_id=1, source_target_pairs={{0,8},{2,10},{4,12},{6,14},{8,0},{10,2},{12,4},{14,6},{1,9},{3,11}... | collective-permute-start | bytes 786440 | tf_op jit(solution)/shard_map/ppermute | solution.py:216
  23.6 10.9 %collective-permute-start.7 = (bf16[256,512]{1,0:T(8,128)(2,1)S(1)}, bf16[256,512]{1,0:T(8,128)(2,1)S(1)}, u32[]{:S(2)}, u32[]{:S(2)}) collective-permute-start(bf16[256,512]{1,0:T(8,128)(2,1)S(1)} %pad_maximum_fusion.13), channel_id=1, source_target_pairs={{0,16},{16,0},{1,17},{17,1},{2,18},{18,2},{3,19},{19,3},{4,20},{20... | collective-permute-start | bytes 786440 | tf_op jit(solution)/shard_map/ppermute | solution.py:213
  34.6 11.8 %collective-permute-start.8 = (bf16[256,512]{1,0:T(8,128)(2,1)S(1)}, bf16[256,512]{1,0:T(8,128)(2,1)}, u32[]{:S(2)}, u32[]{:S(2)}) collective-permute-start(bf16[256,512]{1,0:T(8,128)(2,1)S(1)} %constant_dynamic-slice_fusion.13), channel_id=1, source_target_pairs={{0,2},{2,0},{4,6},{6,4},{8,10},{10,8},{12,14},{14,12},{1,3},{3,1},... | collective-permute-start | bytes 786440 | tf_op jit(solution)/shard_map/ppermute | solution.py:207
  35.3 11.0 %collective-permute-start.9 = (bf16[128,1024]{1,0:T(8,128)(2,1)S(1)}, bf16[128,1024]{1,0:T(8,128)(2,1)S(1)}, u32[]{:S(2)}, u32[]{:S(2)}) collective-permute-start(bf16[128,1024]{1,0:T(8,128)(2,1)S(1)} %get-tuple-element.241), channel_id=1, source_target_pairs={{0,4},{2,6},{4,0},{6,2},{8,12},{10,14},{12,8},{14,10},{1,5},{3,7},... | collective-permute-start | bytes 786440 | tf_op jit(solution)/shard_map/ppermute | solution.py:207
  35.8 10.6 %collective-permute-start.10 = (bf16[256,512]{1,0:T(8,128)(2,1)}, bf16[256,512]{1,0:T(8,128)(2,1)S(1)}, u32[]{:S(2)}, u32[]{:S(2)}) collective-permute-start(bf16[256,512]{1,0:T(8,128)(2,1)} %collective-permute-done.6), channel_id=1, source_target_pairs={{0,16},{16,0},{1,17},{17,1},{2,18},{18,2},{3,19},{19,3},{4,20},{20... | collective-permute-start | bytes 786440 | tf_op jit(solution)/shard_map/ppermute | solution.py:213
  37.4 15.0 %collective-permute-start.11 = (bf16[256,512]{1,0:T(8,128)(2,1)S(1)}, bf16[256,512]{1,0:T(8,128)(2,1)}, u32[]{:S(2)}, u32[]{:S(2)}) collective-permute-start(bf16[256,512]{1,0:T(8,128)(2,1)S(1)} %constant_dynamic-slice_fusion.9), channel_id=1, source_target_pairs={{0,8},{2,10},{4,12},{6,14},{8,0},{10,2},{12,4},{14,6},{1,9},{3,11}... | collective-permute-start | bytes 786440 | tf_op jit(solution)/shard_map/ppermute | solution.py:216
  58.9 12.2 %collective-permute-start.16 = (bf16[256,512]{1,0:T(8,128)(2,1)}, bf16[256,512]{1,0:T(8,128)(2,1)}, u32[]{:S(2)}, u32[]{:S(2)}) collective-permute-start(bf16[256,512]{1,0:T(8,128)(2,1)} %constant_dynamic-slice_fusion.7), channel_id=1, source_target_pairs={{0,2},{2,0},{4,6},{6,4},{8,10},{10,8},{12,14},{14,12},{1,3},{3,1},... | collective-permute-start | bytes 786440 | tf_op jit(solution)/shard_map/ppermute | solution.py:207
  60.4 10.7 %collective-permute-start.17 = (bf16[256,512]{1,0:T(8,128)(2,1)}, bf16[256,512]{1,0:T(8,128)(2,1)}, u32[]{:S(2)}, u32[]{:S(2)}) collective-permute-start(bf16[256,512]{1,0:T(8,128)(2,1)} %collective-permute-done.11), channel_id=1, source_target_pairs={{0,16},{16,0},{1,17},{17,1},{2,18},{18,2},{3,19},{19,3},{4,20},{20... | collective-permute-start | bytes 786440 | tf_op jit(solution)/shard_map/ppermute | solution.py:213
  61.2 12.2 %collective-permute-start.13 = (bf16[64,1024]{1,0:T(8,128)(2,1)S(1)}, bf16[64,1024]{1,0:T(8,128)(2,1)S(1)}, u32[]{:S(2)}, u32[]{:S(2)}) collective-permute-start(bf16[64,1024]{1,0:T(8,128)(2,1)S(1)} %get-tuple-element.230), channel_id=1, source_target_pairs={{0,2},{2,0},{4,6},{6,4},{8,10},{10,8},{12,14},{14,12},{1,3},{3,1},... | collective-permute-start | bytes 393224 | tf_op jit(solution)/shard_map/ppermute | solution.py:207
  61.8 11.7 %collective-permute-start.14 = (bf16[64,1024]{1,0:T(8,128)(2,1)S(1)}, bf16[64,1024]{1,0:T(8,128)(2,1)S(1)}, u32[]{:S(2)}, u32[]{:S(2)}) collective-permute-start(bf16[64,1024]{1,0:T(8,128)(2,1)S(1)} %get-tuple-element.229), channel_id=1, source_target_pairs={{0,4},{2,6},{4,0},{6,2},{8,12},{10,14},{12,8},{14,10},{1,5},{3,7},... | collective-permute-start | bytes 393224 | tf_op jit(solution)/shard_map/ppermute | solution.py:207
  61.8 11.7 %collective-permute-start.15 = (bf16[64,1024]{1,0:T(8,128)(2,1)S(1)}, bf16[64,1024]{1,0:T(8,128)(2,1)S(1)}, u32[]{:S(2)}, u32[]{:S(2)}) collective-permute-start(bf16[64,1024]{1,0:T(8,128)(2,1)S(1)} %get-tuple-element.228), channel_id=1, source_target_pairs={{0,6},{2,4},{4,2},{6,0},{8,14},{10,12},{12,10},{14,8},{1,7},{3,5},... | collective-permute-start | bytes 393224 | tf_op jit(solution)/shard_map/ppermute | solution.py:207
  90.4 20.5 %collective-permute-start.20 = (bf16[2,64,1024]{2,1,0:T(8,128)(2,1)S(1)}, bf16[2,64,1024]{2,1,0:T(8,128)(2,1)S(1)}, u32[]{:S(2)}, u32[]{:S(2)}) collective-permute-start(bf16[2,64,1024]{2,1,0:T(8,128)(2,1)S(1)} %pad_maximum_fusion.14), channel_id=1, source_target_pairs={{0,2},{2,0},{4,6},{6,4},{8,10},{10,8},{12,14},{14,12},{1,3},{3,1},... | collective-permute-start | bytes 786440 | tf_op jit(solution)/shard_map/ppermute | solution.py:207
  91.0 19.9 %collective-permute-start.21 = (bf16[2,64,1024]{2,1,0:T(8,128)(2,1)S(1)}, bf16[2,64,1024]{2,1,0:T(8,128)(2,1)S(1)}, u32[]{:S(2)}, u32[]{:S(2)}) collective-permute-start(bf16[2,64,1024]{2,1,0:T(8,128)(2,1)S(1)} %pad_maximum_fusion.14), channel_id=1, source_target_pairs={{0,4},{2,6},{4,0},{6,2},{8,12},{10,14},{12,8},{14,10},{1,5},{3,7},... | collective-permute-start | bytes 786440 | tf_op jit(solution)/shard_map/ppermute | solution.py:207
  91.0 19.9 %collective-permute-start.22 = (bf16[2,64,1024]{2,1,0:T(8,128)(2,1)S(1)}, bf16[2,64,1024]{2,1,0:T(8,128)(2,1)S(1)}, u32[]{:S(2)}, u32[]{:S(2)}) collective-permute-start(bf16[2,64,1024]{2,1,0:T(8,128)(2,1)S(1)} %pad_maximum_fusion.14), channel_id=1, source_target_pairs={{0,6},{2,4},{4,2},{6,0},{8,14},{10,12},{12,10},{14,8},{1,7},{3,5},... | collective-permute-start | bytes 786440 | tf_op jit(solution)/shard_map/ppermute | solution.py:207
  94.0 14.6 %collective-permute-start.24 = (bf16[64,1024]{1,0:T(8,128)(2,1)}, bf16[64,1024]{1,0:T(8,128)(2,1)S(1)}, u32[]{:S(2)}, u32[]{:S(2)}) collective-permute-start(bf16[64,1024]{1,0:T(8,128)(2,1)} %get-tuple-element.224), channel_id=1, source_target_pairs={{0,4},{2,6},{4,0},{6,2},{8,12},{10,14},{12,8},{14,10},{1,5},{3,7},... | collective-permute-start | bytes 393224 | tf_op jit(solution)/shard_map/ppermute | solution.py:207
  94.7 16.1 %collective-permute-start.25 = (bf16[64,1024]{1,0:T(8,128)(2,1)}, bf16[64,1024]{1,0:T(8,128)(2,1)S(1)}, u32[]{:S(2)}, u32[]{:S(2)}) collective-permute-start(bf16[64,1024]{1,0:T(8,128)(2,1)} %get-tuple-element.223), channel_id=1, source_target_pairs={{0,6},{2,4},{4,2},{6,0},{8,14},{10,12},{12,10},{14,8},{1,7},{3,5},... | collective-permute-start | bytes 393224 | tf_op jit(solution)/shard_map/ppermute | solution.py:207
  111.0 21.9 %collective-permute-start.26 = (bf16[512,1024]{1,0:T(8,128)(2,1)S(1)}, bf16[512,1024]{1,0:T(8,128)(2,1)S(1)}, u32[]{:S(2)}, u32[]{:S(2)}) collective-permute-start(bf16[512,1024]{1,0:T(8,128)(2,1)S(1)} %bitcast.175), channel_id=1, source_target_pairs={{0,1},{1,0},{2,3},{3,2},{4,5},{5,4},{6,7},{7,6},{8,9},{9,8},{10,11... | collective-permute-start | bytes 3145736 | tf_op jit(solution)/shard_map/ppermute | solution.py:210
  112.4 20.5 %collective-permute-start.27 = (bf16[64,1024]{1,0:T(8,128)(2,1)S(1)}, bf16[64,1024]{1,0:T(8,128)(2,1)S(1)}, u32[]{:S(2)}, u32[]{:S(2)}) collective-permute-start(bf16[64,1024]{1,0:T(8,128)(2,1)S(1)} %get-tuple-element.260), channel_id=1, source_target_pairs={{0,8},{2,10},{4,12},{6,14},{8,0},{10,2},{12,4},{14,6},{1,9},{3,11}... | collective-permute-start | bytes 393224 | tf_op jit(solution)/shard_map/ppermute | solution.py:216
  112.7 32.0 %collective-permute-start.31 = (bf16[512,512]{1,0:T(8,128)(2,1)S(1)}, bf16[512,512]{1,0:T(8,128)(2,1)S(1)}, u32[]{:S(2)}, u32[]{:S(2)}) collective-permute-start(bf16[512,512]{1,0:T(8,128)(2,1)S(1)} %pad_maximum_fusion.9), channel_id=1, source_target_pairs={{0,8},{2,10},{4,12},{6,14},{8,0},{10,2},{12,4},{14,6},{1,9},{3,11}... | collective-permute-start | bytes 1572872 | tf_op jit(solution)/shard_map/ppermute | solution.py:216
  132.9 11.8 %collective-permute-start.28 = (bf16[2,64,1024]{2,1,0:T(8,128)(2,1)S(1)}, bf16[2,64,1024]{2,1,0:T(8,128)(2,1)S(1)}, u32[]{:S(2)}, u32[]{:S(2)}) collective-permute-start(bf16[2,64,1024]{2,1,0:T(8,128)(2,1)S(1)} %pad_maximum_fusion.15), channel_id=1, source_target_pairs={{0,2},{2,0},{4,6},{6,4},{8,10},{10,8},{12,14},{14,12},{1,3},{3,1},... | collective-permute-start | bytes 786440 | tf_op jit(solution)/shard_map/ppermute | solution.py:207
  133.5 16.3 %collective-permute-start.29 = (bf16[2,64,1024]{2,1,0:T(8,128)(2,1)S(1)}, bf16[2,64,1024]{2,1,0:T(8,128)(2,1)S(1)}, u32[]{:S(2)}, u32[]{:S(2)}) collective-permute-start(bf16[2,64,1024]{2,1,0:T(8,128)(2,1)S(1)} %pad_maximum_fusion.15), channel_id=1, source_target_pairs={{0,4},{2,6},{4,0},{6,2},{8,12},{10,14},{12,8},{14,10},{1,5},{3,7},... | collective-permute-start | bytes 786440 | tf_op jit(solution)/shard_map/ppermute | solution.py:207
  133.5 21.7 %collective-permute-start.30 = (bf16[2,64,1024]{2,1,0:T(8,128)(2,1)S(1)}, bf16[2,64,1024]{2,1,0:T(8,128)(2,1)S(1)}, u32[]{:S(2)}, u32[]{:S(2)}) collective-permute-start(bf16[2,64,1024]{2,1,0:T(8,128)(2,1)S(1)} %pad_maximum_fusion.15), channel_id=1, source_target_pairs={{0,6},{2,4},{4,2},{6,0},{8,14},{10,12},{12,10},{14,8},{1,7},{3,5},... | collective-permute-start | bytes 786440 | tf_op jit(solution)/shard_map/ppermute | solution.py:207
  156.0 27.8 %collective-permute-start.37 = (bf16[512,512]{1,0:T(8,128)(2,1)S(1)}, bf16[512,512]{1,0:T(8,128)(2,1)}, u32[]{:S(2)}, u32[]{:S(2)}) collective-permute-start(bf16[512,512]{1,0:T(8,128)(2,1)S(1)} %pad_maximum_fusion.10), channel_id=1, source_target_pairs={{0,8},{2,10},{4,12},{6,14},{8,0},{10,2},{12,4},{14,6},{1,9},{3,11}... | collective-permute-start | bytes 1572872 | tf_op jit(solution)/shard_map/ppermute | solution.py:216
  166.7 17.2 %collective-permute-start.34 = (bf16[2,64,1024]{2,1,0:T(8,128)(2,1)S(1)}, bf16[2,64,1024]{2,1,0:T(8,128)(2,1)S(1)}, u32[]{:S(2)}, u32[]{:S(2)}) collective-permute-start(bf16[2,64,1024]{2,1,0:T(8,128)(2,1)S(1)} %bitcast.208), channel_id=1, source_target_pairs={{0,2},{2,0},{4,6},{6,4},{8,10},{10,8},{12,14},{14,12},{1,3},{3,1},... | collective-permute-start | bytes 786440 | tf_op jit(solution)/shard_map/ppermute | solution.py:207
  168.3 18.6 %collective-permute-start.35 = (bf16[2,64,1024]{2,1,0:T(8,128)(2,1)S(1)}, bf16[2,64,1024]{2,1,0:T(8,128)(2,1)S(1)}, u32[]{:S(2)}, u32[]{:S(2)}) collective-permute-start(bf16[2,64,1024]{2,1,0:T(8,128)(2,1)S(1)} %bitcast.206), channel_id=1, source_target_pairs={{0,4},{2,6},{4,0},{6,2},{8,12},{10,14},{12,8},{14,10},{1,5},{3,7},... | collective-permute-start | bytes 786440 | tf_op jit(solution)/shard_map/ppermute | solution.py:207
  170.0 22.9 %collective-permute-start.36 = (bf16[2,64,1024]{2,1,0:T(8,128)(2,1)S(1)}, bf16[2,64,1024]{2,1,0:T(8,128)(2,1)S(1)}, u32[]{:S(2)}, u32[]{:S(2)}) collective-permute-start(bf16[2,64,1024]{2,1,0:T(8,128)(2,1)S(1)} %bitcast.205), channel_id=1, source_target_pairs={{0,6},{2,4},{4,2},{6,0},{8,14},{10,12},{12,10},{14,8},{1,7},{3,5},... | collective-permute-start | bytes 786440 | tf_op jit(solution)/shard_map/ppermute | solution.py:207
  193.1 15.5 %collective-permute-start.42 = (bf16[2,64,1024]{2,1,0:T(8,128)(2,1)S(1)}, bf16[2,64,1024]{2,1,0:T(8,128)(2,1)S(1)}, u32[]{:S(2)}, u32[]{:S(2)}) collective-permute-start(bf16[2,64,1024]{2,1,0:T(8,128)(2,1)S(1)} %add_convert_fusion.3), channel_id=1, source_target_pairs={{0,8},{2,10},{4,12},{6,14},{8,0},{10,2},{12,4},{14,6},{1,9},{3,11}... | collective-permute-start | bytes 786440 | tf_op jit(solution)/shard_map/ppermute | solution.py:216
  196.1 12.6 %collective-permute-start.39 = (bf16[2,64,1024]{2,1,0:T(8,128)(2,1)S(1)}, bf16[2,64,1024]{2,1,0:T(8,128)(2,1)S(1)}, u32[]{:S(2)}, u32[]{:S(2)}) collective-permute-start(bf16[2,64,1024]{2,1,0:T(8,128)(2,1)S(1)} %bitcast.211), channel_id=1, source_target_pairs={{0,2},{2,0},{4,6},{6,4},{8,10},{10,8},{12,14},{14,12},{1,3},{3,1},... | collective-permute-start | bytes 786440 | tf_op jit(solution)/shard_map/ppermute | solution.py:207
  197.1 14.7 %collective-permute-start.40 = (bf16[2,64,1024]{2,1,0:T(8,128)(2,1)S(1)}, bf16[2,64,1024]{2,1,0:T(8,128)(2,1)S(1)}, u32[]{:S(2)}, u32[]{:S(2)}) collective-permute-start(bf16[2,64,1024]{2,1,0:T(8,128)(2,1)S(1)} %bitcast.209), channel_id=1, source_target_pairs={{0,4},{2,6},{4,0},{6,2},{8,12},{10,14},{12,8},{14,10},{1,5},{3,7},... | collective-permute-start | bytes 786440 | tf_op jit(solution)/shard_map/ppermute | solution.py:207
  197.4 19.5 %collective-permute-start.41 = (bf16[2,64,1024]{2,1,0:T(8,128)(2,1)S(1)}, bf16[2,64,1024]{2,1,0:T(8,128)(2,1)S(1)}, u32[]{:S(2)}, u32[]{:S(2)}) collective-permute-start(bf16[2,64,1024]{2,1,0:T(8,128)(2,1)S(1)} %bitcast.207), channel_id=1, source_target_pairs={{0,6},{2,4},{4,2},{6,0},{8,14},{10,12},{12,10},{14,8},{1,7},{3,5},... | collective-permute-start | bytes 786440 | tf_op jit(solution)/shard_map/ppermute | solution.py:207
  217.1 17.5 %collective-permute-start.46 = (bf16[2,64,1024]{2,1,0:T(8,128)(2,1)S(1)}, bf16[2,64,1024]{2,1,0:T(8,128)(2,1)S(1)}, u32[]{:S(2)}, u32[]{:S(2)}) collective-permute-start(bf16[2,64,1024]{2,1,0:T(8,128)(2,1)S(1)} %add_convert_fusion.2), channel_id=1, source_target_pairs={{0,8},{2,10},{4,12},{6,14},{8,0},{10,2},{12,4},{14,6},{1,9},{3,11}... | collective-permute-start | bytes 786440 | tf_op jit(solution)/shard_map/ppermute | solution.py:216
  218.2 13.9 %collective-permute-start.44 = (bf16[64,1536]{1,0:T(8,128)(2,1)S(1)}, bf16[64,1536]{1,0:T(8,128)(2,1)S(1)}, u32[]{:S(2)}, u32[]{:S(2)}) collective-permute-start(bf16[64,1536]{1,0:T(8,128)(2,1)S(1)} %pad_maximum_fusion.16), channel_id=1, source_target_pairs={{0,4},{2,6},{4,0},{6,2},{8,12},{10,14},{12,8},{14,10},{1,5},{3,7},... | collective-permute-start | bytes 589832 | tf_op jit(solution)/shard_map/ppermute | solution.py:207
  220.9 13.8 %collective-permute-start.45 = (bf16[64,1536]{1,0:T(8,128)(2,1)S(1)}, bf16[64,1536]{1,0:T(8,128)(2,1)S(1)}, u32[]{:S(2)}, u32[]{:S(2)}) collective-permute-start(bf16[64,1536]{1,0:T(8,128)(2,1)S(1)} %pad_maximum_fusion.16), channel_id=1, source_target_pairs={{0,6},{2,4},{4,2},{6,0},{8,14},{10,12},{12,10},{14,8},{1,7},{3,5},... | collective-permute-start | bytes 589832 | tf_op jit(solution)/shard_map/ppermute | solution.py:207
  234.9 14.8 %collective-permute-start.47 = (bf16[4,64,1536]{2,1,0:T(8,128)(2,1)S(1)}, bf16[4,64,1536]{2,1,0:T(8,128)(2,1)}, u32[]{:S(2)}, u32[]{:S(2)}) collective-permute-start(bf16[4,64,1536]{2,1,0:T(8,128)(2,1)S(1)} %get-tuple-element.192), channel_id=1, source_target_pairs={{0,1},{1,0},{2,3},{3,2},{4,5},{5,4},{6,7},{7,6},{8,9},{9,8},{10,11... | collective-permute-start | bytes 2359304 | tf_op jit(solution)/shard_map/ppermute | solution.py:210
  235.7 12.3 %collective-permute-start.55 = (bf16[64,1536]{1,0:T(8,128)(2,1)}, bf16[64,1536]{1,0:T(8,128)(2,1)}, u32[]{:S(2)}, u32[]{:S(2)}) collective-permute-start(bf16[64,1536]{1,0:T(8,128)(2,1)} %get-tuple-element.254), channel_id=1, source_target_pairs={{0,4},{2,6},{4,0},{6,2},{8,12},{10,14},{12,8},{14,10},{1,5},{3,7},... | collective-permute-start | bytes 589832 | tf_op jit(solution)/shard_map/ppermute | solution.py:207
  249.6 10.8 %collective-permute-start.57 = (bf16[4,64,1536]{2,1,0:T(8,128)(2,1)S(1)}, bf16[4,64,1536]{2,1,0:T(8,128)(2,1)S(1)}, u32[]{:S(2)}, u32[]{:S(2)}) collective-permute-start(bf16[4,64,1536]{2,1,0:T(8,128)(2,1)S(1)} %get-tuple-element.190), channel_id=1, source_target_pairs={{0,1},{1,0},{2,3},{3,2},{4,5},{5,4},{6,7},{7,6},{8,9},{9,8},{10,11... | collective-permute-start | bytes 2359304 | tf_op jit(solution)/shard_map/ppermute | solution.py:210
  253.6 11.2 %collective-permute-start.48 = (bf16[512,128]{1,0:T(8,128)(2,1)S(1)}, bf16[512,128]{1,0:T(8,128)(2,1)S(1)}, u32[]{:S(2)}, u32[]{:S(2)}) collective-permute-start(bf16[512,128]{1,0:T(8,128)(2,1)S(1)} %get-tuple-element.219), channel_id=1, source_target_pairs={{0,2},{2,0},{4,6},{6,4},{8,10},{10,8},{12,14},{14,12},{1,3},{3,1},... | collective-permute-start | bytes 393224 | tf_op jit(solution)/shard_map/ppermute | solution.py:207
  254.6 12.7 %collective-permute-start.49 = (bf16[512,128]{1,0:T(8,128)(2,1)S(1)}, bf16[512,128]{1,0:T(8,128)(2,1)S(1)}, u32[]{:S(2)}, u32[]{:S(2)}) collective-permute-start(bf16[512,128]{1,0:T(8,128)(2,1)S(1)} %get-tuple-element.218), channel_id=1, source_target_pairs={{0,4},{2,6},{4,0},{6,2},{8,12},{10,14},{12,8},{14,10},{1,5},{3,7},... | collective-permute-start | bytes 393224 | tf_op jit(solution)/shard_map/ppermute | solution.py:207
  254.6 12.8 %collective-permute-start.50 = (bf16[512,128]{1,0:T(8,128)(2,1)S(1)}, bf16[512,128]{1,0:T(8,128)(2,1)S(1)}, u32[]{:S(2)}, u32[]{:S(2)}) collective-permute-start(bf16[512,128]{1,0:T(8,128)(2,1)S(1)} %get-tuple-element.217), channel_id=1, source_target_pairs={{0,6},{2,4},{4,2},{6,0},{8,14},{10,12},{12,10},{14,8},{1,7},{3,5},... | collective-permute-start | bytes 393224 | tf_op jit(solution)/shard_map/ppermute | solution.py:207
  259.3 10.4 %collective-permute-start.51 = (bf16[128,512]{1,0:T(8,128)(2,1)S(1)}, bf16[128,512]{1,0:T(8,128)(2,1)S(1)}, u32[]{:S(2)}, u32[]{:S(2)}) collective-permute-start(bf16[128,512]{1,0:T(8,128)(2,1)S(1)} %get-tuple-element.215), channel_id=1, source_target_pairs={{0,2},{2,0},{4,6},{6,4},{8,10},{10,8},{12,14},{14,12},{1,3},{3,1},... | collective-permute-start | bytes 393224 | tf_op jit(solution)/shard_map/ppermute | solution.py:207
  260.4 11.0 %collective-permute-start.52 = (bf16[128,512]{1,0:T(8,128)(2,1)S(1)}, bf16[128,512]{1,0:T(8,128)(2,1)S(1)}, u32[]{:S(2)}, u32[]{:S(2)}) collective-permute-start(bf16[128,512]{1,0:T(8,128)(2,1)S(1)} %get-tuple-element.214), channel_id=1, source_target_pairs={{0,4},{2,6},{4,0},{6,2},{8,12},{10,14},{12,8},{14,10},{1,5},{3,7},... | collective-permute-start | bytes 393224 | tf_op jit(solution)/shard_map/ppermute | solution.py:207
  267.4 10.4 %collective-permute-start.60 = (bf16[128,512]{1,0:T(8,128)(2,1)S(1)}, bf16[128,512]{1,0:T(8,128)(2,1)S(1)}, u32[]{:S(2)}, u32[]{:S(2)}) collective-permute-start(bf16[128,512]{1,0:T(8,128)(2,1)S(1)} %get-tuple-element.205), channel_id=1, source_target_pairs={{0,6},{2,4},{4,2},{6,0},{8,14},{10,12},{12,10},{14,8},{1,7},{3,5},... | collective-permute-start | bytes 393224 | tf_op jit(solution)/shard_map/ppermute | solution.py:207
  269.8 11.3 %collective-permute-start.58 = (bf16[128,512]{1,0:T(8,128)(2,1)S(1)}, bf16[128,512]{1,0:T(8,128)(2,1)S(1)}, u32[]{:S(2)}, u32[]{:S(2)}) collective-permute-start(bf16[128,512]{1,0:T(8,128)(2,1)S(1)} %get-tuple-element.204), channel_id=1, source_target_pairs={{0,2},{2,0},{4,6},{6,4},{8,10},{10,8},{12,14},{14,12},{1,3},{3,1},... | collective-permute-start | bytes 393224 | tf_op jit(solution)/shard_map/ppermute | solution.py:207
  272.3 10.6 %collective-permute-start.61 = (bf16[512,128]{1,0:T(8,128)(2,1)S(1)}, bf16[512,128]{1,0:T(8,128)(2,1)S(1)}, u32[]{:S(2)}, u32[]{:S(2)}) collective-permute-start(bf16[512,128]{1,0:T(8,128)(2,1)S(1)} %get-tuple-element.201), channel_id=1, source_target_pairs={{0,2},{2,0},{4,6},{6,4},{8,10},{10,8},{12,14},{14,12},{1,3},{3,1},... | collective-permute-start | bytes 393224 | tf_op jit(solution)/shard_map/ppermute | solution.py:207
  (61 other events, 487.5 us)

commit v9 on v5

--- a/solution.py
+++ b/solution.py
@@ -252,21 +252,27 @@
             parts.append(up(parts[-1]))
         return parts
 
-    def square_rows(v):
-        return exchange(
-            lambda r: lax.dynamic_slice_in_dim(v, (q ^ r) * quarter_d, quarter_d, 1)
-        )
-
-    def first_rows(v):
-        size = 2 * quarter_d
-        mine = lax.dynamic_slice_in_dim(v, q // 2 * size, size, 1)
-        other = lax.dynamic_slice_in_dim(v, (1 - q // 2) * size, size, 1)
-        return jnp.concatenate([mine, to_peer(other, 2)], axis=0)
-
-    def second_rows(v):
-        mine = lax.dynamic_slice_in_dim(v, q % 2 * quarter_d, quarter_d, 1)
-        other = lax.dynamic_slice_in_dim(v, (1 - q % 2) * quarter_d, quarter_d, 1)
-        return mine, to_peer(other, 1)
+    def to_square(v, k, r):
+        perm = [(e, (e // 4 + k) % nh * 4 + (e % 4 ^ r)) for e in range(n_expert)]
+        return lax.ppermute(v, "expert", perm)
+
+    def pair_rows(v):
+        def quarters(i):
+            parts = [(2 * j + i) * quarter_d for j in (0, 1)]
+            parts = [lax.dynamic_slice_in_dim(v, at, quarter_d, 1) for at in parts]
+            return jnp.concatenate(parts, axis=1)
+
+        return quarters(q % 2), to_peer(quarters(1 - q % 2), 1)
+
+    def spread_rows(mine, theirs):
+        v = jnp.concatenate([mine, theirs], axis=0)
+        mine = lax.dynamic_slice_in_dim(v, q // 2 * quarter_d, quarter_d, 1)
+        other = lax.dynamic_slice_in_dim(v, (1 - q // 2) * quarter_d, quarter_d, 1)
+        far = [(to_square(mine, k, 0), to_square(other, k, 2)) for k in range(1, nh)]
+        return (mine, other), far
+
+    def join_pairs(parts):
+        return [jnp.concatenate(v, axis=0) for v in parts]
 
     def square_weight(v):
         size = quarter_d // 2 if shared else quarter_d
@@ -285,14 +291,18 @@
     def all_features(v, theirs):
         return flip(jnp.concatenate([v, theirs], axis=0), g, 0) if shared else v
 
-    def project(rows, weights):
-        parts = [dot(rows, weight).astype(bf16) for weight in weights]
-        part = jnp.concatenate(parts, axis=1).reshape(4, 2, half_rows, latent)
-        mine = lax.dynamic_index_in_dim(part, t, 1, keepdims=False)
-        return mine, lax.dynamic_index_in_dim(part, 1 - t, 1, keepdims=False)
-
-    def own_latent(parts):
-        return jnp.concatenate(turn(jnp.split(add(*parts), nh, axis=1)), axis=1)
+    def project(rows, weight):
+        parts = [dot(v, weight).astype(bf16).reshape(4, 2, half_rows, cols) for v in rows]
+        part = jnp.stack(parts, axis=1)
+        mine = lax.dynamic_index_in_dim(part, t, 2, keepdims=False)
+        return mine, lax.dynamic_index_in_dim(part, 1 - t, 2, keepdims=False)
+
+    def own_latent(pieces):
+        rows = []
+        for k in range(nh):
+            blocks = turn([pieces[j][(k - j) % nh] for j in range(nh)])
+            rows.append(jnp.concatenate(blocks, axis=1))
+        return jnp.stack(rows)
 
     def sum_tensor(part):
         part = part.reshape(2, 4, nh, half_rows, latent)
@@ -347,51 +357,46 @@
     def rows_with(part, theirs):
         return jnp.stack([part, theirs]).reshape(-1, latent)
 
-    down_parts = gather_h(join_quarters(square_weight(down_weight)))
-    up_block = square_weight(up_weight)
-    theirs = [swap_features(down_parts[0])]
-    *up_block, down_parts[-1], theirs[0] = together(*up_block, down_parts[-1], theirs[0])
-    up_parts = gather_h(join_quarters(up_block))
-    token_rows = square_rows(after(tokens, down_parts[-1]))
-    theirs += [swap_features(v) for v in down_parts[1:]]
-    *token_rows, theirs[-1], up_parts[-1] = together(*token_rows, theirs[-1], up_parts[-1])
-    cot_rows = first_rows(after(cotangent, token_rows[-1]))
-    token_rows = jnp.concatenate(token_rows, axis=0)
-    down_parts = [all_features(v, w) for v, w in zip(down_parts, theirs)]
-
-    mine, other = project(token_rows, down_parts)
-    theirs = [swap_features(v) for v in up_parts]
+    tok_mine, tok_theirs = pair_rows(tokens)
+    down_half = square_weight(down_weight)
+    cot_mine, cot_theirs = pair_rows(after(cotangent, tok_theirs, *down_half[1:]))
+    up_half = square_weight(after(up_weight, tok_theirs, *down_half[1:]))
+    tok_near, tok_far = spread_rows(tok_mine, tok_theirs)
+    *up_half, cot_theirs, near, far, far2 = together(
+        *up_half, cot_theirs, to_peer(tok_near[1], 2), *tok_far[-1]
+    )
+    token_parts = join_pairs([(tok_near[0], near), *tok_far[:-1], (far, far2)])
+    cot_near, cot_far = spread_rows(cot_mine, cot_theirs)
+    down_half, up_half = join_quarters(down_half), join_quarters(up_half)
+    down_own = all_features(down_half, swap_features(down_half))
+
+    mine, other = project(token_parts, down_own)
     part_x = add(mine, t_swap(other))
-    cot_rows = after(cot_rows, part_x)
     part_x = exchange(lambda r: part_x[r])
-    mine, other = second_rows(cot_rows)
-    *part_x, other, theirs[-1] = together(*part_x, other, theirs[-1])
-    cot_rows = [v[i * tok_rows : (i + 1) * tok_rows] for i in (0, 1) for v in (mine, other)]
-    cot_rows = jnp.concatenate(cot_rows, axis=0)
-    part_x = gather_h(own_latent(part_x))
-    up_parts = [all_features(v, w) for v, w in zip(up_parts, theirs)]
-    mine, other = project(cot_rows, up_parts)
-    *part_x, other = together(*part_x, t_swap(other))
-    part_y = add(mine, other)
-    part_x = jnp.stack(part_x)
-    part_x = exchange(lambda r: part_x)
-    part_y = exchange(lambda r: part_y[r])
-    *part_x, part_y[1], part_y[2], part_y[3] = together(*part_x, *part_y[1:])
-    part_x = jnp.stack(part_x)
-    part_y = gather_h(own_latent(part_y))
-    *part_y, other = together(*part_y, t_swap(part_x))
-    part_y = jnp.stack(part_y)
-    latent_in = rows_with(part_x, other)
-    token_parts = gather_h(after(token_rows, other))
+    sum_x = add(*part_x)
+    near = to_peer(after(cot_near[1], sum_x), 2)
+    up_own = all_features(up_half, swap_features(after(up_half, sum_x)))
+    part_x = gather_h(sum_x)
+    part_x[-1], *far = together(part_x[-1], *cot_far[-1])
+    cot_parts = join_pairs([(cot_near[0], near), *cot_far[:-1], far])
+    part_x = own_latent(part_x)
+    part_x = jnp.stack(exchange(lambda r: part_x))
+    mine, other = project(cot_parts, up_own)
+    part_y = add(mine, t_swap(other))
+    part_y = own_latent(gather_h(add(*exchange(lambda r: part_y[r]))))
+    part_x = after(part_x, part_y)
+    latent_in = rows_with(part_x, t_swap(part_x))
+    up_far = gather_h(after(up_half, part_x))[1:]
 
     hs, cp, cu, out_part = forward(
         latent_in, gate_blocks(gate_columns), gate_proj, up_proj, down_rows
     )
     part_y = exchange(lambda r: part_y)
-    *part_y, token_parts[-1], out_part = together(*part_y, token_parts[-1], out_part)
+    *part_y, up_far[-1], out_part = together(*part_y, up_far[-1], out_part)
     part_y = jnp.stack(part_y)
     latent_grad = rows_with(part_y, t_swap(part_y))
-    cot_parts = gather_h(after(cot_rows, token_parts[-1]))
+    up_theirs = [swap_features(v) for v in up_far]
+    down_far = gather_h(after(down_half, up_far[-1]))[1:]
     out_part = sum_tensor(out_part)
     down_proj_grad = down_grads(hs, latent_grad)
     out_part = after(out_part, down_proj_grad)
@@ -399,14 +404,19 @@
         after(latent_grad, out_part), cp, cu, gate_proj, up_proj, down_rows
     )
     out_part = exchange(lambda r: out_part[r])
-    *out_part, cot_parts[-1], in_part = together(*out_part, cot_parts[-1], in_part)
+    *out_part, up_theirs[-1], down_far[-1], in_part = together(
+        *out_part, up_theirs[-1], down_far[-1], in_part
+    )
+    up_parts = [up_own] + [all_features(v, w) for v, w in zip(up_far, up_theirs)]
+    down_theirs = [swap_features(v) for v in down_far]
     out_part = add(*out_part)
     in_part = sum_tensor(after(in_part, out_part))
     gate_proj_grad, up_proj_grad = input_grads(latent_in, after(dpu, in_part))
     in_part = exchange(lambda r: in_part[r])
-    *in_part, out_theirs, gate_proj_grad = together(
-        *in_part, sum_squares(out_part)[1], gate_proj_grad
-    )
+    *in_part, out_theirs, down_theirs[-1], gate_proj_grad = together(
+        *in_part, sum_squares(out_part)[1], down_theirs[-1], gate_proj_grad
+    )
+    down_parts = [down_own] + [all_features(v, w) for v, w in zip(down_far, down_theirs)]
     out_part = join_squares(out_part, out_theirs)
     in_part, in_theirs = sum_squares(add(*in_part))
     out_part = exchange(lambda r: out_part)

time: 267 us -> 258 us (0.966)
  waiting for transfers between devices: 125 us -> 104 us
  starting transfers between devices: 64.8 us -> 76.2 us
  local copies, waits for them, and re-layouts: 8.09 us -> 11.2 us
    ppermute x47 -> x46, waiting for transfers between devices: 99 us -> 84.8 us  [to_peer(): return lax.ppermute(v, 'expert', [(e, e ^ r) for e in range(n_expert)])]
    ppermute x8 -> x6, waiting for transfers between devices: 21.4 us -> 10.2 us  [up(): lax.ppermute(v, 'expert', [(e, (e + 4) % n_expert) for e in range(n_exper...]
    ppermute x0 -> x4, starting transfers between devices: none -> 6.33 us  [to_square(): return lax.ppermute(v, 'expert', perm)]
    ppermute x4, waiting for transfers between devices: 0.01 us -> 5.93 us  [g_swap(): return lax.ppermute(v, 'group', [(i, i ^ 1) for i in range(n_group)])]
    ppermute x47 -> x46, starting transfers between devices: 53.6 us -> 59.4 us  [to_peer(): return lax.ppermute(v, 'expert', [(e, e ^ r) for e in range(n_expert)])]
    unnamed x96 -> x109, local copies, waits for them, and re-layouts: 2.18 us -> 5.23 us
    ppermute x8 -> x6, starting transfers between devices: 5.5 us -> 5.02 us  [up(): lax.ppermute(v, 'expert', [(e, (e + 4) % n_expert) for e in range(n_exper...]
  transfers between devices with their start and end apart: 67 -> 68, of which waited for: 33 -> 28; matrix products, arithmetic and copies ran while one was open for 7% -> 7% of each run, Pallas kernels for 17% -> 18%
where the time goes in v9:
time: 258 us
  waiting for transfers between devices  104 us (40%)
  starting transfers between devices  76.2 us (30%)
  Pallas kernels  45.7 us (18%)
  other arithmetic  12.2 us (5%)
  local copies, waits for them, and re-layouts  11.2 us (4%)
  matrix products  6.74 us (3%)
    ppermute x46, waiting for transfers between devices, to_peer(): return lax.ppermute(v, 'expert', [(e, e ^ r) for e in range(n_expert)])  84.8 us
    ppermute x46, starting transfers between devices, to_peer(): return lax.ppermute(v, 'expert', [(e, e ^ r) for e in range(n_expert)])  59.4 us
    pallas_call x1, Pallas kernels, local(): forward(latent_in, gate_blocks(gate_columns), gate_proj, up_proj, down_rows)  16 us
    pallas_call x1, Pallas kernels, local(): backward(after(latent_grad, out_part), cp, cu, gate_proj, up_proj, down_r...  15.6 us
    ppermute x6, waiting for transfers between devices, up(): lax.ppermute(v, 'expert', [(e, (e + 4) % n_expert) for e in range(n_exper...  10.2 us
    pallas_call x1, Pallas kernels, local(): gate_proj_grad, up_proj_grad = input_grads(latent_in, after(dpu, in_part))  9.03 us
    dot_general x12, matrix products, dot(): return lax.dot_general(a, b, dims, preferred_element_type=f32)  6.74 us
    ppermute x4, starting transfers between devices, to_square(): return lax.ppermute(v, 'expert', perm)  6.33 us
  transfers between devices with their start and end apart: 68, of which 28 were waited for; matrix products, arithmetic and copies ran while one was open for 7% of the time, Pallas kernels for 18%

profile of v9, /device:TPU:0, one launch (start us, length us, event | category | flops | bytes accessed | tf_op | source)
XLA Modules:
  0.0 257.6 jit_solution(4421117430620948178)
XLA Ops:
  1.9 3.0 %collective-permute-start = (bf16[128,1024]{1,0:T(8,128)(2,1)S(1)}, bf16[128,1024]{1,0:T(8,128)(2,1)S(1)}, u32[]{:S(2)}, u32[]{:S(2)}) collective-permute-start(bf16[128,1024]{1,0:T(8,128)(2,1)S(1)} %pad_maximum_fusion.16), channel_id=1, source_target_pairs={{0,2},{2,0},{4,6},{6,4},{8,10},{10,8},{12,14},{14,12},{1,3},{3,1},... | collective-permute-start | bytes 786440 | tf_op jit(solution)/shard_map/ppermute | solution.py:206
  5.1 2.0 collective-permute-start.2
  8.5 4.8 %collective-permute-done = bf16[128,1024]{1,0:T(8,128)(2,1)S(1)} collective-permute-done((bf16[128,1024]{1,0:T(8,128)(2,1)S(1)}, bf16[128,1024]{1,0:T(8,128)(2,1)S(1)}, u32[]{:S(2)}, u32[]{:S(2)}) %collective-permute-start) | collective-permute-done | bytes 262176 | tf_op jit(solution)/shard_map/ppermute | solution.py:206
  13.5 3.9 %collective-permute-start.10 = (bf16[256,512]{1,0:T(8,128)(2,1)S(1)}, bf16[256,512]{1,0:T(8,128)(2,1)S(1)}, u32[]{:S(2)}, u32[]{:S(2)}) collective-permute-start(bf16[256,512]{1,0:T(8,128)(2,1)S(1)} %get-tuple-element.206), channel_id=1, source_target_pairs={{0,12},{2,14},{4,8},{6,10},{8,4},{10,6},{12,0},{14,2},{1,13},{3,15... | collective-permute-start | bytes 786440 | tf_op jit(solution)/shard_map/ppermute | solution.py:257
  18.8 1.7 collective-permute-start.4
  20.9 2.9 %collective-permute-done.4 = bf16[256,128]{1,0:T(8,128)(2,1)S(1)} collective-permute-done((bf16[256,128]{1,0:T(8,128)(2,1)S(1)}, bf16[256,128]{1,0:T(8,128)(2,1)S(1)}, u32[]{:S(2)}, u32[]{:S(2)}) %collective-permute-start.4) | collective-permute-done | bytes 65568 | tf_op jit(solution)/shard_map/ppermute | solution.py:206
  25.3 8.8 %collective-permute-done.5 = bf16[256,128]{1,0:T(8,128)(2,1)S(1)} collective-permute-done((bf16[256,128]{1,0:T(8,128)(2,1)S(1)}, bf16[256,128]{1,0:T(8,128)(2,1)S(1)}, u32[]{:S(2)}, u32[]{:S(2)}) %collective-permute-start.5) | collective-permute-done | bytes 65568 | tf_op jit(solution)/shard_map/ppermute | solution.py:206
  34.0 3.4 %collective-permute-start.6 = (bf16[256,128]{1,0:T(8,128)(2,1)S(1)}, bf16[256,128]{1,0:T(8,128)(2,1)S(1)}, u32[]{:S(2)}, u32[]{:S(2)}) collective-permute-start(bf16[256,128]{1,0:T(8,128)(2,1)S(1)} %get-tuple-element.211), channel_id=1, source_target_pairs={{0,6},{2,4},{4,2},{6,0},{8,14},{10,12},{12,10},{14,8},{1,7},{3,5},... | collective-permute-start | bytes 196616 | tf_op jit(solution)/shard_map/ppermute | solution.py:206
  37.5 2.9 %collective-permute-done.6 = bf16[256,128]{1,0:T(8,128)(2,1)S(1)} collective-permute-done((bf16[256,128]{1,0:T(8,128)(2,1)S(1)}, bf16[256,128]{1,0:T(8,128)(2,1)S(1)}, u32[]{:S(2)}, u32[]{:S(2)}) %collective-permute-start.6) | collective-permute-done | bytes 65568 | tf_op jit(solution)/shard_map/ppermute | solution.py:206
  42.8 5.9 %collective-permute-done.11 = bf16[256,512]{1,0:T(8,128)(2,1)S(1)} collective-permute-done((bf16[256,512]{1,0:T(8,128)(2,1)S(1)}, bf16[256,512]{1,0:T(8,128)(2,1)S(1)}, u32[]{:S(2)}, u32[]{:S(2)}) %collective-permute-start.11) | collective-permute-done | bytes 262176 | tf_op jit(solution)/shard_map/ppermute | solution.py:212
  51.1 1.7 collective-permute-start.20
  53.0 1.6 collective-permute-start.13
  54.9 1.7 collective-permute-start.15
  56.7 2.3 collective-permute-done.13
  58.9 12.6 %collective-permute-done.14 = bf16[2,64,512]{2,1,0:T(8,128)(2,1)S(1)} collective-permute-done((bf16[2,64,512]{2,1,0:T(8,128)(2,1)S(1)}, bf16[2,64,512]{2,1,0:T(8,128)(2,1)S(1)}, u32[]{:S(2)}, u32[]{:S(2)}) %collective-permute-start.14) | collective-permute-done | bytes 131104 | tf_op jit(solution)/shard_map/ppermute | solution.py:206
  72.9 1.6 collective-permute-start.17
  74.6 2.6 collective-permute-start.16
  77.9 3.5 %collective-permute-done.18 = bf16[2,64,512]{2,1,0:T(8,128)(2,1)S(1)} collective-permute-done((bf16[2,64,512]{2,1,0:T(8,128)(2,1)S(1)}, bf16[2,64,512]{2,1,0:T(8,128)(2,1)S(1)}, u32[]{:S(2)}, u32[]{:S(2)}) %collective-permute-start.18) | collective-permute-done | bytes 131104 | tf_op jit(solution)/shard_map/ppermute | solution.py:215
  85.2 1.8 collective-permute-done.21
  90.0 2.6 %collective-permute-start.31 = (bf16[2,64,1024]{2,1,0:T(8,128)(2,1)S(1)}, bf16[2,64,1024]{2,1,0:T(8,128)(2,1)S(1)}, u32[]{:S(2)}, u32[]{:S(2)}) collective-permute-start(bf16[2,64,1024]{2,1,0:T(8,128)(2,1)S(1)} %get-tuple-element.219), channel_id=1, source_target_pairs={{0,6},{2,4},{4,2},{6,0},{8,14},{10,12},{12,10},{14,8},{1,7},{3,5},... | collective-permute-start | bytes 786440 | tf_op jit(solution)/shard_map/ppermute | solution.py:206
  92.6 1.6 collective-permute-done.22
  96.3 11.3 %collective-permute-done.23 = bf16[2,64,512]{2,1,0:T(8,128)(2,1)S(1)} collective-permute-done((bf16[2,64,512]{2,1,0:T(8,128)(2,1)}, bf16[2,64,512]{2,1,0:T(8,128)(2,1)S(1)}, u32[]{:S(2)}, u32[]{:S(2)}) %collective-permute-start.23) | collective-permute-done | bytes 131104 | tf_op jit(solution)/shard_map/ppermute | solution.py:206
  107.6 2.0 collective-permute-done.24
  110.5 6.7 %collective-permute-done.25 = bf16[2,64,512]{2,1,0:T(8,128)(2,1)S(1)} collective-permute-done((bf16[2,64,512]{2,1,0:T(8,128)(2,1)S(1)}, bf16[2,64,512]{2,1,0:T(8,128)(2,1)S(1)}, u32[]{:S(2)}, u32[]{:S(2)}) %collective-permute-start.25) | collective-permute-done | bytes 131104 | tf_op jit(solution)/shard_map/ppermute | solution.py:215
  119.1 2.6 %collective-permute-start.28 = (bf16[2,64,1024]{2,1,0:T(8,128)(2,1)S(1)}, bf16[2,64,1024]{2,1,0:T(8,128)(2,1)S(1)}, u32[]{:S(2)}, u32[]{:S(2)}) collective-permute-start(bf16[2,64,1024]{2,1,0:T(8,128)(2,1)S(1)} %pad_maximum_fusion.20), channel_id=1, source_target_pairs={{0,6},{2,4},{4,2},{6,0},{8,14},{10,12},{12,10},{14,8},{1,7},{3,5},... | collective-permute-start | bytes 786440 | tf_op jit(solution)/shard_map/ppermute | solution.py:206
  123.5 16.0 %shard_map.144 = (bf16[1024,1536]{1,0:T(8,128)(2,1)S(1)}, bf16[1024,1536]{1,0:T(8,128)(2,1)S(1)}, bf16[1024,1536]{1,0:T(8,128)(2,1)}, bf16[1024,1024]{1,0:T(8,128)(2,1)S(1)}) custom-call(bf16[1024,1024]{1,0:T(8,128)(2,1)S(1)} %bitcast.210, f32[2,1024,2]{2,1,0:T(8,128)S(1)} %bitcast.214, bf16[4,1024,384]{2,1,0:T(8,128)(2,1)} %wg_ref.3, ...), custom_call_target="tpu_custom_call" | custom-call | flops 9663676416 | bytes 23068672 | tf_op jit(solution)/shard_map/pallas_call | solution.py:391
  141.2 2.8 %collective-permute-start.40 = (bf16[256,512]{1,0:T(8,128)(2,1)S(1)}, bf16[256,512]{1,0:T(8,128)(2,1)S(1)}, u32[]{:S(2)}, u32[]{:S(2)}) collective-permute-start(bf16[256,512]{1,0:T(8,128)(2,1)S(1)} %copy-done.9), channel_id=1, source_target_pairs={{0,8},{2,10},{4,12},{6,14},{8,0},{10,2},{12,4},{14,6},{1,9},{3,11}... | collective-permute-start | bytes 786440 | tf_op jit(solution)/shard_map/ppermute | solution.py:215
  144.2 5.0 %shard_map.145 = bf16[1536,1024]{1,0:T(8,128)(2,1)} custom-call(bf16[1024,1536]{1,0:T(8,128)(2,1)S(1)} %get-tuple-element.89.hs_ref, bf16[1024,1024]{1,0:T(8,128)(2,1)S(1)} %bitcast.212), custom_call_target="tpu_custom_call" | custom-call | flops 3221225472 | bytes 8388608 | tf_op jit(solution)/shard_map/pallas_call | solution.py:401
  150.7 2.5 collective-permute-start.38
  153.3 15.6 %shard_map.146 = (bf16[1024,3072]{1,0:T(8,128)(2,1)}, bf16[1024,1024]{1,0:T(8,128)(2,1)S(1)}) custom-call(bf16[1024,1024]{1,0:T(8,128)(2,1)S(1)} %bitcast.213, bf16[1024,1536]{1,0:T(8,128)(2,1)S(1)} %get-tuple-element.98.cp_ref, bf16[1024,1536]{1,0:T(8,128)(2,1)S(1)} %copy-done.2, bf16[4,1024,384]{2,1,0:T(8,128)(2,1)S(1)} %copy-done, ...), custom_call_target="tpu_custom_call" | custom-call | flops 9663676416 | bytes 26214400 | tf_op jit(solution)/shard_map/pallas_call | solution.py:403
  174.3 2.1 collective-permute-start.44
  176.5 9.0 %shard_map.147 = (bf16[4,1024,384]{2,1,0:T(8,128)(2,1)}, bf16[4,1024,384]{2,1,0:T(8,128)(2,1)}) custom-call(bf16[1024,1024]{1,0:T(8,128)(2,1)S(1)} %bitcast.211, bf16[1024,3072]{1,0:T(8,128)(2,1)S(1)} %copy-done.1), custom_call_target="tpu_custom_call" | custom-call | flops 6442450944 | bytes 14680064 | tf_op jit(solution)/shard_map/pallas_call | solution.py:414
  185.5 2.9 %collective-permute-done.43 = bf16[2,64,1024]{2,1,0:T(8,128)(2,1)S(1)} collective-permute-done((bf16[2,64,1024]{2,1,0:T(8,128)(2,1)S(1)}, bf16[2,64,1024]{2,1,0:T(8,128)(2,1)S(1)}, u32[]{:S(2)}, u32[]{:S(2)}) %collective-permute-start.43) | collective-permute-done | bytes 262176 | tf_op jit(solution)/shard_map/ppermute | solution.py:206
  188.4 5.2 %collective-permute-done.44 = bf16[2,64,1024]{2,1,0:T(8,128)(2,1)S(1)} collective-permute-done((bf16[2,64,1024]{2,1,0:T(8,128)(2,1)S(1)}, bf16[2,64,1024]{2,1,0:T(8,128)(2,1)S(1)}, u32[]{:S(2)}, u32[]{:S(2)}) %collective-permute-start.44) | collective-permute-done | bytes 262176 | tf_op jit(solution)/shard_map/ppermute | solution.py:206
  197.6 2.7 %collective-permute-done.47 = bf16[64,1536]{1,0:T(8,128)(2,1)S(1)} collective-permute-done((bf16[64,1536]{1,0:T(8,128)(2,1)S(1)}, bf16[64,1536]{1,0:T(8,128)(2,1)S(1)}, u32[]{:S(2)}, u32[]{:S(2)}) %collective-permute-start.47) | collective-permute-done | bytes 196640 | tf_op jit(solution)/shard_map/ppermute | solution.py:206
  200.3 7.8 %collective-permute-done.48 = bf16[64,1536]{1,0:T(8,128)(2,1)S(1)} collective-permute-done((bf16[64,1536]{1,0:T(8,128)(2,1)S(1)}, bf16[64,1536]{1,0:T(8,128)(2,1)S(1)}, u32[]{:S(2)}, u32[]{:S(2)}) %collective-permute-start.48) | collective-permute-done | bytes 196640 | tf_op jit(solution)/shard_map/ppermute | solution.py:206
  208.1 2.8 %collective-permute-done.49 = bf16[64,1536]{1,0:T(8,128)(2,1)S(1)} collective-permute-done((bf16[64,1536]{1,0:T(8,128)(2,1)S(1)}, bf16[64,1536]{1,0:T(8,128)(2,1)S(1)}, u32[]{:S(2)}, u32[]{:S(2)}) %collective-permute-start.49) | collective-permute-done | bytes 196640 | tf_op jit(solution)/shard_map/ppermute | solution.py:206
  212.7 2.7 %collective-permute-start.60 = (bf16[64,1536]{1,0:T(8,128)(2,1)}, bf16[64,1536]{1,0:T(8,128)(2,1)S(1)}, u32[]{:S(2)}, u32[]{:S(2)}) collective-permute-start(bf16[64,1536]{1,0:T(8,128)(2,1)} %get-tuple-element.233), channel_id=1, source_target_pairs={{0,6},{2,4},{4,2},{6,0},{8,14},{10,12},{12,10},{14,8},{1,7},{3,5},... | collective-permute-start | bytes 589832 | tf_op jit(solution)/shard_map/ppermute | solution.py:206
  215.5 4.0 %collective-permute-done.58 = bf16[64,1536]{1,0:T(8,128)(2,1)S(1)} collective-permute-done((bf16[64,1536]{1,0:T(8,128)(2,1)}, bf16[64,1536]{1,0:T(8,128)(2,1)S(1)}, u32[]{:S(2)}, u32[]{:S(2)}) %collective-permute-start.58) | collective-permute-done | bytes 196640 | tf_op jit(solution)/shard_map/ppermute | solution.py:206
  220.7 4.2 %collective-permute-done.60 = bf16[64,1536]{1,0:T(8,128)(2,1)S(1)} collective-permute-done((bf16[64,1536]{1,0:T(8,128)(2,1)}, bf16[64,1536]{1,0:T(8,128)(2,1)S(1)}, u32[]{:S(2)}, u32[]{:S(2)}) %collective-permute-start.60) | collective-permute-done | bytes 196640 | tf_op jit(solution)/shard_map/ppermute | solution.py:206
  225.1 1.6 maximum_select_fusion
  226.8 1.6 fusion.15
  230.1 2.4 collective-permute-start.57
  238.6 2.5 collective-permute-start.54
  242.8 2.4 collective-permute-start.67
  246.7 2.5 collective-permute-start.63
  249.6 1.9 collective-permute-start.64
  254.3 1.5 collective-permute-done.64
  (295 shorter events, 58.2 us)
Async XLA Ops:
  1.9 11.4 %collective-permute-start = (bf16[128,1024]{1,0:T(8,128)(2,1)S(1)}, bf16[128,1024]{1,0:T(8,128)(2,1)S(1)}, u32[]{:S(2)}, u32[]{:S(2)}) collective-permute-start(bf16[128,1024]{1,0:T(8,128)(2,1)S(1)} %pad_maximum_fusion.16), channel_id=1, source_target_pairs={{0,2},{2,0},{4,6},{6,4},{8,10},{10,8},{12,14},{14,12},{1,3},{3,1},... | collective-permute-start | bytes 786440 | tf_op jit(solution)/shard_map/ppermute | solution.py:206
  5.0 12.4 %collective-permute-start.1 = (bf16[256,128]{1,0:T(8,128)(2,1)S(1)}, bf16[256,128]{1,0:T(8,128)(2,1)S(1)}, u32[]{:S(2)}, u32[]{:S(2)}) collective-permute-start(bf16[256,128]{1,0:T(8,128)(2,1)S(1)} %get-tuple-element.217), channel_id=1, source_target_pairs={{0,2},{2,0},{4,6},{6,4},{8,10},{10,8},{12,14},{14,12},{1,3},{3,1},... | collective-permute-start | bytes 196616 | tf_op jit(solution)/shard_map/ppermute | solution.py:206
  5.1 12.9 %collective-permute-start.2 = (bf16[256,128]{1,0:T(8,128)(2,1)S(1)}, bf16[256,128]{1,0:T(8,128)(2,1)S(1)}, u32[]{:S(2)}, u32[]{:S(2)}) collective-permute-start(bf16[256,128]{1,0:T(8,128)(2,1)S(1)} %get-tuple-element.216), channel_id=1, source_target_pairs={{0,4},{2,6},{4,0},{6,2},{8,12},{10,14},{12,8},{14,10},{1,5},{3,7},... | collective-permute-start | bytes 196616 | tf_op jit(solution)/shard_map/ppermute | solution.py:206
  7.1 10.9 %collective-permute-start.3 = (bf16[256,128]{1,0:T(8,128)(2,1)S(1)}, bf16[256,128]{1,0:T(8,128)(2,1)S(1)}, u32[]{:S(2)}, u32[]{:S(2)}) collective-permute-start(bf16[256,128]{1,0:T(8,128)(2,1)S(1)} %get-tuple-element.215), channel_id=1, source_target_pairs={{0,6},{2,4},{4,2},{6,0},{8,14},{10,12},{12,10},{14,8},{1,7},{3,5},... | collective-permute-start | bytes 196616 | tf_op jit(solution)/shard_map/ppermute | solution.py:206
  13.5 28.5 %collective-permute-start.10 = (bf16[256,512]{1,0:T(8,128)(2,1)S(1)}, bf16[256,512]{1,0:T(8,128)(2,1)S(1)}, u32[]{:S(2)}, u32[]{:S(2)}) collective-permute-start(bf16[256,512]{1,0:T(8,128)(2,1)S(1)} %get-tuple-element.206), channel_id=1, source_target_pairs={{0,12},{2,14},{4,8},{6,10},{8,4},{10,6},{12,0},{14,2},{1,13},{3,15... | collective-permute-start | bytes 786440 | tf_op jit(solution)/shard_map/ppermute | solution.py:257
  17.4 24.6 %collective-permute-start.8 = (bf16[256,512]{1,0:T(8,128)(2,1)S(1)}, bf16[256,512]{1,0:T(8,128)(2,1)S(1)}, u32[]{:S(2)}, u32[]{:S(2)}) collective-permute-start(bf16[256,512]{1,0:T(8,128)(2,1)S(1)} %get-tuple-element.206), channel_id=1, source_target_pairs={{0,4},{2,6},{4,0},{6,2},{8,12},{10,14},{12,8},{14,10},{1,5},{3,7},... | collective-permute-start | bytes 786440 | tf_op jit(solution)/shard_map/ppermute | solution.py:206
  17.4 24.6 %collective-permute-start.9 = (bf16[256,512]{1,0:T(8,128)(2,1)S(1)}, bf16[256,512]{1,0:T(8,128)(2,1)S(1)}, u32[]{:S(2)}, u32[]{:S(2)}) collective-permute-start(bf16[256,512]{1,0:T(8,128)(2,1)S(1)} %get-tuple-element.205), channel_id=1, source_target_pairs={{0,8},{2,10},{4,12},{6,14},{8,0},{10,2},{12,4},{14,6},{1,9},{3,11}... | collective-permute-start | bytes 786440 | tf_op jit(solution)/shard_map/ppermute | solution.py:257
  20.4 21.5 %collective-permute-start.7 = (bf16[128,1024]{1,0:T(8,128)(2,1)S(1)}, bf16[128,1024]{1,0:T(8,128)(2,1)S(1)}, u32[]{:S(2)}, u32[]{:S(2)}) collective-permute-start(bf16[128,1024]{1,0:T(8,128)(2,1)S(1)} %pad_maximum_fusion.17), channel_id=1, source_target_pairs={{0,2},{2,0},{4,6},{6,4},{8,10},{10,8},{12,14},{14,12},{1,3},{3,1},... | collective-permute-start | bytes 786440 | tf_op jit(solution)/shard_map/ppermute | solution.py:206
  23.8 10.3 %collective-permute-start.5 = (bf16[256,128]{1,0:T(8,128)(2,1)S(1)}, bf16[256,128]{1,0:T(8,128)(2,1)S(1)}, u32[]{:S(2)}, u32[]{:S(2)}) collective-permute-start(bf16[256,128]{1,0:T(8,128)(2,1)S(1)} %get-tuple-element.212), channel_id=1, source_target_pairs={{0,4},{2,6},{4,0},{6,2},{8,12},{10,14},{12,8},{14,10},{1,5},{3,7},... | collective-permute-start | bytes 196616 | tf_op jit(solution)/shard_map/ppermute | solution.py:206
  51.0 26.2 %collective-permute-start.19 = (bf16[256,512]{1,0:T(8,128)(2,1)S(1)}, bf16[256,512]{1,0:T(8,128)(2,1)S(1)}, u32[]{:S(2)}, u32[]{:S(2)}) collective-permute-start(bf16[256,512]{1,0:T(8,128)(2,1)S(1)} %get-tuple-element.197), channel_id=1, source_target_pairs={{0,8},{2,10},{4,12},{6,14},{8,0},{10,2},{12,4},{14,6},{1,9},{3,11}... | collective-permute-start | bytes 786440 | tf_op jit(solution)/shard_map/ppermute | solution.py:257
  51.1 26.1 %collective-permute-start.20 = (bf16[256,512]{1,0:T(8,128)(2,1)S(1)}, bf16[256,512]{1,0:T(8,128)(2,1)S(1)}, u32[]{:S(2)}, u32[]{:S(2)}) collective-permute-start(bf16[256,512]{1,0:T(8,128)(2,1)S(1)} %get-tuple-element.76), channel_id=1, source_target_pairs={{0,12},{2,14},{4,8},{6,10},{8,4},{10,6},{12,0},{14,2},{1,13},{3,15... | collective-permute-start | bytes 786440 | tf_op jit(solution)/shard_map/ppermute | solution.py:257
  54.6 16.9 %collective-permute-start.14 = (bf16[2,64,512]{2,1,0:T(8,128)(2,1)S(1)}, bf16[2,64,512]{2,1,0:T(8,128)(2,1)S(1)}, u32[]{:S(2)}, u32[]{:S(2)}) collective-permute-start(bf16[2,64,512]{2,1,0:T(8,128)(2,1)S(1)} %get-tuple-element.204), channel_id=1, source_target_pairs={{0,4},{2,6},{4,0},{6,2},{8,12},{10,14},{12,8},{14,10},{1,5},{3,7},... | collective-permute-start | bytes 393224 | tf_op jit(solution)/shard_map/ppermute | solution.py:206
  54.9 17.8 %collective-permute-start.15 = (bf16[2,64,512]{2,1,0:T(8,128)(2,1)S(1)}, bf16[2,64,512]{2,1,0:T(8,128)(2,1)S(1)}, u32[]{:S(2)}, u32[]{:S(2)}) collective-permute-start(bf16[2,64,512]{2,1,0:T(8,128)(2,1)S(1)} %get-tuple-element.203), channel_id=1, source_target_pairs={{0,6},{2,4},{4,2},{6,0},{8,14},{10,12},{12,10},{14,8},{1,7},{3,5},... | collective-permute-start | bytes 393224 | tf_op jit(solution)/shard_map/ppermute | solution.py:206
  72.9 9.5 %collective-permute-start.17 = (bf16[256,512]{1,0:T(8,128)(2,1)S(1)}, bf16[256,512]{1,0:T(8,128)(2,1)S(1)}, u32[]{:S(2)}, u32[]{:S(2)}) collective-permute-start(bf16[256,512]{1,0:T(8,128)(2,1)S(1)} %pad_maximum_fusion.19), channel_id=1, source_target_pairs={{0,16},{16,0},{1,17},{17,1},{2,18},{18,2},{3,19},{19,3},{4,20},{20... | collective-permute-start | bytes 786440 | tf_op jit(solution)/shard_map/ppermute | solution.py:212
  74.6 9.5 %collective-permute-start.16 = (bf16[256,512]{1,0:T(8,128)(2,1)S(1)}, bf16[256,512]{1,0:T(8,128)(2,1)S(1)}, u32[]{:S(2)}, u32[]{:S(2)}) collective-permute-start(bf16[256,512]{1,0:T(8,128)(2,1)S(1)} %get-tuple-element.76), channel_id=1, source_target_pairs={{0,4},{2,6},{4,0},{6,2},{8,12},{10,14},{12,8},{14,10},{1,5},{3,7},... | collective-permute-start | bytes 786440 | tf_op jit(solution)/shard_map/ppermute | solution.py:206
  89.0 21.3 %collective-permute-start.29 = (bf16[2,64,1024]{2,1,0:T(8,128)(2,1)S(1)}, bf16[2,64,1024]{2,1,0:T(8,128)(2,1)S(1)}, u32[]{:S(2)}, u32[]{:S(2)}) collective-permute-start(bf16[2,64,1024]{2,1,0:T(8,128)(2,1)S(1)} %get-tuple-element.219), channel_id=1, source_target_pairs={{0,2},{2,0},{4,6},{6,4},{8,10},{10,8},{12,14},{14,12},{1,3},{3,1},... | collective-permute-start | bytes 786440 | tf_op jit(solution)/shard_map/ppermute | solution.py:206
  90.0 20.4 %collective-permute-start.30 = (bf16[2,64,1024]{2,1,0:T(8,128)(2,1)S(1)}, bf16[2,64,1024]{2,1,0:T(8,128)(2,1)S(1)}, u32[]{:S(2)}, u32[]{:S(2)}) collective-permute-start(bf16[2,64,1024]{2,1,0:T(8,128)(2,1)S(1)} %get-tuple-element.219), channel_id=1, source_target_pairs={{0,4},{2,6},{4,0},{6,2},{8,12},{10,14},{12,8},{14,10},{1,5},{3,7},... | collective-permute-start | bytes 786440 | tf_op jit(solution)/shard_map/ppermute | solution.py:206
  90.0 20.4 %collective-permute-start.31 = (bf16[2,64,1024]{2,1,0:T(8,128)(2,1)S(1)}, bf16[2,64,1024]{2,1,0:T(8,128)(2,1)S(1)}, u32[]{:S(2)}, u32[]{:S(2)}) collective-permute-start(bf16[2,64,1024]{2,1,0:T(8,128)(2,1)S(1)} %get-tuple-element.219), channel_id=1, source_target_pairs={{0,6},{2,4},{4,2},{6,0},{8,14},{10,12},{12,10},{14,8},{1,7},{3,5},... | collective-permute-start | bytes 786440 | tf_op jit(solution)/shard_map/ppermute | solution.py:206
  92.6 15.1 %collective-permute-start.23 = (bf16[2,64,512]{2,1,0:T(8,128)(2,1)}, bf16[2,64,512]{2,1,0:T(8,128)(2,1)S(1)}, u32[]{:S(2)}, u32[]{:S(2)}) collective-permute-start(bf16[2,64,512]{2,1,0:T(8,128)(2,1)} %get-tuple-element.195), channel_id=1, source_target_pairs={{0,4},{2,6},{4,0},{6,2},{8,12},{10,14},{12,8},{14,10},{1,5},{3,7},... | collective-permute-start | bytes 393224 | tf_op jit(solution)/shard_map/ppermute | solution.py:206
  94.2 15.5 %collective-permute-start.24 = (bf16[2,64,512]{2,1,0:T(8,128)(2,1)S(1)}, bf16[2,64,512]{2,1,0:T(8,128)(2,1)S(1)}, u32[]{:S(2)}, u32[]{:S(2)}) collective-permute-start(bf16[2,64,512]{2,1,0:T(8,128)(2,1)S(1)} %get-tuple-element.194), channel_id=1, source_target_pairs={{0,6},{2,4},{4,2},{6,0},{8,14},{10,12},{12,10},{14,8},{1,7},{3,5},... | collective-permute-start | bytes 393224 | tf_op jit(solution)/shard_map/ppermute | solution.py:206
  118.2 21.3 %collective-permute-start.26 = (bf16[2,64,1024]{2,1,0:T(8,128)(2,1)S(1)}, bf16[2,64,1024]{2,1,0:T(8,128)(2,1)S(1)}, u32[]{:S(2)}, u32[]{:S(2)}) collective-permute-start(bf16[2,64,1024]{2,1,0:T(8,128)(2,1)S(1)} %pad_maximum_fusion.20), channel_id=1, source_target_pairs={{0,2},{2,0},{4,6},{6,4},{8,10},{10,8},{12,14},{14,12},{1,3},{3,1},... | collective-permute-start | bytes 786440 | tf_op jit(solution)/shard_map/ppermute | solution.py:206
  119.1 20.4 %collective-permute-start.27 = (bf16[2,64,1024]{2,1,0:T(8,128)(2,1)S(1)}, bf16[2,64,1024]{2,1,0:T(8,128)(2,1)S(1)}, u32[]{:S(2)}, u32[]{:S(2)}) collective-permute-start(bf16[2,64,1024]{2,1,0:T(8,128)(2,1)S(1)} %pad_maximum_fusion.20), channel_id=1, source_target_pairs={{0,4},{2,6},{4,0},{6,2},{8,12},{10,14},{12,8},{14,10},{1,5},{3,7},... | collective-permute-start | bytes 786440 | tf_op jit(solution)/shard_map/ppermute | solution.py:206
  119.1 20.4 %collective-permute-start.28 = (bf16[2,64,1024]{2,1,0:T(8,128)(2,1)S(1)}, bf16[2,64,1024]{2,1,0:T(8,128)(2,1)S(1)}, u32[]{:S(2)}, u32[]{:S(2)}) collective-permute-start(bf16[2,64,1024]{2,1,0:T(8,128)(2,1)S(1)} %pad_maximum_fusion.20), channel_id=1, source_target_pairs={{0,6},{2,4},{4,2},{6,0},{8,14},{10,12},{12,10},{14,8},{1,7},{3,5},... | collective-permute-start | bytes 786440 | tf_op jit(solution)/shard_map/ppermute | solution.py:206
  121.8 17.8 %collective-permute-start.32 = (bf16[256,512]{1,0:T(8,128)(2,1)}, bf16[256,512]{1,0:T(8,128)(2,1)}, u32[]{:S(2)}, u32[]{:S(2)}) collective-permute-start(bf16[256,512]{1,0:T(8,128)(2,1)} %copy-done.10), channel_id=1, source_target_pairs={{0,8},{2,10},{4,12},{6,14},{8,0},{10,2},{12,4},{14,6},{1,9},{3,11}... | collective-permute-start | bytes 786440 | tf_op jit(solution)/shard_map/ppermute | solution.py:215
  140.0 9.2 %collective-permute-start.34 = (bf16[4,2,64,1024]{3,2,1,0:T(8,128)(2,1)S(1)}, bf16[4,2,64,1024]{3,2,1,0:T(8,128)(2,1)S(1)}, u32[]{:S(2)}, u32[]{:S(2)}) collective-permute-start(bf16[4,2,64,1024]{3,2,1,0:T(8,128)(2,1)S(1)} %bitcast.227), channel_id=1, source_target_pairs={{0,1},{1,0},{2,3},{3,2},{4,5},{5,4},{6,7},{7,6},{8,9},{9,8},{10,11... | collective-permute-start | bytes 3145736 | tf_op jit(solution)/shard_map/ppermute | solution.py:209
  140.6 28.4 %collective-permute-start.39 = (bf16[256,512]{1,0:T(8,128)(2,1)}, bf16[256,512]{1,0:T(8,128)(2,1)S(1)}, u32[]{:S(2)}, u32[]{:S(2)}) collective-permute-start(bf16[256,512]{1,0:T(8,128)(2,1)} %collective-permute-done.32), channel_id=1, source_target_pairs={{0,16},{16,0},{1,17},{17,1},{2,18},{18,2},{3,19},{19,3},{4,20},{20... | collective-permute-start | bytes 786440 | tf_op jit(solution)/shard_map/ppermute | solution.py:212
  141.2 27.7 %collective-permute-start.40 = (bf16[256,512]{1,0:T(8,128)(2,1)S(1)}, bf16[256,512]{1,0:T(8,128)(2,1)S(1)}, u32[]{:S(2)}, u32[]{:S(2)}) collective-permute-start(bf16[256,512]{1,0:T(8,128)(2,1)S(1)} %copy-done.9), channel_id=1, source_target_pairs={{0,8},{2,10},{4,12},{6,14},{8,0},{10,2},{12,4},{14,6},{1,9},{3,11}... | collective-permute-start | bytes 786440 | tf_op jit(solution)/shard_map/ppermute | solution.py:215
  149.7 19.2 %collective-permute-start.36 = (bf16[2,64,1024]{2,1,0:T(8,128)(2,1)S(1)}, bf16[2,64,1024]{2,1,0:T(8,128)(2,1)S(1)}, u32[]{:S(2)}, u32[]{:S(2)}) collective-permute-start(bf16[2,64,1024]{2,1,0:T(8,128)(2,1)S(1)} %get-tuple-element.143), channel_id=1, source_target_pairs={{0,2},{2,0},{4,6},{6,4},{8,10},{10,8},{12,14},{14,12},{1,3},{3,1},... | collective-permute-start | bytes 786440 | tf_op jit(solution)/shard_map/ppermute | solution.py:206
  150.5 18.4 %collective-permute-start.37 = (bf16[2,64,1024]{2,1,0:T(8,128)(2,1)S(1)}, bf16[2,64,1024]{2,1,0:T(8,128)(2,1)S(1)}, u32[]{:S(2)}, u32[]{:S(2)}) collective-permute-start(bf16[2,64,1024]{2,1,0:T(8,128)(2,1)S(1)} %get-tuple-element.142), channel_id=1, source_target_pairs={{0,4},{2,6},{4,0},{6,2},{8,12},{10,14},{12,8},{14,10},{1,5},{3,7},... | collective-permute-start | bytes 786440 | tf_op jit(solution)/shard_map/ppermute | solution.py:206
  150.7 18.2 %collective-permute-start.38 = (bf16[2,64,1024]{2,1,0:T(8,128)(2,1)S(1)}, bf16[2,64,1024]{2,1,0:T(8,128)(2,1)S(1)}, u32[]{:S(2)}, u32[]{:S(2)}) collective-permute-start(bf16[2,64,1024]{2,1,0:T(8,128)(2,1)S(1)} %get-tuple-element.141), channel_id=1, source_target_pairs={{0,6},{2,4},{4,2},{6,0},{8,14},{10,12},{12,10},{14,8},{1,7},{3,5},... | collective-permute-start | bytes 786440 | tf_op jit(solution)/shard_map/ppermute | solution.py:206
  169.7 15.8 %collective-permute-start.45 = (bf16[2,64,1024]{2,1,0:T(8,128)(2,1)S(1)}, bf16[2,64,1024]{2,1,0:T(8,128)(2,1)S(1)}, u32[]{:S(2)}, u32[]{:S(2)}) collective-permute-start(bf16[2,64,1024]{2,1,0:T(8,128)(2,1)S(1)} %add_convert_fusion.1), channel_id=1, source_target_pairs={{0,8},{2,10},{4,12},{6,14},{8,0},{10,2},{12,4},{14,6},{1,9},{3,11}... | collective-permute-start | bytes 786440 | tf_op jit(solution)/shard_map/ppermute | solution.py:215
  170.8 14.7 %collective-permute-start.46 = (bf16[256,512]{1,0:T(8,128)(2,1)S(1)}, bf16[256,512]{1,0:T(8,128)(2,1)S(1)}, u32[]{:S(2)}, u32[]{:S(2)}) collective-permute-start(bf16[256,512]{1,0:T(8,128)(2,1)S(1)} %collective-permute-done.40), channel_id=1, source_target_pairs={{0,16},{16,0},{1,17},{17,1},{2,18},{18,2},{3,19},{19,3},{4,20},{20... | collective-permute-start | bytes 786440 | tf_op jit(solution)/shard_map/ppermute | solution.py:212
  172.9 12.6 %collective-permute-start.42 = (bf16[2,64,1024]{2,1,0:T(8,128)(2,1)S(1)}, bf16[2,64,1024]{2,1,0:T(8,128)(2,1)S(1)}, u32[]{:S(2)}, u32[]{:S(2)}) collective-permute-start(bf16[2,64,1024]{2,1,0:T(8,128)(2,1)S(1)} %get-tuple-element.139), channel_id=1, source_target_pairs={{0,2},{2,0},{4,6},{6,4},{8,10},{10,8},{12,14},{14,12},{1,3},{3,1},... | collective-permute-start | bytes 786440 | tf_op jit(solution)/shard_map/ppermute | solution.py:206
  173.7 14.7 %collective-permute-start.43 = (bf16[2,64,1024]{2,1,0:T(8,128)(2,1)S(1)}, bf16[2,64,1024]{2,1,0:T(8,128)(2,1)S(1)}, u32[]{:S(2)}, u32[]{:S(2)}) collective-permute-start(bf16[2,64,1024]{2,1,0:T(8,128)(2,1)S(1)} %get-tuple-element.138), channel_id=1, source_target_pairs={{0,4},{2,6},{4,0},{6,2},{8,12},{10,14},{12,8},{14,10},{1,5},{3,7},... | collective-permute-start | bytes 786440 | tf_op jit(solution)/shard_map/ppermute | solution.py:206
  174.3 19.3 %collective-permute-start.44 = (bf16[2,64,1024]{2,1,0:T(8,128)(2,1)S(1)}, bf16[2,64,1024]{2,1,0:T(8,128)(2,1)S(1)}, u32[]{:S(2)}, u32[]{:S(2)}) collective-permute-start(bf16[2,64,1024]{2,1,0:T(8,128)(2,1)S(1)} %get-tuple-element.137), channel_id=1, source_target_pairs={{0,6},{2,4},{4,2},{6,0},{8,14},{10,12},{12,10},{14,8},{1,7},{3,5},... | collective-permute-start | bytes 786440 | tf_op jit(solution)/shard_map/ppermute | solution.py:206
  193.9 17.0 %collective-permute-start.50 = (bf16[2,64,1024]{2,1,0:T(8,128)(2,1)S(1)}, bf16[2,64,1024]{2,1,0:T(8,128)(2,1)S(1)}, u32[]{:S(2)}, u32[]{:S(2)}) collective-permute-start(bf16[2,64,1024]{2,1,0:T(8,128)(2,1)S(1)} %add_convert_fusion), channel_id=1, source_target_pairs={{0,8},{2,10},{4,12},{6,14},{8,0},{10,2},{12,4},{14,6},{1,9},{3,11}... | collective-permute-start | bytes 786440 | tf_op jit(solution)/shard_map/ppermute | solution.py:215
  194.9 13.2 %collective-permute-start.48 = (bf16[64,1536]{1,0:T(8,128)(2,1)S(1)}, bf16[64,1536]{1,0:T(8,128)(2,1)S(1)}, u32[]{:S(2)}, u32[]{:S(2)}) collective-permute-start(bf16[64,1536]{1,0:T(8,128)(2,1)S(1)} %pad_maximum_fusion.22), channel_id=1, source_target_pairs={{0,4},{2,6},{4,0},{6,2},{8,12},{10,14},{12,8},{14,10},{1,5},{3,7},... | collective-permute-start | bytes 589832 | tf_op jit(solution)/shard_map/ppermute | solution.py:206
  196.3 14.6 %collective-permute-start.49 = (bf16[64,1536]{1,0:T(8,128)(2,1)S(1)}, bf16[64,1536]{1,0:T(8,128)(2,1)S(1)}, u32[]{:S(2)}, u32[]{:S(2)}) collective-permute-start(bf16[64,1536]{1,0:T(8,128)(2,1)S(1)} %pad_maximum_fusion.22), channel_id=1, source_target_pairs={{0,6},{2,4},{4,2},{6,0},{8,14},{10,12},{12,10},{14,8},{1,7},{3,5},... | collective-permute-start | bytes 589832 | tf_op jit(solution)/shard_map/ppermute | solution.py:206
  211.2 13.9 %collective-permute-start.51 = (bf16[4,64,1536]{2,1,0:T(8,128)(2,1)S(1)}, bf16[4,64,1536]{2,1,0:T(8,128)(2,1)}, u32[]{:S(2)}, u32[]{:S(2)}) collective-permute-start(bf16[4,64,1536]{2,1,0:T(8,128)(2,1)S(1)} %get-tuple-element.162), channel_id=1, source_target_pairs={{0,1},{1,0},{2,3},{3,2},{4,5},{5,4},{6,7},{7,6},{8,9},{9,8},{10,11... | collective-permute-start | bytes 2359304 | tf_op jit(solution)/shard_map/ppermute | solution.py:209
  212.7 12.1 %collective-permute-start.60 = (bf16[64,1536]{1,0:T(8,128)(2,1)}, bf16[64,1536]{1,0:T(8,128)(2,1)S(1)}, u32[]{:S(2)}, u32[]{:S(2)}) collective-permute-start(bf16[64,1536]{1,0:T(8,128)(2,1)} %get-tuple-element.233), channel_id=1, source_target_pairs={{0,6},{2,4},{4,2},{6,0},{8,14},{10,12},{12,10},{14,8},{1,7},{3,5},... | collective-permute-start | bytes 589832 | tf_op jit(solution)/shard_map/ppermute | solution.py:206
  225.0 9.4 %collective-permute-start.61 = (bf16[4,64,1536]{2,1,0:T(8,128)(2,1)S(1)}, bf16[4,64,1536]{2,1,0:T(8,128)(2,1)S(1)}, u32[]{:S(2)}, u32[]{:S(2)}) collective-permute-start(bf16[4,64,1536]{2,1,0:T(8,128)(2,1)S(1)} %get-tuple-element.160), channel_id=1, source_target_pairs={{0,1},{1,0},{2,3},{3,2},{4,5},{5,4},{6,7},{7,6},{8,9},{9,8},{10,11... | collective-permute-start | bytes 2359304 | tf_op jit(solution)/shard_map/ppermute | solution.py:209
  229.0 9.6 %collective-permute-start.55 = (bf16[128,512]{1,0:T(8,128)(2,1)S(1)}, bf16[128,512]{1,0:T(8,128)(2,1)S(1)}, u32[]{:S(2)}, u32[]{:S(2)}) collective-permute-start(bf16[128,512]{1,0:T(8,128)(2,1)S(1)} %get-tuple-element.185), channel_id=1, source_target_pairs={{0,2},{2,0},{4,6},{6,4},{8,10},{10,8},{12,14},{14,12},{1,3},{3,1},... | collective-permute-start | bytes 393224 | tf_op jit(solution)/shard_map/ppermute | solution.py:206
  229.8 11.8 %collective-permute-start.56 = (bf16[128,512]{1,0:T(8,128)(2,1)S(1)}, bf16[128,512]{1,0:T(8,128)(2,1)S(1)}, u32[]{:S(2)}, u32[]{:S(2)}) collective-permute-start(bf16[128,512]{1,0:T(8,128)(2,1)S(1)} %get-tuple-element.184), channel_id=1, source_target_pairs={{0,4},{2,6},{4,0},{6,2},{8,12},{10,14},{12,8},{14,10},{1,5},{3,7},... | collective-permute-start | bytes 393224 | tf_op jit(solution)/shard_map/ppermute | solution.py:206
  230.1 12.3 %collective-permute-start.57 = (bf16[128,512]{1,0:T(8,128)(2,1)S(1)}, bf16[128,512]{1,0:T(8,128)(2,1)S(1)}, u32[]{:S(2)}, u32[]{:S(2)}) collective-permute-start(bf16[128,512]{1,0:T(8,128)(2,1)S(1)} %get-tuple-element.183), channel_id=1, source_target_pairs={{0,6},{2,4},{4,2},{6,0},{8,14},{10,12},{12,10},{14,8},{1,7},{3,5},... | collective-permute-start | bytes 393224 | tf_op jit(solution)/shard_map/ppermute | solution.py:206
  233.6 9.2 %collective-permute-start.52 = (bf16[512,128]{1,0:T(8,128)(2,1)S(1)}, bf16[512,128]{1,0:T(8,128)(2,1)S(1)}, u32[]{:S(2)}, u32[]{:S(2)}) collective-permute-start(bf16[512,128]{1,0:T(8,128)(2,1)S(1)} %get-tuple-element.189), channel_id=1, source_target_pairs={{0,2},{2,0},{4,6},{6,4},{8,10},{10,8},{12,14},{14,12},{1,3},{3,1},... | collective-permute-start | bytes 393224 | tf_op jit(solution)/shard_map/ppermute | solution.py:206
  234.5 10.8 %collective-permute-start.53 = (bf16[512,128]{1,0:T(8,128)(2,1)S(1)}, bf16[512,128]{1,0:T(8,128)(2,1)S(1)}, u32[]{:S(2)}, u32[]{:S(2)}) collective-permute-start(bf16[512,128]{1,0:T(8,128)(2,1)S(1)} %get-tuple-element.188), channel_id=1, source_target_pairs={{0,4},{2,6},{4,0},{6,2},{8,12},{10,14},{12,8},{14,10},{1,5},{3,7},... | collective-permute-start | bytes 393224 | tf_op jit(solution)/shard_map/ppermute | solution.py:206
  242.5 9.0 %collective-permute-start.66 = (bf16[512,128]{1,0:T(8,128)(2,1)S(1)}, bf16[512,128]{1,0:T(8,128)(2,1)S(1)}, u32[]{:S(2)}, u32[]{:S(2)}) collective-permute-start(bf16[512,128]{1,0:T(8,128)(2,1)S(1)} %get-tuple-element.173), channel_id=1, source_target_pairs={{0,4},{2,6},{4,0},{6,2},{8,12},{10,14},{12,8},{14,10},{1,5},{3,7},... | collective-permute-start | bytes 393224 | tf_op jit(solution)/shard_map/ppermute | solution.py:206
  245.2 9.1 %collective-permute-start.62 = (bf16[128,512]{1,0:T(8,128)(2,1)S(1)}, bf16[128,512]{1,0:T(8,128)(2,1)S(1)}, u32[]{:S(2)}, u32[]{:S(2)}) collective-permute-start(bf16[128,512]{1,0:T(8,128)(2,1)S(1)} %get-tuple-element.174), channel_id=1, source_target_pairs={{0,2},{2,0},{4,6},{6,4},{8,10},{10,8},{12,14},{14,12},{1,3},{3,1},... | collective-permute-start | bytes 393224 | tf_op jit(solution)/shard_map/ppermute | solution.py:206
  (72 other events, 596.5 us)

commit v10 on v9

--- a/solution.py
+++ b/solution.py
@@ -264,12 +264,13 @@
 
         return quarters(q % 2), to_peer(quarters(1 - q % 2), 1)
 
-    def spread_rows(mine, theirs):
+    def by_half(mine, theirs):
         v = jnp.concatenate([mine, theirs], axis=0)
         mine = lax.dynamic_slice_in_dim(v, q // 2 * quarter_d, quarter_d, 1)
-        other = lax.dynamic_slice_in_dim(v, (1 - q // 2) * quarter_d, quarter_d, 1)
-        far = [(to_square(mine, k, 0), to_square(other, k, 2)) for k in range(1, nh)]
-        return (mine, other), far
+        return mine, lax.dynamic_slice_in_dim(v, (1 - q // 2) * quarter_d, quarter_d, 1)
+
+    def far_rows(mine, other):
+        return [(to_square(mine, k, 0), to_square(other, k, 2)) for k in range(1, nh)]
 
     def join_pairs(parts):
         return [jnp.concatenate(v, axis=0) for v in parts]
@@ -285,6 +286,24 @@
     def join_quarters(parts):
         return jnp.concatenate(by_quarter(parts), axis=1)
 
+    def first_weight(v):
+        size = quarter_d // 2 if shared else quarter_d
+        first = g * size if shared else 0
+
+        def half(i):
+            starts = [(2 * i + j) * quarter_d + first for j in (0, 1)]
+            return jnp.stack([lax.dynamic_slice_in_dim(v, at, size, 0) for at in starts])
+
+        return half(q // 2), to_peer(half(1 - q // 2), 2)
+
+    def second_weight(mine, theirs):
+        both = jnp.concatenate([mine, theirs], axis=2)
+        other = lax.dynamic_index_in_dim(both, 1 - q % 2, 0, keepdims=False)
+        return lax.dynamic_index_in_dim(both, q % 2, 0, keepdims=False), to_peer(other, 1)
+
+    def join_steps(mine, theirs):
+        return join_quarters([v[:, i * shard : (i + 1) * shard] for i in (0, 1) for v in (mine, theirs)])
+
     def swap_features(v):
         return g_swap(v) if shared else v
 
@@ -296,6 +315,12 @@
         part = jnp.stack(parts, axis=1)
         mine = lax.dynamic_index_in_dim(part, t, 2, keepdims=False)
         return mine, lax.dynamic_index_in_dim(part, 1 - t, 2, keepdims=False)
+
+    def project_square(rows, weights):
+        parts = [dot(rows, weight).astype(bf16) for weight in weights]
+        part = jnp.concatenate(parts, axis=1).reshape(4, 2, half_rows, latent)
+        mine = lax.dynamic_index_in_dim(part, t, 1, keepdims=False)
+        return mine, lax.dynamic_index_in_dim(part, 1 - t, 1, keepdims=False)
 
     def own_latent(pieces):
         rows = []
@@ -358,45 +383,54 @@
         return jnp.stack([part, theirs]).reshape(-1, latent)
 
     tok_mine, tok_theirs = pair_rows(tokens)
-    down_half = square_weight(down_weight)
-    cot_mine, cot_theirs = pair_rows(after(cotangent, tok_theirs, *down_half[1:]))
-    up_half = square_weight(after(up_weight, tok_theirs, *down_half[1:]))
-    tok_near, tok_far = spread_rows(tok_mine, tok_theirs)
-    *up_half, cot_theirs, near, far, far2 = together(
-        *up_half, cot_theirs, to_peer(tok_near[1], 2), *tok_far[-1]
-    )
-    token_parts = join_pairs([(tok_near[0], near), *tok_far[:-1], (far, far2)])
-    cot_near, cot_far = spread_rows(cot_mine, cot_theirs)
-    down_half, up_half = join_quarters(down_half), join_quarters(up_half)
-    down_own = all_features(down_half, swap_features(down_half))
+    down_half = join_quarters(square_weight(down_weight))
+    down_theirs = swap_features(down_half)
+    first = (tok_theirs, down_theirs)
+    up_mine, up_theirs = first_weight(after(up_weight, *first))
+    cot_mine, cot_theirs = pair_rows(after(cotangent, *first))
+    tok_mine, other = by_half(tok_mine, tok_theirs)
+    tok_far = far_rows(tok_mine, other)
+    up_mine, up_theirs = second_weight(up_mine, up_theirs)
+    cot_mine, cot_other = by_half(cot_mine, cot_theirs)
+    near, far, far2, down_theirs, up_theirs, cot_other = together(
+        to_peer(other, 2), *tok_far[-1], down_theirs, up_theirs, to_peer(cot_other, 2)
+    )
+    token_parts = join_pairs([(tok_mine, near), *tok_far[:-1], (far, far2)])
+    cot_rows = jnp.concatenate([cot_mine, cot_other], axis=0)
+    down_own = all_features(down_half, down_theirs)
+    up_halves = gather_h(join_steps(up_mine, up_theirs))
 
     mine, other = project(token_parts, down_own)
     part_x = add(mine, t_swap(other))
     part_x = exchange(lambda r: part_x[r])
-    sum_x = add(*part_x)
-    near = to_peer(after(cot_near[1], sum_x), 2)
-    up_own = all_features(up_half, swap_features(after(up_half, sum_x)))
-    part_x = gather_h(sum_x)
-    part_x[-1], *far = together(part_x[-1], *cot_far[-1])
-    cot_parts = join_pairs([(cot_near[0], near), *cot_far[:-1], far])
+    *part_x, up_halves[-1] = together(*part_x, up_halves[-1])
+    part_x = gather_h(add(*part_x))
+    up_theirs = [swap_features(v) for v in up_halves]
+    part_x[-1], up_theirs[-1] = together(part_x[-1], up_theirs[-1])
+    up_parts = [all_features(v, w) for v, w in zip(up_halves, up_theirs)]
     part_x = own_latent(part_x)
     part_x = jnp.stack(exchange(lambda r: part_x))
-    mine, other = project(cot_parts, up_own)
+    mine, other = project_square(cot_rows, up_parts)
     part_y = add(mine, t_swap(other))
-    part_y = own_latent(gather_h(add(*exchange(lambda r: part_y[r]))))
+    part_y = add(*exchange(lambda r: part_y[r]))
+    part_y = jnp.concatenate(turn(jnp.split(part_y, nh, axis=1)), axis=1)
+    part_y = jnp.stack(gather_h(part_y))
     part_x = after(part_x, part_y)
     latent_in = rows_with(part_x, t_swap(part_x))
-    up_far = gather_h(after(up_half, part_x))[1:]
+    down_far = gather_h(after(down_half, part_x))[1:]
+    cot_first = gather_h(after(cot_rows[: 2 * tok_rows], part_x))
 
     hs, cp, cu, out_part = forward(
         latent_in, gate_blocks(gate_columns), gate_proj, up_proj, down_rows
     )
     part_y = exchange(lambda r: part_y)
-    *part_y, up_far[-1], out_part = together(*part_y, up_far[-1], out_part)
+    *part_y, down_far[-1], cot_first[-1], out_part = together(
+        *part_y, down_far[-1], cot_first[-1], out_part
+    )
     part_y = jnp.stack(part_y)
     latent_grad = rows_with(part_y, t_swap(part_y))
-    up_theirs = [swap_features(v) for v in up_far]
-    down_far = gather_h(after(down_half, up_far[-1]))[1:]
+    down_theirs = [swap_features(v) for v in down_far]
+    cot_second = gather_h(after(cot_rows[2 * tok_rows :], cot_first[-1]))
     out_part = sum_tensor(out_part)
     down_proj_grad = down_grads(hs, latent_grad)
     out_part = after(out_part, down_proj_grad)
@@ -404,19 +438,18 @@
         after(latent_grad, out_part), cp, cu, gate_proj, up_proj, down_rows
     )
     out_part = exchange(lambda r: out_part[r])
-    *out_part, up_theirs[-1], down_far[-1], in_part = together(
-        *out_part, up_theirs[-1], down_far[-1], in_part
-    )
-    up_parts = [up_own] + [all_features(v, w) for v, w in zip(up_far, up_theirs)]
-    down_theirs = [swap_features(v) for v in down_far]
+    *out_part, down_theirs[-1], cot_second[-1], in_part = together(
+        *out_part, down_theirs[-1], cot_second[-1], in_part
+    )
+    down_parts = [down_own] + [all_features(v, w) for v, w in zip(down_far, down_theirs)]
+    cot_parts = join_pairs(zip(cot_first, cot_second))
     out_part = add(*out_part)
     in_part = sum_tensor(after(in_part, out_part))
     gate_proj_grad, up_proj_grad = input_grads(latent_in, after(dpu, in_part))
     in_part = exchange(lambda r: in_part[r])
-    *in_part, out_theirs, down_theirs[-1], gate_proj_grad = together(
-        *in_part, sum_squares(out_part)[1], down_theirs[-1], gate_proj_grad
-    )
-    down_parts = [down_own] + [all_features(v, w) for v, w in zip(down_far, down_theirs)]
+    *in_part, out_theirs, gate_proj_grad = together(
+        *in_part, sum_squares(out_part)[1], gate_proj_grad
+    )
     out_part = join_squares(out_part, out_theirs)
     in_part, in_theirs = sum_squares(add(*in_part))
     out_part = exchange(lambda r: out_part)

time: 258 us -> 252 us (0.977)
  starting transfers between devices: 76.2 us -> 71.1 us
    ppermute x6 -> x8, waiting for transfers between devices: 10.2 us -> 18.4 us  [up(): lax.ppermute(v, 'expert', [(e, (e + 4) % n_expert) for e in range(n_exper...]
    ppermute x46 -> x45, waiting for transfers between devices: 84.8 us -> 77 us  [to_peer(): return lax.ppermute(v, 'expert', [(e, e ^ r) for e in range(n_expert)])]
    ppermute x46 -> x45, starting transfers between devices: 59.4 us -> 53.3 us  [to_peer(): return lax.ppermute(v, 'expert', [(e, e ^ r) for e in range(n_expert)])]
    ppermute x6 -> x8, starting transfers between devices: 5.02 us -> 9.05 us  [up(): lax.ppermute(v, 'expert', [(e, (e + 4) % n_expert) for e in range(n_exper...]
    ppermute x4, waiting for transfers between devices: 5.93 us -> 2.84 us  [g_swap(): return lax.ppermute(v, 'group', [(i, i ^ 1) for i in range(n_group)])]
    ppermute x4 -> x2, starting transfers between devices: 6.33 us -> 3.54 us  [to_square(): return lax.ppermute(v, 'expert', perm)]
    unnamed x109 -> x89, local copies, waits for them, and re-layouts: 5.23 us -> 4.44 us
  transfers between devices with their start and end apart: 68 -> 67, of which waited for: 28 -> 34; matrix products, arithmetic and copies ran while one was open for 7% -> 7% of each run, Pallas kernels for 18% -> 18%
where the time goes in v10:
time: 252 us
  waiting for transfers between devices  103 us (41%)
  starting transfers between devices  71.1 us (28%)
  Pallas kernels  45.5 us (18%)
  other arithmetic  12.7 us (5%)
  local copies, waits for them, and re-layouts  9.89 us (4%)
  matrix products  7.83 us (3%)
    ppermute x45, waiting for transfers between devices, to_peer(): return lax.ppermute(v, 'expert', [(e, e ^ r) for e in range(n_expert)])  77 us
    ppermute x45, starting transfers between devices, to_peer(): return lax.ppermute(v, 'expert', [(e, e ^ r) for e in range(n_expert)])  53.3 us
    ppermute x8, waiting for transfers between devices, up(): lax.ppermute(v, 'expert', [(e, (e + 4) % n_expert) for e in range(n_exper...  18.4 us
    pallas_call x1, Pallas kernels, local(): forward(latent_in, gate_blocks(gate_columns), gate_proj, up_proj, down_rows)  15.8 us
    pallas_call x1, Pallas kernels, local(): backward(after(latent_grad, out_part), cp, cu, gate_proj, up_proj, down_r...  15.6 us
    ppermute x8, starting transfers between devices, up(): lax.ppermute(v, 'expert', [(e, (e + 4) % n_expert) for e in range(n_exper...  9.05 us
    pallas_call x1, Pallas kernels, local(): gate_proj_grad, up_proj_grad = input_grads(latent_in, after(dpu, in_part))  9.04 us
    dot_general x12, matrix products, dot(): return lax.dot_general(a, b, dims, preferred_element_type=f32)  7.83 us
  transfers between devices with their start and end apart: 67, of which 34 were waited for; matrix products, arithmetic and copies ran while one was open for 7% of the time, Pallas kernels for 18%

profile of v10, /device:TPU:0, one launch (start us, length us, event | category | flops | bytes accessed | tf_op | source)
XLA Modules:
  0.0 251.7 jit_solution(13392144276047164420)
XLA Ops:
  1.6 3.0 %collective-permute-start.1 = (bf16[256,128]{1,0:T(8,128)(2,1)S(1)}, bf16[256,128]{1,0:T(8,128)(2,1)S(1)}, u32[]{:S(2)}, u32[]{:S(2)}) collective-permute-start(bf16[256,128]{1,0:T(8,128)(2,1)S(1)} %get-tuple-element.210), channel_id=1, source_target_pairs={{0,2},{2,0},{4,6},{6,4},{8,10},{10,8},{12,14},{14,12},{1,3},{3,1},... | collective-permute-start | bytes 196616 | tf_op jit(solution)/shard_map/ppermute | solution.py:206
  4.6 1.6 collective-permute-start.2
  7.4 2.0 collective-permute-start
  9.4 2.1 collective-permute-done.3
  12.5 1.6 collective-permute-start.4
  14.0 2.0 collective-permute-done
  16.1 2.8 %collective-permute-done.4 = bf16[256,512]{1,0:T(8,128)(2,1)S(1)} collective-permute-done((bf16[256,512]{1,0:T(8,128)(2,1)S(1)}, bf16[256,512]{1,0:T(8,128)(2,1)S(1)}, u32[]{:S(2)}, u32[]{:S(2)}) %collective-permute-start.4) | collective-permute-done | bytes 262176 | tf_op jit(solution)/shard_map/ppermute | solution.py:212
  20.6 3.5 %collective-permute-start.8 = (bf16[256,512]{1,0:T(8,128)(2,1)S(1)}, bf16[256,512]{1,0:T(8,128)(2,1)S(1)}, u32[]{:S(2)}, u32[]{:S(2)}) collective-permute-start(bf16[256,512]{1,0:T(8,128)(2,1)S(1)} %get-tuple-element.214), channel_id=1, source_target_pairs={{0,12},{2,14},{4,8},{6,10},{8,4},{10,6},{12,0},{14,2},{1,13},{3,15... | collective-permute-start | bytes 786440 | tf_op jit(solution)/shard_map/ppermute | solution.py:257
  26.4 14.6 %collective-permute-done.9 = bf16[2,256,128]{2,1,0:T(8,128)(2,1)S(1)} collective-permute-done((bf16[2,256,128]{2,1,0:T(8,128)(2,1)S(1)}, bf16[2,256,128]{2,1,0:T(8,128)(2,1)S(1)}, u32[]{:S(2)}, u32[]{:S(2)}) %collective-permute-start.9) | collective-permute-done | bytes 131104 | tf_op jit(solution)/shard_map/ppermute | solution.py:206
  42.1 2.0 collective-permute-done.7
  44.1 2.0 collective-permute-done.10
  48.3 4.1 %collective-permute-start.16 = (bf16[256,512]{1,0:T(8,128)(2,1)S(1)}, bf16[256,512]{1,0:T(8,128)(2,1)}, u32[]{:S(2)}, u32[]{:S(2)}) collective-permute-start(bf16[256,512]{1,0:T(8,128)(2,1)S(1)} %pad_maximum_fusion.21), channel_id=1, source_target_pairs={{0,8},{2,10},{4,12},{6,14},{8,0},{10,2},{12,4},{14,6},{1,9},{3,11}... | collective-permute-start | bytes 786440 | tf_op jit(solution)/shard_map/ppermute | solution.py:215
  52.4 1.5 collective-permute-start.22
  54.9 2.7 %collective-permute-start.15 = (bf16[2,64,512]{2,1,0:T(8,128)(2,1)S(1)}, bf16[2,64,512]{2,1,0:T(8,128)(2,1)S(1)}, u32[]{:S(2)}, u32[]{:S(2)}) collective-permute-start(bf16[2,64,512]{2,1,0:T(8,128)(2,1)S(1)} %get-tuple-element.196), channel_id=1, source_target_pairs={{0,6},{2,4},{4,2},{6,0},{8,14},{10,12},{12,10},{14,8},{1,7},{3,5},... | collective-permute-start | bytes 393224 | tf_op jit(solution)/shard_map/ppermute | solution.py:206
  57.6 6.9 %collective-permute-done.16 = bf16[256,512]{1,0:T(8,128)(2,1)} collective-permute-done((bf16[256,512]{1,0:T(8,128)(2,1)S(1)}, bf16[256,512]{1,0:T(8,128)(2,1)}, u32[]{:S(2)}, u32[]{:S(2)}) %collective-permute-start.16) | collective-permute-done | bytes 262176 | tf_op jit(solution)/shard_map/ppermute | solution.py:215
  65.8 2.0 collective-permute-done.15
  69.2 6.0 %collective-permute-done.17 = bf16[2,64,512]{2,1,0:T(8,128)(2,1)S(1)} collective-permute-done((bf16[2,64,512]{2,1,0:T(8,128)(2,1)S(1)}, bf16[2,64,512]{2,1,0:T(8,128)(2,1)S(1)}, u32[]{:S(2)}, u32[]{:S(2)}) %collective-permute-start.17) | collective-permute-done | bytes 131104 | tf_op jit(solution)/shard_map/ppermute | solution.py:215
  75.9 1.5 convolution_convert_fusion
  81.3 2.8 %collective-permute-start.26 = (bf16[64,1024]{1,0:T(8,128)(2,1)S(1)}, bf16[64,1024]{1,0:T(8,128)(2,1)S(1)}, u32[]{:S(2)}, u32[]{:S(2)}) collective-permute-start(bf16[64,1024]{1,0:T(8,128)(2,1)S(1)} %get-tuple-element.194), channel_id=1, source_target_pairs={{0,6},{2,4},{4,2},{6,0},{8,14},{10,12},{12,10},{14,8},{1,7},{3,5},... | collective-permute-start | bytes 393224 | tf_op jit(solution)/shard_map/ppermute | solution.py:206
  86.1 1.6 collective-permute-start.21
  87.7 3.5 %collective-permute-done.26 = bf16[64,1024]{1,0:T(8,128)(2,1)S(1)} collective-permute-done((bf16[64,1024]{1,0:T(8,128)(2,1)S(1)}, bf16[64,1024]{1,0:T(8,128)(2,1)S(1)}, u32[]{:S(2)}, u32[]{:S(2)}) %collective-permute-start.26) | collective-permute-done | bytes 131104 | tf_op jit(solution)/shard_map/ppermute | solution.py:206
  91.5 3.1 %collective-permute-done.19 = bf16[2,64,1024]{2,1,0:T(8,128)(2,1)S(1)} collective-permute-done((bf16[2,64,1024]{2,1,0:T(8,128)(2,1)S(1)}, bf16[2,64,1024]{2,1,0:T(8,128)(2,1)S(1)}, u32[]{:S(2)}, u32[]{:S(2)}) %collective-permute-start.19) | collective-permute-done | bytes 262176 | tf_op jit(solution)/shard_map/ppermute | solution.py:206
  94.6 4.4 %collective-permute-done.20 = bf16[2,64,1024]{2,1,0:T(8,128)(2,1)S(1)} collective-permute-done((bf16[2,64,1024]{2,1,0:T(8,128)(2,1)S(1)}, bf16[2,64,1024]{2,1,0:T(8,128)(2,1)S(1)}, u32[]{:S(2)}, u32[]{:S(2)}) %collective-permute-start.20) | collective-permute-done | bytes 262176 | tf_op jit(solution)/shard_map/ppermute | solution.py:206
  98.9 5.2 %collective-permute-done.21 = bf16[2,64,1024]{2,1,0:T(8,128)(2,1)S(1)} collective-permute-done((bf16[2,64,1024]{2,1,0:T(8,128)(2,1)S(1)}, bf16[2,64,1024]{2,1,0:T(8,128)(2,1)S(1)}, u32[]{:S(2)}, u32[]{:S(2)}) %collective-permute-start.21) | collective-permute-done | bytes 262176 | tf_op jit(solution)/shard_map/ppermute | solution.py:206
  106.0 2.8 %collective-permute-start.30 = (bf16[2,64,1024]{2,1,0:T(8,128)(2,1)S(1)}, bf16[2,64,1024]{2,1,0:T(8,128)(2,1)S(1)}, u32[]{:S(2)}, u32[]{:S(2)}) collective-permute-start(bf16[2,64,1024]{2,1,0:T(8,128)(2,1)S(1)} %pad_maximum_fusion.23), channel_id=1, source_target_pairs={{0,6},{2,4},{4,2},{6,0},{8,14},{10,12},{12,10},{14,8},{1,7},{3,5},... | collective-permute-start | bytes 786440 | tf_op jit(solution)/shard_map/ppermute | solution.py:206
  109.1 2.6 %collective-permute-start.31 = (bf16[256,512]{1,0:T(8,128)(2,1)S(1)}, bf16[256,512]{1,0:T(8,128)(2,1)S(1)}, u32[]{:S(2)}, u32[]{:S(2)}) collective-permute-start(bf16[256,512]{1,0:T(8,128)(2,1)S(1)} %pad_maximum_fusion.18), channel_id=1, source_target_pairs={{0,8},{2,10},{4,12},{6,14},{8,0},{10,2},{12,4},{14,6},{1,9},{3,11}... | collective-permute-start | bytes 786440 | tf_op jit(solution)/shard_map/ppermute | solution.py:215
  113.1 15.8 %shard_map.144 = (bf16[1024,1536]{1,0:T(8,128)(2,1)S(1)}, bf16[1024,1536]{1,0:T(8,128)(2,1)S(1)}, bf16[1024,1536]{1,0:T(8,128)(2,1)}, bf16[1024,1024]{1,0:T(8,128)(2,1)S(1)}) custom-call(bf16[1024,1024]{1,0:T(8,128)(2,1)S(1)} %bitcast.204, f32[2,1024,2]{2,1,0:T(8,128)S(1)} %bitcast.208, bf16[4,1024,384]{2,1,0:T(8,128)(2,1)} %wg_ref.3, ...), custom_call_target="tpu_custom_call" | custom-call | flops 9663676416 | bytes 23068672 | tf_op jit(solution)/shard_map/pallas_call | solution.py:423
  129.0 5.5 %collective-permute-done.31 = bf16[256,512]{1,0:T(8,128)(2,1)S(1)} collective-permute-done((bf16[256,512]{1,0:T(8,128)(2,1)S(1)}, bf16[256,512]{1,0:T(8,128)(2,1)S(1)}, u32[]{:S(2)}, u32[]{:S(2)}) %collective-permute-start.31) | collective-permute-done | bytes 262176 | tf_op jit(solution)/shard_map/ppermute | solution.py:215
  137.6 5.0 %shard_map.145 = bf16[1536,1024]{1,0:T(8,128)(2,1)} custom-call(bf16[1024,1536]{1,0:T(8,128)(2,1)S(1)} %get-tuple-element.93.hs_ref, bf16[1024,1024]{1,0:T(8,128)(2,1)S(1)} %bitcast.206), custom_call_target="tpu_custom_call" | custom-call | flops 3221225472 | bytes 8388608 | tf_op jit(solution)/shard_map/pallas_call | solution.py:435
  144.0 2.7 %collective-permute-start.38 = (bf16[2,64,1024]{2,1,0:T(8,128)(2,1)S(1)}, bf16[2,64,1024]{2,1,0:T(8,128)(2,1)S(1)}, u32[]{:S(2)}, u32[]{:S(2)}) collective-permute-start(bf16[2,64,1024]{2,1,0:T(8,128)(2,1)S(1)} %get-tuple-element.143), channel_id=1, source_target_pairs={{0,6},{2,4},{4,2},{6,0},{8,14},{10,12},{12,10},{14,8},{1,7},{3,5},... | collective-permute-start | bytes 786440 | tf_op jit(solution)/shard_map/ppermute | solution.py:206
  146.7 15.6 %shard_map.146 = (bf16[1024,3072]{1,0:T(8,128)(2,1)}, bf16[1024,1024]{1,0:T(8,128)(2,1)S(1)}) custom-call(bf16[1024,1024]{1,0:T(8,128)(2,1)S(1)} %bitcast.207, bf16[1024,1536]{1,0:T(8,128)(2,1)S(1)} %get-tuple-element.101.cp_ref, bf16[1024,1536]{1,0:T(8,128)(2,1)S(1)} %copy-done.2, bf16[4,1024,384]{2,1,0:T(8,128)(2,1)S(1)} %copy-done, ...), custom_call_target="tpu_custom_call" | custom-call | flops 9663676416 | bytes 26214400 | tf_op jit(solution)/shard_map/pallas_call | solution.py:437
  163.2 1.8 collective-permute-start.45
  167.2 2.7 %collective-permute-start.44 = (bf16[2,64,1024]{2,1,0:T(8,128)(2,1)S(1)}, bf16[2,64,1024]{2,1,0:T(8,128)(2,1)S(1)}, u32[]{:S(2)}, u32[]{:S(2)}) collective-permute-start(bf16[2,64,1024]{2,1,0:T(8,128)(2,1)S(1)} %get-tuple-element.139), channel_id=1, source_target_pairs={{0,6},{2,4},{4,2},{6,0},{8,14},{10,12},{12,10},{14,8},{1,7},{3,5},... | collective-permute-start | bytes 786440 | tf_op jit(solution)/shard_map/ppermute | solution.py:206
  169.9 9.0 %shard_map.147 = (bf16[4,1024,384]{2,1,0:T(8,128)(2,1)}, bf16[4,1024,384]{2,1,0:T(8,128)(2,1)}) custom-call(bf16[1024,1024]{1,0:T(8,128)(2,1)S(1)} %bitcast.205, bf16[1024,3072]{1,0:T(8,128)(2,1)S(1)} %copy-done.1), custom_call_target="tpu_custom_call" | custom-call | flops 6442450944 | bytes 14680064 | tf_op jit(solution)/shard_map/pallas_call | solution.py:448
  178.9 2.9 %collective-permute-done.43 = bf16[2,64,1024]{2,1,0:T(8,128)(2,1)S(1)} collective-permute-done((bf16[2,64,1024]{2,1,0:T(8,128)(2,1)S(1)}, bf16[2,64,1024]{2,1,0:T(8,128)(2,1)S(1)}, u32[]{:S(2)}, u32[]{:S(2)}) %collective-permute-start.43) | collective-permute-done | bytes 262176 | tf_op jit(solution)/shard_map/ppermute | solution.py:206
  181.8 5.2 %collective-permute-done.44 = bf16[2,64,1024]{2,1,0:T(8,128)(2,1)S(1)} collective-permute-done((bf16[2,64,1024]{2,1,0:T(8,128)(2,1)S(1)}, bf16[2,64,1024]{2,1,0:T(8,128)(2,1)S(1)}, u32[]{:S(2)}, u32[]{:S(2)}) %collective-permute-start.44) | collective-permute-done | bytes 262176 | tf_op jit(solution)/shard_map/ppermute | solution.py:206
  189.4 1.6 collective-permute-start.48
  191.0 2.7 %collective-permute-done.46 = bf16[64,1536]{1,0:T(8,128)(2,1)S(1)} collective-permute-done((bf16[64,1536]{1,0:T(8,128)(2,1)S(1)}, bf16[64,1536]{1,0:T(8,128)(2,1)S(1)}, u32[]{:S(2)}, u32[]{:S(2)}) %collective-permute-start.46) | collective-permute-done | bytes 196640 | tf_op jit(solution)/shard_map/ppermute | solution.py:206
  193.7 7.7 %collective-permute-done.47 = bf16[64,1536]{1,0:T(8,128)(2,1)S(1)} collective-permute-done((bf16[64,1536]{1,0:T(8,128)(2,1)S(1)}, bf16[64,1536]{1,0:T(8,128)(2,1)S(1)}, u32[]{:S(2)}, u32[]{:S(2)}) %collective-permute-start.47) | collective-permute-done | bytes 196640 | tf_op jit(solution)/shard_map/ppermute | solution.py:206
  201.5 2.8 %collective-permute-done.48 = bf16[64,1536]{1,0:T(8,128)(2,1)S(1)} collective-permute-done((bf16[64,1536]{1,0:T(8,128)(2,1)S(1)}, bf16[64,1536]{1,0:T(8,128)(2,1)S(1)}, u32[]{:S(2)}, u32[]{:S(2)}) %collective-permute-start.48) | collective-permute-done | bytes 196640 | tf_op jit(solution)/shard_map/ppermute | solution.py:206
  206.1 2.7 %collective-permute-start.59 = (bf16[64,1536]{1,0:T(8,128)(2,1)}, bf16[64,1536]{1,0:T(8,128)(2,1)}, u32[]{:S(2)}, u32[]{:S(2)}) collective-permute-start(bf16[64,1536]{1,0:T(8,128)(2,1)} %get-tuple-element.232), channel_id=1, source_target_pairs={{0,6},{2,4},{4,2},{6,0},{8,14},{10,12},{12,10},{14,8},{1,7},{3,5},... | collective-permute-start | bytes 589832 | tf_op jit(solution)/shard_map/ppermute | solution.py:206
  208.8 4.0 %collective-permute-done.57 = bf16[64,1536]{1,0:T(8,128)(2,1)S(1)} collective-permute-done((bf16[64,1536]{1,0:T(8,128)(2,1)}, bf16[64,1536]{1,0:T(8,128)(2,1)S(1)}, u32[]{:S(2)}, u32[]{:S(2)}) %collective-permute-start.57) | collective-permute-done | bytes 196640 | tf_op jit(solution)/shard_map/ppermute | solution.py:206
  214.1 4.2 %collective-permute-done.59 = bf16[64,1536]{1,0:T(8,128)(2,1)} collective-permute-done((bf16[64,1536]{1,0:T(8,128)(2,1)}, bf16[64,1536]{1,0:T(8,128)(2,1)}, u32[]{:S(2)}, u32[]{:S(2)}) %collective-permute-start.59) | collective-permute-done | bytes 196640 | tf_op jit(solution)/shard_map/ppermute | solution.py:206
  220.8 1.6 fusion.12
  224.2 2.4 collective-permute-start.56
  232.1 2.5 collective-permute-start.53
  236.3 2.4 collective-permute-start.66
  240.3 2.2 collective-permute-start.62
  (277 shorter events, 58.8 us)
Async XLA Ops:
  1.6 7.8 %collective-permute-start.1 = (bf16[256,128]{1,0:T(8,128)(2,1)S(1)}, bf16[256,128]{1,0:T(8,128)(2,1)S(1)}, u32[]{:S(2)}, u32[]{:S(2)}) collective-permute-start(bf16[256,128]{1,0:T(8,128)(2,1)S(1)} %get-tuple-element.210), channel_id=1, source_target_pairs={{0,2},{2,0},{4,6},{6,4},{8,10},{10,8},{12,14},{14,12},{1,3},{3,1},... | collective-permute-start | bytes 196616 | tf_op jit(solution)/shard_map/ppermute | solution.py:206
  7.4 8.6 %collective-permute-start = (bf16[128,1024]{1,0:T(8,128)(2,1)S(1)}, bf16[128,1024]{1,0:T(8,128)(2,1)S(1)}, u32[]{:S(2)}, u32[]{:S(2)}) collective-permute-start(bf16[128,1024]{1,0:T(8,128)(2,1)S(1)} %pad_maximum_fusion.17), channel_id=1, source_target_pairs={{0,2},{2,0},{4,6},{6,4},{8,10},{10,8},{12,14},{14,12},{1,3},{3,1},... | collective-permute-start | bytes 786440 | tf_op jit(solution)/shard_map/ppermute | solution.py:206
  20.0 22.1 %collective-permute-start.6 = (bf16[256,512]{1,0:T(8,128)(2,1)S(1)}, bf16[256,512]{1,0:T(8,128)(2,1)S(1)}, u32[]{:S(2)}, u32[]{:S(2)}) collective-permute-start(bf16[256,512]{1,0:T(8,128)(2,1)S(1)} %get-tuple-element.214), channel_id=1, source_target_pairs={{0,4},{2,6},{4,0},{6,2},{8,12},{10,14},{12,8},{14,10},{1,5},{3,7},... | collective-permute-start | bytes 786440 | tf_op jit(solution)/shard_map/ppermute | solution.py:206
  20.6 23.6 %collective-permute-start.8 = (bf16[256,512]{1,0:T(8,128)(2,1)S(1)}, bf16[256,512]{1,0:T(8,128)(2,1)S(1)}, u32[]{:S(2)}, u32[]{:S(2)}) collective-permute-start(bf16[256,512]{1,0:T(8,128)(2,1)S(1)} %get-tuple-element.214), channel_id=1, source_target_pairs={{0,12},{2,14},{4,8},{6,10},{8,4},{10,6},{12,0},{14,2},{1,13},{3,15... | collective-permute-start | bytes 786440 | tf_op jit(solution)/shard_map/ppermute | solution.py:257
  24.1 20.0 %collective-permute-start.7 = (bf16[256,512]{1,0:T(8,128)(2,1)S(1)}, bf16[256,512]{1,0:T(8,128)(2,1)S(1)}, u32[]{:S(2)}, u32[]{:S(2)}) collective-permute-start(bf16[256,512]{1,0:T(8,128)(2,1)S(1)} %get-tuple-element.213), channel_id=1, source_target_pairs={{0,8},{2,10},{4,12},{6,14},{8,0},{10,2},{12,4},{14,6},{1,9},{3,11}... | collective-permute-start | bytes 786440 | tf_op jit(solution)/shard_map/ppermute | solution.py:257
  24.1 16.8 %collective-permute-start.9 = (bf16[2,256,128]{2,1,0:T(8,128)(2,1)S(1)}, bf16[2,256,128]{2,1,0:T(8,128)(2,1)S(1)}, u32[]{:S(2)}, u32[]{:S(2)}) collective-permute-start(bf16[2,256,128]{2,1,0:T(8,128)(2,1)S(1)} %pad_maximum_fusion.26), channel_id=1, source_target_pairs={{0,4},{2,6},{4,0},{6,2},{8,12},{10,14},{12,8},{14,10},{1,5},{3,7},... | collective-permute-start | bytes 393224 | tf_op jit(solution)/shard_map/ppermute | solution.py:206
  25.5 20.6 %collective-permute-start.11 = (bf16[256,512]{1,0:T(8,128)(2,1)S(1)}, bf16[256,512]{1,0:T(8,128)(2,1)S(1)}, u32[]{:S(2)}, u32[]{:S(2)}) collective-permute-start(bf16[256,512]{1,0:T(8,128)(2,1)S(1)} %get-tuple-element.201), channel_id=1, source_target_pairs={{0,4},{2,6},{4,0},{6,2},{8,12},{10,14},{12,8},{14,10},{1,5},{3,7},... | collective-permute-start | bytes 786440 | tf_op jit(solution)/shard_map/ppermute | solution.py:206
  48.3 16.3 %collective-permute-start.16 = (bf16[256,512]{1,0:T(8,128)(2,1)S(1)}, bf16[256,512]{1,0:T(8,128)(2,1)}, u32[]{:S(2)}, u32[]{:S(2)}) collective-permute-start(bf16[256,512]{1,0:T(8,128)(2,1)S(1)} %pad_maximum_fusion.21), channel_id=1, source_target_pairs={{0,8},{2,10},{4,12},{6,14},{8,0},{10,2},{12,4},{14,6},{1,9},{3,11}... | collective-permute-start | bytes 786440 | tf_op jit(solution)/shard_map/ppermute | solution.py:215
  52.4 16.2 %collective-permute-start.22 = (bf16[256,512]{1,0:T(8,128)(2,1)S(1)}, bf16[256,512]{1,0:T(8,128)(2,1)S(1)}, u32[]{:S(2)}, u32[]{:S(2)}) collective-permute-start(bf16[256,512]{1,0:T(8,128)(2,1)S(1)} %pad_maximum_fusion.21), channel_id=1, source_target_pairs={{0,16},{16,0},{1,17},{17,1},{2,18},{18,2},{3,19},{19,3},{4,20},{20... | collective-permute-start | bytes 786440 | tf_op jit(solution)/shard_map/ppermute | solution.py:212
  54.1 10.5 %collective-permute-start.13 = (bf16[2,64,512]{2,1,0:T(8,128)(2,1)S(1)}, bf16[2,64,512]{2,1,0:T(8,128)(2,1)S(1)}, u32[]{:S(2)}, u32[]{:S(2)}) collective-permute-start(bf16[2,64,512]{2,1,0:T(8,128)(2,1)S(1)} %get-tuple-element.198), channel_id=1, source_target_pairs={{0,2},{2,0},{4,6},{6,4},{8,10},{10,8},{12,14},{14,12},{1,3},{3,1},... | collective-permute-start | bytes 393224 | tf_op jit(solution)/shard_map/ppermute | solution.py:206
  54.9 10.9 %collective-permute-start.14 = (bf16[2,64,512]{2,1,0:T(8,128)(2,1)S(1)}, bf16[2,64,512]{2,1,0:T(8,128)(2,1)S(1)}, u32[]{:S(2)}, u32[]{:S(2)}) collective-permute-start(bf16[2,64,512]{2,1,0:T(8,128)(2,1)S(1)} %get-tuple-element.197), channel_id=1, source_target_pairs={{0,4},{2,6},{4,0},{6,2},{8,12},{10,14},{12,8},{14,10},{1,5},{3,7},... | collective-permute-start | bytes 393224 | tf_op jit(solution)/shard_map/ppermute | solution.py:206
  54.9 13.0 %collective-permute-start.15 = (bf16[2,64,512]{2,1,0:T(8,128)(2,1)S(1)}, bf16[2,64,512]{2,1,0:T(8,128)(2,1)S(1)}, u32[]{:S(2)}, u32[]{:S(2)}) collective-permute-start(bf16[2,64,512]{2,1,0:T(8,128)(2,1)S(1)} %get-tuple-element.196), channel_id=1, source_target_pairs={{0,6},{2,4},{4,2},{6,0},{8,14},{10,12},{12,10},{14,8},{1,7},{3,5},... | collective-permute-start | bytes 393224 | tf_op jit(solution)/shard_map/ppermute | solution.py:206
  81.3 9.9 %collective-permute-start.26 = (bf16[64,1024]{1,0:T(8,128)(2,1)S(1)}, bf16[64,1024]{1,0:T(8,128)(2,1)S(1)}, u32[]{:S(2)}, u32[]{:S(2)}) collective-permute-start(bf16[64,1024]{1,0:T(8,128)(2,1)S(1)} %get-tuple-element.194), channel_id=1, source_target_pairs={{0,6},{2,4},{4,2},{6,0},{8,14},{10,12},{12,10},{14,8},{1,7},{3,5},... | collective-permute-start | bytes 393224 | tf_op jit(solution)/shard_map/ppermute | solution.py:206
  84.1 10.4 %collective-permute-start.19 = (bf16[2,64,1024]{2,1,0:T(8,128)(2,1)S(1)}, bf16[2,64,1024]{2,1,0:T(8,128)(2,1)S(1)}, u32[]{:S(2)}, u32[]{:S(2)}) collective-permute-start(bf16[2,64,1024]{2,1,0:T(8,128)(2,1)S(1)} %get-tuple-element.220), channel_id=1, source_target_pairs={{0,2},{2,0},{4,6},{6,4},{8,10},{10,8},{12,14},{14,12},{1,3},{3,1},... | collective-permute-start | bytes 786440 | tf_op jit(solution)/shard_map/ppermute | solution.py:206
  84.9 14.0 %collective-permute-start.20 = (bf16[2,64,1024]{2,1,0:T(8,128)(2,1)S(1)}, bf16[2,64,1024]{2,1,0:T(8,128)(2,1)S(1)}, u32[]{:S(2)}, u32[]{:S(2)}) collective-permute-start(bf16[2,64,1024]{2,1,0:T(8,128)(2,1)S(1)} %get-tuple-element.220), channel_id=1, source_target_pairs={{0,4},{2,6},{4,0},{6,2},{8,12},{10,14},{12,8},{14,10},{1,5},{3,7},... | collective-permute-start | bytes 786440 | tf_op jit(solution)/shard_map/ppermute | solution.py:206
  86.1 18.0 %collective-permute-start.21 = (bf16[2,64,1024]{2,1,0:T(8,128)(2,1)S(1)}, bf16[2,64,1024]{2,1,0:T(8,128)(2,1)S(1)}, u32[]{:S(2)}, u32[]{:S(2)}) collective-permute-start(bf16[2,64,1024]{2,1,0:T(8,128)(2,1)S(1)} %get-tuple-element.220), channel_id=1, source_target_pairs={{0,6},{2,4},{4,2},{6,0},{8,14},{10,12},{12,10},{14,8},{1,7},{3,5},... | collective-permute-start | bytes 786440 | tf_op jit(solution)/shard_map/ppermute | solution.py:206
  91.4 12.9 %collective-permute-start.27 = (bf16[64,1024]{1,0:T(8,128)(2,1)S(1)}, bf16[64,1024]{1,0:T(8,128)(2,1)S(1)}, u32[]{:S(2)}, u32[]{:S(2)}) collective-permute-start(bf16[64,1024]{1,0:T(8,128)(2,1)S(1)} %get-tuple-element.238), channel_id=1, source_target_pairs={{0,8},{2,10},{4,12},{6,14},{8,0},{10,2},{12,4},{14,6},{1,9},{3,11}... | collective-permute-start | bytes 393224 | tf_op jit(solution)/shard_map/ppermute | solution.py:215
  105.2 29.2 %collective-permute-start.28 = (bf16[2,64,1024]{2,1,0:T(8,128)(2,1)S(1)}, bf16[2,64,1024]{2,1,0:T(8,128)(2,1)S(1)}, u32[]{:S(2)}, u32[]{:S(2)}) collective-permute-start(bf16[2,64,1024]{2,1,0:T(8,128)(2,1)S(1)} %pad_maximum_fusion.23), channel_id=1, source_target_pairs={{0,2},{2,0},{4,6},{6,4},{8,10},{10,8},{12,14},{14,12},{1,3},{3,1},... | collective-permute-start | bytes 786440 | tf_op jit(solution)/shard_map/ppermute | solution.py:206
  106.0 28.4 %collective-permute-start.29 = (bf16[2,64,1024]{2,1,0:T(8,128)(2,1)S(1)}, bf16[2,64,1024]{2,1,0:T(8,128)(2,1)S(1)}, u32[]{:S(2)}, u32[]{:S(2)}) collective-permute-start(bf16[2,64,1024]{2,1,0:T(8,128)(2,1)S(1)} %pad_maximum_fusion.23), channel_id=1, source_target_pairs={{0,4},{2,6},{4,0},{6,2},{8,12},{10,14},{12,8},{14,10},{1,5},{3,7},... | collective-permute-start | bytes 786440 | tf_op jit(solution)/shard_map/ppermute | solution.py:206
  106.0 28.4 %collective-permute-start.30 = (bf16[2,64,1024]{2,1,0:T(8,128)(2,1)S(1)}, bf16[2,64,1024]{2,1,0:T(8,128)(2,1)S(1)}, u32[]{:S(2)}, u32[]{:S(2)}) collective-permute-start(bf16[2,64,1024]{2,1,0:T(8,128)(2,1)S(1)} %pad_maximum_fusion.23), channel_id=1, source_target_pairs={{0,6},{2,4},{4,2},{6,0},{8,14},{10,12},{12,10},{14,8},{1,7},{3,5},... | collective-permute-start | bytes 786440 | tf_op jit(solution)/shard_map/ppermute | solution.py:206
  108.8 20.2 %collective-permute-start.32 = (bf16[256,512]{1,0:T(8,128)(2,1)S(1)}, bf16[256,512]{1,0:T(8,128)(2,1)S(1)}, u32[]{:S(2)}, u32[]{:S(2)}) collective-permute-start(bf16[256,512]{1,0:T(8,128)(2,1)S(1)} %get-tuple-element.87), channel_id=1, source_target_pairs={{0,8},{2,10},{4,12},{6,14},{8,0},{10,2},{12,4},{14,6},{1,9},{3,11}... | collective-permute-start | bytes 786440 | tf_op jit(solution)/shard_map/ppermute | solution.py:215
  109.1 25.3 %collective-permute-start.31 = (bf16[256,512]{1,0:T(8,128)(2,1)S(1)}, bf16[256,512]{1,0:T(8,128)(2,1)S(1)}, u32[]{:S(2)}, u32[]{:S(2)}) collective-permute-start(bf16[256,512]{1,0:T(8,128)(2,1)S(1)} %pad_maximum_fusion.18), channel_id=1, source_target_pairs={{0,8},{2,10},{4,12},{6,14},{8,0},{10,2},{12,4},{14,6},{1,9},{3,11}... | collective-permute-start | bytes 786440 | tf_op jit(solution)/shard_map/ppermute | solution.py:215
  135.6 26.7 %collective-permute-start.40 = (bf16[256,512]{1,0:T(8,128)(2,1)S(1)}, bf16[256,512]{1,0:T(8,128)(2,1)S(1)}, u32[]{:S(2)}, u32[]{:S(2)}) collective-permute-start(bf16[256,512]{1,0:T(8,128)(2,1)S(1)} %copy-done.29), channel_id=1, source_target_pairs={{0,8},{2,10},{4,12},{6,14},{8,0},{10,2},{12,4},{14,6},{1,9},{3,11}... | collective-permute-start | bytes 786440 | tf_op jit(solution)/shard_map/ppermute | solution.py:215
  135.6 26.7 %collective-permute-start.39 = (bf16[256,512]{1,0:T(8,128)(2,1)S(1)}, bf16[256,512]{1,0:T(8,128)(2,1)S(1)}, u32[]{:S(2)}, u32[]{:S(2)}) collective-permute-start(bf16[256,512]{1,0:T(8,128)(2,1)S(1)} %collective-permute-done.31), channel_id=1, source_target_pairs={{0,16},{16,0},{1,17},{17,1},{2,18},{18,2},{3,19},{19,3},{4,20},{20... | collective-permute-start | bytes 786440 | tf_op jit(solution)/shard_map/ppermute | solution.py:212
  143.1 19.2 %collective-permute-start.36 = (bf16[2,64,1024]{2,1,0:T(8,128)(2,1)S(1)}, bf16[2,64,1024]{2,1,0:T(8,128)(2,1)S(1)}, u32[]{:S(2)}, u32[]{:S(2)}) collective-permute-start(bf16[2,64,1024]{2,1,0:T(8,128)(2,1)S(1)} %get-tuple-element.145), channel_id=1, source_target_pairs={{0,2},{2,0},{4,6},{6,4},{8,10},{10,8},{12,14},{14,12},{1,3},{3,1},... | collective-permute-start | bytes 786440 | tf_op jit(solution)/shard_map/ppermute | solution.py:206
  143.9 18.4 %collective-permute-start.37 = (bf16[2,64,1024]{2,1,0:T(8,128)(2,1)S(1)}, bf16[2,64,1024]{2,1,0:T(8,128)(2,1)S(1)}, u32[]{:S(2)}, u32[]{:S(2)}) collective-permute-start(bf16[2,64,1024]{2,1,0:T(8,128)(2,1)S(1)} %get-tuple-element.144), channel_id=1, source_target_pairs={{0,4},{2,6},{4,0},{6,2},{8,12},{10,14},{12,8},{14,10},{1,5},{3,7},... | collective-permute-start | bytes 786440 | tf_op jit(solution)/shard_map/ppermute | solution.py:206
  144.0 18.4 %collective-permute-start.38 = (bf16[2,64,1024]{2,1,0:T(8,128)(2,1)S(1)}, bf16[2,64,1024]{2,1,0:T(8,128)(2,1)S(1)}, u32[]{:S(2)}, u32[]{:S(2)}) collective-permute-start(bf16[2,64,1024]{2,1,0:T(8,128)(2,1)S(1)} %get-tuple-element.143), channel_id=1, source_target_pairs={{0,6},{2,4},{4,2},{6,0},{8,14},{10,12},{12,10},{14,8},{1,7},{3,5},... | collective-permute-start | bytes 786440 | tf_op jit(solution)/shard_map/ppermute | solution.py:206
  163.2 15.8 %collective-permute-start.45 = (bf16[2,64,1024]{2,1,0:T(8,128)(2,1)S(1)}, bf16[2,64,1024]{2,1,0:T(8,128)(2,1)S(1)}, u32[]{:S(2)}, u32[]{:S(2)}) collective-permute-start(bf16[2,64,1024]{2,1,0:T(8,128)(2,1)S(1)} %add_convert_fusion.1), channel_id=1, source_target_pairs={{0,8},{2,10},{4,12},{6,14},{8,0},{10,2},{12,4},{14,6},{1,9},{3,11}... | collective-permute-start | bytes 786440 | tf_op jit(solution)/shard_map/ppermute | solution.py:215
  166.3 12.6 %collective-permute-start.42 = (bf16[2,64,1024]{2,1,0:T(8,128)(2,1)S(1)}, bf16[2,64,1024]{2,1,0:T(8,128)(2,1)S(1)}, u32[]{:S(2)}, u32[]{:S(2)}) collective-permute-start(bf16[2,64,1024]{2,1,0:T(8,128)(2,1)S(1)} %get-tuple-element.141), channel_id=1, source_target_pairs={{0,2},{2,0},{4,6},{6,4},{8,10},{10,8},{12,14},{14,12},{1,3},{3,1},... | collective-permute-start | bytes 786440 | tf_op jit(solution)/shard_map/ppermute | solution.py:206
  167.1 14.7 %collective-permute-start.43 = (bf16[2,64,1024]{2,1,0:T(8,128)(2,1)S(1)}, bf16[2,64,1024]{2,1,0:T(8,128)(2,1)S(1)}, u32[]{:S(2)}, u32[]{:S(2)}) collective-permute-start(bf16[2,64,1024]{2,1,0:T(8,128)(2,1)S(1)} %get-tuple-element.140), channel_id=1, source_target_pairs={{0,4},{2,6},{4,0},{6,2},{8,12},{10,14},{12,8},{14,10},{1,5},{3,7},... | collective-permute-start | bytes 786440 | tf_op jit(solution)/shard_map/ppermute | solution.py:206
  167.2 19.9 %collective-permute-start.44 = (bf16[2,64,1024]{2,1,0:T(8,128)(2,1)S(1)}, bf16[2,64,1024]{2,1,0:T(8,128)(2,1)S(1)}, u32[]{:S(2)}, u32[]{:S(2)}) collective-permute-start(bf16[2,64,1024]{2,1,0:T(8,128)(2,1)S(1)} %get-tuple-element.139), channel_id=1, source_target_pairs={{0,6},{2,4},{4,2},{6,0},{8,14},{10,12},{12,10},{14,8},{1,7},{3,5},... | collective-permute-start | bytes 786440 | tf_op jit(solution)/shard_map/ppermute | solution.py:206
  187.4 17.0 %collective-permute-start.49 = (bf16[2,64,1024]{2,1,0:T(8,128)(2,1)S(1)}, bf16[2,64,1024]{2,1,0:T(8,128)(2,1)S(1)}, u32[]{:S(2)}, u32[]{:S(2)}) collective-permute-start(bf16[2,64,1024]{2,1,0:T(8,128)(2,1)S(1)} %add_convert_fusion), channel_id=1, source_target_pairs={{0,8},{2,10},{4,12},{6,14},{8,0},{10,2},{12,4},{14,6},{1,9},{3,11}... | collective-permute-start | bytes 786440 | tf_op jit(solution)/shard_map/ppermute | solution.py:215
  188.2 13.2 %collective-permute-start.47 = (bf16[64,1536]{1,0:T(8,128)(2,1)S(1)}, bf16[64,1536]{1,0:T(8,128)(2,1)S(1)}, u32[]{:S(2)}, u32[]{:S(2)}) collective-permute-start(bf16[64,1536]{1,0:T(8,128)(2,1)S(1)} %pad_maximum_fusion.24), channel_id=1, source_target_pairs={{0,4},{2,6},{4,0},{6,2},{8,12},{10,14},{12,8},{14,10},{1,5},{3,7},... | collective-permute-start | bytes 589832 | tf_op jit(solution)/shard_map/ppermute | solution.py:206
  189.4 14.9 %collective-permute-start.48 = (bf16[64,1536]{1,0:T(8,128)(2,1)S(1)}, bf16[64,1536]{1,0:T(8,128)(2,1)S(1)}, u32[]{:S(2)}, u32[]{:S(2)}) collective-permute-start(bf16[64,1536]{1,0:T(8,128)(2,1)S(1)} %pad_maximum_fusion.24), channel_id=1, source_target_pairs={{0,6},{2,4},{4,2},{6,0},{8,14},{10,12},{12,10},{14,8},{1,7},{3,5},... | collective-permute-start | bytes 589832 | tf_op jit(solution)/shard_map/ppermute | solution.py:206
  204.5 15.1 %collective-permute-start.50 = (bf16[4,64,1536]{2,1,0:T(8,128)(2,1)S(1)}, bf16[4,64,1536]{2,1,0:T(8,128)(2,1)S(1)}, u32[]{:S(2)}, u32[]{:S(2)}) collective-permute-start(bf16[4,64,1536]{2,1,0:T(8,128)(2,1)S(1)} %get-tuple-element.162), channel_id=1, source_target_pairs={{0,1},{1,0},{2,3},{3,2},{4,5},{5,4},{6,7},{7,6},{8,9},{9,8},{10,11... | collective-permute-start | bytes 2359304 | tf_op jit(solution)/shard_map/ppermute | solution.py:209
  206.1 8.1 %collective-permute-start.58 = (bf16[64,1536]{1,0:T(8,128)(2,1)}, bf16[64,1536]{1,0:T(8,128)(2,1)}, u32[]{:S(2)}, u32[]{:S(2)}) collective-permute-start(bf16[64,1536]{1,0:T(8,128)(2,1)} %get-tuple-element.232), channel_id=1, source_target_pairs={{0,4},{2,6},{4,0},{6,2},{8,12},{10,14},{12,8},{14,10},{1,5},{3,7},... | collective-permute-start | bytes 589832 | tf_op jit(solution)/shard_map/ppermute | solution.py:206
  206.1 12.3 %collective-permute-start.59 = (bf16[64,1536]{1,0:T(8,128)(2,1)}, bf16[64,1536]{1,0:T(8,128)(2,1)}, u32[]{:S(2)}, u32[]{:S(2)}) collective-permute-start(bf16[64,1536]{1,0:T(8,128)(2,1)} %get-tuple-element.232), channel_id=1, source_target_pairs={{0,6},{2,4},{4,2},{6,0},{8,14},{10,12},{12,10},{14,8},{1,7},{3,5},... | collective-permute-start | bytes 589832 | tf_op jit(solution)/shard_map/ppermute | solution.py:206
  219.5 9.0 %collective-permute-start.60 = (bf16[4,64,1536]{2,1,0:T(8,128)(2,1)S(1)}, bf16[4,64,1536]{2,1,0:T(8,128)(2,1)S(1)}, u32[]{:S(2)}, u32[]{:S(2)}) collective-permute-start(bf16[4,64,1536]{2,1,0:T(8,128)(2,1)S(1)} %get-tuple-element.160), channel_id=1, source_target_pairs={{0,1},{1,0},{2,3},{3,2},{4,5},{5,4},{6,7},{7,6},{8,9},{9,8},{10,11... | collective-permute-start | bytes 2359304 | tf_op jit(solution)/shard_map/ppermute | solution.py:209
  223.0 9.1 %collective-permute-start.54 = (bf16[128,512]{1,0:T(8,128)(2,1)S(1)}, bf16[128,512]{1,0:T(8,128)(2,1)S(1)}, u32[]{:S(2)}, u32[]{:S(2)}) collective-permute-start(bf16[128,512]{1,0:T(8,128)(2,1)S(1)} %get-tuple-element.185), channel_id=1, source_target_pairs={{0,2},{2,0},{4,6},{6,4},{8,10},{10,8},{12,14},{14,12},{1,3},{3,1},... | collective-permute-start | bytes 393224 | tf_op jit(solution)/shard_map/ppermute | solution.py:206
  223.8 11.3 %collective-permute-start.55 = (bf16[128,512]{1,0:T(8,128)(2,1)S(1)}, bf16[128,512]{1,0:T(8,128)(2,1)S(1)}, u32[]{:S(2)}, u32[]{:S(2)}) collective-permute-start(bf16[128,512]{1,0:T(8,128)(2,1)S(1)} %get-tuple-element.184), channel_id=1, source_target_pairs={{0,4},{2,6},{4,0},{6,2},{8,12},{10,14},{12,8},{14,10},{1,5},{3,7},... | collective-permute-start | bytes 393224 | tf_op jit(solution)/shard_map/ppermute | solution.py:206
  224.2 11.8 %collective-permute-start.56 = (bf16[128,512]{1,0:T(8,128)(2,1)S(1)}, bf16[128,512]{1,0:T(8,128)(2,1)S(1)}, u32[]{:S(2)}, u32[]{:S(2)}) collective-permute-start(bf16[128,512]{1,0:T(8,128)(2,1)S(1)} %get-tuple-element.183), channel_id=1, source_target_pairs={{0,6},{2,4},{4,2},{6,0},{8,14},{10,12},{12,10},{14,8},{1,7},{3,5},... | collective-permute-start | bytes 393224 | tf_op jit(solution)/shard_map/ppermute | solution.py:206
  227.7 8.6 %collective-permute-start.51 = (bf16[512,128]{1,0:T(8,128)(2,1)S(1)}, bf16[512,128]{1,0:T(8,128)(2,1)S(1)}, u32[]{:S(2)}, u32[]{:S(2)}) collective-permute-start(bf16[512,128]{1,0:T(8,128)(2,1)S(1)} %get-tuple-element.189), channel_id=1, source_target_pairs={{0,2},{2,0},{4,6},{6,4},{8,10},{10,8},{12,14},{14,12},{1,3},{3,1},... | collective-permute-start | bytes 393224 | tf_op jit(solution)/shard_map/ppermute | solution.py:206
  228.5 10.2 %collective-permute-start.52 = (bf16[512,128]{1,0:T(8,128)(2,1)S(1)}, bf16[512,128]{1,0:T(8,128)(2,1)S(1)}, u32[]{:S(2)}, u32[]{:S(2)}) collective-permute-start(bf16[512,128]{1,0:T(8,128)(2,1)S(1)} %get-tuple-element.188), channel_id=1, source_target_pairs={{0,4},{2,6},{4,0},{6,2},{8,12},{10,14},{12,8},{14,10},{1,5},{3,7},... | collective-permute-start | bytes 393224 | tf_op jit(solution)/shard_map/ppermute | solution.py:206
  235.2 8.5 %collective-permute-start.64 = (bf16[512,128]{1,0:T(8,128)(2,1)S(1)}, bf16[512,128]{1,0:T(8,128)(2,1)S(1)}, u32[]{:S(2)}, u32[]{:S(2)}) collective-permute-start(bf16[512,128]{1,0:T(8,128)(2,1)S(1)} %get-tuple-element.171), channel_id=1, source_target_pairs={{0,2},{2,0},{4,6},{6,4},{8,10},{10,8},{12,14},{14,12},{1,3},{3,1},... | collective-permute-start | bytes 393224 | tf_op jit(solution)/shard_map/ppermute | solution.py:206
  236.0 9.1 %collective-permute-start.65 = (bf16[512,128]{1,0:T(8,128)(2,1)S(1)}, bf16[512,128]{1,0:T(8,128)(2,1)S(1)}, u32[]{:S(2)}, u32[]{:S(2)}) collective-permute-start(bf16[512,128]{1,0:T(8,128)(2,1)S(1)} %get-tuple-element.173), channel_id=1, source_target_pairs={{0,4},{2,6},{4,0},{6,2},{8,12},{10,14},{12,8},{14,10},{1,5},{3,7},... | collective-permute-start | bytes 393224 | tf_op jit(solution)/shard_map/ppermute | solution.py:206
  236.3 9.5 %collective-permute-start.66 = (bf16[512,128]{1,0:T(8,128)(2,1)S(1)}, bf16[512,128]{1,0:T(8,128)(2,1)S(1)}, u32[]{:S(2)}, u32[]{:S(2)}) collective-permute-start(bf16[512,128]{1,0:T(8,128)(2,1)S(1)} %get-tuple-element.172), channel_id=1, source_target_pairs={{0,6},{2,4},{4,2},{6,0},{8,14},{10,12},{12,10},{14,8},{1,7},{3,5},... | collective-permute-start | bytes 393224 | tf_op jit(solution)/shard_map/ppermute | solution.py:206
  239.5 8.9 %collective-permute-start.61 = (bf16[128,512]{1,0:T(8,128)(2,1)S(1)}, bf16[128,512]{1,0:T(8,128)(2,1)S(1)}, u32[]{:S(2)}, u32[]{:S(2)}) collective-permute-start(bf16[128,512]{1,0:T(8,128)(2,1)S(1)} %get-tuple-element.174), channel_id=1, source_target_pairs={{0,2},{2,0},{4,6},{6,4},{8,10},{10,8},{12,14},{14,12},{1,3},{3,1},... | collective-permute-start | bytes 393224 | tf_op jit(solution)/shard_map/ppermute | solution.py:206
  240.3 8.1 %collective-permute-start.62 = (bf16[128,512]{1,0:T(8,128)(2,1)S(1)}, bf16[128,512]{1,0:T(8,128)(2,1)S(1)}, u32[]{:S(2)}, u32[]{:S(2)}) collective-permute-start(bf16[128,512]{1,0:T(8,128)(2,1)S(1)} %get-tuple-element.176), channel_id=1, source_target_pairs={{0,4},{2,6},{4,0},{6,2},{8,12},{10,14},{12,8},{14,10},{1,5},{3,7},... | collective-permute-start | bytes 393224 | tf_op jit(solution)/shard_map/ppermute | solution.py:206
  (62 other events, 530.8 us)

commit v11 on v10

--- a/solution.py
+++ b/solution.py
@@ -264,8 +264,7 @@
 
         return quarters(q % 2), to_peer(quarters(1 - q % 2), 1)
 
-    def by_half(mine, theirs):
-        v = jnp.concatenate([mine, theirs], axis=0)
+    def by_half(v):
         mine = lax.dynamic_slice_in_dim(v, q // 2 * quarter_d, quarter_d, 1)
         return mine, lax.dynamic_slice_in_dim(v, (1 - q // 2) * quarter_d, quarter_d, 1)
 
@@ -383,19 +382,26 @@
         return jnp.stack([part, theirs]).reshape(-1, latent)
 
     tok_mine, tok_theirs = pair_rows(tokens)
-    down_half = join_quarters(square_weight(down_weight))
-    down_theirs = swap_features(down_half)
-    first = (tok_theirs, down_theirs)
+    mine, other = by_half(tok_mine)
+    far = far_rows(mine, other)
+    down_half = square_weight(down_weight)
+    first = (tok_theirs, *down_half[1:])
     up_mine, up_theirs = first_weight(after(up_weight, *first))
     cot_mine, cot_theirs = pair_rows(after(cotangent, *first))
-    tok_mine, other = by_half(tok_mine, tok_theirs)
-    tok_far = far_rows(tok_mine, other)
+    mine2, other2 = by_half(tok_theirs)
+    near = to_peer(jnp.concatenate([other, other2], axis=0), 2)
+    far2 = far_rows(after(mine2, *far[-1]), after(other2, *far[-1]))
+    down_half = join_quarters(down_half)
+    down_theirs = swap_features(down_half)
     up_mine, up_theirs = second_weight(up_mine, up_theirs)
-    cot_mine, cot_other = by_half(cot_mine, cot_theirs)
-    near, far, far2, down_theirs, up_theirs, cot_other = together(
-        to_peer(other, 2), *tok_far[-1], down_theirs, up_theirs, to_peer(cot_other, 2)
-    )
-    token_parts = join_pairs([(tok_mine, near), *tok_far[:-1], (far, far2)])
+    cot_mine, cot_other = by_half(jnp.concatenate([cot_mine, cot_theirs], axis=0))
+    near, *far2[-1], down_theirs, up_theirs, cot_other = together(
+        near, *far2[-1], down_theirs, up_theirs, to_peer(cot_other, 2)
+    )
+    token_parts = [(mine, mine2, near)] + [
+        (a[0], b[0], a[1], b[1]) for a, b in zip(far, far2)
+    ]
+    token_parts = join_pairs(token_parts)
     cot_rows = jnp.concatenate([cot_mine, cot_other], axis=0)
     down_own = all_features(down_half, down_theirs)
     up_halves = gather_h(join_steps(up_mine, up_theirs))
@@ -417,19 +423,16 @@
     part_y = jnp.stack(gather_h(part_y))
     part_x = after(part_x, part_y)
     latent_in = rows_with(part_x, t_swap(part_x))
-    down_far = gather_h(after(down_half, part_x))[1:]
     cot_first = gather_h(after(cot_rows[: 2 * tok_rows], part_x))
 
     hs, cp, cu, out_part = forward(
         latent_in, gate_blocks(gate_columns), gate_proj, up_proj, down_rows
     )
     part_y = exchange(lambda r: part_y)
-    *part_y, down_far[-1], cot_first[-1], out_part = together(
-        *part_y, down_far[-1], cot_first[-1], out_part
-    )
+    *part_y, cot_first[-1], out_part = together(*part_y, cot_first[-1], out_part)
     part_y = jnp.stack(part_y)
     latent_grad = rows_with(part_y, t_swap(part_y))
-    down_theirs = [swap_features(v) for v in down_far]
+    down_far = gather_h(after(down_half, cot_first[-1]))[1:]
     cot_second = gather_h(after(cot_rows[2 * tok_rows :], cot_first[-1]))
     out_part = sum_tensor(out_part)
     down_proj_grad = down_grads(hs, latent_grad)
@@ -438,26 +441,29 @@
         after(latent_grad, out_part), cp, cu, gate_proj, up_proj, down_rows
     )
     out_part = exchange(lambda r: out_part[r])
-    *out_part, down_theirs[-1], cot_second[-1], in_part = together(
-        *out_part, down_theirs[-1], cot_second[-1], in_part
-    )
-    down_parts = [down_own] + [all_features(v, w) for v, w in zip(down_far, down_theirs)]
+    *out_part, down_far[-1], cot_second[-1], in_part = together(
+        *out_part, down_far[-1], cot_second[-1], in_part
+    )
+    down_theirs = [swap_features(v) for v in down_far]
     cot_parts = join_pairs(zip(cot_first, cot_second))
     out_part = add(*out_part)
     in_part = sum_tensor(after(in_part, out_part))
     gate_proj_grad, up_proj_grad = input_grads(latent_in, after(dpu, in_part))
     in_part = exchange(lambda r: in_part[r])
-    *in_part, out_theirs, gate_proj_grad = together(
-        *in_part, sum_squares(out_part)[1], gate_proj_grad
-    )
+    *in_part, out_theirs, down_theirs[-1], gate_proj_grad = together(
+        *in_part, sum_squares(out_part)[1], down_theirs[-1], gate_proj_grad
+    )
+    down_parts = [down_own] + [all_features(v, w) for v, w in zip(down_far, down_theirs)]
     out_part = join_squares(out_part, out_theirs)
     in_part, in_theirs = sum_squares(add(*in_part))
     out_part = exchange(lambda r: out_part)
     *out_part, in_theirs = together(*out_part, in_theirs)
     out_part = jnp.stack(out_part)
     in_part = join_squares(in_part, in_theirs)
-    in_part = jnp.stack(exchange(lambda r: in_part))
-    out_sent = send_products(*products(square_blocks(out_part), cot_parts, up_parts))
+    in_part = exchange(lambda r: in_part)
+    out_products = products(square_blocks(out_part), cot_parts, up_parts)
+    in_part = jnp.stack(together(*in_part, *out_products)[:4])
+    out_sent = send_products(*out_products)
     in_products = products(square_blocks(in_part), token_parts, down_parts)
     received = together(*out_sent[0], *out_sent[1], *in_products)
     out, up_grad = join_products(received[:4], received[4:8])

time: 252 us -> 241 us (0.956)
  waiting for transfers between devices: 103 us -> 92 us
  starting transfers between devices: 71.1 us -> 74.8 us
  other arithmetic: 12.7 us -> 9.3 us
    ppermute x45, waiting for transfers between devices: 77 us -> 63.1 us  [to_peer(): return lax.ppermute(v, 'expert', [(e, e ^ r) for e in range(n_expert)])]
    ppermute x2 -> x4, waiting for transfers between devices: 2.01 us -> 10.7 us  [to_square(): return lax.ppermute(v, 'expert', perm)]
    ppermute x2 -> x4, starting transfers between devices: 3.54 us -> 8.27 us  [to_square(): return lax.ppermute(v, 'expert', perm)]
    ppermute x8, waiting for transfers between devices: 18.4 us -> 14.1 us  [up(): lax.ppermute(v, 'expert', [(e, (e + 4) % n_expert) for e in range(n_exper...]
    ppermute x8, starting transfers between devices: 9.05 us -> 5.84 us  [up(): lax.ppermute(v, 'expert', [(e, (e + 4) % n_expert) for e in range(n_exper...]
    ppermute x4, waiting for transfers between devices: 2.84 us -> 0.01 us  [g_swap(): return lax.ppermute(v, 'group', [(i, i ^ 1) for i in range(n_group)])]
    unnamed x89 -> x95, local copies, waits for them, and re-layouts: 4.44 us -> 6.07 us
  transfers between devices with their start and end apart: 67 -> 69, of which waited for: 34 -> 29; matrix products, arithmetic and copies ran while one was open for 7% -> 6% of each run, Pallas kernels for 18% -> 19%
where the time goes in v11:
time: 241 us; the launch traced here: 240 us
  waiting for transfers between devices  92 us (38%)
  starting transfers between devices  74.8 us (31%)
  Pallas kernels  45.6 us (19%)
  local copies, waits for them, and re-layouts  10.8 us (4%)
  other arithmetic  9.3 us (4%)
  matrix products  5.7 us (2%)
    ppermute x45, waiting for transfers between devices, to_peer(): return lax.ppermute(v, 'expert', [(e, e ^ r) for e in range(n_expert)])  63.1 us
    ppermute x45, starting transfers between devices, to_peer(): return lax.ppermute(v, 'expert', [(e, e ^ r) for e in range(n_expert)])  55.5 us
    pallas_call x1, Pallas kernels, local(): forward(latent_in, gate_blocks(gate_columns), gate_proj, up_proj, down_rows)  15.8 us
    pallas_call x1, Pallas kernels, local(): backward(after(latent_grad, out_part), cp, cu, gate_proj, up_proj, down_r...  15.7 us
    ppermute x8, waiting for transfers between devices, up(): lax.ppermute(v, 'expert', [(e, (e + 4) % n_expert) for e in range(n_exper...  14.1 us
    ppermute x4, waiting for transfers between devices, to_square(): return lax.ppermute(v, 'expert', perm)  10.7 us
    pallas_call x1, Pallas kernels, local(): gate_proj_grad, up_proj_grad = input_grads(latent_in, after(dpu, in_part))  9.04 us
    ppermute x4, starting transfers between devices, to_square(): return lax.ppermute(v, 'expert', perm)  8.27 us
  transfers between devices with their start and end apart: 69, of which 29 were waited for; matrix products, arithmetic and copies ran while one was open for 6% of the time, Pallas kernels for 19%

profile of v11, /device:TPU:0, one launch (start us, length us, event | category | flops | bytes accessed | tf_op | source)
XLA Modules:
  0.0 240.1 jit_solution(3819333329090403610)
XLA Ops:
  1.6 3.0 %collective-permute-start.1 = (bf16[256,128]{1,0:T(8,128)(2,1)S(1)}, bf16[256,128]{1,0:T(8,128)(2,1)S(1)}, u32[]{:S(2)}, u32[]{:S(2)}) collective-permute-start(bf16[256,128]{1,0:T(8,128)(2,1)S(1)} %get-tuple-element.222), channel_id=1, source_target_pairs={{0,2},{2,0},{4,6},{6,4},{8,10},{10,8},{12,14},{14,12},{1,3},{3,1},... | collective-permute-start | bytes 196616 | tf_op jit(solution)/shard_map/ppermute | solution.py:206
  4.6 1.6 collective-permute-start.2
  7.4 2.0 collective-permute-start
  9.5 2.7 %collective-permute-start.6 = (bf16[128,512]{1,0:T(8,128)(2,1)S(1)}, bf16[128,512]{1,0:T(8,128)(2,1)S(1)}, u32[]{:S(2)}, u32[]{:S(2)}) collective-permute-start(bf16[128,512]{1,0:T(8,128)(2,1)S(1)} %get-tuple-element.241), channel_id=1, source_target_pairs={{0,8},{2,10},{4,12},{6,14},{8,0},{10,2},{12,4},{14,6},{1,9},{3,11}... | collective-permute-start | bytes 393224 | tf_op jit(solution)/shard_map/ppermute | solution.py:257
  14.5 1.6 collective-permute-start.10
  18.5 2.9 %collective-permute-done.6 = bf16[128,512]{1,0:T(8,128)(2,1)S(1)} collective-permute-done((bf16[128,512]{1,0:T(8,128)(2,1)S(1)}, bf16[128,512]{1,0:T(8,128)(2,1)S(1)}, u32[]{:S(2)}, u32[]{:S(2)}) %collective-permute-start.6) | collective-permute-done | bytes 131104 | tf_op jit(solution)/shard_map/ppermute | solution.py:257
  21.4 2.5 %collective-permute-start.9 = (bf16[128,512]{1,0:T(8,128)(2,1)S(1)}, bf16[128,512]{1,0:T(8,128)(2,1)S(1)}, u32[]{:S(2)}, u32[]{:S(2)}) collective-permute-start(bf16[128,512]{1,0:T(8,128)(2,1)S(1)} %get-tuple-element.79), channel_id=1, source_target_pairs={{0,12},{2,14},{4,8},{6,10},{8,4},{10,6},{12,0},{14,2},{1,13},{3,15... | collective-permute-start | bytes 393224 | tf_op jit(solution)/shard_map/ppermute | solution.py:257
  23.9 1.8 collective-permute-start.8
  26.5 1.5 collective-permute-start.13
  28.6 7.8 %collective-permute-done.8 = bf16[128,512]{1,0:T(8,128)(2,1)S(1)} collective-permute-done((bf16[128,512]{1,0:T(8,128)(2,1)S(1)}, bf16[128,512]{1,0:T(8,128)(2,1)S(1)}, u32[]{:S(2)}, u32[]{:S(2)}) %collective-permute-start.8) | collective-permute-done | bytes 131104 | tf_op jit(solution)/shard_map/ppermute | solution.py:257
  37.8 4.5 %collective-permute-done.13 = bf16[256,512]{1,0:T(8,128)(2,1)S(1)} collective-permute-done((bf16[256,512]{1,0:T(8,128)(2,1)S(1)}, bf16[256,512]{1,0:T(8,128)(2,1)S(1)}, u32[]{:S(2)}, u32[]{:S(2)}) %collective-permute-start.13) | collective-permute-done | bytes 262176 | tf_op jit(solution)/shard_map/ppermute | solution.py:206
  46.6 1.5 collective-permute-start.24
  48.8 2.5 %collective-permute-start.16 = (bf16[2,64,512]{2,1,0:T(8,128)(2,1)S(1)}, bf16[2,64,512]{2,1,0:T(8,128)(2,1)S(1)}, u32[]{:S(2)}, u32[]{:S(2)}) collective-permute-start(bf16[2,64,512]{2,1,0:T(8,128)(2,1)S(1)} %get-tuple-element.209), channel_id=1, source_target_pairs={{0,4},{2,6},{4,0},{6,2},{8,12},{10,14},{12,8},{14,10},{1,5},{3,7},... | collective-permute-start | bytes 393224 | tf_op jit(solution)/shard_map/ppermute | solution.py:206
  52.3 7.8 %collective-permute-done.18 = bf16[256,512]{1,0:T(8,128)(2,1)S(1)} collective-permute-done((bf16[256,512]{1,0:T(8,128)(2,1)S(1)}, bf16[256,512]{1,0:T(8,128)(2,1)S(1)}, u32[]{:S(2)}, u32[]{:S(2)}) %collective-permute-start.18) | collective-permute-done | bytes 262176 | tf_op jit(solution)/shard_map/ppermute | solution.py:215
  60.1 2.8 %collective-permute-done.17 = bf16[2,64,512]{2,1,0:T(8,128)(2,1)S(1)} collective-permute-done((bf16[2,64,512]{2,1,0:T(8,128)(2,1)S(1)}, bf16[2,64,512]{2,1,0:T(8,128)(2,1)S(1)}, u32[]{:S(2)}, u32[]{:S(2)}) %collective-permute-start.17) | collective-permute-done | bytes 131104 | tf_op jit(solution)/shard_map/ppermute | solution.py:206
  64.7 6.2 %collective-permute-done.19 = bf16[2,64,512]{2,1,0:T(8,128)(2,1)S(1)} collective-permute-done((bf16[2,64,512]{2,1,0:T(8,128)(2,1)S(1)}, bf16[2,64,512]{2,1,0:T(8,128)(2,1)S(1)}, u32[]{:S(2)}, u32[]{:S(2)}) %collective-permute-start.19) | collective-permute-done | bytes 131104 | tf_op jit(solution)/shard_map/ppermute | solution.py:215
  73.2 1.7 collective-permute-done.25
  76.5 2.3 collective-permute-start.28
  80.8 1.6 collective-permute-start.23
  82.8 3.0 %collective-permute-done.28 = bf16[64,1024]{1,0:T(8,128)(2,1)S(1)} collective-permute-done((bf16[64,1024]{1,0:T(8,128)(2,1)S(1)}, bf16[64,1024]{1,0:T(8,128)(2,1)S(1)}, u32[]{:S(2)}, u32[]{:S(2)}) %collective-permute-start.28) | collective-permute-done | bytes 131104 | tf_op jit(solution)/shard_map/ppermute | solution.py:206
  86.6 2.6 %collective-permute-done.21 = bf16[2,64,1024]{2,1,0:T(8,128)(2,1)S(1)} collective-permute-done((bf16[2,64,1024]{2,1,0:T(8,128)(2,1)S(1)}, bf16[2,64,1024]{2,1,0:T(8,128)(2,1)S(1)}, u32[]{:S(2)}, u32[]{:S(2)}) %collective-permute-start.21) | collective-permute-done | bytes 262176 | tf_op jit(solution)/shard_map/ppermute | solution.py:206
  89.2 4.9 %collective-permute-done.22 = bf16[2,64,1024]{2,1,0:T(8,128)(2,1)S(1)} collective-permute-done((bf16[2,64,1024]{2,1,0:T(8,128)(2,1)S(1)}, bf16[2,64,1024]{2,1,0:T(8,128)(2,1)S(1)}, u32[]{:S(2)}, u32[]{:S(2)}) %collective-permute-start.22) | collective-permute-done | bytes 262176 | tf_op jit(solution)/shard_map/ppermute | solution.py:206
  94.1 4.7 %collective-permute-done.23 = bf16[2,64,1024]{2,1,0:T(8,128)(2,1)S(1)} collective-permute-done((bf16[2,64,1024]{2,1,0:T(8,128)(2,1)S(1)}, bf16[2,64,1024]{2,1,0:T(8,128)(2,1)S(1)}, u32[]{:S(2)}, u32[]{:S(2)}) %collective-permute-start.23) | collective-permute-done | bytes 262176 | tf_op jit(solution)/shard_map/ppermute | solution.py:206
  101.2 2.3 collective-permute-start.32
  104.5 15.8 %shard_map.144 = (bf16[1024,1536]{1,0:T(8,128)(2,1)S(1)}, bf16[1024,1536]{1,0:T(8,128)(2,1)S(1)}, bf16[1024,1536]{1,0:T(8,128)(2,1)}, bf16[1024,1024]{1,0:T(8,128)(2,1)S(1)}) custom-call(bf16[1024,1024]{1,0:T(8,128)(2,1)S(1)} %bitcast.203, f32[2,1024,2]{2,1,0:T(8,128)S(1)} %bitcast.207, bf16[4,1024,384]{2,1,0:T(8,128)(2,1)} %wg_ref.3, ...), custom_call_target="tpu_custom_call" | custom-call | flops 9663676416 | bytes 23068672 | tf_op jit(solution)/shard_map/pallas_call | solution.py:428
  123.5 1.6 collective-permute-start.40
  125.3 5.0 %shard_map.145 = bf16[1536,1024]{1,0:T(8,128)(2,1)} custom-call(bf16[1024,1536]{1,0:T(8,128)(2,1)S(1)} %get-tuple-element.100.hs_ref, bf16[1024,1024]{1,0:T(8,128)(2,1)S(1)} %bitcast.205), custom_call_target="tpu_custom_call" | custom-call | flops 3221225472 | bytes 8388608 | tf_op jit(solution)/shard_map/pallas_call | solution.py:438
  132.8 1.6 collective-permute-start.39
  134.4 15.7 %shard_map.146 = (bf16[1024,3072]{1,0:T(8,128)(2,1)}, bf16[1024,1024]{1,0:T(8,128)(2,1)S(1)}) custom-call(bf16[1024,1024]{1,0:T(8,128)(2,1)S(1)} %bitcast.206, bf16[1024,1536]{1,0:T(8,128)(2,1)S(1)} %get-tuple-element.108.cp_ref, bf16[1024,1536]{1,0:T(8,128)(2,1)S(1)} %copy-done.2, bf16[4,1024,384]{2,1,0:T(8,128)(2,1)S(1)} %copy-done, ...), custom_call_target="tpu_custom_call" | custom-call | flops 9663676416 | bytes 26214400 | tf_op jit(solution)/shard_map/pallas_call | solution.py:440
  150.1 2.0 collective-permute-done.38
  152.2 4.2 %collective-permute-done.39 = bf16[2,64,1024]{2,1,0:T(8,128)(2,1)S(1)} collective-permute-done((bf16[2,64,1024]{2,1,0:T(8,128)(2,1)S(1)}, bf16[2,64,1024]{2,1,0:T(8,128)(2,1)S(1)}, u32[]{:S(2)}, u32[]{:S(2)}) %collective-permute-start.39) | collective-permute-done | bytes 262176 | tf_op jit(solution)/shard_map/ppermute | solution.py:206
  157.1 2.4 collective-permute-done.42
  161.6 1.9 collective-permute-start.45
  163.5 9.0 %shard_map.147 = (bf16[4,1024,384]{2,1,0:T(8,128)(2,1)}, bf16[4,1024,384]{2,1,0:T(8,128)(2,1)}) custom-call(bf16[1024,1024]{1,0:T(8,128)(2,1)S(1)} %bitcast.204, bf16[1024,3072]{1,0:T(8,128)(2,1)S(1)} %copy-done.1), custom_call_target="tpu_custom_call" | custom-call | flops 6442450944 | bytes 14680064 | tf_op jit(solution)/shard_map/pallas_call | solution.py:451
  172.6 3.1 %collective-permute-done.44 = bf16[2,64,1024]{2,1,0:T(8,128)(2,1)S(1)} collective-permute-done((bf16[2,64,1024]{2,1,0:T(8,128)(2,1)S(1)}, bf16[2,64,1024]{2,1,0:T(8,128)(2,1)S(1)}, u32[]{:S(2)}, u32[]{:S(2)}) %collective-permute-start.44) | collective-permute-done | bytes 262176 | tf_op jit(solution)/shard_map/ppermute | solution.py:206
  175.7 5.0 %collective-permute-done.45 = bf16[2,64,1024]{2,1,0:T(8,128)(2,1)S(1)} collective-permute-done((bf16[2,64,1024]{2,1,0:T(8,128)(2,1)S(1)}, bf16[2,64,1024]{2,1,0:T(8,128)(2,1)S(1)}, u32[]{:S(2)}, u32[]{:S(2)}) %collective-permute-start.45) | collective-permute-done | bytes 262176 | tf_op jit(solution)/shard_map/ppermute | solution.py:206
  182.1 2.3 collective-permute-start.49
  184.7 3.0 %collective-permute-done.48 = bf16[64,1536]{1,0:T(8,128)(2,1)S(1)} collective-permute-done((bf16[64,1536]{1,0:T(8,128)(2,1)S(1)}, bf16[64,1536]{1,0:T(8,128)(2,1)S(1)}, u32[]{:S(2)}, u32[]{:S(2)}) %collective-permute-start.48) | collective-permute-done | bytes 196640 | tf_op jit(solution)/shard_map/ppermute | solution.py:206
  187.6 8.0 %collective-permute-done.49 = bf16[64,1536]{1,0:T(8,128)(2,1)S(1)} collective-permute-done((bf16[64,1536]{1,0:T(8,128)(2,1)S(1)}, bf16[64,1536]{1,0:T(8,128)(2,1)S(1)}, u32[]{:S(2)}, u32[]{:S(2)}) %collective-permute-start.49) | collective-permute-done | bytes 196640 | tf_op jit(solution)/shard_map/ppermute | solution.py:206
  195.6 2.4 collective-permute-done.50
  199.6 2.3 collective-permute-start.61
  207.4 3.8 %collective-permute-done.61 = bf16[64,1536]{1,0:T(8,128)(2,1)S(1)} collective-permute-done((bf16[64,1536]{1,0:T(8,128)(2,1)S(1)}, bf16[64,1536]{1,0:T(8,128)(2,1)S(1)}, u32[]{:S(2)}, u32[]{:S(2)}) %collective-permute-start.61) | collective-permute-done | bytes 196640 | tf_op jit(solution)/shard_map/ppermute | solution.py:206
  212.9 2.0 collective-permute-start.58
  220.0 2.1 collective-permute-start.55
  224.2 2.0 collective-permute-start.68
  226.2 1.6 collective-permute-done.55
  230.1 2.8 %collective-permute-start.65 = (bf16[128,512]{1,0:T(8,128)(2,1)S(1)}, bf16[128,512]{1,0:T(8,128)(2,1)S(1)}, u32[]{:S(2)}, u32[]{:S(2)}) collective-permute-start(bf16[128,512]{1,0:T(8,128)(2,1)S(1)} %get-tuple-element.187), channel_id=1, source_target_pairs={{0,6},{2,4},{4,2},{6,0},{8,14},{10,12},{12,10},{14,8},{1,7},{3,5},... | collective-permute-start | bytes 393224 | tf_op jit(solution)/shard_map/ppermute | solution.py:206
  236.0 2.3 collective-permute-done.65
  (288 shorter events, 60.7 us)
Async XLA Ops:
  1.6 10.6 %collective-permute-start.1 = (bf16[256,128]{1,0:T(8,128)(2,1)S(1)}, bf16[256,128]{1,0:T(8,128)(2,1)S(1)}, u32[]{:S(2)}, u32[]{:S(2)}) collective-permute-start(bf16[256,128]{1,0:T(8,128)(2,1)S(1)} %get-tuple-element.222), channel_id=1, source_target_pairs={{0,2},{2,0},{4,6},{6,4},{8,10},{10,8},{12,14},{14,12},{1,3},{3,1},... | collective-permute-start | bytes 196616 | tf_op jit(solution)/shard_map/ppermute | solution.py:206
  4.6 8.9 %collective-permute-start.2 = (bf16[256,128]{1,0:T(8,128)(2,1)S(1)}, bf16[256,128]{1,0:T(8,128)(2,1)S(1)}, u32[]{:S(2)}, u32[]{:S(2)}) collective-permute-start(bf16[256,128]{1,0:T(8,128)(2,1)S(1)} %get-tuple-element.223), channel_id=1, source_target_pairs={{0,4},{2,6},{4,0},{6,2},{8,12},{10,14},{12,8},{14,10},{1,5},{3,7},... | collective-permute-start | bytes 196616 | tf_op jit(solution)/shard_map/ppermute | solution.py:206
  7.4 8.7 %collective-permute-start = (bf16[128,1024]{1,0:T(8,128)(2,1)S(1)}, bf16[128,1024]{1,0:T(8,128)(2,1)S(1)}, u32[]{:S(2)}, u32[]{:S(2)}) collective-permute-start(bf16[128,1024]{1,0:T(8,128)(2,1)S(1)} %pad_maximum_fusion.14), channel_id=1, source_target_pairs={{0,2},{2,0},{4,6},{6,4},{8,10},{10,8},{12,14},{14,12},{1,3},{3,1},... | collective-permute-start | bytes 786440 | tf_op jit(solution)/shard_map/ppermute | solution.py:206
  9.5 11.9 %collective-permute-start.6 = (bf16[128,512]{1,0:T(8,128)(2,1)S(1)}, bf16[128,512]{1,0:T(8,128)(2,1)S(1)}, u32[]{:S(2)}, u32[]{:S(2)}) collective-permute-start(bf16[128,512]{1,0:T(8,128)(2,1)S(1)} %get-tuple-element.241), channel_id=1, source_target_pairs={{0,8},{2,10},{4,12},{6,14},{8,0},{10,2},{12,4},{14,6},{1,9},{3,11}... | collective-permute-start | bytes 393224 | tf_op jit(solution)/shard_map/ppermute | solution.py:257
  12.2 9.2 %collective-permute-start.7 = (bf16[128,512]{1,0:T(8,128)(2,1)S(1)}, bf16[128,512]{1,0:T(8,128)(2,1)S(1)}, u32[]{:S(2)}, u32[]{:S(2)}) collective-permute-start(bf16[128,512]{1,0:T(8,128)(2,1)S(1)} %get-tuple-element.242), channel_id=1, source_target_pairs={{0,12},{2,14},{4,8},{6,10},{8,4},{10,6},{12,0},{14,2},{1,13},{3,15... | collective-permute-start | bytes 393224 | tf_op jit(solution)/shard_map/ppermute | solution.py:257
  14.5 13.5 %collective-permute-start.10 = (bf16[256,512]{1,0:T(8,128)(2,1)S(1)}, bf16[256,512]{1,0:T(8,128)(2,1)S(1)}, u32[]{:S(2)}, u32[]{:S(2)}) collective-permute-start(bf16[256,512]{1,0:T(8,128)(2,1)S(1)} %pad_maximum_fusion.17), channel_id=1, source_target_pairs={{0,16},{16,0},{1,17},{17,1},{2,18},{18,2},{3,19},{19,3},{4,20},{20... | collective-permute-start | bytes 786440 | tf_op jit(solution)/shard_map/ppermute | solution.py:212
  16.2 9.5 %collective-permute-start.4 = (bf16[128,1024]{1,0:T(8,128)(2,1)S(1)}, bf16[128,1024]{1,0:T(8,128)(2,1)S(1)}, u32[]{:S(2)}, u32[]{:S(2)}) collective-permute-start(bf16[128,1024]{1,0:T(8,128)(2,1)S(1)} %pad_maximum_fusion.15), channel_id=1, source_target_pairs={{0,2},{2,0},{4,6},{6,4},{8,10},{10,8},{12,14},{14,12},{1,3},{3,1},... | collective-permute-start | bytes 786440 | tf_op jit(solution)/shard_map/ppermute | solution.py:206
  17.5 9.0 %collective-permute-start.11 = (bf16[2,256,128]{2,1,0:T(8,128)(2,1)S(1)}, bf16[2,256,128]{2,1,0:T(8,128)(2,1)S(1)}, u32[]{:S(2)}, u32[]{:S(2)}) collective-permute-start(bf16[2,256,128]{2,1,0:T(8,128)(2,1)S(1)} %pad_maximum_fusion.26), channel_id=1, source_target_pairs={{0,4},{2,6},{4,0},{6,2},{8,12},{10,14},{12,8},{14,10},{1,5},{3,7},... | collective-permute-start | bytes 393224 | tf_op jit(solution)/shard_map/ppermute | solution.py:206
  23.9 12.6 %collective-permute-start.8 = (bf16[128,512]{1,0:T(8,128)(2,1)S(1)}, bf16[128,512]{1,0:T(8,128)(2,1)S(1)}, u32[]{:S(2)}, u32[]{:S(2)}) collective-permute-start(bf16[128,512]{1,0:T(8,128)(2,1)S(1)} %get-tuple-element.78), channel_id=1, source_target_pairs={{0,8},{2,10},{4,12},{6,14},{8,0},{10,2},{12,4},{14,6},{1,9},{3,11}... | collective-permute-start | bytes 393224 | tf_op jit(solution)/shard_map/ppermute | solution.py:257
  25.7 12.1 %collective-permute-start.5 = (bf16[256,512]{1,0:T(8,128)(2,1)S(1)}, bf16[256,512]{1,0:T(8,128)(2,1)S(1)}, u32[]{:S(2)}, u32[]{:S(2)}) collective-permute-start(bf16[256,512]{1,0:T(8,128)(2,1)S(1)} %pad_maximum_fusion.16), channel_id=1, source_target_pairs={{0,4},{2,6},{4,0},{6,2},{8,12},{10,14},{12,8},{14,10},{1,5},{3,7},... | collective-permute-start | bytes 786440 | tf_op jit(solution)/shard_map/ppermute | solution.py:206
  26.5 15.9 %collective-permute-start.13 = (bf16[256,512]{1,0:T(8,128)(2,1)S(1)}, bf16[256,512]{1,0:T(8,128)(2,1)S(1)}, u32[]{:S(2)}, u32[]{:S(2)}) collective-permute-start(bf16[256,512]{1,0:T(8,128)(2,1)S(1)} %get-tuple-element.213), channel_id=1, source_target_pairs={{0,4},{2,6},{4,0},{6,2},{8,12},{10,14},{12,8},{14,10},{1,5},{3,7},... | collective-permute-start | bytes 786440 | tf_op jit(solution)/shard_map/ppermute | solution.py:206
  28.1 8.4 %collective-permute-start.12 = (bf16[256,256]{1,0:T(8,128)(2,1)S(1)}, bf16[256,256]{1,0:T(8,128)(2,1)S(1)}, u32[]{:S(2)}, u32[]{:S(2)}) collective-permute-start(bf16[256,256]{1,0:T(8,128)(2,1)S(1)} %get-tuple-element.240), channel_id=1, source_target_pairs={{0,2},{2,0},{4,6},{6,4},{8,10},{10,8},{12,14},{14,12},{1,3},{3,1},... | collective-permute-start | bytes 393224 | tf_op jit(solution)/shard_map/ppermute | solution.py:206
  45.3 14.8 %collective-permute-start.18 = (bf16[256,512]{1,0:T(8,128)(2,1)S(1)}, bf16[256,512]{1,0:T(8,128)(2,1)S(1)}, u32[]{:S(2)}, u32[]{:S(2)}) collective-permute-start(bf16[256,512]{1,0:T(8,128)(2,1)S(1)} %pad_maximum_fusion.19), channel_id=1, source_target_pairs={{0,8},{2,10},{4,12},{6,14},{8,0},{10,2},{12,4},{14,6},{1,9},{3,11}... | collective-permute-start | bytes 786440 | tf_op jit(solution)/shard_map/ppermute | solution.py:215
  46.6 17.3 %collective-permute-start.24 = (bf16[256,512]{1,0:T(8,128)(2,1)S(1)}, bf16[256,512]{1,0:T(8,128)(2,1)S(1)}, u32[]{:S(2)}, u32[]{:S(2)}) collective-permute-start(bf16[256,512]{1,0:T(8,128)(2,1)S(1)} %pad_maximum_fusion.19), channel_id=1, source_target_pairs={{0,16},{16,0},{1,17},{17,1},{2,18},{18,2},{3,19},{19,3},{4,20},{20... | collective-permute-start | bytes 786440 | tf_op jit(solution)/shard_map/ppermute | solution.py:212
  48.3 11.8 %collective-permute-start.15 = (bf16[2,64,512]{2,1,0:T(8,128)(2,1)S(1)}, bf16[2,64,512]{2,1,0:T(8,128)(2,1)S(1)}, u32[]{:S(2)}, u32[]{:S(2)}) collective-permute-start(bf16[2,64,512]{2,1,0:T(8,128)(2,1)S(1)} %get-tuple-element.210), channel_id=1, source_target_pairs={{0,2},{2,0},{4,6},{6,4},{8,10},{10,8},{12,14},{14,12},{1,3},{3,1},... | collective-permute-start | bytes 393224 | tf_op jit(solution)/shard_map/ppermute | solution.py:206
  48.8 11.3 %collective-permute-start.16 = (bf16[2,64,512]{2,1,0:T(8,128)(2,1)S(1)}, bf16[2,64,512]{2,1,0:T(8,128)(2,1)S(1)}, u32[]{:S(2)}, u32[]{:S(2)}) collective-permute-start(bf16[2,64,512]{2,1,0:T(8,128)(2,1)S(1)} %get-tuple-element.209), channel_id=1, source_target_pairs={{0,4},{2,6},{4,0},{6,2},{8,12},{10,14},{12,8},{14,10},{1,5},{3,7},... | collective-permute-start | bytes 393224 | tf_op jit(solution)/shard_map/ppermute | solution.py:206
  51.3 11.6 %collective-permute-start.17 = (bf16[2,64,512]{2,1,0:T(8,128)(2,1)S(1)}, bf16[2,64,512]{2,1,0:T(8,128)(2,1)S(1)}, u32[]{:S(2)}, u32[]{:S(2)}) collective-permute-start(bf16[2,64,512]{2,1,0:T(8,128)(2,1)S(1)} %get-tuple-element.208), channel_id=1, source_target_pairs={{0,6},{2,4},{4,2},{6,0},{8,14},{10,12},{12,10},{14,8},{1,7},{3,5},... | collective-permute-start | bytes 393224 | tf_op jit(solution)/shard_map/ppermute | solution.py:206
  76.5 9.4 %collective-permute-start.28 = (bf16[64,1024]{1,0:T(8,128)(2,1)S(1)}, bf16[64,1024]{1,0:T(8,128)(2,1)S(1)}, u32[]{:S(2)}, u32[]{:S(2)}) collective-permute-start(bf16[64,1024]{1,0:T(8,128)(2,1)S(1)} %get-tuple-element.206), channel_id=1, source_target_pairs={{0,6},{2,4},{4,2},{6,0},{8,14},{10,12},{12,10},{14,8},{1,7},{3,5},... | collective-permute-start | bytes 393224 | tf_op jit(solution)/shard_map/ppermute | solution.py:206
  78.8 10.4 %collective-permute-start.21 = (bf16[2,64,1024]{2,1,0:T(8,128)(2,1)S(1)}, bf16[2,64,1024]{2,1,0:T(8,128)(2,1)S(1)}, u32[]{:S(2)}, u32[]{:S(2)}) collective-permute-start(bf16[2,64,1024]{2,1,0:T(8,128)(2,1)S(1)} %get-tuple-element.230), channel_id=1, source_target_pairs={{0,2},{2,0},{4,6},{6,4},{8,10},{10,8},{12,14},{14,12},{1,3},{3,1},... | collective-permute-start | bytes 786440 | tf_op jit(solution)/shard_map/ppermute | solution.py:206
  80.1 14.0 %collective-permute-start.22 = (bf16[2,64,1024]{2,1,0:T(8,128)(2,1)S(1)}, bf16[2,64,1024]{2,1,0:T(8,128)(2,1)S(1)}, u32[]{:S(2)}, u32[]{:S(2)}) collective-permute-start(bf16[2,64,1024]{2,1,0:T(8,128)(2,1)S(1)} %get-tuple-element.230), channel_id=1, source_target_pairs={{0,4},{2,6},{4,0},{6,2},{8,12},{10,14},{12,8},{14,10},{1,5},{3,7},... | collective-permute-start | bytes 786440 | tf_op jit(solution)/shard_map/ppermute | solution.py:206
  80.8 18.0 %collective-permute-start.23 = (bf16[2,64,1024]{2,1,0:T(8,128)(2,1)S(1)}, bf16[2,64,1024]{2,1,0:T(8,128)(2,1)S(1)}, u32[]{:S(2)}, u32[]{:S(2)}) collective-permute-start(bf16[2,64,1024]{2,1,0:T(8,128)(2,1)S(1)} %get-tuple-element.230), channel_id=1, source_target_pairs={{0,6},{2,4},{4,2},{6,0},{8,14},{10,12},{12,10},{14,8},{1,7},{3,5},... | collective-permute-start | bytes 786440 | tf_op jit(solution)/shard_map/ppermute | solution.py:206
  86.0 12.9 %collective-permute-start.29 = (bf16[64,1024]{1,0:T(8,128)(2,1)S(1)}, bf16[64,1024]{1,0:T(8,128)(2,1)S(1)}, u32[]{:S(2)}, u32[]{:S(2)}) collective-permute-start(bf16[64,1024]{1,0:T(8,128)(2,1)S(1)} %get-tuple-element.250), channel_id=1, source_target_pairs={{0,8},{2,10},{4,12},{6,14},{8,0},{10,2},{12,4},{14,6},{1,9},{3,11}... | collective-permute-start | bytes 393224 | tf_op jit(solution)/shard_map/ppermute | solution.py:215
  99.9 20.4 %collective-permute-start.30 = (bf16[2,64,1024]{2,1,0:T(8,128)(2,1)S(1)}, bf16[2,64,1024]{2,1,0:T(8,128)(2,1)S(1)}, u32[]{:S(2)}, u32[]{:S(2)}) collective-permute-start(bf16[2,64,1024]{2,1,0:T(8,128)(2,1)S(1)} %pad_maximum_fusion.21), channel_id=1, source_target_pairs={{0,2},{2,0},{4,6},{6,4},{8,10},{10,8},{12,14},{14,12},{1,3},{3,1},... | collective-permute-start | bytes 786440 | tf_op jit(solution)/shard_map/ppermute | solution.py:206
  101.1 19.1 %collective-permute-start.31 = (bf16[2,64,1024]{2,1,0:T(8,128)(2,1)S(1)}, bf16[2,64,1024]{2,1,0:T(8,128)(2,1)S(1)}, u32[]{:S(2)}, u32[]{:S(2)}) collective-permute-start(bf16[2,64,1024]{2,1,0:T(8,128)(2,1)S(1)} %pad_maximum_fusion.21), channel_id=1, source_target_pairs={{0,4},{2,6},{4,0},{6,2},{8,12},{10,14},{12,8},{14,10},{1,5},{3,7},... | collective-permute-start | bytes 786440 | tf_op jit(solution)/shard_map/ppermute | solution.py:206
  101.2 19.9 %collective-permute-start.32 = (bf16[2,64,1024]{2,1,0:T(8,128)(2,1)S(1)}, bf16[2,64,1024]{2,1,0:T(8,128)(2,1)S(1)}, u32[]{:S(2)}, u32[]{:S(2)}) collective-permute-start(bf16[2,64,1024]{2,1,0:T(8,128)(2,1)S(1)} %pad_maximum_fusion.21), channel_id=1, source_target_pairs={{0,6},{2,4},{4,2},{6,0},{8,14},{10,12},{12,10},{14,8},{1,7},{3,5},... | collective-permute-start | bytes 786440 | tf_op jit(solution)/shard_map/ppermute | solution.py:206
  103.4 16.9 %collective-permute-start.33 = (bf16[256,512]{1,0:T(8,128)(2,1)}, bf16[256,512]{1,0:T(8,128)(2,1)S(1)}, u32[]{:S(2)}, u32[]{:S(2)}) collective-permute-start(bf16[256,512]{1,0:T(8,128)(2,1)} %copy-done.6), channel_id=1, source_target_pairs={{0,8},{2,10},{4,12},{6,14},{8,0},{10,2},{12,4},{14,6},{1,9},{3,11}... | collective-permute-start | bytes 786440 | tf_op jit(solution)/shard_map/ppermute | solution.py:215
  121.5 8.8 %collective-permute-start.35 = (bf16[4,2,64,1024]{3,2,1,0:T(8,128)(2,1)S(1)}, bf16[4,2,64,1024]{3,2,1,0:T(8,128)(2,1)S(1)}, u32[]{:S(2)}, u32[]{:S(2)}) collective-permute-start(bf16[4,2,64,1024]{3,2,1,0:T(8,128)(2,1)S(1)} %bitcast.223), channel_id=1, source_target_pairs={{0,1},{1,0},{2,3},{3,2},{4,5},{5,4},{6,7},{7,6},{8,9},{9,8},{10,11... | collective-permute-start | bytes 3145736 | tf_op jit(solution)/shard_map/ppermute | solution.py:209
  122.2 27.9 %collective-permute-start.41 = (bf16[256,512]{1,0:T(8,128)(2,1)S(1)}, bf16[256,512]{1,0:T(8,128)(2,1)S(1)}, u32[]{:S(2)}, u32[]{:S(2)}) collective-permute-start(bf16[256,512]{1,0:T(8,128)(2,1)S(1)} %copy-done.34), channel_id=1, source_target_pairs={{0,8},{2,10},{4,12},{6,14},{8,0},{10,2},{12,4},{14,6},{1,9},{3,11}... | collective-permute-start | bytes 786440 | tf_op jit(solution)/shard_map/ppermute | solution.py:215
  123.5 26.6 %collective-permute-start.40 = (bf16[256,512]{1,0:T(8,128)(2,1)S(1)}, bf16[256,512]{1,0:T(8,128)(2,1)S(1)}, u32[]{:S(2)}, u32[]{:S(2)}) collective-permute-start(bf16[256,512]{1,0:T(8,128)(2,1)S(1)} %copy-done.9), channel_id=1, source_target_pairs={{0,8},{2,10},{4,12},{6,14},{8,0},{10,2},{12,4},{14,6},{1,9},{3,11}... | collective-permute-start | bytes 786440 | tf_op jit(solution)/shard_map/ppermute | solution.py:215
  130.9 19.3 %collective-permute-start.37 = (bf16[2,64,1024]{2,1,0:T(8,128)(2,1)S(1)}, bf16[2,64,1024]{2,1,0:T(8,128)(2,1)S(1)}, u32[]{:S(2)}, u32[]{:S(2)}) collective-permute-start(bf16[2,64,1024]{2,1,0:T(8,128)(2,1)S(1)} %get-tuple-element.157), channel_id=1, source_target_pairs={{0,2},{2,0},{4,6},{6,4},{8,10},{10,8},{12,14},{14,12},{1,3},{3,1},... | collective-permute-start | bytes 786440 | tf_op jit(solution)/shard_map/ppermute | solution.py:206
  132.2 20.0 %collective-permute-start.38 = (bf16[2,64,1024]{2,1,0:T(8,128)(2,1)S(1)}, bf16[2,64,1024]{2,1,0:T(8,128)(2,1)S(1)}, u32[]{:S(2)}, u32[]{:S(2)}) collective-permute-start(bf16[2,64,1024]{2,1,0:T(8,128)(2,1)S(1)} %get-tuple-element.156), channel_id=1, source_target_pairs={{0,4},{2,6},{4,0},{6,2},{8,12},{10,14},{12,8},{14,10},{1,5},{3,7},... | collective-permute-start | bytes 786440 | tf_op jit(solution)/shard_map/ppermute | solution.py:206
  132.8 23.6 %collective-permute-start.39 = (bf16[2,64,1024]{2,1,0:T(8,128)(2,1)S(1)}, bf16[2,64,1024]{2,1,0:T(8,128)(2,1)S(1)}, u32[]{:S(2)}, u32[]{:S(2)}) collective-permute-start(bf16[2,64,1024]{2,1,0:T(8,128)(2,1)S(1)} %get-tuple-element.155), channel_id=1, source_target_pairs={{0,6},{2,4},{4,2},{6,0},{8,14},{10,12},{12,10},{14,8},{1,7},{3,5},... | collective-permute-start | bytes 786440 | tf_op jit(solution)/shard_map/ppermute | solution.py:206
  156.8 15.8 %collective-permute-start.46 = (bf16[2,64,1024]{2,1,0:T(8,128)(2,1)S(1)}, bf16[2,64,1024]{2,1,0:T(8,128)(2,1)S(1)}, u32[]{:S(2)}, u32[]{:S(2)}) collective-permute-start(bf16[2,64,1024]{2,1,0:T(8,128)(2,1)S(1)} %add_convert_fusion.1), channel_id=1, source_target_pairs={{0,8},{2,10},{4,12},{6,14},{8,0},{10,2},{12,4},{14,6},{1,9},{3,11}... | collective-permute-start | bytes 786440 | tf_op jit(solution)/shard_map/ppermute | solution.py:215
  156.9 15.7 %collective-permute-start.47 = (bf16[256,512]{1,0:T(8,128)(2,1)S(1)}, bf16[256,512]{1,0:T(8,128)(2,1)S(1)}, u32[]{:S(2)}, u32[]{:S(2)}) collective-permute-start(bf16[256,512]{1,0:T(8,128)(2,1)S(1)} %collective-permute-done.40), channel_id=1, source_target_pairs={{0,16},{16,0},{1,17},{17,1},{2,18},{18,2},{3,19},{19,3},{4,20},{20... | collective-permute-start | bytes 786440 | tf_op jit(solution)/shard_map/ppermute | solution.py:212
  160.0 12.6 %collective-permute-start.43 = (bf16[2,64,1024]{2,1,0:T(8,128)(2,1)S(1)}, bf16[2,64,1024]{2,1,0:T(8,128)(2,1)S(1)}, u32[]{:S(2)}, u32[]{:S(2)}) collective-permute-start(bf16[2,64,1024]{2,1,0:T(8,128)(2,1)S(1)} %get-tuple-element.153), channel_id=1, source_target_pairs={{0,2},{2,0},{4,6},{6,4},{8,10},{10,8},{12,14},{14,12},{1,3},{3,1},... | collective-permute-start | bytes 786440 | tf_op jit(solution)/shard_map/ppermute | solution.py:206
  161.0 14.7 %collective-permute-start.44 = (bf16[2,64,1024]{2,1,0:T(8,128)(2,1)S(1)}, bf16[2,64,1024]{2,1,0:T(8,128)(2,1)S(1)}, u32[]{:S(2)}, u32[]{:S(2)}) collective-permute-start(bf16[2,64,1024]{2,1,0:T(8,128)(2,1)S(1)} %get-tuple-element.152), channel_id=1, source_target_pairs={{0,4},{2,6},{4,0},{6,2},{8,12},{10,14},{12,8},{14,10},{1,5},{3,7},... | collective-permute-start | bytes 786440 | tf_op jit(solution)/shard_map/ppermute | solution.py:206
  161.6 19.1 %collective-permute-start.45 = (bf16[2,64,1024]{2,1,0:T(8,128)(2,1)S(1)}, bf16[2,64,1024]{2,1,0:T(8,128)(2,1)S(1)}, u32[]{:S(2)}, u32[]{:S(2)}) collective-permute-start(bf16[2,64,1024]{2,1,0:T(8,128)(2,1)S(1)} %get-tuple-element.151), channel_id=1, source_target_pairs={{0,6},{2,4},{4,2},{6,0},{8,14},{10,12},{12,10},{14,8},{1,7},{3,5},... | collective-permute-start | bytes 786440 | tf_op jit(solution)/shard_map/ppermute | solution.py:206
  181.0 17.0 %collective-permute-start.51 = (bf16[2,64,1024]{2,1,0:T(8,128)(2,1)S(1)}, bf16[2,64,1024]{2,1,0:T(8,128)(2,1)S(1)}, u32[]{:S(2)}, u32[]{:S(2)}) collective-permute-start(bf16[2,64,1024]{2,1,0:T(8,128)(2,1)S(1)} %add_convert_fusion), channel_id=1, source_target_pairs={{0,8},{2,10},{4,12},{6,14},{8,0},{10,2},{12,4},{14,6},{1,9},{3,11}... | collective-permute-start | bytes 786440 | tf_op jit(solution)/shard_map/ppermute | solution.py:215
  182.1 13.5 %collective-permute-start.49 = (bf16[64,1536]{1,0:T(8,128)(2,1)S(1)}, bf16[64,1536]{1,0:T(8,128)(2,1)S(1)}, u32[]{:S(2)}, u32[]{:S(2)}) collective-permute-start(bf16[64,1536]{1,0:T(8,128)(2,1)S(1)} %pad_maximum_fusion.24), channel_id=1, source_target_pairs={{0,4},{2,6},{4,0},{6,2},{8,12},{10,14},{12,8},{14,10},{1,5},{3,7},... | collective-permute-start | bytes 589832 | tf_op jit(solution)/shard_map/ppermute | solution.py:206
  184.4 13.6 %collective-permute-start.50 = (bf16[64,1536]{1,0:T(8,128)(2,1)S(1)}, bf16[64,1536]{1,0:T(8,128)(2,1)S(1)}, u32[]{:S(2)}, u32[]{:S(2)}) collective-permute-start(bf16[64,1536]{1,0:T(8,128)(2,1)S(1)} %pad_maximum_fusion.24), channel_id=1, source_target_pairs={{0,6},{2,4},{4,2},{6,0},{8,14},{10,12},{12,10},{14,8},{1,7},{3,5},... | collective-permute-start | bytes 589832 | tf_op jit(solution)/shard_map/ppermute | solution.py:206
  199.6 11.5 %collective-permute-start.61 = (bf16[64,1536]{1,0:T(8,128)(2,1)S(1)}, bf16[64,1536]{1,0:T(8,128)(2,1)S(1)}, u32[]{:S(2)}, u32[]{:S(2)}) collective-permute-start(bf16[64,1536]{1,0:T(8,128)(2,1)S(1)} %pad_maximum_fusion.25), channel_id=1, source_target_pairs={{0,6},{2,4},{4,2},{6,0},{8,14},{10,12},{12,10},{14,8},{1,7},{3,5},... | collective-permute-start | bytes 589832 | tf_op jit(solution)/shard_map/ppermute | solution.py:206
  211.4 8.6 %collective-permute-start.56 = (bf16[128,512]{1,0:T(8,128)(2,1)S(1)}, bf16[128,512]{1,0:T(8,128)(2,1)S(1)}, u32[]{:S(2)}, u32[]{:S(2)}) collective-permute-start(bf16[128,512]{1,0:T(8,128)(2,1)S(1)} %get-tuple-element.197), channel_id=1, source_target_pairs={{0,2},{2,0},{4,6},{6,4},{8,10},{10,8},{12,14},{14,12},{1,3},{3,1},... | collective-permute-start | bytes 393224 | tf_op jit(solution)/shard_map/ppermute | solution.py:206
  212.7 10.0 %collective-permute-start.57 = (bf16[128,512]{1,0:T(8,128)(2,1)S(1)}, bf16[128,512]{1,0:T(8,128)(2,1)S(1)}, u32[]{:S(2)}, u32[]{:S(2)}) collective-permute-start(bf16[128,512]{1,0:T(8,128)(2,1)S(1)} %get-tuple-element.196), channel_id=1, source_target_pairs={{0,4},{2,6},{4,0},{6,2},{8,12},{10,14},{12,8},{14,10},{1,5},{3,7},... | collective-permute-start | bytes 393224 | tf_op jit(solution)/shard_map/ppermute | solution.py:206
  212.9 11.0 %collective-permute-start.58 = (bf16[128,512]{1,0:T(8,128)(2,1)S(1)}, bf16[128,512]{1,0:T(8,128)(2,1)S(1)}, u32[]{:S(2)}, u32[]{:S(2)}) collective-permute-start(bf16[128,512]{1,0:T(8,128)(2,1)S(1)} %get-tuple-element.195), channel_id=1, source_target_pairs={{0,6},{2,4},{4,2},{6,0},{8,14},{10,12},{12,10},{14,8},{1,7},{3,5},... | collective-permute-start | bytes 393224 | tf_op jit(solution)/shard_map/ppermute | solution.py:206
  215.0 9.2 %collective-permute-start.53 = (bf16[512,128]{1,0:T(8,128)(2,1)S(1)}, bf16[512,128]{1,0:T(8,128)(2,1)S(1)}, u32[]{:S(2)}, u32[]{:S(2)}) collective-permute-start(bf16[512,128]{1,0:T(8,128)(2,1)S(1)} %get-tuple-element.201), channel_id=1, source_target_pairs={{0,2},{2,0},{4,6},{6,4},{8,10},{10,8},{12,14},{14,12},{1,3},{3,1},... | collective-permute-start | bytes 393224 | tf_op jit(solution)/shard_map/ppermute | solution.py:206
  216.3 9.9 %collective-permute-start.54 = (bf16[512,128]{1,0:T(8,128)(2,1)S(1)}, bf16[512,128]{1,0:T(8,128)(2,1)S(1)}, u32[]{:S(2)}, u32[]{:S(2)}) collective-permute-start(bf16[512,128]{1,0:T(8,128)(2,1)S(1)} %get-tuple-element.200), channel_id=1, source_target_pairs={{0,4},{2,6},{4,0},{6,2},{8,12},{10,14},{12,8},{14,10},{1,5},{3,7},... | collective-permute-start | bytes 393224 | tf_op jit(solution)/shard_map/ppermute | solution.py:206
  223.9 9.0 %collective-permute-start.67 = (bf16[512,128]{1,0:T(8,128)(2,1)S(1)}, bf16[512,128]{1,0:T(8,128)(2,1)S(1)}, u32[]{:S(2)}, u32[]{:S(2)}) collective-permute-start(bf16[512,128]{1,0:T(8,128)(2,1)S(1)} %get-tuple-element.185), channel_id=1, source_target_pairs={{0,4},{2,6},{4,0},{6,2},{8,12},{10,14},{12,8},{14,10},{1,5},{3,7},... | collective-permute-start | bytes 393224 | tf_op jit(solution)/shard_map/ppermute | solution.py:206
  224.2 9.2 %collective-permute-start.68 = (bf16[512,128]{1,0:T(8,128)(2,1)S(1)}, bf16[512,128]{1,0:T(8,128)(2,1)S(1)}, u32[]{:S(2)}, u32[]{:S(2)}) collective-permute-start(bf16[512,128]{1,0:T(8,128)(2,1)S(1)} %get-tuple-element.184), channel_id=1, source_target_pairs={{0,6},{2,4},{4,2},{6,0},{8,14},{10,12},{12,10},{14,8},{1,7},{3,5},... | collective-permute-start | bytes 393224 | tf_op jit(solution)/shard_map/ppermute | solution.py:206
  (66 other events, 536.0 us)

commit v12 on v11

--- a/solution.py
+++ b/solution.py
@@ -30,7 +30,7 @@
 ):
     step = pl.program_id(0)
     pair, _, width = wg_ref.shape
-    block = 256
+    block = 512
     join_projections(wg_ref, wu_ref, wgu)
 
     @pl.when(step == 0)
@@ -63,7 +63,7 @@
 ):
     step = pl.program_id(0)
     pair, _, width = wg_ref.shape
-    block = 256
+    block = 512
     join_projections(wg_ref, wu_ref, wgu)
 
     @pl.when(step == 0)
@@ -271,6 +271,22 @@
     def far_rows(mine, other):
         return [(to_square(mine, k, 0), to_square(other, k, 2)) for k in range(1, nh)]
 
+    def near_rows(v):
+        size = 2 * quarter_d
+        mine = lax.dynamic_slice_in_dim(v, q // 2 * size, size, 1)
+        other = lax.dynamic_slice_in_dim(v, (1 - q // 2) * size, size, 1)
+        return mine, to_peer(other, 2)
+
+    def near_quarters(mine, theirs):
+        v = jnp.concatenate([mine, theirs], axis=0)
+        mine = lax.dynamic_slice_in_dim(v, q % 2 * quarter_d, quarter_d, 1)
+        other = lax.dynamic_slice_in_dim(v, (1 - q % 2) * quarter_d, quarter_d, 1)
+        return mine, to_peer(other, 1)
+
+    def join_rows(mine, theirs):
+        parts = [v[i * tok_rows : (i + 1) * tok_rows] for i in (0, 1) for v in (mine, theirs)]
+        return jnp.concatenate(parts, axis=0)
+
     def join_pairs(parts):
         return [jnp.concatenate(v, axis=0) for v in parts]
 
@@ -387,22 +403,22 @@
     down_half = square_weight(down_weight)
     first = (tok_theirs, *down_half[1:])
     up_mine, up_theirs = first_weight(after(up_weight, *first))
-    cot_mine, cot_theirs = pair_rows(after(cotangent, *first))
+    cot_mine, cot_theirs = near_rows(after(cotangent, *down_half[1:]))
     mine2, other2 = by_half(tok_theirs)
     near = to_peer(jnp.concatenate([other, other2], axis=0), 2)
     far2 = far_rows(after(mine2, *far[-1]), after(other2, *far[-1]))
     down_half = join_quarters(down_half)
     down_theirs = swap_features(down_half)
     up_mine, up_theirs = second_weight(up_mine, up_theirs)
-    cot_mine, cot_other = by_half(jnp.concatenate([cot_mine, cot_theirs], axis=0))
+    cot_mine, cot_other = near_quarters(cot_mine, cot_theirs)
     near, *far2[-1], down_theirs, up_theirs, cot_other = together(
-        near, *far2[-1], down_theirs, up_theirs, to_peer(cot_other, 2)
+        near, *far2[-1], down_theirs, up_theirs, cot_other
     )
     token_parts = [(mine, mine2, near)] + [
         (a[0], b[0], a[1], b[1]) for a, b in zip(far, far2)
     ]
     token_parts = join_pairs(token_parts)
-    cot_rows = jnp.concatenate([cot_mine, cot_other], axis=0)
+    cot_rows = join_rows(cot_mine, cot_other)
     down_own = all_features(down_half, down_theirs)
     up_halves = gather_h(join_steps(up_mine, up_theirs))
 
@@ -435,8 +451,6 @@
     down_far = gather_h(after(down_half, cot_first[-1]))[1:]
     cot_second = gather_h(after(cot_rows[2 * tok_rows :], cot_first[-1]))
     out_part = sum_tensor(out_part)
-    down_proj_grad = down_grads(hs, latent_grad)
-    out_part = after(out_part, down_proj_grad)
     dpu, in_part = backward(
         after(latent_grad, out_part), cp, cu, gate_proj, up_proj, down_rows
     )
@@ -447,7 +461,7 @@
     down_theirs = [swap_features(v) for v in down_far]
     cot_parts = join_pairs(zip(cot_first, cot_second))
     out_part = add(*out_part)
-    in_part = sum_tensor(after(in_part, out_part))
+    in_part = sum_tensor(in_part)
     gate_proj_grad, up_proj_grad = input_grads(latent_in, after(dpu, in_part))
     in_part = exchange(lambda r: in_part[r])
     *in_part, out_theirs, down_theirs[-1], gate_proj_grad = together(
@@ -457,7 +471,8 @@
     out_part = join_squares(out_part, out_theirs)
     in_part, in_theirs = sum_squares(add(*in_part))
     out_part = exchange(lambda r: out_part)
-    *out_part, in_theirs = together(*out_part, in_theirs)
+    down_proj_grad = down_grads(hs, after(latent_grad, in_part))
+    *out_part, in_theirs, down_proj_grad = together(*out_part, in_theirs, down_proj_grad)
     out_part = jnp.stack(out_part)
     in_part = join_squares(in_part, in_theirs)
     in_part = exchange(lambda r: in_part)

time: 241 us -> 231 us (0.959)
  waiting for transfers between devices: 92 us -> 79.4 us
  starting transfers between devices: 74.8 us -> 78 us
    ppermute x45, waiting for transfers between devices: 63.1 us -> 49.5 us  [to_peer(): return lax.ppermute(v, 'expert', [(e, e ^ r) for e in range(n_expert)])]
    ppermute x8, starting transfers between devices: 5.84 us -> 12.1 us  [up(): lax.ppermute(v, 'expert', [(e, (e + 4) % n_expert) for e in range(n_exper...]
    ppermute x45, starting transfers between devices: 55.5 us -> 52.1 us  [to_peer(): return lax.ppermute(v, 'expert', [(e, e ^ r) for e in range(n_expert)])]
    ppermute x8, waiting for transfers between devices: 14.1 us -> 17.2 us  [up(): lax.ppermute(v, 'expert', [(e, (e + 4) % n_expert) for e in range(n_exper...]
    unnamed x95 -> x107, local copies, waits for them, and re-layouts: 6.07 us -> 5.29 us
  transfers between devices with their start and end apart: 69 -> 69, of which waited for: 29 -> 30; matrix products, arithmetic and copies ran while one was open for 6% -> 6% of each run, Pallas kernels for 19% -> 20%
where the time goes in v12:
time: 231 us
  waiting for transfers between devices  79.4 us (34%)
  starting transfers between devices  78 us (34%)
  Pallas kernels  45.7 us (20%)
  other arithmetic  10.3 us (4%)
  local copies, waits for them, and re-layouts  10.1 us (4%)
  matrix products  5.68 us (2%)
    ppermute x45, starting transfers between devices, to_peer(): return lax.ppermute(v, 'expert', [(e, e ^ r) for e in range(n_expert)])  52.1 us
    ppermute x45, waiting for transfers between devices, to_peer(): return lax.ppermute(v, 'expert', [(e, e ^ r) for e in range(n_expert)])  49.5 us
    ppermute x8, waiting for transfers between devices, up(): lax.ppermute(v, 'expert', [(e, (e + 4) % n_expert) for e in range(n_exper...  17.2 us
    pallas_call x1, Pallas kernels, local(): forward(latent_in, gate_blocks(gate_columns), gate_proj, up_proj, down_rows)  16 us
    pallas_call x1, Pallas kernels, local(): backward(after(latent_grad, out_part), cp, cu, gate_proj, up_proj, down_r...  15.6 us
    ppermute x8, starting transfers between devices, up(): lax.ppermute(v, 'expert', [(e, (e + 4) % n_expert) for e in range(n_exper...  12.1 us
    ppermute x4, waiting for transfers between devices, to_square(): return lax.ppermute(v, 'expert', perm)  10.4 us
    pallas_call x1, Pallas kernels, local(): gate_proj_grad, up_proj_grad = input_grads(latent_in, after(dpu, in_part))  9.03 us
  transfers between devices with their start and end apart: 69, of which 30 were waited for; matrix products, arithmetic and copies ran while one was open for 6% of the time, Pallas kernels for 20%

profile of v12, /device:TPU:0, one launch (start us, length us, event | category | flops | bytes accessed | tf_op | source)
XLA Modules:
  0.0 231.1 jit_solution(13399885145551736089)
XLA Ops:
  1.7 3.0 %collective-permute-start = (bf16[256,128]{1,0:T(8,128)(2,1)S(1)}, bf16[256,128]{1,0:T(8,128)(2,1)S(1)}, u32[]{:S(2)}, u32[]{:S(2)}) collective-permute-start(bf16[256,128]{1,0:T(8,128)(2,1)S(1)} %get-tuple-element.220), channel_id=1, source_target_pairs={{0,2},{2,0},{4,6},{6,4},{8,10},{10,8},{12,14},{14,12},{1,3},{3,1},... | collective-permute-start | bytes 196616 | tf_op jit(solution)/shard_map/ppermute | solution.py:206
  4.7 1.6 collective-permute-start.1
  7.5 2.0 collective-permute-start.4
  9.6 2.7 %collective-permute-start.6 = (bf16[128,512]{1,0:T(8,128)(2,1)S(1)}, bf16[128,512]{1,0:T(8,128)(2,1)S(1)}, u32[]{:S(2)}, u32[]{:S(2)}) collective-permute-start(bf16[128,512]{1,0:T(8,128)(2,1)S(1)} %get-tuple-element.243), channel_id=1, source_target_pairs={{0,8},{2,10},{4,12},{6,14},{8,0},{10,2},{12,4},{14,6},{1,9},{3,11}... | collective-permute-start | bytes 393224 | tf_op jit(solution)/shard_map/ppermute | solution.py:257
  15.2 1.6 collective-permute-start.10
  16.8 1.8 collective-permute-start.11
  18.7 2.8 %collective-permute-done.6 = bf16[128,512]{1,0:T(8,128)(2,1)S(1)} collective-permute-done((bf16[128,512]{1,0:T(8,128)(2,1)S(1)}, bf16[128,512]{1,0:T(8,128)(2,1)S(1)}, u32[]{:S(2)}, u32[]{:S(2)}) %collective-permute-start.6) | collective-permute-done | bytes 131104 | tf_op jit(solution)/shard_map/ppermute | solution.py:257
  21.5 2.4 %collective-permute-start.9 = (bf16[128,512]{1,0:T(8,128)(2,1)S(1)}, bf16[128,512]{1,0:T(8,128)(2,1)S(1)}, u32[]{:S(2)}, u32[]{:S(2)}) collective-permute-start(bf16[128,512]{1,0:T(8,128)(2,1)S(1)} %get-tuple-element.79), channel_id=1, source_target_pairs={{0,12},{2,14},{4,8},{6,10},{8,4},{10,6},{12,0},{14,2},{1,13},{3,15... | collective-permute-start | bytes 393224 | tf_op jit(solution)/shard_map/ppermute | solution.py:257
  23.9 1.8 collective-permute-start.8
  26.3 1.7 collective-permute-done.11
  28.4 1.9 collective-permute-start.12
  30.3 1.7 collective-permute-done.9
  32.0 5.9 %collective-permute-done.8 = bf16[128,512]{1,0:T(8,128)(2,1)S(1)} collective-permute-done((bf16[128,512]{1,0:T(8,128)(2,1)S(1)}, bf16[128,512]{1,0:T(8,128)(2,1)S(1)}, u32[]{:S(2)}, u32[]{:S(2)}) %collective-permute-start.8) | collective-permute-done | bytes 131104 | tf_op jit(solution)/shard_map/ppermute | solution.py:257
  40.8 2.2 collective-permute-start.18
  43.0 1.5 collective-permute-start.24
  45.3 2.5 %collective-permute-start.16 = (bf16[2,64,512]{2,1,0:T(8,128)(2,1)S(1)}, bf16[2,64,512]{2,1,0:T(8,128)(2,1)S(1)}, u32[]{:S(2)}, u32[]{:S(2)}) collective-permute-start(bf16[2,64,512]{2,1,0:T(8,128)(2,1)S(1)} %get-tuple-element.209), channel_id=1, source_target_pairs={{0,4},{2,6},{4,0},{6,2},{8,12},{10,14},{12,8},{14,10},{1,5},{3,7},... | collective-permute-start | bytes 393224 | tf_op jit(solution)/shard_map/ppermute | solution.py:206
  48.8 7.4 %collective-permute-done.18 = bf16[256,512]{1,0:T(8,128)(2,1)S(1)} collective-permute-done((bf16[256,512]{1,0:T(8,128)(2,1)S(1)}, bf16[256,512]{1,0:T(8,128)(2,1)S(1)}, u32[]{:S(2)}, u32[]{:S(2)}) %collective-permute-start.18) | collective-permute-done | bytes 262176 | tf_op jit(solution)/shard_map/ppermute | solution.py:215
  56.2 2.6 %collective-permute-done.17 = bf16[2,64,512]{2,1,0:T(8,128)(2,1)S(1)} collective-permute-done((bf16[2,64,512]{2,1,0:T(8,128)(2,1)S(1)}, bf16[2,64,512]{2,1,0:T(8,128)(2,1)S(1)}, u32[]{:S(2)}, u32[]{:S(2)}) %collective-permute-start.17) | collective-permute-done | bytes 131104 | tf_op jit(solution)/shard_map/ppermute | solution.py:206
  61.4 6.0 %collective-permute-done.19 = bf16[2,64,512]{2,1,0:T(8,128)(2,1)S(1)} collective-permute-done((bf16[2,64,512]{2,1,0:T(8,128)(2,1)S(1)}, bf16[2,64,512]{2,1,0:T(8,128)(2,1)S(1)}, u32[]{:S(2)}, u32[]{:S(2)}) %collective-permute-start.19) | collective-permute-done | bytes 131104 | tf_op jit(solution)/shard_map/ppermute | solution.py:215
  69.4 1.7 collective-permute-done.25
  72.0 2.9 %collective-permute-start.28 = (bf16[64,1024]{1,0:T(8,128)(2,1)S(1)}, bf16[64,1024]{1,0:T(8,128)(2,1)S(1)}, u32[]{:S(2)}, u32[]{:S(2)}) collective-permute-start(bf16[64,1024]{1,0:T(8,128)(2,1)S(1)} %get-tuple-element.206), channel_id=1, source_target_pairs={{0,6},{2,4},{4,2},{6,0},{8,14},{10,12},{12,10},{14,8},{1,7},{3,5},... | collective-permute-start | bytes 393224 | tf_op jit(solution)/shard_map/ppermute | solution.py:206
  76.9 1.6 collective-permute-start.23
  78.5 3.5 %collective-permute-done.28 = bf16[64,1024]{1,0:T(8,128)(2,1)S(1)} collective-permute-done((bf16[64,1024]{1,0:T(8,128)(2,1)S(1)}, bf16[64,1024]{1,0:T(8,128)(2,1)S(1)}, u32[]{:S(2)}, u32[]{:S(2)}) %collective-permute-start.28) | collective-permute-done | bytes 131104 | tf_op jit(solution)/shard_map/ppermute | solution.py:206
  83.2 2.1 collective-permute-done.21
  85.3 4.1 %collective-permute-done.22 = bf16[2,64,1024]{2,1,0:T(8,128)(2,1)S(1)} collective-permute-done((bf16[2,64,1024]{2,1,0:T(8,128)(2,1)S(1)}, bf16[2,64,1024]{2,1,0:T(8,128)(2,1)S(1)}, u32[]{:S(2)}, u32[]{:S(2)}) %collective-permute-start.22) | collective-permute-done | bytes 262176 | tf_op jit(solution)/shard_map/ppermute | solution.py:206
  89.4 5.6 %collective-permute-done.23 = bf16[2,64,1024]{2,1,0:T(8,128)(2,1)S(1)} collective-permute-done((bf16[2,64,1024]{2,1,0:T(8,128)(2,1)S(1)}, bf16[2,64,1024]{2,1,0:T(8,128)(2,1)S(1)}, u32[]{:S(2)}, u32[]{:S(2)}) %collective-permute-start.23) | collective-permute-done | bytes 262176 | tf_op jit(solution)/shard_map/ppermute | solution.py:206
  98.7 1.7 collective-permute-start.32
  101.7 16.0 %shard_map.144 = (bf16[1024,1536]{1,0:T(8,128)(2,1)S(1)}, bf16[1024,1536]{1,0:T(8,128)(2,1)S(1)}, bf16[1024,1536]{1,0:T(8,128)(2,1)}, bf16[1024,1024]{1,0:T(8,128)(2,1)S(1)}) custom-call(bf16[1024,1024]{1,0:T(8,128)(2,1)S(1)} %bitcast.203, f32[2,1024,2]{2,1,0:T(8,128)S(1)} %bitcast.207, bf16[4,1024,384]{2,1,0:T(8,128)(2,1)} %wg_ref.3, ...), custom_call_target="tpu_custom_call" | custom-call | flops 9663676416 | bytes 23068672 | tf_op jit(solution)/shard_map/pallas_call | solution.py:444
  119.3 2.0 collective-permute-start.40
  124.1 2.0 collective-permute-start.37
  126.6 15.6 %shard_map.145 = (bf16[1024,3072]{1,0:T(8,128)(2,1)}, bf16[1024,1024]{1,0:T(8,128)(2,1)S(1)}) custom-call(bf16[1024,1024]{1,0:T(8,128)(2,1)S(1)} %bitcast.205, bf16[1024,1536]{1,0:T(8,128)(2,1)S(1)} %get-tuple-element.106.cp_ref, bf16[1024,1536]{1,0:T(8,128)(2,1)S(1)} %copy-done.2, bf16[4,1024,384]{2,1,0:T(8,128)(2,1)S(1)} %copy-done, ...), custom_call_target="tpu_custom_call" | custom-call | flops 9663676416 | bytes 26214400 | tf_op jit(solution)/shard_map/pallas_call | solution.py:454
  142.3 3.7 %collective-permute-done.39 = bf16[256,512]{1,0:T(8,128)(2,1)S(1)} collective-permute-done((bf16[256,512]{1,0:T(8,128)(2,1)S(1)}, bf16[256,512]{1,0:T(8,128)(2,1)S(1)}, u32[]{:S(2)}, u32[]{:S(2)}) %collective-permute-start.39) | collective-permute-done | bytes 262176 | tf_op jit(solution)/shard_map/ppermute | solution.py:215
  146.0 2.1 collective-permute-done.38
  155.0 9.0 %shard_map.146 = (bf16[4,1024,384]{2,1,0:T(8,128)(2,1)}, bf16[4,1024,384]{2,1,0:T(8,128)(2,1)}) custom-call(bf16[1024,1024]{1,0:T(8,128)(2,1)S(1)} %bitcast.204, bf16[1024,3072]{1,0:T(8,128)(2,1)S(1)} %copy-done.1), custom_call_target="tpu_custom_call" | custom-call | flops 6442450944 | bytes 14680064 | tf_op jit(solution)/shard_map/pallas_call | solution.py:465
  164.1 2.2 collective-permute-done.44
  166.3 5.3 %collective-permute-done.45 = bf16[2,64,1024]{2,1,0:T(8,128)(2,1)S(1)} collective-permute-done((bf16[2,64,1024]{2,1,0:T(8,128)(2,1)S(1)}, bf16[2,64,1024]{2,1,0:T(8,128)(2,1)S(1)}, u32[]{:S(2)}, u32[]{:S(2)}) %collective-permute-start.45) | collective-permute-done | bytes 262176 | tf_op jit(solution)/shard_map/ppermute | solution.py:206
  172.5 2.9 %collective-permute-start.50 = (bf16[64,1536]{1,0:T(8,128)(2,1)S(1)}, bf16[64,1536]{1,0:T(8,128)(2,1)S(1)}, u32[]{:S(2)}, u32[]{:S(2)}) collective-permute-start(bf16[64,1536]{1,0:T(8,128)(2,1)S(1)} %pad_maximum_fusion.22), channel_id=1, source_target_pairs={{0,6},{2,4},{4,2},{6,0},{8,14},{10,12},{12,10},{14,8},{1,7},{3,5},... | collective-permute-start | bytes 589832 | tf_op jit(solution)/shard_map/ppermute | solution.py:206
  175.5 2.7 %collective-permute-start.51 = (bf16[2,64,1024]{2,1,0:T(8,128)(2,1)S(1)}, bf16[2,64,1024]{2,1,0:T(8,128)(2,1)S(1)}, u32[]{:S(2)}, u32[]{:S(2)}) collective-permute-start(bf16[2,64,1024]{2,1,0:T(8,128)(2,1)S(1)} %add_convert_fusion), channel_id=1, source_target_pairs={{0,8},{2,10},{4,12},{6,14},{8,0},{10,2},{12,4},{14,6},{1,9},{3,11}... | collective-permute-start | bytes 786440 | tf_op jit(solution)/shard_map/ppermute | solution.py:215
  178.2 5.0 %shard_map.147 = bf16[1536,1024]{1,0:T(8,128)(2,1)} custom-call(bf16[1024,1536]{1,0:T(8,128)(2,1)S(1)} %get-tuple-element.123.hs_ref, bf16[1024,1024]{1,0:T(8,128)(2,1)S(1)} %bitcast.206), custom_call_target="tpu_custom_call" | custom-call | flops 3221225472 | bytes 8388608 | tf_op jit(solution)/shard_map/pallas_call | solution.py:474
  183.2 2.5 %collective-permute-done.49 = bf16[64,1536]{1,0:T(8,128)(2,1)S(1)} collective-permute-done((bf16[64,1536]{1,0:T(8,128)(2,1)S(1)}, bf16[64,1536]{1,0:T(8,128)(2,1)S(1)}, u32[]{:S(2)}, u32[]{:S(2)}) %collective-permute-start.49) | collective-permute-done | bytes 196640 | tf_op jit(solution)/shard_map/ppermute | solution.py:206
  185.7 3.0 %collective-permute-done.50 = bf16[64,1536]{1,0:T(8,128)(2,1)S(1)} collective-permute-done((bf16[64,1536]{1,0:T(8,128)(2,1)S(1)}, bf16[64,1536]{1,0:T(8,128)(2,1)S(1)}, u32[]{:S(2)}, u32[]{:S(2)}) %collective-permute-start.50) | collective-permute-done | bytes 196640 | tf_op jit(solution)/shard_map/ppermute | solution.py:206
  189.7 2.8 %collective-permute-start.60 = (bf16[64,1536]{1,0:T(8,128)(2,1)S(1)}, bf16[64,1536]{1,0:T(8,128)(2,1)S(1)}, u32[]{:S(2)}, u32[]{:S(2)}) collective-permute-start(bf16[64,1536]{1,0:T(8,128)(2,1)S(1)} %pad_maximum_fusion.23), channel_id=1, source_target_pairs={{0,4},{2,6},{4,0},{6,2},{8,12},{10,14},{12,8},{14,10},{1,5},{3,7},... | collective-permute-start | bytes 589832 | tf_op jit(solution)/shard_map/ppermute | solution.py:206
  198.2 3.9 %collective-permute-done.61 = bf16[64,1536]{1,0:T(8,128)(2,1)S(1)} collective-permute-done((bf16[64,1536]{1,0:T(8,128)(2,1)S(1)}, bf16[64,1536]{1,0:T(8,128)(2,1)S(1)}, u32[]{:S(2)}, u32[]{:S(2)}) %collective-permute-start.61) | collective-permute-done | bytes 196640 | tf_op jit(solution)/shard_map/ppermute | solution.py:206
  203.9 1.7 collective-permute-start.57
  207.5 1.7 collective-permute-start.54
  215.1 1.7 collective-permute-start.67
  217.3 2.6 %collective-permute-done.55 = bf16[512,128]{1,0:T(8,128)(2,1)S(1)} collective-permute-done((bf16[512,128]{1,0:T(8,128)(2,1)S(1)}, bf16[512,128]{1,0:T(8,128)(2,1)S(1)}, u32[]{:S(2)}, u32[]{:S(2)}) %collective-permute-start.55) | collective-permute-done | bytes 131104 | tf_op jit(solution)/shard_map/ppermute | solution.py:206
  223.7 1.5 collective-permute-done.68
  (302 shorter events, 62.8 us)
Async XLA Ops:
  1.7 10.7 %collective-permute-start = (bf16[256,128]{1,0:T(8,128)(2,1)S(1)}, bf16[256,128]{1,0:T(8,128)(2,1)S(1)}, u32[]{:S(2)}, u32[]{:S(2)}) collective-permute-start(bf16[256,128]{1,0:T(8,128)(2,1)S(1)} %get-tuple-element.220), channel_id=1, source_target_pairs={{0,2},{2,0},{4,6},{6,4},{8,10},{10,8},{12,14},{14,12},{1,3},{3,1},... | collective-permute-start | bytes 196616 | tf_op jit(solution)/shard_map/ppermute | solution.py:206
  4.7 9.1 %collective-permute-start.1 = (bf16[256,128]{1,0:T(8,128)(2,1)S(1)}, bf16[256,128]{1,0:T(8,128)(2,1)S(1)}, u32[]{:S(2)}, u32[]{:S(2)}) collective-permute-start(bf16[256,128]{1,0:T(8,128)(2,1)S(1)} %get-tuple-element.221), channel_id=1, source_target_pairs={{0,4},{2,6},{4,0},{6,2},{8,12},{10,14},{12,8},{14,10},{1,5},{3,7},... | collective-permute-start | bytes 196616 | tf_op jit(solution)/shard_map/ppermute | solution.py:206
  7.5 9.3 %collective-permute-start.4 = (bf16[128,1024]{1,0:T(8,128)(2,1)S(1)}, bf16[128,1024]{1,0:T(8,128)(2,1)S(1)}, u32[]{:S(2)}, u32[]{:S(2)}) collective-permute-start(bf16[128,1024]{1,0:T(8,128)(2,1)S(1)} %pad_maximum_fusion.11), channel_id=1, source_target_pairs={{0,2},{2,0},{4,6},{6,4},{8,10},{10,8},{12,14},{14,12},{1,3},{3,1},... | collective-permute-start | bytes 786440 | tf_op jit(solution)/shard_map/ppermute | solution.py:206
  9.6 11.9 %collective-permute-start.6 = (bf16[128,512]{1,0:T(8,128)(2,1)S(1)}, bf16[128,512]{1,0:T(8,128)(2,1)S(1)}, u32[]{:S(2)}, u32[]{:S(2)}) collective-permute-start(bf16[128,512]{1,0:T(8,128)(2,1)S(1)} %get-tuple-element.243), channel_id=1, source_target_pairs={{0,8},{2,10},{4,12},{6,14},{8,0},{10,2},{12,4},{14,6},{1,9},{3,11}... | collective-permute-start | bytes 393224 | tf_op jit(solution)/shard_map/ppermute | solution.py:257
  12.4 9.1 %collective-permute-start.7 = (bf16[128,512]{1,0:T(8,128)(2,1)S(1)}, bf16[128,512]{1,0:T(8,128)(2,1)S(1)}, u32[]{:S(2)}, u32[]{:S(2)}) collective-permute-start(bf16[128,512]{1,0:T(8,128)(2,1)S(1)} %get-tuple-element.244), channel_id=1, source_target_pairs={{0,12},{2,14},{4,8},{6,10},{8,4},{10,6},{12,0},{14,2},{1,13},{3,15... | collective-permute-start | bytes 393224 | tf_op jit(solution)/shard_map/ppermute | solution.py:257
  13.9 12.0 %collective-permute-start.3 = (bf16[128,1024]{1,0:T(8,128)(2,1)S(1)}, bf16[128,1024]{1,0:T(8,128)(2,1)S(1)}, u32[]{:S(2)}, u32[]{:S(2)}) collective-permute-start(bf16[128,1024]{1,0:T(8,128)(2,1)S(1)} %get-tuple-element.214), channel_id=1, source_target_pairs={{0,4},{2,6},{4,0},{6,2},{8,12},{10,14},{12,8},{14,10},{1,5},{3,7},... | collective-permute-start | bytes 786440 | tf_op jit(solution)/shard_map/ppermute | solution.py:206
  15.2 13.2 %collective-permute-start.10 = (bf16[256,512]{1,0:T(8,128)(2,1)S(1)}, bf16[256,512]{1,0:T(8,128)(2,1)S(1)}, u32[]{:S(2)}, u32[]{:S(2)}) collective-permute-start(bf16[256,512]{1,0:T(8,128)(2,1)S(1)} %pad_maximum_fusion.13), channel_id=1, source_target_pairs={{0,16},{16,0},{1,17},{17,1},{2,18},{18,2},{3,19},{19,3},{4,20},{20... | collective-permute-start | bytes 786440 | tf_op jit(solution)/shard_map/ppermute | solution.py:212
  16.8 11.2 %collective-permute-start.11 = (bf16[2,256,128]{2,1,0:T(8,128)(2,1)S(1)}, bf16[2,256,128]{2,1,0:T(8,128)(2,1)S(1)}, u32[]{:S(2)}, u32[]{:S(2)}) collective-permute-start(bf16[2,256,128]{2,1,0:T(8,128)(2,1)S(1)} %pad_maximum_fusion.24), channel_id=1, source_target_pairs={{0,4},{2,6},{4,0},{6,2},{8,12},{10,14},{12,8},{14,10},{1,5},{3,7},... | collective-permute-start | bytes 393224 | tf_op jit(solution)/shard_map/ppermute | solution.py:206
  21.5 10.5 %collective-permute-start.9 = (bf16[128,512]{1,0:T(8,128)(2,1)S(1)}, bf16[128,512]{1,0:T(8,128)(2,1)S(1)}, u32[]{:S(2)}, u32[]{:S(2)}) collective-permute-start(bf16[128,512]{1,0:T(8,128)(2,1)S(1)} %get-tuple-element.79), channel_id=1, source_target_pairs={{0,12},{2,14},{4,8},{6,10},{8,4},{10,6},{12,0},{14,2},{1,13},{3,15... | collective-permute-start | bytes 393224 | tf_op jit(solution)/shard_map/ppermute | solution.py:257
  23.9 14.0 %collective-permute-start.8 = (bf16[128,512]{1,0:T(8,128)(2,1)S(1)}, bf16[128,512]{1,0:T(8,128)(2,1)S(1)}, u32[]{:S(2)}, u32[]{:S(2)}) collective-permute-start(bf16[128,512]{1,0:T(8,128)(2,1)S(1)} %get-tuple-element.78), channel_id=1, source_target_pairs={{0,8},{2,10},{4,12},{6,14},{8,0},{10,2},{12,4},{14,6},{1,9},{3,11}... | collective-permute-start | bytes 393224 | tf_op jit(solution)/shard_map/ppermute | solution.py:257
  25.9 12.6 %collective-permute-start.5 = (bf16[256,512]{1,0:T(8,128)(2,1)S(1)}, bf16[256,512]{1,0:T(8,128)(2,1)S(1)}, u32[]{:S(2)}, u32[]{:S(2)}) collective-permute-start(bf16[256,512]{1,0:T(8,128)(2,1)S(1)} %pad_maximum_fusion.12), channel_id=1, source_target_pairs={{0,4},{2,6},{4,0},{6,2},{8,12},{10,14},{12,8},{14,10},{1,5},{3,7},... | collective-permute-start | bytes 786440 | tf_op jit(solution)/shard_map/ppermute | solution.py:206
  28.0 10.5 %collective-permute-start.13 = (bf16[256,512]{1,0:T(8,128)(2,1)S(1)}, bf16[256,512]{1,0:T(8,128)(2,1)S(1)}, u32[]{:S(2)}, u32[]{:S(2)}) collective-permute-start(bf16[256,512]{1,0:T(8,128)(2,1)S(1)} %get-tuple-element.213), channel_id=1, source_target_pairs={{0,2},{2,0},{4,6},{6,4},{8,10},{10,8},{12,14},{14,12},{1,3},{3,1},... | collective-permute-start | bytes 786440 | tf_op jit(solution)/shard_map/ppermute | solution.py:206
  28.4 9.5 %collective-permute-start.12 = (bf16[256,256]{1,0:T(8,128)(2,1)S(1)}, bf16[256,256]{1,0:T(8,128)(2,1)S(1)}, u32[]{:S(2)}, u32[]{:S(2)}) collective-permute-start(bf16[256,256]{1,0:T(8,128)(2,1)S(1)} %get-tuple-element.238), channel_id=1, source_target_pairs={{0,2},{2,0},{4,6},{6,4},{8,10},{10,8},{12,14},{14,12},{1,3},{3,1},... | collective-permute-start | bytes 393224 | tf_op jit(solution)/shard_map/ppermute | solution.py:206
  40.8 15.4 %collective-permute-start.18 = (bf16[256,512]{1,0:T(8,128)(2,1)S(1)}, bf16[256,512]{1,0:T(8,128)(2,1)S(1)}, u32[]{:S(2)}, u32[]{:S(2)}) collective-permute-start(bf16[256,512]{1,0:T(8,128)(2,1)S(1)} %pad_maximum_fusion.16), channel_id=1, source_target_pairs={{0,8},{2,10},{4,12},{6,14},{8,0},{10,2},{12,4},{14,6},{1,9},{3,11}... | collective-permute-start | bytes 786440 | tf_op jit(solution)/shard_map/ppermute | solution.py:215
  43.0 17.7 %collective-permute-start.24 = (bf16[256,512]{1,0:T(8,128)(2,1)S(1)}, bf16[256,512]{1,0:T(8,128)(2,1)S(1)}, u32[]{:S(2)}, u32[]{:S(2)}) collective-permute-start(bf16[256,512]{1,0:T(8,128)(2,1)S(1)} %pad_maximum_fusion.16), channel_id=1, source_target_pairs={{0,16},{16,0},{1,17},{17,1},{2,18},{18,2},{3,19},{19,3},{4,20},{20... | collective-permute-start | bytes 786440 | tf_op jit(solution)/shard_map/ppermute | solution.py:212
  44.7 11.5 %collective-permute-start.15 = (bf16[2,64,512]{2,1,0:T(8,128)(2,1)S(1)}, bf16[2,64,512]{2,1,0:T(8,128)(2,1)S(1)}, u32[]{:S(2)}, u32[]{:S(2)}) collective-permute-start(bf16[2,64,512]{2,1,0:T(8,128)(2,1)S(1)} %get-tuple-element.210), channel_id=1, source_target_pairs={{0,2},{2,0},{4,6},{6,4},{8,10},{10,8},{12,14},{14,12},{1,3},{3,1},... | collective-permute-start | bytes 393224 | tf_op jit(solution)/shard_map/ppermute | solution.py:206
  45.3 10.9 %collective-permute-start.16 = (bf16[2,64,512]{2,1,0:T(8,128)(2,1)S(1)}, bf16[2,64,512]{2,1,0:T(8,128)(2,1)S(1)}, u32[]{:S(2)}, u32[]{:S(2)}) collective-permute-start(bf16[2,64,512]{2,1,0:T(8,128)(2,1)S(1)} %get-tuple-element.209), channel_id=1, source_target_pairs={{0,4},{2,6},{4,0},{6,2},{8,12},{10,14},{12,8},{14,10},{1,5},{3,7},... | collective-permute-start | bytes 393224 | tf_op jit(solution)/shard_map/ppermute | solution.py:206
  47.8 11.1 %collective-permute-start.17 = (bf16[2,64,512]{2,1,0:T(8,128)(2,1)S(1)}, bf16[2,64,512]{2,1,0:T(8,128)(2,1)S(1)}, u32[]{:S(2)}, u32[]{:S(2)}) collective-permute-start(bf16[2,64,512]{2,1,0:T(8,128)(2,1)S(1)} %get-tuple-element.208), channel_id=1, source_target_pairs={{0,6},{2,4},{4,2},{6,0},{8,14},{10,12},{12,10},{14,8},{1,7},{3,5},... | collective-permute-start | bytes 393224 | tf_op jit(solution)/shard_map/ppermute | solution.py:206
  72.0 10.0 %collective-permute-start.28 = (bf16[64,1024]{1,0:T(8,128)(2,1)S(1)}, bf16[64,1024]{1,0:T(8,128)(2,1)S(1)}, u32[]{:S(2)}, u32[]{:S(2)}) collective-permute-start(bf16[64,1024]{1,0:T(8,128)(2,1)S(1)} %get-tuple-element.206), channel_id=1, source_target_pairs={{0,6},{2,4},{4,2},{6,0},{8,14},{10,12},{12,10},{14,8},{1,7},{3,5},... | collective-permute-start | bytes 393224 | tf_op jit(solution)/shard_map/ppermute | solution.py:206
  74.9 10.4 %collective-permute-start.21 = (bf16[2,64,1024]{2,1,0:T(8,128)(2,1)S(1)}, bf16[2,64,1024]{2,1,0:T(8,128)(2,1)S(1)}, u32[]{:S(2)}, u32[]{:S(2)}) collective-permute-start(bf16[2,64,1024]{2,1,0:T(8,128)(2,1)S(1)} %get-tuple-element.228), channel_id=1, source_target_pairs={{0,2},{2,0},{4,6},{6,4},{8,10},{10,8},{12,14},{14,12},{1,3},{3,1},... | collective-permute-start | bytes 786440 | tf_op jit(solution)/shard_map/ppermute | solution.py:206
  75.4 14.0 %collective-permute-start.22 = (bf16[2,64,1024]{2,1,0:T(8,128)(2,1)S(1)}, bf16[2,64,1024]{2,1,0:T(8,128)(2,1)S(1)}, u32[]{:S(2)}, u32[]{:S(2)}) collective-permute-start(bf16[2,64,1024]{2,1,0:T(8,128)(2,1)S(1)} %get-tuple-element.228), channel_id=1, source_target_pairs={{0,4},{2,6},{4,0},{6,2},{8,12},{10,14},{12,8},{14,10},{1,5},{3,7},... | collective-permute-start | bytes 786440 | tf_op jit(solution)/shard_map/ppermute | solution.py:206
  76.9 18.0 %collective-permute-start.23 = (bf16[2,64,1024]{2,1,0:T(8,128)(2,1)S(1)}, bf16[2,64,1024]{2,1,0:T(8,128)(2,1)S(1)}, u32[]{:S(2)}, u32[]{:S(2)}) collective-permute-start(bf16[2,64,1024]{2,1,0:T(8,128)(2,1)S(1)} %get-tuple-element.228), channel_id=1, source_target_pairs={{0,6},{2,4},{4,2},{6,0},{8,14},{10,12},{12,10},{14,8},{1,7},{3,5},... | collective-permute-start | bytes 786440 | tf_op jit(solution)/shard_map/ppermute | solution.py:206
  82.1 12.9 %collective-permute-start.29 = (bf16[64,1024]{1,0:T(8,128)(2,1)S(1)}, bf16[64,1024]{1,0:T(8,128)(2,1)S(1)}, u32[]{:S(2)}, u32[]{:S(2)}) collective-permute-start(bf16[64,1024]{1,0:T(8,128)(2,1)S(1)} %get-tuple-element.252), channel_id=1, source_target_pairs={{0,8},{2,10},{4,12},{6,14},{8,0},{10,2},{12,4},{14,6},{1,9},{3,11}... | collective-permute-start | bytes 393224 | tf_op jit(solution)/shard_map/ppermute | solution.py:215
  96.9 20.8 %collective-permute-start.30 = (bf16[2,64,1024]{2,1,0:T(8,128)(2,1)S(1)}, bf16[2,64,1024]{2,1,0:T(8,128)(2,1)S(1)}, u32[]{:S(2)}, u32[]{:S(2)}) collective-permute-start(bf16[2,64,1024]{2,1,0:T(8,128)(2,1)S(1)} %pad_maximum_fusion.18), channel_id=1, source_target_pairs={{0,2},{2,0},{4,6},{6,4},{8,10},{10,8},{12,14},{14,12},{1,3},{3,1},... | collective-permute-start | bytes 786440 | tf_op jit(solution)/shard_map/ppermute | solution.py:206
  97.4 20.3 %collective-permute-start.31 = (bf16[2,64,1024]{2,1,0:T(8,128)(2,1)S(1)}, bf16[2,64,1024]{2,1,0:T(8,128)(2,1)S(1)}, u32[]{:S(2)}, u32[]{:S(2)}) collective-permute-start(bf16[2,64,1024]{2,1,0:T(8,128)(2,1)S(1)} %pad_maximum_fusion.18), channel_id=1, source_target_pairs={{0,4},{2,6},{4,0},{6,2},{8,12},{10,14},{12,8},{14,10},{1,5},{3,7},... | collective-permute-start | bytes 786440 | tf_op jit(solution)/shard_map/ppermute | solution.py:206
  98.7 19.3 %collective-permute-start.32 = (bf16[2,64,1024]{2,1,0:T(8,128)(2,1)S(1)}, bf16[2,64,1024]{2,1,0:T(8,128)(2,1)S(1)}, u32[]{:S(2)}, u32[]{:S(2)}) collective-permute-start(bf16[2,64,1024]{2,1,0:T(8,128)(2,1)S(1)} %pad_maximum_fusion.18), channel_id=1, source_target_pairs={{0,6},{2,4},{4,2},{6,0},{8,14},{10,12},{12,10},{14,8},{1,7},{3,5},... | collective-permute-start | bytes 786440 | tf_op jit(solution)/shard_map/ppermute | solution.py:206
  100.4 17.2 %collective-permute-start.33 = (bf16[256,512]{1,0:T(8,128)(2,1)S(1)}, bf16[256,512]{1,0:T(8,128)(2,1)S(1)}, u32[]{:S(2)}, u32[]{:S(2)}) collective-permute-start(bf16[256,512]{1,0:T(8,128)(2,1)S(1)} %pad_maximum_fusion.15), channel_id=1, source_target_pairs={{0,8},{2,10},{4,12},{6,14},{8,0},{10,2},{12,4},{14,6},{1,9},{3,11}... | collective-permute-start | bytes 786440 | tf_op jit(solution)/shard_map/ppermute | solution.py:215
  119.3 22.9 %collective-permute-start.40 = (bf16[256,512]{1,0:T(8,128)(2,1)S(1)}, bf16[256,512]{1,0:T(8,128)(2,1)S(1)}, u32[]{:S(2)}, u32[]{:S(2)}) collective-permute-start(bf16[256,512]{1,0:T(8,128)(2,1)S(1)} %pad_maximum_fusion.19), channel_id=1, source_target_pairs={{0,8},{2,10},{4,12},{6,14},{8,0},{10,2},{12,4},{14,6},{1,9},{3,11}... | collective-permute-start | bytes 786440 | tf_op jit(solution)/shard_map/ppermute | solution.py:215
  121.3 24.7 %collective-permute-start.39 = (bf16[256,512]{1,0:T(8,128)(2,1)S(1)}, bf16[256,512]{1,0:T(8,128)(2,1)S(1)}, u32[]{:S(2)}, u32[]{:S(2)}) collective-permute-start(bf16[256,512]{1,0:T(8,128)(2,1)S(1)} %copy-done.11), channel_id=1, source_target_pairs={{0,8},{2,10},{4,12},{6,14},{8,0},{10,2},{12,4},{14,6},{1,9},{3,11}... | collective-permute-start | bytes 786440 | tf_op jit(solution)/shard_map/ppermute | solution.py:215
  123.1 22.9 %collective-permute-start.36 = (bf16[2,64,1024]{2,1,0:T(8,128)(2,1)S(1)}, bf16[2,64,1024]{2,1,0:T(8,128)(2,1)S(1)}, u32[]{:S(2)}, u32[]{:S(2)}) collective-permute-start(bf16[2,64,1024]{2,1,0:T(8,128)(2,1)S(1)} %get-tuple-element.159), channel_id=1, source_target_pairs={{0,2},{2,0},{4,6},{6,4},{8,10},{10,8},{12,14},{14,12},{1,3},{3,1},... | collective-permute-start | bytes 786440 | tf_op jit(solution)/shard_map/ppermute | solution.py:206
  124.1 21.9 %collective-permute-start.37 = (bf16[2,64,1024]{2,1,0:T(8,128)(2,1)S(1)}, bf16[2,64,1024]{2,1,0:T(8,128)(2,1)S(1)}, u32[]{:S(2)}, u32[]{:S(2)}) collective-permute-start(bf16[2,64,1024]{2,1,0:T(8,128)(2,1)S(1)} %get-tuple-element.158), channel_id=1, source_target_pairs={{0,4},{2,6},{4,0},{6,2},{8,12},{10,14},{12,8},{14,10},{1,5},{3,7},... | collective-permute-start | bytes 786440 | tf_op jit(solution)/shard_map/ppermute | solution.py:206
  126.1 21.9 %collective-permute-start.38 = (bf16[2,64,1024]{2,1,0:T(8,128)(2,1)S(1)}, bf16[2,64,1024]{2,1,0:T(8,128)(2,1)S(1)}, u32[]{:S(2)}, u32[]{:S(2)}) collective-permute-start(bf16[2,64,1024]{2,1,0:T(8,128)(2,1)S(1)} %get-tuple-element.157), channel_id=1, source_target_pairs={{0,6},{2,4},{4,2},{6,0},{8,14},{10,12},{12,10},{14,8},{1,7},{3,5},... | collective-permute-start | bytes 786440 | tf_op jit(solution)/shard_map/ppermute | solution.py:206
  148.5 15.6 %collective-permute-start.46 = (bf16[2,64,1024]{2,1,0:T(8,128)(2,1)S(1)}, bf16[2,64,1024]{2,1,0:T(8,128)(2,1)S(1)}, u32[]{:S(2)}, u32[]{:S(2)}) collective-permute-start(bf16[2,64,1024]{2,1,0:T(8,128)(2,1)S(1)} %add_convert_fusion.1), channel_id=1, source_target_pairs={{0,8},{2,10},{4,12},{6,14},{8,0},{10,2},{12,4},{14,6},{1,9},{3,11}... | collective-permute-start | bytes 786440 | tf_op jit(solution)/shard_map/ppermute | solution.py:215
  149.4 14.7 %collective-permute-start.47 = (bf16[256,512]{1,0:T(8,128)(2,1)S(1)}, bf16[256,512]{1,0:T(8,128)(2,1)S(1)}, u32[]{:S(2)}, u32[]{:S(2)}) collective-permute-start(bf16[256,512]{1,0:T(8,128)(2,1)S(1)} %collective-permute-done.39), channel_id=1, source_target_pairs={{0,16},{16,0},{1,17},{17,1},{2,18},{18,2},{3,19},{19,3},{4,20},{20... | collective-permute-start | bytes 786440 | tf_op jit(solution)/shard_map/ppermute | solution.py:212
  151.5 12.6 %collective-permute-start.43 = (bf16[2,64,1024]{2,1,0:T(8,128)(2,1)S(1)}, bf16[2,64,1024]{2,1,0:T(8,128)(2,1)S(1)}, u32[]{:S(2)}, u32[]{:S(2)}) collective-permute-start(bf16[2,64,1024]{2,1,0:T(8,128)(2,1)S(1)} %get-tuple-element.153), channel_id=1, source_target_pairs={{0,2},{2,0},{4,6},{6,4},{8,10},{10,8},{12,14},{14,12},{1,3},{3,1},... | collective-permute-start | bytes 786440 | tf_op jit(solution)/shard_map/ppermute | solution.py:206
  152.5 13.8 %collective-permute-start.44 = (bf16[2,64,1024]{2,1,0:T(8,128)(2,1)S(1)}, bf16[2,64,1024]{2,1,0:T(8,128)(2,1)S(1)}, u32[]{:S(2)}, u32[]{:S(2)}) collective-permute-start(bf16[2,64,1024]{2,1,0:T(8,128)(2,1)S(1)} %get-tuple-element.152), channel_id=1, source_target_pairs={{0,4},{2,6},{4,0},{6,2},{8,12},{10,14},{12,8},{14,10},{1,5},{3,7},... | collective-permute-start | bytes 786440 | tf_op jit(solution)/shard_map/ppermute | solution.py:206
  153.9 17.8 %collective-permute-start.45 = (bf16[2,64,1024]{2,1,0:T(8,128)(2,1)S(1)}, bf16[2,64,1024]{2,1,0:T(8,128)(2,1)S(1)}, u32[]{:S(2)}, u32[]{:S(2)}) collective-permute-start(bf16[2,64,1024]{2,1,0:T(8,128)(2,1)S(1)} %get-tuple-element.151), channel_id=1, source_target_pairs={{0,6},{2,4},{4,2},{6,0},{8,14},{10,12},{12,10},{14,8},{1,7},{3,5},... | collective-permute-start | bytes 786440 | tf_op jit(solution)/shard_map/ppermute | solution.py:206
  171.8 11.4 %collective-permute-start.48 = (bf16[64,1536]{1,0:T(8,128)(2,1)S(1)}, bf16[64,1536]{1,0:T(8,128)(2,1)S(1)}, u32[]{:S(2)}, u32[]{:S(2)}) collective-permute-start(bf16[64,1536]{1,0:T(8,128)(2,1)S(1)} %pad_maximum_fusion.22), channel_id=1, source_target_pairs={{0,2},{2,0},{4,6},{6,4},{8,10},{10,8},{12,14},{14,12},{1,3},{3,1},... | collective-permute-start | bytes 589832 | tf_op jit(solution)/shard_map/ppermute | solution.py:206
  172.5 13.2 %collective-permute-start.49 = (bf16[64,1536]{1,0:T(8,128)(2,1)S(1)}, bf16[64,1536]{1,0:T(8,128)(2,1)S(1)}, u32[]{:S(2)}, u32[]{:S(2)}) collective-permute-start(bf16[64,1536]{1,0:T(8,128)(2,1)S(1)} %pad_maximum_fusion.22), channel_id=1, source_target_pairs={{0,4},{2,6},{4,0},{6,2},{8,12},{10,14},{12,8},{14,10},{1,5},{3,7},... | collective-permute-start | bytes 589832 | tf_op jit(solution)/shard_map/ppermute | solution.py:206
  172.5 16.2 %collective-permute-start.50 = (bf16[64,1536]{1,0:T(8,128)(2,1)S(1)}, bf16[64,1536]{1,0:T(8,128)(2,1)S(1)}, u32[]{:S(2)}, u32[]{:S(2)}) collective-permute-start(bf16[64,1536]{1,0:T(8,128)(2,1)S(1)} %pad_maximum_fusion.22), channel_id=1, source_target_pairs={{0,6},{2,4},{4,2},{6,0},{8,14},{10,12},{12,10},{14,8},{1,7},{3,5},... | collective-permute-start | bytes 589832 | tf_op jit(solution)/shard_map/ppermute | solution.py:206
  175.5 13.2 %collective-permute-start.51 = (bf16[2,64,1024]{2,1,0:T(8,128)(2,1)S(1)}, bf16[2,64,1024]{2,1,0:T(8,128)(2,1)S(1)}, u32[]{:S(2)}, u32[]{:S(2)}) collective-permute-start(bf16[2,64,1024]{2,1,0:T(8,128)(2,1)S(1)} %add_convert_fusion), channel_id=1, source_target_pairs={{0,8},{2,10},{4,12},{6,14},{8,0},{10,2},{12,4},{14,6},{1,9},{3,11}... | collective-permute-start | bytes 786440 | tf_op jit(solution)/shard_map/ppermute | solution.py:215
  192.6 9.6 %collective-permute-start.61 = (bf16[64,1536]{1,0:T(8,128)(2,1)S(1)}, bf16[64,1536]{1,0:T(8,128)(2,1)S(1)}, u32[]{:S(2)}, u32[]{:S(2)}) collective-permute-start(bf16[64,1536]{1,0:T(8,128)(2,1)S(1)} %pad_maximum_fusion.23), channel_id=1, source_target_pairs={{0,6},{2,4},{4,2},{6,0},{8,14},{10,12},{12,10},{14,8},{1,7},{3,5},... | collective-permute-start | bytes 589832 | tf_op jit(solution)/shard_map/ppermute | solution.py:206
  202.4 10.2 %collective-permute-start.56 = (bf16[128,512]{1,0:T(8,128)(2,1)S(1)}, bf16[128,512]{1,0:T(8,128)(2,1)S(1)}, u32[]{:S(2)}, u32[]{:S(2)}) collective-permute-start(bf16[128,512]{1,0:T(8,128)(2,1)S(1)} %get-tuple-element.197), channel_id=1, source_target_pairs={{0,2},{2,0},{4,6},{6,4},{8,10},{10,8},{12,14},{14,12},{1,3},{3,1},... | collective-permute-start | bytes 393224 | tf_op jit(solution)/shard_map/ppermute | solution.py:206
  203.9 9.9 %collective-permute-start.57 = (bf16[128,512]{1,0:T(8,128)(2,1)S(1)}, bf16[128,512]{1,0:T(8,128)(2,1)S(1)}, u32[]{:S(2)}, u32[]{:S(2)}) collective-permute-start(bf16[128,512]{1,0:T(8,128)(2,1)S(1)} %get-tuple-element.196), channel_id=1, source_target_pairs={{0,4},{2,6},{4,0},{6,2},{8,12},{10,14},{12,8},{14,10},{1,5},{3,7},... | collective-permute-start | bytes 393224 | tf_op jit(solution)/shard_map/ppermute | solution.py:206
  205.6 9.5 %collective-permute-start.58 = (bf16[128,512]{1,0:T(8,128)(2,1)S(1)}, bf16[128,512]{1,0:T(8,128)(2,1)S(1)}, u32[]{:S(2)}, u32[]{:S(2)}) collective-permute-start(bf16[128,512]{1,0:T(8,128)(2,1)S(1)} %get-tuple-element.195), channel_id=1, source_target_pairs={{0,6},{2,4},{4,2},{6,0},{8,14},{10,12},{12,10},{14,8},{1,7},{3,5},... | collective-permute-start | bytes 393224 | tf_op jit(solution)/shard_map/ppermute | solution.py:206
  206.1 10.8 %collective-permute-start.53 = (bf16[512,128]{1,0:T(8,128)(2,1)S(1)}, bf16[512,128]{1,0:T(8,128)(2,1)S(1)}, u32[]{:S(2)}, u32[]{:S(2)}) collective-permute-start(bf16[512,128]{1,0:T(8,128)(2,1)S(1)} %get-tuple-element.201), channel_id=1, source_target_pairs={{0,2},{2,0},{4,6},{6,4},{8,10},{10,8},{12,14},{14,12},{1,3},{3,1},... | collective-permute-start | bytes 393224 | tf_op jit(solution)/shard_map/ppermute | solution.py:206
  207.5 9.8 %collective-permute-start.54 = (bf16[512,128]{1,0:T(8,128)(2,1)S(1)}, bf16[512,128]{1,0:T(8,128)(2,1)S(1)}, u32[]{:S(2)}, u32[]{:S(2)}) collective-permute-start(bf16[512,128]{1,0:T(8,128)(2,1)S(1)} %get-tuple-element.200), channel_id=1, source_target_pairs={{0,4},{2,6},{4,0},{6,2},{8,12},{10,14},{12,8},{14,10},{1,5},{3,7},... | collective-permute-start | bytes 393224 | tf_op jit(solution)/shard_map/ppermute | solution.py:206
  213.8 9.4 %collective-permute-start.66 = (bf16[512,128]{1,0:T(8,128)(2,1)S(1)}, bf16[512,128]{1,0:T(8,128)(2,1)S(1)}, u32[]{:S(2)}, u32[]{:S(2)}) collective-permute-start(bf16[512,128]{1,0:T(8,128)(2,1)S(1)} %get-tuple-element.183), channel_id=1, source_target_pairs={{0,2},{2,0},{4,6},{6,4},{8,10},{10,8},{12,14},{14,12},{1,3},{3,1},... | collective-permute-start | bytes 393224 | tf_op jit(solution)/shard_map/ppermute | solution.py:206
  (72 other events, 572.5 us)

commit v13 on v12

--- a/solution.py
+++ b/solution.py
@@ -371,13 +371,21 @@
         return grad.astype(bf16), whole.astype(bf16)
 
     def send_products(grad, whole):
-        whole = whole.reshape(4, tok_rows, quarter_d)
-        grads = exchange(lambda r: lax.dynamic_slice_in_dim(grad, (q ^ r) * shard, shard, 1))
-        return grads, exchange(lambda r: whole[r])
-
-    def join_products(grads, wholes):
-        grad = jnp.concatenate(by_quarter(grads), axis=0).astype(f32)
-        return jnp.concatenate(by_quarter(wholes), axis=1), grad
+        slabs = [whole[:, i : i + shard] for i in range(0, quarter_d, shard)]
+        slabs = jnp.stack([v.reshape(4, tok_rows, shard) for v in slabs], axis=1)
+        slabs = slabs.reshape(4, -1, shard)
+
+        def block_for(r):
+            part = lax.dynamic_slice_in_dim(grad, (q ^ r) * shard, shard, 1)
+            return jnp.concatenate([part, slabs[r]], axis=0)
+
+        return exchange(block_for)
+
+    def join_products(parts):
+        grad = jnp.concatenate(by_quarter([v[:quarter_d] for v in parts]), axis=0).astype(f32)
+        wholes = by_quarter([v[quarter_d:] for v in parts])
+        slabs = [v[i : i + tok_rows] for v in wholes for i in range(0, v.shape[0], tok_rows)]
+        return jnp.concatenate(slabs, axis=1), grad
 
     local_ids = own * exp_local + jnp.arange(exp_local, dtype=jnp.int32)
     hit = routes[:, :, None] == local_ids[None, None, :]
@@ -400,10 +408,10 @@
     tok_mine, tok_theirs = pair_rows(tokens)
     mine, other = by_half(tok_mine)
     far = far_rows(mine, other)
-    down_half = square_weight(down_weight)
+    down_half = square_weight(after(down_weight, tok_theirs))
     first = (tok_theirs, *down_half[1:])
     up_mine, up_theirs = first_weight(after(up_weight, *first))
-    cot_mine, cot_theirs = near_rows(after(cotangent, *down_half[1:]))
+    cot_mine, cot_theirs = near_rows(after(cotangent, tok_theirs))
     mine2, other2 = by_half(tok_theirs)
     near = to_peer(jnp.concatenate([other, other2], axis=0), 2)
     far2 = far_rows(after(mine2, *far[-1]), after(other2, *far[-1]))
@@ -480,9 +488,9 @@
     in_part = jnp.stack(together(*in_part, *out_products)[:4])
     out_sent = send_products(*out_products)
     in_products = products(square_blocks(in_part), token_parts, down_parts)
-    received = together(*out_sent[0], *out_sent[1], *in_products)
-    out, up_grad = join_products(received[:4], received[4:8])
-    tokens_grad, down_grad = join_products(*send_products(*in_products))
+    received = together(*out_sent, *in_products)
+    out, up_grad = join_products(received[:4])
+    tokens_grad, down_grad = join_products(send_products(*in_products))
     down_proj_grad = down_proj_grad.reshape(down_proj.shape)
     return (out, tokens_grad, gate_proj_grad, up_proj_grad, down_proj_grad, down_grad, up_grad)
 

time: 231 us -> 250 us (1.082)
  waiting for transfers between devices: 79.4 us -> 107 us
  starting transfers between devices: 78 us -> 69.5 us
    ppermute x45 -> x39, waiting for transfers between devices: 49.5 us -> 80.2 us  [to_peer(): return lax.ppermute(v, 'expert', [(e, e ^ r) for e in range(n_expert)])]
    ppermute x4, waiting for transfers between devices: 10.4 us -> 2.58 us  [to_square(): return lax.ppermute(v, 'expert', perm)]
    ppermute x45 -> x39, starting transfers between devices: 52.1 us -> 46.6 us  [to_peer(): return lax.ppermute(v, 'expert', [(e, e ^ r) for e in range(n_expert)])]
    ppermute x8, starting transfers between devices: 12.1 us -> 8.5 us  [up(): lax.ppermute(v, 'expert', [(e, (e + 4) % n_expert) for e in range(n_exper...]
    ppermute x4, waiting for transfers between devices: 0.01 us -> 3.2 us  [g_swap(): return lax.ppermute(v, 'group', [(i, i ^ 1) for i in range(n_group)])]
    unnamed x107 -> x143, local copies, waits for them, and re-layouts: 5.29 us -> 5.9 us
  transfers between devices with their start and end apart: 69 -> 63, of which waited for: 30 -> 33; matrix products, arithmetic and copies ran while one was open for 6% -> 5% of each run, Pallas kernels for 20% -> 18%
where the time goes in v13:
time: 250 us
  waiting for transfers between devices  107 us (43%)
  starting transfers between devices  69.5 us (28%)
  Pallas kernels  45.7 us (18%)
  local copies, waits for them, and re-layouts  10 us (4%)
  other arithmetic  8.08 us (3%)
  matrix products  7.64 us (3%)
    ppermute x39, waiting for transfers between devices, to_peer(): return lax.ppermute(v, 'expert', [(e, e ^ r) for e in range(n_expert)])  80.2 us
    ppermute x39, starting transfers between devices, to_peer(): return lax.ppermute(v, 'expert', [(e, e ^ r) for e in range(n_expert)])  46.6 us
    ppermute x8, waiting for transfers between devices, up(): lax.ppermute(v, 'expert', [(e, (e + 4) % n_expert) for e in range(n_exper...  18.2 us
    pallas_call x1, Pallas kernels, local(): forward(latent_in, gate_blocks(gate_columns), gate_proj, up_proj, down_rows)  16 us
    pallas_call x1, Pallas kernels, local(): backward(after(latent_grad, out_part), cp, cu, gate_proj, up_proj, down_r...  15.6 us
    pallas_call x1, Pallas kernels, local(): gate_proj_grad, up_proj_grad = input_grads(latent_in, after(dpu, in_part))  9.03 us
    ppermute x8, starting transfers between devices, up(): lax.ppermute(v, 'expert', [(e, (e + 4) % n_expert) for e in range(n_exper...  8.5 us
    ppermute x4, starting transfers between devices, to_square(): return lax.ppermute(v, 'expert', perm)  8.3 us
  transfers between devices with their start and end apart: 63, of which 33 were waited for; matrix products, arithmetic and copies ran while one was open for 5% of the time, Pallas kernels for 18%

profile of v13, /device:TPU:0, one launch (start us, length us, event | category | flops | bytes accessed | tf_op | source)
XLA Modules:
  0.0 249.8 jit_solution(12602464111513512698)
XLA Ops:
  2.0 3.0 %collective-permute-start = (bf16[128,1024]{1,0:T(8,128)(2,1)S(1)}, bf16[128,1024]{1,0:T(8,128)(2,1)S(1)}, u32[]{:S(2)}, u32[]{:S(2)}) collective-permute-start(bf16[128,1024]{1,0:T(8,128)(2,1)S(1)} %pad_maximum_fusion.11), channel_id=1, source_target_pairs={{0,2},{2,0},{4,6},{6,4},{8,10},{10,8},{12,14},{14,12},{1,3},{3,1},... | collective-permute-start | bytes 786440 | tf_op jit(solution)/shard_map/ppermute | solution.py:206
  5.1 2.7 %collective-permute-start.3 = (bf16[128,512]{1,0:T(8,128)(2,1)S(1)}, bf16[128,512]{1,0:T(8,128)(2,1)S(1)}, u32[]{:S(2)}, u32[]{:S(2)}) collective-permute-start(bf16[128,512]{1,0:T(8,128)(2,1)S(1)} %get-tuple-element.246), channel_id=1, source_target_pairs={{0,8},{2,10},{4,12},{6,14},{8,0},{10,2},{12,4},{14,6},{1,9},{3,11}... | collective-permute-start | bytes 393224 | tf_op jit(solution)/shard_map/ppermute | solution.py:257
  9.3 2.0 collective-permute-done
  11.4 1.9 collective-permute-start.1
  13.2 1.6 collective-permute-start.7
  15.3 2.6 %collective-permute-done.3 = bf16[128,512]{1,0:T(8,128)(2,1)S(1)} collective-permute-done((bf16[128,512]{1,0:T(8,128)(2,1)S(1)}, bf16[128,512]{1,0:T(8,128)(2,1)S(1)}, u32[]{:S(2)}, u32[]{:S(2)}) %collective-permute-start.3) | collective-permute-done | bytes 131104 | tf_op jit(solution)/shard_map/ppermute | solution.py:257
  17.9 2.4 collective-permute-start.6
  20.3 1.9 collective-permute-start.5
  22.2 3.5 %collective-permute-done.8 = bf16[256,128]{1,0:T(8,128)(2,1)S(1)} collective-permute-done((bf16[256,128]{1,0:T(8,128)(2,1)S(1)}, bf16[256,128]{1,0:T(8,128)(2,1)S(1)}, u32[]{:S(2)}, u32[]{:S(2)}) %collective-permute-start.8) | collective-permute-done | bytes 65568 | tf_op jit(solution)/shard_map/ppermute | solution.py:206
  28.0 11.2 %collective-permute-done.11 = bf16[2,256,128]{2,1,0:T(8,128)(2,1)S(1)} collective-permute-done((bf16[2,256,128]{2,1,0:T(8,128)(2,1)S(1)}, bf16[2,256,128]{2,1,0:T(8,128)(2,1)S(1)}, u32[]{:S(2)}, u32[]{:S(2)}) %collective-permute-start.11) | collective-permute-done | bytes 131104 | tf_op jit(solution)/shard_map/ppermute | solution.py:206
  43.0 3.2 %collective-permute-done.10 = bf16[256,512]{1,0:T(8,128)(2,1)S(1)} collective-permute-done((bf16[256,512]{1,0:T(8,128)(2,1)S(1)}, bf16[256,512]{1,0:T(8,128)(2,1)S(1)}, u32[]{:S(2)}, u32[]{:S(2)}) %collective-permute-start.10) | collective-permute-done | bytes 262176 | tf_op jit(solution)/shard_map/ppermute | solution.py:212
  47.2 3.1 %collective-permute-done.13 = bf16[256,512]{1,0:T(8,128)(2,1)S(1)} collective-permute-done((bf16[256,512]{1,0:T(8,128)(2,1)S(1)}, bf16[256,512]{1,0:T(8,128)(2,1)S(1)}, u32[]{:S(2)}, u32[]{:S(2)}) %collective-permute-start.13) | collective-permute-done | bytes 262176 | tf_op jit(solution)/shard_map/ppermute | solution.py:206
  53.5 3.4 %collective-permute-start.18 = (bf16[256,512]{1,0:T(8,128)(2,1)S(1)}, bf16[256,512]{1,0:T(8,128)(2,1)S(1)}, u32[]{:S(2)}, u32[]{:S(2)}) collective-permute-start(bf16[256,512]{1,0:T(8,128)(2,1)S(1)} %pad_maximum_fusion.16), channel_id=1, source_target_pairs={{0,8},{2,10},{4,12},{6,14},{8,0},{10,2},{12,4},{14,6},{1,9},{3,11}... | collective-permute-start | bytes 786440 | tf_op jit(solution)/shard_map/ppermute | solution.py:215
  58.2 2.5 collective-permute-start.16
  61.7 7.9 %collective-permute-done.18 = bf16[256,512]{1,0:T(8,128)(2,1)S(1)} collective-permute-done((bf16[256,512]{1,0:T(8,128)(2,1)S(1)}, bf16[256,512]{1,0:T(8,128)(2,1)S(1)}, u32[]{:S(2)}, u32[]{:S(2)}) %collective-permute-start.18) | collective-permute-done | bytes 262176 | tf_op jit(solution)/shard_map/ppermute | solution.py:215
  69.6 1.8 collective-permute-done.17
  74.3 6.6 %collective-permute-done.19 = bf16[2,64,512]{2,1,0:T(8,128)(2,1)S(1)} collective-permute-done((bf16[2,64,512]{2,1,0:T(8,128)(2,1)S(1)}, bf16[2,64,512]{2,1,0:T(8,128)(2,1)S(1)}, u32[]{:S(2)}, u32[]{:S(2)}) %collective-permute-start.19) | collective-permute-done | bytes 131104 | tf_op jit(solution)/shard_map/ppermute | solution.py:215
  82.8 1.7 collective-permute-done.25
  85.1 3.1 %collective-permute-start.28 = (bf16[64,1024]{1,0:T(8,128)(2,1)S(1)}, bf16[64,1024]{1,0:T(8,128)(2,1)S(1)}, u32[]{:S(2)}, u32[]{:S(2)}) collective-permute-start(bf16[64,1024]{1,0:T(8,128)(2,1)S(1)} %get-tuple-element.209), channel_id=1, source_target_pairs={{0,6},{2,4},{4,2},{6,0},{8,14},{10,12},{12,10},{14,8},{1,7},{3,5},... | collective-permute-start | bytes 393224 | tf_op jit(solution)/shard_map/ppermute | solution.py:206
  90.3 1.6 collective-permute-start.23
  91.9 3.5 %collective-permute-done.28 = bf16[64,1024]{1,0:T(8,128)(2,1)S(1)} collective-permute-done((bf16[64,1024]{1,0:T(8,128)(2,1)S(1)}, bf16[64,1024]{1,0:T(8,128)(2,1)S(1)}, u32[]{:S(2)}, u32[]{:S(2)}) %collective-permute-start.28) | collective-permute-done | bytes 131104 | tf_op jit(solution)/shard_map/ppermute | solution.py:206
  96.3 2.5 collective-permute-done.21
  98.7 4.0 %collective-permute-done.22 = bf16[2,64,1024]{2,1,0:T(8,128)(2,1)S(1)} collective-permute-done((bf16[2,64,1024]{2,1,0:T(8,128)(2,1)S(1)}, bf16[2,64,1024]{2,1,0:T(8,128)(2,1)S(1)}, u32[]{:S(2)}, u32[]{:S(2)}) %collective-permute-start.22) | collective-permute-done | bytes 262176 | tf_op jit(solution)/shard_map/ppermute | solution.py:206
  102.7 5.6 %collective-permute-done.23 = bf16[2,64,1024]{2,1,0:T(8,128)(2,1)S(1)} collective-permute-done((bf16[2,64,1024]{2,1,0:T(8,128)(2,1)S(1)}, bf16[2,64,1024]{2,1,0:T(8,128)(2,1)S(1)}, u32[]{:S(2)}, u32[]{:S(2)}) %collective-permute-start.23) | collective-permute-done | bytes 262176 | tf_op jit(solution)/shard_map/ppermute | solution.py:206
  111.8 2.1 collective-permute-start.32
  114.7 16.0 %shard_map.144 = (bf16[1024,1536]{1,0:T(8,128)(2,1)S(1)}, bf16[1024,1536]{1,0:T(8,128)(2,1)S(1)}, bf16[1024,1536]{1,0:T(8,128)(2,1)}, bf16[1024,1024]{1,0:T(8,128)(2,1)S(1)}) custom-call(bf16[1024,1024]{1,0:T(8,128)(2,1)S(1)} %bitcast.245, f32[2,1024,2]{2,1,0:T(8,128)S(1)} %bitcast.249, bf16[4,1024,384]{2,1,0:T(8,128)(2,1)} %wg_ref.3, ...), custom_call_target="tpu_custom_call" | custom-call | flops 9663676416 | bytes 23068672 | tf_op jit(solution)/shard_map/pallas_call | solution.py:452
  132.7 2.3 collective-permute-start.40
  137.4 1.9 collective-permute-start.37
  140.0 15.6 %shard_map.145 = (bf16[1024,3072]{1,0:T(8,128)(2,1)}, bf16[1024,1024]{1,0:T(8,128)(2,1)S(1)}) custom-call(bf16[1024,1024]{1,0:T(8,128)(2,1)S(1)} %bitcast.247, bf16[1024,1536]{1,0:T(8,128)(2,1)S(1)} %get-tuple-element.104.cp_ref, bf16[1024,1536]{1,0:T(8,128)(2,1)S(1)} %copy-done.2, bf16[4,1024,384]{2,1,0:T(8,128)(2,1)S(1)} %copy-done, ...), custom_call_target="tpu_custom_call" | custom-call | flops 9663676416 | bytes 26214400 | tf_op jit(solution)/shard_map/pallas_call | solution.py:462
  155.6 3.7 %collective-permute-done.39 = bf16[256,512]{1,0:T(8,128)(2,1)S(1)} collective-permute-done((bf16[256,512]{1,0:T(8,128)(2,1)S(1)}, bf16[256,512]{1,0:T(8,128)(2,1)S(1)}, u32[]{:S(2)}, u32[]{:S(2)}) %collective-permute-start.39) | collective-permute-done | bytes 262176 | tf_op jit(solution)/shard_map/ppermute | solution.py:215
  159.3 2.2 collective-permute-done.38
  162.0 1.6 collective-permute-start.47
  165.7 2.5 collective-permute-start.44
  168.9 9.0 %shard_map.146 = (bf16[4,1024,384]{2,1,0:T(8,128)(2,1)}, bf16[4,1024,384]{2,1,0:T(8,128)(2,1)}) custom-call(bf16[1024,1024]{1,0:T(8,128)(2,1)S(1)} %bitcast.246, bf16[1024,3072]{1,0:T(8,128)(2,1)S(1)} %copy-done.1), custom_call_target="tpu_custom_call" | custom-call | flops 6442450944 | bytes 14680064 | tf_op jit(solution)/shard_map/pallas_call | solution.py:473
  177.9 2.8 %collective-permute-done.44 = bf16[2,64,1024]{2,1,0:T(8,128)(2,1)S(1)} collective-permute-done((bf16[2,64,1024]{2,1,0:T(8,128)(2,1)S(1)}, bf16[2,64,1024]{2,1,0:T(8,128)(2,1)S(1)}, u32[]{:S(2)}, u32[]{:S(2)}) %collective-permute-start.44) | collective-permute-done | bytes 262176 | tf_op jit(solution)/shard_map/ppermute | solution.py:206
  180.8 5.4 %collective-permute-done.45 = bf16[2,64,1024]{2,1,0:T(8,128)(2,1)S(1)} collective-permute-done((bf16[2,64,1024]{2,1,0:T(8,128)(2,1)S(1)}, bf16[2,64,1024]{2,1,0:T(8,128)(2,1)S(1)}, u32[]{:S(2)}, u32[]{:S(2)}) %collective-permute-start.45) | collective-permute-done | bytes 262176 | tf_op jit(solution)/shard_map/ppermute | solution.py:206
  187.5 2.3 collective-permute-start.49
  190.9 5.0 %shard_map.147 = bf16[1536,1024]{1,0:T(8,128)(2,1)} custom-call(bf16[1024,1536]{1,0:T(8,128)(2,1)S(1)} %get-tuple-element.121.hs_ref, bf16[1024,1024]{1,0:T(8,128)(2,1)S(1)} %bitcast.248), custom_call_target="tpu_custom_call" | custom-call | flops 3221225472 | bytes 8388608 | tf_op jit(solution)/shard_map/pallas_call | solution.py:482
  195.9 4.9 %collective-permute-done.49 = bf16[64,1536]{1,0:T(8,128)(2,1)S(1)} collective-permute-done((bf16[64,1536]{1,0:T(8,128)(2,1)S(1)}, bf16[64,1536]{1,0:T(8,128)(2,1)S(1)}, u32[]{:S(2)}, u32[]{:S(2)}) %collective-permute-start.49) | collective-permute-done | bytes 196640 | tf_op jit(solution)/shard_map/ppermute | solution.py:206
  200.8 3.3 %collective-permute-done.50 = bf16[64,1536]{1,0:T(8,128)(2,1)S(1)} collective-permute-done((bf16[64,1536]{1,0:T(8,128)(2,1)S(1)}, bf16[64,1536]{1,0:T(8,128)(2,1)S(1)}, u32[]{:S(2)}, u32[]{:S(2)}) %collective-permute-start.50) | collective-permute-done | bytes 196640 | tf_op jit(solution)/shard_map/ppermute | solution.py:206
  205.1 3.0 %collective-permute-start.58 = (bf16[64,1536]{1,0:T(8,128)(2,1)S(1)}, bf16[64,1536]{1,0:T(8,128)(2,1)S(1)}, u32[]{:S(2)}, u32[]{:S(2)}) collective-permute-start(bf16[64,1536]{1,0:T(8,128)(2,1)S(1)} %pad_maximum_fusion.30), channel_id=1, source_target_pairs={{0,6},{2,4},{4,2},{6,0},{8,14},{10,12},{12,10},{14,8},{1,7},{3,5},... | collective-permute-start | bytes 589832 | tf_op jit(solution)/shard_map/ppermute | solution.py:206
  212.8 4.4 %collective-permute-done.58 = bf16[64,1536]{1,0:T(8,128)(2,1)S(1)} collective-permute-done((bf16[64,1536]{1,0:T(8,128)(2,1)S(1)}, bf16[64,1536]{1,0:T(8,128)(2,1)S(1)}, u32[]{:S(2)}, u32[]{:S(2)}) %collective-permute-start.58) | collective-permute-done | bytes 196640 | tf_op jit(solution)/shard_map/ppermute | solution.py:206
  218.0 1.8 collective-permute-start.54
  219.8 1.6 collective-permute-start.53
  227.8 4.3 %collective-permute-done.54 = bf16[1024,128]{1,0:T(8,128)(2,1)S(1)} collective-permute-done((bf16[1024,128]{1,0:T(8,128)(2,1)S(1)}, bf16[1024,128]{1,0:T(8,128)(2,1)S(1)}, u32[]{:S(2)}, u32[]{:S(2)}) %collective-permute-start.54) | collective-permute-done | bytes 262176 | tf_op jit(solution)/shard_map/ppermute | solution.py:206
  233.8 1.8 collective-permute-start.61
  238.6 5.0 %collective-permute-done.62 = bf16[1024,128]{1,0:T(8,128)(2,1)S(1)} collective-permute-done((bf16[1024,128]{1,0:T(8,128)(2,1)S(1)}, bf16[1024,128]{1,0:T(8,128)(2,1)S(1)}, u32[]{:S(2)}, u32[]{:S(2)}) %collective-permute-start.62) | collective-permute-done | bytes 262176 | tf_op jit(solution)/shard_map/ppermute | solution.py:206
  243.6 3.7 %collective-permute-done.61 = bf16[1024,128]{1,0:T(8,128)(2,1)S(1)} collective-permute-done((bf16[1024,128]{1,0:T(8,128)(2,1)S(1)}, bf16[1024,128]{1,0:T(8,128)(2,1)S(1)}, u32[]{:S(2)}, u32[]{:S(2)}) %collective-permute-start.61) | collective-permute-done | bytes 262176 | tf_op jit(solution)/shard_map/ppermute | solution.py:206
  (338 shorter events, 58.3 us)
Async XLA Ops:
  2.0 9.3 %collective-permute-start = (bf16[128,1024]{1,0:T(8,128)(2,1)S(1)}, bf16[128,1024]{1,0:T(8,128)(2,1)S(1)}, u32[]{:S(2)}, u32[]{:S(2)}) collective-permute-start(bf16[128,1024]{1,0:T(8,128)(2,1)S(1)} %pad_maximum_fusion.11), channel_id=1, source_target_pairs={{0,2},{2,0},{4,6},{6,4},{8,10},{10,8},{12,14},{14,12},{1,3},{3,1},... | collective-permute-start | bytes 786440 | tf_op jit(solution)/shard_map/ppermute | solution.py:206
  5.1 12.7 %collective-permute-start.3 = (bf16[128,512]{1,0:T(8,128)(2,1)S(1)}, bf16[128,512]{1,0:T(8,128)(2,1)S(1)}, u32[]{:S(2)}, u32[]{:S(2)}) collective-permute-start(bf16[128,512]{1,0:T(8,128)(2,1)S(1)} %get-tuple-element.246), channel_id=1, source_target_pairs={{0,8},{2,10},{4,12},{6,14},{8,0},{10,2},{12,4},{14,6},{1,9},{3,11}... | collective-permute-start | bytes 393224 | tf_op jit(solution)/shard_map/ppermute | solution.py:257
  7.8 10.1 %collective-permute-start.4 = (bf16[128,512]{1,0:T(8,128)(2,1)S(1)}, bf16[128,512]{1,0:T(8,128)(2,1)S(1)}, u32[]{:S(2)}, u32[]{:S(2)}) collective-permute-start(bf16[128,512]{1,0:T(8,128)(2,1)S(1)} %get-tuple-element.247), channel_id=1, source_target_pairs={{0,12},{2,14},{4,8},{6,10},{8,4},{10,6},{12,0},{14,2},{1,13},{3,15... | collective-permute-start | bytes 393224 | tf_op jit(solution)/shard_map/ppermute | solution.py:257
  11.4 29.3 %collective-permute-start.1 = (bf16[128,1024]{1,0:T(8,128)(2,1)S(1)}, bf16[128,1024]{1,0:T(8,128)(2,1)S(1)}, u32[]{:S(2)}, u32[]{:S(2)}) collective-permute-start(bf16[128,1024]{1,0:T(8,128)(2,1)S(1)} %get-tuple-element.217), channel_id=1, source_target_pairs={{0,4},{2,6},{4,0},{6,2},{8,12},{10,14},{12,8},{14,10},{1,5},{3,7},... | collective-permute-start | bytes 786440 | tf_op jit(solution)/shard_map/ppermute | solution.py:206
  14.8 10.8 %collective-permute-start.8 = (bf16[256,128]{1,0:T(8,128)(2,1)S(1)}, bf16[256,128]{1,0:T(8,128)(2,1)S(1)}, u32[]{:S(2)}, u32[]{:S(2)}) collective-permute-start(bf16[256,128]{1,0:T(8,128)(2,1)S(1)} %get-tuple-element.225), channel_id=1, source_target_pairs={{0,4},{2,6},{4,0},{6,2},{8,12},{10,14},{12,8},{14,10},{1,5},{3,7},... | collective-permute-start | bytes 196616 | tf_op jit(solution)/shard_map/ppermute | solution.py:206
  17.9 8.5 %collective-permute-start.9 = (bf16[256,128]{1,0:T(8,128)(2,1)S(1)}, bf16[256,128]{1,0:T(8,128)(2,1)S(1)}, u32[]{:S(2)}, u32[]{:S(2)}) collective-permute-start(bf16[256,128]{1,0:T(8,128)(2,1)S(1)} %get-tuple-element.224), channel_id=1, source_target_pairs={{0,6},{2,4},{4,2},{6,0},{8,14},{10,12},{12,10},{14,8},{1,7},{3,5},... | collective-permute-start | bytes 196616 | tf_op jit(solution)/shard_map/ppermute | solution.py:206
  17.9 23.6 %collective-permute-start.6 = (bf16[128,512]{1,0:T(8,128)(2,1)S(1)}, bf16[128,512]{1,0:T(8,128)(2,1)S(1)}, u32[]{:S(2)}, u32[]{:S(2)}) collective-permute-start(bf16[128,512]{1,0:T(8,128)(2,1)S(1)} %get-tuple-element.76), channel_id=1, source_target_pairs={{0,12},{2,14},{4,8},{6,10},{8,4},{10,6},{12,0},{14,2},{1,13},{3,15... | collective-permute-start | bytes 393224 | tf_op jit(solution)/shard_map/ppermute | solution.py:257
  20.3 22.6 %collective-permute-start.5 = (bf16[128,512]{1,0:T(8,128)(2,1)S(1)}, bf16[128,512]{1,0:T(8,128)(2,1)S(1)}, u32[]{:S(2)}, u32[]{:S(2)}) collective-permute-start(bf16[128,512]{1,0:T(8,128)(2,1)S(1)} %get-tuple-element.75), channel_id=1, source_target_pairs={{0,8},{2,10},{4,12},{6,14},{8,0},{10,2},{12,4},{14,6},{1,9},{3,11}... | collective-permute-start | bytes 393224 | tf_op jit(solution)/shard_map/ppermute | solution.py:257
  25.7 17.3 %collective-permute-start.2 = (bf16[256,512]{1,0:T(8,128)(2,1)S(1)}, bf16[256,512]{1,0:T(8,128)(2,1)}, u32[]{:S(2)}, u32[]{:S(2)}) collective-permute-start(bf16[256,512]{1,0:T(8,128)(2,1)S(1)} %pad_maximum_fusion.12), channel_id=1, source_target_pairs={{0,4},{2,6},{4,0},{6,2},{8,12},{10,14},{12,8},{14,10},{1,5},{3,7},... | collective-permute-start | bytes 786440 | tf_op jit(solution)/shard_map/ppermute | solution.py:206
  26.4 12.7 %collective-permute-start.11 = (bf16[2,256,128]{2,1,0:T(8,128)(2,1)S(1)}, bf16[2,256,128]{2,1,0:T(8,128)(2,1)S(1)}, u32[]{:S(2)}, u32[]{:S(2)}) collective-permute-start(bf16[2,256,128]{2,1,0:T(8,128)(2,1)S(1)} %pad_maximum_fusion.31), channel_id=1, source_target_pairs={{0,4},{2,6},{4,0},{6,2},{8,12},{10,14},{12,8},{14,10},{1,5},{3,7},... | collective-permute-start | bytes 393224 | tf_op jit(solution)/shard_map/ppermute | solution.py:206
  41.5 8.8 %collective-permute-start.13 = (bf16[256,512]{1,0:T(8,128)(2,1)S(1)}, bf16[256,512]{1,0:T(8,128)(2,1)S(1)}, u32[]{:S(2)}, u32[]{:S(2)}) collective-permute-start(bf16[256,512]{1,0:T(8,128)(2,1)S(1)} %get-tuple-element.216), channel_id=1, source_target_pairs={{0,2},{2,0},{4,6},{6,4},{8,10},{10,8},{12,14},{14,12},{1,3},{3,1},... | collective-permute-start | bytes 786440 | tf_op jit(solution)/shard_map/ppermute | solution.py:206
  53.5 16.1 %collective-permute-start.18 = (bf16[256,512]{1,0:T(8,128)(2,1)S(1)}, bf16[256,512]{1,0:T(8,128)(2,1)S(1)}, u32[]{:S(2)}, u32[]{:S(2)}) collective-permute-start(bf16[256,512]{1,0:T(8,128)(2,1)S(1)} %pad_maximum_fusion.16), channel_id=1, source_target_pairs={{0,8},{2,10},{4,12},{6,14},{8,0},{10,2},{12,4},{14,6},{1,9},{3,11}... | collective-permute-start | bytes 786440 | tf_op jit(solution)/shard_map/ppermute | solution.py:215
  56.9 16.7 %collective-permute-start.24 = (bf16[256,512]{1,0:T(8,128)(2,1)S(1)}, bf16[256,512]{1,0:T(8,128)(2,1)S(1)}, u32[]{:S(2)}, u32[]{:S(2)}) collective-permute-start(bf16[256,512]{1,0:T(8,128)(2,1)S(1)} %pad_maximum_fusion.16), channel_id=1, source_target_pairs={{0,16},{16,0},{1,17},{17,1},{2,18},{18,2},{3,19},{19,3},{4,20},{20... | collective-permute-start | bytes 786440 | tf_op jit(solution)/shard_map/ppermute | solution.py:212
  57.6 12.0 %collective-permute-start.15 = (bf16[2,64,512]{2,1,0:T(8,128)(2,1)S(1)}, bf16[2,64,512]{2,1,0:T(8,128)(2,1)S(1)}, u32[]{:S(2)}, u32[]{:S(2)}) collective-permute-start(bf16[2,64,512]{2,1,0:T(8,128)(2,1)S(1)} %get-tuple-element.213), channel_id=1, source_target_pairs={{0,2},{2,0},{4,6},{6,4},{8,10},{10,8},{12,14},{14,12},{1,3},{3,1},... | collective-permute-start | bytes 393224 | tf_op jit(solution)/shard_map/ppermute | solution.py:206
  58.2 11.4 %collective-permute-start.16 = (bf16[2,64,512]{2,1,0:T(8,128)(2,1)S(1)}, bf16[2,64,512]{2,1,0:T(8,128)(2,1)S(1)}, u32[]{:S(2)}, u32[]{:S(2)}) collective-permute-start(bf16[2,64,512]{2,1,0:T(8,128)(2,1)S(1)} %get-tuple-element.212), channel_id=1, source_target_pairs={{0,4},{2,6},{4,0},{6,2},{8,12},{10,14},{12,8},{14,10},{1,5},{3,7},... | collective-permute-start | bytes 393224 | tf_op jit(solution)/shard_map/ppermute | solution.py:206
  60.6 10.7 %collective-permute-start.17 = (bf16[2,64,512]{2,1,0:T(8,128)(2,1)S(1)}, bf16[2,64,512]{2,1,0:T(8,128)(2,1)S(1)}, u32[]{:S(2)}, u32[]{:S(2)}) collective-permute-start(bf16[2,64,512]{2,1,0:T(8,128)(2,1)S(1)} %get-tuple-element.211), channel_id=1, source_target_pairs={{0,6},{2,4},{4,2},{6,0},{8,14},{10,12},{12,10},{14,8},{1,7},{3,5},... | collective-permute-start | bytes 393224 | tf_op jit(solution)/shard_map/ppermute | solution.py:206
  71.4 9.5 %collective-permute-start.20 = (bf16[256,512]{1,0:T(8,128)(2,1)S(1)}, bf16[256,512]{1,0:T(8,128)(2,1)S(1)}, u32[]{:S(2)}, u32[]{:S(2)}) collective-permute-start(bf16[256,512]{1,0:T(8,128)(2,1)S(1)} %collective-permute-done.18), channel_id=1, source_target_pairs={{0,16},{16,0},{1,17},{17,1},{2,18},{18,2},{3,19},{19,3},{4,20},{20... | collective-permute-start | bytes 786440 | tf_op jit(solution)/shard_map/ppermute | solution.py:212
  85.1 10.3 %collective-permute-start.28 = (bf16[64,1024]{1,0:T(8,128)(2,1)S(1)}, bf16[64,1024]{1,0:T(8,128)(2,1)S(1)}, u32[]{:S(2)}, u32[]{:S(2)}) collective-permute-start(bf16[64,1024]{1,0:T(8,128)(2,1)S(1)} %get-tuple-element.209), channel_id=1, source_target_pairs={{0,6},{2,4},{4,2},{6,0},{8,14},{10,12},{12,10},{14,8},{1,7},{3,5},... | collective-permute-start | bytes 393224 | tf_op jit(solution)/shard_map/ppermute | solution.py:206
  88.3 10.4 %collective-permute-start.21 = (bf16[2,64,1024]{2,1,0:T(8,128)(2,1)S(1)}, bf16[2,64,1024]{2,1,0:T(8,128)(2,1)S(1)}, u32[]{:S(2)}, u32[]{:S(2)}) collective-permute-start(bf16[2,64,1024]{2,1,0:T(8,128)(2,1)S(1)} %get-tuple-element.231), channel_id=1, source_target_pairs={{0,2},{2,0},{4,6},{6,4},{8,10},{10,8},{12,14},{14,12},{1,3},{3,1},... | collective-permute-start | bytes 786440 | tf_op jit(solution)/shard_map/ppermute | solution.py:206
  88.7 14.0 %collective-permute-start.22 = (bf16[2,64,1024]{2,1,0:T(8,128)(2,1)S(1)}, bf16[2,64,1024]{2,1,0:T(8,128)(2,1)S(1)}, u32[]{:S(2)}, u32[]{:S(2)}) collective-permute-start(bf16[2,64,1024]{2,1,0:T(8,128)(2,1)S(1)} %get-tuple-element.231), channel_id=1, source_target_pairs={{0,4},{2,6},{4,0},{6,2},{8,12},{10,14},{12,8},{14,10},{1,5},{3,7},... | collective-permute-start | bytes 786440 | tf_op jit(solution)/shard_map/ppermute | solution.py:206
  90.3 18.0 %collective-permute-start.23 = (bf16[2,64,1024]{2,1,0:T(8,128)(2,1)S(1)}, bf16[2,64,1024]{2,1,0:T(8,128)(2,1)S(1)}, u32[]{:S(2)}, u32[]{:S(2)}) collective-permute-start(bf16[2,64,1024]{2,1,0:T(8,128)(2,1)S(1)} %get-tuple-element.231), channel_id=1, source_target_pairs={{0,6},{2,4},{4,2},{6,0},{8,14},{10,12},{12,10},{14,8},{1,7},{3,5},... | collective-permute-start | bytes 786440 | tf_op jit(solution)/shard_map/ppermute | solution.py:206
  95.6 12.9 %collective-permute-start.29 = (bf16[64,1024]{1,0:T(8,128)(2,1)S(1)}, bf16[64,1024]{1,0:T(8,128)(2,1)S(1)}, u32[]{:S(2)}, u32[]{:S(2)}) collective-permute-start(bf16[64,1024]{1,0:T(8,128)(2,1)S(1)} %get-tuple-element.255), channel_id=1, source_target_pairs={{0,8},{2,10},{4,12},{6,14},{8,0},{10,2},{12,4},{14,6},{1,9},{3,11}... | collective-permute-start | bytes 393224 | tf_op jit(solution)/shard_map/ppermute | solution.py:215
  110.3 20.4 %collective-permute-start.30 = (bf16[2,64,1024]{2,1,0:T(8,128)(2,1)S(1)}, bf16[2,64,1024]{2,1,0:T(8,128)(2,1)S(1)}, u32[]{:S(2)}, u32[]{:S(2)}) collective-permute-start(bf16[2,64,1024]{2,1,0:T(8,128)(2,1)S(1)} %pad_maximum_fusion.18), channel_id=1, source_target_pairs={{0,2},{2,0},{4,6},{6,4},{8,10},{10,8},{12,14},{14,12},{1,3},{3,1},... | collective-permute-start | bytes 786440 | tf_op jit(solution)/shard_map/ppermute | solution.py:206
  110.7 20.0 %collective-permute-start.31 = (bf16[2,64,1024]{2,1,0:T(8,128)(2,1)S(1)}, bf16[2,64,1024]{2,1,0:T(8,128)(2,1)S(1)}, u32[]{:S(2)}, u32[]{:S(2)}) collective-permute-start(bf16[2,64,1024]{2,1,0:T(8,128)(2,1)S(1)} %pad_maximum_fusion.18), channel_id=1, source_target_pairs={{0,4},{2,6},{4,0},{6,2},{8,12},{10,14},{12,8},{14,10},{1,5},{3,7},... | collective-permute-start | bytes 786440 | tf_op jit(solution)/shard_map/ppermute | solution.py:206
  111.8 19.7 %collective-permute-start.32 = (bf16[2,64,1024]{2,1,0:T(8,128)(2,1)S(1)}, bf16[2,64,1024]{2,1,0:T(8,128)(2,1)S(1)}, u32[]{:S(2)}, u32[]{:S(2)}) collective-permute-start(bf16[2,64,1024]{2,1,0:T(8,128)(2,1)S(1)} %pad_maximum_fusion.18), channel_id=1, source_target_pairs={{0,6},{2,4},{4,2},{6,0},{8,14},{10,12},{12,10},{14,8},{1,7},{3,5},... | collective-permute-start | bytes 786440 | tf_op jit(solution)/shard_map/ppermute | solution.py:206
  113.9 16.9 %collective-permute-start.33 = (bf16[256,512]{1,0:T(8,128)(2,1)S(1)}, bf16[256,512]{1,0:T(8,128)(2,1)S(1)}, u32[]{:S(2)}, u32[]{:S(2)}) collective-permute-start(bf16[256,512]{1,0:T(8,128)(2,1)S(1)} %pad_maximum_fusion.15), channel_id=1, source_target_pairs={{0,8},{2,10},{4,12},{6,14},{8,0},{10,2},{12,4},{14,6},{1,9},{3,11}... | collective-permute-start | bytes 786440 | tf_op jit(solution)/shard_map/ppermute | solution.py:215
  132.7 22.9 %collective-permute-start.40 = (bf16[256,512]{1,0:T(8,128)(2,1)S(1)}, bf16[256,512]{1,0:T(8,128)(2,1)S(1)}, u32[]{:S(2)}, u32[]{:S(2)}) collective-permute-start(bf16[256,512]{1,0:T(8,128)(2,1)S(1)} %pad_maximum_fusion.19), channel_id=1, source_target_pairs={{0,8},{2,10},{4,12},{6,14},{8,0},{10,2},{12,4},{14,6},{1,9},{3,11}... | collective-permute-start | bytes 786440 | tf_op jit(solution)/shard_map/ppermute | solution.py:215
  135.0 24.3 %collective-permute-start.39 = (bf16[256,512]{1,0:T(8,128)(2,1)S(1)}, bf16[256,512]{1,0:T(8,128)(2,1)S(1)}, u32[]{:S(2)}, u32[]{:S(2)}) collective-permute-start(bf16[256,512]{1,0:T(8,128)(2,1)S(1)} %copy-done.11), channel_id=1, source_target_pairs={{0,8},{2,10},{4,12},{6,14},{8,0},{10,2},{12,4},{14,6},{1,9},{3,11}... | collective-permute-start | bytes 786440 | tf_op jit(solution)/shard_map/ppermute | solution.py:215
  136.4 22.9 %collective-permute-start.36 = (bf16[2,64,1024]{2,1,0:T(8,128)(2,1)S(1)}, bf16[2,64,1024]{2,1,0:T(8,128)(2,1)S(1)}, u32[]{:S(2)}, u32[]{:S(2)}) collective-permute-start(bf16[2,64,1024]{2,1,0:T(8,128)(2,1)S(1)} %get-tuple-element.165), channel_id=1, source_target_pairs={{0,2},{2,0},{4,6},{6,4},{8,10},{10,8},{12,14},{14,12},{1,3},{3,1},... | collective-permute-start | bytes 786440 | tf_op jit(solution)/shard_map/ppermute | solution.py:206
  137.4 21.9 %collective-permute-start.37 = (bf16[2,64,1024]{2,1,0:T(8,128)(2,1)S(1)}, bf16[2,64,1024]{2,1,0:T(8,128)(2,1)S(1)}, u32[]{:S(2)}, u32[]{:S(2)}) collective-permute-start(bf16[2,64,1024]{2,1,0:T(8,128)(2,1)S(1)} %get-tuple-element.164), channel_id=1, source_target_pairs={{0,4},{2,6},{4,0},{6,2},{8,12},{10,14},{12,8},{14,10},{1,5},{3,7},... | collective-permute-start | bytes 786440 | tf_op jit(solution)/shard_map/ppermute | solution.py:206
  139.3 22.2 %collective-permute-start.38 = (bf16[2,64,1024]{2,1,0:T(8,128)(2,1)S(1)}, bf16[2,64,1024]{2,1,0:T(8,128)(2,1)S(1)}, u32[]{:S(2)}, u32[]{:S(2)}) collective-permute-start(bf16[2,64,1024]{2,1,0:T(8,128)(2,1)S(1)} %get-tuple-element.163), channel_id=1, source_target_pairs={{0,6},{2,4},{4,2},{6,0},{8,14},{10,12},{12,10},{14,8},{1,7},{3,5},... | collective-permute-start | bytes 786440 | tf_op jit(solution)/shard_map/ppermute | solution.py:206
  161.9 16.0 %collective-permute-start.46 = (bf16[2,64,1024]{2,1,0:T(8,128)(2,1)S(1)}, bf16[2,64,1024]{2,1,0:T(8,128)(2,1)S(1)}, u32[]{:S(2)}, u32[]{:S(2)}) collective-permute-start(bf16[2,64,1024]{2,1,0:T(8,128)(2,1)S(1)} %add_convert_fusion.1), channel_id=1, source_target_pairs={{0,8},{2,10},{4,12},{6,14},{8,0},{10,2},{12,4},{14,6},{1,9},{3,11}... | collective-permute-start | bytes 786440 | tf_op jit(solution)/shard_map/ppermute | solution.py:215
  162.0 15.9 %collective-permute-start.47 = (bf16[256,512]{1,0:T(8,128)(2,1)S(1)}, bf16[256,512]{1,0:T(8,128)(2,1)S(1)}, u32[]{:S(2)}, u32[]{:S(2)}) collective-permute-start(bf16[256,512]{1,0:T(8,128)(2,1)S(1)} %collective-permute-done.39), channel_id=1, source_target_pairs={{0,16},{16,0},{1,17},{17,1},{2,18},{18,2},{3,19},{19,3},{4,20},{20... | collective-permute-start | bytes 786440 | tf_op jit(solution)/shard_map/ppermute | solution.py:212
  164.9 13.0 %collective-permute-start.43 = (bf16[2,64,1024]{2,1,0:T(8,128)(2,1)S(1)}, bf16[2,64,1024]{2,1,0:T(8,128)(2,1)S(1)}, u32[]{:S(2)}, u32[]{:S(2)}) collective-permute-start(bf16[2,64,1024]{2,1,0:T(8,128)(2,1)S(1)} %get-tuple-element.159), channel_id=1, source_target_pairs={{0,2},{2,0},{4,6},{6,4},{8,10},{10,8},{12,14},{14,12},{1,3},{3,1},... | collective-permute-start | bytes 786440 | tf_op jit(solution)/shard_map/ppermute | solution.py:206
  165.7 15.0 %collective-permute-start.44 = (bf16[2,64,1024]{2,1,0:T(8,128)(2,1)S(1)}, bf16[2,64,1024]{2,1,0:T(8,128)(2,1)S(1)}, u32[]{:S(2)}, u32[]{:S(2)}) collective-permute-start(bf16[2,64,1024]{2,1,0:T(8,128)(2,1)S(1)} %get-tuple-element.158), channel_id=1, source_target_pairs={{0,4},{2,6},{4,0},{6,2},{8,12},{10,14},{12,8},{14,10},{1,5},{3,7},... | collective-permute-start | bytes 786440 | tf_op jit(solution)/shard_map/ppermute | solution.py:206
  168.2 17.9 %collective-permute-start.45 = (bf16[2,64,1024]{2,1,0:T(8,128)(2,1)S(1)}, bf16[2,64,1024]{2,1,0:T(8,128)(2,1)S(1)}, u32[]{:S(2)}, u32[]{:S(2)}) collective-permute-start(bf16[2,64,1024]{2,1,0:T(8,128)(2,1)S(1)} %get-tuple-element.157), channel_id=1, source_target_pairs={{0,6},{2,4},{4,2},{6,0},{8,14},{10,12},{12,10},{14,8},{1,7},{3,5},... | collective-permute-start | bytes 786440 | tf_op jit(solution)/shard_map/ppermute | solution.py:206
  186.3 17.8 %collective-permute-start.51 = (bf16[2,64,1024]{2,1,0:T(8,128)(2,1)S(1)}, bf16[2,64,1024]{2,1,0:T(8,128)(2,1)S(1)}, u32[]{:S(2)}, u32[]{:S(2)}) collective-permute-start(bf16[2,64,1024]{2,1,0:T(8,128)(2,1)S(1)} %add_convert_fusion), channel_id=1, source_target_pairs={{0,8},{2,10},{4,12},{6,14},{8,0},{10,2},{12,4},{14,6},{1,9},{3,11}... | collective-permute-start | bytes 786440 | tf_op jit(solution)/shard_map/ppermute | solution.py:215
  186.5 9.4 %collective-permute-start.48 = (bf16[64,1536]{1,0:T(8,128)(2,1)S(1)}, bf16[64,1536]{1,0:T(8,128)(2,1)S(1)}, u32[]{:S(2)}, u32[]{:S(2)}) collective-permute-start(bf16[64,1536]{1,0:T(8,128)(2,1)S(1)} %pad_maximum_fusion.29), channel_id=1, source_target_pairs={{0,2},{2,0},{4,6},{6,4},{8,10},{10,8},{12,14},{14,12},{1,3},{3,1},... | collective-permute-start | bytes 589832 | tf_op jit(solution)/shard_map/ppermute | solution.py:206
  187.5 13.3 %collective-permute-start.49 = (bf16[64,1536]{1,0:T(8,128)(2,1)S(1)}, bf16[64,1536]{1,0:T(8,128)(2,1)S(1)}, u32[]{:S(2)}, u32[]{:S(2)}) collective-permute-start(bf16[64,1536]{1,0:T(8,128)(2,1)S(1)} %pad_maximum_fusion.29), channel_id=1, source_target_pairs={{0,4},{2,6},{4,0},{6,2},{8,12},{10,14},{12,8},{14,10},{1,5},{3,7},... | collective-permute-start | bytes 589832 | tf_op jit(solution)/shard_map/ppermute | solution.py:206
  189.8 14.3 %collective-permute-start.50 = (bf16[64,1536]{1,0:T(8,128)(2,1)S(1)}, bf16[64,1536]{1,0:T(8,128)(2,1)S(1)}, u32[]{:S(2)}, u32[]{:S(2)}) collective-permute-start(bf16[64,1536]{1,0:T(8,128)(2,1)S(1)} %pad_maximum_fusion.29), channel_id=1, source_target_pairs={{0,6},{2,4},{4,2},{6,0},{8,14},{10,12},{12,10},{14,8},{1,7},{3,5},... | collective-permute-start | bytes 589832 | tf_op jit(solution)/shard_map/ppermute | solution.py:206
  204.5 8.0 %collective-permute-start.56 = (bf16[64,1536]{1,0:T(8,128)(2,1)S(1)}, bf16[64,1536]{1,0:T(8,128)(2,1)S(1)}, u32[]{:S(2)}, u32[]{:S(2)}) collective-permute-start(bf16[64,1536]{1,0:T(8,128)(2,1)S(1)} %pad_maximum_fusion.30), channel_id=1, source_target_pairs={{0,2},{2,0},{4,6},{6,4},{8,10},{10,8},{12,14},{14,12},{1,3},{3,1},... | collective-permute-start | bytes 589832 | tf_op jit(solution)/shard_map/ppermute | solution.py:206
  205.1 12.1 %collective-permute-start.58 = (bf16[64,1536]{1,0:T(8,128)(2,1)S(1)}, bf16[64,1536]{1,0:T(8,128)(2,1)S(1)}, u32[]{:S(2)}, u32[]{:S(2)}) collective-permute-start(bf16[64,1536]{1,0:T(8,128)(2,1)S(1)} %pad_maximum_fusion.30), channel_id=1, source_target_pairs={{0,6},{2,4},{4,2},{6,0},{8,14},{10,12},{12,10},{14,8},{1,7},{3,5},... | collective-permute-start | bytes 589832 | tf_op jit(solution)/shard_map/ppermute | solution.py:206
  217.7 10.1 %collective-permute-start.55 = (bf16[1024,128]{1,0:T(8,128)(2,1)S(1)}, bf16[1024,128]{1,0:T(8,128)(2,1)S(1)}, u32[]{:S(2)}, u32[]{:S(2)}) collective-permute-start(bf16[1024,128]{1,0:T(8,128)(2,1)S(1)} %pad_maximum_fusion.23), channel_id=1, source_target_pairs={{0,6},{2,4},{4,2},{6,0},{8,14},{10,12},{12,10},{14,8},{1,7},{3,5},... | collective-permute-start | bytes 786440 | tf_op jit(solution)/shard_map/ppermute | solution.py:206
  218.0 14.0 %collective-permute-start.54 = (bf16[1024,128]{1,0:T(8,128)(2,1)S(1)}, bf16[1024,128]{1,0:T(8,128)(2,1)S(1)}, u32[]{:S(2)}, u32[]{:S(2)}) collective-permute-start(bf16[1024,128]{1,0:T(8,128)(2,1)S(1)} %pad_maximum_fusion.22), channel_id=1, source_target_pairs={{0,4},{2,6},{4,0},{6,2},{8,12},{10,14},{12,8},{14,10},{1,5},{3,7},... | collective-permute-start | bytes 786440 | tf_op jit(solution)/shard_map/ppermute | solution.py:206
  219.8 13.1 %collective-permute-start.53 = (bf16[1024,128]{1,0:T(8,128)(2,1)S(1)}, bf16[1024,128]{1,0:T(8,128)(2,1)S(1)}, u32[]{:S(2)}, u32[]{:S(2)}) collective-permute-start(bf16[1024,128]{1,0:T(8,128)(2,1)S(1)} %pad_maximum_fusion.21), channel_id=1, source_target_pairs={{0,2},{2,0},{4,6},{6,4},{8,10},{10,8},{12,14},{14,12},{1,3},{3,1},... | collective-permute-start | bytes 786440 | tf_op jit(solution)/shard_map/ppermute | solution.py:206
  233.4 10.2 %collective-permute-start.62 = (bf16[1024,128]{1,0:T(8,128)(2,1)S(1)}, bf16[1024,128]{1,0:T(8,128)(2,1)S(1)}, u32[]{:S(2)}, u32[]{:S(2)}) collective-permute-start(bf16[1024,128]{1,0:T(8,128)(2,1)S(1)} %pad_maximum_fusion.26), channel_id=1, source_target_pairs={{0,6},{2,4},{4,2},{6,0},{8,14},{10,12},{12,10},{14,8},{1,7},{3,5},... | collective-permute-start | bytes 786440 | tf_op jit(solution)/shard_map/ppermute | solution.py:206
  233.8 13.5 %collective-permute-start.61 = (bf16[1024,128]{1,0:T(8,128)(2,1)S(1)}, bf16[1024,128]{1,0:T(8,128)(2,1)S(1)}, u32[]{:S(2)}, u32[]{:S(2)}) collective-permute-start(bf16[1024,128]{1,0:T(8,128)(2,1)S(1)} %pad_maximum_fusion.25), channel_id=1, source_target_pairs={{0,4},{2,6},{4,0},{6,2},{8,12},{10,14},{12,8},{14,10},{1,5},{3,7},... | collective-permute-start | bytes 786440 | tf_op jit(solution)/shard_map/ppermute | solution.py:206
  235.7 12.6 %collective-permute-start.60 = (bf16[1024,128]{1,0:T(8,128)(2,1)S(1)}, bf16[1024,128]{1,0:T(8,128)(2,1)S(1)}, u32[]{:S(2)}, u32[]{:S(2)}) collective-permute-start(bf16[1024,128]{1,0:T(8,128)(2,1)S(1)} %pad_maximum_fusion.24), channel_id=1, source_target_pairs={{0,2},{2,0},{4,6},{6,4},{8,10},{10,8},{12,14},{14,12},{1,3},{3,1},... | collective-permute-start | bytes 786440 | tf_op jit(solution)/shard_map/ppermute | solution.py:206
  (69 other events, 586.5 us)

commit v14 on v12

--- a/solution.py
+++ b/solution.py
@@ -23,6 +23,10 @@
     for j in range(pair):
         wgu[:, 2 * j * width : (2 * j + 1) * width] = wg_ref[j]
         wgu[:, (2 * j + 1) * width : (2 * j + 2) * width] = wu_ref[j]
+
+
+def accumulate(total, rows, part, step):
+    total[rows, :] = jnp.where(step > 0, total[rows, :] + part, part)
 
 
 def forward_kernel(
@@ -32,10 +36,6 @@
     pair, _, width = wg_ref.shape
     block = 512
     join_projections(wg_ref, wu_ref, wgu)
-
-    @pl.when(step == 0)
-    def _():
-        lo_acc[...] = jnp.zeros_like(lo_acc)
 
     for i in range(x_ref.shape[0] // block):
         rows = slice(i * block, (i + 1) * block)
@@ -45,13 +45,13 @@
             both = dot(x, wgu[:, 2 * j * width : (2 * j + 2) * width])
             gate_pre, up_pre = both[:, :width], both[:, width:]
             gate = g_ref[0, rows, j : j + 1]
-            sig = jax.nn.sigmoid(gate_pre)
-            act = gate_pre * sig * gate
-            hs_ref[rows, cols] = (act * up_pre).astype(bf16)
-            cu_ref[rows, cols] = act.astype(bf16)
-            slope = up_pre * (sig * (1.0 + gate_pre * (1.0 - sig)))
-            cp_ref[rows, cols] = (slope * gate).astype(bf16)
-        lo_acc[rows, :] += dot(hs_ref[rows, :], wd_ref[...])
+            sig = 0.5 * jnp.tanh(0.5 * gate_pre) + 0.5
+            act = gate_pre * sig
+            scaled = up_pre * gate
+            hs_ref[rows, cols] = (act * scaled).astype(bf16)
+            cu_ref[rows, cols] = (act * gate).astype(bf16)
+            cp_ref[rows, cols] = (scaled * (sig + act * (1.0 - sig))).astype(bf16)
+        accumulate(lo_acc, rows, dot(hs_ref[rows, :], wd_ref[...]), step)
 
     @pl.when(step == pl.num_programs(0) - 1)
     def _():
@@ -65,10 +65,6 @@
     pair, _, width = wg_ref.shape
     block = 512
     join_projections(wg_ref, wu_ref, wgu)
-
-    @pl.when(step == 0)
-    def _():
-        lig_acc[...] = jnp.zeros_like(lig_acc)
 
     for i in range(y_ref.shape[0] // block):
         rows = slice(i * block, (i + 1) * block)
@@ -80,7 +76,7 @@
             du = hg * cu_ref[rows, cols].astype(f32)
             dpu_ref[rows, 2 * j * width : (2 * j + 1) * width] = dp.astype(bf16)
             dpu_ref[rows, (2 * j + 1) * width : (2 * j + 2) * width] = du.astype(bf16)
-        lig_acc[rows, :] += dot(dpu_ref[rows, :], wgu[...], NT)
+        accumulate(lig_acc, rows, dot(dpu_ref[rows, :], wgu[...], NT), step)
 
     @pl.when(step == pl.num_programs(0) - 1)
     def _():
@@ -431,6 +427,7 @@
     part_x[-1], up_theirs[-1] = together(part_x[-1], up_theirs[-1])
     up_parts = [all_features(v, w) for v, w in zip(up_halves, up_theirs)]
     part_x = own_latent(part_x)
+    cot_first = after(cot_rows[: 2 * tok_rows], part_x)
     part_x = jnp.stack(exchange(lambda r: part_x))
     mine, other = project_square(cot_rows, up_parts)
     part_y = add(mine, t_swap(other))
@@ -439,7 +436,7 @@
     part_y = jnp.stack(gather_h(part_y))
     part_x = after(part_x, part_y)
     latent_in = rows_with(part_x, t_swap(part_x))
-    cot_first = gather_h(after(cot_rows[: 2 * tok_rows], part_x))
+    cot_first = gather_h(cot_first)
 
     hs, cp, cu, out_part = forward(
         latent_in, gate_blocks(gate_columns), gate_proj, up_proj, down_rows

time: 231 us -> 233 us (level)
  waiting for transfers between devices: 79.4 us -> 83 us
    ppermute x45, waiting for transfers between devices: 49.5 us -> 52.5 us  [to_peer(): return lax.ppermute(v, 'expert', [(e, e ^ r) for e in range(n_expert)])]
    ppermute x8, starting transfers between devices: 12.1 us -> 9.29 us  [up(): lax.ppermute(v, 'expert', [(e, (e + 4) % n_expert) for e in range(n_exper...]
  transfers between devices with their start and end apart: 69 -> 69, of which waited for: 30 -> 30; matrix products, arithmetic and copies ran while one was open for 6% -> 6% of each run, Pallas kernels for 20% -> 19%
where the time goes in v14:
time: 233 us; the launch traced here: 232 us
  waiting for transfers between devices  83 us (36%)
  starting transfers between devices  77.4 us (33%)
  Pallas kernels  44.3 us (19%)
  other arithmetic  10.3 us (4%)
  local copies, waits for them, and re-layouts  9.84 us (4%)
  matrix products  5.68 us (2%)
    ppermute x45, starting transfers between devices, to_peer(): return lax.ppermute(v, 'expert', [(e, e ^ r) for e in range(n_expert)])  53.9 us
    ppermute x45, waiting for transfers between devices, to_peer(): return lax.ppermute(v, 'expert', [(e, e ^ r) for e in range(n_expert)])  52.5 us
    ppermute x8, waiting for transfers between devices, up(): lax.ppermute(v, 'expert', [(e, (e + 4) % n_expert) for e in range(n_exper...  17.6 us
    pallas_call x1, Pallas kernels, local(): backward(after(latent_grad, out_part), cp, cu, gate_proj, up_proj, down_r...  15.2 us
    pallas_call x1, Pallas kernels, local(): forward(latent_in, gate_blocks(gate_columns), gate_proj, up_proj, down_rows)  15.1 us
    ppermute x4, waiting for transfers between devices, to_square(): return lax.ppermute(v, 'expert', perm)  10.4 us
    ppermute x8, starting transfers between devices, up(): lax.ppermute(v, 'expert', [(e, (e + 4) % n_expert) for e in range(n_exper...  9.29 us
    pallas_call x1, Pallas kernels, local(): gate_proj_grad, up_proj_grad = input_grads(latent_in, after(dpu, in_part))  9.03 us
  transfers between devices with their start and end apart: 69, of which 30 were waited for; matrix products, arithmetic and copies ran while one was open for 6% of the time, Pallas kernels for 19%

profile of v14, /device:TPU:0, one launch (start us, length us, event | category | flops | bytes accessed | tf_op | source)
XLA Modules:
  0.0 232.5 jit_solution(13696055378643985198)
XLA Ops:
  1.7 3.0 %collective-permute-start = (bf16[256,128]{1,0:T(8,128)(2,1)S(1)}, bf16[256,128]{1,0:T(8,128)(2,1)S(1)}, u32[]{:S(2)}, u32[]{:S(2)}) collective-permute-start(bf16[256,128]{1,0:T(8,128)(2,1)S(1)} %get-tuple-element.220), channel_id=1, source_target_pairs={{0,2},{2,0},{4,6},{6,4},{8,10},{10,8},{12,14},{14,12},{1,3},{3,1},... | collective-permute-start | bytes 196616 | tf_op jit(solution)/shard_map/ppermute | solution.py:202
  4.7 1.6 collective-permute-start.1
  7.5 2.0 collective-permute-start.4
  9.6 2.7 %collective-permute-start.6 = (bf16[128,512]{1,0:T(8,128)(2,1)S(1)}, bf16[128,512]{1,0:T(8,128)(2,1)S(1)}, u32[]{:S(2)}, u32[]{:S(2)}) collective-permute-start(bf16[128,512]{1,0:T(8,128)(2,1)S(1)} %get-tuple-element.243), channel_id=1, source_target_pairs={{0,8},{2,10},{4,12},{6,14},{8,0},{10,2},{12,4},{14,6},{1,9},{3,11}... | collective-permute-start | bytes 393224 | tf_op jit(solution)/shard_map/ppermute | solution.py:253
  15.2 1.6 collective-permute-start.10
  16.8 1.8 collective-permute-start.11
  18.7 2.8 %collective-permute-done.6 = bf16[128,512]{1,0:T(8,128)(2,1)S(1)} collective-permute-done((bf16[128,512]{1,0:T(8,128)(2,1)S(1)}, bf16[128,512]{1,0:T(8,128)(2,1)S(1)}, u32[]{:S(2)}, u32[]{:S(2)}) %collective-permute-start.6) | collective-permute-done | bytes 131104 | tf_op jit(solution)/shard_map/ppermute | solution.py:253
  21.5 2.4 %collective-permute-start.9 = (bf16[128,512]{1,0:T(8,128)(2,1)S(1)}, bf16[128,512]{1,0:T(8,128)(2,1)S(1)}, u32[]{:S(2)}, u32[]{:S(2)}) collective-permute-start(bf16[128,512]{1,0:T(8,128)(2,1)S(1)} %get-tuple-element.79), channel_id=1, source_target_pairs={{0,12},{2,14},{4,8},{6,10},{8,4},{10,6},{12,0},{14,2},{1,13},{3,15... | collective-permute-start | bytes 393224 | tf_op jit(solution)/shard_map/ppermute | solution.py:253
  23.9 1.8 collective-permute-start.8
  26.3 1.7 collective-permute-done.11
  28.4 1.9 collective-permute-start.12
  30.3 1.7 collective-permute-done.9
  32.0 5.9 %collective-permute-done.8 = bf16[128,512]{1,0:T(8,128)(2,1)S(1)} collective-permute-done((bf16[128,512]{1,0:T(8,128)(2,1)S(1)}, bf16[128,512]{1,0:T(8,128)(2,1)S(1)}, u32[]{:S(2)}, u32[]{:S(2)}) %collective-permute-start.8) | collective-permute-done | bytes 131104 | tf_op jit(solution)/shard_map/ppermute | solution.py:253
  40.8 2.2 collective-permute-start.18
  43.0 1.5 collective-permute-start.21
  45.3 2.5 %collective-permute-start.16 = (bf16[2,64,512]{2,1,0:T(8,128)(2,1)S(1)}, bf16[2,64,512]{2,1,0:T(8,128)(2,1)S(1)}, u32[]{:S(2)}, u32[]{:S(2)}) collective-permute-start(bf16[2,64,512]{2,1,0:T(8,128)(2,1)S(1)} %get-tuple-element.209), channel_id=1, source_target_pairs={{0,4},{2,6},{4,0},{6,2},{8,12},{10,14},{12,8},{14,10},{1,5},{3,7},... | collective-permute-start | bytes 393224 | tf_op jit(solution)/shard_map/ppermute | solution.py:202
  48.8 7.4 %collective-permute-done.18 = bf16[256,512]{1,0:T(8,128)(2,1)S(1)} collective-permute-done((bf16[256,512]{1,0:T(8,128)(2,1)S(1)}, bf16[256,512]{1,0:T(8,128)(2,1)S(1)}, u32[]{:S(2)}, u32[]{:S(2)}) %collective-permute-start.18) | collective-permute-done | bytes 262176 | tf_op jit(solution)/shard_map/ppermute | solution.py:211
  56.2 2.6 %collective-permute-done.17 = bf16[2,64,512]{2,1,0:T(8,128)(2,1)S(1)} collective-permute-done((bf16[2,64,512]{2,1,0:T(8,128)(2,1)S(1)}, bf16[2,64,512]{2,1,0:T(8,128)(2,1)S(1)}, u32[]{:S(2)}, u32[]{:S(2)}) %collective-permute-start.17) | collective-permute-done | bytes 131104 | tf_op jit(solution)/shard_map/ppermute | solution.py:202
  61.4 6.0 %collective-permute-done.19 = bf16[2,64,512]{2,1,0:T(8,128)(2,1)S(1)} collective-permute-done((bf16[2,64,512]{2,1,0:T(8,128)(2,1)S(1)}, bf16[2,64,512]{2,1,0:T(8,128)(2,1)S(1)}, u32[]{:S(2)}, u32[]{:S(2)}) %collective-permute-start.19) | collective-permute-done | bytes 131104 | tf_op jit(solution)/shard_map/ppermute | solution.py:211
  69.4 1.7 collective-permute-done.22
  72.0 2.9 %collective-permute-start.25 = (bf16[64,1024]{1,0:T(8,128)(2,1)S(1)}, bf16[64,1024]{1,0:T(8,128)(2,1)S(1)}, u32[]{:S(2)}, u32[]{:S(2)}) collective-permute-start(bf16[64,1024]{1,0:T(8,128)(2,1)S(1)} %get-tuple-element.206), channel_id=1, source_target_pairs={{0,6},{2,4},{4,2},{6,0},{8,14},{10,12},{12,10},{14,8},{1,7},{3,5},... | collective-permute-start | bytes 393224 | tf_op jit(solution)/shard_map/ppermute | solution.py:202
  76.9 1.6 collective-permute-start.33
  78.5 3.5 %collective-permute-done.25 = bf16[64,1024]{1,0:T(8,128)(2,1)S(1)} collective-permute-done((bf16[64,1024]{1,0:T(8,128)(2,1)S(1)}, bf16[64,1024]{1,0:T(8,128)(2,1)S(1)}, u32[]{:S(2)}, u32[]{:S(2)}) %collective-permute-start.25) | collective-permute-done | bytes 131104 | tf_op jit(solution)/shard_map/ppermute | solution.py:202
  83.2 2.1 collective-permute-done.31
  85.3 4.1 %collective-permute-done.32 = bf16[2,64,1024]{2,1,0:T(8,128)(2,1)S(1)} collective-permute-done((bf16[2,64,1024]{2,1,0:T(8,128)(2,1)S(1)}, bf16[2,64,1024]{2,1,0:T(8,128)(2,1)S(1)}, u32[]{:S(2)}, u32[]{:S(2)}) %collective-permute-start.32) | collective-permute-done | bytes 262176 | tf_op jit(solution)/shard_map/ppermute | solution.py:202
  89.4 5.6 %collective-permute-done.33 = bf16[2,64,1024]{2,1,0:T(8,128)(2,1)S(1)} collective-permute-done((bf16[2,64,1024]{2,1,0:T(8,128)(2,1)S(1)}, bf16[2,64,1024]{2,1,0:T(8,128)(2,1)S(1)}, u32[]{:S(2)}, u32[]{:S(2)}) %collective-permute-start.33) | collective-permute-done | bytes 262176 | tf_op jit(solution)/shard_map/ppermute | solution.py:202
  97.0 1.6 collective-permute-start.27
  98.6 2.4 %collective-permute-start.28 = (bf16[2,64,1024]{2,1,0:T(8,128)(2,1)S(1)}, bf16[2,64,1024]{2,1,0:T(8,128)(2,1)S(1)}, u32[]{:S(2)}, u32[]{:S(2)}) collective-permute-start(bf16[2,64,1024]{2,1,0:T(8,128)(2,1)S(1)} %pad_maximum_fusion.19), channel_id=1, source_target_pairs={{0,4},{2,6},{4,0},{6,2},{8,12},{10,14},{12,8},{14,10},{1,5},{3,7},... | collective-permute-start | bytes 786440 | tf_op jit(solution)/shard_map/ppermute | solution.py:202
  101.7 15.1 %shard_map.144 = (bf16[1024,1536]{1,0:T(8,128)(2,1)S(1)}, bf16[1024,1536]{1,0:T(8,128)(2,1)S(1)}, bf16[1024,1536]{1,0:T(8,128)(2,1)}, bf16[1024,1024]{1,0:T(8,128)(2,1)S(1)}) custom-call(bf16[1024,1024]{1,0:T(8,128)(2,1)S(1)} %bitcast.203, f32[2,1024,2]{2,1,0:T(8,128)S(1)} %bitcast.207, bf16[4,1024,384]{2,1,0:T(8,128)(2,1)} %wg_ref.3, ...), custom_call_target="tpu_custom_call" | custom-call | flops 9663676416 | bytes 23068672 | tf_op jit(solution)/shard_map/pallas_call | solution.py:441
  120.3 2.0 collective-permute-start.39
  123.1 1.7 collective-permute-start.36
  125.2 1.5 collective-permute-start.38
  126.7 15.2 %shard_map.145 = (bf16[1024,3072]{1,0:T(8,128)(2,1)}, bf16[1024,1024]{1,0:T(8,128)(2,1)S(1)}) custom-call(bf16[1024,1024]{1,0:T(8,128)(2,1)S(1)} %bitcast.205, bf16[1024,1536]{1,0:T(8,128)(2,1)S(1)} %get-tuple-element.106.cp_ref, bf16[1024,1536]{1,0:T(8,128)(2,1)S(1)} %copy-done.2, bf16[4,1024,384]{2,1,0:T(8,128)(2,1)S(1)} %copy-done, ...), custom_call_target="tpu_custom_call" | custom-call | flops 9663676416 | bytes 26214400 | tf_op jit(solution)/shard_map/pallas_call | solution.py:451
  141.9 4.1 %collective-permute-done.39 = bf16[256,512]{1,0:T(8,128)(2,1)S(1)} collective-permute-done((bf16[256,512]{1,0:T(8,128)(2,1)S(1)}, bf16[256,512]{1,0:T(8,128)(2,1)S(1)}, u32[]{:S(2)}, u32[]{:S(2)}) %collective-permute-start.39) | collective-permute-done | bytes 262176 | tf_op jit(solution)/shard_map/ppermute | solution.py:211
  146.0 3.3 %collective-permute-done.38 = bf16[2,64,1024]{2,1,0:T(8,128)(2,1)S(1)} collective-permute-done((bf16[2,64,1024]{2,1,0:T(8,128)(2,1)S(1)}, bf16[2,64,1024]{2,1,0:T(8,128)(2,1)S(1)}, u32[]{:S(2)}, u32[]{:S(2)}) %collective-permute-start.38) | collective-permute-done | bytes 262176 | tf_op jit(solution)/shard_map/ppermute | solution.py:202
  156.3 9.0 %shard_map.146 = (bf16[4,1024,384]{2,1,0:T(8,128)(2,1)}, bf16[4,1024,384]{2,1,0:T(8,128)(2,1)}) custom-call(bf16[1024,1024]{1,0:T(8,128)(2,1)S(1)} %bitcast.204, bf16[1024,3072]{1,0:T(8,128)(2,1)S(1)} %copy-done.1), custom_call_target="tpu_custom_call" | custom-call | flops 6442450944 | bytes 14680064 | tf_op jit(solution)/shard_map/pallas_call | solution.py:462
  165.3 3.3 %collective-permute-done.44 = bf16[2,64,1024]{2,1,0:T(8,128)(2,1)S(1)} collective-permute-done((bf16[2,64,1024]{2,1,0:T(8,128)(2,1)S(1)}, bf16[2,64,1024]{2,1,0:T(8,128)(2,1)S(1)}, u32[]{:S(2)}, u32[]{:S(2)}) %collective-permute-start.44) | collective-permute-done | bytes 262176 | tf_op jit(solution)/shard_map/ppermute | solution.py:202
  168.6 4.8 %collective-permute-done.45 = bf16[2,64,1024]{2,1,0:T(8,128)(2,1)S(1)} collective-permute-done((bf16[2,64,1024]{2,1,0:T(8,128)(2,1)S(1)}, bf16[2,64,1024]{2,1,0:T(8,128)(2,1)S(1)}, u32[]{:S(2)}, u32[]{:S(2)}) %collective-permute-start.45) | collective-permute-done | bytes 262176 | tf_op jit(solution)/shard_map/ppermute | solution.py:202
  174.8 2.3 %collective-permute-start.50 = (bf16[64,1536]{1,0:T(8,128)(2,1)S(1)}, bf16[64,1536]{1,0:T(8,128)(2,1)S(1)}, u32[]{:S(2)}, u32[]{:S(2)}) collective-permute-start(bf16[64,1536]{1,0:T(8,128)(2,1)S(1)} %pad_maximum_fusion.22), channel_id=1, source_target_pairs={{0,6},{2,4},{4,2},{6,0},{8,14},{10,12},{12,10},{14,8},{1,7},{3,5},... | collective-permute-start | bytes 589832 | tf_op jit(solution)/shard_map/ppermute | solution.py:202
  178.6 5.0 %shard_map.147 = bf16[1536,1024]{1,0:T(8,128)(2,1)} custom-call(bf16[1024,1536]{1,0:T(8,128)(2,1)S(1)} %get-tuple-element.123.hs_ref, bf16[1024,1024]{1,0:T(8,128)(2,1)S(1)} %bitcast.206), custom_call_target="tpu_custom_call" | custom-call | flops 3221225472 | bytes 8388608 | tf_op jit(solution)/shard_map/pallas_call | solution.py:471
  183.6 4.5 %collective-permute-done.49 = bf16[64,1536]{1,0:T(8,128)(2,1)S(1)} collective-permute-done((bf16[64,1536]{1,0:T(8,128)(2,1)S(1)}, bf16[64,1536]{1,0:T(8,128)(2,1)S(1)}, u32[]{:S(2)}, u32[]{:S(2)}) %collective-permute-start.49) | collective-permute-done | bytes 196640 | tf_op jit(solution)/shard_map/ppermute | solution.py:202
  188.0 2.4 %collective-permute-done.50 = bf16[64,1536]{1,0:T(8,128)(2,1)S(1)} collective-permute-done((bf16[64,1536]{1,0:T(8,128)(2,1)S(1)}, bf16[64,1536]{1,0:T(8,128)(2,1)S(1)}, u32[]{:S(2)}, u32[]{:S(2)}) %collective-permute-start.50) | collective-permute-done | bytes 196640 | tf_op jit(solution)/shard_map/ppermute | solution.py:202
  192.9 1.5 collective-permute-start.61
  199.8 3.8 %collective-permute-done.61 = bf16[64,1536]{1,0:T(8,128)(2,1)S(1)} collective-permute-done((bf16[64,1536]{1,0:T(8,128)(2,1)S(1)}, bf16[64,1536]{1,0:T(8,128)(2,1)S(1)}, u32[]{:S(2)}, u32[]{:S(2)}) %collective-permute-start.61) | collective-permute-done | bytes 196640 | tf_op jit(solution)/shard_map/ppermute | solution.py:202
  205.9 1.5 collective-permute-start.58
  213.0 1.5 collective-permute-start.55
  218.7 1.8 collective-permute-done.55
  228.5 2.2 collective-permute-done.65
  (302 shorter events, 65.6 us)
Async XLA Ops:
  1.7 10.7 %collective-permute-start = (bf16[256,128]{1,0:T(8,128)(2,1)S(1)}, bf16[256,128]{1,0:T(8,128)(2,1)S(1)}, u32[]{:S(2)}, u32[]{:S(2)}) collective-permute-start(bf16[256,128]{1,0:T(8,128)(2,1)S(1)} %get-tuple-element.220), channel_id=1, source_target_pairs={{0,2},{2,0},{4,6},{6,4},{8,10},{10,8},{12,14},{14,12},{1,3},{3,1},... | collective-permute-start | bytes 196616 | tf_op jit(solution)/shard_map/ppermute | solution.py:202
  4.7 9.1 %collective-permute-start.1 = (bf16[256,128]{1,0:T(8,128)(2,1)S(1)}, bf16[256,128]{1,0:T(8,128)(2,1)S(1)}, u32[]{:S(2)}, u32[]{:S(2)}) collective-permute-start(bf16[256,128]{1,0:T(8,128)(2,1)S(1)} %get-tuple-element.221), channel_id=1, source_target_pairs={{0,4},{2,6},{4,0},{6,2},{8,12},{10,14},{12,8},{14,10},{1,5},{3,7},... | collective-permute-start | bytes 196616 | tf_op jit(solution)/shard_map/ppermute | solution.py:202
  7.5 9.3 %collective-permute-start.4 = (bf16[128,1024]{1,0:T(8,128)(2,1)S(1)}, bf16[128,1024]{1,0:T(8,128)(2,1)S(1)}, u32[]{:S(2)}, u32[]{:S(2)}) collective-permute-start(bf16[128,1024]{1,0:T(8,128)(2,1)S(1)} %pad_maximum_fusion.11), channel_id=1, source_target_pairs={{0,2},{2,0},{4,6},{6,4},{8,10},{10,8},{12,14},{14,12},{1,3},{3,1},... | collective-permute-start | bytes 786440 | tf_op jit(solution)/shard_map/ppermute | solution.py:202
  9.6 11.9 %collective-permute-start.6 = (bf16[128,512]{1,0:T(8,128)(2,1)S(1)}, bf16[128,512]{1,0:T(8,128)(2,1)S(1)}, u32[]{:S(2)}, u32[]{:S(2)}) collective-permute-start(bf16[128,512]{1,0:T(8,128)(2,1)S(1)} %get-tuple-element.243), channel_id=1, source_target_pairs={{0,8},{2,10},{4,12},{6,14},{8,0},{10,2},{12,4},{14,6},{1,9},{3,11}... | collective-permute-start | bytes 393224 | tf_op jit(solution)/shard_map/ppermute | solution.py:253
  12.4 9.1 %collective-permute-start.7 = (bf16[128,512]{1,0:T(8,128)(2,1)S(1)}, bf16[128,512]{1,0:T(8,128)(2,1)S(1)}, u32[]{:S(2)}, u32[]{:S(2)}) collective-permute-start(bf16[128,512]{1,0:T(8,128)(2,1)S(1)} %get-tuple-element.244), channel_id=1, source_target_pairs={{0,12},{2,14},{4,8},{6,10},{8,4},{10,6},{12,0},{14,2},{1,13},{3,15... | collective-permute-start | bytes 393224 | tf_op jit(solution)/shard_map/ppermute | solution.py:253
  13.9 12.0 %collective-permute-start.3 = (bf16[128,1024]{1,0:T(8,128)(2,1)S(1)}, bf16[128,1024]{1,0:T(8,128)(2,1)S(1)}, u32[]{:S(2)}, u32[]{:S(2)}) collective-permute-start(bf16[128,1024]{1,0:T(8,128)(2,1)S(1)} %get-tuple-element.214), channel_id=1, source_target_pairs={{0,4},{2,6},{4,0},{6,2},{8,12},{10,14},{12,8},{14,10},{1,5},{3,7},... | collective-permute-start | bytes 786440 | tf_op jit(solution)/shard_map/ppermute | solution.py:202
  15.2 13.2 %collective-permute-start.10 = (bf16[256,512]{1,0:T(8,128)(2,1)S(1)}, bf16[256,512]{1,0:T(8,128)(2,1)S(1)}, u32[]{:S(2)}, u32[]{:S(2)}) collective-permute-start(bf16[256,512]{1,0:T(8,128)(2,1)S(1)} %pad_maximum_fusion.13), channel_id=1, source_target_pairs={{0,16},{16,0},{1,17},{17,1},{2,18},{18,2},{3,19},{19,3},{4,20},{20... | collective-permute-start | bytes 786440 | tf_op jit(solution)/shard_map/ppermute | solution.py:208
  16.8 11.2 %collective-permute-start.11 = (bf16[2,256,128]{2,1,0:T(8,128)(2,1)S(1)}, bf16[2,256,128]{2,1,0:T(8,128)(2,1)S(1)}, u32[]{:S(2)}, u32[]{:S(2)}) collective-permute-start(bf16[2,256,128]{2,1,0:T(8,128)(2,1)S(1)} %pad_maximum_fusion.24), channel_id=1, source_target_pairs={{0,4},{2,6},{4,0},{6,2},{8,12},{10,14},{12,8},{14,10},{1,5},{3,7},... | collective-permute-start | bytes 393224 | tf_op jit(solution)/shard_map/ppermute | solution.py:202
  21.5 10.5 %collective-permute-start.9 = (bf16[128,512]{1,0:T(8,128)(2,1)S(1)}, bf16[128,512]{1,0:T(8,128)(2,1)S(1)}, u32[]{:S(2)}, u32[]{:S(2)}) collective-permute-start(bf16[128,512]{1,0:T(8,128)(2,1)S(1)} %get-tuple-element.79), channel_id=1, source_target_pairs={{0,12},{2,14},{4,8},{6,10},{8,4},{10,6},{12,0},{14,2},{1,13},{3,15... | collective-permute-start | bytes 393224 | tf_op jit(solution)/shard_map/ppermute | solution.py:253
  23.9 14.0 %collective-permute-start.8 = (bf16[128,512]{1,0:T(8,128)(2,1)S(1)}, bf16[128,512]{1,0:T(8,128)(2,1)S(1)}, u32[]{:S(2)}, u32[]{:S(2)}) collective-permute-start(bf16[128,512]{1,0:T(8,128)(2,1)S(1)} %get-tuple-element.78), channel_id=1, source_target_pairs={{0,8},{2,10},{4,12},{6,14},{8,0},{10,2},{12,4},{14,6},{1,9},{3,11}... | collective-permute-start | bytes 393224 | tf_op jit(solution)/shard_map/ppermute | solution.py:253
  25.9 12.6 %collective-permute-start.5 = (bf16[256,512]{1,0:T(8,128)(2,1)S(1)}, bf16[256,512]{1,0:T(8,128)(2,1)S(1)}, u32[]{:S(2)}, u32[]{:S(2)}) collective-permute-start(bf16[256,512]{1,0:T(8,128)(2,1)S(1)} %pad_maximum_fusion.12), channel_id=1, source_target_pairs={{0,4},{2,6},{4,0},{6,2},{8,12},{10,14},{12,8},{14,10},{1,5},{3,7},... | collective-permute-start | bytes 786440 | tf_op jit(solution)/shard_map/ppermute | solution.py:202
  28.0 10.5 %collective-permute-start.13 = (bf16[256,512]{1,0:T(8,128)(2,1)S(1)}, bf16[256,512]{1,0:T(8,128)(2,1)S(1)}, u32[]{:S(2)}, u32[]{:S(2)}) collective-permute-start(bf16[256,512]{1,0:T(8,128)(2,1)S(1)} %get-tuple-element.213), channel_id=1, source_target_pairs={{0,2},{2,0},{4,6},{6,4},{8,10},{10,8},{12,14},{14,12},{1,3},{3,1},... | collective-permute-start | bytes 786440 | tf_op jit(solution)/shard_map/ppermute | solution.py:202
  28.4 9.5 %collective-permute-start.12 = (bf16[256,256]{1,0:T(8,128)(2,1)S(1)}, bf16[256,256]{1,0:T(8,128)(2,1)S(1)}, u32[]{:S(2)}, u32[]{:S(2)}) collective-permute-start(bf16[256,256]{1,0:T(8,128)(2,1)S(1)} %get-tuple-element.238), channel_id=1, source_target_pairs={{0,2},{2,0},{4,6},{6,4},{8,10},{10,8},{12,14},{14,12},{1,3},{3,1},... | collective-permute-start | bytes 393224 | tf_op jit(solution)/shard_map/ppermute | solution.py:202
  40.8 15.4 %collective-permute-start.18 = (bf16[256,512]{1,0:T(8,128)(2,1)S(1)}, bf16[256,512]{1,0:T(8,128)(2,1)S(1)}, u32[]{:S(2)}, u32[]{:S(2)}) collective-permute-start(bf16[256,512]{1,0:T(8,128)(2,1)S(1)} %pad_maximum_fusion.16), channel_id=1, source_target_pairs={{0,8},{2,10},{4,12},{6,14},{8,0},{10,2},{12,4},{14,6},{1,9},{3,11}... | collective-permute-start | bytes 786440 | tf_op jit(solution)/shard_map/ppermute | solution.py:211
  43.0 17.7 %collective-permute-start.21 = (bf16[256,512]{1,0:T(8,128)(2,1)S(1)}, bf16[256,512]{1,0:T(8,128)(2,1)S(1)}, u32[]{:S(2)}, u32[]{:S(2)}) collective-permute-start(bf16[256,512]{1,0:T(8,128)(2,1)S(1)} %pad_maximum_fusion.16), channel_id=1, source_target_pairs={{0,16},{16,0},{1,17},{17,1},{2,18},{18,2},{3,19},{19,3},{4,20},{20... | collective-permute-start | bytes 786440 | tf_op jit(solution)/shard_map/ppermute | solution.py:208
  44.7 11.5 %collective-permute-start.15 = (bf16[2,64,512]{2,1,0:T(8,128)(2,1)S(1)}, bf16[2,64,512]{2,1,0:T(8,128)(2,1)S(1)}, u32[]{:S(2)}, u32[]{:S(2)}) collective-permute-start(bf16[2,64,512]{2,1,0:T(8,128)(2,1)S(1)} %get-tuple-element.210), channel_id=1, source_target_pairs={{0,2},{2,0},{4,6},{6,4},{8,10},{10,8},{12,14},{14,12},{1,3},{3,1},... | collective-permute-start | bytes 393224 | tf_op jit(solution)/shard_map/ppermute | solution.py:202
  45.3 10.9 %collective-permute-start.16 = (bf16[2,64,512]{2,1,0:T(8,128)(2,1)S(1)}, bf16[2,64,512]{2,1,0:T(8,128)(2,1)S(1)}, u32[]{:S(2)}, u32[]{:S(2)}) collective-permute-start(bf16[2,64,512]{2,1,0:T(8,128)(2,1)S(1)} %get-tuple-element.209), channel_id=1, source_target_pairs={{0,4},{2,6},{4,0},{6,2},{8,12},{10,14},{12,8},{14,10},{1,5},{3,7},... | collective-permute-start | bytes 393224 | tf_op jit(solution)/shard_map/ppermute | solution.py:202
  47.8 11.1 %collective-permute-start.17 = (bf16[2,64,512]{2,1,0:T(8,128)(2,1)S(1)}, bf16[2,64,512]{2,1,0:T(8,128)(2,1)S(1)}, u32[]{:S(2)}, u32[]{:S(2)}) collective-permute-start(bf16[2,64,512]{2,1,0:T(8,128)(2,1)S(1)} %get-tuple-element.208), channel_id=1, source_target_pairs={{0,6},{2,4},{4,2},{6,0},{8,14},{10,12},{12,10},{14,8},{1,7},{3,5},... | collective-permute-start | bytes 393224 | tf_op jit(solution)/shard_map/ppermute | solution.py:202
  72.0 10.0 %collective-permute-start.25 = (bf16[64,1024]{1,0:T(8,128)(2,1)S(1)}, bf16[64,1024]{1,0:T(8,128)(2,1)S(1)}, u32[]{:S(2)}, u32[]{:S(2)}) collective-permute-start(bf16[64,1024]{1,0:T(8,128)(2,1)S(1)} %get-tuple-element.206), channel_id=1, source_target_pairs={{0,6},{2,4},{4,2},{6,0},{8,14},{10,12},{12,10},{14,8},{1,7},{3,5},... | collective-permute-start | bytes 393224 | tf_op jit(solution)/shard_map/ppermute | solution.py:202
  74.9 10.4 %collective-permute-start.31 = (bf16[2,64,1024]{2,1,0:T(8,128)(2,1)S(1)}, bf16[2,64,1024]{2,1,0:T(8,128)(2,1)S(1)}, u32[]{:S(2)}, u32[]{:S(2)}) collective-permute-start(bf16[2,64,1024]{2,1,0:T(8,128)(2,1)S(1)} %get-tuple-element.228), channel_id=1, source_target_pairs={{0,2},{2,0},{4,6},{6,4},{8,10},{10,8},{12,14},{14,12},{1,3},{3,1},... | collective-permute-start | bytes 786440 | tf_op jit(solution)/shard_map/ppermute | solution.py:202
  75.4 14.0 %collective-permute-start.32 = (bf16[2,64,1024]{2,1,0:T(8,128)(2,1)S(1)}, bf16[2,64,1024]{2,1,0:T(8,128)(2,1)S(1)}, u32[]{:S(2)}, u32[]{:S(2)}) collective-permute-start(bf16[2,64,1024]{2,1,0:T(8,128)(2,1)S(1)} %get-tuple-element.228), channel_id=1, source_target_pairs={{0,4},{2,6},{4,0},{6,2},{8,12},{10,14},{12,8},{14,10},{1,5},{3,7},... | collective-permute-start | bytes 786440 | tf_op jit(solution)/shard_map/ppermute | solution.py:202
  76.9 18.0 %collective-permute-start.33 = (bf16[2,64,1024]{2,1,0:T(8,128)(2,1)S(1)}, bf16[2,64,1024]{2,1,0:T(8,128)(2,1)S(1)}, u32[]{:S(2)}, u32[]{:S(2)}) collective-permute-start(bf16[2,64,1024]{2,1,0:T(8,128)(2,1)S(1)} %get-tuple-element.228), channel_id=1, source_target_pairs={{0,6},{2,4},{4,2},{6,0},{8,14},{10,12},{12,10},{14,8},{1,7},{3,5},... | collective-permute-start | bytes 786440 | tf_op jit(solution)/shard_map/ppermute | solution.py:202
  82.1 12.9 %collective-permute-start.26 = (bf16[64,1024]{1,0:T(8,128)(2,1)S(1)}, bf16[64,1024]{1,0:T(8,128)(2,1)S(1)}, u32[]{:S(2)}, u32[]{:S(2)}) collective-permute-start(bf16[64,1024]{1,0:T(8,128)(2,1)S(1)} %get-tuple-element.252), channel_id=1, source_target_pairs={{0,8},{2,10},{4,12},{6,14},{8,0},{10,2},{12,4},{14,6},{1,9},{3,11}... | collective-permute-start | bytes 393224 | tf_op jit(solution)/shard_map/ppermute | solution.py:211
  96.9 19.9 %collective-permute-start.30 = (bf16[256,512]{1,0:T(8,128)(2,1)S(1)}, bf16[256,512]{1,0:T(8,128)(2,1)S(1)}, u32[]{:S(2)}, u32[]{:S(2)}) collective-permute-start(bf16[256,512]{1,0:T(8,128)(2,1)S(1)} %pad_maximum_fusion.15), channel_id=1, source_target_pairs={{0,8},{2,10},{4,12},{6,14},{8,0},{10,2},{12,4},{14,6},{1,9},{3,11}... | collective-permute-start | bytes 786440 | tf_op jit(solution)/shard_map/ppermute | solution.py:211
  97.0 19.7 %collective-permute-start.27 = (bf16[2,64,1024]{2,1,0:T(8,128)(2,1)S(1)}, bf16[2,64,1024]{2,1,0:T(8,128)(2,1)S(1)}, u32[]{:S(2)}, u32[]{:S(2)}) collective-permute-start(bf16[2,64,1024]{2,1,0:T(8,128)(2,1)S(1)} %pad_maximum_fusion.19), channel_id=1, source_target_pairs={{0,2},{2,0},{4,6},{6,4},{8,10},{10,8},{12,14},{14,12},{1,3},{3,1},... | collective-permute-start | bytes 786440 | tf_op jit(solution)/shard_map/ppermute | solution.py:202
  98.6 18.2 %collective-permute-start.28 = (bf16[2,64,1024]{2,1,0:T(8,128)(2,1)S(1)}, bf16[2,64,1024]{2,1,0:T(8,128)(2,1)S(1)}, u32[]{:S(2)}, u32[]{:S(2)}) collective-permute-start(bf16[2,64,1024]{2,1,0:T(8,128)(2,1)S(1)} %pad_maximum_fusion.19), channel_id=1, source_target_pairs={{0,4},{2,6},{4,0},{6,2},{8,12},{10,14},{12,8},{14,10},{1,5},{3,7},... | collective-permute-start | bytes 786440 | tf_op jit(solution)/shard_map/ppermute | solution.py:202
  101.0 17.2 %collective-permute-start.29 = (bf16[2,64,1024]{2,1,0:T(8,128)(2,1)S(1)}, bf16[2,64,1024]{2,1,0:T(8,128)(2,1)S(1)}, u32[]{:S(2)}, u32[]{:S(2)}) collective-permute-start(bf16[2,64,1024]{2,1,0:T(8,128)(2,1)S(1)} %pad_maximum_fusion.19), channel_id=1, source_target_pairs={{0,6},{2,4},{4,2},{6,0},{8,14},{10,12},{12,10},{14,8},{1,7},{3,5},... | collective-permute-start | bytes 786440 | tf_op jit(solution)/shard_map/ppermute | solution.py:202
  119.4 22.5 %collective-permute-start.40 = (bf16[256,512]{1,0:T(8,128)(2,1)S(1)}, bf16[256,512]{1,0:T(8,128)(2,1)S(1)}, u32[]{:S(2)}, u32[]{:S(2)}) collective-permute-start(bf16[256,512]{1,0:T(8,128)(2,1)S(1)} %pad_maximum_fusion.18), channel_id=1, source_target_pairs={{0,8},{2,10},{4,12},{6,14},{8,0},{10,2},{12,4},{14,6},{1,9},{3,11}... | collective-permute-start | bytes 786440 | tf_op jit(solution)/shard_map/ppermute | solution.py:211
  120.3 25.7 %collective-permute-start.39 = (bf16[256,512]{1,0:T(8,128)(2,1)S(1)}, bf16[256,512]{1,0:T(8,128)(2,1)S(1)}, u32[]{:S(2)}, u32[]{:S(2)}) collective-permute-start(bf16[256,512]{1,0:T(8,128)(2,1)S(1)} %copy-done.11), channel_id=1, source_target_pairs={{0,8},{2,10},{4,12},{6,14},{8,0},{10,2},{12,4},{14,6},{1,9},{3,11}... | collective-permute-start | bytes 786440 | tf_op jit(solution)/shard_map/ppermute | solution.py:211
  123.1 22.9 %collective-permute-start.36 = (bf16[2,64,1024]{2,1,0:T(8,128)(2,1)S(1)}, bf16[2,64,1024]{2,1,0:T(8,128)(2,1)S(1)}, u32[]{:S(2)}, u32[]{:S(2)}) collective-permute-start(bf16[2,64,1024]{2,1,0:T(8,128)(2,1)S(1)} %get-tuple-element.159), channel_id=1, source_target_pairs={{0,2},{2,0},{4,6},{6,4},{8,10},{10,8},{12,14},{14,12},{1,3},{3,1},... | collective-permute-start | bytes 786440 | tf_op jit(solution)/shard_map/ppermute | solution.py:202
  124.8 21.2 %collective-permute-start.37 = (bf16[2,64,1024]{2,1,0:T(8,128)(2,1)S(1)}, bf16[2,64,1024]{2,1,0:T(8,128)(2,1)S(1)}, u32[]{:S(2)}, u32[]{:S(2)}) collective-permute-start(bf16[2,64,1024]{2,1,0:T(8,128)(2,1)S(1)} %get-tuple-element.158), channel_id=1, source_target_pairs={{0,4},{2,6},{4,0},{6,2},{8,12},{10,14},{12,8},{14,10},{1,5},{3,7},... | collective-permute-start | bytes 786440 | tf_op jit(solution)/shard_map/ppermute | solution.py:202
  125.2 24.1 %collective-permute-start.38 = (bf16[2,64,1024]{2,1,0:T(8,128)(2,1)S(1)}, bf16[2,64,1024]{2,1,0:T(8,128)(2,1)S(1)}, u32[]{:S(2)}, u32[]{:S(2)}) collective-permute-start(bf16[2,64,1024]{2,1,0:T(8,128)(2,1)S(1)} %get-tuple-element.157), channel_id=1, source_target_pairs={{0,6},{2,4},{4,2},{6,0},{8,14},{10,12},{12,10},{14,8},{1,7},{3,5},... | collective-permute-start | bytes 786440 | tf_op jit(solution)/shard_map/ppermute | solution.py:202
  149.7 15.6 %collective-permute-start.46 = (bf16[2,64,1024]{2,1,0:T(8,128)(2,1)S(1)}, bf16[2,64,1024]{2,1,0:T(8,128)(2,1)S(1)}, u32[]{:S(2)}, u32[]{:S(2)}) collective-permute-start(bf16[2,64,1024]{2,1,0:T(8,128)(2,1)S(1)} %add_convert_fusion.1), channel_id=1, source_target_pairs={{0,8},{2,10},{4,12},{6,14},{8,0},{10,2},{12,4},{14,6},{1,9},{3,11}... | collective-permute-start | bytes 786440 | tf_op jit(solution)/shard_map/ppermute | solution.py:211
  150.1 15.2 %collective-permute-start.47 = (bf16[256,512]{1,0:T(8,128)(2,1)S(1)}, bf16[256,512]{1,0:T(8,128)(2,1)S(1)}, u32[]{:S(2)}, u32[]{:S(2)}) collective-permute-start(bf16[256,512]{1,0:T(8,128)(2,1)S(1)} %collective-permute-done.39), channel_id=1, source_target_pairs={{0,16},{16,0},{1,17},{17,1},{2,18},{18,2},{3,19},{19,3},{4,20},{20... | collective-permute-start | bytes 786440 | tf_op jit(solution)/shard_map/ppermute | solution.py:208
  152.7 12.6 %collective-permute-start.43 = (bf16[2,64,1024]{2,1,0:T(8,128)(2,1)S(1)}, bf16[2,64,1024]{2,1,0:T(8,128)(2,1)S(1)}, u32[]{:S(2)}, u32[]{:S(2)}) collective-permute-start(bf16[2,64,1024]{2,1,0:T(8,128)(2,1)S(1)} %get-tuple-element.153), channel_id=1, source_target_pairs={{0,2},{2,0},{4,6},{6,4},{8,10},{10,8},{12,14},{14,12},{1,3},{3,1},... | collective-permute-start | bytes 786440 | tf_op jit(solution)/shard_map/ppermute | solution.py:202
  153.9 14.7 %collective-permute-start.44 = (bf16[2,64,1024]{2,1,0:T(8,128)(2,1)S(1)}, bf16[2,64,1024]{2,1,0:T(8,128)(2,1)S(1)}, u32[]{:S(2)}, u32[]{:S(2)}) collective-permute-start(bf16[2,64,1024]{2,1,0:T(8,128)(2,1)S(1)} %get-tuple-element.152), channel_id=1, source_target_pairs={{0,4},{2,6},{4,0},{6,2},{8,12},{10,14},{12,8},{14,10},{1,5},{3,7},... | collective-permute-start | bytes 786440 | tf_op jit(solution)/shard_map/ppermute | solution.py:202
  155.3 18.1 %collective-permute-start.45 = (bf16[2,64,1024]{2,1,0:T(8,128)(2,1)S(1)}, bf16[2,64,1024]{2,1,0:T(8,128)(2,1)S(1)}, u32[]{:S(2)}, u32[]{:S(2)}) collective-permute-start(bf16[2,64,1024]{2,1,0:T(8,128)(2,1)S(1)} %get-tuple-element.151), channel_id=1, source_target_pairs={{0,6},{2,4},{4,2},{6,0},{8,14},{10,12},{12,10},{14,8},{1,7},{3,5},... | collective-permute-start | bytes 786440 | tf_op jit(solution)/shard_map/ppermute | solution.py:202
  173.6 10.0 %collective-permute-start.48 = (bf16[64,1536]{1,0:T(8,128)(2,1)S(1)}, bf16[64,1536]{1,0:T(8,128)(2,1)S(1)}, u32[]{:S(2)}, u32[]{:S(2)}) collective-permute-start(bf16[64,1536]{1,0:T(8,128)(2,1)S(1)} %pad_maximum_fusion.22), channel_id=1, source_target_pairs={{0,2},{2,0},{4,6},{6,4},{8,10},{10,8},{12,14},{14,12},{1,3},{3,1},... | collective-permute-start | bytes 589832 | tf_op jit(solution)/shard_map/ppermute | solution.py:202
  174.8 13.2 %collective-permute-start.49 = (bf16[64,1536]{1,0:T(8,128)(2,1)S(1)}, bf16[64,1536]{1,0:T(8,128)(2,1)S(1)}, u32[]{:S(2)}, u32[]{:S(2)}) collective-permute-start(bf16[64,1536]{1,0:T(8,128)(2,1)S(1)} %pad_maximum_fusion.22), channel_id=1, source_target_pairs={{0,4},{2,6},{4,0},{6,2},{8,12},{10,14},{12,8},{14,10},{1,5},{3,7},... | collective-permute-start | bytes 589832 | tf_op jit(solution)/shard_map/ppermute | solution.py:202
  174.8 15.6 %collective-permute-start.50 = (bf16[64,1536]{1,0:T(8,128)(2,1)S(1)}, bf16[64,1536]{1,0:T(8,128)(2,1)S(1)}, u32[]{:S(2)}, u32[]{:S(2)}) collective-permute-start(bf16[64,1536]{1,0:T(8,128)(2,1)S(1)} %pad_maximum_fusion.22), channel_id=1, source_target_pairs={{0,6},{2,4},{4,2},{6,0},{8,14},{10,12},{12,10},{14,8},{1,7},{3,5},... | collective-permute-start | bytes 589832 | tf_op jit(solution)/shard_map/ppermute | solution.py:202
  177.3 13.1 %collective-permute-start.51 = (bf16[2,64,1024]{2,1,0:T(8,128)(2,1)S(1)}, bf16[2,64,1024]{2,1,0:T(8,128)(2,1)S(1)}, u32[]{:S(2)}, u32[]{:S(2)}) collective-permute-start(bf16[2,64,1024]{2,1,0:T(8,128)(2,1)S(1)} %add_convert_fusion), channel_id=1, source_target_pairs={{0,8},{2,10},{4,12},{6,14},{8,0},{10,2},{12,4},{14,6},{1,9},{3,11}... | collective-permute-start | bytes 786440 | tf_op jit(solution)/shard_map/ppermute | solution.py:211
  192.9 10.7 %collective-permute-start.61 = (bf16[64,1536]{1,0:T(8,128)(2,1)S(1)}, bf16[64,1536]{1,0:T(8,128)(2,1)S(1)}, u32[]{:S(2)}, u32[]{:S(2)}) collective-permute-start(bf16[64,1536]{1,0:T(8,128)(2,1)S(1)} %pad_maximum_fusion.23), channel_id=1, source_target_pairs={{0,6},{2,4},{4,2},{6,0},{8,14},{10,12},{12,10},{14,8},{1,7},{3,5},... | collective-permute-start | bytes 589832 | tf_op jit(solution)/shard_map/ppermute | solution.py:202
  203.8 9.1 %collective-permute-start.56 = (bf16[128,512]{1,0:T(8,128)(2,1)S(1)}, bf16[128,512]{1,0:T(8,128)(2,1)S(1)}, u32[]{:S(2)}, u32[]{:S(2)}) collective-permute-start(bf16[128,512]{1,0:T(8,128)(2,1)S(1)} %get-tuple-element.197), channel_id=1, source_target_pairs={{0,2},{2,0},{4,6},{6,4},{8,10},{10,8},{12,14},{14,12},{1,3},{3,1},... | collective-permute-start | bytes 393224 | tf_op jit(solution)/shard_map/ppermute | solution.py:202
  205.1 10.0 %collective-permute-start.57 = (bf16[128,512]{1,0:T(8,128)(2,1)S(1)}, bf16[128,512]{1,0:T(8,128)(2,1)S(1)}, u32[]{:S(2)}, u32[]{:S(2)}) collective-permute-start(bf16[128,512]{1,0:T(8,128)(2,1)S(1)} %get-tuple-element.196), channel_id=1, source_target_pairs={{0,4},{2,6},{4,0},{6,2},{8,12},{10,14},{12,8},{14,10},{1,5},{3,7},... | collective-permute-start | bytes 393224 | tf_op jit(solution)/shard_map/ppermute | solution.py:202
  205.9 10.4 %collective-permute-start.58 = (bf16[128,512]{1,0:T(8,128)(2,1)S(1)}, bf16[128,512]{1,0:T(8,128)(2,1)S(1)}, u32[]{:S(2)}, u32[]{:S(2)}) collective-permute-start(bf16[128,512]{1,0:T(8,128)(2,1)S(1)} %get-tuple-element.195), channel_id=1, source_target_pairs={{0,6},{2,4},{4,2},{6,0},{8,14},{10,12},{12,10},{14,8},{1,7},{3,5},... | collective-permute-start | bytes 393224 | tf_op jit(solution)/shard_map/ppermute | solution.py:202
  207.5 9.7 %collective-permute-start.53 = (bf16[512,128]{1,0:T(8,128)(2,1)S(1)}, bf16[512,128]{1,0:T(8,128)(2,1)S(1)}, u32[]{:S(2)}, u32[]{:S(2)}) collective-permute-start(bf16[512,128]{1,0:T(8,128)(2,1)S(1)} %get-tuple-element.201), channel_id=1, source_target_pairs={{0,2},{2,0},{4,6},{6,4},{8,10},{10,8},{12,14},{14,12},{1,3},{3,1},... | collective-permute-start | bytes 393224 | tf_op jit(solution)/shard_map/ppermute | solution.py:202
  208.7 9.9 %collective-permute-start.54 = (bf16[512,128]{1,0:T(8,128)(2,1)S(1)}, bf16[512,128]{1,0:T(8,128)(2,1)S(1)}, u32[]{:S(2)}, u32[]{:S(2)}) collective-permute-start(bf16[512,128]{1,0:T(8,128)(2,1)S(1)} %get-tuple-element.200), channel_id=1, source_target_pairs={{0,4},{2,6},{4,0},{6,2},{8,12},{10,14},{12,8},{14,10},{1,5},{3,7},... | collective-permute-start | bytes 393224 | tf_op jit(solution)/shard_map/ppermute | solution.py:202
  217.2 8.8 %collective-permute-start.68 = (bf16[512,128]{1,0:T(8,128)(2,1)S(1)}, bf16[512,128]{1,0:T(8,128)(2,1)S(1)}, u32[]{:S(2)}, u32[]{:S(2)}) collective-permute-start(bf16[512,128]{1,0:T(8,128)(2,1)S(1)} %get-tuple-element.184), channel_id=1, source_target_pairs={{0,6},{2,4},{4,2},{6,0},{8,14},{10,12},{12,10},{14,8},{1,7},{3,5},... | collective-permute-start | bytes 393224 | tf_op jit(solution)/shard_map/ppermute | solution.py:202
  (72 other events, 574.1 us)

commit v15 on v14

--- a/solution.py
+++ b/solution.py
@@ -445,31 +445,31 @@
     *part_y, cot_first[-1], out_part = together(*part_y, cot_first[-1], out_part)
     part_y = jnp.stack(part_y)
     latent_grad = rows_with(part_y, t_swap(part_y))
-    down_far = gather_h(after(down_half, cot_first[-1]))[1:]
     cot_second = gather_h(after(cot_rows[2 * tok_rows :], cot_first[-1]))
     out_part = sum_tensor(out_part)
     dpu, in_part = backward(
         after(latent_grad, out_part), cp, cu, gate_proj, up_proj, down_rows
     )
     out_part = exchange(lambda r: out_part[r])
-    *out_part, down_far[-1], cot_second[-1], in_part = together(
-        *out_part, down_far[-1], cot_second[-1], in_part
-    )
-    down_theirs = [swap_features(v) for v in down_far]
+    *out_part, cot_second[-1], in_part = together(*out_part, cot_second[-1], in_part)
+    down_far = gather_h(after(down_half, in_part))[1:]
     cot_parts = join_pairs(zip(cot_first, cot_second))
     out_part = add(*out_part)
     in_part = sum_tensor(in_part)
     gate_proj_grad, up_proj_grad = input_grads(latent_in, after(dpu, in_part))
     in_part = exchange(lambda r: in_part[r])
-    *in_part, out_theirs, down_theirs[-1], gate_proj_grad = together(
-        *in_part, sum_squares(out_part)[1], down_theirs[-1], gate_proj_grad
-    )
-    down_parts = [down_own] + [all_features(v, w) for v, w in zip(down_far, down_theirs)]
+    *in_part, out_theirs, down_far[-1], gate_proj_grad = together(
+        *in_part, sum_squares(out_part)[1], down_far[-1], gate_proj_grad
+    )
+    down_theirs = [swap_features(v) for v in down_far]
     out_part = join_squares(out_part, out_theirs)
     in_part, in_theirs = sum_squares(add(*in_part))
     out_part = exchange(lambda r: out_part)
     down_proj_grad = down_grads(hs, after(latent_grad, in_part))
-    *out_part, in_theirs, down_proj_grad = together(*out_part, in_theirs, down_proj_grad)
+    *out_part, in_theirs, down_theirs[-1], down_proj_grad = together(
+        *out_part, in_theirs, down_theirs[-1], down_proj_grad
+    )
+    down_parts = [down_own] + [all_features(v, w) for v, w in zip(down_far, down_theirs)]
     out_part = jnp.stack(out_part)
     in_part = join_squares(in_part, in_theirs)
     in_part = exchange(lambda r: in_part)

time: 233 us -> 237 us (1.017)
  waiting for transfers between devices: 83 us -> 95.1 us
  starting transfers between devices: 77.4 us -> 68.3 us
    ppermute x8, waiting for transfers between devices: 17.6 us -> 27.3 us  [up(): lax.ppermute(v, 'expert', [(e, (e + 4) % n_expert) for e in range(n_exper...]
    ppermute x45, waiting for transfers between devices: 52.5 us -> 61.9 us  [to_peer(): return lax.ppermute(v, 'expert', [(e, e ^ r) for e in range(n_expert)])]
    ppermute x4, waiting for transfers between devices: 10.4 us -> 2.35 us  [to_square(): return lax.ppermute(v, 'expert', perm)]
    ppermute x45, starting transfers between devices: 53.9 us -> 49 us  [to_peer(): return lax.ppermute(v, 'expert', [(e, e ^ r) for e in range(n_expert)])]
    ppermute x8, starting transfers between devices: 9.29 us -> 6.9 us  [up(): lax.ppermute(v, 'expert', [(e, (e + 4) % n_expert) for e in range(n_exper...]
    unnamed x107 -> x103, local copies, waits for them, and re-layouts: 5.05 us -> 5.83 us
  transfers between devices with their start and end apart: 69 -> 69, of which waited for: 30 -> 33; matrix products, arithmetic and copies ran while one was open for 6% -> 6% of each run, Pallas kernels for 19% -> 19%
where the time goes in v15:
time: 237 us; the launch traced here: 236 us
  waiting for transfers between devices  95.1 us (40%)
  starting transfers between devices  68.3 us (29%)
  Pallas kernels  44.3 us (19%)
  local copies, waits for them, and re-layouts  10.6 us (4%)
  other arithmetic  10.3 us (4%)
  matrix products  5.72 us (2%)
    ppermute x45, waiting for transfers between devices, to_peer(): return lax.ppermute(v, 'expert', [(e, e ^ r) for e in range(n_expert)])  61.9 us
    ppermute x45, starting transfers between devices, to_peer(): return lax.ppermute(v, 'expert', [(e, e ^ r) for e in range(n_expert)])  49 us
    ppermute x8, waiting for transfers between devices, up(): lax.ppermute(v, 'expert', [(e, (e + 4) % n_expert) for e in range(n_exper...  27.3 us
    pallas_call x1, Pallas kernels, local(): backward(after(latent_grad, out_part), cp, cu, gate_proj, up_proj, down_r...  15.2 us
    pallas_call x1, Pallas kernels, local(): forward(latent_in, gate_blocks(gate_columns), gate_proj, up_proj, down_rows)  15.1 us
    pallas_call x1, Pallas kernels, local(): gate_proj_grad, up_proj_grad = input_grads(latent_in, after(dpu, in_part))  9.03 us
    ppermute x8, starting transfers between devices, up(): lax.ppermute(v, 'expert', [(e, (e + 4) % n_expert) for e in range(n_exper...  6.9 us
    ppermute x4, starting transfers between devices, to_square(): return lax.ppermute(v, 'expert', perm)  6.53 us
  transfers between devices with their start and end apart: 69, of which 33 were waited for; matrix products, arithmetic and copies ran while one was open for 6% of the time, Pallas kernels for 19%

profile of v15, /device:TPU:0, one launch (start us, length us, event | category | flops | bytes accessed | tf_op | source)
XLA Modules:
  0.0 236.2 jit_solution(13359081658286385189)
XLA Ops:
  1.6 3.0 %collective-permute-start = (bf16[256,128]{1,0:T(8,128)(2,1)S(1)}, bf16[256,128]{1,0:T(8,128)(2,1)S(1)}, u32[]{:S(2)}, u32[]{:S(2)}) collective-permute-start(bf16[256,128]{1,0:T(8,128)(2,1)S(1)} %get-tuple-element.220), channel_id=1, source_target_pairs={{0,2},{2,0},{4,6},{6,4},{8,10},{10,8},{12,14},{14,12},{1,3},{3,1},... | collective-permute-start | bytes 196616 | tf_op jit(solution)/shard_map/ppermute | solution.py:202
  4.7 1.6 collective-permute-start.1
  7.6 4.1 %collective-permute-start.7 = (bf16[128,512]{1,0:T(8,128)(2,1)S(1)}, bf16[128,512]{1,0:T(8,128)(2,1)S(1)}, u32[]{:S(2)}, u32[]{:S(2)}) collective-permute-start(bf16[128,512]{1,0:T(8,128)(2,1)S(1)} %get-tuple-element.244), channel_id=1, source_target_pairs={{0,12},{2,14},{4,8},{6,10},{8,4},{10,6},{12,0},{14,2},{1,13},{3,15... | collective-permute-start | bytes 393224 | tf_op jit(solution)/shard_map/ppermute | solution.py:253
  11.8 1.6 collective-permute-start.4
  14.4 1.6 collective-permute-start.10
  16.9 1.9 collective-permute-done.4
  19.6 2.3 collective-permute-done.6
  22.1 2.4 %collective-permute-start.9 = (bf16[128,512]{1,0:T(8,128)(2,1)S(1)}, bf16[128,512]{1,0:T(8,128)(2,1)S(1)}, u32[]{:S(2)}, u32[]{:S(2)}) collective-permute-start(bf16[128,512]{1,0:T(8,128)(2,1)S(1)} %get-tuple-element.79), channel_id=1, source_target_pairs={{0,12},{2,14},{4,8},{6,10},{8,4},{10,6},{12,0},{14,2},{1,13},{3,15... | collective-permute-start | bytes 393224 | tf_op jit(solution)/shard_map/ppermute | solution.py:253
  24.5 7.0 %collective-permute-done.3 = bf16[128,1024]{1,0:T(8,128)(2,1)S(1)} collective-permute-done((bf16[128,1024]{1,0:T(8,128)(2,1)S(1)}, bf16[128,1024]{1,0:T(8,128)(2,1)S(1)}, u32[]{:S(2)}, u32[]{:S(2)}) %collective-permute-start.3) | collective-permute-done | bytes 262176 | tf_op jit(solution)/shard_map/ppermute | solution.py:202
  31.5 3.7 %collective-permute-done.11 = bf16[2,256,128]{2,1,0:T(8,128)(2,1)S(1)} collective-permute-done((bf16[2,256,128]{2,1,0:T(8,128)(2,1)S(1)}, bf16[2,256,128]{2,1,0:T(8,128)(2,1)S(1)}, u32[]{:S(2)}, u32[]{:S(2)}) %collective-permute-start.11) | collective-permute-done | bytes 131104 | tf_op jit(solution)/shard_map/ppermute | solution.py:202
  35.2 1.5 collective-permute-start.13
  37.5 5.6 %collective-permute-done.12 = bf16[256,256]{1,0:T(8,128)(2,1)S(1)} collective-permute-done((bf16[256,256]{1,0:T(8,128)(2,1)S(1)}, bf16[256,256]{1,0:T(8,128)(2,1)S(1)}, u32[]{:S(2)}, u32[]{:S(2)}) %collective-permute-start.12) | collective-permute-done | bytes 131104 | tf_op jit(solution)/shard_map/ppermute | solution.py:202
  44.8 1.5 collective-permute-start.21
  46.7 1.5 collective-permute-start.17
  48.2 1.5 collective-permute-start.16
  50.3 10.0 %collective-permute-done.18 = bf16[256,512]{1,0:T(8,128)(2,1)S(1)} collective-permute-done((bf16[256,512]{1,0:T(8,128)(2,1)S(1)}, bf16[256,512]{1,0:T(8,128)(2,1)S(1)}, u32[]{:S(2)}, u32[]{:S(2)}) %collective-permute-start.18) | collective-permute-done | bytes 262176 | tf_op jit(solution)/shard_map/ppermute | solution.py:211
  63.2 6.5 %collective-permute-done.19 = bf16[2,64,512]{2,1,0:T(8,128)(2,1)S(1)} collective-permute-done((bf16[2,64,512]{2,1,0:T(8,128)(2,1)S(1)}, bf16[2,64,512]{2,1,0:T(8,128)(2,1)S(1)}, u32[]{:S(2)}, u32[]{:S(2)}) %collective-permute-start.19) | collective-permute-done | bytes 131104 | tf_op jit(solution)/shard_map/ppermute | solution.py:211
  71.6 1.7 collective-permute-done.22
  74.8 2.3 collective-permute-start.24
  78.5 4.2 %collective-permute-done.23 = bf16[64,1024]{1,0:T(8,128)(2,1)S(1)} collective-permute-done((bf16[64,1024]{1,0:T(8,128)(2,1)S(1)}, bf16[64,1024]{1,0:T(8,128)(2,1)S(1)}, u32[]{:S(2)}, u32[]{:S(2)}) %collective-permute-start.23) | collective-permute-done | bytes 131104 | tf_op jit(solution)/shard_map/ppermute | solution.py:202
  82.7 1.5 collective-permute-done.24
  84.4 2.0 collective-permute-start.26
  86.3 6.3 %collective-permute-done.32 = bf16[2,64,1024]{2,1,0:T(8,128)(2,1)S(1)} collective-permute-done((bf16[2,64,1024]{2,1,0:T(8,128)(2,1)S(1)}, bf16[2,64,1024]{2,1,0:T(8,128)(2,1)S(1)}, u32[]{:S(2)}, u32[]{:S(2)}) %collective-permute-start.32) | collective-permute-done | bytes 262176 | tf_op jit(solution)/shard_map/ppermute | solution.py:202
  92.7 5.2 %collective-permute-done.33 = bf16[2,64,1024]{2,1,0:T(8,128)(2,1)S(1)} collective-permute-done((bf16[2,64,1024]{2,1,0:T(8,128)(2,1)S(1)}, bf16[2,64,1024]{2,1,0:T(8,128)(2,1)S(1)}, u32[]{:S(2)}, u32[]{:S(2)}) %collective-permute-start.33) | collective-permute-done | bytes 262176 | tf_op jit(solution)/shard_map/ppermute | solution.py:202
  100.0 2.9 %collective-permute-start.29 = (bf16[2,64,1024]{2,1,0:T(8,128)(2,1)S(1)}, bf16[2,64,1024]{2,1,0:T(8,128)(2,1)S(1)}, u32[]{:S(2)}, u32[]{:S(2)}) collective-permute-start(bf16[2,64,1024]{2,1,0:T(8,128)(2,1)S(1)} %pad_maximum_fusion.19), channel_id=1, source_target_pairs={{0,6},{2,4},{4,2},{6,0},{8,14},{10,12},{12,10},{14,8},{1,7},{3,5},... | collective-permute-start | bytes 786440 | tf_op jit(solution)/shard_map/ppermute | solution.py:202
  104.3 15.1 %shard_map.144 = (bf16[1024,1536]{1,0:T(8,128)(2,1)S(1)}, bf16[1024,1536]{1,0:T(8,128)(2,1)S(1)}, bf16[1024,1536]{1,0:T(8,128)(2,1)}, bf16[1024,1024]{1,0:T(8,128)(2,1)S(1)}) custom-call(bf16[1024,1024]{1,0:T(8,128)(2,1)S(1)} %bitcast.205, f32[2,1024,2]{2,1,0:T(8,128)S(1)} %bitcast.207, bf16[4,1024,384]{2,1,0:T(8,128)(2,1)} %wg_ref.3, ...), custom_call_target="tpu_custom_call" | custom-call | flops 9663676416 | bytes 23068672 | tf_op jit(solution)/shard_map/pallas_call | solution.py:441
  128.7 15.2 %shard_map.145 = (bf16[1024,3072]{1,0:T(8,128)(2,1)}, bf16[1024,1024]{1,0:T(8,128)(2,1)S(1)}) custom-call(bf16[1024,1024]{1,0:T(8,128)(2,1)S(1)} %bitcast.203, bf16[1024,1536]{1,0:T(8,128)(2,1)S(1)} %get-tuple-element.105.cp_ref, bf16[1024,1536]{1,0:T(8,128)(2,1)S(1)} %copy-done.2, bf16[4,1024,384]{2,1,0:T(8,128)(2,1)S(1)} %copy-done, ...), custom_call_target="tpu_custom_call" | custom-call | flops 9663676416 | bytes 26214400 | tf_op jit(solution)/shard_map/pallas_call | solution.py:450
  146.3 2.6 %collective-permute-start.45 = (bf16[2,64,1024]{2,1,0:T(8,128)(2,1)S(1)}, bf16[2,64,1024]{2,1,0:T(8,128)(2,1)S(1)}, u32[]{:S(2)}, u32[]{:S(2)}) collective-permute-start(bf16[2,64,1024]{2,1,0:T(8,128)(2,1)S(1)} %add_convert_fusion.1), channel_id=1, source_target_pairs={{0,8},{2,10},{4,12},{6,14},{8,0},{10,2},{12,4},{14,6},{1,9},{3,11}... | collective-permute-start | bytes 786440 | tf_op jit(solution)/shard_map/ppermute | solution.py:211
  149.8 2.4 %collective-permute-start.43 = (bf16[2,64,1024]{2,1,0:T(8,128)(2,1)S(1)}, bf16[2,64,1024]{2,1,0:T(8,128)(2,1)S(1)}, u32[]{:S(2)}, u32[]{:S(2)}) collective-permute-start(bf16[2,64,1024]{2,1,0:T(8,128)(2,1)S(1)} %get-tuple-element.152), channel_id=1, source_target_pairs={{0,4},{2,6},{4,0},{6,2},{8,12},{10,14},{12,8},{14,10},{1,5},{3,7},... | collective-permute-start | bytes 786440 | tf_op jit(solution)/shard_map/ppermute | solution.py:202
  153.0 9.0 %shard_map.146 = (bf16[4,1024,384]{2,1,0:T(8,128)(2,1)}, bf16[4,1024,384]{2,1,0:T(8,128)(2,1)}) custom-call(bf16[1024,1024]{1,0:T(8,128)(2,1)S(1)} %bitcast.206, bf16[1024,3072]{1,0:T(8,128)(2,1)S(1)} %copy-done.1), custom_call_target="tpu_custom_call" | custom-call | flops 6442450944 | bytes 14680064 | tf_op jit(solution)/shard_map/pallas_call | solution.py:459
  162.0 3.7 %collective-permute-done.46 = bf16[256,512]{1,0:T(8,128)(2,1)S(1)} collective-permute-done((bf16[256,512]{1,0:T(8,128)(2,1)S(1)}, bf16[256,512]{1,0:T(8,128)(2,1)S(1)}, u32[]{:S(2)}, u32[]{:S(2)}) %collective-permute-start.46) | collective-permute-done | bytes 262176 | tf_op jit(solution)/shard_map/ppermute | solution.py:211
  165.8 5.5 %collective-permute-done.45 = bf16[2,64,1024]{2,1,0:T(8,128)(2,1)S(1)} collective-permute-done((bf16[2,64,1024]{2,1,0:T(8,128)(2,1)S(1)}, bf16[2,64,1024]{2,1,0:T(8,128)(2,1)S(1)}, u32[]{:S(2)}, u32[]{:S(2)}) %collective-permute-start.45) | collective-permute-done | bytes 262176 | tf_op jit(solution)/shard_map/ppermute | solution.py:211
  171.3 3.1 %collective-permute-done.43 = bf16[2,64,1024]{2,1,0:T(8,128)(2,1)S(1)} collective-permute-done((bf16[2,64,1024]{2,1,0:T(8,128)(2,1)S(1)}, bf16[2,64,1024]{2,1,0:T(8,128)(2,1)S(1)}, u32[]{:S(2)}, u32[]{:S(2)}) %collective-permute-start.43) | collective-permute-done | bytes 262176 | tf_op jit(solution)/shard_map/ppermute | solution.py:202
  174.6 2.3 collective-permute-start.48
  179.9 5.0 %shard_map.147 = bf16[1536,1024]{1,0:T(8,128)(2,1)} custom-call(bf16[1024,1536]{1,0:T(8,128)(2,1)S(1)} %get-tuple-element.123.hs_ref, bf16[1024,1024]{1,0:T(8,128)(2,1)S(1)} %bitcast.204), custom_call_target="tpu_custom_call" | custom-call | flops 3221225472 | bytes 8388608 | tf_op jit(solution)/shard_map/pallas_call | solution.py:468
  184.9 2.8 %collective-permute-done.49 = bf16[64,1536]{1,0:T(8,128)(2,1)S(1)} collective-permute-done((bf16[64,1536]{1,0:T(8,128)(2,1)S(1)}, bf16[64,1536]{1,0:T(8,128)(2,1)S(1)}, u32[]{:S(2)}, u32[]{:S(2)}) %collective-permute-start.49) | collective-permute-done | bytes 196640 | tf_op jit(solution)/shard_map/ppermute | solution.py:202
  187.7 1.3 collective-permute-done.48
  189.1 1.6 collective-permute-done.50
  192.0 2.1 collective-permute-start.60
  198.9 1.3 collective-permute-done.61
  200.2 3.4 %collective-permute-done.60 = bf16[64,1536]{1,0:T(8,128)(2,1)S(1)} collective-permute-done((bf16[64,1536]{1,0:T(8,128)(2,1)S(1)}, bf16[64,1536]{1,0:T(8,128)(2,1)S(1)}, u32[]{:S(2)}, u32[]{:S(2)}) %collective-permute-start.60) | collective-permute-done | bytes 196640 | tf_op jit(solution)/shard_map/ppermute | solution.py:202
  204.8 2.1 collective-permute-start.54
  208.5 2.0 collective-permute-start.57
  217.2 1.8 collective-permute-start.64
  219.6 4.1 %collective-permute-done.56 = bf16[128,512]{1,0:T(8,128)(2,1)S(1)} collective-permute-done((bf16[128,512]{1,0:T(8,128)(2,1)S(1)}, bf16[128,512]{1,0:T(8,128)(2,1)S(1)}, u32[]{:S(2)}, u32[]{:S(2)}) %collective-permute-start.56) | collective-permute-done | bytes 131104 | tf_op jit(solution)/shard_map/ppermute | solution.py:202
  225.7 2.3 collective-permute-done.63
  229.0 1.9 collective-permute-done.66
  230.9 2.1 collective-permute-done.67
  (298 shorter events, 58.3 us)
Async XLA Ops:
  1.6 10.2 %collective-permute-start = (bf16[256,128]{1,0:T(8,128)(2,1)S(1)}, bf16[256,128]{1,0:T(8,128)(2,1)S(1)}, u32[]{:S(2)}, u32[]{:S(2)}) collective-permute-start(bf16[256,128]{1,0:T(8,128)(2,1)S(1)} %get-tuple-element.220), channel_id=1, source_target_pairs={{0,2},{2,0},{4,6},{6,4},{8,10},{10,8},{12,14},{14,12},{1,3},{3,1},... | collective-permute-start | bytes 196616 | tf_op jit(solution)/shard_map/ppermute | solution.py:202
  7.6 12.0 %collective-permute-start.7 = (bf16[128,512]{1,0:T(8,128)(2,1)S(1)}, bf16[128,512]{1,0:T(8,128)(2,1)S(1)}, u32[]{:S(2)}, u32[]{:S(2)}) collective-permute-start(bf16[128,512]{1,0:T(8,128)(2,1)S(1)} %get-tuple-element.244), channel_id=1, source_target_pairs={{0,12},{2,14},{4,8},{6,10},{8,4},{10,6},{12,0},{14,2},{1,13},{3,15... | collective-permute-start | bytes 393224 | tf_op jit(solution)/shard_map/ppermute | solution.py:253
  11.6 10.3 %collective-permute-start.6 = (bf16[128,512]{1,0:T(8,128)(2,1)S(1)}, bf16[128,512]{1,0:T(8,128)(2,1)S(1)}, u32[]{:S(2)}, u32[]{:S(2)}) collective-permute-start(bf16[128,512]{1,0:T(8,128)(2,1)S(1)} %get-tuple-element.243), channel_id=1, source_target_pairs={{0,8},{2,10},{4,12},{6,14},{8,0},{10,2},{12,4},{14,6},{1,9},{3,11}... | collective-permute-start | bytes 393224 | tf_op jit(solution)/shard_map/ppermute | solution.py:253
  14.4 22.3 %collective-permute-start.10 = (bf16[256,512]{1,0:T(8,128)(2,1)S(1)}, bf16[256,512]{1,0:T(8,128)(2,1)S(1)}, u32[]{:S(2)}, u32[]{:S(2)}) collective-permute-start(bf16[256,512]{1,0:T(8,128)(2,1)S(1)} %pad_maximum_fusion.13), channel_id=1, source_target_pairs={{0,16},{16,0},{1,17},{17,1},{2,18},{18,2},{3,19},{19,3},{4,20},{20... | collective-permute-start | bytes 786440 | tf_op jit(solution)/shard_map/ppermute | solution.py:208
  16.0 15.4 %collective-permute-start.3 = (bf16[128,1024]{1,0:T(8,128)(2,1)S(1)}, bf16[128,1024]{1,0:T(8,128)(2,1)S(1)}, u32[]{:S(2)}, u32[]{:S(2)}) collective-permute-start(bf16[128,1024]{1,0:T(8,128)(2,1)S(1)} %get-tuple-element.214), channel_id=1, source_target_pairs={{0,4},{2,6},{4,0},{6,2},{8,12},{10,14},{12,8},{14,10},{1,5},{3,7},... | collective-permute-start | bytes 786440 | tf_op jit(solution)/shard_map/ppermute | solution.py:202
  18.9 16.4 %collective-permute-start.11 = (bf16[2,256,128]{2,1,0:T(8,128)(2,1)S(1)}, bf16[2,256,128]{2,1,0:T(8,128)(2,1)S(1)}, u32[]{:S(2)}, u32[]{:S(2)}) collective-permute-start(bf16[2,256,128]{2,1,0:T(8,128)(2,1)S(1)} %pad_maximum_fusion.24), channel_id=1, source_target_pairs={{0,4},{2,6},{4,0},{6,2},{8,12},{10,14},{12,8},{14,10},{1,5},{3,7},... | collective-permute-start | bytes 393224 | tf_op jit(solution)/shard_map/ppermute | solution.py:202
  22.0 15.4 %collective-permute-start.8 = (bf16[128,512]{1,0:T(8,128)(2,1)S(1)}, bf16[128,512]{1,0:T(8,128)(2,1)S(1)}, u32[]{:S(2)}, u32[]{:S(2)}) collective-permute-start(bf16[128,512]{1,0:T(8,128)(2,1)S(1)} %get-tuple-element.78), channel_id=1, source_target_pairs={{0,8},{2,10},{4,12},{6,14},{8,0},{10,2},{12,4},{14,6},{1,9},{3,11}... | collective-permute-start | bytes 393224 | tf_op jit(solution)/shard_map/ppermute | solution.py:253
  22.1 15.4 %collective-permute-start.9 = (bf16[128,512]{1,0:T(8,128)(2,1)S(1)}, bf16[128,512]{1,0:T(8,128)(2,1)S(1)}, u32[]{:S(2)}, u32[]{:S(2)}) collective-permute-start(bf16[128,512]{1,0:T(8,128)(2,1)S(1)} %get-tuple-element.79), channel_id=1, source_target_pairs={{0,12},{2,14},{4,8},{6,10},{8,4},{10,6},{12,0},{14,2},{1,13},{3,15... | collective-permute-start | bytes 393224 | tf_op jit(solution)/shard_map/ppermute | solution.py:253
  31.5 11.5 %collective-permute-start.5 = (bf16[256,512]{1,0:T(8,128)(2,1)S(1)}, bf16[256,512]{1,0:T(8,128)(2,1)S(1)}, u32[]{:S(2)}, u32[]{:S(2)}) collective-permute-start(bf16[256,512]{1,0:T(8,128)(2,1)S(1)} %pad_maximum_fusion.12), channel_id=1, source_target_pairs={{0,4},{2,6},{4,0},{6,2},{8,12},{10,14},{12,8},{14,10},{1,5},{3,7},... | collective-permute-start | bytes 786440 | tf_op jit(solution)/shard_map/ppermute | solution.py:202
  44.8 17.7 %collective-permute-start.21 = (bf16[256,512]{1,0:T(8,128)(2,1)S(1)}, bf16[256,512]{1,0:T(8,128)(2,1)S(1)}, u32[]{:S(2)}, u32[]{:S(2)}) collective-permute-start(bf16[256,512]{1,0:T(8,128)(2,1)S(1)} %pad_maximum_fusion.16), channel_id=1, source_target_pairs={{0,16},{16,0},{1,17},{17,1},{2,18},{18,2},{3,19},{19,3},{4,20},{20... | collective-permute-start | bytes 786440 | tf_op jit(solution)/shard_map/ppermute | solution.py:208
  46.3 14.0 %collective-permute-start.18 = (bf16[256,512]{1,0:T(8,128)(2,1)S(1)}, bf16[256,512]{1,0:T(8,128)(2,1)S(1)}, u32[]{:S(2)}, u32[]{:S(2)}) collective-permute-start(bf16[256,512]{1,0:T(8,128)(2,1)S(1)} %pad_maximum_fusion.16), channel_id=1, source_target_pairs={{0,8},{2,10},{4,12},{6,14},{8,0},{10,2},{12,4},{14,6},{1,9},{3,11}... | collective-permute-start | bytes 786440 | tf_op jit(solution)/shard_map/ppermute | solution.py:211
  46.7 13.6 %collective-permute-start.17 = (bf16[2,64,512]{2,1,0:T(8,128)(2,1)S(1)}, bf16[2,64,512]{2,1,0:T(8,128)(2,1)S(1)}, u32[]{:S(2)}, u32[]{:S(2)}) collective-permute-start(bf16[2,64,512]{2,1,0:T(8,128)(2,1)S(1)} %get-tuple-element.208), channel_id=1, source_target_pairs={{0,6},{2,4},{4,2},{6,0},{8,14},{10,12},{12,10},{14,8},{1,7},{3,5},... | collective-permute-start | bytes 393224 | tf_op jit(solution)/shard_map/ppermute | solution.py:202
  48.2 13.4 %collective-permute-start.16 = (bf16[2,64,512]{2,1,0:T(8,128)(2,1)S(1)}, bf16[2,64,512]{2,1,0:T(8,128)(2,1)S(1)}, u32[]{:S(2)}, u32[]{:S(2)}) collective-permute-start(bf16[2,64,512]{2,1,0:T(8,128)(2,1)S(1)} %get-tuple-element.209), channel_id=1, source_target_pairs={{0,4},{2,6},{4,0},{6,2},{8,12},{10,14},{12,8},{14,10},{1,5},{3,7},... | collective-permute-start | bytes 393224 | tf_op jit(solution)/shard_map/ppermute | solution.py:202
  49.7 11.9 %collective-permute-start.15 = (bf16[2,64,512]{2,1,0:T(8,128)(2,1)S(1)}, bf16[2,64,512]{2,1,0:T(8,128)(2,1)S(1)}, u32[]{:S(2)}, u32[]{:S(2)}) collective-permute-start(bf16[2,64,512]{2,1,0:T(8,128)(2,1)S(1)} %get-tuple-element.210), channel_id=1, source_target_pairs={{0,2},{2,0},{4,6},{6,4},{8,10},{10,8},{12,14},{14,12},{1,3},{3,1},... | collective-permute-start | bytes 393224 | tf_op jit(solution)/shard_map/ppermute | solution.py:202
  73.5 9.2 %collective-permute-start.23 = (bf16[64,1024]{1,0:T(8,128)(2,1)S(1)}, bf16[64,1024]{1,0:T(8,128)(2,1)S(1)}, u32[]{:S(2)}, u32[]{:S(2)}) collective-permute-start(bf16[64,1024]{1,0:T(8,128)(2,1)S(1)} %get-tuple-element.205), channel_id=1, source_target_pairs={{0,2},{2,0},{4,6},{6,4},{8,10},{10,8},{12,14},{14,12},{1,3},{3,1},... | collective-permute-start | bytes 393224 | tf_op jit(solution)/shard_map/ppermute | solution.py:202
  74.8 9.4 %collective-permute-start.24 = (bf16[64,1024]{1,0:T(8,128)(2,1)S(1)}, bf16[64,1024]{1,0:T(8,128)(2,1)S(1)}, u32[]{:S(2)}, u32[]{:S(2)}) collective-permute-start(bf16[64,1024]{1,0:T(8,128)(2,1)S(1)} %get-tuple-element.207), channel_id=1, source_target_pairs={{0,4},{2,6},{4,0},{6,2},{8,12},{10,14},{12,8},{14,10},{1,5},{3,7},... | collective-permute-start | bytes 393224 | tf_op jit(solution)/shard_map/ppermute | solution.py:202
  77.1 15.5 %collective-permute-start.32 = (bf16[2,64,1024]{2,1,0:T(8,128)(2,1)S(1)}, bf16[2,64,1024]{2,1,0:T(8,128)(2,1)S(1)}, u32[]{:S(2)}, u32[]{:S(2)}) collective-permute-start(bf16[2,64,1024]{2,1,0:T(8,128)(2,1)S(1)} %get-tuple-element.228), channel_id=1, source_target_pairs={{0,4},{2,6},{4,0},{6,2},{8,12},{10,14},{12,8},{14,10},{1,5},{3,7},... | collective-permute-start | bytes 786440 | tf_op jit(solution)/shard_map/ppermute | solution.py:202
  77.2 15.5 %collective-permute-start.31 = (bf16[2,64,1024]{2,1,0:T(8,128)(2,1)S(1)}, bf16[2,64,1024]{2,1,0:T(8,128)(2,1)S(1)}, u32[]{:S(2)}, u32[]{:S(2)}) collective-permute-start(bf16[2,64,1024]{2,1,0:T(8,128)(2,1)S(1)} %get-tuple-element.228), channel_id=1, source_target_pairs={{0,2},{2,0},{4,6},{6,4},{8,10},{10,8},{12,14},{14,12},{1,3},{3,1},... | collective-permute-start | bytes 786440 | tf_op jit(solution)/shard_map/ppermute | solution.py:202
  82.7 15.1 %collective-permute-start.33 = (bf16[2,64,1024]{2,1,0:T(8,128)(2,1)S(1)}, bf16[2,64,1024]{2,1,0:T(8,128)(2,1)S(1)}, u32[]{:S(2)}, u32[]{:S(2)}) collective-permute-start(bf16[2,64,1024]{2,1,0:T(8,128)(2,1)S(1)} %get-tuple-element.228), channel_id=1, source_target_pairs={{0,6},{2,4},{4,2},{6,0},{8,14},{10,12},{12,10},{14,8},{1,7},{3,5},... | collective-permute-start | bytes 786440 | tf_op jit(solution)/shard_map/ppermute | solution.py:202
  84.4 13.6 %collective-permute-start.26 = (bf16[64,1024]{1,0:T(8,128)(2,1)S(1)}, bf16[64,1024]{1,0:T(8,128)(2,1)S(1)}, u32[]{:S(2)}, u32[]{:S(2)}) collective-permute-start(bf16[64,1024]{1,0:T(8,128)(2,1)S(1)} %get-tuple-element.252), channel_id=1, source_target_pairs={{0,8},{2,10},{4,12},{6,14},{8,0},{10,2},{12,4},{14,6},{1,9},{3,11}... | collective-permute-start | bytes 393224 | tf_op jit(solution)/shard_map/ppermute | solution.py:211
  99.8 19.6 %collective-permute-start.30 = (bf16[256,512]{1,0:T(8,128)(2,1)S(1)}, bf16[256,512]{1,0:T(8,128)(2,1)S(1)}, u32[]{:S(2)}, u32[]{:S(2)}) collective-permute-start(bf16[256,512]{1,0:T(8,128)(2,1)S(1)} %pad_maximum_fusion.15), channel_id=1, source_target_pairs={{0,8},{2,10},{4,12},{6,14},{8,0},{10,2},{12,4},{14,6},{1,9},{3,11}... | collective-permute-start | bytes 786440 | tf_op jit(solution)/shard_map/ppermute | solution.py:211
  100.0 19.4 %collective-permute-start.29 = (bf16[2,64,1024]{2,1,0:T(8,128)(2,1)S(1)}, bf16[2,64,1024]{2,1,0:T(8,128)(2,1)S(1)}, u32[]{:S(2)}, u32[]{:S(2)}) collective-permute-start(bf16[2,64,1024]{2,1,0:T(8,128)(2,1)S(1)} %pad_maximum_fusion.19), channel_id=1, source_target_pairs={{0,6},{2,4},{4,2},{6,0},{8,14},{10,12},{12,10},{14,8},{1,7},{3,5},... | collective-permute-start | bytes 786440 | tf_op jit(solution)/shard_map/ppermute | solution.py:202
  102.9 17.7 %collective-permute-start.28 = (bf16[2,64,1024]{2,1,0:T(8,128)(2,1)S(1)}, bf16[2,64,1024]{2,1,0:T(8,128)(2,1)S(1)}, u32[]{:S(2)}, u32[]{:S(2)}) collective-permute-start(bf16[2,64,1024]{2,1,0:T(8,128)(2,1)S(1)} %pad_maximum_fusion.19), channel_id=1, source_target_pairs={{0,4},{2,6},{4,0},{6,2},{8,12},{10,14},{12,8},{14,10},{1,5},{3,7},... | collective-permute-start | bytes 786440 | tf_op jit(solution)/shard_map/ppermute | solution.py:202
  102.9 17.7 %collective-permute-start.27 = (bf16[2,64,1024]{2,1,0:T(8,128)(2,1)S(1)}, bf16[2,64,1024]{2,1,0:T(8,128)(2,1)S(1)}, u32[]{:S(2)}, u32[]{:S(2)}) collective-permute-start(bf16[2,64,1024]{2,1,0:T(8,128)(2,1)S(1)} %pad_maximum_fusion.19), channel_id=1, source_target_pairs={{0,2},{2,0},{4,6},{6,4},{8,10},{10,8},{12,14},{14,12},{1,3},{3,1},... | collective-permute-start | bytes 786440 | tf_op jit(solution)/shard_map/ppermute | solution.py:202
  121.8 22.2 %collective-permute-start.39 = (bf16[256,512]{1,0:T(8,128)(2,1)S(1)}, bf16[256,512]{1,0:T(8,128)(2,1)S(1)}, u32[]{:S(2)}, u32[]{:S(2)}) collective-permute-start(bf16[256,512]{1,0:T(8,128)(2,1)S(1)} %pad_maximum_fusion.18), channel_id=1, source_target_pairs={{0,8},{2,10},{4,12},{6,14},{8,0},{10,2},{12,4},{14,6},{1,9},{3,11}... | collective-permute-start | bytes 786440 | tf_op jit(solution)/shard_map/ppermute | solution.py:211
  125.2 18.8 %collective-permute-start.38 = (bf16[2,64,1024]{2,1,0:T(8,128)(2,1)S(1)}, bf16[2,64,1024]{2,1,0:T(8,128)(2,1)S(1)}, u32[]{:S(2)}, u32[]{:S(2)}) collective-permute-start(bf16[2,64,1024]{2,1,0:T(8,128)(2,1)S(1)} %get-tuple-element.157), channel_id=1, source_target_pairs={{0,6},{2,4},{4,2},{6,0},{8,14},{10,12},{12,10},{14,8},{1,7},{3,5},... | collective-permute-start | bytes 786440 | tf_op jit(solution)/shard_map/ppermute | solution.py:202
  126.3 18.5 %collective-permute-start.37 = (bf16[2,64,1024]{2,1,0:T(8,128)(2,1)S(1)}, bf16[2,64,1024]{2,1,0:T(8,128)(2,1)S(1)}, u32[]{:S(2)}, u32[]{:S(2)}) collective-permute-start(bf16[2,64,1024]{2,1,0:T(8,128)(2,1)S(1)} %get-tuple-element.158), channel_id=1, source_target_pairs={{0,4},{2,6},{4,0},{6,2},{8,12},{10,14},{12,8},{14,10},{1,5},{3,7},... | collective-permute-start | bytes 786440 | tf_op jit(solution)/shard_map/ppermute | solution.py:202
  127.5 17.3 %collective-permute-start.36 = (bf16[2,64,1024]{2,1,0:T(8,128)(2,1)S(1)}, bf16[2,64,1024]{2,1,0:T(8,128)(2,1)S(1)}, u32[]{:S(2)}, u32[]{:S(2)}) collective-permute-start(bf16[2,64,1024]{2,1,0:T(8,128)(2,1)S(1)} %get-tuple-element.159), channel_id=1, source_target_pairs={{0,2},{2,0},{4,6},{6,4},{8,10},{10,8},{12,14},{14,12},{1,3},{3,1},... | collective-permute-start | bytes 786440 | tf_op jit(solution)/shard_map/ppermute | solution.py:202
  145.8 20.0 %collective-permute-start.46 = (bf16[256,512]{1,0:T(8,128)(2,1)S(1)}, bf16[256,512]{1,0:T(8,128)(2,1)S(1)}, u32[]{:S(2)}, u32[]{:S(2)}) collective-permute-start(bf16[256,512]{1,0:T(8,128)(2,1)S(1)} %copy-done.11), channel_id=1, source_target_pairs={{0,8},{2,10},{4,12},{6,14},{8,0},{10,2},{12,4},{14,6},{1,9},{3,11}... | collective-permute-start | bytes 786440 | tf_op jit(solution)/shard_map/ppermute | solution.py:211
  146.3 25.0 %collective-permute-start.45 = (bf16[2,64,1024]{2,1,0:T(8,128)(2,1)S(1)}, bf16[2,64,1024]{2,1,0:T(8,128)(2,1)S(1)}, u32[]{:S(2)}, u32[]{:S(2)}) collective-permute-start(bf16[2,64,1024]{2,1,0:T(8,128)(2,1)S(1)} %add_convert_fusion.1), channel_id=1, source_target_pairs={{0,8},{2,10},{4,12},{6,14},{8,0},{10,2},{12,4},{14,6},{1,9},{3,11}... | collective-permute-start | bytes 786440 | tf_op jit(solution)/shard_map/ppermute | solution.py:211
  149.4 21.8 %collective-permute-start.44 = (bf16[2,64,1024]{2,1,0:T(8,128)(2,1)S(1)}, bf16[2,64,1024]{2,1,0:T(8,128)(2,1)S(1)}, u32[]{:S(2)}, u32[]{:S(2)}) collective-permute-start(bf16[2,64,1024]{2,1,0:T(8,128)(2,1)S(1)} %get-tuple-element.151), channel_id=1, source_target_pairs={{0,6},{2,4},{4,2},{6,0},{8,14},{10,12},{12,10},{14,8},{1,7},{3,5},... | collective-permute-start | bytes 786440 | tf_op jit(solution)/shard_map/ppermute | solution.py:202
  149.8 24.6 %collective-permute-start.43 = (bf16[2,64,1024]{2,1,0:T(8,128)(2,1)S(1)}, bf16[2,64,1024]{2,1,0:T(8,128)(2,1)S(1)}, u32[]{:S(2)}, u32[]{:S(2)}) collective-permute-start(bf16[2,64,1024]{2,1,0:T(8,128)(2,1)S(1)} %get-tuple-element.152), channel_id=1, source_target_pairs={{0,4},{2,6},{4,0},{6,2},{8,12},{10,14},{12,8},{14,10},{1,5},{3,7},... | collective-permute-start | bytes 786440 | tf_op jit(solution)/shard_map/ppermute | solution.py:202
  152.2 22.2 %collective-permute-start.42 = (bf16[2,64,1024]{2,1,0:T(8,128)(2,1)S(1)}, bf16[2,64,1024]{2,1,0:T(8,128)(2,1)S(1)}, u32[]{:S(2)}, u32[]{:S(2)}) collective-permute-start(bf16[2,64,1024]{2,1,0:T(8,128)(2,1)S(1)} %get-tuple-element.153), channel_id=1, source_target_pairs={{0,2},{2,0},{4,6},{6,4},{8,10},{10,8},{12,14},{14,12},{1,3},{3,1},... | collective-permute-start | bytes 786440 | tf_op jit(solution)/shard_map/ppermute | solution.py:202
  174.6 13.2 %collective-permute-start.49 = (bf16[64,1536]{1,0:T(8,128)(2,1)S(1)}, bf16[64,1536]{1,0:T(8,128)(2,1)S(1)}, u32[]{:S(2)}, u32[]{:S(2)}) collective-permute-start(bf16[64,1536]{1,0:T(8,128)(2,1)S(1)} %pad_maximum_fusion.22), channel_id=1, source_target_pairs={{0,6},{2,4},{4,2},{6,0},{8,14},{10,12},{12,10},{14,8},{1,7},{3,5},... | collective-permute-start | bytes 589832 | tf_op jit(solution)/shard_map/ppermute | solution.py:202
  174.6 14.4 %collective-permute-start.48 = (bf16[64,1536]{1,0:T(8,128)(2,1)S(1)}, bf16[64,1536]{1,0:T(8,128)(2,1)S(1)}, u32[]{:S(2)}, u32[]{:S(2)}) collective-permute-start(bf16[64,1536]{1,0:T(8,128)(2,1)S(1)} %pad_maximum_fusion.22), channel_id=1, source_target_pairs={{0,4},{2,6},{4,0},{6,2},{8,12},{10,14},{12,8},{14,10},{1,5},{3,7},... | collective-permute-start | bytes 589832 | tf_op jit(solution)/shard_map/ppermute | solution.py:202
  176.9 12.2 %collective-permute-start.47 = (bf16[64,1536]{1,0:T(8,128)(2,1)S(1)}, bf16[64,1536]{1,0:T(8,128)(2,1)S(1)}, u32[]{:S(2)}, u32[]{:S(2)}) collective-permute-start(bf16[64,1536]{1,0:T(8,128)(2,1)S(1)} %pad_maximum_fusion.22), channel_id=1, source_target_pairs={{0,2},{2,0},{4,6},{6,4},{8,10},{10,8},{12,14},{14,12},{1,3},{3,1},... | collective-permute-start | bytes 589832 | tf_op jit(solution)/shard_map/ppermute | solution.py:202
  178.3 12.4 %collective-permute-start.50 = (bf16[2,64,1024]{2,1,0:T(8,128)(2,1)S(1)}, bf16[2,64,1024]{2,1,0:T(8,128)(2,1)S(1)}, u32[]{:S(2)}, u32[]{:S(2)}) collective-permute-start(bf16[2,64,1024]{2,1,0:T(8,128)(2,1)S(1)} %add_convert_fusion), channel_id=1, source_target_pairs={{0,8},{2,10},{4,12},{6,14},{8,0},{10,2},{12,4},{14,6},{1,9},{3,11}... | collective-permute-start | bytes 786440 | tf_op jit(solution)/shard_map/ppermute | solution.py:211
  178.9 11.8 %collective-permute-start.51 = (bf16[256,512]{1,0:T(8,128)(2,1)S(1)}, bf16[256,512]{1,0:T(8,128)(2,1)S(1)}, u32[]{:S(2)}, u32[]{:S(2)}) collective-permute-start(bf16[256,512]{1,0:T(8,128)(2,1)S(1)} %collective-permute-done.46), channel_id=1, source_target_pairs={{0,16},{16,0},{1,17},{17,1},{2,18},{18,2},{3,19},{19,3},{4,20},{20... | collective-permute-start | bytes 786440 | tf_op jit(solution)/shard_map/ppermute | solution.py:208
  192.0 11.6 %collective-permute-start.60 = (bf16[64,1536]{1,0:T(8,128)(2,1)S(1)}, bf16[64,1536]{1,0:T(8,128)(2,1)S(1)}, u32[]{:S(2)}, u32[]{:S(2)}) collective-permute-start(bf16[64,1536]{1,0:T(8,128)(2,1)S(1)} %pad_maximum_fusion.23), channel_id=1, source_target_pairs={{0,4},{2,6},{4,0},{6,2},{8,12},{10,14},{12,8},{14,10},{1,5},{3,7},... | collective-permute-start | bytes 589832 | tf_op jit(solution)/shard_map/ppermute | solution.py:202
  194.1 9.9 %collective-permute-start.59 = (bf16[64,1536]{1,0:T(8,128)(2,1)S(1)}, bf16[64,1536]{1,0:T(8,128)(2,1)S(1)}, u32[]{:S(2)}, u32[]{:S(2)}) collective-permute-start(bf16[64,1536]{1,0:T(8,128)(2,1)S(1)} %pad_maximum_fusion.23), channel_id=1, source_target_pairs={{0,2},{2,0},{4,6},{6,4},{8,10},{10,8},{12,14},{14,12},{1,3},{3,1},... | collective-permute-start | bytes 589832 | tf_op jit(solution)/shard_map/ppermute | solution.py:202
  204.4 10.1 %collective-permute-start.55 = (bf16[512,128]{1,0:T(8,128)(2,1)S(1)}, bf16[512,128]{1,0:T(8,128)(2,1)S(1)}, u32[]{:S(2)}, u32[]{:S(2)}) collective-permute-start(bf16[512,128]{1,0:T(8,128)(2,1)S(1)} %get-tuple-element.199), channel_id=1, source_target_pairs={{0,6},{2,4},{4,2},{6,0},{8,14},{10,12},{12,10},{14,8},{1,7},{3,5},... | collective-permute-start | bytes 393224 | tf_op jit(solution)/shard_map/ppermute | solution.py:202
  204.8 10.7 %collective-permute-start.54 = (bf16[512,128]{1,0:T(8,128)(2,1)S(1)}, bf16[512,128]{1,0:T(8,128)(2,1)S(1)}, u32[]{:S(2)}, u32[]{:S(2)}) collective-permute-start(bf16[512,128]{1,0:T(8,128)(2,1)S(1)} %get-tuple-element.200), channel_id=1, source_target_pairs={{0,4},{2,6},{4,0},{6,2},{8,12},{10,14},{12,8},{14,10},{1,5},{3,7},... | collective-permute-start | bytes 393224 | tf_op jit(solution)/shard_map/ppermute | solution.py:202
  206.9 9.7 %collective-permute-start.53 = (bf16[512,128]{1,0:T(8,128)(2,1)S(1)}, bf16[512,128]{1,0:T(8,128)(2,1)S(1)}, u32[]{:S(2)}, u32[]{:S(2)}) collective-permute-start(bf16[512,128]{1,0:T(8,128)(2,1)S(1)} %get-tuple-element.201), channel_id=1, source_target_pairs={{0,2},{2,0},{4,6},{6,4},{8,10},{10,8},{12,14},{14,12},{1,3},{3,1},... | collective-permute-start | bytes 393224 | tf_op jit(solution)/shard_map/ppermute | solution.py:202
  208.0 9.3 %collective-permute-start.58 = (bf16[128,512]{1,0:T(8,128)(2,1)S(1)}, bf16[128,512]{1,0:T(8,128)(2,1)S(1)}, u32[]{:S(2)}, u32[]{:S(2)}) collective-permute-start(bf16[128,512]{1,0:T(8,128)(2,1)S(1)} %get-tuple-element.195), channel_id=1, source_target_pairs={{0,6},{2,4},{4,2},{6,0},{8,14},{10,12},{12,10},{14,8},{1,7},{3,5},... | collective-permute-start | bytes 393224 | tf_op jit(solution)/shard_map/ppermute | solution.py:202
  208.5 11.1 %collective-permute-start.57 = (bf16[128,512]{1,0:T(8,128)(2,1)S(1)}, bf16[128,512]{1,0:T(8,128)(2,1)S(1)}, u32[]{:S(2)}, u32[]{:S(2)}) collective-permute-start(bf16[128,512]{1,0:T(8,128)(2,1)S(1)} %get-tuple-element.196), channel_id=1, source_target_pairs={{0,4},{2,6},{4,0},{6,2},{8,12},{10,14},{12,8},{14,10},{1,5},{3,7},... | collective-permute-start | bytes 393224 | tf_op jit(solution)/shard_map/ppermute | solution.py:202
  215.6 12.4 %collective-permute-start.63 = (bf16[128,512]{1,0:T(8,128)(2,1)S(1)}, bf16[128,512]{1,0:T(8,128)(2,1)S(1)}, u32[]{:S(2)}, u32[]{:S(2)}) collective-permute-start(bf16[128,512]{1,0:T(8,128)(2,1)S(1)} %get-tuple-element.186), channel_id=1, source_target_pairs={{0,2},{2,0},{4,6},{6,4},{8,10},{10,8},{12,14},{14,12},{1,3},{3,1},... | collective-permute-start | bytes 393224 | tf_op jit(solution)/shard_map/ppermute | solution.py:202
  216.6 11.4 %collective-permute-start.65 = (bf16[128,512]{1,0:T(8,128)(2,1)S(1)}, bf16[128,512]{1,0:T(8,128)(2,1)S(1)}, u32[]{:S(2)}, u32[]{:S(2)}) collective-permute-start(bf16[128,512]{1,0:T(8,128)(2,1)S(1)} %get-tuple-element.187), channel_id=1, source_target_pairs={{0,6},{2,4},{4,2},{6,0},{8,14},{10,12},{12,10},{14,8},{1,7},{3,5},... | collective-permute-start | bytes 393224 | tf_op jit(solution)/shard_map/ppermute | solution.py:202
  217.2 10.8 %collective-permute-start.64 = (bf16[128,512]{1,0:T(8,128)(2,1)S(1)}, bf16[128,512]{1,0:T(8,128)(2,1)S(1)}, u32[]{:S(2)}, u32[]{:S(2)}) collective-permute-start(bf16[128,512]{1,0:T(8,128)(2,1)S(1)} %get-tuple-element.188), channel_id=1, source_target_pairs={{0,4},{2,6},{4,0},{6,2},{8,12},{10,14},{12,8},{14,10},{1,5},{3,7},... | collective-permute-start | bytes 393224 | tf_op jit(solution)/shard_map/ppermute | solution.py:202
  (70 other events, 582.5 us)
